TPU v7x, 32 devices: a whole 2x2x4 slice. The times are simulated.
32 devices in a mesh: rep: 2 (over x), grp: 2 (over core), ep: 8 (over z, y).
Axes of the slice: x: 2, y: 2, z: 4, core: 2. Of those that a mesh axis runs over, the one named last changes fastest.
Arguments:
- tokens: bfloat16 [4096, 4096], P(('rep', 'grp', 'ep')), parts along dimension 0, may hold values from -6 to 6
- expert_ids: int32 [4096, 8], P(('rep', 'grp', 'ep')), parts along dimension 0, may hold values from 0 to 15, all different within a row; in each aligned block of 128 rows (0 to 127, 128 to 255, ...) at most 128 rows name the same one
- route_scores: float32 [4096, 8], P(('rep', 'grp', 'ep')), parts along dimension 0, may hold values from -8 to 8
- down_latent: bfloat16 [4096, 1024], P('ep'), may hold values from -0.09375 to 0.09375
- gate_weight: bfloat16 [16, 1024, 2048], P(('grp', 'ep')), may hold values from -0.1875 to 0.1875
- up_weight: bfloat16 [16, 1024, 2048], P(('grp', 'ep')), may hold values from -0.1875 to 0.1875
- out_weight: bfloat16 [16, 2048, 1024], P(('grp', 'ep')), may hold values from -0.125 to 0.125
- up_latent: bfloat16 [1024, 4096], P(None, 'ep'), may hold values from -0.1875 to 0.1875
Outputs:
- layer_out: bfloat16 [4096, 4096], P(('rep', 'grp', 'ep')), parts along dimension 0
There are 2 independent parts, one for each index of `rep`. A program takes and returns all parts, laid end to end along the dimension named above; an argument that names none is the same for every part. Nothing has to cross between parts.
Inputs may be any that keep to these rules, and one draw needn't show every extreme that they name: `expert_ids`: each token names 8 different experts. Among the 128 tokens of one device no expert is named more than 128 times, and in every draw some expert is named exactly 128 times there.
All inputs are finite; a program needn't handle non-finite values.
Results may differ from a plain program's by a relative error of at most 0.014.
Values may be sent and summed in bfloat16 or wider, within the bound.
No kernel may reach another device: no remote copies, remote signals or barrier semaphores. Data moves between devices by JAX's collectives and lax.ppermute only.
A program may use at most 128 MiB of HBM per device.

v0:
```python
import jax
import jax.numpy as jnp
from jax import lax
from jax.sharding import PartitionSpec as P

route_scale = 2.5


def expert_apply(arrived, gate_weight, up_weight, out_weight):
    gate_value = jnp.einsum(
        "sekl,elh->sekh", arrived, gate_weight, preferred_element_type=jnp.float32
    )
    up_value = jnp.einsum("sekl,elh->sekh", arrived, up_weight, preferred_element_type=jnp.float32)
    hidden = (jax.nn.silu(gate_value) * up_value).astype(jnp.bfloat16)
    return jnp.einsum(
        "sekh,ehl->sekl", hidden, out_weight, preferred_element_type=jnp.float32
    ).astype(jnp.bfloat16)


def slot_ranks(targets, valid, slot_width):
    onehot = (
        (targets[:, None] == jnp.arange(slot_width, dtype=jnp.int32)[None, :]) & valid[:, None]
    ).astype(jnp.int32)
    before = jnp.cumsum(onehot, axis=0) - onehot
    return jnp.sum(before * onehot, axis=1)


def group_sums(routes, weights, replies, per_group, group_list):
    route_owner = routes // per_group
    answers = replies.astype(jnp.float32)
    group_terms = []
    for group_index in group_list:
        scaled = jnp.where(route_owner == group_index, weights.astype(jnp.float32), 0.0)
        group_terms.append(jnp.sum(scaled[:, :, None] * answers, axis=1))
    return jnp.stack(group_terms, axis=1)


def body(
    tokens, expert_ids, route_scores, down_latent, gate_weight, up_weight, out_weight, up_latent
):
    group_count = lax.axis_size("grp")
    ep_count = lax.axis_size("ep")
    per_device = gate_weight.shape[0]
    per_group = ep_count * per_device
    expert_count = group_count * per_group
    token_count, route_count = expert_ids.shape
    capacity = 2 * token_count * route_count // expert_count
    latent_width = down_latent.shape[1]
    latent = jnp.dot(
        tokens,
        lax.all_gather(down_latent, "ep", axis=0, tiled=True),
        preferred_element_type=jnp.float32,
    ).astype(jnp.bfloat16)
    sigmoids = jax.nn.sigmoid(route_scores)
    weights = (route_scale * sigmoids / jnp.sum(sigmoids, axis=1, keepdims=True)).astype(
        jnp.bfloat16
    )
    flat_ids = expert_ids.reshape(-1)
    all_valid = jnp.ones(flat_ids.shape, bool)
    slot_index = slot_ranks(flat_ids, all_valid, expert_count)
    target = flat_ids * capacity + slot_index
    source_row = jnp.arange(flat_ids.shape[0], dtype=jnp.int32) // route_count
    total_slots = expert_count * capacity
    row_of_slot = jnp.zeros((total_slots,), jnp.int32).at[target].set(source_row)
    filled = jnp.zeros((total_slots,), bool).at[target].set(True)
    outgoing = jnp.where(filled[:, None], latent[row_of_slot], jnp.zeros((), jnp.bfloat16))
    outgoing = outgoing.reshape(group_count * ep_count, per_device, capacity, latent_width)
    returned = lax.all_to_all(
        expert_apply(
            lax.all_to_all(outgoing, ("grp", "ep"), split_axis=0, concat_axis=0, tiled=True),
            gate_weight,
            up_weight,
            out_weight,
        ),
        ("grp", "ep"),
        split_axis=0,
        concat_axis=0,
        tiled=True,
    )
    replies = returned.reshape(total_slots, latent_width)[target].reshape(
        token_count, route_count, latent_width
    )
    owner_sums = group_sums(expert_ids, weights, replies, per_group, range(group_count))
    rounded = lax.optimization_barrier(owner_sums.astype(jnp.bfloat16))
    combined = jnp.sum(rounded.astype(jnp.float32), axis=1).astype(jnp.bfloat16)
    return jnp.dot(
        combined,
        lax.all_gather(up_latent, "ep", axis=1, tiled=True),
        preferred_element_type=jnp.float32,
    ).astype(jnp.bfloat16)


def solution(mesh):
    in_specs = (
        P(("rep", "grp", "ep"), None),
        P(("rep", "grp", "ep"), None),
        P(("rep", "grp", "ep"), None),
        P("ep", None),
        P(("grp", "ep"), None, None),
        P(("grp", "ep"), None, None),
        P(("grp", "ep"), None, None),
        P(None, "ep"),
    )
    out_specs = P(("rep", "grp", "ep"), None)
    return jax.shard_map(body, mesh=mesh, in_specs=in_specs, out_specs=out_specs, check_vma=False)
```

profile of v0, /device:TPU:0, one launch (start us, length us, event | category | flops | bytes accessed | tf_op | source)
XLA Modules:
  0.0 481.3 jit_solution(7701832104516286773)
XLA Ops:
  6.5 0.0 copy-start
  6.5 0.0 all-gather.3.cloned.1.call-start
  6.5 0.7 all-gather.3.cloned.1.call-update
  7.3 0.8 copy.22
  8.0 0.1 eq.38
  8.1 0.1 eq.34
  8.2 4.5 reduce-window.6
  12.8 0.1 slice.12
  12.8 0.1 copy.24
  13.0 0.1 copy.25
  13.1 0.7 broadcast_multiply_fusion
  13.8 0.1 copy.21
  13.9 0.1 mul.53
  14.0 0.1 broadcast_add_fusion
  14.1 4.3 scatter_custom_fusion.1
  18.5 4.3 scatter_custom_fusion
  22.8 114.3 %all-gather.3.cloned.1.call-done = bf16[4096,1024]{1,0:T(8,128)(2,1)} async-done(((bf16[512,1024]{1,0:T(8,128)(2,1)}), bf16[4096,1024]{1,0:T(8,128)(2,1)}) %all-gather.3.cloned.1.call-update) | async-done | bytes 8388624 | tf_op jit(solution)/shard_map/all_gather | solution.py:51
  137.2 0.0 copy-done
  137.2 4.6 convolution_convert_fusion.1
  141.8 9.7 %gather_fusion = bf16[2048,1024]{1,0:T(8,128)(2,1)} fusion(bf16[128,1024]{1,0:T(8,128)(2,1)S(1)} %convolution_convert_fusion.1, s32[2048]{0:T(1024)S(1)} %fusion.31), kind=kCustom, calls=%fused_computation | custom fusion | bytes 8396800 | tf_op jit(solution)/shard_map/gather | solution.py:66
  151.5 3.7 broadcast_select_fusion
  155.2 4.5 all-to-all-start
  159.8 0.2 all-gather.5.cloned.1.call-start
  160.0 0.5 all-gather.5.cloned.1.call-update
  160.5 154.5 %all-to-all-done = bf16[16,1,128,1024]{3,2,1,0:T(8,128)(2,1)} async-done(((bf16[16,1,128,1024]{3,2,1,0:T(8,128)(2,1)}), bf16[16,1,128,1024]{3,2,1,0:T(8,128)(2,1)}, u32[]{:S(2)}, u32[]{:S(2)}) %all-to-all-start) | async-done | bytes 4194336 | tf_op jit(solution)/shard_map/all_to_all | solution.py:70
  315.0 15.1 %fusion.14 = f32[16,128,2048]{2,1,0:T(8,128)} fusion(bf16[1,1024,2048]{2,1,0:T(8,128)(2,1)} %param.12, bf16[16,1,128,1024]{3,2,1,0:T(8,128)(2,1)} %all-to-all-done), kind=kOutput, calls=%fused_computation.21 | convolution fusion | flops 8589934592 | bytes 25165824 | tf_op jit(solution)/shard_map/sekl,elh->sekh/dot_general | solution.py:10
  330.1 25.5 %convert_bitcast_fusion = bf16[16,1,128,1024]{3,2,1,0:T(8,128)(2,1)} fusion(bf16[1,2048,1024]{2,1,0:T(8,128)(2,1)} %param.14, f32[16,128,2048]{2,1,0:T(8,128)} %fusion.14, bf16[1,1024,2048]{2,1,0:T(8,128)(2,1)} %param.13, bf16[16,1,128,1024]{3,2,1,0:T(8,128)(2,1)} %all-to-all-done), kind=kOutput, calls=%fused_computation.25 | convolution fusion | flops 17207132160 | bytes 33554432 | tf_op jit(solution)/shard_map/sekh,ehl->sekl/dot_general | solution.py:15
  355.6 0.0 copy-start.3
  355.6 0.0 copy-start.2
  355.6 12.9 %all-to-all-start.1 = ((bf16[16,1,128,1024]{3,2,1,0:T(8,128)(2,1)}), bf16[16,1,128,1024]{3,2,1,0:T(8,128)(2,1)}, u32[]{:S(2)}, u32[]{:S(2)}) async-start(bf16[16,1,128,1024]{3,2,1,0:T(8,128)(2,1)} %convert_bitcast_fusion), calls=%async_computation.1 | async-start | bytes 8388608 | tf_op jit(solution)/shard_map/all_to_all | solution.py:68
  368.5 0.0 copy-done.3
  368.5 0.0 copy-done.2
  368.6 0.1 copy.20
  368.7 0.1 copy.28
  368.8 89.5 %all-to-all-done.1 = bf16[16,1,128,1024]{3,2,1,0:T(8,128)(2,1)} async-done(((bf16[16,1,128,1024]{3,2,1,0:T(8,128)(2,1)}), bf16[16,1,128,1024]{3,2,1,0:T(8,128)(2,1)}, u32[]{:S(2)}, u32[]{:S(2)}) %all-to-all-start.1) | async-done | bytes 4194336 | tf_op jit(solution)/shard_map/all_to_all | solution.py:68
  458.3 7.7 %gather_fusion.1 = bf16[1024,1024]{1,0:T(8,128)(2,1)S(1)} fusion(bf16[2048,1024]{1,0:T(8,128)(2,1)} %bitcast.27, s32[1024]{0:T(1024)S(1)} %broadcast_clamp_fusion), kind=kCustom, calls=%fused_computation.1 | custom fusion | bytes 4198400 | tf_op jit(solution)/shard_map/gather | solution.py:80
  466.0 2.5 fusion.9
  468.5 0.1 pad_maximum_fusion
  468.6 0.0 copy-start.1
  468.6 0.1 reduce_sum.55
  468.7 0.0 all-gather.5.cloned.1.call-done
  468.7 5.7 %convolution_convert_fusion = bf16[128,4096]{1,0:T(8,128)(2,1)} fusion(bf16[128,1024]{1,0:T(8,128)(2,1)S(1)} %reduce_sum.55, bf16[1024,4096]{1,0:T(8,128)(2,1)} %all-gather.5.cloned.1.call-done), kind=kOutput, calls=%fused_computation.16 | convolution fusion | flops 1074266112 | bytes 9699328 | tf_op jit(solution)/shard_map/dot_general | solution.py:86
  474.4 0.0 copy-done.1
  (11 shorter events, 0.1 us)
Async XLA Ops:
  6.5 130.6 %copy-start = (bf16[128,4096]{1,0:T(8,128)(2,1)S(1)}, bf16[128,4096]{1,0:T(8,128)(2,1)}, u32[]{:S(2)}) copy-start(bf16[128,4096]{1,0:T(8,128)(2,1)} %param.8) | copy-start | bytes 3145732
  6.5 130.6 %all-gather.3.cloned.1.call-start = ((), (), s32[]{:S(2)}) async-start(), calls=%async_computation.2 | async-start | bytes 9437184 | tf_op jit(solution)/shard_map/all_gather | solution.py:51
  155.2 159.8 %all-to-all-start = ((bf16[16,1,128,1024]{3,2,1,0:T(8,128)(2,1)}), bf16[16,1,128,1024]{3,2,1,0:T(8,128)(2,1)}, u32[]{:S(2)}, u32[]{:S(2)}) async-start(bf16[16,1,128,1024]{3,2,1,0:T(8,128)(2,1)} %broadcast_select_fusion), calls=%async_computation | async-start | bytes 8388608 | tf_op jit(solution)/shard_map/all_to_all | solution.py:70
  159.8 308.9 %all-gather.5.cloned.1.call-start = ((), (), s32[]{:S(2)}) async-start(), calls=%async_computation.3 | async-start | bytes 9437184 | tf_op jit(solution)/shard_map/all_gather | solution.py:88
  355.6 12.9 %copy-start.3 = (f32[128,8]{0,1:T(8,128)S(1)}, f32[128,8]{0,1:T(8,128)}, u32[]{:S(2)}) copy-start(f32[128,8]{0,1:T(8,128)} %param.10) | copy-start | bytes 12292
  355.6 13.0 %copy-start.2 = (s32[128,8]{0,1:T(8,128)S(1)}, s32[128,8]{0,1:T(8,128)}, u32[]{:S(2)}) copy-start(s32[128,8]{0,1:T(8,128)} %param.9) | copy-start | bytes 12292
  355.6 102.7 %all-to-all-start.1 = ((bf16[16,1,128,1024]{3,2,1,0:T(8,128)(2,1)}), bf16[16,1,128,1024]{3,2,1,0:T(8,128)(2,1)}, u32[]{:S(2)}, u32[]{:S(2)}) async-start(bf16[16,1,128,1024]{3,2,1,0:T(8,128)(2,1)} %convert_bitcast_fusion), calls=%async_computation.1 | async-start | bytes 8388608 | tf_op jit(solution)/shard_map/all_to_all | solution.py:68
  468.6 5.8 %copy-start.1 = (bf16[128,4096]{1,0:T(8,128)(2,1)S(1)}, bf16[128,4096]{1,0:T(8,128)(2,1)}, u32[]{:S(2)}) copy-start(bf16[128,4096]{1,0:T(8,128)(2,1)} %param.8) | copy-start | bytes 3145732
Sparse Core Ops, SparseCore 0:
  9.5 127.6 all-gather.2
  162.7 192.9 all-gather.4
where the time goes:
time: 484 us; the launch traced here: 481 us
  waiting for transfers between devices  360 us (74%)
  matrix products  50.9 us (11%)
  local copies, waits for them, and re-layouts  27.7 us (6%)
  starting transfers between devices  17.7 us (4%)
  between operations  13.6 us (3%)
  other arithmetic  11.8 us (2%)
    all_to_all x1, waiting for transfers between devices, body(): lax.all_to_all(outgoing, ('grp', 'ep'), split_axis=0, concat_axis=0, tile...  154 us
    all_gather x1, waiting for transfers between devices, body(): lax.all_gather(down_latent, 'ep', axis=0, tiled=True)  114 us
    all_to_all x1, waiting for transfers between devices, body(): lax.all_to_all(expert_apply(lax.all_to_all(outgoing, ('grp', 'ep'), split...  89.5 us
    dot_general x1, matrix products, expert_apply(): jnp.einsum('sekh,ehl->sekl', hidden, out_weight, preferred_element_type=j...  25.5 us
    dot_general x1, matrix products, expert_apply(): jnp.einsum('sekl,elh->sekh', arrived, gate_weight, preferred_element_type...  15.1 us
    all_to_all x1, starting transfers between devices, body(): lax.all_to_all(expert_apply(lax.all_to_all(outgoing, ('grp', 'ep'), split...  12.9 us
  transfers between devices with their start and end apart: 4, of which 3 were waited for; matrix products, arithmetic and copies ran while one was open for 14% of the time, Pallas kernels for 0%

commit v1 on v0

v1 whole, which is shorter than its diff:
```python
import jax
import jax.numpy as jnp
from jax import lax
from jax.sharding import PartitionSpec as P

route_scale = 2.5


def swap_cores(array):
    return lax.ppermute(array, "grp", [(0, 1), (1, 0)])


def dense_weights(expert_ids, route_scores, expert_count):
    sigmoids = jax.nn.sigmoid(route_scores)
    weights = (route_scale * sigmoids / jnp.sum(sigmoids, axis=1, keepdims=True)).astype(
        jnp.bfloat16
    )
    named = expert_ids[:, :, None] == jnp.arange(expert_count, dtype=jnp.int32)[None, None, :]
    return jnp.sum(jnp.where(named, weights.astype(jnp.float32)[:, :, None], 0.0), axis=1)


def expert_apply(rows, scale, gate_weight, up_weight, out_weight):
    gate_value = jnp.dot(rows, gate_weight, preferred_element_type=jnp.float32)
    up_value = jnp.dot(rows, up_weight, preferred_element_type=jnp.float32)
    hidden = (jax.nn.silu(gate_value) * up_value).astype(jnp.bfloat16)
    out = jnp.dot(hidden, out_weight, preferred_element_type=jnp.float32)
    return (out * scale).astype(jnp.bfloat16)


def body(
    tokens, expert_ids, route_scores, down_latent, gate_weight, up_weight, out_weight, up_latent
):
    group_count = lax.axis_size("grp")
    ep_count = lax.axis_size("ep")
    expert_count = group_count * ep_count * gate_weight.shape[0]
    group = lax.axis_index("grp")
    token_count = tokens.shape[0]
    latent_width = down_latent.shape[1]

    half = down_latent.shape[0] // 2
    own_down = lax.all_gather(
        lax.dynamic_slice_in_dim(down_latent, group * half, half, 0), "ep", axis=0, tiled=True
    )
    other_down = swap_cores(own_down)

    weights = dense_weights(expert_ids, route_scores, expert_count)
    weights = lax.all_gather(weights, ("grp", "ep"), axis=0, tiled=True)
    expert = group * ep_count + lax.axis_index("ep")
    scale = lax.dynamic_slice_in_dim(weights, expert, 1, 1)
    scale = scale.reshape(group_count, ep_count * token_count, 1)
    own_scale = lax.dynamic_index_in_dim(scale, group, 0, keepdims=False)
    other_scale = lax.dynamic_index_in_dim(scale, 1 - group, 0, keepdims=False)

    halves = tokens.reshape(token_count, ep_count, 2, half)
    own_tokens = lax.dynamic_index_in_dim(halves, group, 2, keepdims=False)
    other_tokens = lax.dynamic_index_in_dim(halves, 1 - group, 2, keepdims=False)
    latent = jnp.dot(
        own_tokens.reshape(token_count, -1), own_down, preferred_element_type=jnp.float32
    ) + jnp.dot(
        other_tokens.reshape(token_count, -1), other_down, preferred_element_type=jnp.float32
    )
    own_rows = lax.all_gather(latent.astype(jnp.bfloat16), "ep", axis=0, tiled=True)
    other_rows = swap_cores(own_rows)

    own_part = expert_apply(own_rows, own_scale, gate_weight[0], up_weight[0], out_weight[0])
    other_part = expert_apply(other_rows, other_scale, gate_weight[0], up_weight[0], out_weight[0])
    both = (own_part.astype(jnp.float32) + swap_cores(other_part).astype(jnp.float32)).astype(
        jnp.bfloat16
    )
    combined = lax.psum_scatter(both, "ep", scatter_dimension=0, tiled=True)

    width = up_latent.shape[1] // 2
    own_up = lax.all_gather(
        lax.dynamic_slice_in_dim(up_latent, group * width, width, 1), "ep", axis=0
    )
    other_up = swap_cores(own_up)
    own_out = jnp.einsum(
        "tl,elw->tew", combined, own_up, preferred_element_type=jnp.float32
    ).astype(jnp.bfloat16)
    other_out = jnp.einsum(
        "tl,elw->tew", combined, other_up, preferred_element_type=jnp.float32
    ).astype(jnp.bfloat16)
    first = jnp.where(group == 0, own_out, other_out)
    second = jnp.where(group == 0, other_out, own_out)
    return jnp.stack([first, second], axis=2).reshape(token_count, -1)


def solution(mesh):
    in_specs = (
        P(("rep", "grp", "ep"), None),
        P(("rep", "grp", "ep"), None),
        P(("rep", "grp", "ep"), None),
        P("ep", None),
        P(("grp", "ep"), None, None),
        P(("grp", "ep"), None, None),
        P(("grp", "ep"), None, None),
        P(None, "ep"),
    )
    out_specs = P(("rep", "grp", "ep"), None)
    return jax.shard_map(body, mesh=mesh, in_specs=in_specs, out_specs=out_specs, check_vma=False)
```

time: 484 us -> 311 us (0.64)
  waiting for transfers between devices: 360 us -> 192 us
  blocking collectives: 0 us -> 32 us
  local copies, waits for them, and re-layouts: 27.7 us -> 6.63 us
  starting transfers between devices: 17.7 us -> 0.7 us
  matrix products: 50.9 us -> 66.2 us
  other arithmetic: 11.8 us -> 0.15 us
    all_to_all x2 -> x0, waiting for transfers between devices: 244 us -> none  [the longest x1 154 us: body(): lax.all_to_all(outgoing, ('grp', 'ep'), split_axis=0, concat_axis=0, tile...]
    reduce_scatter x0 -> x1, waiting for transfers between devices: none -> 64.6 us  [body(): combined = lax.psum_scatter(both, 'ep', scatter_dimension=0, tiled=True)]
    all_gather x0 -> x1, blocking collectives: none -> 32 us  [body(): weights = lax.all_gather(weights, ('grp', 'ep'), axis=0, tiled=True)]
    all_to_all x2 -> x0, starting transfers between devices: 17.5 us -> none  [the longest x1 12.9 us: body(): lax.all_to_all(expert_apply(lax.all_to_all(outgoing, ('grp', 'ep'), split...]
    gather x2 -> x0, local copies, waits for them, and re-layouts: 17.4 us -> none  [the longest x1 9.66 us: body(): latent[row_of_slot]]
    dot_general x4 -> x8, matrix products: 50.9 us -> 66.2 us  [the longest x2 33.8 us: expert_apply(): out = jnp.dot(hidden, out_weight, preferred_element_type=jnp.float32)]
    all_gather x2 -> x3, waiting for transfers between devices: 114 us -> 125 us  [the longest x1 77 us: body(): lax.all_gather(lax.dynamic_slice_in_dim(down_latent, group * half, half,...]
    scatter x2 -> x0, local copies, waits for them, and re-layouts: 8.66 us -> none  [the longest x1 4.34 us: body(): filled = jnp.zeros((total_slots,), bool).at[target].set(True)]
  transfers between devices with their start and end apart: 4 -> 8, of which waited for: 3 -> 4; matrix products, arithmetic and copies ran while one was open for 14% -> 20% of each run, Pallas kernels for 0% -> 0%
where the time goes in v1:
time: 311 us
  waiting for transfers between devices  192 us (62%)
  matrix products  66.2 us (21%)
  blocking collectives  32 us (10%)
  between operations  13.3 us (4%)
  local copies, waits for them, and re-layouts  6.63 us (2%)
    all_gather x1, waiting for transfers between devices, body(): lax.all_gather(lax.dynamic_slice_in_dim(down_latent, group * half, half,...  77 us
    reduce_scatter x1, waiting for transfers between devices, body(): combined = lax.psum_scatter(both, 'ep', scatter_dimension=0, tiled=True)  64.6 us
    all_gather x1, waiting for transfers between devices, body(): lax.all_gather(latent.astype(jnp.bfloat16), 'ep', axis=0, tiled=True)  47.6 us
    dot_general x2, matrix products, expert_apply(): out = jnp.dot(hidden, out_weight, preferred_element_type=jnp.float32)  33.8 us
    all_gather x1, blocking collectives, body(): weights = lax.all_gather(weights, ('grp', 'ep'), axis=0, tiled=True)  32 us
    dot_general x1, matrix products, expert_apply(): up_value = jnp.dot(rows, up_weight, preferred_element_type=jnp.float32)  11 us
    dot_general x1, matrix products, expert_apply(): gate_value = jnp.dot(rows, gate_weight, preferred_element_type=jnp.float32)  8.85 us
  transfers between devices with their start and end apart: 8, of which 4 were waited for; matrix products, arithmetic and copies ran while one was open for 20% of the time, Pallas kernels for 0%

profile of v1, /device:TPU:0, one launch (start us, length us, event | category | flops | bytes accessed | tf_op | source)
XLA Modules:
  0.0 311.2 jit_solution(5453552284818955520)
XLA Ops:
  6.5 0.0 copy-start
  6.5 0.0 all-gather.5.cloned.1.call-start
  6.5 1.2 copy-done
  7.8 0.8 constant_dynamic-slice_fusion.4
  8.6 0.0 all-gather.5.cloned.1.call-update
  8.6 0.0 all-gather.7.cloned.1.call-start
  8.7 77.0 %all-gather.5.cloned.1.call-done = bf16[2048,1024]{1,0:T(8,128)(2,1)} async-done(((bf16[256,1024]{1,0:T(8,128)(2,1)}), bf16[2048,1024]{1,0:T(8,128)(2,1)}) %all-gather.5.cloned.1.call-update) | async-done | bytes 4194320 | tf_op jit(solution)/shard_map/all_gather | solution.py:41
  85.6 0.0 collective-permute-start
  85.6 1.6 copy.20
  87.2 0.1 constant_dynamic-slice_fusion.3
  87.3 2.9 fusion.32
  90.3 0.0 copy-start.3
  90.3 0.0 copy-start.4
  90.3 0.0 copy-start.5
  90.3 2.8 collective-permute-done
  93.1 3.7 %fusion.17 = bf16[128,1024]{1,0:T(8,128)(2,1)} fusion(f32[128,1024]{1,0:T(8,128)S(1)} %fusion.32, bf16[128,2048]{0,1:T(8,128)(2,1)S(1)} %bitcast.60, bf16[2048,1024]{1,0:T(8,128)(2,1)} %collective-permute-done), kind=kOutput, calls=%fused_computation.19 | convolution fusion | flops 537133056 | bytes 5505024 | tf_op jit(solution)/shard_map/dot_general | solution.py:59
  96.8 0.0 all-gather.7.cloned.1.call-update
  96.8 0.0 all-gather.9.cloned.1.call-start
  96.9 47.6 %all-gather.7.cloned.1.call-done = bf16[1024,1024]{1,0:T(8,128)(2,1)} async-done(((bf16[128,1024]{1,0:T(8,128)(2,1)}), bf16[1024,1024]{1,0:T(8,128)(2,1)}) %all-gather.7.cloned.1.call-update) | async-done | bytes 2097168 | tf_op jit(solution)/shard_map/all_gather | solution.py:62
  144.5 0.0 collective-permute-start.1
  144.5 0.0 copy-done.3
  144.5 0.8 constant_dynamic-slice_fusion
  145.3 0.0 all-gather.9.cloned.1.call-update
  145.4 0.0 reduce-scatter.2.cloned.1.call-start
  145.4 0.0 copy-done.4
  145.5 0.0 copy-done.5
  145.5 32.0 %all_gather.17 = f32[2048,16]{0,1:T(8,128)S(1)} all-gather(f32[128,16]{0,1:T(8,128)S(1)} %select_reduce_fusion), channel_id=1, replica_groups=mesh['rep'=2,'grp'=2,'ep'=8] {'grp','ep'}, dimensions={0}, use_global_device_ids=true | all-gather | bytes 139264 | tf_op jit(solution)/shard_map/all_gather | solution.py:47
  177.6 0.0 collective-permute-done.1
  177.6 11.0 %fusion.4 = f32[1024,2048]{1,0:T(8,128)} fusion(bf16[1024,1024]{1,0:T(8,128)(2,1)} %collective-permute-done.1, bf16[1,1024,2048]{2,1,0:T(8,128)(2,1)} %param.13), kind=kOutput, calls=%fused_computation.6 | convolution fusion | flops 4294967296 | bytes 14680064 | tf_op jit(solution)/shard_map/dot_general | solution.py:24
  188.6 17.2 %multiply_convert_fusion.2 = bf16[1024,1024]{1,0:T(8,128)(2,1)} fusion(f32[1024]{0:T(1024)S(1)} %bitcast.62, bf16[1,2048,1024]{2,1,0:T(8,128)(2,1)} %param.14, f32[1024,2048]{1,0:T(8,128)} %fusion.4, bf16[1024,1024]{1,0:T(8,128)(2,1)} %collective-permute-done.1, bf16[1,1024,2048]{2,1,0:T(8,128)(2,1)} %param.12), kind=kOutput, calls=%fused_computation.14 | convolution fusion | flops 8604614656 | bytes 20975616 | tf_op jit(solution)/shard_map/dot_general | solution.py:26
  205.8 0.2 collective-permute-start.2
  206.0 0.0 copy-done.6
  206.0 8.8 %fusion.9 = f32[1024,2048]{1,0:T(8,128)} fusion(bf16[1024,1024]{1,0:T(8,128)(2,1)S(1)} %copy-done.6, bf16[1,1024,2048]{2,1,0:T(8,128)(2,1)} %param.12), kind=kOutput, calls=%fused_computation.11 | convolution fusion | flops 4294967296 | bytes 14680064 | tf_op jit(solution)/shard_map/dot_general | solution.py:23
  214.9 0.0 collective-permute-done.2
  214.9 16.6 %add_convert_fusion = bf16[1024,1024]{1,0:T(8,128)(2,1)} fusion(bf16[1024,1024]{1,0:T(8,128)(2,1)} %collective-permute-done.2, f32[1024]{0:T(1024)S(1)} %bitcast.61, bf16[1,2048,1024]{2,1,0:T(8,128)(2,1)} %param.14, f32[1024,2048]{1,0:T(8,128)} %fusion.9, bf16[1024,1024]{1,0:T(8,128)(2,1)S(1)} %copy-done.6, bf16[1,1024,2048]{2,1,0:T(8,128)(2,1)} %param.13), kind=kOutput, calls=%fused_computation.13 | convolution fusion | flops 8608808960 | bytes 23072768 | tf_op jit(solution)/shard_map/dot_general | solution.py:26
  231.4 0.0 reduce-scatter.2.cloned.1.call-update
  231.4 0.0 all-gather.9.cloned.1.call-done
  231.5 0.3 collective-permute-start.3
  231.8 64.6 %reduce-scatter.2.cloned.1.call-done = bf16[128,1024]{1,0:T(8,128)(2,1)} async-done(((bf16[1024,1024]{1,0:T(8,128)(2,1)}), bf16[128,1024]{1,0:T(8,128)(2,1)}) %reduce-scatter.2.cloned.1.call-update) | async-done | bytes 262160 | tf_op jit(solution)/shard_map/reduce_scatter | solution.py:70
  296.4 3.0 convolution_convert_fusion.1
  299.5 0.0 collective-permute-done.3
  299.5 0.0 copy-done.2
  299.5 0.0 copy-start.1
  299.5 3.0 select_bitcast_fusion.1
  302.5 0.1 pad_maximum_fusion
  302.6 0.7 copy.21
  303.3 1.3 copy.22
  304.6 0.0 copy-done.1
  (8 shorter events, 0.1 us)
Async XLA Ops:
  6.5 1.2 copy-start
  6.5 79.1 %all-gather.5.cloned.1.call-start = ((), (), s32[]{:S(2)}) async-start(), calls=%async_computation.1 | async-start | bytes 4718592 | tf_op jit(solution)/shard_map/all_gather | solution.py:41
  8.6 135.9 %all-gather.7.cloned.1.call-start = ((), (), s32[]{:S(2)}) async-start(), calls=%async_computation.2 | async-start | bytes 2359296 | tf_op jit(solution)/shard_map/all_gather | solution.py:62
  85.6 7.5 %collective-permute-start = (bf16[2048,1024]{1,0:T(8,128)(2,1)}, bf16[2048,1024]{1,0:T(8,128)(2,1)}, u32[]{:S(2)}, u32[]{:S(2)}) collective-permute-start(bf16[2048,1024]{1,0:T(8,128)(2,1)} %all-gather.5.cloned.1.call-done), channel_id=1, source_target_pairs={{0,8},{8,0},{1,9},{9,1},{2,10},{10,2},{3,11},{11,3},{4,12},{12,4},... | collective-permute-start | bytes 12582920 | tf_op jit(solution)/shard_map/ppermute | solution.py:10
  90.3 54.2 %copy-start.3 = (bf16[1024,512]{1,0:T(8,128)(2,1)S(1)}, bf16[1024,512]{1,0:T(8,128)(2,1)}, u32[]{:S(2)}) copy-start(bf16[1024,512]{1,0:T(8,128)(2,1)} %param.15) | copy-start | bytes 3145732
  90.3 55.1 %copy-start.4 = (f32[128,8]{0,1:T(8,128)S(1)}, f32[128,8]{0,1:T(8,128)}, u32[]{:S(2)}) copy-start(f32[128,8]{0,1:T(8,128)} %param.10) | copy-start | bytes 12292
  90.3 55.2 %copy-start.5 = (s32[128,8]{0,1:T(8,128)S(1)}, s32[128,8]{0,1:T(8,128)}, u32[]{:S(2)}) copy-start(s32[128,8]{0,1:T(8,128)} %param.9) | copy-start | bytes 12292
  96.8 134.7 %all-gather.9.cloned.1.call-start = ((), (), s32[]{:S(2)}) async-start(), calls=%async_computation.4 | async-start | bytes 4718592 | tf_op jit(solution)/shard_map/all_gather | solution.py:73
  144.5 33.1 %collective-permute-start.1 = (bf16[1024,1024]{1,0:T(8,128)(2,1)}, bf16[1024,1024]{1,0:T(8,128)(2,1)}, u32[]{:S(2)}, u32[]{:S(2)}) collective-permute-start(bf16[1024,1024]{1,0:T(8,128)(2,1)} %all-gather.7.cloned.1.call-done), channel_id=1, source_target_pairs={{0,8},{8,0},{1,9},{9,1},{2,10},{10,2},{3,11},{11,3},{4,12},{12,4},... | collective-permute-start | bytes 6291464 | tf_op jit(solution)/shard_map/ppermute | solution.py:10
  145.4 151.1 %reduce-scatter.2.cloned.1.call-start = ((), (), s32[]{:S(2)}) async-start(), calls=%async_computation.3 | async-start | bytes 2359296 | tf_op jit(solution)/shard_map/reduce_scatter | solution.py:70
  188.5 17.5 %copy-start.6 = (bf16[1024,1024]{1,0:T(8,128)(2,1)S(1)}, bf16[1024,1024]{1,0:T(8,128)(2,1)}, u32[]{:S(2)}) copy-start(bf16[1024,1024]{1,0:T(8,128)(2,1)} %all-gather.7.cloned.1.call-done) | copy-start | bytes 6291460
  205.8 9.1 %collective-permute-start.2 = (bf16[1024,1024]{1,0:T(8,128)(2,1)}, bf16[1024,1024]{1,0:T(8,128)(2,1)}, u32[]{:S(2)}, u32[]{:S(2)}) collective-permute-start(bf16[1024,1024]{1,0:T(8,128)(2,1)} %multiply_convert_fusion.2), channel_id=1, source_target_pairs={{0,8},{8,0},{1,9},{9,1},{2,10},{10,2},{3,11},{11,3},{4,12},{12,4},... | collective-permute-start | bytes 6291464 | tf_op jit(solution)/shard_map/ppermute | solution.py:10
  231.5 68.0 %collective-permute-start.3 = (bf16[8,1024,256]{2,1,0:T(8,128)(2,1)}, bf16[8,1024,256]{2,1,0:T(8,128)(2,1)}, u32[]{:S(2)}, u32[]{:S(2)}) collective-permute-start(bf16[8,1024,256]{2,1,0:T(8,128)(2,1)} %bitcast.55), channel_id=1, source_target_pairs={{0,8},{8,0},{1,9},{9,1},{2,10},{10,2},{3,11},{11,3},{4,12},{12,4},... | collective-permute-start | bytes 12582920 | tf_op jit(solution)/shard_map/ppermute | solution.py:10
  296.4 3.0 copy-start.2
  299.5 5.1 %copy-start.1 = (bf16[512,1024]{1,0:T(8,128)(2,1)S(1)}, bf16[512,1024]{1,0:T(8,128)(2,1)}, u32[]{:S(2)}) copy-start(bf16[512,1024]{1,0:T(8,128)(2,1)} %param.11) | copy-start | bytes 3145732
Sparse Core Ops, SparseCore 0:
  9.5 76.0 all-gather.4
  96.9 47.5 all-gather.6
  146.6 72.7 all-gather.8
  231.6 64.8 reduce-scatter.1

commit v2 on v1

v2 whole, which is shorter than its diff:
```python
import functools

import jax
import jax.numpy as jnp
from jax import lax
from jax.experimental import pallas as pl
from jax.experimental.pallas import tpu as pltpu
from jax.sharding import PartitionSpec as P

route_scale = 2.5


def swap_cores(array):
    return lax.ppermute(array, "grp", [(0, 1), (1, 0)])


def swap_reps(array):
    return lax.ppermute(array, "rep", [(i, i ^ 1) for i in range(lax.axis_size("rep"))])


def swap_ep(array, mask):
    return lax.ppermute(array, "ep", [(i, i ^ mask) for i in range(lax.axis_size("ep"))])


def gather_ep(piece):
    along = [piece] + [swap_ep(piece, 2 * k) for k in range(1, lax.axis_size("ep") // 2)]
    return [(near, swap_ep(near, 1)) for near in along]


def dense_weights(expert_ids, route_scores, expert_count):
    sigmoids = jax.nn.sigmoid(route_scores)
    weights = (route_scale * sigmoids / jnp.sum(sigmoids, axis=1, keepdims=True)).astype(
        jnp.bfloat16
    )
    named = expert_ids[None, :, :] == jnp.arange(expert_count, dtype=jnp.int32)[:, None, None]
    return jnp.sum(jnp.where(named, weights.astype(jnp.float32)[None, :, :], 0.0), axis=2)


def expert_kernel(
    steps, near, far, other, scale, gate, up, out, own_sum, other_sum, rows, total
):
    step = pl.program_id(0)
    count = near.shape[0]

    @pl.when(step == 0)
    def _():
        rows[:count] = near[...]
        rows[count : 2 * count] = far[...]
        rows[2 * count :] = other[...]
        total[...] = jnp.zeros_like(total)

    width = 256
    for start in range(0, gate.shape[2], width):
        columns = slice(start, start + width)
        gate_value = jnp.dot(rows[...], gate[0, :, columns], preferred_element_type=jnp.float32)
        up_value = jnp.dot(rows[...], up[0, :, columns], preferred_element_type=jnp.float32)
        hidden = gate_value / (1.0 + jnp.exp(-gate_value)) * up_value
        total[...] += jnp.dot(
            hidden.astype(jnp.bfloat16), out[0, columns, :], preferred_element_type=jnp.float32
        )

    @pl.when(step == steps - 1)
    def _():
        factor = scale[:, :1]
        own_sum[...] = (total[: 2 * count] * factor[: 2 * count]).astype(jnp.bfloat16)
        other_sum[...] = (total[2 * count :] * factor[2 * count :]).astype(jnp.bfloat16)


def expert_apply(near, far, other, scale, gate_weight, up_weight, out_weight):
    count, latent_width = near.shape
    hidden_width = gate_weight.shape[2]
    block = 512
    steps = hidden_width // block
    whole = lambda array: pl.BlockSpec(array.shape, lambda i: (0,) * array.ndim)
    sums = jax.ShapeDtypeStruct((2 * count, latent_width), jnp.bfloat16)
    return pl.pallas_call(
        functools.partial(expert_kernel, steps),
        grid=(steps,),
        out_shape=(sums, sums),
        in_specs=[
            whole(near),
            whole(far),
            whole(other),
            whole(scale),
            pl.BlockSpec((1, latent_width, block), lambda i: (0, 0, i)),
            pl.BlockSpec((1, latent_width, block), lambda i: (0, 0, i)),
            pl.BlockSpec((1, block, latent_width), lambda i: (0, i, 0)),
        ],
        out_specs=(whole(sums), whole(sums)),
        scratch_shapes=[
            pltpu.VMEM((4 * count, latent_width), jnp.bfloat16),
            pltpu.VMEM((4 * count, latent_width), jnp.float32),
        ],
        compiler_params=pltpu.CompilerParams(vmem_limit_bytes=40 * 1024 * 1024),
        cost_estimate=pl.CostEstimate(
            flops=24 * count * latent_width * hidden_width,
            bytes_accessed=6 * latent_width * hidden_width,
            transcendentals=4 * count * hidden_width,
        ),
        name="expert",
    )(near, far, other, scale, gate_weight, up_weight, out_weight)


def body(
    tokens, expert_ids, route_scores, down_latent, gate_weight, up_weight, out_weight, up_latent
):
    group_count = lax.axis_size("grp")
    ep_count = lax.axis_size("ep")
    expert_count = group_count * ep_count * gate_weight.shape[0]
    group = lax.axis_index("grp")
    place = lax.axis_index("ep")
    side = lax.axis_index("rep") % 2
    token_count = tokens.shape[0]
    latent_width = down_latent.shape[1]
    pieces = ep_count // 2

    quarter = down_latent.shape[0] // 4
    down_piece = lax.dynamic_slice_in_dim(down_latent, (2 * side + group) * quarter, quarter, 0)
    down_pieces = gather_ep(down_piece)
    cut = tokens.reshape(token_count, ep_count, 2, 2 * quarter)
    kept = lax.dynamic_index_in_dim(cut, side, 2, keepdims=False)
    given = lax.dynamic_index_in_dim(cut, 1 - side, 2, keepdims=False)
    inner = jnp.concatenate([kept, swap_reps(given)], axis=0)
    inner = inner.reshape(2 * token_count, ep_count, 2, quarter).transpose(1, 2, 0, 3)

    def columns(core, k):
        parts = [
            lax.dynamic_slice(
                inner, (place ^ (2 * k + y), core, 0, 0), (1, 1, 2 * token_count, quarter)
            )[0, 0]
            for y in range(2)
        ]
        return jnp.concatenate(parts, axis=1)

    partial = jnp.zeros((2 * token_count, latent_width), jnp.float32)
    for k, (near, far) in enumerate(down_pieces):
        both = jnp.concatenate([near, far], axis=0)
        swapped = swap_cores(both)
        partial += jnp.dot(columns(group, k), both, preferred_element_type=jnp.float32)
        partial += jnp.dot(columns(1 - group, k), swapped, preferred_element_type=jnp.float32)
    arrived = swap_reps(partial[token_count:].astype(jnp.bfloat16))
    latent = (partial[:token_count] + arrived.astype(jnp.float32)).astype(jnp.bfloat16)

    weights = dense_weights(expert_ids, route_scores, expert_count)
    scale = lax.all_to_all(weights, ("grp", "ep"), split_axis=0, concat_axis=0, tiled=True)
    scale = scale.reshape(group_count, ep_count, token_count)

    def scale_of(k):
        rows = [
            lax.dynamic_slice(scale, (core, place ^ (2 * k + y), 0), (1, 1, token_count))
            for core in (group, 1 - group)
            for y in range(2)
        ]
        rows = jnp.concatenate(rows, axis=0).reshape(4 * token_count, 1)
        return jnp.broadcast_to(rows, (4 * token_count, 128))

    latent_pieces = gather_ep(latent)
    combined = jnp.zeros((token_count, latent_width), jnp.float32)
    for k, (near, far) in enumerate(latent_pieces):
        other = swap_cores(jnp.concatenate([near, far], axis=0))
        own_sum, other_sum = expert_apply(
            near, far, other, scale_of(k), gate_weight, up_weight, out_weight
        )
        chip = own_sum.astype(jnp.float32) + swap_cores(other_sum).astype(jnp.float32)
        away = swap_ep(chip[token_count:].astype(jnp.bfloat16), 1)
        pair = chip[:token_count] + away.astype(jnp.float32)
        if k == 0:
            combined += pair
        else:
            combined += swap_ep(pair.astype(jnp.bfloat16), 2 * k).astype(jnp.float32)
    combined = combined.astype(jnp.bfloat16)

    inner_quarter = latent_width // 4
    up_piece = lax.dynamic_slice_in_dim(
        up_latent, (2 * side + group) * inner_quarter, inner_quarter, 0
    )
    mine = lax.all_gather(up_piece, "ep", axis=0)
    across = swap_reps(mine)
    layer_out = 0.0
    for array, side_of, core_of in (
        (mine, side, group),
        (across, 1 - side, group),
        (swap_cores(mine), side, 1 - group),
        (swap_cores(across), 1 - side, 1 - group),
    ):
        part = lax.dynamic_slice_in_dim(
            combined, (2 * side_of + core_of) * inner_quarter, inner_quarter, 1
        )
        layer_out += jnp.einsum("tl,elw->tew", part, array, preferred_element_type=jnp.float32)
    return layer_out.astype(jnp.bfloat16).reshape(token_count, -1)


def solution(mesh):
    in_specs = (
        P(("rep", "grp", "ep"), None),
        P(("rep", "grp", "ep"), None),
        P(("rep", "grp", "ep"), None),
        P("ep", None),
        P(("grp", "ep"), None, None),
        P(("grp", "ep"), None, None),
        P(("grp", "ep"), None, None),
        P(None, "ep"),
    )
    out_specs = P(("rep", "grp", "ep"), None)
    return jax.shard_map(body, mesh=mesh, in_specs=in_specs, out_specs=out_specs, check_vma=False)
```

time: 311 us -> 234 us (0.75)
  waiting for transfers between devices: 192 us -> 107 us
  matrix products: 66.2 us -> 10.9 us
  Pallas kernels: 0 us -> 39.6 us
  starting transfers between devices: 0.7 us -> 38.2 us
  blocking collectives: 32 us -> 0 us
  local copies, waits for them, and re-layouts: 6.63 us -> 16 us
  other arithmetic: 0.15 us -> 7.85 us
    all_gather x3 -> x1, waiting for transfers between devices: 125 us -> 0.01 us  [body(): mine = lax.all_gather(up_piece, 'ep', axis=0)]
    ppermute x0 -> x24, waiting for transfers between devices: none -> 94 us  [the longest x21 82.2 us: swap_ep(): lax.ppermute(array, 'ep', [(i, i ^ mask) for i in range(lax.axis_size('ep...]
    reduce_scatter x1 -> x0, waiting for transfers between devices: 64.6 us -> none  [body(): combined = lax.psum_scatter(both, 'ep', scatter_dimension=0, tiled=True)]
    dot_general x8 -> x12, matrix products: 66.2 us -> 10.9 us  [the longest x4 8.5 us: body(): jnp.einsum('tl,elw->tew', part, array, preferred_element_type=jnp.float32)]
    pallas_call x0 -> x4, Pallas kernels: none -> 39.6 us  [expert_apply(): pl.pallas_call(functools.partial(expert_kernel, steps), grid=(steps,), ou...]
    all_gather x1 -> x0, blocking collectives: 32 us -> none  [body(): weights = lax.all_gather(weights, ('grp', 'ep'), axis=0, tiled=True)]
    ppermute x0 -> x24, starting transfers between devices: none -> 30.5 us  [the longest x21 25.9 us: swap_ep(): lax.ppermute(array, 'ep', [(i, i ^ mask) for i in range(lax.axis_size('ep...]
    all_to_all x0 -> x1, waiting for transfers between devices: none -> 13 us  [body(): lax.all_to_all(weights, ('grp', 'ep'), split_axis=0, concat_axis=0, tiled...]
  transfers between devices with their start and end apart: 8 -> 40, of which waited for: 4 -> 14; matrix products, arithmetic and copies ran while one was open for 20% -> 10% of each run, Pallas kernels for 0% -> 17%
where the time goes in v2:
time: 234 us
  waiting for transfers between devices  107 us (46%)
  Pallas kernels  39.6 us (17%)
  starting transfers between devices  38.2 us (16%)
  local copies, waits for them, and re-layouts  16 us (7%)
  between operations  14.1 us (6%)
  matrix products  10.9 us (5%)
  other arithmetic  7.85 us (3%)
    ppermute x21, waiting for transfers between devices, swap_ep(): lax.ppermute(array, 'ep', [(i, i ^ mask) for i in range(lax.axis_size('ep...  82.2 us
    pallas_call x4, Pallas kernels, expert_apply(): pl.pallas_call(functools.partial(expert_kernel, steps), grid=(steps,), ou...  39.6 us
    ppermute x21, starting transfers between devices, swap_ep(): lax.ppermute(array, 'ep', [(i, i ^ mask) for i in range(lax.axis_size('ep...  25.9 us
    all_to_all x1, waiting for transfers between devices, body(): lax.all_to_all(weights, ('grp', 'ep'), split_axis=0, concat_axis=0, tiled...  13 us
    ppermute x3, waiting for transfers between devices, swap_reps(): lax.ppermute(array, 'rep', [(i, i ^ 1) for i in range(lax.axis_size('rep'...  11.8 us
    unnamed x30, local copies, waits for them, and re-layouts  10.7 us
    dot_general x4, matrix products, body(): jnp.einsum('tl,elw->tew', part, array, preferred_element_type=jnp.float32)  8.5 us
    all_to_all x1, starting transfers between devices, body(): lax.all_to_all(weights, ('grp', 'ep'), split_axis=0, concat_axis=0, tiled...  5.62 us
  transfers between devices with their start and end apart: 40, of which 14 were waited for; matrix products, arithmetic and copies ran while one was open for 10% of the time, Pallas kernels for 17%

profile of v2, /device:TPU:0, one launch (start us, length us, event | category | flops | bytes accessed | tf_op | source)
XLA Modules:
  0.0 233.7 jit_solution(5835147742107282460)
XLA Ops:
  6.5 1.2 copy-done
  7.8 3.0 %collective-permute-start.1 = (bf16[128,1024]{1,0:T(8,128)(2,1)S(1)}, bf16[128,1024]{1,0:T(8,128)(2,1)S(1)}, u32[]{:S(2)}, u32[]{:S(2)}) collective-permute-start(bf16[128,1024]{1,0:T(8,128)(2,1)S(1)} %constant_dynamic-slice_fusion.17), channel_id=1, source_target_pairs={{0,1},{1,0},{2,3},{3,2},{4,5},{5,4},{6,7},{7,6},{8,9},{9,8},{10,11... | collective-permute-start | bytes 786440 | tf_op jit(solution)/shard_map/ppermute | solution.py:22
  10.8 3.6 %collective-permute-start.9 = (bf16[128,1024]{1,0:T(8,128)(2,1)S(1)}, bf16[128,1024]{1,0:T(8,128)(2,1)}, u32[]{:S(2)}, u32[]{:S(2)}) collective-permute-start(bf16[128,1024]{1,0:T(8,128)(2,1)S(1)} %constant_dynamic-slice_fusion.17), channel_id=1, source_target_pairs={{0,6},{1,7},{2,4},{3,5},{4,2},{5,3},{6,0},{7,1},{8,14},{9,15},{10,... | collective-permute-start | bytes 786440 | tf_op jit(solution)/shard_map/ppermute | solution.py:22
  15.2 1.7 constant_dynamic-slice_fusion
  18.1 1.6 collective-permute-start
  20.2 1.8 collective-permute-done.9
  22.3 15.1 %collective-permute-done.3 = bf16[128,1024]{1,0:T(8,128)(2,1)S(1)} collective-permute-done((bf16[128,1024]{1,0:T(8,128)(2,1)S(1)}, bf16[128,1024]{1,0:T(8,128)(2,1)S(1)}, u32[]{:S(2)}, u32[]{:S(2)}) %collective-permute-start.3) | collective-permute-done | bytes 262176 | tf_op jit(solution)/shard_map/ppermute | solution.py:22
  37.4 7.6 %collective-permute-done.6 = bf16[128,1024]{1,0:T(8,128)(2,1)} collective-permute-done((bf16[128,1024]{1,0:T(8,128)(2,1)S(1)}, bf16[128,1024]{1,0:T(8,128)(2,1)}, u32[]{:S(2)}, u32[]{:S(2)}) %collective-permute-start.6) | collective-permute-done | bytes 262176 | tf_op jit(solution)/shard_map/ppermute | solution.py:22
  45.5 1.0 constant_dynamic-update-slice_fusion.3
  46.5 1.0 constant_dynamic-update-slice_fusion.5
  47.6 10.1 %collective-permute-done.7 = bf16[128,1024]{1,0:T(8,128)(2,1)S(1)} collective-permute-done((bf16[128,1024]{1,0:T(8,128)(2,1)}, bf16[128,1024]{1,0:T(8,128)(2,1)S(1)}, u32[]{:S(2)}, u32[]{:S(2)}) %collective-permute-start.7) | collective-permute-done | bytes 262176 | tf_op jit(solution)/shard_map/ppermute | solution.py:22
  63.5 1.6 collective-permute-start.12
  65.1 6.7 %collective-permute-done.12 = bf16[128,1024]{1,0:T(8,128)(2,1)S(1)} collective-permute-done((bf16[128,1024]{1,0:T(8,128)(2,1)S(1)}, bf16[128,1024]{1,0:T(8,128)(2,1)S(1)}, u32[]{:S(2)}, u32[]{:S(2)}) %collective-permute-start.12) | collective-permute-done | bytes 262176 | tf_op jit(solution)/shard_map/ppermute | solution.py:18
  73.1 4.2 %collective-permute-start.23 = (bf16[128,1024]{1,0:T(8,128)(2,1)S(1)}, bf16[128,1024]{1,0:T(8,128)(2,1)S(1)}, u32[]{:S(2)}, u32[]{:S(2)}) collective-permute-start(bf16[128,1024]{1,0:T(8,128)(2,1)S(1)} %fusion.10.near), channel_id=1, source_target_pairs={{0,4},{1,5},{2,6},{3,7},{4,0},{5,1},{6,2},{7,3},{8,12},{9,13},{10,... | collective-permute-start | bytes 786440 | tf_op jit(solution)/shard_map/ppermute | solution.py:22
  77.9 5.6 %all-to-all-start = ((f32[16,1,128]{2,1,0:T(1,128)}), f32[16,1,128]{2,1,0:T(1,128)S(1)}, u32[]{:S(2)}, u32[]{:S(2)}) async-start(f32[16,1,128]{2,1,0:T(1,128)} %bitcast.5), calls=%async_computation | async-start | bytes 16384 | tf_op jit(solution)/shard_map/all_to_all | solution.py:145
  83.5 2.0 collective-permute-start.17
  85.5 13.0 %all-to-all-done = f32[16,1,128]{2,1,0:T(1,128)S(1)} async-done(((f32[16,1,128]{2,1,0:T(1,128)}), f32[16,1,128]{2,1,0:T(1,128)S(1)}, u32[]{:S(2)}, u32[]{:S(2)}) %all-to-all-start) | async-done | bytes 8224 | tf_op jit(solution)/shard_map/all_to_all | solution.py:145
  98.5 1.3 collective-permute-start.30
  100.8 1.3 collective-permute-start.18
  102.1 5.6 %collective-permute-done.30.far = bf16[128,1024]{1,0:T(8,128)(2,1)S(1)} collective-permute-done((bf16[128,1024]{1,0:T(8,128)(2,1)S(1)}, bf16[128,1024]{1,0:T(8,128)(2,1)S(1)}, u32[]{:S(2)}, u32[]{:S(2)}) %collective-permute-start.30) | collective-permute-done | bytes 262176 | tf_op jit(solution)/shard_map/ppermute | solution.py:22
  107.9 5.5 %collective-permute-done.24.far = bf16[128,1024]{1,0:T(8,128)(2,1)S(1)} collective-permute-done((bf16[128,1024]{1,0:T(8,128)(2,1)S(1)}, bf16[128,1024]{1,0:T(8,128)(2,1)S(1)}, u32[]{:S(2)}, u32[]{:S(2)}) %collective-permute-start.24) | collective-permute-done | bytes 262176 | tf_op jit(solution)/shard_map/ppermute | solution.py:22
  114.2 3.7 %collective-permute-done.18.far = bf16[128,1024]{1,0:T(8,128)(2,1)S(1)} collective-permute-done((bf16[128,1024]{1,0:T(8,128)(2,1)S(1)}, bf16[128,1024]{1,0:T(8,128)(2,1)S(1)}, u32[]{:S(2)}, u32[]{:S(2)}) %collective-permute-start.18) | collective-permute-done | bytes 262176 | tf_op jit(solution)/shard_map/ppermute | solution.py:22
  117.9 0.9 pad_maximum_fusion.2
  118.9 2.2 copy-done.4
  121.1 10.2 %expert.4 = (bf16[256,1024]{1,0:T(8,128)(2,1)S(1)}, bf16[256,1024]{1,0:T(8,128)(2,1)}) custom-call(bf16[128,1024]{1,0:T(8,128)(2,1)S(1)} %fusion.10.near, bf16[128,1024]{1,0:T(8,128)(2,1)S(1)} %collective-permute-done.13.far, bf16[256,1024]{1,0:T(8,128)(2,1)S(1)} %collective-permute-done.14.other, f32[512,128]{1,0:T(8,128)S(1)} %broadcast_in_dim.47.scale, ...), custom_call_target="tpu_custom_call" | custom-call | flops 6442450944 | bytes 12582912 | tf_op jit(solution)/shard_map/expert/pallas_call | solution.py:76
  131.9 10.2 %expert.7 = (bf16[256,1024]{1,0:T(8,128)(2,1)S(1)}, bf16[256,1024]{1,0:T(8,128)(2,1)}) custom-call(bf16[128,1024]{1,0:T(8,128)(2,1)S(1)} %collective-permute-done.29.near, bf16[128,1024]{1,0:T(8,128)(2,1)S(1)} %collective-permute-done.30.far, bf16[256,1024]{1,0:T(8,128)(2,1)S(1)} %collective-permute-done.31.other, f32[512,128]{1,0:T(8,128)S(1)} %broadcast_in_dim.53.scale, ...), custom_call_target="tpu_custom_call" | custom-call | flops 6442450944 | bytes 12582912 | tf_op jit(solution)/shard_map/expert/pallas_call | solution.py:76
  142.1 1.5 collective-permute-start.35
  143.8 2.2 copy-done.3
  146.0 2.2 copy-done.5
  148.1 9.5 %expert.6 = (bf16[256,1024]{1,0:T(8,128)(2,1)S(1)}, bf16[256,1024]{1,0:T(8,128)(2,1)S(1)}) custom-call(bf16[128,1024]{1,0:T(8,128)(2,1)S(1)} %collective-permute-done.23.near, bf16[128,1024]{1,0:T(8,128)(2,1)S(1)} %collective-permute-done.24.far, bf16[256,1024]{1,0:T(8,128)(2,1)} %collective-permute-done.25.other, f32[512,128]{1,0:T(8,128)S(1)} %broadcast_in_dim.51.scale, ...), custom_call_target="tpu_custom_call" | custom-call | flops 6442450944 | bytes 12582912 | tf_op jit(solution)/shard_map/expert/pallas_call | solution.py:76
  158.1 9.6 %expert.5 = (bf16[256,1024]{1,0:T(8,128)(2,1)S(1)}, bf16[256,1024]{1,0:T(8,128)(2,1)S(1)}) custom-call(bf16[128,1024]{1,0:T(8,128)(2,1)S(1)} %collective-permute-done.17.near, bf16[128,1024]{1,0:T(8,128)(2,1)S(1)} %collective-permute-done.18.far, bf16[256,1024]{1,0:T(8,128)(2,1)S(1)} %collective-permute-done.19.other, ...), custom_call_target="tpu_custom_call" | custom-call | flops 6442450944 | bytes 12582912 | tf_op jit(solution)/shard_map/expert/pallas_call | solution.py:76
  168.1 1.2 convert_add_fusion.3
  169.4 1.3 collective-permute-start.16
  170.6 1.2 convert_add_fusion
  171.9 0.9 collective-permute-start.33
  173.0 1.3 collective-permute-start.27
  174.5 9.7 %collective-permute-done.33 = bf16[128,1024]{1,0:T(8,128)(2,1)S(1)} collective-permute-done((bf16[128,1024]{1,0:T(8,128)(2,1)S(1)}, bf16[128,1024]{1,0:T(8,128)(2,1)S(1)}, u32[]{:S(2)}, u32[]{:S(2)}) %collective-permute-start.33) | collective-permute-done | bytes 262176 | tf_op jit(solution)/shard_map/ppermute | solution.py:22
  184.2 1.2 collective-permute-start.21
  185.4 5.1 %collective-permute-done.35 = bf16[8,256,512]{2,1,0:T(8,128)(2,1)} collective-permute-done((bf16[8,256,512]{2,1,0:T(8,128)(2,1)}, bf16[8,256,512]{2,1,0:T(8,128)(2,1)}, u32[]{:S(2)}, u32[]{:S(2)}) %collective-permute-start.35) | collective-permute-done | bytes 2097184 | tf_op jit(solution)/shard_map/ppermute | solution.py:18
  191.5 3.3 %collective-permute-done.21 = bf16[128,1024]{1,0:T(8,128)(2,1)S(1)} collective-permute-done((bf16[128,1024]{1,0:T(8,128)(2,1)S(1)}, bf16[128,1024]{1,0:T(8,128)(2,1)S(1)}, u32[]{:S(2)}, u32[]{:S(2)}) %collective-permute-start.21) | collective-permute-done | bytes 262176 | tf_op jit(solution)/shard_map/ppermute | solution.py:22
  194.8 1.4 collective-permute-start.22
  196.2 5.4 %collective-permute-done.34 = bf16[128,1024]{1,0:T(8,128)(2,1)S(1)} collective-permute-done((bf16[128,1024]{1,0:T(8,128)(2,1)S(1)}, bf16[128,1024]{1,0:T(8,128)(2,1)S(1)}, u32[]{:S(2)}, u32[]{:S(2)}) %collective-permute-start.34) | collective-permute-done | bytes 262176 | tf_op jit(solution)/shard_map/ppermute | solution.py:22
  201.7 14.4 %collective-permute-done.28 = bf16[128,1024]{1,0:T(8,128)(2,1)S(1)} collective-permute-done((bf16[128,1024]{1,0:T(8,128)(2,1)S(1)}, bf16[128,1024]{1,0:T(8,128)(2,1)S(1)}, u32[]{:S(2)}, u32[]{:S(2)}) %collective-permute-start.28) | collective-permute-done | bytes 262176 | tf_op jit(solution)/shard_map/ppermute | solution.py:22
  216.3 2.0 fusion.60
  218.3 2.0 fusion.58
  220.4 2.0 fusion.56
  222.5 2.4 %add_convert_fusion = bf16[128,8,512]{2,0,1:T(8,128)(2,1)S(1)} fusion(f32[128,8,512]{2,0,1:T(8,128)S(1)} %fusion.56, f32[128,8,512]{2,0,1:T(8,128)S(1)} %fusion.60, f32[128,8,512]{2,0,1:T(8,128)S(1)} %fusion.58, bf16[8,256,512]{2,1,0:T(8,128)(2,1)} %collective-permute-done.37, bf16[128,1024]{1,0:T(8,128)(2,1)S(1)} %fusion.9, s32[]{:T(128)S(6)} %select_n.66), kind=kOutput, calls=%fused_computation.32 | convolution fusion | flops 270532608 | bytes 9502724 | tf_op jit(solution)/shard_map/tl,elw->tew/dot_general | solution.py:189
  225.5 1.3 copy.35
  (121 shorter events, 16.8 us)
Async XLA Ops:
  6.5 10.4 %copy-start.6 = (bf16[128,4096]{1,0:T(8,128)(2,1)S(1)}, bf16[128,4096]{1,0:T(8,128)(2,1)}, u32[]{:S(2)}) copy-start(bf16[128,4096]{1,0:T(8,128)(2,1)} %param.8) | copy-start | bytes 3145732
  6.5 135.6 %all-gather.3.cloned.1.call-start = ((), (), s32[]{:S(2)}) async-start(), calls=%async_computation.1 | async-start | bytes 2359296 | tf_op jit(solution)/shard_map/all_gather | solution.py:177
  7.8 12.3 %collective-permute-start.1 = (bf16[128,1024]{1,0:T(8,128)(2,1)S(1)}, bf16[128,1024]{1,0:T(8,128)(2,1)S(1)}, u32[]{:S(2)}, u32[]{:S(2)}) collective-permute-start(bf16[128,1024]{1,0:T(8,128)(2,1)S(1)} %constant_dynamic-slice_fusion.17), channel_id=1, source_target_pairs={{0,1},{1,0},{2,3},{3,2},{4,5},{5,4},{6,7},{7,6},{8,9},{9,8},{10,11... | collective-permute-start | bytes 786440 | tf_op jit(solution)/shard_map/ppermute | solution.py:22
  10.8 11.2 %collective-permute-start.9 = (bf16[128,1024]{1,0:T(8,128)(2,1)S(1)}, bf16[128,1024]{1,0:T(8,128)(2,1)}, u32[]{:S(2)}, u32[]{:S(2)}) collective-permute-start(bf16[128,1024]{1,0:T(8,128)(2,1)S(1)} %constant_dynamic-slice_fusion.17), channel_id=1, source_target_pairs={{0,6},{1,7},{2,4},{3,5},{4,2},{5,3},{6,0},{7,1},{8,14},{9,15},{10,... | collective-permute-start | bytes 786440 | tf_op jit(solution)/shard_map/ppermute | solution.py:22
  14.4 30.6 %collective-permute-start.6 = (bf16[128,1024]{1,0:T(8,128)(2,1)S(1)}, bf16[128,1024]{1,0:T(8,128)(2,1)}, u32[]{:S(2)}, u32[]{:S(2)}) collective-permute-start(bf16[128,1024]{1,0:T(8,128)(2,1)S(1)} %constant_dynamic-slice_fusion.17), channel_id=1, source_target_pairs={{0,4},{1,5},{2,6},{3,7},{4,0},{5,1},{6,2},{7,3},{8,12},{9,13},{10,... | collective-permute-start | bytes 786440 | tf_op jit(solution)/shard_map/ppermute | solution.py:22
  14.4 23.0 %collective-permute-start.3 = (bf16[128,1024]{1,0:T(8,128)(2,1)S(1)}, bf16[128,1024]{1,0:T(8,128)(2,1)S(1)}, u32[]{:S(2)}, u32[]{:S(2)}) collective-permute-start(bf16[128,1024]{1,0:T(8,128)(2,1)S(1)} %constant_dynamic-slice_fusion.17), channel_id=1, source_target_pairs={{0,2},{1,3},{2,0},{3,1},{4,6},{5,7},{6,4},{7,5},{8,10},{9,11},{10,... | collective-permute-start | bytes 786440 | tf_op jit(solution)/shard_map/ppermute | solution.py:22
  18.1 40.4 %collective-permute-start = (bf16[128,8,256]{2,1,0:T(8,128)(2,1)S(1)}, bf16[128,8,256]{2,1,0:T(8,128)(2,1)S(1)}, u32[]{:S(2)}, u32[]{:S(2)}) collective-permute-start(bf16[128,8,256]{2,1,0:T(8,128)(2,1)S(1)} %bitcast.77), channel_id=1, source_target_pairs={{0,16},{16,0},{1,17},{17,1},{2,18},{18,2},{3,19},{19,3},{4,20},{20... | collective-permute-start | bytes 1572872 | tf_op jit(solution)/shard_map/ppermute | solution.py:18
  20.2 40.8 %collective-permute-start.2 = (bf16[256,1024]{1,0:T(8,128)(2,1)S(1)}, bf16[256,1024]{1,0:T(8,128)(2,1)S(1)}, u32[]{:S(2)}, u32[]{:S(2)}) collective-permute-start(bf16[256,1024]{1,0:T(8,128)(2,1)S(1)} %pad_maximum_fusion), channel_id=1, source_target_pairs={{0,8},{8,0},{1,9},{9,1},{2,10},{10,2},{3,11},{11,3},{4,12},{12,4},... | collective-permute-start | bytes 1572872 | tf_op jit(solution)/shard_map/ppermute | solution.py:14
  22.0 25.5 %collective-permute-start.10 = (bf16[128,1024]{1,0:T(8,128)(2,1)}, bf16[128,1024]{1,0:T(8,128)(2,1)S(1)}, u32[]{:S(2)}, u32[]{:S(2)}) collective-permute-start(bf16[128,1024]{1,0:T(8,128)(2,1)} %collective-permute-done.9), channel_id=1, source_target_pairs={{0,1},{1,0},{2,3},{3,2},{4,5},{5,4},{6,7},{7,6},{8,9},{9,8},{10,11... | collective-permute-start | bytes 786440 | tf_op jit(solution)/shard_map/ppermute | solution.py:22
  37.4 20.5 %collective-permute-start.4 = (bf16[128,1024]{1,0:T(8,128)(2,1)S(1)}, bf16[128,1024]{1,0:T(8,128)(2,1)S(1)}, u32[]{:S(2)}, u32[]{:S(2)}) collective-permute-start(bf16[128,1024]{1,0:T(8,128)(2,1)S(1)} %collective-permute-done.3), channel_id=1, source_target_pairs={{0,1},{1,0},{2,3},{3,2},{4,5},{5,4},{6,7},{7,6},{8,9},{9,8},{10,11... | collective-permute-start | bytes 786440 | tf_op jit(solution)/shard_map/ppermute | solution.py:22
  45.0 12.8 %collective-permute-start.7 = (bf16[128,1024]{1,0:T(8,128)(2,1)}, bf16[128,1024]{1,0:T(8,128)(2,1)S(1)}, u32[]{:S(2)}, u32[]{:S(2)}) collective-permute-start(bf16[128,1024]{1,0:T(8,128)(2,1)} %collective-permute-done.6), channel_id=1, source_target_pairs={{0,1},{1,0},{2,3},{3,2},{4,5},{5,4},{6,7},{7,6},{8,9},{9,8},{10,11... | collective-permute-start | bytes 786440 | tf_op jit(solution)/shard_map/ppermute | solution.py:22
  47.6 14.0 %collective-permute-start.11 = (bf16[256,1024]{1,0:T(8,128)(2,1)S(1)}, bf16[256,1024]{1,0:T(8,128)(2,1)S(1)}, u32[]{:S(2)}, u32[]{:S(2)}) collective-permute-start(bf16[256,1024]{1,0:T(8,128)(2,1)S(1)} %constant_dynamic-update-slice_fusion.4), channel_id=1, source_target_pairs={{0,8},{8,0},{1,9},{9,1},{2,10},{10,2},{3,11},{11,3},{4,12},{12,4},... | collective-permute-start | bytes 1572872 | tf_op jit(solution)/shard_map/ppermute | solution.py:14
  57.8 4.7 %collective-permute-start.8 = (bf16[256,1024]{1,0:T(8,128)(2,1)S(1)}, bf16[256,1024]{1,0:T(8,128)(2,1)S(1)}, u32[]{:S(2)}, u32[]{:S(2)}) collective-permute-start(bf16[256,1024]{1,0:T(8,128)(2,1)S(1)} %constant_dynamic-update-slice_fusion.2), channel_id=1, source_target_pairs={{0,8},{8,0},{1,9},{9,1},{2,10},{10,2},{3,11},{11,3},{4,12},{12,4},... | collective-permute-start | bytes 1572872 | tf_op jit(solution)/shard_map/ppermute | solution.py:14
  57.9 4.0 %collective-permute-start.5 = (bf16[256,1024]{1,0:T(8,128)(2,1)S(1)}, bf16[256,1024]{1,0:T(8,128)(2,1)S(1)}, u32[]{:S(2)}, u32[]{:S(2)}) collective-permute-start(bf16[256,1024]{1,0:T(8,128)(2,1)S(1)} %constant_dynamic-update-slice_fusion), channel_id=1, source_target_pairs={{0,8},{8,0},{1,9},{9,1},{2,10},{10,2},{3,11},{11,3},{4,12},{12,4},... | collective-permute-start | bytes 1572872 | tf_op jit(solution)/shard_map/ppermute | solution.py:14
  63.1 2.0 copy-start.7
  63.1 14.1 %copy-start.8 = (s32[128,8]{0,1:T(8,128)S(1)}, s32[128,8]{0,1:T(8,128)}, u32[]{:S(2)}) copy-start(s32[128,8]{0,1:T(8,128)} %param.9) | copy-start | bytes 12292
  63.5 8.3 %collective-permute-start.12 = (bf16[128,1024]{1,0:T(8,128)(2,1)S(1)}, bf16[128,1024]{1,0:T(8,128)(2,1)S(1)}, u32[]{:S(2)}, u32[]{:S(2)}) collective-permute-start(bf16[128,1024]{1,0:T(8,128)(2,1)S(1)} %slice.85), channel_id=1, source_target_pairs={{0,16},{16,0},{1,17},{17,1},{2,18},{18,2},{3,19},{19,3},{4,20},{20... | collective-permute-start | bytes 786440 | tf_op jit(solution)/shard_map/ppermute | solution.py:18
  71.9 26.6 %collective-permute-start.29 = (bf16[128,1024]{1,0:T(8,128)(2,1)S(1)}, bf16[128,1024]{1,0:T(8,128)(2,1)S(1)}, u32[]{:S(2)}, u32[]{:S(2)}) collective-permute-start(bf16[128,1024]{1,0:T(8,128)(2,1)S(1)} %fusion.10.near), channel_id=1, source_target_pairs={{0,6},{1,7},{2,4},{3,5},{4,2},{5,3},{6,0},{7,1},{8,14},{9,15},{10,... | collective-permute-start | bytes 786440 | tf_op jit(solution)/shard_map/ppermute | solution.py:22
  72.7 27.1 %collective-permute-start.13 = (bf16[128,1024]{1,0:T(8,128)(2,1)S(1)}, bf16[128,1024]{1,0:T(8,128)(2,1)S(1)}, u32[]{:S(2)}, u32[]{:S(2)}) collective-permute-start(bf16[128,1024]{1,0:T(8,128)(2,1)S(1)} %fusion.10.near), channel_id=1, source_target_pairs={{0,1},{1,0},{2,3},{3,2},{4,5},{5,4},{6,7},{7,6},{8,9},{9,8},{10,11... | collective-permute-start | bytes 786440 | tf_op jit(solution)/shard_map/ppermute | solution.py:22
  73.1 26.9 %collective-permute-start.23 = (bf16[128,1024]{1,0:T(8,128)(2,1)S(1)}, bf16[128,1024]{1,0:T(8,128)(2,1)S(1)}, u32[]{:S(2)}, u32[]{:S(2)}) collective-permute-start(bf16[128,1024]{1,0:T(8,128)(2,1)S(1)} %fusion.10.near), channel_id=1, source_target_pairs={{0,4},{1,5},{2,6},{3,7},{4,0},{5,1},{6,2},{7,3},{8,12},{9,13},{10,... | collective-permute-start | bytes 786440 | tf_op jit(solution)/shard_map/ppermute | solution.py:22
  77.9 20.6 %all-to-all-start = ((f32[16,1,128]{2,1,0:T(1,128)}), f32[16,1,128]{2,1,0:T(1,128)S(1)}, u32[]{:S(2)}, u32[]{:S(2)}) async-start(f32[16,1,128]{2,1,0:T(1,128)} %bitcast.5), calls=%async_computation | async-start | bytes 16384 | tf_op jit(solution)/shard_map/all_to_all | solution.py:145
  83.5 17.3 %collective-permute-start.17 = (bf16[128,1024]{1,0:T(8,128)(2,1)S(1)}, bf16[128,1024]{1,0:T(8,128)(2,1)S(1)}, u32[]{:S(2)}, u32[]{:S(2)}) collective-permute-start(bf16[128,1024]{1,0:T(8,128)(2,1)S(1)} %fusion.10.near), channel_id=1, source_target_pairs={{0,2},{1,3},{2,0},{3,1},{4,6},{5,7},{6,4},{7,5},{8,10},{9,11},{10,... | collective-permute-start | bytes 786440 | tf_op jit(solution)/shard_map/ppermute | solution.py:22
  98.5 20.4 %copy-start.2 = (bf16[1,1024,2048]{2,1,0:T(8,128)(2,1)S(1)}, bf16[1,1024,2048]{2,1,0:T(8,128)(2,1)}, u32[]{:S(2)}) copy-start(bf16[1,1024,2048]{2,1,0:T(8,128)(2,1)} %gate.7) | copy-start | bytes 12582916
  98.5 9.3 %collective-permute-start.30 = (bf16[128,1024]{1,0:T(8,128)(2,1)S(1)}, bf16[128,1024]{1,0:T(8,128)(2,1)S(1)}, u32[]{:S(2)}, u32[]{:S(2)}) collective-permute-start(bf16[128,1024]{1,0:T(8,128)(2,1)S(1)} %collective-permute-done.29.near), channel_id=1, source_target_pairs={{0,1},{1,0},{2,3},{3,2},{4,5},{5,4},{6,7},{7,6},{8,9},{9,8},{10,11... | collective-permute-start | bytes 786440 | tf_op jit(solution)/shard_map/ppermute | solution.py:22
  99.9 18.9 %collective-permute-start.14 = (bf16[256,1024]{1,0:T(8,128)(2,1)S(1)}, bf16[256,1024]{1,0:T(8,128)(2,1)S(1)}, u32[]{:S(2)}, u32[]{:S(2)}) collective-permute-start(bf16[256,1024]{1,0:T(8,128)(2,1)S(1)} %pad_maximum_fusion.1), channel_id=1, source_target_pairs={{0,8},{8,0},{1,9},{9,1},{2,10},{10,2},{3,11},{11,3},{4,12},{12,4},... | collective-permute-start | bytes 1572872 | tf_op jit(solution)/shard_map/ppermute | solution.py:14
  100.0 13.4 %collective-permute-start.24 = (bf16[128,1024]{1,0:T(8,128)(2,1)S(1)}, bf16[128,1024]{1,0:T(8,128)(2,1)S(1)}, u32[]{:S(2)}, u32[]{:S(2)}) collective-permute-start(bf16[128,1024]{1,0:T(8,128)(2,1)S(1)} %collective-permute-done.23.near), channel_id=1, source_target_pairs={{0,1},{1,0},{2,3},{3,2},{4,5},{5,4},{6,7},{7,6},{8,9},{9,8},{10,11... | collective-permute-start | bytes 786440 | tf_op jit(solution)/shard_map/ppermute | solution.py:22
  100.8 17.1 %collective-permute-start.18 = (bf16[128,1024]{1,0:T(8,128)(2,1)S(1)}, bf16[128,1024]{1,0:T(8,128)(2,1)S(1)}, u32[]{:S(2)}, u32[]{:S(2)}) collective-permute-start(bf16[128,1024]{1,0:T(8,128)(2,1)S(1)} %collective-permute-done.17.near), channel_id=1, source_target_pairs={{0,1},{1,0},{2,3},{3,2},{4,5},{5,4},{6,7},{7,6},{8,9},{9,8},{10,11... | collective-permute-start | bytes 786440 | tf_op jit(solution)/shard_map/ppermute | solution.py:22
  107.8 24.0 %collective-permute-start.31 = (bf16[256,1024]{1,0:T(8,128)(2,1)S(1)}, bf16[256,1024]{1,0:T(8,128)(2,1)S(1)}, u32[]{:S(2)}, u32[]{:S(2)}) collective-permute-start(bf16[256,1024]{1,0:T(8,128)(2,1)S(1)} %pad_maximum_fusion.4), channel_id=1, source_target_pairs={{0,8},{8,0},{1,9},{9,1},{2,10},{10,2},{3,11},{11,3},{4,12},{12,4},... | collective-permute-start | bytes 1572872 | tf_op jit(solution)/shard_map/ppermute | solution.py:14
  114.2 29.4 %collective-permute-start.25 = (bf16[256,1024]{1,0:T(8,128)(2,1)}, bf16[256,1024]{1,0:T(8,128)(2,1)}, u32[]{:S(2)}, u32[]{:S(2)}) collective-permute-start(bf16[256,1024]{1,0:T(8,128)(2,1)} %pad_maximum_fusion.3), channel_id=1, source_target_pairs={{0,8},{8,0},{1,9},{9,1},{2,10},{10,2},{3,11},{11,3},{4,12},{12,4},... | collective-permute-start | bytes 1572872 | tf_op jit(solution)/shard_map/ppermute | solution.py:14
  118.7 39.3 %collective-permute-start.19 = (bf16[256,1024]{1,0:T(8,128)(2,1)}, bf16[256,1024]{1,0:T(8,128)(2,1)S(1)}, u32[]{:S(2)}, u32[]{:S(2)}) collective-permute-start(bf16[256,1024]{1,0:T(8,128)(2,1)} %pad_maximum_fusion.2), channel_id=1, source_target_pairs={{0,8},{8,0},{1,9},{9,1},{2,10},{10,2},{3,11},{11,3},{4,12},{12,4},... | collective-permute-start | bytes 1572872 | tf_op jit(solution)/shard_map/ppermute | solution.py:14
  118.9 2.2 copy-start.4
  131.3 36.9 %collective-permute-start.15 = (bf16[256,1024]{1,0:T(8,128)(2,1)}, bf16[256,1024]{1,0:T(8,128)(2,1)}, u32[]{:S(2)}, u32[]{:S(2)}) collective-permute-start(bf16[256,1024]{1,0:T(8,128)(2,1)} %get-tuple-element.14), channel_id=1, source_target_pairs={{0,8},{8,0},{1,9},{9,1},{2,10},{10,2},{3,11},{11,3},{4,12},{12,4},... | collective-permute-start | bytes 1572872 | tf_op jit(solution)/shard_map/ppermute | solution.py:14
  142.1 28.5 %collective-permute-start.32 = (bf16[256,1024]{1,0:T(8,128)(2,1)}, bf16[256,1024]{1,0:T(8,128)(2,1)}, u32[]{:S(2)}, u32[]{:S(2)}) collective-permute-start(bf16[256,1024]{1,0:T(8,128)(2,1)} %get-tuple-element.20), channel_id=1, source_target_pairs={{0,8},{8,0},{1,9},{9,1},{2,10},{10,2},{3,11},{11,3},{4,12},{12,4},... | collective-permute-start | bytes 1572872 | tf_op jit(solution)/shard_map/ppermute | solution.py:14
  142.1 48.4 %collective-permute-start.35 = (bf16[8,256,512]{2,1,0:T(8,128)(2,1)}, bf16[8,256,512]{2,1,0:T(8,128)(2,1)}, u32[]{:S(2)}, u32[]{:S(2)}) collective-permute-start(bf16[8,256,512]{2,1,0:T(8,128)(2,1)} %bitcast.12), channel_id=1, source_target_pairs={{0,16},{16,0},{1,17},{17,1},{2,18},{18,2},{3,19},{19,3},{4,20},{20... | collective-permute-start | bytes 6291464 | tf_op jit(solution)/shard_map/ppermute | solution.py:18
  143.8 2.2 copy-start.3
  146.0 2.2 copy-start.5
  157.7 15.1 %collective-permute-start.26 = (bf16[256,1024]{1,0:T(8,128)(2,1)S(1)}, bf16[256,1024]{1,0:T(8,128)(2,1)S(1)}, u32[]{:S(2)}, u32[]{:S(2)}) collective-permute-start(bf16[256,1024]{1,0:T(8,128)(2,1)S(1)} %get-tuple-element.18), channel_id=1, source_target_pairs={{0,8},{8,0},{1,9},{9,1},{2,10},{10,2},{3,11},{11,3},{4,12},{12,4},... | collective-permute-start | bytes 1572872 | tf_op jit(solution)/shard_map/ppermute | solution.py:14
  167.8 6.5 %collective-permute-start.20 = (bf16[256,1024]{1,0:T(8,128)(2,1)S(1)}, bf16[256,1024]{1,0:T(8,128)(2,1)S(1)}, u32[]{:S(2)}, u32[]{:S(2)}) collective-permute-start(bf16[256,1024]{1,0:T(8,128)(2,1)S(1)} %get-tuple-element.16), channel_id=1, source_target_pairs={{0,8},{8,0},{1,9},{9,1},{2,10},{10,2},{3,11},{11,3},{4,12},{12,4},... | collective-permute-start | bytes 1572872 | tf_op jit(solution)/shard_map/ppermute | solution.py:14
  169.4 25.4 %collective-permute-start.16 = (bf16[128,1024]{1,0:T(8,128)(2,1)S(1)}, bf16[128,1024]{1,0:T(8,128)(2,1)S(1)}, u32[]{:S(2)}, u32[]{:S(2)}) collective-permute-start(bf16[128,1024]{1,0:T(8,128)(2,1)S(1)} %slice.84), channel_id=1, source_target_pairs={{0,1},{1,0},{2,3},{3,2},{4,5},{5,4},{6,7},{7,6},{8,9},{9,8},{10,11... | collective-permute-start | bytes 786440 | tf_op jit(solution)/shard_map/ppermute | solution.py:22
  171.9 12.3 %collective-permute-start.33 = (bf16[128,1024]{1,0:T(8,128)(2,1)S(1)}, bf16[128,1024]{1,0:T(8,128)(2,1)S(1)}, u32[]{:S(2)}, u32[]{:S(2)}) collective-permute-start(bf16[128,1024]{1,0:T(8,128)(2,1)S(1)} %slice.81), channel_id=1, source_target_pairs={{0,1},{1,0},{2,3},{3,2},{4,5},{5,4},{6,7},{7,6},{8,9},{9,8},{10,11... | collective-permute-start | bytes 786440 | tf_op jit(solution)/shard_map/ppermute | solution.py:22
  173.0 17.5 %collective-permute-start.27 = (bf16[128,1024]{1,0:T(8,128)(2,1)S(1)}, bf16[128,1024]{1,0:T(8,128)(2,1)S(1)}, u32[]{:S(2)}, u32[]{:S(2)}) collective-permute-start(bf16[128,1024]{1,0:T(8,128)(2,1)S(1)} %slice.82), channel_id=1, source_target_pairs={{0,1},{1,0},{2,3},{3,2},{4,5},{5,4},{6,7},{7,6},{8,9},{9,8},{10,11... | collective-permute-start | bytes 786440 | tf_op jit(solution)/shard_map/ppermute | solution.py:22
  174.3 46.1 %collective-permute-start.36 = (bf16[8,256,512]{2,1,0:T(8,128)(2,1)}, bf16[8,256,512]{2,1,0:T(8,128)(2,1)}, u32[]{:S(2)}, u32[]{:S(2)}) collective-permute-start(bf16[8,256,512]{2,1,0:T(8,128)(2,1)} %bitcast.12), channel_id=1, source_target_pairs={{0,8},{8,0},{1,9},{9,1},{2,10},{10,2},{3,11},{11,3},{4,12},{12,4},... | collective-permute-start | bytes 6291464 | tf_op jit(solution)/shard_map/ppermute | solution.py:14
  184.2 10.5 %collective-permute-start.21 = (bf16[128,1024]{1,0:T(8,128)(2,1)S(1)}, bf16[128,1024]{1,0:T(8,128)(2,1)S(1)}, u32[]{:S(2)}, u32[]{:S(2)}) collective-permute-start(bf16[128,1024]{1,0:T(8,128)(2,1)S(1)} %slice.83), channel_id=1, source_target_pairs={{0,1},{1,0},{2,3},{3,2},{4,5},{5,4},{6,7},{7,6},{8,9},{9,8},{10,11... | collective-permute-start | bytes 786440 | tf_op jit(solution)/shard_map/ppermute | solution.py:22
  190.5 32.0 %collective-permute-start.37 = (bf16[8,256,512]{2,1,0:T(8,128)(2,1)}, bf16[8,256,512]{2,1,0:T(8,128)(2,1)}, u32[]{:S(2)}, u32[]{:S(2)}) collective-permute-start(bf16[8,256,512]{2,1,0:T(8,128)(2,1)} %collective-permute-done.35), channel_id=1, source_target_pairs={{0,8},{8,0},{1,9},{9,1},{2,10},{10,2},{3,11},{11,3},{4,12},{12,4},... | collective-permute-start | bytes 6291464 | tf_op jit(solution)/shard_map/ppermute | solution.py:14
  190.6 11.1 %collective-permute-start.34 = (bf16[128,1024]{1,0:T(8,128)(2,1)S(1)}, bf16[128,1024]{1,0:T(8,128)(2,1)S(1)}, u32[]{:S(2)}, u32[]{:S(2)}) collective-permute-start(bf16[128,1024]{1,0:T(8,128)(2,1)S(1)} %fusion.3), channel_id=1, source_target_pairs={{0,6},{1,7},{2,4},{3,5},{4,2},{5,3},{6,0},{7,1},{8,14},{9,15},{10,... | collective-permute-start | bytes 786440 | tf_op jit(solution)/shard_map/ppermute | solution.py:22
  194.7 21.4 %collective-permute-start.28 = (bf16[128,1024]{1,0:T(8,128)(2,1)S(1)}, bf16[128,1024]{1,0:T(8,128)(2,1)S(1)}, u32[]{:S(2)}, u32[]{:S(2)}) collective-permute-start(bf16[128,1024]{1,0:T(8,128)(2,1)S(1)} %fusion.4), channel_id=1, source_target_pairs={{0,4},{1,5},{2,6},{3,7},{4,0},{5,1},{6,2},{7,3},{8,12},{9,13},{10,... | collective-permute-start | bytes 786440 | tf_op jit(solution)/shard_map/ppermute | solution.py:22
  194.8 21.3 %collective-permute-start.22 = (bf16[128,1024]{1,0:T(8,128)(2,1)S(1)}, bf16[128,1024]{1,0:T(8,128)(2,1)S(1)}, u32[]{:S(2)}, u32[]{:S(2)}) collective-permute-start(bf16[128,1024]{1,0:T(8,128)(2,1)S(1)} %fusion.5), channel_id=1, source_target_pairs={{0,2},{1,3},{2,0},{3,1},{4,6},{5,7},{6,4},{7,5},{8,10},{9,11},{10,... | collective-permute-start | bytes 786440 | tf_op jit(solution)/shard_map/ppermute | solution.py:22
  222.5 4.4 %copy-start.1 = (bf16[512,1024]{1,0:T(8,128)(2,1)S(1)}, bf16[512,1024]{1,0:T(8,128)(2,1)}, u32[]{:S(2)}) copy-start(bf16[512,1024]{1,0:T(8,128)(2,1)} %param.11) | copy-start | bytes 3145732
  (1 other events, 1.2 us)
Sparse Core Ops, SparseCore 0:
  17.0 56.5 all-gather.2

commit v3 on v1

v3 whole, which is shorter than its diff:
```python
import jax
import jax.numpy as jnp
from jax import lax
from jax.experimental import pallas as pl
from jax.experimental.pallas import tpu as pltpu
from jax.sharding import PartitionSpec as P

route_scale = 2.5
mebi = 1024 * 1024
in_vmem = pl.BlockSpec(memory_space=pltpu.VMEM)
anywhere = pl.BlockSpec(memory_space=pl.ANY)
after = lax.optimization_barrier


def swap_cores(array):
    return lax.ppermute(array, "grp", [(0, 1), (1, 0)])


def swap_reps(array):
    return lax.ppermute(array, "rep", [(i, i ^ 1) for i in range(lax.axis_size("rep"))])


def swap_ep(array, mask):
    return lax.ppermute(array, "ep", [(i, i ^ mask) for i in range(lax.axis_size("ep"))])


def gather_line(piece):
    line = [piece]
    for k in range(1, lax.axis_size("ep") // 2):
        low = k & -k
        line.append(swap_ep(line[k ^ low], 2 * low))
    return line


def dense_weights(expert_ids, route_scores, expert_count):
    sigmoids = jax.nn.sigmoid(route_scores)
    weights = (route_scale * sigmoids / jnp.sum(sigmoids, axis=1, keepdims=True)).astype(
        jnp.bfloat16
    )
    named = expert_ids[None, :, :] == jnp.arange(expert_count, dtype=jnp.int32)[:, None, None]
    return jnp.sum(jnp.where(named, weights.astype(jnp.float32)[None, :, :], 0.0), axis=2)


def expert_kernel(own, other, scale, gate, up, out, own_sum, other_sum, rows, hidden, held):
    count = own.shape[0]
    width = 256
    rows[:count] = own[...]
    rows[count:] = other[...]

    def products(start):
        columns = pl.ds(pl.multiple_of(start, width), width)
        return (
            jnp.dot(rows[...], gate[0, :, columns], preferred_element_type=jnp.float32),
            jnp.dot(rows[...], up[0, :, columns], preferred_element_type=jnp.float32),
        )

    def activate(gate_value, up_value, start):
        value = gate_value / (1.0 + jnp.exp(-gate_value)) * up_value
        hidden[:, pl.ds(pl.multiple_of(start, width), width)] = value.astype(jnp.bfloat16)

    hidden_width = gate.shape[2]
    held[0], held[1] = products(0)

    def step(i, carry):
        start = i * 2 * width
        first = products(start + width)
        activate(held[0], held[1], start)
        second = products(start + 2 * width)
        activate(*first, start + width)
        held[0], held[1] = second
        return carry

    steps = hidden_width // (2 * width)
    lax.fori_loop(0, steps - 1, step, 0)
    last = products(hidden_width - width)
    activate(held[0], held[1], hidden_width - 2 * width)
    activate(*last, hidden_width - width)

    def finish(i, carry):
        columns = pl.ds(pl.multiple_of(i * width, width), width)
        value = jnp.dot(hidden[...], out[0, :, columns], preferred_element_type=jnp.float32)
        value = (value * scale[:, :1]).astype(jnp.bfloat16)
        own_sum[:, columns] = value[:count]
        other_sum[:, columns] = value[count:]
        return carry

    lax.fori_loop(0, out.shape[2] // width, finish, 0)


def expert_apply(own, other, scale, gate_weight, up_weight, out_weight):
    count, latent_width = own.shape
    hidden_width = gate_weight.shape[2]
    sums = jax.ShapeDtypeStruct((count, latent_width), jnp.bfloat16)
    return pl.pallas_call(
        expert_kernel,
        out_shape=(sums, sums),
        in_specs=[in_vmem] * 6,
        out_specs=(in_vmem,) * 2,
        scratch_shapes=[
            pltpu.VMEM((2 * count, latent_width), jnp.bfloat16),
            pltpu.VMEM((2 * count, hidden_width), jnp.bfloat16),
            pltpu.VMEM((2, 2 * count, 256), jnp.float32),
        ],
        compiler_params=pltpu.CompilerParams(vmem_limit_bytes=16 * mebi),
        cost_estimate=pl.CostEstimate(
            flops=12 * count * latent_width * hidden_width,
            bytes_accessed=8 * count * latent_width,
            transcendentals=2 * count * hidden_width,
        ),
        name="expert",
    )(own, other, scale, gate_weight, up_weight, out_weight)


def project_kernel(order, *refs):
    terms, stacks, (layer_out, combined) = refs[:-10], refs[-10:-2], refs[-2:]
    quarter, block = stacks[0].shape[1:]

    @pl.when(pl.program_id(0) == 0)
    def _():
        total = terms[0][...].astype(jnp.float32)
        for term in terms[1:]:
            total += term[...].astype(jnp.float32)
        combined[...] = total.astype(jnp.bfloat16)

    for y in range(2):
        value = 0.0
        for source in range(4):
            columns = pl.ds(pl.multiple_of(order[1 + source] * quarter, quarter), quarter)
            value += jnp.dot(
                combined[:, columns], stacks[4 * y + source][0], preferred_element_type=jnp.float32
            )
        start = pl.multiple_of((order[5] ^ y) * block, block)
        layer_out[:, pl.ds(start, block)] = value.astype(jnp.bfloat16)


def project(order, terms, stacks):
    count, latent_width = terms[0].shape
    pieces, quarter, block = stacks[0].shape
    whole = pl.BlockSpec((count, latent_width), lambda i, order: (0, 0))
    return pl.pallas_call(
        project_kernel,
        grid_spec=pltpu.PrefetchScalarGridSpec(
            num_scalar_prefetch=1,
            grid=(pieces,),
            in_specs=[whole] * len(terms)
            + [pl.BlockSpec((1, quarter, block), lambda i, order: (i, 0, 0))] * len(stacks),
            out_specs=pl.BlockSpec((count, 2 * block), lambda i, order: (0, order[0] ^ i)),
            scratch_shapes=[pltpu.VMEM((count, latent_width), jnp.bfloat16)],
        ),
        out_shape=jax.ShapeDtypeStruct((count, 2 * pieces * block), jnp.bfloat16),
        compiler_params=pltpu.CompilerParams(vmem_limit_bytes=28 * mebi),
        cost_estimate=pl.CostEstimate(
            flops=4 * count * latent_width * pieces * block,
            bytes_accessed=8 * latent_width * pieces * block,
            transcendentals=0,
        ),
        name="project",
    )(order, *terms, *stacks)


def body(
    tokens, expert_ids, route_scores, down_latent, gate_weight, up_weight, out_weight, up_latent
):
    group_count = lax.axis_size("grp")
    ep_count = lax.axis_size("ep")
    expert_count = group_count * ep_count * gate_weight.shape[0]
    group = lax.axis_index("grp")
    place = lax.axis_index("ep")
    side = lax.axis_index("rep") % 2
    own_quarter = 2 * side + group
    token_count = tokens.shape[0]
    latent_width = down_latent.shape[1]
    pieces = ep_count // 2

    quarter = down_latent.shape[0] // 4
    line = gather_line(lax.dynamic_slice_in_dim(down_latent, own_quarter * quarter, quarter, 0))
    cut = tokens.reshape(token_count, ep_count, 2, 2 * quarter)
    kept = lax.dynamic_index_in_dim(cut, side, 2, keepdims=False)
    given = lax.dynamic_index_in_dim(cut, 1 - side, 2, keepdims=False)
    inner = jnp.concatenate([kept, swap_reps(given)], axis=0)
    inner = inner.reshape(2 * token_count, ep_count, 2, quarter).transpose(1, 2, 0, 3)

    weights = dense_weights(expert_ids, route_scores, expert_count)
    scale = lax.all_to_all(weights, ("grp", "ep"), split_axis=0, concat_axis=0, tiled=True)
    scale = scale.reshape(group_count, ep_count, token_count)

    def scale_of(offset):
        rows = [
            lax.dynamic_slice(scale, (core, place ^ offset, 0), (1, 1, token_count))
            for core in (group, 1 - group)
        ]
        rows = jnp.concatenate(rows, axis=0).reshape(2 * token_count, 1)
        return jnp.broadcast_to(rows, (2 * token_count, 128))

    def columns_of(core, k):
        parts = [
            lax.dynamic_slice(
                inner, (place ^ (2 * k + y), core, 0, 0), (1, 1, 2 * token_count, quarter)
            )[0, 0]
            for y in range(2)
        ]
        return jnp.concatenate(parts, axis=1)

    scales = [scale_of(offset) for offset in range(ep_count)]
    columns = [(columns_of(group, k), columns_of(1 - group, k)) for k in range(pieces)]
    line[-1], scales, columns = after((line[-1], scales, columns))

    inner_quarter = latent_width // 4
    up_piece = lax.dynamic_slice_in_dim(up_latent, own_quarter * inner_quarter, inner_quarter, 0)
    line[-1], up_piece = after((line[-1], up_piece))
    up_line = gather_line(up_piece)

    partial = jnp.zeros((2 * token_count, latent_width), jnp.float32)
    for k, near in enumerate(line):
        if k == pieces - 1:
            near, partial = after((near, partial))
        both = jnp.concatenate([near, swap_ep(near, 1)], axis=0)
        swapped = swap_cores(both)
        if k == pieces - 2:
            waiting = both, swapped
            continue
        if k == pieces - 1:
            for given, block in zip(columns[k - 1], waiting):
                partial += jnp.dot(given, block, preferred_element_type=jnp.float32)
        for given, block in zip(columns[k], (both, swapped)):
            partial += jnp.dot(given, block, preferred_element_type=jnp.float32)
    arrived = swap_reps(partial[token_count:].astype(jnp.bfloat16))
    latent = (partial[:token_count] + arrived.astype(jnp.float32)).astype(jnp.bfloat16)

    state = {("near", 0): latent}
    swaps = {}

    def fetch(k):
        low = k & -k
        state["near", k] = swap_ep(state["near", k ^ low], 2 * low)

    def fetch_far(k):
        state["far", k] = swap_ep(state["near", k], 1)

    def work(kind, k, previous):
        own = state[kind, k]
        operands = (own, swap_cores(own))
        if previous is not None:
            operands, previous = after((operands, previous))
        own_sum, other_sum = expert_apply(
            *operands, scales[2 * k + (kind == "far")], gate_weight, up_weight, out_weight
        )
        swaps[kind, k] = own_sum, swap_cores(other_sum)
        return own_sum

    def chip_sum(kind, k):
        own_sum, swapped = swaps[kind, k]
        return own_sum.astype(jnp.float32) + swapped.astype(jnp.float32)

    order_of_work = [("near", 0), ("far", 0)]
    for k in range(1, pieces):
        order_of_work += [("near", k), ("far", k)]
    order_of_work[-2:] = order_of_work[:-3:-1]
    for k in range(1, pieces):
        fetch(k)
    for k in range(pieces):
        fetch_far(k)
    sent, pairs, previous = {}, {}, None
    for number, (kind, k) in enumerate(order_of_work):
        token = work(kind, k, previous)
        previous = [token]
        done = order_of_work[number - 1] if number >= 1 else None
        if done is not None and done[0] == "far":
            sent[done[1]] = chip_sum(*done).astype(jnp.bfloat16)
            sent[done[1]], token = after((sent[done[1]], token))
            previous = [token, sent[done[1]]]
        if number >= 3:
            kind, k = order_of_work[number - 3]
            if kind == "far" and k < pieces - 1:
                away = swap_ep(sent[k], 1).astype(jnp.float32)
                pairs[k] = (chip_sum("near", k) + away).astype(jnp.bfloat16)
                pairs[k], token = after((pairs[k], token))
                previous = [token, pairs[k]]
    k = pieces - 1
    away = swap_ep(sent[k], 1).astype(jnp.float32)
    pairs[k] = (chip_sum("near", k) + away).astype(jnp.bfloat16)
    if k - 1 not in pairs:
        away = swap_ep(sent[k - 1], 1).astype(jnp.float32)
        pairs[k - 1] = (chip_sum("near", k - 1) + away).astype(jnp.bfloat16)
    terms = [pairs[0]] + [swap_ep(pairs[k], 2 * k) for k in range(1, pieces)]

    up_near = jnp.stack(up_line)
    up_far = swap_ep(up_near, 1)
    across_near, across_far = swap_reps(up_near), swap_reps(up_far)
    stacks = [
        up_near,
        across_near,
        swap_cores(up_near),
        swap_cores(across_near),
        up_far,
        across_far,
        swap_cores(up_far),
        swap_cores(across_far),
    ]

    order = jnp.stack(
        [
            place // 2,
            own_quarter,
            own_quarter ^ 2,
            own_quarter ^ 1,
            own_quarter ^ 3,
            place % 2,
        ]
    ).astype(jnp.int32)
    return project(order, terms, stacks)


def solution(mesh):
    in_specs = (
        P(("rep", "grp", "ep"), None),
        P(("rep", "grp", "ep"), None),
        P(("rep", "grp", "ep"), None),
        P("ep", None),
        P(("grp", "ep"), None, None),
        P(("grp", "ep"), None, None),
        P(("grp", "ep"), None, None),
        P(None, "ep"),
    )
    out_specs = P(("rep", "grp", "ep"), None)
    return jax.shard_map(body, mesh=mesh, in_specs=in_specs, out_specs=out_specs, check_vma=False)
```

time: 311 us -> 221 us (0.71)
  waiting for transfers between devices: 192 us -> 99.8 us
  matrix products: 66.2 us -> 3.42 us
  Pallas kernels: 0 us -> 47.5 us
  starting transfers between devices: 0.7 us -> 46.4 us
  blocking collectives: 32 us -> 0 us
  between operations: 13.3 us -> 0.8 us
  other arithmetic: 0.15 us -> 9.11 us
  local copies, waits for them, and re-layouts: 6.63 us -> 13 us
    all_gather x3 -> x0, waiting for transfers between devices: 125 us -> none  [the longest x1 77 us: body(): lax.all_gather(lax.dynamic_slice_in_dim(down_latent, group * half, half,...]
    ppermute x0 -> x29, waiting for transfers between devices: none -> 96.9 us  [the longest x25 70.9 us: swap_ep(): lax.ppermute(array, 'ep', [(i, i ^ mask) for i in range(lax.axis_size('ep...]
    reduce_scatter x1 -> x0, waiting for transfers between devices: 64.6 us -> none  [body(): combined = lax.psum_scatter(both, 'ep', scatter_dimension=0, tiled=True)]
    dot_general x8, matrix products: 66.2 us -> 3.42 us  [body(): partial += jnp.dot(given, block, preferred_element_type=jnp.float32)]
    pallas_call x0 -> x9, Pallas kernels: none -> 47.5 us  [the longest x8 41.7 us: expert_apply(): pl.pallas_call(expert_kernel, out_shape=(sums, sums), in_specs=[in_vmem]...]
    ppermute x0 -> x29, starting transfers between devices: none -> 38.8 us  [the longest x25 33.6 us: swap_ep(): lax.ppermute(array, 'ep', [(i, i ^ mask) for i in range(lax.axis_size('ep...]
    all_gather x1 -> x0, blocking collectives: 32 us -> none  [body(): weights = lax.all_gather(weights, ('grp', 'ep'), axis=0, tiled=True)]
    unnamed x15 -> x28, local copies, waits for them, and re-layouts: 2.87 us -> 9.41 us
  transfers between devices with their start and end apart: 8 -> 54, of which waited for: 4 -> 21; matrix products, arithmetic and copies ran while one was open for 20% -> 9% of each run, Pallas kernels for 0% -> 19%
where the time goes in v3:
time: 221 us; the launch traced here: 220 us
  waiting for transfers between devices  99.8 us (45%)
  Pallas kernels  47.5 us (21%)
  starting transfers between devices  46.4 us (21%)
  local copies, waits for them, and re-layouts  13 us (6%)
  other arithmetic  9.11 us (4%)
  matrix products  3.42 us (2%)
    ppermute x25, waiting for transfers between devices, swap_ep(): lax.ppermute(array, 'ep', [(i, i ^ mask) for i in range(lax.axis_size('ep...  70.9 us
    pallas_call x8, Pallas kernels, expert_apply(): pl.pallas_call(expert_kernel, out_shape=(sums, sums), in_specs=[in_vmem]...  41.7 us
    ppermute x25, starting transfers between devices, swap_ep(): lax.ppermute(array, 'ep', [(i, i ^ mask) for i in range(lax.axis_size('ep...  33.6 us
    ppermute x4, waiting for transfers between devices, swap_reps(): lax.ppermute(array, 'rep', [(i, i ^ 1) for i in range(lax.axis_size('rep'...  26 us
    unnamed x28, local copies, waits for them, and re-layouts  9.41 us
    pallas_call x1, Pallas kernels, project(): pl.pallas_call(project_kernel, grid_spec=pltpu.PrefetchScalarGridSpec(num...  5.8 us
    ppermute x4, starting transfers between devices, swap_reps(): lax.ppermute(array, 'rep', [(i, i ^ 1) for i in range(lax.axis_size('rep'...  5.14 us
  transfers between devices with their start and end apart: 54, of which 21 were waited for; matrix products, arithmetic and copies ran while one was open for 9% of the time, Pallas kernels for 19%

profile of v3, /device:TPU:0, one launch (start us, length us, event | category | flops | bytes accessed | tf_op | source)
XLA Modules:
  0.0 220.1 jit_solution(2104169768622898564)
XLA Ops:
  1.2 3.1 %collective-permute-start.5 = (bf16[128,1024]{1,0:T(8,128)(2,1)S(1)}, bf16[128,1024]{1,0:T(8,128)(2,1)}, u32[]{:S(2)}, u32[]{:S(2)}) collective-permute-start(bf16[128,1024]{1,0:T(8,128)(2,1)S(1)} %constant_dynamic-slice_fusion.19), channel_id=1, source_target_pairs={{0,2},{1,3},{2,0},{3,1},{4,6},{5,7},{6,4},{7,5},{8,10},{9,11},{10,... | collective-permute-start | bytes 786440 | tf_op jit(solution)/shard_map/ppermute | solution.py:24
  4.3 1.5 collective-permute-start.3
  5.9 2.6 %collective-permute-start = (bf16[128,1024]{1,0:T(8,128)(2,1)S(1)}, bf16[128,1024]{1,0:T(8,128)(2,1)}, u32[]{:S(2)}, u32[]{:S(2)}) collective-permute-start(bf16[128,1024]{1,0:T(8,128)(2,1)S(1)} %constant_dynamic-slice_fusion.19), channel_id=1, source_target_pairs={{0,4},{1,5},{2,6},{3,7},{4,0},{5,1},{6,2},{7,3},{8,12},{9,13},{10,... | collective-permute-start | bytes 786440 | tf_op jit(solution)/shard_map/ppermute | solution.py:24
  9.9 1.3 select_reduce_fusion
  11.2 3.4 %all-to-all-start = ((f32[16,1,128]{2,1,0:T(1,128)}), f32[16,1,128]{2,1,0:T(1,128)S(1)}, u32[]{:S(2)}, u32[]{:S(2)}) async-start(f32[16,1,128]{2,1,0:T(1,128)} %bitcast.7), calls=%async_computation | async-start | bytes 16384 | tf_op jit(solution)/shard_map/all_to_all | solution.py:184
  14.6 1.6 copy.25
  17.5 1.5 collective-permute-start.2
  22.0 1.5 collective-permute-start.8
  23.5 1.5 collective-permute-start.1
  27.5 4.4 %collective-permute-done.2 = bf16[128,8,256]{2,1,0:T(8,128)(2,1)S(1)} collective-permute-done((bf16[128,8,256]{2,1,0:T(8,128)(2,1)}, bf16[128,8,256]{2,1,0:T(8,128)(2,1)S(1)}, u32[]{:S(2)}, u32[]{:S(2)}) %collective-permute-start.2) | collective-permute-done | bytes 524320 | tf_op jit(solution)/shard_map/ppermute | solution.py:20
  33.3 3.3 %collective-permute-done.6 = bf16[128,1024]{1,0:T(8,128)(2,1)S(1)} collective-permute-done((bf16[128,1024]{1,0:T(8,128)(2,1)}, bf16[128,1024]{1,0:T(8,128)(2,1)S(1)}, u32[]{:S(2)}, u32[]{:S(2)}) %collective-permute-start.6) | collective-permute-done | bytes 262176 | tf_op jit(solution)/shard_map/ppermute | solution.py:24
  39.6 1.3 convolution_add_fusion.2
  41.5 1.5 collective-permute-start.10
  43.0 2.4 %collective-permute-start.44 = (bf16[256,512]{1,0:T(8,128)(2,1)S(1)}, bf16[256,512]{1,0:T(8,128)(2,1)S(1)}, u32[]{:S(2)}, u32[]{:S(2)}) collective-permute-start(bf16[256,512]{1,0:T(8,128)(2,1)S(1)} %constant_dynamic-slice_fusion), channel_id=1, source_target_pairs={{0,4},{1,5},{2,6},{3,7},{4,0},{5,1},{6,2},{7,3},{8,12},{9,13},{10,... | collective-permute-start | bytes 786440 | tf_op jit(solution)/shard_map/ppermute | solution.py:24
  45.4 4.4 %collective-permute-done.10 = bf16[128,1024]{1,0:T(8,128)(2,1)S(1)} collective-permute-done((bf16[128,1024]{1,0:T(8,128)(2,1)S(1)}, bf16[128,1024]{1,0:T(8,128)(2,1)S(1)}, u32[]{:S(2)}, u32[]{:S(2)}) %collective-permute-start.10) | collective-permute-done | bytes 262176 | tf_op jit(solution)/shard_map/ppermute | solution.py:24
  50.6 1.3 collective-permute-done.11
  52.6 1.6 collective-permute-start.12
  54.7 2.9 %collective-permute-done.44 = bf16[256,512]{1,0:T(8,128)(2,1)S(1)} collective-permute-done((bf16[256,512]{1,0:T(8,128)(2,1)S(1)}, bf16[256,512]{1,0:T(8,128)(2,1)S(1)}, u32[]{:S(2)}, u32[]{:S(2)}) %collective-permute-start.44) | collective-permute-done | bytes 262176 | tf_op jit(solution)/shard_map/ppermute | solution.py:24
  58.0 3.0 %collective-permute-done.12 = bf16[128,1024]{1,0:T(8,128)(2,1)S(1)} collective-permute-done((bf16[128,1024]{1,0:T(8,128)(2,1)S(1)}, bf16[128,1024]{1,0:T(8,128)(2,1)S(1)}, u32[]{:S(2)}, u32[]{:S(2)}) %collective-permute-start.12) | collective-permute-done | bytes 262176 | tf_op jit(solution)/shard_map/ppermute | solution.py:20
  61.0 1.5 collective-permute-start.15
  63.3 5.4 %collective-permute-done.45 = bf16[256,512]{1,0:T(8,128)(2,1)S(1)} collective-permute-done((bf16[256,512]{1,0:T(8,128)(2,1)S(1)}, bf16[256,512]{1,0:T(8,128)(2,1)S(1)}, u32[]{:S(2)}, u32[]{:S(2)}) %collective-permute-start.45) | collective-permute-done | bytes 262176 | tf_op jit(solution)/shard_map/ppermute | solution.py:24
  69.5 1.3 collective-permute-start.25
  70.9 2.5 %collective-permute-start.18 = (bf16[128,1024]{1,0:T(8,128)(2,1)S(1)}, bf16[128,1024]{1,0:T(8,128)(2,1)S(1)}, u32[]{:S(2)}, u32[]{:S(2)}) collective-permute-start(bf16[128,1024]{1,0:T(8,128)(2,1)S(1)} %fusion.4.own), channel_id=1, source_target_pairs={{0,2},{1,3},{2,0},{3,1},{4,6},{5,7},{6,4},{7,5},{8,10},{9,11},{10,... | collective-permute-start | bytes 786440 | tf_op jit(solution)/shard_map/ppermute | solution.py:24
  73.4 5.2 %expert.8 = (bf16[128,1024]{1,0:T(8,128)(2,1)S(1)}, bf16[128,1024]{1,0:T(8,128)(2,1)S(1)}) custom-call(bf16[128,1024]{1,0:T(8,128)(2,1)S(1)} %fusion.4.own, bf16[128,1024]{1,0:T(8,128)(2,1)S(1)} %collective-permute-done.13.other, f32[256,128]{1,0:T(8,128)S(1)} %broadcast_in_dim.75.scale, bf16[1,1024,2048]{2,1,0:T(8,128)(2,1)S(1)} %copy-done.1, ...), custom_call_target="tpu_custom_call" | custom-call | flops 3221225472 | bytes 1048576 | tf_op jit(solution)/shard_map/expert/pallas_call | solution.py:94
  79.1 4.9 %collective-permute-done.18.own = bf16[128,1024]{1,0:T(8,128)(2,1)S(1)} collective-permute-done((bf16[128,1024]{1,0:T(8,128)(2,1)S(1)}, bf16[128,1024]{1,0:T(8,128)(2,1)S(1)}, u32[]{:S(2)}, u32[]{:S(2)}) %collective-permute-start.18) | collective-permute-done | bytes 262176 | tf_op jit(solution)/shard_map/ppermute | solution.py:24
  84.1 1.4 collective-permute-start.22
  86.0 5.4 %expert.9 = (bf16[128,1024]{1,0:T(8,128)(2,1)S(1)}, bf16[128,1024]{1,0:T(8,128)(2,1)S(1)}) custom-call(bf16[128,1024]{1,0:T(8,128)(2,1)S(1)} %collective-permute-done.15.own, bf16[128,1024]{1,0:T(8,128)(2,1)S(1)} %collective-permute-done.16.other, f32[256,128]{1,0:T(8,128)S(1)} %broadcast_in_dim.77.scale, bf16[1,1024,2048]{2,1,0:T(8,128)(2,1)S(1)} %copy-done.1, ...), custom_call_target="tpu_custom_call" | custom-call | flops 3221225472 | bytes 1048576 | tf_op jit(solution)/shard_map/expert/pallas_call | solution.py:94
  91.6 7.9 %collective-permute-done.22.own = bf16[128,1024]{1,0:T(8,128)(2,1)S(1)} collective-permute-done((bf16[128,1024]{1,0:T(8,128)(2,1)S(1)}, bf16[128,1024]{1,0:T(8,128)(2,1)S(1)}, u32[]{:S(2)}, u32[]{:S(2)}) %collective-permute-start.22) | collective-permute-done | bytes 262176 | tf_op jit(solution)/shard_map/ppermute | solution.py:24
  99.5 5.2 %expert.10 = (bf16[128,1024]{1,0:T(8,128)(2,1)S(1)}, bf16[128,1024]{1,0:T(8,128)(2,1)S(1)}) custom-call(bf16[128,1024]{1,0:T(8,128)(2,1)S(1)} %collective-permute-done.18.own, bf16[128,1024]{1,0:T(8,128)(2,1)S(1)} %collective-permute-done.19.other, f32[256,128]{1,0:T(8,128)S(1)} %broadcast_in_dim.79.scale, bf16[1,1024,2048]{2,1,0:T(8,128)(2,1)S(1)} %copy-done.1, ...), custom_call_target="tpu_custom_call" | custom-call | flops 3221225472 | bytes 1048576 | tf_op jit(solution)/shard_map/expert/pallas_call | solution.py:94
  105.8 5.2 %expert.11 = (bf16[128,1024]{1,0:T(8,128)(2,1)S(1)}, bf16[128,1024]{1,0:T(8,128)(2,1)S(1)}) custom-call(bf16[128,1024]{1,0:T(8,128)(2,1)S(1)} %collective-permute-done.22.own, bf16[128,1024]{1,0:T(8,128)(2,1)S(1)} %collective-permute-done.23.other, f32[256,128]{1,0:T(8,128)S(1)} %broadcast_in_dim.81.scale, bf16[1,1024,2048]{2,1,0:T(8,128)(2,1)S(1)} %copy-done.1, ...), custom_call_target="tpu_custom_call" | custom-call | flops 3221225472 | bytes 1048576 | tf_op jit(solution)/shard_map/expert/pallas_call | solution.py:94
  111.0 1.5 collective-permute-start.20
  112.5 5.2 %expert.12 = (bf16[128,1024]{1,0:T(8,128)(2,1)S(1)}, bf16[128,1024]{1,0:T(8,128)(2,1)S(1)}) custom-call(bf16[128,1024]{1,0:T(8,128)(2,1)S(1)} %collective-permute-done.25.own, bf16[128,1024]{1,0:T(8,128)(2,1)S(1)} %collective-permute-done.26.other, f32[256,128]{1,0:T(8,128)S(1)} %broadcast_in_dim.83.scale, bf16[1,1024,2048]{2,1,0:T(8,128)(2,1)S(1)} %copy-done.1, ...), custom_call_target="tpu_custom_call" | custom-call | flops 3221225472 | bytes 1048576 | tf_op jit(solution)/shard_map/expert/pallas_call | solution.py:94
  118.7 1.7 collective-permute-start.46
  120.9 5.5 %collective-permute-done.34.own = bf16[128,1024]{1,0:T(8,128)(2,1)S(1)} collective-permute-done((bf16[128,1024]{1,0:T(8,128)(2,1)S(1)}, bf16[128,1024]{1,0:T(8,128)(2,1)S(1)}, u32[]{:S(2)}, u32[]{:S(2)}) %collective-permute-start.34) | collective-permute-done | bytes 262176 | tf_op jit(solution)/shard_map/ppermute | solution.py:24
  127.0 5.2 %expert.13 = (bf16[128,1024]{1,0:T(8,128)(2,1)S(1)}, bf16[128,1024]{1,0:T(8,128)(2,1)S(1)}) custom-call(bf16[128,1024]{1,0:T(8,128)(2,1)S(1)} %collective-permute-done.30.own, bf16[128,1024]{1,0:T(8,128)(2,1)S(1)} %collective-permute-done.31.other, f32[256,128]{1,0:T(8,128)S(1)} %broadcast_in_dim.85.scale, bf16[1,1024,2048]{2,1,0:T(8,128)(2,1)S(1)} %copy-done.1, ...), custom_call_target="tpu_custom_call" | custom-call | flops 3221225472 | bytes 1048576 | tf_op jit(solution)/shard_map/expert/pallas_call | solution.py:94
  132.9 5.2 %expert.14 = (bf16[128,1024]{1,0:T(8,128)(2,1)S(1)}, bf16[128,1024]{1,0:T(8,128)(2,1)S(1)}) custom-call(bf16[128,1024]{1,0:T(8,128)(2,1)S(1)} %collective-permute-done.34.own, bf16[128,1024]{1,0:T(8,128)(2,1)S(1)} %collective-permute-done.35.other, f32[256,128]{1,0:T(8,128)S(1)} %broadcast_in_dim.89.scale, bf16[1,1024,2048]{2,1,0:T(8,128)(2,1)S(1)} %copy-done.1, ...), custom_call_target="tpu_custom_call" | custom-call | flops 3221225472 | bytes 1048576 | tf_op jit(solution)/shard_map/expert/pallas_call | solution.py:94
  138.1 2.8 %collective-permute-done.27 = bf16[128,1024]{1,0:T(8,128)(2,1)S(1)} collective-permute-done((bf16[128,1024]{1,0:T(8,128)(2,1)S(1)}, bf16[128,1024]{1,0:T(8,128)(2,1)S(1)}, u32[]{:S(2)}, u32[]{:S(2)}) %collective-permute-start.27) | collective-permute-done | bytes 262176 | tf_op jit(solution)/shard_map/ppermute | solution.py:24
  142.3 2.5 %collective-permute-done.46.refs_5_ = bf16[4,256,512]{2,1,0:T(8,128)(2,1)} collective-permute-done((bf16[4,256,512]{2,1,0:T(8,128)(2,1)S(1)}, bf16[4,256,512]{2,1,0:T(8,128)(2,1)}, u32[]{:S(2)}, u32[]{:S(2)}) %collective-permute-start.46) | collective-permute-done | bytes 1048608 | tf_op jit(solution)/shard_map/ppermute | solution.py:20
  145.3 5.2 %expert.15 = (bf16[128,1024]{1,0:T(8,128)(2,1)S(1)}, bf16[128,1024]{1,0:T(8,128)(2,1)S(1)}) custom-call(bf16[128,1024]{1,0:T(8,128)(2,1)S(1)} %collective-permute-done.33.own, bf16[128,1024]{1,0:T(8,128)(2,1)S(1)} %collective-permute-done.38.other, f32[256,128]{1,0:T(8,128)S(1)} %broadcast_in_dim.87.scale, bf16[1,1024,2048]{2,1,0:T(8,128)(2,1)S(1)} %copy-done.1, ...), custom_call_target="tpu_custom_call" | custom-call | flops 3221225472 | bytes 1048576 | tf_op jit(solution)/shard_map/expert/pallas_call | solution.py:94
  150.5 16.1 %collective-permute-done.50.refs_9_ = bf16[4,256,512]{2,1,0:T(8,128)(2,1)} collective-permute-done((bf16[4,256,512]{2,1,0:T(8,128)(2,1)S(1)}, bf16[4,256,512]{2,1,0:T(8,128)(2,1)}, u32[]{:S(2)}, u32[]{:S(2)}) %collective-permute-start.50) | collective-permute-done | bytes 1048608 | tf_op jit(solution)/shard_map/ppermute | solution.py:20
  168.5 1.4 collective-permute-start.41
  170.0 6.9 %collective-permute-done.41 = bf16[128,1024]{1,0:T(8,128)(2,1)S(1)} collective-permute-done((bf16[128,1024]{1,0:T(8,128)(2,1)S(1)}, bf16[128,1024]{1,0:T(8,128)(2,1)S(1)}, u32[]{:S(2)}, u32[]{:S(2)}) %collective-permute-start.41) | collective-permute-done | bytes 262176 | tf_op jit(solution)/shard_map/ppermute | solution.py:24
  176.8 1.4 collective-permute-start.36
  179.1 5.3 %collective-permute-done.36 = bf16[128,1024]{1,0:T(8,128)(2,1)S(1)} collective-permute-done((bf16[128,1024]{1,0:T(8,128)(2,1)S(1)}, bf16[128,1024]{1,0:T(8,128)(2,1)S(1)}, u32[]{:S(2)}, u32[]{:S(2)}) %collective-permute-start.36) | collective-permute-done | bytes 262176 | tf_op jit(solution)/shard_map/ppermute | solution.py:24
  186.2 3.3 %collective-permute-start.42 = (bf16[128,1024]{1,0:T(8,128)(2,1)}, bf16[128,1024]{1,0:T(8,128)(2,1)}, u32[]{:S(2)}, u32[]{:S(2)}) collective-permute-start(bf16[128,1024]{1,0:T(8,128)(2,1)} %add_convert_fusion), channel_id=1, source_target_pairs={{0,6},{1,7},{2,4},{3,5},{4,2},{5,3},{6,0},{7,1},{8,14},{9,15},{10,... | collective-permute-start | bytes 786440 | tf_op jit(solution)/shard_map/ppermute | solution.py:24
  192.1 8.9 %collective-permute-done.42.refs_3_ = bf16[128,1024]{1,0:T(8,128)(2,1)} collective-permute-done((bf16[128,1024]{1,0:T(8,128)(2,1)}, bf16[128,1024]{1,0:T(8,128)(2,1)}, u32[]{:S(2)}, u32[]{:S(2)}) %collective-permute-start.42) | collective-permute-done | bytes 262176 | tf_op jit(solution)/shard_map/ppermute | solution.py:24
  201.0 10.9 %collective-permute-done.37.refs_2_ = bf16[128,1024]{1,0:T(8,128)(2,1)} collective-permute-done((bf16[128,1024]{1,0:T(8,128)(2,1)}, bf16[128,1024]{1,0:T(8,128)(2,1)}, u32[]{:S(2)}, u32[]{:S(2)}) %collective-permute-start.37) | collective-permute-done | bytes 262176 | tf_op jit(solution)/shard_map/ppermute | solution.py:24
  214.3 5.8 %project.1 = bf16[128,4096]{1,0:T(8,128)(2,1)} custom-call(s32[6]{0:T(128)S(1)} %stack.42.order, bf16[128,1024]{1,0:T(8,128)(2,1)S(1)} %add_convert_fusion.6.refs_0_, bf16[128,1024]{1,0:T(8,128)(2,1)} %collective-permute-done.28.refs_1_, bf16[128,1024]{1,0:T(8,128)(2,1)} %collective-permute-done.37.refs_2_, ...), custom_call_target="tpu_custom_call" | custom-call | flops 1073741824 | bytes 16777216 | tf_op jit(solution)/shard_map/project/pallas_call | solution.py:140
  (153 shorter events, 34.8 us)
Async XLA Ops:
  1.2 23.7 %collective-permute-start.5 = (bf16[128,1024]{1,0:T(8,128)(2,1)S(1)}, bf16[128,1024]{1,0:T(8,128)(2,1)}, u32[]{:S(2)}, u32[]{:S(2)}) collective-permute-start(bf16[128,1024]{1,0:T(8,128)(2,1)S(1)} %constant_dynamic-slice_fusion.19), channel_id=1, source_target_pairs={{0,2},{1,3},{2,0},{3,1},{4,6},{5,7},{6,4},{7,5},{8,10},{9,11},{10,... | collective-permute-start | bytes 786440 | tf_op jit(solution)/shard_map/ppermute | solution.py:24
  4.3 16.6 %collective-permute-start.3 = (bf16[128,1024]{1,0:T(8,128)(2,1)S(1)}, bf16[128,1024]{1,0:T(8,128)(2,1)}, u32[]{:S(2)}, u32[]{:S(2)}) collective-permute-start(bf16[128,1024]{1,0:T(8,128)(2,1)S(1)} %constant_dynamic-slice_fusion.19), channel_id=1, source_target_pairs={{0,1},{1,0},{2,3},{3,2},{4,5},{5,4},{6,7},{7,6},{8,9},{9,8},{10,11... | collective-permute-start | bytes 786440 | tf_op jit(solution)/shard_map/ppermute | solution.py:24
  5.9 16.2 %collective-permute-start = (bf16[128,1024]{1,0:T(8,128)(2,1)S(1)}, bf16[128,1024]{1,0:T(8,128)(2,1)}, u32[]{:S(2)}, u32[]{:S(2)}) collective-permute-start(bf16[128,1024]{1,0:T(8,128)(2,1)S(1)} %constant_dynamic-slice_fusion.19), channel_id=1, source_target_pairs={{0,4},{1,5},{2,6},{3,7},{4,0},{5,1},{6,2},{7,3},{8,12},{9,13},{10,... | collective-permute-start | bytes 786440 | tf_op jit(solution)/shard_map/ppermute | solution.py:24
  11.2 9.7 %all-to-all-start = ((f32[16,1,128]{2,1,0:T(1,128)}), f32[16,1,128]{2,1,0:T(1,128)S(1)}, u32[]{:S(2)}, u32[]{:S(2)}) async-start(f32[16,1,128]{2,1,0:T(1,128)} %bitcast.7), calls=%async_computation | async-start | bytes 16384 | tf_op jit(solution)/shard_map/all_to_all | solution.py:184
  17.5 14.4 %collective-permute-start.2 = (bf16[128,8,256]{2,1,0:T(8,128)(2,1)}, bf16[128,8,256]{2,1,0:T(8,128)(2,1)S(1)}, u32[]{:S(2)}, u32[]{:S(2)}) collective-permute-start(bf16[128,8,256]{2,1,0:T(8,128)(2,1)} %bitcast.19), channel_id=1, source_target_pairs={{0,16},{16,0},{1,17},{17,1},{2,18},{18,2},{3,19},{19,3},{4,20},{20... | collective-permute-start | bytes 1572872 | tf_op jit(solution)/shard_map/ppermute | solution.py:20
  21.9 17.4 %collective-permute-start.4 = (bf16[256,1024]{1,0:T(8,128)(2,1)S(1)}, bf16[256,1024]{1,0:T(8,128)(2,1)S(1)}, u32[]{:S(2)}, u32[]{:S(2)}) collective-permute-start(bf16[256,1024]{1,0:T(8,128)(2,1)S(1)} %pad_maximum_fusion.1), channel_id=1, source_target_pairs={{0,8},{8,0},{1,9},{9,1},{2,10},{10,2},{3,11},{11,3},{4,12},{12,4},... | collective-permute-start | bytes 1572872 | tf_op jit(solution)/shard_map/ppermute | solution.py:16
  22.0 15.5 %collective-permute-start.8 = (bf16[128,1024]{1,0:T(8,128)(2,1)}, bf16[128,1024]{1,0:T(8,128)(2,1)S(1)}, u32[]{:S(2)}, u32[]{:S(2)}) collective-permute-start(bf16[128,1024]{1,0:T(8,128)(2,1)} %collective-permute-done), channel_id=1, source_target_pairs={{0,1},{1,0},{2,3},{3,2},{4,5},{5,4},{6,7},{7,6},{8,9},{9,8},{10,11... | collective-permute-start | bytes 786440 | tf_op jit(solution)/shard_map/ppermute | solution.py:24
  23.5 15.0 %collective-permute-start.1 = (bf16[128,1024]{1,0:T(8,128)(2,1)}, bf16[128,1024]{1,0:T(8,128)(2,1)S(1)}, u32[]{:S(2)}, u32[]{:S(2)}) collective-permute-start(bf16[128,1024]{1,0:T(8,128)(2,1)} %collective-permute-done), channel_id=1, source_target_pairs={{0,2},{1,3},{2,0},{3,1},{4,6},{5,7},{6,4},{7,5},{8,10},{9,11},{10,... | collective-permute-start | bytes 786440 | tf_op jit(solution)/shard_map/ppermute | solution.py:24
  25.0 11.6 %collective-permute-start.6 = (bf16[128,1024]{1,0:T(8,128)(2,1)}, bf16[128,1024]{1,0:T(8,128)(2,1)S(1)}, u32[]{:S(2)}, u32[]{:S(2)}) collective-permute-start(bf16[128,1024]{1,0:T(8,128)(2,1)} %collective-permute-done.5), channel_id=1, source_target_pairs={{0,1},{1,0},{2,3},{3,2},{4,5},{5,4},{6,7},{7,6},{8,9},{9,8},{10,11... | collective-permute-start | bytes 786440 | tf_op jit(solution)/shard_map/ppermute | solution.py:24
  37.5 12.4 %collective-permute-start.9 = (bf16[256,1024]{1,0:T(8,128)(2,1)S(1)}, bf16[256,1024]{1,0:T(8,128)(2,1)S(1)}, u32[]{:S(2)}, u32[]{:S(2)}) collective-permute-start(bf16[256,1024]{1,0:T(8,128)(2,1)S(1)} %constant_dynamic-update-slice_fusion.2), channel_id=1, source_target_pairs={{0,8},{8,0},{1,9},{9,1},{2,10},{10,2},{3,11},{11,3},{4,12},{12,4},... | collective-permute-start | bytes 1572872 | tf_op jit(solution)/shard_map/ppermute | solution.py:16
  41.5 8.3 %collective-permute-start.10 = (bf16[128,1024]{1,0:T(8,128)(2,1)S(1)}, bf16[128,1024]{1,0:T(8,128)(2,1)S(1)}, u32[]{:S(2)}, u32[]{:S(2)}) collective-permute-start(bf16[128,1024]{1,0:T(8,128)(2,1)S(1)} %collective-permute-done.1), channel_id=1, source_target_pairs={{0,1},{1,0},{2,3},{3,2},{4,5},{5,4},{6,7},{7,6},{8,9},{9,8},{10,11... | collective-permute-start | bytes 786440 | tf_op jit(solution)/shard_map/ppermute | solution.py:24
  43.0 14.6 %collective-permute-start.44 = (bf16[256,512]{1,0:T(8,128)(2,1)S(1)}, bf16[256,512]{1,0:T(8,128)(2,1)S(1)}, u32[]{:S(2)}, u32[]{:S(2)}) collective-permute-start(bf16[256,512]{1,0:T(8,128)(2,1)S(1)} %constant_dynamic-slice_fusion), channel_id=1, source_target_pairs={{0,4},{1,5},{2,6},{3,7},{4,0},{5,1},{6,2},{7,3},{8,12},{9,13},{10,... | collective-permute-start | bytes 786440 | tf_op jit(solution)/shard_map/ppermute | solution.py:24
  52.6 8.4 %collective-permute-start.12 = (bf16[128,1024]{1,0:T(8,128)(2,1)S(1)}, bf16[128,1024]{1,0:T(8,128)(2,1)S(1)}, u32[]{:S(2)}, u32[]{:S(2)}) collective-permute-start(bf16[128,1024]{1,0:T(8,128)(2,1)S(1)} %slice.15), channel_id=1, source_target_pairs={{0,16},{16,0},{1,17},{17,1},{2,18},{18,2},{3,19},{19,3},{4,20},{20... | collective-permute-start | bytes 786440 | tf_op jit(solution)/shard_map/ppermute | solution.py:20
  54.1 9.2 %collective-permute-start.43 = (bf16[256,512]{1,0:T(8,128)(2,1)S(1)}, bf16[256,512]{1,0:T(8,128)(2,1)S(1)}, u32[]{:S(2)}, u32[]{:S(2)}) collective-permute-start(bf16[256,512]{1,0:T(8,128)(2,1)S(1)} %constant_dynamic-slice_fusion), channel_id=1, source_target_pairs={{0,2},{1,3},{2,0},{3,1},{4,6},{5,7},{6,4},{7,5},{8,10},{9,11},{10,... | collective-permute-start | bytes 786440 | tf_op jit(solution)/shard_map/ppermute | solution.py:24
  57.6 11.1 %collective-permute-start.45 = (bf16[256,512]{1,0:T(8,128)(2,1)S(1)}, bf16[256,512]{1,0:T(8,128)(2,1)S(1)}, u32[]{:S(2)}, u32[]{:S(2)}) collective-permute-start(bf16[256,512]{1,0:T(8,128)(2,1)S(1)} %collective-permute-done.44), channel_id=1, source_target_pairs={{0,2},{1,3},{2,0},{3,1},{4,6},{5,7},{6,4},{7,5},{8,10},{9,11},{10,... | collective-permute-start | bytes 786440 | tf_op jit(solution)/shard_map/ppermute | solution.py:24
  61.0 12.3 %collective-permute-start.15 = (bf16[128,1024]{1,0:T(8,128)(2,1)S(1)}, bf16[128,1024]{1,0:T(8,128)(2,1)S(1)}, u32[]{:S(2)}, u32[]{:S(2)}) collective-permute-start(bf16[128,1024]{1,0:T(8,128)(2,1)S(1)} %fusion.4.own), channel_id=1, source_target_pairs={{0,1},{1,0},{2,3},{3,2},{4,5},{5,4},{6,7},{7,6},{8,9},{9,8},{10,11... | collective-permute-start | bytes 786440 | tf_op jit(solution)/shard_map/ppermute | solution.py:24
  62.5 10.8 %collective-permute-start.13 = (bf16[128,1024]{1,0:T(8,128)(2,1)S(1)}, bf16[128,1024]{1,0:T(8,128)(2,1)S(1)}, u32[]{:S(2)}, u32[]{:S(2)}) collective-permute-start(bf16[128,1024]{1,0:T(8,128)(2,1)S(1)} %fusion.4.own), channel_id=1, source_target_pairs={{0,8},{8,0},{1,9},{9,1},{2,10},{10,2},{3,11},{11,3},{4,12},{12,4},... | collective-permute-start | bytes 786440 | tf_op jit(solution)/shard_map/ppermute | solution.py:16
  68.9 49.8 %collective-permute-start.49 = (bf16[4,256,512]{2,1,0:T(8,128)(2,1)S(1)}, bf16[4,256,512]{2,1,0:T(8,128)(2,1)S(1)}, u32[]{:S(2)}, u32[]{:S(2)}) collective-permute-start(bf16[4,256,512]{2,1,0:T(8,128)(2,1)S(1)} %pad_maximum_fusion.refs_4_), channel_id=1, source_target_pairs={{0,1},{1,0},{2,3},{3,2},{4,5},{5,4},{6,7},{7,6},{8,9},{9,8},{10,11... | collective-permute-start | bytes 3145736 | tf_op jit(solution)/shard_map/ppermute | solution.py:24
  69.5 16.0 %collective-permute-start.25 = (bf16[128,1024]{1,0:T(8,128)(2,1)S(1)}, bf16[128,1024]{1,0:T(8,128)(2,1)S(1)}, u32[]{:S(2)}, u32[]{:S(2)}) collective-permute-start(bf16[128,1024]{1,0:T(8,128)(2,1)S(1)} %fusion.4.own), channel_id=1, source_target_pairs={{0,4},{1,5},{2,6},{3,7},{4,0},{5,1},{6,2},{7,3},{8,12},{9,13},{10,... | collective-permute-start | bytes 786440 | tf_op jit(solution)/shard_map/ppermute | solution.py:24
  70.9 13.2 %collective-permute-start.18 = (bf16[128,1024]{1,0:T(8,128)(2,1)S(1)}, bf16[128,1024]{1,0:T(8,128)(2,1)S(1)}, u32[]{:S(2)}, u32[]{:S(2)}) collective-permute-start(bf16[128,1024]{1,0:T(8,128)(2,1)S(1)} %fusion.4.own), channel_id=1, source_target_pairs={{0,2},{1,3},{2,0},{3,1},{4,6},{5,7},{6,4},{7,5},{8,10},{9,11},{10,... | collective-permute-start | bytes 786440 | tf_op jit(solution)/shard_map/ppermute | solution.py:24
  73.3 12.2 %collective-permute-start.16 = (bf16[128,1024]{1,0:T(8,128)(2,1)S(1)}, bf16[128,1024]{1,0:T(8,128)(2,1)S(1)}, u32[]{:S(2)}, u32[]{:S(2)}) collective-permute-start(bf16[128,1024]{1,0:T(8,128)(2,1)S(1)} %collective-permute-done.15.own), channel_id=1, source_target_pairs={{0,8},{8,0},{1,9},{9,1},{2,10},{10,2},{3,11},{11,3},{4,12},{12,4},... | collective-permute-start | bytes 786440 | tf_op jit(solution)/shard_map/ppermute | solution.py:16
  78.6 41.8 %collective-permute-start.14 = (bf16[128,1024]{1,0:T(8,128)(2,1)S(1)}, bf16[128,1024]{1,0:T(8,128)(2,1)S(1)}, u32[]{:S(2)}, u32[]{:S(2)}) collective-permute-start(bf16[128,1024]{1,0:T(8,128)(2,1)S(1)} %get-tuple-element.74), channel_id=1, source_target_pairs={{0,8},{8,0},{1,9},{9,1},{2,10},{10,2},{3,11},{11,3},{4,12},{12,4},... | collective-permute-start | bytes 786440 | tf_op jit(solution)/shard_map/ppermute | solution.py:16
  84.1 15.5 %collective-permute-start.22 = (bf16[128,1024]{1,0:T(8,128)(2,1)S(1)}, bf16[128,1024]{1,0:T(8,128)(2,1)S(1)}, u32[]{:S(2)}, u32[]{:S(2)}) collective-permute-start(bf16[128,1024]{1,0:T(8,128)(2,1)S(1)} %collective-permute-done.18.own), channel_id=1, source_target_pairs={{0,1},{1,0},{2,3},{3,2},{4,5},{5,4},{6,7},{7,6},{8,9},{9,8},{10,11... | collective-permute-start | bytes 786440 | tf_op jit(solution)/shard_map/ppermute | solution.py:24
  85.5 26.9 %collective-permute-start.33 = (bf16[128,1024]{1,0:T(8,128)(2,1)S(1)}, bf16[128,1024]{1,0:T(8,128)(2,1)S(1)}, u32[]{:S(2)}, u32[]{:S(2)}) collective-permute-start(bf16[128,1024]{1,0:T(8,128)(2,1)S(1)} %collective-permute-done.25.own), channel_id=1, source_target_pairs={{0,2},{1,3},{2,0},{3,1},{4,6},{5,7},{6,4},{7,5},{8,10},{9,11},{10,... | collective-permute-start | bytes 786440 | tf_op jit(solution)/shard_map/ppermute | solution.py:24
  91.4 13.3 %collective-permute-start.17 = (bf16[128,1024]{1,0:T(8,128)(2,1)S(1)}, bf16[128,1024]{1,0:T(8,128)(2,1)S(1)}, u32[]{:S(2)}, u32[]{:S(2)}) collective-permute-start(bf16[128,1024]{1,0:T(8,128)(2,1)S(1)} %get-tuple-element.79), channel_id=1, source_target_pairs={{0,8},{8,0},{1,9},{9,1},{2,10},{10,2},{3,11},{11,3},{4,12},{12,4},... | collective-permute-start | bytes 786440 | tf_op jit(solution)/shard_map/ppermute | solution.py:16
  99.5 5.9 %collective-permute-start.23 = (bf16[128,1024]{1,0:T(8,128)(2,1)S(1)}, bf16[128,1024]{1,0:T(8,128)(2,1)S(1)}, u32[]{:S(2)}, u32[]{:S(2)}) collective-permute-start(bf16[128,1024]{1,0:T(8,128)(2,1)S(1)} %collective-permute-done.22.own), channel_id=1, source_target_pairs={{0,8},{8,0},{1,9},{9,1},{2,10},{10,2},{3,11},{11,3},{4,12},{12,4},... | collective-permute-start | bytes 786440 | tf_op jit(solution)/shard_map/ppermute | solution.py:16
  104.7 12.9 %collective-permute-start.30 = (bf16[128,1024]{1,0:T(8,128)(2,1)S(1)}, bf16[128,1024]{1,0:T(8,128)(2,1)S(1)}, u32[]{:S(2)}, u32[]{:S(2)}) collective-permute-start(bf16[128,1024]{1,0:T(8,128)(2,1)S(1)} %collective-permute-done.25.own), channel_id=1, source_target_pairs={{0,1},{1,0},{2,3},{3,2},{4,5},{5,4},{6,7},{7,6},{8,9},{9,8},{10,11... | collective-permute-start | bytes 786440 | tf_op jit(solution)/shard_map/ppermute | solution.py:24
  111.0 9.8 %collective-permute-start.20 = (bf16[128,1024]{1,0:T(8,128)(2,1)S(1)}, bf16[128,1024]{1,0:T(8,128)(2,1)S(1)}, u32[]{:S(2)}, u32[]{:S(2)}) collective-permute-start(bf16[128,1024]{1,0:T(8,128)(2,1)S(1)} %add_convert_fusion.7), channel_id=1, source_target_pairs={{0,1},{1,0},{2,3},{3,2},{4,5},{5,4},{6,7},{7,6},{8,9},{9,8},{10,11... | collective-permute-start | bytes 786440 | tf_op jit(solution)/shard_map/ppermute | solution.py:24
  112.5 5.9 %collective-permute-start.24 = (bf16[128,1024]{1,0:T(8,128)(2,1)S(1)}, bf16[128,1024]{1,0:T(8,128)(2,1)S(1)}, u32[]{:S(2)}, u32[]{:S(2)}) collective-permute-start(bf16[128,1024]{1,0:T(8,128)(2,1)S(1)} %get-tuple-element.90), channel_id=1, source_target_pairs={{0,8},{8,0},{1,9},{9,1},{2,10},{10,2},{3,11},{11,3},{4,12},{12,4},... | collective-permute-start | bytes 786440 | tf_op jit(solution)/shard_map/ppermute | solution.py:16
  117.7 8.8 %collective-permute-start.34 = (bf16[128,1024]{1,0:T(8,128)(2,1)S(1)}, bf16[128,1024]{1,0:T(8,128)(2,1)S(1)}, u32[]{:S(2)}, u32[]{:S(2)}) collective-permute-start(bf16[128,1024]{1,0:T(8,128)(2,1)S(1)} %collective-permute-done.33.own), channel_id=1, source_target_pairs={{0,1},{1,0},{2,3},{3,2},{4,5},{5,4},{6,7},{7,6},{8,9},{9,8},{10,11... | collective-permute-start | bytes 786440 | tf_op jit(solution)/shard_map/ppermute | solution.py:24
  118.4 8.1 %collective-permute-start.31 = (bf16[128,1024]{1,0:T(8,128)(2,1)S(1)}, bf16[128,1024]{1,0:T(8,128)(2,1)S(1)}, u32[]{:S(2)}, u32[]{:S(2)}) collective-permute-start(bf16[128,1024]{1,0:T(8,128)(2,1)S(1)} %collective-permute-done.30.own), channel_id=1, source_target_pairs={{0,8},{8,0},{1,9},{9,1},{2,10},{10,2},{3,11},{11,3},{4,12},{12,4},... | collective-permute-start | bytes 786440 | tf_op jit(solution)/shard_map/ppermute | solution.py:16
  118.7 26.2 %collective-permute-start.46 = (bf16[4,256,512]{2,1,0:T(8,128)(2,1)S(1)}, bf16[4,256,512]{2,1,0:T(8,128)(2,1)}, u32[]{:S(2)}, u32[]{:S(2)}) collective-permute-start(bf16[4,256,512]{2,1,0:T(8,128)(2,1)S(1)} %pad_maximum_fusion.refs_4_), channel_id=1, source_target_pairs={{0,16},{16,0},{1,17},{17,1},{2,18},{18,2},{3,19},{19,3},{4,20},{20... | collective-permute-start | bytes 3145736 | tf_op jit(solution)/shard_map/ppermute | solution.py:20
  120.3 46.3 %collective-permute-start.50 = (bf16[4,256,512]{2,1,0:T(8,128)(2,1)S(1)}, bf16[4,256,512]{2,1,0:T(8,128)(2,1)}, u32[]{:S(2)}, u32[]{:S(2)}) collective-permute-start(bf16[4,256,512]{2,1,0:T(8,128)(2,1)S(1)} %collective-permute-done.49.refs_8_), channel_id=1, source_target_pairs={{0,16},{16,0},{1,17},{17,1},{2,18},{18,2},{3,19},{19,3},{4,20},{20... | collective-permute-start | bytes 3145736 | tf_op jit(solution)/shard_map/ppermute | solution.py:20
  120.8 11.5 %collective-permute-start.21 = (bf16[128,1024]{1,0:T(8,128)(2,1)S(1)}, bf16[128,1024]{1,0:T(8,128)(2,1)S(1)}, u32[]{:S(2)}, u32[]{:S(2)}) collective-permute-start(bf16[128,1024]{1,0:T(8,128)(2,1)S(1)} %get-tuple-element.85), channel_id=1, source_target_pairs={{0,8},{8,0},{1,9},{9,1},{2,10},{10,2},{3,11},{11,3},{4,12},{12,4},... | collective-permute-start | bytes 786440 | tf_op jit(solution)/shard_map/ppermute | solution.py:16
  126.4 15.3 %collective-permute-start.38 = (bf16[128,1024]{1,0:T(8,128)(2,1)S(1)}, bf16[128,1024]{1,0:T(8,128)(2,1)S(1)}, u32[]{:S(2)}, u32[]{:S(2)}) collective-permute-start(bf16[128,1024]{1,0:T(8,128)(2,1)S(1)} %collective-permute-done.33.own), channel_id=1, source_target_pairs={{0,8},{8,0},{1,9},{9,1},{2,10},{10,2},{3,11},{11,3},{4,12},{12,4},... | collective-permute-start | bytes 786440 | tf_op jit(solution)/shard_map/ppermute | solution.py:16
  132.2 12.7 %collective-permute-start.29 = (bf16[128,1024]{1,0:T(8,128)(2,1)S(1)}, bf16[128,1024]{1,0:T(8,128)(2,1)S(1)}, u32[]{:S(2)}, u32[]{:S(2)}) collective-permute-start(bf16[128,1024]{1,0:T(8,128)(2,1)S(1)} %get-tuple-element.96), channel_id=1, source_target_pairs={{0,8},{8,0},{1,9},{9,1},{2,10},{10,2},{3,11},{11,3},{4,12},{12,4},... | collective-permute-start | bytes 786440 | tf_op jit(solution)/shard_map/ppermute | solution.py:16
  132.3 8.7 %collective-permute-start.27 = (bf16[128,1024]{1,0:T(8,128)(2,1)S(1)}, bf16[128,1024]{1,0:T(8,128)(2,1)S(1)}, u32[]{:S(2)}, u32[]{:S(2)}) collective-permute-start(bf16[128,1024]{1,0:T(8,128)(2,1)S(1)} %add_convert_fusion.5), channel_id=1, source_target_pairs={{0,1},{1,0},{2,3},{3,2},{4,5},{5,4},{6,7},{7,6},{8,9},{9,8},{10,11... | collective-permute-start | bytes 786440 | tf_op jit(solution)/shard_map/ppermute | solution.py:24
  141.0 44.2 %collective-permute-start.47 = (bf16[4,256,512]{2,1,0:T(8,128)(2,1)S(1)}, bf16[4,256,512]{2,1,0:T(8,128)(2,1)S(1)}, u32[]{:S(2)}, u32[]{:S(2)}) collective-permute-start(bf16[4,256,512]{2,1,0:T(8,128)(2,1)S(1)} %pad_maximum_fusion.refs_4_), channel_id=1, source_target_pairs={{0,8},{8,0},{1,9},{9,1},{2,10},{10,2},{3,11},{11,3},{4,12},{12,4},... | collective-permute-start | bytes 3145736 | tf_op jit(solution)/shard_map/ppermute | solution.py:16
  141.8 47.7 %collective-permute-start.51 = (bf16[4,256,512]{2,1,0:T(8,128)(2,1)S(1)}, bf16[4,256,512]{2,1,0:T(8,128)(2,1)S(1)}, u32[]{:S(2)}, u32[]{:S(2)}) collective-permute-start(bf16[4,256,512]{2,1,0:T(8,128)(2,1)S(1)} %collective-permute-done.49.refs_8_), channel_id=1, source_target_pairs={{0,8},{8,0},{1,9},{9,1},{2,10},{10,2},{3,11},{11,3},{4,12},{12,4},... | collective-permute-start | bytes 3145736 | tf_op jit(solution)/shard_map/ppermute | solution.py:16
  144.8 21.9 %collective-permute-start.40 = (bf16[128,1024]{1,0:T(8,128)(2,1)S(1)}, bf16[128,1024]{1,0:T(8,128)(2,1)S(1)}, u32[]{:S(2)}, u32[]{:S(2)}) collective-permute-start(bf16[128,1024]{1,0:T(8,128)(2,1)S(1)} %get-tuple-element.112), channel_id=1, source_target_pairs={{0,8},{8,0},{1,9},{9,1},{2,10},{10,2},{3,11},{11,3},{4,12},{12,4},... | collective-permute-start | bytes 786440 | tf_op jit(solution)/shard_map/ppermute | solution.py:16
  144.8 22.4 %collective-permute-start.32 = (bf16[128,1024]{1,0:T(8,128)(2,1)S(1)}, bf16[128,1024]{1,0:T(8,128)(2,1)S(1)}, u32[]{:S(2)}, u32[]{:S(2)}) collective-permute-start(bf16[128,1024]{1,0:T(8,128)(2,1)S(1)} %get-tuple-element.101), channel_id=1, source_target_pairs={{0,8},{8,0},{1,9},{9,1},{2,10},{10,2},{3,11},{11,3},{4,12},{12,4},... | collective-permute-start | bytes 786440 | tf_op jit(solution)/shard_map/ppermute | solution.py:16
  166.7 24.5 %collective-permute-start.48 = (bf16[4,256,512]{2,1,0:T(8,128)(2,1)}, bf16[4,256,512]{2,1,0:T(8,128)(2,1)}, u32[]{:S(2)}, u32[]{:S(2)}) collective-permute-start(bf16[4,256,512]{2,1,0:T(8,128)(2,1)} %collective-permute-done.46.refs_5_), channel_id=1, source_target_pairs={{0,8},{8,0},{1,9},{9,1},{2,10},{10,2},{3,11},{11,3},{4,12},{12,4},... | collective-permute-start | bytes 3145736 | tf_op jit(solution)/shard_map/ppermute | solution.py:16
  167.2 44.6 %collective-permute-start.52 = (bf16[4,256,512]{2,1,0:T(8,128)(2,1)}, bf16[4,256,512]{2,1,0:T(8,128)(2,1)}, u32[]{:S(2)}, u32[]{:S(2)}) collective-permute-start(bf16[4,256,512]{2,1,0:T(8,128)(2,1)} %collective-permute-done.50.refs_9_), channel_id=1, source_target_pairs={{0,8},{8,0},{1,9},{9,1},{2,10},{10,2},{3,11},{11,3},{4,12},{12,4},... | collective-permute-start | bytes 3145736 | tf_op jit(solution)/shard_map/ppermute | solution.py:16
  168.5 8.3 %collective-permute-start.41 = (bf16[128,1024]{1,0:T(8,128)(2,1)S(1)}, bf16[128,1024]{1,0:T(8,128)(2,1)S(1)}, u32[]{:S(2)}, u32[]{:S(2)}) collective-permute-start(bf16[128,1024]{1,0:T(8,128)(2,1)S(1)} %add_convert_fusion.1), channel_id=1, source_target_pairs={{0,1},{1,0},{2,3},{3,2},{4,5},{5,4},{6,7},{7,6},{8,9},{9,8},{10,11... | collective-permute-start | bytes 786440 | tf_op jit(solution)/shard_map/ppermute | solution.py:24
  176.8 7.5 %collective-permute-start.36 = (bf16[128,1024]{1,0:T(8,128)(2,1)S(1)}, bf16[128,1024]{1,0:T(8,128)(2,1)S(1)}, u32[]{:S(2)}, u32[]{:S(2)}) collective-permute-start(bf16[128,1024]{1,0:T(8,128)(2,1)S(1)} %add_convert_fusion.3), channel_id=1, source_target_pairs={{0,1},{1,0},{2,3},{3,2},{4,5},{5,4},{6,7},{7,6},{8,9},{9,8},{10,11... | collective-permute-start | bytes 786440 | tf_op jit(solution)/shard_map/ppermute | solution.py:24
  184.4 7.7 %collective-permute-start.28 = (bf16[128,1024]{1,0:T(8,128)(2,1)}, bf16[128,1024]{1,0:T(8,128)(2,1)}, u32[]{:S(2)}, u32[]{:S(2)}) collective-permute-start(bf16[128,1024]{1,0:T(8,128)(2,1)} %add_convert_fusion.4), channel_id=1, source_target_pairs={{0,2},{1,3},{2,0},{3,1},{4,6},{5,7},{6,4},{7,5},{8,10},{9,11},{10,... | collective-permute-start | bytes 786440 | tf_op jit(solution)/shard_map/ppermute | solution.py:24
  186.2 14.8 %collective-permute-start.42 = (bf16[128,1024]{1,0:T(8,128)(2,1)}, bf16[128,1024]{1,0:T(8,128)(2,1)}, u32[]{:S(2)}, u32[]{:S(2)}) collective-permute-start(bf16[128,1024]{1,0:T(8,128)(2,1)} %add_convert_fusion), channel_id=1, source_target_pairs={{0,6},{1,7},{2,4},{3,5},{4,2},{5,3},{6,0},{7,1},{8,14},{9,15},{10,... | collective-permute-start | bytes 786440 | tf_op jit(solution)/shard_map/ppermute | solution.py:24
  190.5 21.3 %collective-permute-start.37 = (bf16[128,1024]{1,0:T(8,128)(2,1)}, bf16[128,1024]{1,0:T(8,128)(2,1)}, u32[]{:S(2)}, u32[]{:S(2)}) collective-permute-start(bf16[128,1024]{1,0:T(8,128)(2,1)} %add_convert_fusion.2), channel_id=1, source_target_pairs={{0,4},{1,5},{2,6},{3,7},{4,0},{5,1},{6,2},{7,3},{8,12},{9,13},{10,... | collective-permute-start | bytes 786440 | tf_op jit(solution)/shard_map/ppermute | solution.py:24
  (14 other events, 96.4 us)

commit v4 on v1

v4 whole, which is shorter than its diff:
```python
import functools

import jax
import jax.numpy as jnp
from jax import lax
from jax.experimental import pallas as pl
from jax.experimental.pallas import tpu as pltpu
from jax.sharding import PartitionSpec as P

route_scale = 2.5
mebi = 1024 * 1024
in_vmem = pl.BlockSpec(memory_space=pltpu.VMEM)
in_smem = pl.BlockSpec(memory_space=pltpu.SMEM)
anywhere = pl.BlockSpec(memory_space=pl.ANY)


def after(value, *others):
    return lax.optimization_barrier((value, *others))[0]


def join(*values):
    return lax.optimization_barrier(values)


def swap_cores(array):
    return lax.ppermute(array, "grp", [(0, 1), (1, 0)])


def swap_reps(array):
    return lax.ppermute(array, "rep", [(i, i ^ 1) for i in range(lax.axis_size("rep"))])


def swap_ep(array, mask):
    return lax.ppermute(array, "ep", [(i, i ^ mask) for i in range(lax.axis_size("ep"))])


def first_steps(piece, steps):
    return {0: piece} | {k: swap_ep(piece, 2 * k) for k in range(1, steps) if k & (k - 1) == 0}


def dense_weights(expert_ids, route_scores, expert_count):
    sigmoids = jax.nn.sigmoid(route_scores)
    weights = (route_scale * sigmoids / jnp.sum(sigmoids, axis=1, keepdims=True)).astype(
        jnp.bfloat16
    )
    named = expert_ids[None, :, :] == jnp.arange(expert_count, dtype=jnp.int32)[:, None, None]
    return jnp.sum(jnp.where(named, weights.astype(jnp.float32)[None, :, :], 0.0), axis=2)


def columns_kernel(ep_count, quarter, where, tokens, kept, given):
    place, side, group = where[0], where[1], where[2]
    for offset in range(ep_count):
        for core in range(2):
            to = pl.ds(((offset // 2 * 2 + core) * 2 + offset % 2) * quarter, quarter)
            shard = (place ^ offset) * 4 + (group ^ core)
            for half, part in ((side, kept), (1 - side, given)):
                start = pl.multiple_of((shard + 2 * half) * quarter, quarter)
                part[:, to] = tokens[:, pl.ds(start, quarter)]


def split_columns(tokens, ep_count, quarter, place, side, group):
    count = tokens.shape[0]
    if quarter % 128 == 0:
        half = jax.ShapeDtypeStruct((count, 2 * ep_count * quarter), tokens.dtype)
        return pl.pallas_call(
            functools.partial(columns_kernel, ep_count, quarter),
            out_shape=(half, half),
            in_specs=[in_smem, in_vmem],
            out_specs=(in_vmem, in_vmem),
            compiler_params=pltpu.CompilerParams(vmem_limit_bytes=8 * mebi),
            name="split_columns",
        )(jnp.stack([place, side, group]).astype(jnp.int32), tokens)
    cut = tokens.reshape(count, ep_count, 2, 2, quarter)
    parts = [], []
    for step in range(ep_count // 2):
        for core in (group, 1 - group):
            for offset in (2 * step, 2 * step + 1):
                for half, part in zip((side, 1 - side), parts):
                    start = (0, place ^ offset, half, core, 0)
                    part.append(lax.dynamic_slice(cut, start, (count, 1, 1, 1, quarter)))
    kept, given = [jnp.stack(part, axis=1).reshape(count, -1) for part in parts]
    return kept, given


def down_kernel(steps, last, *refs):
    (kept, given), blocks = refs[:2], refs[2 : 2 + 4 * len(steps)]
    so_far, results = (refs[-3], refs[-2:]) if last else (None, refs[-1:])
    depth = 2 * blocks[0].shape[0]
    width = 256
    for start in range(0, blocks[0].shape[1], width):
        columns = slice(start, start + width)
        total = 0.0 if so_far is None else so_far[:, columns]
        for i, step in enumerate(steps):
            for core in range(2):
                inner = pl.ds((2 * step + core) * depth, depth)
                rows = jnp.concatenate([kept[:, inner], given[:, inner]], axis=0)
                near, far = blocks[4 * i + 2 * core], blocks[4 * i + 2 * core + 1]
                block = jnp.concatenate([near[:, columns], far[:, columns]], axis=0)
                total += jnp.dot(rows, block, preferred_element_type=jnp.float32)
        if last:
            count = kept.shape[0]
            results[0][:, columns] = total[:count]
            results[1][:, columns] = total[count:].astype(jnp.bfloat16)
        else:
            results[0][:, columns] = total


def down_project(steps, kept, given, blocks, so_far=None):
    count, inner = kept.shape
    latent_width = blocks[0].shape[1]
    operands = (kept, given, *blocks) + (() if so_far is None else (so_far,))
    if so_far is None:
        shapes = (jax.ShapeDtypeStruct((2 * count, latent_width), jnp.float32),)
    else:
        shapes = (
            jax.ShapeDtypeStruct((count, latent_width), jnp.float32),
            jax.ShapeDtypeStruct((count, latent_width), jnp.bfloat16),
        )
    return pl.pallas_call(
        functools.partial(down_kernel, steps, so_far is not None),
        out_shape=shapes,
        in_specs=[in_vmem] * len(operands),
        out_specs=(in_vmem,) * len(shapes),
        compiler_params=pltpu.CompilerParams(vmem_limit_bytes=16 * mebi),
        cost_estimate=pl.CostEstimate(
            flops=16 * len(steps) * count * blocks[0].shape[0] * latent_width,
            bytes_accessed=2 * len(blocks) * blocks[0].shape[0] * latent_width,
            transcendentals=0,
        ),
        name="down_project",
    )(*operands)


def expert_kernel(positions, *refs):
    owns, others, scales = [refs[i * positions : (i + 1) * positions] for i in range(3)]
    gate, up, out = refs[3 * positions : 3 * positions + 3]
    sums = refs[3 * positions + 3 : 5 * positions + 3]
    rows, hidden, held = refs[-3:]
    count = owns[0].shape[0]
    width = 256
    for i in range(positions):
        rows[2 * i * count : (2 * i + 1) * count] = owns[i][...]
        rows[(2 * i + 1) * count : (2 * i + 2) * count] = others[i][...]

    def products(start):
        columns = pl.ds(pl.multiple_of(start, width), width)
        return (
            jnp.dot(rows[...], gate[0, :, columns], preferred_element_type=jnp.float32),
            jnp.dot(rows[...], up[0, :, columns], preferred_element_type=jnp.float32),
        )

    def activate(gate_value, up_value, start):
        value = gate_value / (1.0 + jnp.exp(-gate_value)) * up_value
        hidden[:, pl.ds(pl.multiple_of(start, width), width)] = value.astype(jnp.bfloat16)

    hidden_width = gate.shape[2]
    held[0], held[1] = products(0)

    def step(i, carry):
        start = i * 2 * width
        first = products(start + width)
        activate(held[0], held[1], start)
        second = products(start + 2 * width)
        activate(*first, start + width)
        held[0], held[1] = second
        return carry

    steps = hidden_width // (2 * width)
    lax.fori_loop(0, steps - 1, step, 0)
    last = products(hidden_width - width)
    activate(held[0], held[1], hidden_width - 2 * width)
    activate(*last, hidden_width - width)

    def finish(i, carry):
        columns = pl.ds(pl.multiple_of(i * width, width), width)
        value = jnp.dot(hidden[...], out[0, :, columns], preferred_element_type=jnp.float32)
        for j in range(positions):
            scaled = value[2 * j * count : 2 * (j + 1) * count] * scales[j][:, :1]
            sums[2 * j][:, columns] = scaled[:count].astype(jnp.bfloat16)
            sums[2 * j + 1][:, columns] = scaled[count:].astype(jnp.bfloat16)
        return carry

    lax.fori_loop(0, out.shape[2] // width, finish, 0)


def expert_apply(owns, others, scales, gate_weight, up_weight, out_weight):
    positions = len(owns)
    count, latent_width = owns[0].shape
    hidden_width = gate_weight.shape[2]
    rows = 2 * positions * count
    sums = jax.ShapeDtypeStruct((count, latent_width), jnp.bfloat16)
    return pl.pallas_call(
        functools.partial(expert_kernel, positions),
        out_shape=(sums,) * (2 * positions),
        in_specs=[in_vmem] * (3 * positions + 3),
        out_specs=(in_vmem,) * (2 * positions),
        scratch_shapes=[
            pltpu.VMEM((rows, latent_width), jnp.bfloat16),
            pltpu.VMEM((rows, hidden_width), jnp.bfloat16),
            pltpu.VMEM((2, rows, 256), jnp.float32),
        ],
        compiler_params=pltpu.CompilerParams(vmem_limit_bytes=16 * mebi),
        cost_estimate=pl.CostEstimate(
            flops=6 * rows * latent_width * hidden_width,
            bytes_accessed=4 * rows * latent_width,
            transcendentals=rows * hidden_width,
        ),
        name="expert",
    )(*owns, *others, *scales, gate_weight, up_weight, out_weight)


def project_kernel(rep_count, where, *refs):
    terms, refs = refs[:-8], refs[-8:]
    mine, swapped, layer_out, combined, held, blocks, read_sems, sems = refs
    inner, width = mine.shape[1:]
    ep_count = mine.shape[0] // rep_count
    group = where[0]

    def read(e, rep):
        shard = rep * ep_count + e
        return pltpu.make_async_copy(mine.at[shard], held.at[shard], read_sems.at[shard])

    for e in range(ep_count):
        for rep in range(rep_count):
            read(e, rep).start()
    total = terms[0][...].astype(jnp.float32)
    for term in terms[1:]:
        total += term[...].astype(jnp.float32)
    combined[...] = total.astype(jnp.bfloat16)

    def sent(e):
        columns = pl.ds(e * width, width)
        return pltpu.make_async_copy(blocks.at[:, columns], layer_out.at[:, columns], sems.at[e])

    for e in range(ep_count):
        value = 0.0
        for rep in range(rep_count):
            read(e, rep).wait()
            for core, array in ((1 - group, swapped), (group, held)):
                columns = pl.ds(pl.multiple_of((2 * rep + core) * inner, inner), inner)
                value += jnp.dot(
                    combined[:, columns],
                    array[rep * ep_count + e],
                    preferred_element_type=jnp.float32,
                )
        blocks[:, e * width : (e + 1) * width] = value.astype(jnp.bfloat16)
        sent(e).start()
    for e in range(ep_count):
        sent(e).wait()


def project(terms, mine, swapped, rep_count, group):
    count, latent_width = terms[0].shape
    shards, inner, width = mine.shape
    ep_count = shards // rep_count
    return pl.pallas_call(
        functools.partial(project_kernel, rep_count),
        in_specs=[in_smem] + [in_vmem] * len(terms) + [anywhere, in_vmem],
        out_specs=anywhere,
        out_shape=jax.ShapeDtypeStruct((count, ep_count * width), jnp.bfloat16),
        scratch_shapes=[
            pltpu.VMEM((count, latent_width), jnp.bfloat16),
            pltpu.VMEM(mine.shape, mine.dtype),
            pltpu.VMEM((count, ep_count * width), jnp.bfloat16),
            pltpu.SemaphoreType.DMA((shards,)),
            pltpu.SemaphoreType.DMA((ep_count,)),
        ],
        compiler_params=pltpu.CompilerParams(vmem_limit_bytes=16 * mebi),
        cost_estimate=pl.CostEstimate(
            flops=2 * count * latent_width * ep_count * width,
            bytes_accessed=2 * latent_width * ep_count * width,
            transcendentals=0,
        ),
        name="project",
    )(group.reshape(1).astype(jnp.int32), *terms, mine, swapped)


def body(
    tokens, expert_ids, route_scores, down_latent, gate_weight, up_weight, out_weight, up_latent
):
    rep_count = lax.axis_size("rep")
    group_count = lax.axis_size("grp")
    ep_count = lax.axis_size("ep")
    expert_count = group_count * ep_count * gate_weight.shape[0]
    rep, group, place = lax.axis_index("rep"), lax.axis_index("grp"), lax.axis_index("ep")
    side = rep % 2
    token_count = tokens.shape[0]
    latent_width = down_latent.shape[1]
    steps = ep_count // 2

    quarter = down_latent.shape[0] // 4
    kept, given = split_columns(tokens, ep_count, quarter, place, side, group)
    shard = after(down_latent, kept)

    def own_piece(core):
        start = (2 * side + core) * quarter
        return lax.dynamic_slice_in_dim(shard, start, quarter, 0)

    taken = swap_reps(given)
    near = first_steps(own_piece(group), steps)
    far = {0: swap_ep(near[0], 1)}
    weights = dense_weights(after(expert_ids, kept), route_scores, expert_count)
    near[1], far[0], weights = join(near[1], far[0], weights)
    far[1] = swap_ep(near[1], 1)
    others = {k: near[k] for k in near if k > 1}
    near[1], taken, *arrived = join(near[1], taken, *others.values())
    near.update(zip(others, arrived))

    scale = lax.all_to_all(weights, ("grp", "ep"), split_axis=0, concat_axis=0, tiled=True)
    scale = scale.reshape(group_count, ep_count, token_count)

    def scale_of(offset):
        rows = [
            lax.dynamic_slice(scale, (core, place ^ offset, 0), (1, 1, token_count))
            for core in (group, 1 - group)
        ]
        rows = jnp.concatenate(rows, axis=0).reshape(2 * token_count, 1)
        return jnp.broadcast_to(rows, (2 * token_count, 128))

    last = steps - 1
    for k in range(2, steps):
        if k & (k - 1):
            low = k & -k
            near[k] = swap_ep(near[k ^ low], 2 * low)
        if k == last:
            near[k], scale, far[1] = join(near[k], scale, far[1])
        far[k] = swap_ep(near[k], 1)
    scales = [scale_of(offset) for offset in range(ep_count)]
    blocks = []
    for k in range(steps):
        other = own_piece(1 - group) if k == 0 else swap_cores(near[k])
        blocks.append((near[k], far[k], other, swap_cores(far[k])))
    early = list(range(last))
    (partial,) = down_project(early, kept, taken, [b for k in early for b in blocks[k]])
    late = [after(blocks[-1][0], partial, *scales), *blocks[-1][1:]]
    own_part, sent_part = down_project([last], kept, taken, late, partial)
    latent = (own_part + swap_reps(sent_part).astype(jnp.float32)).astype(jnp.bfloat16)

    inner = latent_width // (2 * rep_count)
    up_piece = lax.dynamic_slice_in_dim(up_latent, (2 * rep + group) * inner, inner, 0)
    mine = lax.all_gather(after(up_piece, sent_part), ("rep", "ep"), axis=0)

    near = first_steps(latent, steps)
    far = {0: swap_ep(latent, 1)}
    away, sent, pairs, back = {}, {}, {}, {}

    def run(which, coming):
        owns = [(near, far)[y][k] for k, y in which]
        operands = owns + [swap_cores(own) for own in owns]
        if back:
            operands = join(*operands, *sent.values(), *pairs.values(), *[b[1] for b in back.values()])
        count = len(which)
        sums = expert_apply(
            operands[:count],
            operands[count : 2 * count],
            [scales[2 * k + y] for k, y in which],
            gate_weight,
            up_weight,
            out_weight,
        )
        names = [(table, key) for table, keys in coming for key in keys]
        sums = join(*sums, *[table[key] for table, key in names])
        for (table, key), value in zip(names, sums[2 * count :]):
            table[key] = value
        for i, (k, y) in enumerate(which):
            back[k, y] = sums[2 * i], swap_cores(sums[2 * i + 1])
            if y == 1:
                sent[k] = chip_sum(k, 1).astype(jnp.bfloat16)
        for k in list(sent):
            if k not in away:
                away[k] = swap_ep(sent[k], 1)

    def chip_sum(k, y):
        own, swapped = back[k, y]
        return own.astype(jnp.float32) + swapped.astype(jnp.float32)

    def pair_sum(k):
        return (chip_sum(k, 0) + away[k].astype(jnp.float32)).astype(jnp.bfloat16)

    calls = [[(0, 0)]] + [[(k - 1, 1), (k, 0)] for k in range(1, last)]
    calls += [[(last - 1, 1), (last, 1)], [(last, 0)]]
    coming = [(near, [k for k in near if k]), (far, [0])]
    for which in calls:
        returning = [k for k in away if k not in pairs]
        run(which, coming + [(away, returning)])
        for k in returning:
            if (k, 0) in back:
                pairs[k] = pair_sum(k)
        new_far = [k for k in near if k not in far]
        new_near = [
            k for k in range(1, steps) if k not in near and k ^ (k & -k) in near
        ]
        for k in new_far:
            far[k] = swap_ep(near[k], 1)
        for k in new_near:
            near[k] = swap_ep(near[k ^ (k & -k)], 2 * (k & -k))
        coming = [(near, new_near), (far, new_far)]
    mine = after(mine, back[last, 0][0])
    swapped = swap_cores(mine)
    for k in range(steps):
        if k not in pairs:
            pairs[k] = pair_sum(k)
    terms = [pairs[0]] + [swap_ep(pairs[k], 2 * k) for k in range(1, steps)]
    return project(terms, mine, swapped, rep_count, group)


def solution(mesh):
    in_specs = (
        P(("rep", "grp", "ep"), None),
        P(("rep", "grp", "ep"), None),
        P(("rep", "grp", "ep"), None),
        P("ep", None),
        P(("grp", "ep"), None, None),
        P(("grp", "ep"), None, None),
        P(("grp", "ep"), None, None),
        P(None, "ep"),
    )
    out_specs = P(("rep", "grp", "ep"), None)
    return jax.shard_map(body, mesh=mesh, in_specs=in_specs, out_specs=out_specs, check_vma=False)
```

time: 311 us -> 197 us (0.63); the launches traced: 311 us -> 194 us
  waiting for transfers between devices: 192 us -> 69.1 us
  matrix products: 66.2 us -> 0 us
  starting transfers between devices: 0.7 us -> 47 us
  Pallas kernels: 0 us -> 45 us
  blocking collectives: 32 us -> 0 us
  local copies, waits for them, and re-layouts: 6.63 us -> 15.4 us
  other arithmetic: 0.15 us -> 3.63 us
    all_gather x3 -> x1, waiting for transfers between devices: 125 us -> 0.01 us  [body(): mine = lax.all_gather(after(up_piece, sent_part), ('rep', 'ep'), axis=0)]
    dot_general x8 -> x0, matrix products: 66.2 us -> none  [the longest x2 33.8 us: expert_apply(): out = jnp.dot(hidden, out_weight, preferred_element_type=jnp.float32)]
    reduce_scatter x1 -> x0, waiting for transfers between devices: 64.6 us -> none  [body(): combined = lax.psum_scatter(both, 'ep', scatter_dimension=0, tiled=True)]
    ppermute x0 -> x23, waiting for transfers between devices: none -> 63.4 us  [the longest x21 55 us: swap_ep(): lax.ppermute(array, 'ep', [(i, i ^ mask) for i in range(lax.axis_size('ep...]
    pallas_call x0 -> x9, Pallas kernels: none -> 45 us  [the longest x5 36.4 us: expert_apply(): pl.pallas_call(functools.partial(expert_kernel, positions), out_shape=(su...]
    ppermute x0 -> x23, starting transfers between devices: none -> 37.5 us  [the longest x21 34 us: swap_ep(): lax.ppermute(array, 'ep', [(i, i ^ mask) for i in range(lax.axis_size('ep...]
    all_gather x1 -> x0, blocking collectives: 32 us -> none  [body(): weights = lax.all_gather(weights, ('grp', 'ep'), axis=0, tiled=True)]
    unnamed x15 -> x22, local copies, waits for them, and re-layouts: 2.87 us -> 10.8 us
  transfers between devices with their start and end apart: 8 -> 49, of which waited for: 4 -> 19; matrix products, arithmetic and copies ran while one was open for 20% -> 4% of each run, Pallas kernels for 0% -> 20%
where the time goes in v4:
time: 197 us; the launch traced here: 194 us
  waiting for transfers between devices  69.1 us (35%)
  starting transfers between devices  47 us (24%)
  Pallas kernels  45 us (23%)
  local copies, waits for them, and re-layouts  15.4 us (8%)
  between operations  13.8 us (7%)
  other arithmetic  3.63 us (2%)
    ppermute x21, waiting for transfers between devices, swap_ep(): lax.ppermute(array, 'ep', [(i, i ^ mask) for i in range(lax.axis_size('ep...  55 us
    pallas_call x5, Pallas kernels, expert_apply(): pl.pallas_call(functools.partial(expert_kernel, positions), out_shape=(su...  36.4 us
    ppermute x21, starting transfers between devices, swap_ep(): lax.ppermute(array, 'ep', [(i, i ^ mask) for i in range(lax.axis_size('ep...  34 us
    unnamed x22, local copies, waits for them, and re-layouts  10.8 us
    ppermute x2, waiting for transfers between devices, swap_reps(): lax.ppermute(array, 'rep', [(i, i ^ 1) for i in range(lax.axis_size('rep'...  8.39 us
    ppermute x24, starting transfers between devices, swap_cores(): return lax.ppermute(array, 'grp', [(0, 1), (1, 0)])  5.34 us
    pallas_call x1, Pallas kernels, project(): pl.pallas_call(functools.partial(project_kernel, rep_count), in_specs=[in...  4.17 us
    all_to_all x1, starting transfers between devices, body(): lax.all_to_all(weights, ('grp', 'ep'), split_axis=0, concat_axis=0, tiled...  4.14 us
  transfers between devices with their start and end apart: 49, of which 19 were waited for; matrix products, arithmetic and copies ran while one was open for 4% of the time, Pallas kernels for 20%

profile of v4, /device:TPU:0, one launch (start us, length us, event | category | flops | bytes accessed | tf_op | source)
XLA Modules:
  0.0 194.0 jit_solution(99050752618903224)
XLA Ops:
  6.6 1.3 copy-done.6
  7.9 1.6 split_columns.1
  9.5 2.9 %collective-permute-start.2 = (bf16[128,2048]{1,0:T(8,128)(2,1)}, bf16[128,2048]{1,0:T(8,128)(2,1)S(1)}, u32[]{:S(2)}, u32[]{:S(2)}) collective-permute-start(bf16[128,2048]{1,0:T(8,128)(2,1)} %get-tuple-element.84), channel_id=1, source_target_pairs={{0,16},{16,0},{1,17},{17,1},{2,18},{18,2},{3,19},{19,3},{4,20},{20... | collective-permute-start | bytes 1572872 | tf_op jit(solution)/shard_map/ppermute | solution.py:30
  12.5 1.1 constant_dynamic-slice_fusion.17
  13.5 2.7 %collective-permute-start.3 = (bf16[128,1024]{1,0:T(8,128)(2,1)S(1)}, bf16[128,1024]{1,0:T(8,128)(2,1)S(1)}, u32[]{:S(2)}, u32[]{:S(2)}) collective-permute-start(bf16[128,1024]{1,0:T(8,128)(2,1)S(1)} %get-tuple-element.156.refs_2_), channel_id=1, source_target_pairs={{0,4},{1,5},{2,6},{3,7},{4,0},{5,1},{6,2},{7,3},{8,12},{9,13},{10,... | collective-permute-start | bytes 786440 | tf_op jit(solution)/shard_map/ppermute | solution.py:34
  16.2 1.5 collective-permute-start.1
  17.7 1.6 collective-permute-start
  20.7 1.3 select_reduce_fusion
  22.0 1.7 collective-permute-done.1.refs_3_
  23.7 5.8 %collective-permute-done.refs_6_ = bf16[128,1024]{1,0:T(8,128)(2,1)} collective-permute-done((bf16[128,1024]{1,0:T(8,128)(2,1)S(1)}, bf16[128,1024]{1,0:T(8,128)(2,1)}, u32[]{:S(2)}, u32[]{:S(2)}) %collective-permute-start) | collective-permute-done | bytes 262176 | tf_op jit(solution)/shard_map/ppermute | solution.py:34
  30.0 1.2 collective-permute-start.4
  31.3 4.1 %all-to-all-start = ((f32[16,1,128]{2,1,0:T(1,128)}), f32[16,1,128]{2,1,0:T(1,128)S(1)}, u32[]{:S(2)}, u32[]{:S(2)}) async-start(f32[16,1,128]{2,1,0:T(1,128)} %bitcast.4), calls=%async_computation | async-start | bytes 16384 | tf_op jit(solution)/shard_map/all_to_all | solution.py:309
  35.9 1.7 collective-permute-start.9
  38.8 2.9 %all-to-all-done = f32[16,1,128]{2,1,0:T(1,128)S(1)} async-done(((f32[16,1,128]{2,1,0:T(1,128)}), f32[16,1,128]{2,1,0:T(1,128)S(1)}, u32[]{:S(2)}, u32[]{:S(2)}) %all-to-all-start) | async-done | bytes 8224 | tf_op jit(solution)/shard_map/all_to_all | solution.py:309
  42.5 2.4 %collective-permute-done.9.refs_11_ = bf16[128,1024]{1,0:T(8,128)(2,1)} collective-permute-done((bf16[128,1024]{1,0:T(8,128)(2,1)S(1)}, bf16[128,1024]{1,0:T(8,128)(2,1)}, u32[]{:S(2)}, u32[]{:S(2)}) %collective-permute-start.9) | collective-permute-done | bytes 262176 | tf_op jit(solution)/shard_map/ppermute | solution.py:34
  45.4 4.7 %collective-permute-done.12.refs_3_ = bf16[128,1024]{1,0:T(8,128)(2,1)S(1)} collective-permute-done((bf16[128,1024]{1,0:T(8,128)(2,1)S(1)}, bf16[128,1024]{1,0:T(8,128)(2,1)S(1)}, u32[]{:S(2)}, u32[]{:S(2)}) %collective-permute-start.12) | collective-permute-done | bytes 262176 | tf_op jit(solution)/shard_map/ppermute | solution.py:34
  50.2 2.3 %down_project.2.refs_6_ = f32[256,1024]{1,0:T(8,128)S(1)} custom-call(bf16[128,2048]{1,0:T(8,128)(2,1)S(1)} %get-tuple-element.80.refs_0_, bf16[128,2048]{1,0:T(8,128)(2,1)S(1)} %collective-permute-done.2.refs_1_, bf16[128,1024]{1,0:T(8,128)(2,1)S(1)} %get-tuple-element.156.refs_2_, bf16[128,1024]{1,0:T(8,128)(2,1)S(1)} %collective-permute-done.1.refs_3_, ...), custom_call_target="tpu_custom_call" | custom-call | flops 805306368 | bytes 3145728 | tf_op jit(solution)/shard_map/down_project/pallas_call | solution.py:119
  57.1 8.4 %collective-permute-done.15 = bf16[128,1024]{1,0:T(8,128)(2,1)S(1)} collective-permute-done((bf16[128,1024]{1,0:T(8,128)(2,1)}, bf16[128,1024]{1,0:T(8,128)(2,1)S(1)}, u32[]{:S(2)}, u32[]{:S(2)}) %collective-permute-start.15) | collective-permute-done | bytes 262176 | tf_op jit(solution)/shard_map/ppermute | solution.py:30
  65.6 1.8 collective-permute-start.19
  67.4 2.3 %collective-permute-start.18 = (bf16[128,1024]{1,0:T(8,128)(2,1)S(1)}, bf16[128,1024]{1,0:T(8,128)(2,1)S(1)}, u32[]{:S(2)}, u32[]{:S(2)}) collective-permute-start(bf16[128,1024]{1,0:T(8,128)(2,1)S(1)} %add_convert_fusion.8.refs_0_), channel_id=1, source_target_pairs={{0,4},{1,5},{2,6},{3,7},{4,0},{5,1},{6,2},{7,3},{8,12},{9,13},{10,... | collective-permute-start | bytes 786440 | tf_op jit(solution)/shard_map/ppermute | solution.py:34
  69.7 1.5 collective-permute-start.17
  71.2 2.2 %copy-done.1 = bf16[1,1024,2048]{2,1,0:T(8,128)(2,1)S(1)} copy-done((bf16[1,1024,2048]{2,1,0:T(8,128)(2,1)S(1)}, bf16[1,1024,2048]{2,1,0:T(8,128)(2,1)}, u32[]{:S(2)}) %copy-start.1) | copy-done | bytes 4194328
  73.4 2.2 %copy-done.3 = bf16[1,1024,2048]{2,1,0:T(8,128)(2,1)S(1)} copy-done((bf16[1,1024,2048]{2,1,0:T(8,128)(2,1)S(1)}, bf16[1,1024,2048]{2,1,0:T(8,128)(2,1)}, u32[]{:S(2)}) %copy-start.3) | copy-done | bytes 4194328
  75.6 2.2 %copy-done.4 = bf16[1,2048,1024]{2,1,0:T(8,128)(2,1)S(1)} copy-done((bf16[1,2048,1024]{2,1,0:T(8,128)(2,1)S(1)}, bf16[1,2048,1024]{2,1,0:T(8,128)(2,1)}, u32[]{:S(2)}) %copy-start.4) | copy-done | bytes 4194328
  77.8 5.4 %expert.5 = (bf16[128,1024]{1,0:T(8,128)(2,1)S(1)}, bf16[128,1024]{1,0:T(8,128)(2,1)S(1)}) custom-call(bf16[128,1024]{1,0:T(8,128)(2,1)S(1)} %add_convert_fusion.8.refs_0_, bf16[128,1024]{1,0:T(8,128)(2,1)S(1)} %collective-permute-done.16.refs_1_, f32[256,128]{1,0:T(8,128)S(1)} %broadcast_in_dim.75.refs_2_, bf16[1,1024,2048]{2,1,0:T(8,128)(2,1)S(1)} %copy-done.1, ...), custom_call_target="tpu_custom_call" | custom-call | flops 3221225472 | bytes 1048576 | tf_op jit(solution)/shard_map/expert/pallas_call | solution.py:192
  83.2 3.3 %collective-permute-done.18.refs_1_ = bf16[128,1024]{1,0:T(8,128)(2,1)S(1)} collective-permute-done((bf16[128,1024]{1,0:T(8,128)(2,1)S(1)}, bf16[128,1024]{1,0:T(8,128)(2,1)S(1)}, u32[]{:S(2)}, u32[]{:S(2)}) %collective-permute-start.18) | collective-permute-done | bytes 262176 | tf_op jit(solution)/shard_map/ppermute | solution.py:34
  87.1 1.3 collective-permute-start.24
  89.9 8.6 %expert.6 = (bf16[128,1024]{1,0:T(8,128)(2,1)S(1)}, bf16[128,1024]{1,0:T(8,128)(2,1)S(1)}, bf16[128,1024]{1,0:T(8,128)(2,1)S(1)}, bf16[128,1024]{1,0:T(8,128)(2,1)S(1)}) custom-call(bf16[128,1024]{1,0:T(8,128)(2,1)S(1)} %collective-permute-done.19.refs_0_, bf16[128,1024]{1,0:T(8,128)(2,1)S(1)} %collective-permute-done.17.refs_1_, ...), custom_call_target="tpu_custom_call" | custom-call | flops 6442450944 | bytes 2097152 | tf_op jit(solution)/shard_map/expert/pallas_call | solution.py:192
  98.5 1.5 collective-permute-done.24.refs_0_
  100.0 5.2 %collective-permute-done.25.refs_0_ = bf16[128,1024]{1,0:T(8,128)(2,1)S(1)} collective-permute-done((bf16[128,1024]{1,0:T(8,128)(2,1)S(1)}, bf16[128,1024]{1,0:T(8,128)(2,1)S(1)}, u32[]{:S(2)}, u32[]{:S(2)}) %collective-permute-start.25) | collective-permute-done | bytes 262176 | tf_op jit(solution)/shard_map/ppermute | solution.py:34
  105.1 0.9 collective-permute-done.23.refs_0_
  107.0 1.8 collective-permute-start.30
  109.5 8.5 %expert.7 = (bf16[128,1024]{1,0:T(8,128)(2,1)S(1)}, bf16[128,1024]{1,0:T(8,128)(2,1)S(1)}, bf16[128,1024]{1,0:T(8,128)(2,1)S(1)}, bf16[128,1024]{1,0:T(8,128)(2,1)S(1)}) custom-call(bf16[128,1024]{1,0:T(8,128)(2,1)S(1)} %collective-permute-done.24.refs_0_, bf16[128,1024]{1,0:T(8,128)(2,1)S(1)} %collective-permute-done.18.refs_1_, ...), custom_call_target="tpu_custom_call" | custom-call | flops 6442450944 | bytes 2097152 | tf_op jit(solution)/shard_map/expert/pallas_call | solution.py:192
  118.1 9.9 %collective-permute-done.31 = bf16[128,1024]{1,0:T(8,128)(2,1)S(1)} collective-permute-done((bf16[128,1024]{1,0:T(8,128)(2,1)S(1)}, bf16[128,1024]{1,0:T(8,128)(2,1)S(1)}, u32[]{:S(2)}, u32[]{:S(2)}) %collective-permute-start.31) | collective-permute-done | bytes 262176 | tf_op jit(solution)/shard_map/ppermute | solution.py:34
  129.6 2.5 %collective-permute-start.36 = (bf16[128,1024]{1,0:T(8,128)(2,1)S(1)}, bf16[128,1024]{1,0:T(8,128)(2,1)S(1)}, u32[]{:S(2)}, u32[]{:S(2)}) collective-permute-start(bf16[128,1024]{1,0:T(8,128)(2,1)S(1)} %add_convert_fusion.5), channel_id=1, source_target_pairs={{0,1},{1,0},{2,3},{3,2},{4,5},{5,4},{6,7},{7,6},{8,9},{9,8},{10,11... | collective-permute-start | bytes 786440 | tf_op jit(solution)/shard_map/ppermute | solution.py:34
  132.1 8.8 %expert.8 = (bf16[128,1024]{1,0:T(8,128)(2,1)S(1)}, bf16[128,1024]{1,0:T(8,128)(2,1)S(1)}, bf16[128,1024]{1,0:T(8,128)(2,1)S(1)}, bf16[128,1024]{1,0:T(8,128)(2,1)S(1)}) custom-call(bf16[128,1024]{1,0:T(8,128)(2,1)S(1)} %collective-permute-done.25.refs_0_, bf16[128,1024]{1,0:T(8,128)(2,1)S(1)} %collective-permute-done.30.refs_1_, ...), custom_call_target="tpu_custom_call" | custom-call | flops 6442450944 | bytes 2097152 | tf_op jit(solution)/shard_map/expert/pallas_call | solution.py:192
  142.1 0.9 collective-permute-done.39
  143.1 1.8 collective-permute-start.41
  145.6 5.2 %expert.9 = (bf16[128,1024]{1,0:T(8,128)(2,1)S(1)}, bf16[128,1024]{1,0:T(8,128)(2,1)S(1)}) custom-call(bf16[128,1024]{1,0:T(8,128)(2,1)S(1)} %collective-permute-done.23.refs_0_, bf16[128,1024]{1,0:T(8,128)(2,1)S(1)} %collective-permute-done.38.refs_1_, f32[256,128]{1,0:T(8,128)S(1)} %broadcast_in_dim.87.refs_2_, bf16[1,1024,2048]{2,1,0:T(8,128)(2,1)S(1)} %copy-done.2, ...), custom_call_target="tpu_custom_call" | custom-call | flops 3221225472 | bytes 1048576 | tf_op jit(solution)/shard_map/expert/pallas_call | solution.py:192
  150.8 1.5 collective-permute-done.41
  152.3 4.8 %collective-permute-done.42 = bf16[128,1024]{1,0:T(8,128)(2,1)S(1)} collective-permute-done((bf16[128,1024]{1,0:T(8,128)(2,1)S(1)}, bf16[128,1024]{1,0:T(8,128)(2,1)S(1)}, u32[]{:S(2)}, u32[]{:S(2)}) %collective-permute-start.42) | collective-permute-done | bytes 262176 | tf_op jit(solution)/shard_map/ppermute | solution.py:34
  157.8 4.5 %collective-permute-start.43 = (bf16[128,1024]{1,0:T(8,128)(2,1)S(1)}, bf16[128,1024]{1,0:T(8,128)(2,1)S(1)}, u32[]{:S(2)}, u32[]{:S(2)}) collective-permute-start(bf16[128,1024]{1,0:T(8,128)(2,1)S(1)} %add_convert_fusion.1), channel_id=1, source_target_pairs={{0,4},{1,5},{2,6},{3,7},{4,0},{5,1},{6,2},{7,3},{8,12},{9,13},{10,... | collective-permute-start | bytes 786440 | tf_op jit(solution)/shard_map/ppermute | solution.py:34
  162.3 1.4 collective-permute-done.44
  163.9 4.0 %collective-permute-start.45 = (bf16[128,1024]{1,0:T(8,128)(2,1)S(1)}, bf16[128,1024]{1,0:T(8,128)(2,1)S(1)}, u32[]{:S(2)}, u32[]{:S(2)}) collective-permute-start(bf16[128,1024]{1,0:T(8,128)(2,1)S(1)} %add_convert_fusion), channel_id=1, source_target_pairs={{0,6},{1,7},{2,4},{3,5},{4,2},{5,3},{6,0},{7,1},{8,14},{9,15},{10,... | collective-permute-start | bytes 786440 | tf_op jit(solution)/shard_map/ppermute | solution.py:34
  167.8 2.9 %collective-permute-done.37.refs_1_ = bf16[128,1024]{1,0:T(8,128)(2,1)S(1)} collective-permute-done((bf16[128,1024]{1,0:T(8,128)(2,1)S(1)}, bf16[128,1024]{1,0:T(8,128)(2,1)S(1)}, u32[]{:S(2)}, u32[]{:S(2)}) %collective-permute-start.37) | collective-permute-done | bytes 262176 | tf_op jit(solution)/shard_map/ppermute | solution.py:34
  170.8 10.0 %collective-permute-done.43.refs_2_ = bf16[128,1024]{1,0:T(8,128)(2,1)S(1)} collective-permute-done((bf16[128,1024]{1,0:T(8,128)(2,1)S(1)}, bf16[128,1024]{1,0:T(8,128)(2,1)S(1)}, u32[]{:S(2)}, u32[]{:S(2)}) %collective-permute-start.43) | collective-permute-done | bytes 262176 | tf_op jit(solution)/shard_map/ppermute | solution.py:34
  180.7 2.2 %copy-done.5 = bf16[4096,512]{1,0:T(8,128)(2,1)S(1)} copy-done((bf16[4096,512]{1,0:T(8,128)(2,1)S(1)}, bf16[4096,512]{1,0:T(8,128)(2,1)}, u32[]{:S(2)}) %copy-start.5) | copy-done | bytes 4194328
  182.9 4.2 %project.1 = bf16[128,4096]{1,0:T(8,128)(2,1)} custom-call(s32[1]{0:T(128)} %bitcast.where, bf16[128,1024]{1,0:T(8,128)(2,1)S(1)} %add_convert_fusion.6.refs_0_, bf16[128,1024]{1,0:T(8,128)(2,1)S(1)} %collective-permute-done.37.refs_1_, bf16[128,1024]{1,0:T(8,128)(2,1)S(1)} %collective-permute-done.43.refs_2_, ...), custom_call_target="tpu_custom_call" | custom-call | flops 1073741824 | bytes 8388608 | tf_op jit(solution)/shard_map/project/pallas_call | solution.py:256
  (110 shorter events, 17.8 us)
Async XLA Ops:
  9.5 20.5 %collective-permute-start.2 = (bf16[128,2048]{1,0:T(8,128)(2,1)}, bf16[128,2048]{1,0:T(8,128)(2,1)S(1)}, u32[]{:S(2)}, u32[]{:S(2)}) collective-permute-start(bf16[128,2048]{1,0:T(8,128)(2,1)} %get-tuple-element.84), channel_id=1, source_target_pairs={{0,16},{16,0},{1,17},{17,1},{2,18},{18,2},{3,19},{19,3},{4,20},{20... | collective-permute-start | bytes 1572872 | tf_op jit(solution)/shard_map/ppermute | solution.py:30
  13.5 16.5 %collective-permute-start.3 = (bf16[128,1024]{1,0:T(8,128)(2,1)S(1)}, bf16[128,1024]{1,0:T(8,128)(2,1)S(1)}, u32[]{:S(2)}, u32[]{:S(2)}) collective-permute-start(bf16[128,1024]{1,0:T(8,128)(2,1)S(1)} %get-tuple-element.156.refs_2_), channel_id=1, source_target_pairs={{0,4},{1,5},{2,6},{3,7},{4,0},{5,1},{6,2},{7,3},{8,12},{9,13},{10,... | collective-permute-start | bytes 786440 | tf_op jit(solution)/shard_map/ppermute | solution.py:34
  16.2 7.5 %collective-permute-start.1 = (bf16[128,1024]{1,0:T(8,128)(2,1)S(1)}, bf16[128,1024]{1,0:T(8,128)(2,1)S(1)}, u32[]{:S(2)}, u32[]{:S(2)}) collective-permute-start(bf16[128,1024]{1,0:T(8,128)(2,1)S(1)} %get-tuple-element.156.refs_2_), channel_id=1, source_target_pairs={{0,1},{1,0},{2,3},{3,2},{4,5},{5,4},{6,7},{7,6},{8,9},{9,8},{10,11... | collective-permute-start | bytes 786440 | tf_op jit(solution)/shard_map/ppermute | solution.py:34
  17.7 11.8 %collective-permute-start = (bf16[128,1024]{1,0:T(8,128)(2,1)S(1)}, bf16[128,1024]{1,0:T(8,128)(2,1)}, u32[]{:S(2)}, u32[]{:S(2)}) collective-permute-start(bf16[128,1024]{1,0:T(8,128)(2,1)S(1)} %get-tuple-element.156.refs_2_), channel_id=1, source_target_pairs={{0,2},{1,3},{2,0},{3,1},{4,6},{5,7},{6,4},{7,5},{8,10},{9,11},{10,... | collective-permute-start | bytes 786440 | tf_op jit(solution)/shard_map/ppermute | solution.py:34
  29.5 8.9 %collective-permute-start.5 = (bf16[128,1024]{1,0:T(8,128)(2,1)}, bf16[128,1024]{1,0:T(8,128)(2,1)}, u32[]{:S(2)}, u32[]{:S(2)}) collective-permute-start(bf16[128,1024]{1,0:T(8,128)(2,1)} %collective-permute-done.refs_6_), channel_id=1, source_target_pairs={{0,1},{1,0},{2,3},{3,2},{4,5},{5,4},{6,7},{7,6},{8,9},{9,8},{10,11... | collective-permute-start | bytes 786440 | tf_op jit(solution)/shard_map/ppermute | solution.py:34
  30.0 11.7 %collective-permute-start.4 = (bf16[128,1024]{1,0:T(8,128)(2,1)S(1)}, bf16[128,1024]{1,0:T(8,128)(2,1)S(1)}, u32[]{:S(2)}, u32[]{:S(2)}) collective-permute-start(bf16[128,1024]{1,0:T(8,128)(2,1)S(1)} %collective-permute-done.3.refs_10_), channel_id=1, source_target_pairs={{0,2},{1,3},{2,0},{3,1},{4,6},{5,7},{6,4},{7,5},{8,10},{9,11},{10,... | collective-permute-start | bytes 786440 | tf_op jit(solution)/shard_map/ppermute | solution.py:34
  31.3 10.5 %all-to-all-start = ((f32[16,1,128]{2,1,0:T(1,128)}), f32[16,1,128]{2,1,0:T(1,128)S(1)}, u32[]{:S(2)}, u32[]{:S(2)}) async-start(f32[16,1,128]{2,1,0:T(1,128)} %bitcast.4), calls=%async_computation | async-start | bytes 16384 | tf_op jit(solution)/shard_map/all_to_all | solution.py:309
  35.4 121.7 %all-gather.3.cloned.1.call-start = ((), (), s32[]{:S(2)}) async-start(), calls=%async_computation.1 | async-start | bytes 4456448 | tf_op jit(solution)/shard_map/all_gather | solution.py:341
  35.4 6.9 %collective-permute-start.6 = (bf16[128,1024]{1,0:T(8,128)(2,1)S(1)}, bf16[128,1024]{1,0:T(8,128)(2,1)}, u32[]{:S(2)}, u32[]{:S(2)}) collective-permute-start(bf16[128,1024]{1,0:T(8,128)(2,1)S(1)} %collective-permute-done.1.refs_3_), channel_id=1, source_target_pairs={{0,8},{8,0},{1,9},{9,1},{2,10},{10,2},{3,11},{11,3},{4,12},{12,4},... | collective-permute-start | bytes 786440 | tf_op jit(solution)/shard_map/ppermute | solution.py:26
  35.9 8.9 %collective-permute-start.9 = (bf16[128,1024]{1,0:T(8,128)(2,1)S(1)}, bf16[128,1024]{1,0:T(8,128)(2,1)}, u32[]{:S(2)}, u32[]{:S(2)}) collective-permute-start(bf16[128,1024]{1,0:T(8,128)(2,1)S(1)} %collective-permute-done.3.refs_10_), channel_id=1, source_target_pairs={{0,1},{1,0},{2,3},{3,2},{4,5},{5,4},{6,7},{7,6},{8,9},{9,8},{10,11... | collective-permute-start | bytes 786440 | tf_op jit(solution)/shard_map/ppermute | solution.py:34
  38.3 11.8 %collective-permute-start.10 = (bf16[128,1024]{1,0:T(8,128)(2,1)S(1)}, bf16[128,1024]{1,0:T(8,128)(2,1)}, u32[]{:S(2)}, u32[]{:S(2)}) collective-permute-start(bf16[128,1024]{1,0:T(8,128)(2,1)S(1)} %collective-permute-done.3.refs_10_), channel_id=1, source_target_pairs={{0,8},{8,0},{1,9},{9,1},{2,10},{10,2},{3,11},{11,3},{4,12},{12,4},... | collective-permute-start | bytes 786440 | tf_op jit(solution)/shard_map/ppermute | solution.py:26
  38.4 6.4 %collective-permute-start.7 = (bf16[128,1024]{1,0:T(8,128)(2,1)}, bf16[128,1024]{1,0:T(8,128)(2,1)}, u32[]{:S(2)}, u32[]{:S(2)}) collective-permute-start(bf16[128,1024]{1,0:T(8,128)(2,1)} %collective-permute-done.refs_6_), channel_id=1, source_target_pairs={{0,8},{8,0},{1,9},{9,1},{2,10},{10,2},{3,11},{11,3},{4,12},{12,4},... | collective-permute-start | bytes 786440 | tf_op jit(solution)/shard_map/ppermute | solution.py:26
  41.8 8.3 %collective-permute-start.12 = (bf16[128,1024]{1,0:T(8,128)(2,1)S(1)}, bf16[128,1024]{1,0:T(8,128)(2,1)S(1)}, u32[]{:S(2)}, u32[]{:S(2)}) collective-permute-start(bf16[128,1024]{1,0:T(8,128)(2,1)S(1)} %collective-permute-done.4.refs_2_), channel_id=1, source_target_pairs={{0,1},{1,0},{2,3},{3,2},{4,5},{5,4},{6,7},{7,6},{8,9},{9,8},{10,11... | collective-permute-start | bytes 786440 | tf_op jit(solution)/shard_map/ppermute | solution.py:34
  42.4 7.8 %collective-permute-start.8 = (bf16[128,1024]{1,0:T(8,128)(2,1)}, bf16[128,1024]{1,0:T(8,128)(2,1)S(1)}, u32[]{:S(2)}, u32[]{:S(2)}) collective-permute-start(bf16[128,1024]{1,0:T(8,128)(2,1)} %collective-permute-done.5.refs_7_), channel_id=1, source_target_pairs={{0,8},{8,0},{1,9},{9,1},{2,10},{10,2},{3,11},{11,3},{4,12},{12,4},... | collective-permute-start | bytes 786440 | tf_op jit(solution)/shard_map/ppermute | solution.py:26
  44.8 5.3 %collective-permute-start.11 = (bf16[128,1024]{1,0:T(8,128)(2,1)}, bf16[128,1024]{1,0:T(8,128)(2,1)S(1)}, u32[]{:S(2)}, u32[]{:S(2)}) collective-permute-start(bf16[128,1024]{1,0:T(8,128)(2,1)} %collective-permute-done.9.refs_11_), channel_id=1, source_target_pairs={{0,8},{8,0},{1,9},{9,1},{2,10},{10,2},{3,11},{11,3},{4,12},{12,4},... | collective-permute-start | bytes 786440 | tf_op jit(solution)/shard_map/ppermute | solution.py:26
  44.9 10.5 %collective-permute-start.13 = (bf16[128,1024]{1,0:T(8,128)(2,1)S(1)}, bf16[128,1024]{1,0:T(8,128)(2,1)S(1)}, u32[]{:S(2)}, u32[]{:S(2)}) collective-permute-start(bf16[128,1024]{1,0:T(8,128)(2,1)S(1)} %collective-permute-done.4.refs_2_), channel_id=1, source_target_pairs={{0,8},{8,0},{1,9},{9,1},{2,10},{10,2},{3,11},{11,3},{4,12},{12,4},... | collective-permute-start | bytes 786440 | tf_op jit(solution)/shard_map/ppermute | solution.py:26
  50.1 5.2 %collective-permute-start.14 = (bf16[128,1024]{1,0:T(8,128)(2,1)S(1)}, bf16[128,1024]{1,0:T(8,128)(2,1)S(1)}, u32[]{:S(2)}, u32[]{:S(2)}) collective-permute-start(bf16[128,1024]{1,0:T(8,128)(2,1)S(1)} %collective-permute-done.12.refs_3_), channel_id=1, source_target_pairs={{0,8},{8,0},{1,9},{9,1},{2,10},{10,2},{3,11},{11,3},{4,12},{12,4},... | collective-permute-start | bytes 786440 | tf_op jit(solution)/shard_map/ppermute | solution.py:26
  56.5 9.0 %collective-permute-start.15 = (bf16[128,1024]{1,0:T(8,128)(2,1)}, bf16[128,1024]{1,0:T(8,128)(2,1)S(1)}, u32[]{:S(2)}, u32[]{:S(2)}) collective-permute-start(bf16[128,1024]{1,0:T(8,128)(2,1)} %copy-done.10), channel_id=1, source_target_pairs={{0,16},{16,0},{1,17},{17,1},{2,18},{18,2},{3,19},{19,3},{4,20},{20... | collective-permute-start | bytes 786440 | tf_op jit(solution)/shard_map/ppermute | solution.py:30
  65.6 5.6 %collective-permute-start.16 = (bf16[128,1024]{1,0:T(8,128)(2,1)S(1)}, bf16[128,1024]{1,0:T(8,128)(2,1)S(1)}, u32[]{:S(2)}, u32[]{:S(2)}) collective-permute-start(bf16[128,1024]{1,0:T(8,128)(2,1)S(1)} %add_convert_fusion.8.refs_0_), channel_id=1, source_target_pairs={{0,8},{8,0},{1,9},{9,1},{2,10},{10,2},{3,11},{11,3},{4,12},{12,4},... | collective-permute-start | bytes 786440 | tf_op jit(solution)/shard_map/ppermute | solution.py:26
  65.6 17.5 %collective-permute-start.19 = (bf16[128,1024]{1,0:T(8,128)(2,1)S(1)}, bf16[128,1024]{1,0:T(8,128)(2,1)S(1)}, u32[]{:S(2)}, u32[]{:S(2)}) collective-permute-start(bf16[128,1024]{1,0:T(8,128)(2,1)S(1)} %add_convert_fusion.8.refs_0_), channel_id=1, source_target_pairs={{0,1},{1,0},{2,3},{3,2},{4,5},{5,4},{6,7},{7,6},{8,9},{9,8},{10,11... | collective-permute-start | bytes 786440 | tf_op jit(solution)/shard_map/ppermute | solution.py:34
  67.4 19.1 %collective-permute-start.18 = (bf16[128,1024]{1,0:T(8,128)(2,1)S(1)}, bf16[128,1024]{1,0:T(8,128)(2,1)S(1)}, u32[]{:S(2)}, u32[]{:S(2)}) collective-permute-start(bf16[128,1024]{1,0:T(8,128)(2,1)S(1)} %add_convert_fusion.8.refs_0_), channel_id=1, source_target_pairs={{0,4},{1,5},{2,6},{3,7},{4,0},{5,1},{6,2},{7,3},{8,12},{9,13},{10,... | collective-permute-start | bytes 786440 | tf_op jit(solution)/shard_map/ppermute | solution.py:34
  69.7 16.8 %collective-permute-start.17 = (bf16[128,1024]{1,0:T(8,128)(2,1)S(1)}, bf16[128,1024]{1,0:T(8,128)(2,1)S(1)}, u32[]{:S(2)}, u32[]{:S(2)}) collective-permute-start(bf16[128,1024]{1,0:T(8,128)(2,1)S(1)} %add_convert_fusion.8.refs_0_), channel_id=1, source_target_pairs={{0,2},{1,3},{2,0},{3,1},{4,6},{5,7},{6,4},{7,5},{8,10},{9,11},{10,... | collective-permute-start | bytes 786440 | tf_op jit(solution)/shard_map/ppermute | solution.py:34
  86.5 2.6 %collective-permute-start.20 = (bf16[128,1024]{1,0:T(8,128)(2,1)S(1)}, bf16[128,1024]{1,0:T(8,128)(2,1)S(1)}, u32[]{:S(2)}, u32[]{:S(2)}) collective-permute-start(bf16[128,1024]{1,0:T(8,128)(2,1)S(1)} %get-tuple-element.99), channel_id=1, source_target_pairs={{0,8},{8,0},{1,9},{9,1},{2,10},{10,2},{3,11},{11,3},{4,12},{12,4},... | collective-permute-start | bytes 786440 | tf_op jit(solution)/shard_map/ppermute | solution.py:26
  86.5 3.4 %collective-permute-start.21 = (bf16[128,1024]{1,0:T(8,128)(2,1)S(1)}, bf16[128,1024]{1,0:T(8,128)(2,1)S(1)}, u32[]{:S(2)}, u32[]{:S(2)}) collective-permute-start(bf16[128,1024]{1,0:T(8,128)(2,1)S(1)} %collective-permute-done.19.refs_0_), channel_id=1, source_target_pairs={{0,8},{8,0},{1,9},{9,1},{2,10},{10,2},{3,11},{11,3},{4,12},{12,4},... | collective-permute-start | bytes 786440 | tf_op jit(solution)/shard_map/ppermute | solution.py:26
  87.0 2.9 %collective-permute-start.22 = (bf16[128,1024]{1,0:T(8,128)(2,1)S(1)}, bf16[128,1024]{1,0:T(8,128)(2,1)S(1)}, u32[]{:S(2)}, u32[]{:S(2)}) collective-permute-start(bf16[128,1024]{1,0:T(8,128)(2,1)S(1)} %collective-permute-done.17.refs_1_), channel_id=1, source_target_pairs={{0,8},{8,0},{1,9},{9,1},{2,10},{10,2},{3,11},{11,3},{4,12},{12,4},... | collective-permute-start | bytes 786440 | tf_op jit(solution)/shard_map/ppermute | solution.py:26
  87.1 12.9 %collective-permute-start.24 = (bf16[128,1024]{1,0:T(8,128)(2,1)S(1)}, bf16[128,1024]{1,0:T(8,128)(2,1)S(1)}, u32[]{:S(2)}, u32[]{:S(2)}) collective-permute-start(bf16[128,1024]{1,0:T(8,128)(2,1)S(1)} %collective-permute-done.17.refs_1_), channel_id=1, source_target_pairs={{0,1},{1,0},{2,3},{3,2},{4,5},{5,4},{6,7},{7,6},{8,9},{9,8},{10,11... | collective-permute-start | bytes 786440 | tf_op jit(solution)/shard_map/ppermute | solution.py:34
  88.4 16.7 %collective-permute-start.25 = (bf16[128,1024]{1,0:T(8,128)(2,1)S(1)}, bf16[128,1024]{1,0:T(8,128)(2,1)S(1)}, u32[]{:S(2)}, u32[]{:S(2)}) collective-permute-start(bf16[128,1024]{1,0:T(8,128)(2,1)S(1)} %collective-permute-done.18.refs_1_), channel_id=1, source_target_pairs={{0,1},{1,0},{2,3},{3,2},{4,5},{5,4},{6,7},{7,6},{8,9},{9,8},{10,11... | collective-permute-start | bytes 786440 | tf_op jit(solution)/shard_map/ppermute | solution.py:34
  89.1 16.9 %collective-permute-start.23 = (bf16[128,1024]{1,0:T(8,128)(2,1)S(1)}, bf16[128,1024]{1,0:T(8,128)(2,1)S(1)}, u32[]{:S(2)}, u32[]{:S(2)}) collective-permute-start(bf16[128,1024]{1,0:T(8,128)(2,1)S(1)} %collective-permute-done.18.refs_1_), channel_id=1, source_target_pairs={{0,2},{1,3},{2,0},{3,1},{4,6},{5,7},{6,4},{7,5},{8,10},{9,11},{10,... | collective-permute-start | bytes 786440 | tf_op jit(solution)/shard_map/ppermute | solution.py:34
  106.0 2.8 %collective-permute-start.28 = (bf16[128,1024]{1,0:T(8,128)(2,1)S(1)}, bf16[128,1024]{1,0:T(8,128)(2,1)S(1)}, u32[]{:S(2)}, u32[]{:S(2)}) collective-permute-start(bf16[128,1024]{1,0:T(8,128)(2,1)S(1)} %get-tuple-element.113), channel_id=1, source_target_pairs={{0,8},{8,0},{1,9},{9,1},{2,10},{10,2},{3,11},{11,3},{4,12},{12,4},... | collective-permute-start | bytes 786440 | tf_op jit(solution)/shard_map/ppermute | solution.py:26
  106.0 3.5 %collective-permute-start.27 = (bf16[128,1024]{1,0:T(8,128)(2,1)S(1)}, bf16[128,1024]{1,0:T(8,128)(2,1)S(1)}, u32[]{:S(2)}, u32[]{:S(2)}) collective-permute-start(bf16[128,1024]{1,0:T(8,128)(2,1)S(1)} %collective-permute-done.18.refs_1_), channel_id=1, source_target_pairs={{0,8},{8,0},{1,9},{9,1},{2,10},{10,2},{3,11},{11,3},{4,12},{12,4},... | collective-permute-start | bytes 786440 | tf_op jit(solution)/shard_map/ppermute | solution.py:26
  106.5 3.0 %collective-permute-start.29 = (bf16[128,1024]{1,0:T(8,128)(2,1)S(1)}, bf16[128,1024]{1,0:T(8,128)(2,1)S(1)}, u32[]{:S(2)}, u32[]{:S(2)}) collective-permute-start(bf16[128,1024]{1,0:T(8,128)(2,1)S(1)} %get-tuple-element.114), channel_id=1, source_target_pairs={{0,8},{8,0},{1,9},{9,1},{2,10},{10,2},{3,11},{11,3},{4,12},{12,4},... | collective-permute-start | bytes 786440 | tf_op jit(solution)/shard_map/ppermute | solution.py:26
  106.5 3.0 %collective-permute-start.26 = (bf16[128,1024]{1,0:T(8,128)(2,1)S(1)}, bf16[128,1024]{1,0:T(8,128)(2,1)S(1)}, u32[]{:S(2)}, u32[]{:S(2)}) collective-permute-start(bf16[128,1024]{1,0:T(8,128)(2,1)S(1)} %collective-permute-done.24.refs_0_), channel_id=1, source_target_pairs={{0,8},{8,0},{1,9},{9,1},{2,10},{10,2},{3,11},{11,3},{4,12},{12,4},... | collective-permute-start | bytes 786440 | tf_op jit(solution)/shard_map/ppermute | solution.py:26
  107.0 11.0 %collective-permute-start.30 = (bf16[128,1024]{1,0:T(8,128)(2,1)S(1)}, bf16[128,1024]{1,0:T(8,128)(2,1)S(1)}, u32[]{:S(2)}, u32[]{:S(2)}) collective-permute-start(bf16[128,1024]{1,0:T(8,128)(2,1)S(1)} %collective-permute-done.23.refs_0_), channel_id=1, source_target_pairs={{0,1},{1,0},{2,3},{3,2},{4,5},{5,4},{6,7},{7,6},{8,9},{9,8},{10,11... | collective-permute-start | bytes 786440 | tf_op jit(solution)/shard_map/ppermute | solution.py:34
  108.9 19.1 %collective-permute-start.31 = (bf16[128,1024]{1,0:T(8,128)(2,1)S(1)}, bf16[128,1024]{1,0:T(8,128)(2,1)S(1)}, u32[]{:S(2)}, u32[]{:S(2)}) collective-permute-start(bf16[128,1024]{1,0:T(8,128)(2,1)S(1)} %add_convert_fusion.7), channel_id=1, source_target_pairs={{0,1},{1,0},{2,3},{3,2},{4,5},{5,4},{6,7},{7,6},{8,9},{9,8},{10,11... | collective-permute-start | bytes 786440 | tf_op jit(solution)/shard_map/ppermute | solution.py:34
  128.0 1.5 collective-permute-start.34
  128.0 4.2 %collective-permute-start.32 = (bf16[128,1024]{1,0:T(8,128)(2,1)S(1)}, bf16[128,1024]{1,0:T(8,128)(2,1)S(1)}, u32[]{:S(2)}, u32[]{:S(2)}) collective-permute-start(bf16[128,1024]{1,0:T(8,128)(2,1)S(1)} %collective-permute-done.25.refs_0_), channel_id=1, source_target_pairs={{0,8},{8,0},{1,9},{9,1},{2,10},{10,2},{3,11},{11,3},{4,12},{12,4},... | collective-permute-start | bytes 786440 | tf_op jit(solution)/shard_map/ppermute | solution.py:26
  128.5 3.6 %collective-permute-start.35 = (bf16[128,1024]{1,0:T(8,128)(2,1)S(1)}, bf16[128,1024]{1,0:T(8,128)(2,1)S(1)}, u32[]{:S(2)}, u32[]{:S(2)}) collective-permute-start(bf16[128,1024]{1,0:T(8,128)(2,1)S(1)} %get-tuple-element.130), channel_id=1, source_target_pairs={{0,8},{8,0},{1,9},{9,1},{2,10},{10,2},{3,11},{11,3},{4,12},{12,4},... | collective-permute-start | bytes 786440 | tf_op jit(solution)/shard_map/ppermute | solution.py:26
  128.5 3.6 %collective-permute-start.33 = (bf16[128,1024]{1,0:T(8,128)(2,1)S(1)}, bf16[128,1024]{1,0:T(8,128)(2,1)S(1)}, u32[]{:S(2)}, u32[]{:S(2)}) collective-permute-start(bf16[128,1024]{1,0:T(8,128)(2,1)S(1)} %collective-permute-done.30.refs_1_), channel_id=1, source_target_pairs={{0,8},{8,0},{1,9},{9,1},{2,10},{10,2},{3,11},{11,3},{4,12},{12,4},... | collective-permute-start | bytes 786440 | tf_op jit(solution)/shard_map/ppermute | solution.py:26
  129.6 11.9 %collective-permute-start.36 = (bf16[128,1024]{1,0:T(8,128)(2,1)S(1)}, bf16[128,1024]{1,0:T(8,128)(2,1)S(1)}, u32[]{:S(2)}, u32[]{:S(2)}) collective-permute-start(bf16[128,1024]{1,0:T(8,128)(2,1)S(1)} %add_convert_fusion.5), channel_id=1, source_target_pairs={{0,1},{1,0},{2,3},{3,2},{4,5},{5,4},{6,7},{7,6},{8,9},{9,8},{10,11... | collective-permute-start | bytes 786440 | tf_op jit(solution)/shard_map/ppermute | solution.py:34
  141.5 4.2 %collective-permute-start.38 = (bf16[128,1024]{1,0:T(8,128)(2,1)S(1)}, bf16[128,1024]{1,0:T(8,128)(2,1)S(1)}, u32[]{:S(2)}, u32[]{:S(2)}) collective-permute-start(bf16[128,1024]{1,0:T(8,128)(2,1)S(1)} %collective-permute-done.23.refs_0_), channel_id=1, source_target_pairs={{0,8},{8,0},{1,9},{9,1},{2,10},{10,2},{3,11},{11,3},{4,12},{12,4},... | collective-permute-start | bytes 786440 | tf_op jit(solution)/shard_map/ppermute | solution.py:26
  142.0 2.9 %collective-permute-start.40 = (bf16[128,1024]{1,0:T(8,128)(2,1)S(1)}, bf16[128,1024]{1,0:T(8,128)(2,1)S(1)}, u32[]{:S(2)}, u32[]{:S(2)}) collective-permute-start(bf16[128,1024]{1,0:T(8,128)(2,1)S(1)} %get-tuple-element.144), channel_id=1, source_target_pairs={{0,8},{8,0},{1,9},{9,1},{2,10},{10,2},{3,11},{11,3},{4,12},{12,4},... | collective-permute-start | bytes 786440 | tf_op jit(solution)/shard_map/ppermute | solution.py:26
  143.1 9.2 %collective-permute-start.41 = (bf16[128,1024]{1,0:T(8,128)(2,1)S(1)}, bf16[128,1024]{1,0:T(8,128)(2,1)S(1)}, u32[]{:S(2)}, u32[]{:S(2)}) collective-permute-start(bf16[128,1024]{1,0:T(8,128)(2,1)S(1)} %add_convert_fusion.3), channel_id=1, source_target_pairs={{0,1},{1,0},{2,3},{3,2},{4,5},{5,4},{6,7},{7,6},{8,9},{9,8},{10,11... | collective-permute-start | bytes 786440 | tf_op jit(solution)/shard_map/ppermute | solution.py:34
  145.0 12.2 %collective-permute-start.42 = (bf16[128,1024]{1,0:T(8,128)(2,1)S(1)}, bf16[128,1024]{1,0:T(8,128)(2,1)S(1)}, u32[]{:S(2)}, u32[]{:S(2)}) collective-permute-start(bf16[128,1024]{1,0:T(8,128)(2,1)S(1)} %add_convert_fusion.2), channel_id=1, source_target_pairs={{0,1},{1,0},{2,3},{3,2},{4,5},{5,4},{6,7},{7,6},{8,9},{9,8},{10,11... | collective-permute-start | bytes 786440 | tf_op jit(solution)/shard_map/ppermute | solution.py:34
  157.1 23.6 %collective-permute-start.46 = (bf16[16,256,512]{2,1,0:T(8,128)(2,1)}, bf16[16,256,512]{2,1,0:T(8,128)(2,1)S(1)}, u32[]{:S(2)}, u32[]{:S(2)}) collective-permute-start(bf16[16,256,512]{2,1,0:T(8,128)(2,1)} %bitcast.16), channel_id=1, source_target_pairs={{0,8},{8,0},{1,9},{9,1},{2,10},{10,2},{3,11},{11,3},{4,12},{12,4},... | collective-permute-start | bytes 12582920 | tf_op jit(solution)/shard_map/ppermute | solution.py:26
  157.1 6.6 %collective-permute-start.44 = (bf16[128,1024]{1,0:T(8,128)(2,1)S(1)}, bf16[128,1024]{1,0:T(8,128)(2,1)S(1)}, u32[]{:S(2)}, u32[]{:S(2)}) collective-permute-start(bf16[128,1024]{1,0:T(8,128)(2,1)S(1)} %get-tuple-element.151), channel_id=1, source_target_pairs={{0,8},{8,0},{1,9},{9,1},{2,10},{10,2},{3,11},{11,3},{4,12},{12,4},... | collective-permute-start | bytes 786440 | tf_op jit(solution)/shard_map/ppermute | solution.py:26
  157.6 13.1 %collective-permute-start.37 = (bf16[128,1024]{1,0:T(8,128)(2,1)S(1)}, bf16[128,1024]{1,0:T(8,128)(2,1)S(1)}, u32[]{:S(2)}, u32[]{:S(2)}) collective-permute-start(bf16[128,1024]{1,0:T(8,128)(2,1)S(1)} %add_convert_fusion.4), channel_id=1, source_target_pairs={{0,2},{1,3},{2,0},{3,1},{4,6},{5,7},{6,4},{7,5},{8,10},{9,11},{10,... | collective-permute-start | bytes 786440 | tf_op jit(solution)/shard_map/ppermute | solution.py:34
  157.8 23.0 %collective-permute-start.43 = (bf16[128,1024]{1,0:T(8,128)(2,1)S(1)}, bf16[128,1024]{1,0:T(8,128)(2,1)S(1)}, u32[]{:S(2)}, u32[]{:S(2)}) collective-permute-start(bf16[128,1024]{1,0:T(8,128)(2,1)S(1)} %add_convert_fusion.1), channel_id=1, source_target_pairs={{0,4},{1,5},{2,6},{3,7},{4,0},{5,1},{6,2},{7,3},{8,12},{9,13},{10,... | collective-permute-start | bytes 786440 | tf_op jit(solution)/shard_map/ppermute | solution.py:34
  163.9 16.9 %collective-permute-start.45 = (bf16[128,1024]{1,0:T(8,128)(2,1)S(1)}, bf16[128,1024]{1,0:T(8,128)(2,1)S(1)}, u32[]{:S(2)}, u32[]{:S(2)}) collective-permute-start(bf16[128,1024]{1,0:T(8,128)(2,1)S(1)} %add_convert_fusion), channel_id=1, source_target_pairs={{0,6},{1,7},{2,4},{3,5},{4,2},{5,3},{6,0},{7,1},{8,14},{9,15},{10,... | collective-permute-start | bytes 786440 | tf_op jit(solution)/shard_map/ppermute | solution.py:34
  (12 other events, 127.4 us)
Sparse Core Ops, SparseCore 0:
  56.6 94.0 all-gather.2

commit v5 on v4

v5 whole, which is shorter than its diff:
```python
import functools

import jax
import jax.numpy as jnp
from jax import lax
from jax.experimental import pallas as pl
from jax.experimental.pallas import tpu as pltpu
from jax.sharding import PartitionSpec as P

route_scale = 2.5
mebi = 1024 * 1024
in_vmem = pl.BlockSpec(memory_space=pltpu.VMEM)
in_smem = pl.BlockSpec(memory_space=pltpu.SMEM)
in_hbm = pl.BlockSpec(memory_space=pltpu.HBM)
anywhere = pl.BlockSpec(memory_space=pl.ANY)


def after(value, *others):
    return lax.optimization_barrier((value, *others))[0]


def join(*values):
    return lax.optimization_barrier(values)


def swap_cores(array):
    return lax.ppermute(array, "grp", [(0, 1), (1, 0)])


def swap_reps(array):
    return lax.ppermute(array, "rep", [(i, i ^ 1) for i in range(lax.axis_size("rep"))])


def swap_ep(array, mask):
    return lax.ppermute(array, "ep", [(i, i ^ mask) for i in range(lax.axis_size("ep"))])


def first_steps(piece, steps):
    return {0: piece} | {k: swap_ep(piece, 2 * k) for k in range(1, steps) if k & (k - 1) == 0}


def dense_weights(expert_ids, route_scores, expert_count):
    sigmoids = jax.nn.sigmoid(route_scores)
    weights = (route_scale * sigmoids / jnp.sum(sigmoids, axis=1, keepdims=True)).astype(
        jnp.bfloat16
    )
    named = expert_ids[None, :, :] == jnp.arange(expert_count, dtype=jnp.int32)[:, None, None]
    return jnp.sum(jnp.where(named, weights.astype(jnp.float32)[None, :, :], 0.0), axis=2)


def columns_kernel(ep_count, quarter, where, tokens, kept, given):
    place, side, group = where[0], where[1], where[2]
    for offset in range(ep_count):
        for core in range(2):
            to = pl.ds(((offset // 2 * 2 + core) * 2 + offset % 2) * quarter, quarter)
            shard = (place ^ offset) * 4 + (group ^ core)
            for half, part in ((side, kept), (1 - side, given)):
                start = pl.multiple_of((shard + 2 * half) * quarter, quarter)
                part[:, to] = tokens[:, pl.ds(start, quarter)]


def split_columns(tokens, ep_count, quarter, place, side, group):
    count = tokens.shape[0]
    if quarter % 128 == 0:
        half = jax.ShapeDtypeStruct((count, 2 * ep_count * quarter), tokens.dtype)
        return pl.pallas_call(
            functools.partial(columns_kernel, ep_count, quarter),
            out_shape=(half, half),
            in_specs=[in_smem, in_vmem],
            out_specs=(in_vmem, in_vmem),
            compiler_params=pltpu.CompilerParams(vmem_limit_bytes=8 * mebi),
            name="split_columns",
        )(jnp.stack([place, side, group]).astype(jnp.int32), tokens)
    cut = tokens.reshape(count, ep_count, 2, 2, quarter)
    parts = [], []
    for step in range(ep_count // 2):
        for core in (group, 1 - group):
            for offset in (2 * step, 2 * step + 1):
                for half, part in zip((side, 1 - side), parts):
                    start = (0, place ^ offset, half, core, 0)
                    part.append(lax.dynamic_slice(cut, start, (count, 1, 1, 1, quarter)))
    kept, given = [jnp.stack(part, axis=1).reshape(count, -1) for part in parts]
    return kept, given


def down_kernel(steps, last, *refs):
    (kept, given), blocks = refs[:2], refs[2 : 2 + 4 * len(steps)]
    so_far, results = (refs[-3], refs[-2:]) if last else (None, refs[-1:])
    depth = 2 * blocks[0].shape[0]
    width = 256
    for start in range(0, blocks[0].shape[1], width):
        columns = slice(start, start + width)
        total = 0.0 if so_far is None else so_far[:, columns]
        for i, step in enumerate(steps):
            for core in range(2):
                inner = pl.ds((2 * step + core) * depth, depth)
                rows = jnp.concatenate([kept[:, inner], given[:, inner]], axis=0)
                near, far = blocks[4 * i + 2 * core], blocks[4 * i + 2 * core + 1]
                block = jnp.concatenate([near[:, columns], far[:, columns]], axis=0)
                total += jnp.dot(rows, block, preferred_element_type=jnp.float32)
        if last:
            count = kept.shape[0]
            results[0][:, columns] = total[:count]
            results[1][:, columns] = total[count:].astype(jnp.bfloat16)
        else:
            results[0][:, columns] = total


def down_project(steps, kept, given, blocks, so_far=None):
    count, inner = kept.shape
    latent_width = blocks[0].shape[1]
    operands = (kept, given, *blocks) + (() if so_far is None else (so_far,))
    if so_far is None:
        shapes = (jax.ShapeDtypeStruct((2 * count, latent_width), jnp.float32),)
    else:
        shapes = (
            jax.ShapeDtypeStruct((count, latent_width), jnp.float32),
            jax.ShapeDtypeStruct((count, latent_width), jnp.bfloat16),
        )
    return pl.pallas_call(
        functools.partial(down_kernel, steps, so_far is not None),
        out_shape=shapes,
        in_specs=[in_vmem] * len(operands),
        out_specs=(in_vmem,) * len(shapes),
        compiler_params=pltpu.CompilerParams(vmem_limit_bytes=16 * mebi),
        cost_estimate=pl.CostEstimate(
            flops=16 * len(steps) * count * blocks[0].shape[0] * latent_width,
            bytes_accessed=2 * len(blocks) * blocks[0].shape[0] * latent_width,
            transcendentals=0,
        ),
        name="down_project",
    )(*operands)


def latent_kernel(own_part, arrived, weights, piece):
    count = own_part.shape[0]
    total = own_part[...] + arrived[...].astype(jnp.float32)
    piece[:count] = total.astype(jnp.bfloat16)
    extra = piece.shape[0] - count
    piece[count:] = jnp.zeros((extra, piece.shape[1]), jnp.bfloat16)
    piece[count:, :count] = weights[...]


def finish_latent(own_part, arrived, weights):
    count, latent_width = own_part.shape
    return pl.pallas_call(
        latent_kernel,
        out_shape=jax.ShapeDtypeStruct((count + weights.shape[0], latent_width), jnp.bfloat16),
        in_specs=[in_vmem] * 3,
        out_specs=in_vmem,
        compiler_params=pltpu.CompilerParams(vmem_limit_bytes=4 * mebi),
        name="finish_latent",
    )(own_part, arrived, weights)


def expert_kernel(positions, count, where, *refs):
    pieces = refs[: 2 * positions]
    gate, up, out = refs[2 * positions : 2 * positions + 3]
    own_sums = refs[2 * positions + 3 : 3 * positions + 3]
    other_sums, rows, hidden, held, gate_block, up_block, out_block, sems = refs[-8:]
    width = 256
    blocks = gate.shape[2] // width

    def columns_at(start):
        return pl.ds(pl.multiple_of(start, width), width)

    def read(i, part):
        source, target = ((gate, gate_block), (up, up_block), (out, out_block))[part]
        columns = columns_at(i * width)
        return pltpu.make_async_copy(
            source.at[0, :, columns], target.at[:, columns], sems.at[part * blocks + i]
        )

    for i in range(blocks):
        read(i, 0).start()
        read(i, 1).start()
    for i in range(out.shape[2] // width):
        read(i, 2).start()
    for i, piece in enumerate(pieces):
        rows[i * count : (i + 1) * count] = piece[:count]

    def scale_of(piece):
        weights = piece[count:, :count].astype(jnp.float32)
        expert = lax.broadcasted_iota(jnp.int32, weights.shape, 0)
        line = jnp.sum(jnp.where(expert == where[0], weights, 0.0), axis=0, keepdims=True)
        row = lax.broadcasted_iota(jnp.int32, (count, count), 0)
        column = lax.broadcasted_iota(jnp.int32, (count, count), 1)
        return jnp.sum(jnp.where(row == column, line, 0.0), axis=1, keepdims=True)

    scales = [scale_of(piece) for piece in pieces]

    def arrive(i):
        read(i, 0).wait()
        read(i, 1).wait()

    def products(i):
        columns = columns_at(i * width)
        return (
            jnp.dot(rows[...], gate_block[:, columns], preferred_element_type=jnp.float32),
            jnp.dot(rows[...], up_block[:, columns], preferred_element_type=jnp.float32),
        )

    def activate(gate_value, up_value, i):
        value = gate_value / (1.0 + jnp.exp(-gate_value)) * up_value
        hidden[:, columns_at(i * width)] = value.astype(jnp.bfloat16)

    arrive(0)
    held[0], held[1] = products(0)

    def step(i, carry):
        arrive(2 * i + 1)
        arrive(2 * i + 2)
        first = products(2 * i + 1)
        activate(held[0], held[1], 2 * i)
        second = products(2 * i + 2)
        activate(*first, 2 * i + 1)
        held[0], held[1] = second
        return carry

    lax.fori_loop(0, blocks // 2 - 1, step, 0)
    arrive(blocks - 1)
    last = products(blocks - 1)
    activate(held[0], held[1], blocks - 2)
    activate(*last, blocks - 1)

    def finish(i, carry):
        columns = columns_at(i * width)
        read(i, 2).wait()
        value = jnp.dot(hidden[...], out_block[:, columns], preferred_element_type=jnp.float32)
        for j, scale in enumerate(scales):
            scaled = (value[j * count : (j + 1) * count] * scale).astype(jnp.bfloat16)
            if j < positions:
                own_sums[j][:, columns] = scaled
            else:
                other_sums[(j - positions) * count : (j - positions + 1) * count, columns] = scaled
        return carry

    lax.fori_loop(0, out.shape[2] // width, finish, 0)


def expert_apply(expert, owns, others, gate_weight, up_weight, out_weight, count):
    positions = len(owns)
    latent_width = owns[0].shape[1]
    hidden_width = gate_weight.shape[2]
    rows = 2 * positions * count
    own_sum = jax.ShapeDtypeStruct((count, latent_width), jnp.bfloat16)
    other_sums = jax.ShapeDtypeStruct((positions * count, latent_width), jnp.bfloat16)
    return pl.pallas_call(
        functools.partial(expert_kernel, positions, count),
        out_shape=(own_sum,) * positions + (other_sums,),
        in_specs=[in_smem] + [in_vmem] * (2 * positions) + [in_hbm] * 3,
        out_specs=(in_vmem,) * (positions + 1),
        scratch_shapes=[
            pltpu.VMEM((rows, latent_width), jnp.bfloat16),
            pltpu.VMEM((rows, hidden_width), jnp.bfloat16),
            pltpu.VMEM((2, rows, 256), jnp.float32),
            pltpu.VMEM((latent_width, hidden_width), jnp.bfloat16),
            pltpu.VMEM((latent_width, hidden_width), jnp.bfloat16),
            pltpu.VMEM((hidden_width, latent_width), jnp.bfloat16),
            pltpu.SemaphoreType.DMA(((2 * hidden_width + latent_width) // 256,)),
        ],
        compiler_params=pltpu.CompilerParams(vmem_limit_bytes=32 * mebi),
        cost_estimate=pl.CostEstimate(
            flops=6 * rows * latent_width * hidden_width,
            bytes_accessed=4 * rows * latent_width,
            transcendentals=rows * hidden_width,
        ),
        name="expert",
    )(expert, *owns, *others, gate_weight, up_weight, out_weight)


def project_kernel(where, *refs):
    terms, refs = refs[:-11], refs[-11:]
    mine, across, near_core, far_core, layer_out, combined, held, held_across, blocks = refs[:9]
    read_sems, sems = refs[9:]
    ep_count, inner, width = mine.shape

    def read(e, i):
        source, target = ((mine, held), (across, held_across))[i]
        return pltpu.make_async_copy(source.at[e], target.at[e], read_sems.at[2 * e + i])

    for e in range(ep_count):
        for i in range(2):
            read(e, i).start()
    total = terms[0][...].astype(jnp.float32)
    for term in terms[1:]:
        total += term[...].astype(jnp.float32)
    combined[...] = total.astype(jnp.bfloat16)

    def sent(e):
        columns = pl.ds(e * width, width)
        return pltpu.make_async_copy(blocks.at[:, columns], layer_out.at[:, columns], sems.at[e])

    for e in range(ep_count):
        value = 0.0
        for i, array in enumerate((near_core, far_core, held, held_across)):
            if i >= 2:
                read(e, i - 2).wait()
            columns = pl.ds(pl.multiple_of(where[i] * inner, inner), inner)
            value += jnp.dot(combined[:, columns], array[e], preferred_element_type=jnp.float32)
        blocks[:, e * width : (e + 1) * width] = value.astype(jnp.bfloat16)
        sent(e).start()
    for e in range(ep_count):
        sent(e).wait()


def project(where, terms, mine, across, near_core, far_core):
    count, latent_width = terms[0].shape
    ep_count, inner, width = mine.shape
    return pl.pallas_call(
        project_kernel,
        in_specs=[in_smem] + [in_vmem] * len(terms) + [in_hbm] * 2 + [in_vmem] * 2,
        out_specs=anywhere,
        out_shape=jax.ShapeDtypeStruct((count, ep_count * width), jnp.bfloat16),
        scratch_shapes=[
            pltpu.VMEM((count, latent_width), jnp.bfloat16),
            pltpu.VMEM(mine.shape, mine.dtype),
            pltpu.VMEM(mine.shape, mine.dtype),
            pltpu.VMEM((count, ep_count * width), jnp.bfloat16),
            pltpu.SemaphoreType.DMA((2 * ep_count,)),
            pltpu.SemaphoreType.DMA((ep_count,)),
        ],
        compiler_params=pltpu.CompilerParams(vmem_limit_bytes=16 * mebi),
        cost_estimate=pl.CostEstimate(
            flops=2 * count * latent_width * ep_count * width,
            bytes_accessed=2 * latent_width * ep_count * width,
            transcendentals=0,
        ),
        name="project",
    )(where, *terms, mine, across, near_core, far_core)


def body(
    tokens, expert_ids, route_scores, down_latent, gate_weight, up_weight, out_weight, up_latent
):
    group_count = lax.axis_size("grp")
    ep_count = lax.axis_size("ep")
    expert_count = group_count * ep_count * gate_weight.shape[0]
    rep, group, place = lax.axis_index("rep"), lax.axis_index("grp"), lax.axis_index("ep")
    side = rep % 2
    own_quarter = 2 * side + group
    token_count = tokens.shape[0]
    latent_width = down_latent.shape[1]
    steps = ep_count // 2
    last = steps - 1

    inner = latent_width // 4
    up_piece = lax.dynamic_slice_in_dim(up_latent, own_quarter * inner, inner, 0)
    mine = lax.all_gather(up_piece, "ep", axis=0)

    quarter = down_latent.shape[0] // 4

    def own_piece(core):
        return lax.dynamic_slice_in_dim(down_latent, (2 * side + core) * quarter, quarter, 0)

    kept, given = split_columns(tokens, ep_count, quarter, place, side, group)
    taken = swap_reps(given)
    near = first_steps(own_piece(group), steps)
    far = {0: swap_ep(near[0], 1)}
    near[1], kept = join(near[1], kept)
    far[1] = swap_ep(near[1], 1)
    weights = dense_weights(after(expert_ids, near[1]), route_scores, expert_count)
    others = {k: near[k] for k in near if k > 1}
    *arrived, weights = join(*others.values(), weights)
    near.update(zip(others, arrived))
    for k in range(2, steps):
        if k & (k - 1):
            low = k & -k
            near[k] = swap_ep(near[k ^ low], 2 * low)
        if k == last:
            near[k], far[1], taken = join(near[k], far[1], taken)
        far[k] = swap_ep(near[k], 1)
    blocks = []
    for k in range(steps):
        other = own_piece(1 - group) if k == 0 else swap_cores(near[k])
        blocks.append((near[k], far[k], other, swap_cores(far[k])))
    early = list(range(last))
    (partial,) = down_project(early, kept, taken, [b for k in early for b in blocks[k]])
    late = [after(blocks[-1][0], partial), *blocks[-1][1:]]
    own_part, sent_part = down_project([last], kept, taken, late, partial)
    latent = finish_latent(own_part, swap_reps(sent_part), weights.astype(jnp.bfloat16))

    gate_weight, up_weight, out_weight = [
        pltpu.with_memory_space_constraint(w, pltpu.HBM) for w in (gate_weight, up_weight, out_weight)
    ]
    expert = (group * ep_count + place).astype(jnp.int32).reshape(1)
    near = first_steps(latent, steps)
    far, away, sent, pairs, own_sums, swapped = {}, {}, {}, {}, {}, {}

    def run(which, coming, *waits):
        owns = [(near, far)[y][k] for k, y in which]
        operands = owns + [swap_cores(own) for own in owns]
        operands = join(*operands, *waits)[: len(operands)]
        count = len(which)
        sums = expert_apply(
            expert,
            operands[:count],
            operands[count:],
            gate_weight,
            up_weight,
            out_weight,
            token_count,
        )
        names = [(table, key) for table, keys in coming for key in keys]
        sums = join(*sums, *[table[key] for table, key in names])
        for (table, key), value in zip(names, sums[count + 1 :]):
            table[key] = value
        others = swap_cores(sums[count])
        for i, place_of in enumerate(which):
            own_sums[place_of] = sums[i]
            swapped[place_of] = others[i * token_count : (i + 1) * token_count]
        return sums[0]

    def chip_sum(k, y):
        return own_sums[k, y].astype(jnp.float32) + swapped[k, y].astype(jnp.float32)

    def send_far(k):
        sent[k] = chip_sum(k, 1).astype(jnp.bfloat16)
        away[k] = swap_ep(sent[k], 1)

    def pair_sum(k):
        pairs[k] = (chip_sum(k, 0) + away[k].astype(jnp.float32)).astype(jnp.bfloat16)

    def start_near(k):
        near[k] = swap_ep(near[k ^ (k & -k)], 2 * (k & -k))

    def start_far(k):
        far[k] = swap_ep(near[k], 1)

    gathered = {"mine": mine}
    powers = [k for k in near if k]
    run([(0, 0)], [(near, powers)])
    if last >= 3:
        start_near(3)
    start_far(2)
    run([(1, 0), (2, 0)], [(near, [3]), (far, [2]), (gathered, ["mine"])])
    mine = gathered["mine"]
    gathered["across"] = swap_reps(mine)
    returning = []
    for k in range(3, steps):
        start_far(k)
        if k == 3:
            start_far(0)
        coming = [(far, [0, k] if k == 3 else [k]), (away, returning)]
        if k + 1 < steps and k + 1 not in near:
            start_near(k + 1)
            coming.append((near, [k + 1]))
        run([(k, 0), (k - 1, 1)], coming, *pairs.values())
        for j in returning:
            pair_sum(j)
        send_far(k - 1)
        returning = [k - 1]
    start_far(1)
    near_home = chip_sum(1, 0).astype(jnp.bfloat16)
    run([(last, 1)], [(away, returning), (far, [1])], near_home, *sent.values(), *pairs.values())
    for j in returning:
        pair_sum(j)
    send_far(last)
    homeward = {"near": swap_ep(near_home, 2)}
    run(
        [(0, 1), (1, 1)],
        [(away, [last]), (gathered, ["across"]), (homeward, ["near"])],
        sent[last],
        *pairs.values(),
    )
    across = gathered["across"]
    pair_sum(last)
    send_far(0)
    far_home = chip_sum(1, 1).astype(jnp.bfloat16)
    pair_sum(0)
    terms = [pairs[0], homeward["near"], swap_ep(far_home, 3)]
    terms += [swap_ep(pairs[k], 2 * k) for k in range(2, steps)]

    where = [own_quarter ^ 1, own_quarter ^ 3, own_quarter, own_quarter ^ 2]
    where = jnp.stack(where).astype(jnp.int32)
    return project(where, terms, mine, across, swap_cores(mine), swap_cores(across))


def solution(mesh):
    in_specs = (
        P(("rep", "grp", "ep"), None),
        P(("rep", "grp", "ep"), None),
        P(("rep", "grp", "ep"), None),
        P("ep", None),
        P(("grp", "ep"), None, None),
        P(("grp", "ep"), None, None),
        P(("grp", "ep"), None, None),
        P(None, "ep"),
    )
    out_specs = P(("rep", "grp", "ep"), None)
    return jax.shard_map(body, mesh=mesh, in_specs=in_specs, out_specs=out_specs, check_vma=False)
```

time: 197 us -> 219 us (1.11); the launches traced: 194 us -> 219 us
  waiting for transfers between devices: 69.1 us -> 98.7 us
  Pallas kernels: 45 us -> 53.9 us
  local copies, waits for them, and re-layouts: 15.4 us -> 6.85 us
  starting transfers between devices: 47 us -> 40.6 us
    ppermute x2 -> x3, waiting for transfers between devices: 8.39 us -> 23.6 us  [swap_reps(): lax.ppermute(array, 'rep', [(i, i ^ 1) for i in range(lax.axis_size('rep'...]
    ppermute x21, waiting for transfers between devices: 55 us -> 68.9 us  [swap_ep(): lax.ppermute(array, 'ep', [(i, i ^ mask) for i in range(lax.axis_size('ep...]
    pallas_call x6 -> x7, Pallas kernels: 40.6 us -> 51.6 us  [the longest x5 45.4 us: expert_apply(): pl.pallas_call(functools.partial(expert_kernel, positions, count), out_sh...]
    unnamed x22 -> x36, local copies, waits for them, and re-layouts: 10.8 us -> 5.08 us
    all_to_all x1 -> x0, starting transfers between devices: 4.14 us -> none  [body(): lax.all_to_all(weights, ('grp', 'ep'), split_axis=0, concat_axis=0, tiled...]
    convert_element_type x9 -> x7, other arithmetic: 0.81 us -> 4.49 us  [the longest x3 3.29 us: pair_sum(): (chip_sum(k, 0) + away[k].astype(jnp.float32)).astype(jnp.bfloat16)]
    ppermute x24 -> x22, waiting for transfers between devices: 2.77 us -> 6.24 us  [swap_cores(): return lax.ppermute(array, 'grp', [(0, 1), (1, 0)])]
    all_to_all x1 -> x0, waiting for transfers between devices: 2.94 us -> none  [body(): lax.all_to_all(weights, ('grp', 'ep'), split_axis=0, concat_axis=0, tiled...]
  transfers between devices with their start and end apart: 49 -> 47, of which waited for: 19 -> 21; matrix products, arithmetic and copies ran while one was open for 4% -> 3% of each run, Pallas kernels for 20% -> 22%
where the time goes in v5:
time: 219 us
  waiting for transfers between devices  98.7 us (45%)
  Pallas kernels  53.9 us (25%)
  starting transfers between devices  40.6 us (19%)
  between operations  13.8 us (6%)
  local copies, waits for them, and re-layouts  6.85 us (3%)
  other arithmetic  4.71 us (2%)
    ppermute x21, waiting for transfers between devices, swap_ep(): lax.ppermute(array, 'ep', [(i, i ^ mask) for i in range(lax.axis_size('ep...  68.9 us
    pallas_call x5, Pallas kernels, expert_apply(): pl.pallas_call(functools.partial(expert_kernel, positions, count), out_sh...  45.4 us
    ppermute x21, starting transfers between devices, swap_ep(): lax.ppermute(array, 'ep', [(i, i ^ mask) for i in range(lax.axis_size('ep...  32.2 us
    ppermute x3, waiting for transfers between devices, swap_reps(): lax.ppermute(array, 'rep', [(i, i ^ 1) for i in range(lax.axis_size('rep'...  23.6 us
    ppermute x22, waiting for transfers between devices, swap_cores(): return lax.ppermute(array, 'grp', [(0, 1), (1, 0)])  6.24 us
    pallas_call x1, Pallas kernels, project(): pl.pallas_call(project_kernel, in_specs=[in_smem] + [in_vmem] * len(terms...  6.17 us
    ppermute x3, starting transfers between devices, swap_reps(): lax.ppermute(array, 'rep', [(i, i ^ 1) for i in range(lax.axis_size('rep'...  5.08 us
    unnamed x36, local copies, waits for them, and re-layouts  5.08 us
  transfers between devices with their start and end apart: 47, of which 21 were waited for; matrix products, arithmetic and copies ran while one was open for 3% of the time, Pallas kernels for 22%

profile of v5, /device:TPU:0, one launch (start us, length us, event | category | flops | bytes accessed | tf_op | source)
XLA Modules:
  0.0 218.5 jit_solution(12092745169411872848)
XLA Ops:
  6.6 1.2 copy-done
  8.5 1.1 constant_dynamic-slice_fusion.1
  9.6 3.0 %collective-permute-start.5 = (bf16[128,1024]{1,0:T(8,128)(2,1)S(1)}, bf16[128,1024]{1,0:T(8,128)(2,1)S(1)}, u32[]{:S(2)}, u32[]{:S(2)}) collective-permute-start(bf16[128,1024]{1,0:T(8,128)(2,1)S(1)} %get-tuple-element.140.refs_2_), channel_id=1, source_target_pairs={{0,1},{1,0},{2,3},{3,2},{4,5},{5,4},{6,7},{7,6},{8,9},{9,8},{10,11... | collective-permute-start | bytes 786440 | tf_op jit(solution)/shard_map/ppermute | solution.py:35
  12.6 2.6 %collective-permute-start.1 = (bf16[128,1024]{1,0:T(8,128)(2,1)S(1)}, bf16[128,1024]{1,0:T(8,128)(2,1)S(1)}, u32[]{:S(2)}, u32[]{:S(2)}) collective-permute-start(bf16[128,1024]{1,0:T(8,128)(2,1)S(1)} %get-tuple-element.140.refs_2_), channel_id=1, source_target_pairs={{0,4},{1,5},{2,6},{3,7},{4,0},{5,1},{6,2},{7,3},{8,12},{9,13},{10,... | collective-permute-start | bytes 786440 | tf_op jit(solution)/shard_map/ppermute | solution.py:35
  15.2 1.6 collective-permute-start
  16.9 0.8 split_columns.1
  17.7 1.6 collective-permute-start.4
  19.3 11.3 %collective-permute-done.refs_6_ = bf16[128,1024]{1,0:T(8,128)(2,1)S(1)} collective-permute-done((bf16[128,1024]{1,0:T(8,128)(2,1)S(1)}, bf16[128,1024]{1,0:T(8,128)(2,1)S(1)}, u32[]{:S(2)}, u32[]{:S(2)}) %collective-permute-start) | collective-permute-done | bytes 262176 | tf_op jit(solution)/shard_map/ppermute | solution.py:35
  30.8 2.8 %collective-permute-start.2 = (bf16[128,1024]{1,0:T(8,128)(2,1)S(1)}, bf16[128,1024]{1,0:T(8,128)(2,1)S(1)}, u32[]{:S(2)}, u32[]{:S(2)}) collective-permute-start(bf16[128,1024]{1,0:T(8,128)(2,1)S(1)} %collective-permute-done.1.refs_10_), channel_id=1, source_target_pairs={{0,2},{1,3},{2,0},{3,1},{4,6},{5,7},{6,4},{7,5},{8,10},{9,11},{10,... | collective-permute-start | bytes 786440 | tf_op jit(solution)/shard_map/ppermute | solution.py:35
  33.6 2.0 collective-permute-start.9
  35.6 5.7 %collective-permute-done.2.refs_2_ = bf16[128,1024]{1,0:T(8,128)(2,1)S(1)} collective-permute-done((bf16[128,1024]{1,0:T(8,128)(2,1)S(1)}, bf16[128,1024]{1,0:T(8,128)(2,1)S(1)}, u32[]{:S(2)}, u32[]{:S(2)}) %collective-permute-start.2) | collective-permute-done | bytes 262176 | tf_op jit(solution)/shard_map/ppermute | solution.py:35
  41.3 1.5 collective-permute-done.3.refs_7_
  42.9 8.5 %collective-permute-done.9.refs_11_ = bf16[128,1024]{1,0:T(8,128)(2,1)S(1)} collective-permute-done((bf16[128,1024]{1,0:T(8,128)(2,1)S(1)}, bf16[128,1024]{1,0:T(8,128)(2,1)S(1)}, u32[]{:S(2)}, u32[]{:S(2)}) %collective-permute-start.9) | collective-permute-done | bytes 262176 | tf_op jit(solution)/shard_map/ppermute | solution.py:35
  52.0 8.7 %collective-permute-done.12.refs_3_ = bf16[128,1024]{1,0:T(8,128)(2,1)S(1)} collective-permute-done((bf16[128,1024]{1,0:T(8,128)(2,1)S(1)}, bf16[128,1024]{1,0:T(8,128)(2,1)S(1)}, u32[]{:S(2)}, u32[]{:S(2)}) %collective-permute-start.12) | collective-permute-done | bytes 262176 | tf_op jit(solution)/shard_map/ppermute | solution.py:35
  60.8 1.0 down_project.2.refs_6_
  62.7 1.8 collective-permute-start.15
  64.5 6.6 %collective-permute-done.15.arrived = bf16[128,1024]{1,0:T(8,128)(2,1)S(1)} collective-permute-done((bf16[128,1024]{1,0:T(8,128)(2,1)S(1)}, bf16[128,1024]{1,0:T(8,128)(2,1)S(1)}, u32[]{:S(2)}, u32[]{:S(2)}) %collective-permute-start.15) | collective-permute-done | bytes 262176 | tf_op jit(solution)/shard_map/ppermute | solution.py:31
  71.3 6.2 %collective-permute-start.18 = (bf16[144,1024]{1,0:T(8,128)(2,1)S(1)}, bf16[144,1024]{1,0:T(8,128)(2,1)S(1)}, u32[]{:S(2)}, u32[]{:S(2)}) collective-permute-start(bf16[144,1024]{1,0:T(8,128)(2,1)S(1)} %finish_latent.1.refs_0_), channel_id=1, source_target_pairs={{0,4},{1,5},{2,6},{3,7},{4,0},{5,1},{6,2},{7,3},{8,12},{9,13},{10,... | collective-permute-start | bytes 884744 | tf_op jit(solution)/shard_map/ppermute | solution.py:35
  77.5 7.5 %expert.5 = (bf16[128,1024]{1,0:T(8,128)(2,1)S(1)}, bf16[128,1024]{1,0:T(8,128)(2,1)}) custom-call(s32[1]{0:T(128)} %bitcast.4.where, bf16[144,1024]{1,0:T(8,128)(2,1)S(1)} %finish_latent.1.refs_0_, bf16[144,1024]{1,0:T(8,128)(2,1)S(1)} %collective-permute-done.16.refs_1_, bf16[1,1024,2048]{2,1,0:T(8,128)(2,1)} %refs_4_.9, bf16[1,1024,2048]{2,1,0:T(8,128)(2,1)} %refs_5_.5, ...), custom_call_target="tpu_custom_call" | custom-call | flops 3221225472 | bytes 1048576 | tf_op jit(solution)/shard_map/expert/pallas_call | solution.py:248
  85.0 4.7 %collective-permute-done.18.refs_1_ = bf16[144,1024]{1,0:T(8,128)(2,1)S(1)} collective-permute-done((bf16[144,1024]{1,0:T(8,128)(2,1)S(1)}, bf16[144,1024]{1,0:T(8,128)(2,1)S(1)}, u32[]{:S(2)}, u32[]{:S(2)}) %collective-permute-start.18) | collective-permute-done | bytes 294944 | tf_op jit(solution)/shard_map/ppermute | solution.py:35
  89.7 3.1 %collective-permute-done.17.refs_0_ = bf16[144,1024]{1,0:T(8,128)(2,1)S(1)} collective-permute-done((bf16[144,1024]{1,0:T(8,128)(2,1)S(1)}, bf16[144,1024]{1,0:T(8,128)(2,1)S(1)}, u32[]{:S(2)}, u32[]{:S(2)}) %collective-permute-start.17) | collective-permute-done | bytes 294944 | tf_op jit(solution)/shard_map/ppermute | solution.py:35
  94.8 10.0 %expert.6 = (bf16[128,1024]{1,0:T(8,128)(2,1)S(1)}, bf16[128,1024]{1,0:T(8,128)(2,1)S(1)}, bf16[256,1024]{1,0:T(8,128)(2,1)S(1)}) custom-call(s32[1]{0:T(128)} %bitcast.4.where, bf16[144,1024]{1,0:T(8,128)(2,1)S(1)} %collective-permute-done.17.refs_0_, bf16[144,1024]{1,0:T(8,128)(2,1)S(1)} %collective-permute-done.18.refs_1_, ...), custom_call_target="tpu_custom_call" | custom-call | flops 6442450944 | bytes 2097152 | tf_op jit(solution)/shard_map/expert/pallas_call | solution.py:248
  106.2 0.8 copy-done.9
  108.3 1.0 collective-permute-start.26
  109.3 1.1 collective-permute-start.27
  110.3 1.0 copy-done.13
  111.3 10.9 %expert.7 = (bf16[128,1024]{1,0:T(8,128)(2,1)S(1)}, bf16[128,1024]{1,0:T(8,128)(2,1)S(1)}, bf16[256,1024]{1,0:T(8,128)(2,1)S(1)}) custom-call(s32[1]{0:T(128)} %bitcast.4.where, bf16[144,1024]{1,0:T(8,128)(2,1)} %collective-permute-done.22.refs_0_, bf16[144,1024]{1,0:T(8,128)(2,1)S(1)} %copy-done.13, bf16[144,1024]{1,0:T(8,128)(2,1)S(1)} %collective-permute-done.24.refs_2_, ...), custom_call_target="tpu_custom_call" | custom-call | flops 6442450944 | bytes 2097152 | tf_op jit(solution)/shard_map/expert/pallas_call | solution.py:248
  122.2 1.4 collective-permute-done.27.refs_0_
  123.7 1.7 collective-permute-start.37
  125.4 0.9 collective-permute-start.32
  126.5 1.2 collective-permute-start.31
  127.9 6.8 %expert.8 = (bf16[128,1024]{1,0:T(8,128)(2,1)S(1)}, bf16[128,1024]{1,0:T(8,128)(2,1)S(1)}) custom-call(s32[1]{0:T(128)} %bitcast.4.where, bf16[144,1024]{1,0:T(8,128)(2,1)S(1)} %collective-permute-done.27.refs_0_, bf16[144,1024]{1,0:T(8,128)(2,1)S(1)} %collective-permute-done.28.refs_1_, bf16[1,1024,2048]{2,1,0:T(8,128)(2,1)} %refs_4_.9, ...), custom_call_target="tpu_custom_call" | custom-call | flops 3221225472 | bytes 1048576 | tf_op jit(solution)/shard_map/expert/pallas_call | solution.py:248
  135.3 4.9 %collective-permute-done.31 = bf16[128,1024]{1,0:T(8,128)(2,1)S(1)} collective-permute-done((bf16[128,1024]{1,0:T(8,128)(2,1)S(1)}, bf16[128,1024]{1,0:T(8,128)(2,1)S(1)}, u32[]{:S(2)}, u32[]{:S(2)}) %collective-permute-start.31) | collective-permute-done | bytes 262176 | tf_op jit(solution)/shard_map/ppermute | solution.py:35
  141.2 0.8 add_convert_fusion.4
  142.9 1.8 collective-permute-start.36
  144.7 10.2 %expert.9 = (bf16[128,1024]{1,0:T(8,128)(2,1)S(1)}, bf16[128,1024]{1,0:T(8,128)(2,1)S(1)}, bf16[256,1024]{1,0:T(8,128)(2,1)S(1)}) custom-call(s32[1]{0:T(128)} %bitcast.4.where, bf16[144,1024]{1,0:T(8,128)(2,1)S(1)} %collective-permute-done.26.refs_0_, bf16[144,1024]{1,0:T(8,128)(2,1)S(1)} %collective-permute-done.32.refs_1_, ...), custom_call_target="tpu_custom_call" | custom-call | flops 6442450944 | bytes 2097152 | tf_op jit(solution)/shard_map/expert/pallas_call | solution.py:248
  154.9 16.9 %collective-permute-done.37.refs_6_ = bf16[8,256,512]{2,1,0:T(8,128)(2,1)} collective-permute-done((bf16[8,256,512]{2,1,0:T(8,128)(2,1)S(1)}, bf16[8,256,512]{2,1,0:T(8,128)(2,1)}, u32[]{:S(2)}, u32[]{:S(2)}) %collective-permute-start.37) | collective-permute-done | bytes 2097184 | tf_op jit(solution)/shard_map/ppermute | solution.py:31
  172.3 4.4 %collective-permute-done.39 = bf16[256,1024]{1,0:T(8,128)(2,1)S(1)} collective-permute-done((bf16[256,1024]{1,0:T(8,128)(2,1)S(1)}, bf16[256,1024]{1,0:T(8,128)(2,1)S(1)}, u32[]{:S(2)}, u32[]{:S(2)}) %collective-permute-start.39) | collective-permute-done | bytes 524320 | tf_op jit(solution)/shard_map/ppermute | solution.py:27
  176.7 1.0 add_convert_fusion.1
  177.7 0.9 collective-permute-start.40
  178.7 1.2 add_convert_fusion
  179.9 4.0 %collective-permute-start.43 = (bf16[128,1024]{1,0:T(8,128)(2,1)S(1)}, bf16[128,1024]{1,0:T(8,128)(2,1)S(1)}, u32[]{:S(2)}, u32[]{:S(2)}) collective-permute-start(bf16[128,1024]{1,0:T(8,128)(2,1)S(1)} %add_convert_fusion), channel_id=1, source_target_pairs={{0,6},{1,7},{2,4},{3,5},{4,2},{5,3},{6,0},{7,1},{8,14},{9,15},{10,... | collective-permute-start | bytes 786440 | tf_op jit(solution)/shard_map/ppermute | solution.py:35
  183.9 2.7 %collective-permute-done.40 = bf16[128,1024]{1,0:T(8,128)(2,1)} collective-permute-done((bf16[128,1024]{1,0:T(8,128)(2,1)}, bf16[128,1024]{1,0:T(8,128)(2,1)}, u32[]{:S(2)}, u32[]{:S(2)}) %collective-permute-start.40) | collective-permute-done | bytes 262176 | tf_op jit(solution)/shard_map/ppermute | solution.py:35
  186.6 1.9 collective-permute-start.41
  188.7 1.2 add_convert_fusion.2.refs_0_
  189.9 10.3 %collective-permute-done.42.refs_3_ = bf16[128,1024]{1,0:T(8,128)(2,1)S(1)} collective-permute-done((bf16[128,1024]{1,0:T(8,128)(2,1)}, bf16[128,1024]{1,0:T(8,128)(2,1)S(1)}, u32[]{:S(2)}, u32[]{:S(2)}) %collective-permute-start.42) | collective-permute-done | bytes 262176 | tf_op jit(solution)/shard_map/ppermute | solution.py:35
  200.2 5.2 %collective-permute-done.41.refs_2_ = bf16[128,1024]{1,0:T(8,128)(2,1)S(1)} collective-permute-done((bf16[128,1024]{1,0:T(8,128)(2,1)}, bf16[128,1024]{1,0:T(8,128)(2,1)S(1)}, u32[]{:S(2)}, u32[]{:S(2)}) %collective-permute-start.41) | collective-permute-done | bytes 262176 | tf_op jit(solution)/shard_map/ppermute | solution.py:35
  205.5 6.2 %project.1 = bf16[128,4096]{1,0:T(8,128)(2,1)} custom-call(s32[4]{0:T(128)S(1)} %pad_add_fusion.where, bf16[128,1024]{1,0:T(8,128)(2,1)S(1)} %add_convert_fusion.2.refs_0_, bf16[128,1024]{1,0:T(8,128)(2,1)S(1)} %collective-permute-done.38.refs_1_, bf16[128,1024]{1,0:T(8,128)(2,1)S(1)} %collective-permute-done.41.refs_2_, ...), custom_call_target="tpu_custom_call" | custom-call | flops 1073741824 | bytes 8388608 | tf_op jit(solution)/shard_map/project/pallas_call | solution.py:310
  (107 shorter events, 10.9 us)
Async XLA Ops:
  6.5 24.0 %copy-start.17 = (s32[128,8]{0,1:T(8,128)S(1)}, s32[128,8]{0,1:T(8,128)}, u32[]{:S(2)}) copy-start(s32[128,8]{0,1:T(8,128)} %param.9) | copy-start | bytes 12292
  6.5 101.2 %all-gather.3.cloned.1.call-start = ((), (), s32[]{:S(2)}) async-start(), calls=%async_computation | async-start | bytes 2359296 | tf_op jit(solution)/shard_map/all_gather | solution.py:349
  9.6 26.1 %collective-permute-start.5 = (bf16[128,1024]{1,0:T(8,128)(2,1)S(1)}, bf16[128,1024]{1,0:T(8,128)(2,1)S(1)}, u32[]{:S(2)}, u32[]{:S(2)}) collective-permute-start(bf16[128,1024]{1,0:T(8,128)(2,1)S(1)} %get-tuple-element.140.refs_2_), channel_id=1, source_target_pairs={{0,1},{1,0},{2,3},{3,2},{4,5},{5,4},{6,7},{7,6},{8,9},{9,8},{10,11... | collective-permute-start | bytes 786440 | tf_op jit(solution)/shard_map/ppermute | solution.py:35
  12.6 18.2 %collective-permute-start.1 = (bf16[128,1024]{1,0:T(8,128)(2,1)S(1)}, bf16[128,1024]{1,0:T(8,128)(2,1)S(1)}, u32[]{:S(2)}, u32[]{:S(2)}) collective-permute-start(bf16[128,1024]{1,0:T(8,128)(2,1)S(1)} %get-tuple-element.140.refs_2_), channel_id=1, source_target_pairs={{0,4},{1,5},{2,6},{3,7},{4,0},{5,1},{6,2},{7,3},{8,12},{9,13},{10,... | collective-permute-start | bytes 786440 | tf_op jit(solution)/shard_map/ppermute | solution.py:35
  15.2 15.4 %collective-permute-start = (bf16[128,1024]{1,0:T(8,128)(2,1)S(1)}, bf16[128,1024]{1,0:T(8,128)(2,1)S(1)}, u32[]{:S(2)}, u32[]{:S(2)}) collective-permute-start(bf16[128,1024]{1,0:T(8,128)(2,1)S(1)} %get-tuple-element.140.refs_2_), channel_id=1, source_target_pairs={{0,2},{1,3},{2,0},{3,1},{4,6},{5,7},{6,4},{7,5},{8,10},{9,11},{10,... | collective-permute-start | bytes 786440 | tf_op jit(solution)/shard_map/ppermute | solution.py:35
  17.7 25.2 %collective-permute-start.4 = (bf16[128,2048]{1,0:T(8,128)(2,1)S(1)}, bf16[128,2048]{1,0:T(8,128)(2,1)S(1)}, u32[]{:S(2)}, u32[]{:S(2)}) collective-permute-start(bf16[128,2048]{1,0:T(8,128)(2,1)S(1)} %get-tuple-element.77), channel_id=1, source_target_pairs={{0,16},{16,0},{1,17},{17,1},{2,18},{18,2},{3,19},{19,3},{4,20},{20... | collective-permute-start | bytes 1572872 | tf_op jit(solution)/shard_map/ppermute | solution.py:31
  30.8 10.5 %collective-permute-start.2 = (bf16[128,1024]{1,0:T(8,128)(2,1)S(1)}, bf16[128,1024]{1,0:T(8,128)(2,1)S(1)}, u32[]{:S(2)}, u32[]{:S(2)}) collective-permute-start(bf16[128,1024]{1,0:T(8,128)(2,1)S(1)} %collective-permute-done.1.refs_10_), channel_id=1, source_target_pairs={{0,2},{1,3},{2,0},{3,1},{4,6},{5,7},{6,4},{7,5},{8,10},{9,11},{10,... | collective-permute-start | bytes 786440 | tf_op jit(solution)/shard_map/ppermute | solution.py:35
  33.6 9.2 %collective-permute-start.3 = (bf16[128,1024]{1,0:T(8,128)(2,1)S(1)}, bf16[128,1024]{1,0:T(8,128)(2,1)S(1)}, u32[]{:S(2)}, u32[]{:S(2)}) collective-permute-start(bf16[128,1024]{1,0:T(8,128)(2,1)S(1)} %collective-permute-done.refs_6_), channel_id=1, source_target_pairs={{0,1},{1,0},{2,3},{3,2},{4,5},{5,4},{6,7},{7,6},{8,9},{9,8},{10,11... | collective-permute-start | bytes 786440 | tf_op jit(solution)/shard_map/ppermute | solution.py:35
  33.6 17.8 %collective-permute-start.9 = (bf16[128,1024]{1,0:T(8,128)(2,1)S(1)}, bf16[128,1024]{1,0:T(8,128)(2,1)S(1)}, u32[]{:S(2)}, u32[]{:S(2)}) collective-permute-start(bf16[128,1024]{1,0:T(8,128)(2,1)S(1)} %collective-permute-done.1.refs_10_), channel_id=1, source_target_pairs={{0,1},{1,0},{2,3},{3,2},{4,5},{5,4},{6,7},{7,6},{8,9},{9,8},{10,11... | collective-permute-start | bytes 786440 | tf_op jit(solution)/shard_map/ppermute | solution.py:35
  35.6 15.8 %collective-permute-start.6 = (bf16[128,1024]{1,0:T(8,128)(2,1)S(1)}, bf16[128,1024]{1,0:T(8,128)(2,1)S(1)}, u32[]{:S(2)}, u32[]{:S(2)}) collective-permute-start(bf16[128,1024]{1,0:T(8,128)(2,1)S(1)} %collective-permute-done.5.refs_3_), channel_id=1, source_target_pairs={{0,8},{8,0},{1,9},{9,1},{2,10},{10,2},{3,11},{11,3},{4,12},{12,4},... | collective-permute-start | bytes 786440 | tf_op jit(solution)/shard_map/ppermute | solution.py:27
  41.3 10.6 %collective-permute-start.10 = (bf16[128,1024]{1,0:T(8,128)(2,1)S(1)}, bf16[128,1024]{1,0:T(8,128)(2,1)S(1)}, u32[]{:S(2)}, u32[]{:S(2)}) collective-permute-start(bf16[128,1024]{1,0:T(8,128)(2,1)S(1)} %collective-permute-done.1.refs_10_), channel_id=1, source_target_pairs={{0,8},{8,0},{1,9},{9,1},{2,10},{10,2},{3,11},{11,3},{4,12},{12,4},... | collective-permute-start | bytes 786440 | tf_op jit(solution)/shard_map/ppermute | solution.py:27
  42.9 17.9 %collective-permute-start.12 = (bf16[128,1024]{1,0:T(8,128)(2,1)S(1)}, bf16[128,1024]{1,0:T(8,128)(2,1)S(1)}, u32[]{:S(2)}, u32[]{:S(2)}) collective-permute-start(bf16[128,1024]{1,0:T(8,128)(2,1)S(1)} %collective-permute-done.2.refs_2_), channel_id=1, source_target_pairs={{0,1},{1,0},{2,3},{3,2},{4,5},{5,4},{6,7},{7,6},{8,9},{9,8},{10,11... | collective-permute-start | bytes 786440 | tf_op jit(solution)/shard_map/ppermute | solution.py:35
  42.9 17.9 %collective-permute-start.7 = (bf16[128,1024]{1,0:T(8,128)(2,1)S(1)}, bf16[128,1024]{1,0:T(8,128)(2,1)S(1)}, u32[]{:S(2)}, u32[]{:S(2)}) collective-permute-start(bf16[128,1024]{1,0:T(8,128)(2,1)S(1)} %collective-permute-done.refs_6_), channel_id=1, source_target_pairs={{0,8},{8,0},{1,9},{9,1},{2,10},{10,2},{3,11},{11,3},{4,12},{12,4},... | collective-permute-start | bytes 786440 | tf_op jit(solution)/shard_map/ppermute | solution.py:27
  51.4 9.3 %collective-permute-start.11 = (bf16[128,1024]{1,0:T(8,128)(2,1)S(1)}, bf16[128,1024]{1,0:T(8,128)(2,1)S(1)}, u32[]{:S(2)}, u32[]{:S(2)}) collective-permute-start(bf16[128,1024]{1,0:T(8,128)(2,1)S(1)} %collective-permute-done.9.refs_11_), channel_id=1, source_target_pairs={{0,8},{8,0},{1,9},{9,1},{2,10},{10,2},{3,11},{11,3},{4,12},{12,4},... | collective-permute-start | bytes 786440 | tf_op jit(solution)/shard_map/ppermute | solution.py:27
  51.4 9.3 %collective-permute-start.8 = (bf16[128,1024]{1,0:T(8,128)(2,1)S(1)}, bf16[128,1024]{1,0:T(8,128)(2,1)S(1)}, u32[]{:S(2)}, u32[]{:S(2)}) collective-permute-start(bf16[128,1024]{1,0:T(8,128)(2,1)S(1)} %collective-permute-done.3.refs_7_), channel_id=1, source_target_pairs={{0,8},{8,0},{1,9},{9,1},{2,10},{10,2},{3,11},{11,3},{4,12},{12,4},... | collective-permute-start | bytes 786440 | tf_op jit(solution)/shard_map/ppermute | solution.py:27
  51.9 9.8 %collective-permute-start.13 = (bf16[128,1024]{1,0:T(8,128)(2,1)S(1)}, bf16[128,1024]{1,0:T(8,128)(2,1)S(1)}, u32[]{:S(2)}, u32[]{:S(2)}) collective-permute-start(bf16[128,1024]{1,0:T(8,128)(2,1)S(1)} %collective-permute-done.2.refs_2_), channel_id=1, source_target_pairs={{0,8},{8,0},{1,9},{9,1},{2,10},{10,2},{3,11},{11,3},{4,12},{12,4},... | collective-permute-start | bytes 786440 | tf_op jit(solution)/shard_map/ppermute | solution.py:27
  60.7 1.5 collective-permute-start.14
  62.7 8.4 %collective-permute-start.15 = (bf16[128,1024]{1,0:T(8,128)(2,1)S(1)}, bf16[128,1024]{1,0:T(8,128)(2,1)S(1)}, u32[]{:S(2)}, u32[]{:S(2)}) collective-permute-start(bf16[128,1024]{1,0:T(8,128)(2,1)S(1)} %get-tuple-element.83), channel_id=1, source_target_pairs={{0,16},{16,0},{1,17},{17,1},{2,18},{18,2},{3,19},{19,3},{4,20},{20... | collective-permute-start | bytes 786440 | tf_op jit(solution)/shard_map/ppermute | solution.py:31
  71.2 6.3 %collective-permute-start.16 = (bf16[144,1024]{1,0:T(8,128)(2,1)S(1)}, bf16[144,1024]{1,0:T(8,128)(2,1)S(1)}, u32[]{:S(2)}, u32[]{:S(2)}) collective-permute-start(bf16[144,1024]{1,0:T(8,128)(2,1)S(1)} %finish_latent.1.refs_0_), channel_id=1, source_target_pairs={{0,8},{8,0},{1,9},{9,1},{2,10},{10,2},{3,11},{11,3},{4,12},{12,4},... | collective-permute-start | bytes 884744 | tf_op jit(solution)/shard_map/ppermute | solution.py:27
  71.3 18.4 %collective-permute-start.18 = (bf16[144,1024]{1,0:T(8,128)(2,1)S(1)}, bf16[144,1024]{1,0:T(8,128)(2,1)S(1)}, u32[]{:S(2)}, u32[]{:S(2)}) collective-permute-start(bf16[144,1024]{1,0:T(8,128)(2,1)S(1)} %finish_latent.1.refs_0_), channel_id=1, source_target_pairs={{0,4},{1,5},{2,6},{3,7},{4,0},{5,1},{6,2},{7,3},{8,12},{9,13},{10,... | collective-permute-start | bytes 884744 | tf_op jit(solution)/shard_map/ppermute | solution.py:35
  77.5 15.3 %collective-permute-start.17 = (bf16[144,1024]{1,0:T(8,128)(2,1)S(1)}, bf16[144,1024]{1,0:T(8,128)(2,1)S(1)}, u32[]{:S(2)}, u32[]{:S(2)}) collective-permute-start(bf16[144,1024]{1,0:T(8,128)(2,1)S(1)} %finish_latent.1.refs_0_), channel_id=1, source_target_pairs={{0,2},{1,3},{2,0},{3,1},{4,6},{5,7},{6,4},{7,5},{8,10},{9,11},{10,... | collective-permute-start | bytes 884744 | tf_op jit(solution)/shard_map/ppermute | solution.py:35
  92.8 1.6 collective-permute-start.20
  92.8 2.0 collective-permute-start.21
  93.3 13.7 %collective-permute-start.23 = (bf16[144,1024]{1,0:T(8,128)(2,1)S(1)}, bf16[144,1024]{1,0:T(8,128)(2,1)S(1)}, u32[]{:S(2)}, u32[]{:S(2)}) collective-permute-start(bf16[144,1024]{1,0:T(8,128)(2,1)S(1)} %collective-permute-done.18.refs_1_), channel_id=1, source_target_pairs={{0,1},{1,0},{2,3},{3,2},{4,5},{5,4},{6,7},{7,6},{8,9},{9,8},{10,11... | collective-permute-start | bytes 884744 | tf_op jit(solution)/shard_map/ppermute | solution.py:35
  93.3 14.4 %collective-permute-start.22 = (bf16[144,1024]{1,0:T(8,128)(2,1)S(1)}, bf16[144,1024]{1,0:T(8,128)(2,1)}, u32[]{:S(2)}, u32[]{:S(2)}) collective-permute-start(bf16[144,1024]{1,0:T(8,128)(2,1)S(1)} %collective-permute-done.18.refs_1_), channel_id=1, source_target_pairs={{0,2},{1,3},{2,0},{3,1},{4,6},{5,7},{6,4},{7,5},{8,10},{9,11},{10,... | collective-permute-start | bytes 884744 | tf_op jit(solution)/shard_map/ppermute | solution.py:35
  107.7 2.6 %collective-permute-start.25 = (bf16[144,1024]{1,0:T(8,128)(2,1)}, bf16[144,1024]{1,0:T(8,128)(2,1)S(1)}, u32[]{:S(2)}, u32[]{:S(2)}) collective-permute-start(bf16[144,1024]{1,0:T(8,128)(2,1)} %copy-done.12), channel_id=1, source_target_pairs={{0,8},{8,0},{1,9},{9,1},{2,10},{10,2},{3,11},{11,3},{4,12},{12,4},... | collective-permute-start | bytes 884744 | tf_op jit(solution)/shard_map/ppermute | solution.py:27
  107.9 2.4 %collective-permute-start.24 = (bf16[144,1024]{1,0:T(8,128)(2,1)}, bf16[144,1024]{1,0:T(8,128)(2,1)S(1)}, u32[]{:S(2)}, u32[]{:S(2)}) collective-permute-start(bf16[144,1024]{1,0:T(8,128)(2,1)} %collective-permute-done.22.refs_0_), channel_id=1, source_target_pairs={{0,8},{8,0},{1,9},{9,1},{2,10},{10,2},{3,11},{11,3},{4,12},{12,4},... | collective-permute-start | bytes 884744 | tf_op jit(solution)/shard_map/ppermute | solution.py:27
  108.3 13.9 %collective-permute-start.26 = (bf16[144,1024]{1,0:T(8,128)(2,1)S(1)}, bf16[144,1024]{1,0:T(8,128)(2,1)S(1)}, u32[]{:S(2)}, u32[]{:S(2)}) collective-permute-start(bf16[144,1024]{1,0:T(8,128)(2,1)S(1)} %finish_latent.1.refs_0_), channel_id=1, source_target_pairs={{0,1},{1,0},{2,3},{3,2},{4,5},{5,4},{6,7},{7,6},{8,9},{9,8},{10,11... | collective-permute-start | bytes 884744 | tf_op jit(solution)/shard_map/ppermute | solution.py:35
  109.3 14.4 %collective-permute-start.27 = (bf16[144,1024]{1,0:T(8,128)(2,1)}, bf16[144,1024]{1,0:T(8,128)(2,1)S(1)}, u32[]{:S(2)}, u32[]{:S(2)}) collective-permute-start(bf16[144,1024]{1,0:T(8,128)(2,1)} %collective-permute-done.22.refs_0_), channel_id=1, source_target_pairs={{0,1},{1,0},{2,3},{3,2},{4,5},{5,4},{6,7},{7,6},{8,9},{9,8},{10,11... | collective-permute-start | bytes 884744 | tf_op jit(solution)/shard_map/ppermute | solution.py:35
  110.3 16.0 %collective-permute-start.29 = (bf16[256,1024]{1,0:T(8,128)(2,1)}, bf16[256,1024]{1,0:T(8,128)(2,1)S(1)}, u32[]{:S(2)}, u32[]{:S(2)}) collective-permute-start(bf16[256,1024]{1,0:T(8,128)(2,1)} %copy-done.9), channel_id=1, source_target_pairs={{0,8},{8,0},{1,9},{9,1},{2,10},{10,2},{3,11},{11,3},{4,12},{12,4},... | collective-permute-start | bytes 1572872 | tf_op jit(solution)/shard_map/ppermute | solution.py:27
  123.7 2.7 %collective-permute-start.30 = (bf16[256,1024]{1,0:T(8,128)(2,1)S(1)}, bf16[256,1024]{1,0:T(8,128)(2,1)S(1)}, u32[]{:S(2)}, u32[]{:S(2)}) collective-permute-start(bf16[256,1024]{1,0:T(8,128)(2,1)S(1)} %get-tuple-element.114), channel_id=1, source_target_pairs={{0,8},{8,0},{1,9},{9,1},{2,10},{10,2},{3,11},{11,3},{4,12},{12,4},... | collective-permute-start | bytes 1572872 | tf_op jit(solution)/shard_map/ppermute | solution.py:27
  123.7 48.1 %collective-permute-start.37 = (bf16[8,256,512]{2,1,0:T(8,128)(2,1)S(1)}, bf16[8,256,512]{2,1,0:T(8,128)(2,1)}, u32[]{:S(2)}, u32[]{:S(2)}) collective-permute-start(bf16[8,256,512]{2,1,0:T(8,128)(2,1)S(1)} %bitcast.9), channel_id=1, source_target_pairs={{0,16},{16,0},{1,17},{17,1},{2,18},{18,2},{3,19},{19,3},{4,20},{20... | collective-permute-start | bytes 6291464 | tf_op jit(solution)/shard_map/ppermute | solution.py:31
  125.4 9.8 %collective-permute-start.32 = (bf16[144,1024]{1,0:T(8,128)(2,1)S(1)}, bf16[144,1024]{1,0:T(8,128)(2,1)S(1)}, u32[]{:S(2)}, u32[]{:S(2)}) collective-permute-start(bf16[144,1024]{1,0:T(8,128)(2,1)S(1)} %copy-done.11), channel_id=1, source_target_pairs={{0,1},{1,0},{2,3},{3,2},{4,5},{5,4},{6,7},{7,6},{8,9},{9,8},{10,11... | collective-permute-start | bytes 884744 | tf_op jit(solution)/shard_map/ppermute | solution.py:35
  126.3 1.6 collective-permute-start.28
  126.5 13.7 %collective-permute-start.31 = (bf16[128,1024]{1,0:T(8,128)(2,1)S(1)}, bf16[128,1024]{1,0:T(8,128)(2,1)S(1)}, u32[]{:S(2)}, u32[]{:S(2)}) collective-permute-start(bf16[128,1024]{1,0:T(8,128)(2,1)S(1)} %add_convert_fusion.6), channel_id=1, source_target_pairs={{0,1},{1,0},{2,3},{3,2},{4,5},{5,4},{6,7},{7,6},{8,9},{9,8},{10,11... | collective-permute-start | bytes 786440 | tf_op jit(solution)/shard_map/ppermute | solution.py:35
  140.2 1.9 collective-permute-start.35
  140.2 60.0 %collective-permute-start.44 = (bf16[8,256,512]{2,1,0:T(8,128)(2,1)S(1)}, bf16[8,256,512]{2,1,0:T(8,128)(2,1)}, u32[]{:S(2)}, u32[]{:S(2)}) collective-permute-start(bf16[8,256,512]{2,1,0:T(8,128)(2,1)S(1)} %bitcast.10), channel_id=1, source_target_pairs={{0,8},{8,0},{1,9},{9,1},{2,10},{10,2},{3,11},{11,3},{4,12},{12,4},... | collective-permute-start | bytes 6291464 | tf_op jit(solution)/shard_map/ppermute | solution.py:27
  140.7 2.2 %collective-permute-start.33 = (bf16[144,1024]{1,0:T(8,128)(2,1)S(1)}, bf16[144,1024]{1,0:T(8,128)(2,1)S(1)}, u32[]{:S(2)}, u32[]{:S(2)}) collective-permute-start(bf16[144,1024]{1,0:T(8,128)(2,1)S(1)} %collective-permute-done.26.refs_0_), channel_id=1, source_target_pairs={{0,8},{8,0},{1,9},{9,1},{2,10},{10,2},{3,11},{11,3},{4,12},{12,4},... | collective-permute-start | bytes 884744 | tf_op jit(solution)/shard_map/ppermute | solution.py:27
  140.7 4.0 %collective-permute-start.34 = (bf16[144,1024]{1,0:T(8,128)(2,1)S(1)}, bf16[144,1024]{1,0:T(8,128)(2,1)S(1)}, u32[]{:S(2)}, u32[]{:S(2)}) collective-permute-start(bf16[144,1024]{1,0:T(8,128)(2,1)S(1)} %collective-permute-done.32.refs_1_), channel_id=1, source_target_pairs={{0,8},{8,0},{1,9},{9,1},{2,10},{10,2},{3,11},{11,3},{4,12},{12,4},... | collective-permute-start | bytes 884744 | tf_op jit(solution)/shard_map/ppermute | solution.py:27
  142.1 12.8 %collective-permute-start.38 = (bf16[128,1024]{1,0:T(8,128)(2,1)S(1)}, bf16[128,1024]{1,0:T(8,128)(2,1)S(1)}, u32[]{:S(2)}, u32[]{:S(2)}) collective-permute-start(bf16[128,1024]{1,0:T(8,128)(2,1)S(1)} %add_convert_fusion.7), channel_id=1, source_target_pairs={{0,2},{1,3},{2,0},{3,1},{4,6},{5,7},{6,4},{7,5},{8,10},{9,11},{10,... | collective-permute-start | bytes 786440 | tf_op jit(solution)/shard_map/ppermute | solution.py:35
  142.9 12.0 %collective-permute-start.36 = (bf16[128,1024]{1,0:T(8,128)(2,1)S(1)}, bf16[128,1024]{1,0:T(8,128)(2,1)S(1)}, u32[]{:S(2)}, u32[]{:S(2)}) collective-permute-start(bf16[128,1024]{1,0:T(8,128)(2,1)S(1)} %add_convert_fusion.5), channel_id=1, source_target_pairs={{0,1},{1,0},{2,3},{3,2},{4,5},{5,4},{6,7},{7,6},{8,9},{9,8},{10,11... | collective-permute-start | bytes 786440 | tf_op jit(solution)/shard_map/ppermute | solution.py:35
  171.8 33.6 %collective-permute-start.45 = (bf16[8,256,512]{2,1,0:T(8,128)(2,1)}, bf16[8,256,512]{2,1,0:T(8,128)(2,1)}, u32[]{:S(2)}, u32[]{:S(2)}) collective-permute-start(bf16[8,256,512]{2,1,0:T(8,128)(2,1)} %collective-permute-done.37.refs_6_), channel_id=1, source_target_pairs={{0,8},{8,0},{1,9},{9,1},{2,10},{10,2},{3,11},{11,3},{4,12},{12,4},... | collective-permute-start | bytes 6291464 | tf_op jit(solution)/shard_map/ppermute | solution.py:27
  171.8 4.9 %collective-permute-start.39 = (bf16[256,1024]{1,0:T(8,128)(2,1)S(1)}, bf16[256,1024]{1,0:T(8,128)(2,1)S(1)}, u32[]{:S(2)}, u32[]{:S(2)}) collective-permute-start(bf16[256,1024]{1,0:T(8,128)(2,1)S(1)} %get-tuple-element.133), channel_id=1, source_target_pairs={{0,8},{8,0},{1,9},{9,1},{2,10},{10,2},{3,11},{11,3},{4,12},{12,4},... | collective-permute-start | bytes 1572872 | tf_op jit(solution)/shard_map/ppermute | solution.py:27
  172.3 7.6 %collective-permute-start.19 = (bf16[128,1024]{1,0:T(8,128)(2,1)}, bf16[128,1024]{1,0:T(8,128)(2,1)}, u32[]{:S(2)}, u32[]{:S(2)}) collective-permute-start(bf16[128,1024]{1,0:T(8,128)(2,1)} %get-tuple-element.90), channel_id=1, source_target_pairs={{0,8},{8,0},{1,9},{9,1},{2,10},{10,2},{3,11},{11,3},{4,12},{12,4},... | collective-permute-start | bytes 786440 | tf_op jit(solution)/shard_map/ppermute | solution.py:27
  177.7 8.9 %collective-permute-start.40 = (bf16[128,1024]{1,0:T(8,128)(2,1)}, bf16[128,1024]{1,0:T(8,128)(2,1)}, u32[]{:S(2)}, u32[]{:S(2)}) collective-permute-start(bf16[128,1024]{1,0:T(8,128)(2,1)} %get-tuple-element.142), channel_id=1, source_target_pairs={{0,1},{1,0},{2,3},{3,2},{4,5},{5,4},{6,7},{7,6},{8,9},{9,8},{10,11... | collective-permute-start | bytes 786440 | tf_op jit(solution)/shard_map/ppermute | solution.py:35
  178.7 21.6 %collective-permute-start.42 = (bf16[128,1024]{1,0:T(8,128)(2,1)}, bf16[128,1024]{1,0:T(8,128)(2,1)S(1)}, u32[]{:S(2)}, u32[]{:S(2)}) collective-permute-start(bf16[128,1024]{1,0:T(8,128)(2,1)} %add_convert_fusion.4), channel_id=1, source_target_pairs={{0,4},{1,5},{2,6},{3,7},{4,0},{5,1},{6,2},{7,3},{8,12},{9,13},{10,... | collective-permute-start | bytes 786440 | tf_op jit(solution)/shard_map/ppermute | solution.py:35
  179.9 20.3 %collective-permute-start.43 = (bf16[128,1024]{1,0:T(8,128)(2,1)S(1)}, bf16[128,1024]{1,0:T(8,128)(2,1)S(1)}, u32[]{:S(2)}, u32[]{:S(2)}) collective-permute-start(bf16[128,1024]{1,0:T(8,128)(2,1)S(1)} %add_convert_fusion), channel_id=1, source_target_pairs={{0,6},{1,7},{2,4},{3,5},{4,2},{5,3},{6,0},{7,1},{8,14},{9,15},{10,... | collective-permute-start | bytes 786440 | tf_op jit(solution)/shard_map/ppermute | solution.py:35
  186.6 18.8 %collective-permute-start.41 = (bf16[128,1024]{1,0:T(8,128)(2,1)}, bf16[128,1024]{1,0:T(8,128)(2,1)S(1)}, u32[]{:S(2)}, u32[]{:S(2)}) collective-permute-start(bf16[128,1024]{1,0:T(8,128)(2,1)} %get-tuple-element.141), channel_id=1, source_target_pairs={{0,3},{1,2},{2,1},{3,0},{4,7},{5,6},{6,5},{7,4},{8,11},{9,10},{10,... | collective-permute-start | bytes 786440 | tf_op jit(solution)/shard_map/ppermute | solution.py:35
  (17 other events, 163.6 us)
Sparse Core Ops, SparseCore 0:
  9.5 65.0 all-gather.2

commit v6 on v5

--- a/solution.py
+++ b/solution.py
@@ -153,13 +153,17 @@
     )(own_part, arrived, weights)
 
 
-def expert_kernel(positions, count, where, *refs):
+def expert_kernel(positions, count, stream, where, *refs):
     pieces = refs[: 2 * positions]
     gate, up, out = refs[2 * positions : 2 * positions + 3]
     own_sums = refs[2 * positions + 3 : 3 * positions + 3]
-    other_sums, rows, hidden, held, gate_block, up_block, out_block, sems = refs[-8:]
+    other_sums, rows, hidden, held = refs[3 * positions + 3 : 3 * positions + 7]
     width = 256
     blocks = gate.shape[2] // width
+    if stream:
+        gate_block, up_block, out_block, sems = refs[-4:]
+    else:
+        gate_block, up_block, out_block = gate.at[0], up.at[0], out.at[0]
 
     def columns_at(start):
         return pl.ds(pl.multiple_of(start, width), width)
@@ -171,10 +175,10 @@
             source.at[0, :, columns], target.at[:, columns], sems.at[part * blocks + i]
         )
 
-    for i in range(blocks):
+    for i in range(blocks if stream else 0):
         read(i, 0).start()
         read(i, 1).start()
-    for i in range(out.shape[2] // width):
+    for i in range(out.shape[2] // width if stream else 0):
         read(i, 2).start()
     for i, piece in enumerate(pieces):
         rows[i * count : (i + 1) * count] = piece[:count]
@@ -190,8 +194,9 @@
     scales = [scale_of(piece) for piece in pieces]
 
     def arrive(i):
-        read(i, 0).wait()
-        read(i, 1).wait()
+        if stream:
+            read(i, 0).wait()
+            read(i, 1).wait()
 
     def products(i):
         columns = columns_at(i * width)
@@ -225,7 +230,8 @@
 
     def finish(i, carry):
         columns = columns_at(i * width)
-        read(i, 2).wait()
+        if stream:
+            read(i, 2).wait()
         value = jnp.dot(hidden[...], out_block[:, columns], preferred_element_type=jnp.float32)
         for j, scale in enumerate(scales):
             scaled = (value[j * count : (j + 1) * count] * scale).astype(jnp.bfloat16)
@@ -238,35 +244,38 @@
     lax.fori_loop(0, out.shape[2] // width, finish, 0)
 
 
-def expert_apply(expert, owns, others, gate_weight, up_weight, out_weight, count):
+def expert_apply(expert, owns, others, weights, count, stream):
     positions = len(owns)
     latent_width = owns[0].shape[1]
-    hidden_width = gate_weight.shape[2]
+    hidden_width = weights[0].shape[2]
     rows = 2 * positions * count
     own_sum = jax.ShapeDtypeStruct((count, latent_width), jnp.bfloat16)
     other_sums = jax.ShapeDtypeStruct((positions * count, latent_width), jnp.bfloat16)
+    scratch = [
+        pltpu.VMEM((rows, latent_width), jnp.bfloat16),
+        pltpu.VMEM((rows, hidden_width), jnp.bfloat16),
+        pltpu.VMEM((2, rows, 256), jnp.float32),
+    ]
+    if stream:
+        weights = [pltpu.with_memory_space_constraint(w, pltpu.HBM) for w in weights]
+        scratch += [pltpu.VMEM(w.shape[1:], w.dtype) for w in weights]
+        scratch += [pltpu.SemaphoreType.DMA(((2 * hidden_width + latent_width) // 256,))]
     return pl.pallas_call(
-        functools.partial(expert_kernel, positions, count),
+        functools.partial(expert_kernel, positions, count, stream),
         out_shape=(own_sum,) * positions + (other_sums,),
-        in_specs=[in_smem] + [in_vmem] * (2 * positions) + [in_hbm] * 3,
+        in_specs=[in_smem]
+        + [in_vmem] * (2 * positions)
+        + [in_hbm if stream else in_vmem] * 3,
         out_specs=(in_vmem,) * (positions + 1),
-        scratch_shapes=[
-            pltpu.VMEM((rows, latent_width), jnp.bfloat16),
-            pltpu.VMEM((rows, hidden_width), jnp.bfloat16),
-            pltpu.VMEM((2, rows, 256), jnp.float32),
-            pltpu.VMEM((latent_width, hidden_width), jnp.bfloat16),
-            pltpu.VMEM((latent_width, hidden_width), jnp.bfloat16),
-            pltpu.VMEM((hidden_width, latent_width), jnp.bfloat16),
-            pltpu.SemaphoreType.DMA(((2 * hidden_width + latent_width) // 256,)),
-        ],
-        compiler_params=pltpu.CompilerParams(vmem_limit_bytes=32 * mebi),
+        scratch_shapes=scratch,
+        compiler_params=pltpu.CompilerParams(vmem_limit_bytes=(24 if stream else 14) * mebi),
         cost_estimate=pl.CostEstimate(
             flops=6 * rows * latent_width * hidden_width,
             bytes_accessed=4 * rows * latent_width,
             transcendentals=rows * hidden_width,
         ),
         name="expert",
-    )(expert, *owns, *others, gate_weight, up_weight, out_weight)
+    )(expert, *owns, *others, *weights)
 
 
 def project_kernel(where, *refs):
@@ -361,14 +370,14 @@
     far[1] = swap_ep(near[1], 1)
     weights = dense_weights(after(expert_ids, near[1]), route_scores, expert_count)
     others = {k: near[k] for k in near if k > 1}
-    *arrived, weights = join(*others.values(), weights)
+    far[1], weights, *arrived = join(far[1], weights, *others.values())
     near.update(zip(others, arrived))
     for k in range(2, steps):
         if k & (k - 1):
             low = k & -k
             near[k] = swap_ep(near[k ^ low], 2 * low)
         if k == last:
-            near[k], far[1], taken = join(near[k], far[1], taken)
+            near[k], far[0], taken = join(near[k], far[0], taken)
         far[k] = swap_ep(near[k], 1)
     blocks = []
     for k in range(steps):
@@ -378,11 +387,12 @@
     (partial,) = down_project(early, kept, taken, [b for k in early for b in blocks[k]])
     late = [after(blocks[-1][0], partial), *blocks[-1][1:]]
     own_part, sent_part = down_project([last], kept, taken, late, partial)
-    latent = finish_latent(own_part, swap_reps(sent_part), weights.astype(jnp.bfloat16))
-
-    gate_weight, up_weight, out_weight = [
-        pltpu.with_memory_space_constraint(w, pltpu.HBM) for w in (gate_weight, up_weight, out_weight)
-    ]
+    arrived, mine = join(swap_reps(sent_part), mine)
+    latent = finish_latent(own_part, arrived, weights.astype(jnp.bfloat16))
+
+    sides = [[i, i + 1] for i in range(0, lax.axis_size("rep"), 2)]
+    both_sides = lax.all_gather(mine, "rep", axis=0, axis_index_groups=sides)
+
     expert = (group * ep_count + place).astype(jnp.int32).reshape(1)
     near = first_steps(latent, steps)
     far, away, sent, pairs, own_sums, swapped = {}, {}, {}, {}, {}, {}
@@ -396,10 +406,9 @@
             expert,
             operands[:count],
             operands[count:],
-            gate_weight,
-            up_weight,
-            out_weight,
+            (gate_weight, up_weight, out_weight),
             token_count,
+            len(own_sums) <= 1,
         )
         names = [(table, key) for table, keys in coming for key in keys]
         sums = join(*sums, *[table[key] for table, key in names])
@@ -427,15 +436,12 @@
     def start_far(k):
         far[k] = swap_ep(near[k], 1)
 
-    gathered = {"mine": mine}
     powers = [k for k in near if k]
     run([(0, 0)], [(near, powers)])
     if last >= 3:
         start_near(3)
     start_far(2)
-    run([(1, 0), (2, 0)], [(near, [3]), (far, [2]), (gathered, ["mine"])])
-    mine = gathered["mine"]
-    gathered["across"] = swap_reps(mine)
+    run([(1, 0), (2, 0)], [(near, [3] if last >= 3 else []), (far, [2])])
     returning = []
     for k in range(3, steps):
         start_far(k)
@@ -459,11 +465,10 @@
     homeward = {"near": swap_ep(near_home, 2)}
     run(
         [(0, 1), (1, 1)],
-        [(away, [last]), (gathered, ["across"]), (homeward, ["near"])],
+        [(away, [last]), (homeward, ["near"])],
         sent[last],
         *pairs.values(),
     )
-    across = gathered["across"]
     pair_sum(last)
     send_far(0)
     far_home = chip_sum(1, 1).astype(jnp.bfloat16)
@@ -471,6 +476,8 @@
     terms = [pairs[0], homeward["near"], swap_ep(far_home, 3)]
     terms += [swap_ep(pairs[k], 2 * k) for k in range(2, steps)]
 
+    both_sides = after(both_sides, pairs[0])
+    across = lax.dynamic_index_in_dim(both_sides, 1 - side, 0, keepdims=False)
     where = [own_quarter ^ 1, own_quarter ^ 3, own_quarter, own_quarter ^ 2]
     where = jnp.stack(where).astype(jnp.int32)
     return project(where, terms, mine, across, swap_cores(mine), swap_cores(across))

time: 219 us -> 203 us (0.927)
  waiting for transfers between devices: 98.7 us -> 81.3 us
  local copies, waits for them, and re-layouts: 6.85 us -> 17.4 us
  starting transfers between devices: 40.6 us -> 34.3 us
  Pallas kernels: 53.9 us -> 49 us
    ppermute x3 -> x2, waiting for transfers between devices: 23.6 us -> 6.86 us  [swap_reps(): lax.ppermute(array, 'rep', [(i, i ^ 1) for i in range(lax.axis_size('rep'...]
    all_gather x1, waiting for transfers between devices: 0.01 us -> 7.79 us  [body(): mine = lax.all_gather(up_piece, 'ep', axis=0)]
    unnamed x36 -> x32, local copies, waits for them, and re-layouts: 5.08 us -> 12.4 us
    ppermute x21, waiting for transfers between devices: 68.9 us -> 63.8 us  [swap_ep(): lax.ppermute(array, 'ep', [(i, i ^ mask) for i in range(lax.axis_size('ep...]
    ppermute x21, starting transfers between devices: 32.2 us -> 27.1 us  [swap_ep(): lax.ppermute(array, 'ep', [(i, i ^ mask) for i in range(lax.axis_size('ep...]
    pallas_call x5, Pallas kernels: 45.4 us -> 40.3 us  [expert_apply(): pl.pallas_call(functools.partial(expert_kernel, positions, count, stream)...]
    ppermute x22, waiting for transfers between devices: 6.24 us -> 2.85 us  [swap_cores(): return lax.ppermute(array, 'grp', [(0, 1), (1, 0)])]
    squeeze x0 -> x1, local copies, waits for them, and re-layouts: none -> 3.18 us  [body(): across = lax.dynamic_index_in_dim(both_sides, 1 - side, 0, keepdims=False)]
  transfers between devices with their start and end apart: 47 -> 47, of which waited for: 21 -> 17; matrix products, arithmetic and copies ran while one was open for 3% -> 5% of each run, Pallas kernels for 22% -> 21%
where the time goes in v6:
time: 203 us; the launch traced here: 202 us
  waiting for transfers between devices  81.3 us (40%)
  Pallas kernels  49 us (24%)
  starting transfers between devices  34.3 us (17%)
  local copies, waits for them, and re-layouts  17.4 us (9%)
  between operations  13.7 us (7%)
  other arithmetic  6.37 us (3%)
    ppermute x21, waiting for transfers between devices, swap_ep(): lax.ppermute(array, 'ep', [(i, i ^ mask) for i in range(lax.axis_size('ep...  63.8 us
    pallas_call x5, Pallas kernels, expert_apply(): pl.pallas_call(functools.partial(expert_kernel, positions, count, stream)...  40.3 us
    ppermute x21, starting transfers between devices, swap_ep(): lax.ppermute(array, 'ep', [(i, i ^ mask) for i in range(lax.axis_size('ep...  27.1 us
    unnamed x32, local copies, waits for them, and re-layouts  12.4 us
    all_gather x1, waiting for transfers between devices, body(): mine = lax.all_gather(up_piece, 'ep', axis=0)  7.79 us
    ppermute x2, waiting for transfers between devices, swap_reps(): lax.ppermute(array, 'rep', [(i, i ^ 1) for i in range(lax.axis_size('rep'...  6.86 us
    pallas_call x1, Pallas kernels, project(): pl.pallas_call(project_kernel, in_specs=[in_smem] + [in_vmem] * len(terms...  6.44 us
  transfers between devices with their start and end apart: 47, of which 17 were waited for; matrix products, arithmetic and copies ran while one was open for 5% of the time, Pallas kernels for 21%

profile of v6, /device:TPU:0, one launch (start us, length us, event | category | flops | bytes accessed | tf_op | source)
XLA Modules:
  0.0 202.2 jit_solution(14549513484081252862)
XLA Ops:
  6.5 1.2 copy-done
  8.6 1.1 constant_dynamic-slice_fusion.1
  9.6 3.1 %collective-permute-start = (bf16[128,1024]{1,0:T(8,128)(2,1)S(1)}, bf16[128,1024]{1,0:T(8,128)(2,1)S(1)}, u32[]{:S(2)}, u32[]{:S(2)}) collective-permute-start(bf16[128,1024]{1,0:T(8,128)(2,1)S(1)} %get-tuple-element.144.refs_2_), channel_id=1, source_target_pairs={{0,2},{1,3},{2,0},{3,1},{4,6},{5,7},{6,4},{7,5},{8,10},{9,11},{10,... | collective-permute-start | bytes 786440 | tf_op jit(solution)/shard_map/ppermute | solution.py:35
  12.7 2.6 %collective-permute-start.2 = (bf16[128,1024]{1,0:T(8,128)(2,1)S(1)}, bf16[128,1024]{1,0:T(8,128)(2,1)S(1)}, u32[]{:S(2)}, u32[]{:S(2)}) collective-permute-start(bf16[128,1024]{1,0:T(8,128)(2,1)S(1)} %get-tuple-element.144.refs_2_), channel_id=1, source_target_pairs={{0,4},{1,5},{2,6},{3,7},{4,0},{5,1},{6,2},{7,3},{8,12},{9,13},{10,... | collective-permute-start | bytes 786440 | tf_op jit(solution)/shard_map/ppermute | solution.py:35
  15.3 1.5 collective-permute-start.4
  16.9 1.2 copy-done.6
  19.0 1.6 collective-permute-start.5
  21.2 4.8 %collective-permute-done.refs_6_ = bf16[128,1024]{1,0:T(8,128)(2,1)S(1)} collective-permute-done((bf16[128,1024]{1,0:T(8,128)(2,1)S(1)}, bf16[128,1024]{1,0:T(8,128)(2,1)S(1)}, u32[]{:S(2)}, u32[]{:S(2)}) %collective-permute-start) | collective-permute-done | bytes 262176 | tf_op jit(solution)/shard_map/ppermute | solution.py:35
  26.1 1.8 collective-permute-start.1
  29.4 3.3 %collective-permute-done.1.refs_7_ = bf16[128,1024]{1,0:T(8,128)(2,1)S(1)} collective-permute-done((bf16[128,1024]{1,0:T(8,128)(2,1)S(1)}, bf16[128,1024]{1,0:T(8,128)(2,1)S(1)}, u32[]{:S(2)}, u32[]{:S(2)}) %collective-permute-start.1) | collective-permute-done | bytes 262176 | tf_op jit(solution)/shard_map/ppermute | solution.py:35
  32.8 1.5 collective-permute-start.9
  34.5 6.2 %collective-permute-done.3.refs_2_ = bf16[128,1024]{1,0:T(8,128)(2,1)S(1)} collective-permute-done((bf16[128,1024]{1,0:T(8,128)(2,1)S(1)}, bf16[128,1024]{1,0:T(8,128)(2,1)S(1)}, u32[]{:S(2)}, u32[]{:S(2)}) %collective-permute-start.3) | collective-permute-done | bytes 262176 | tf_op jit(solution)/shard_map/ppermute | solution.py:35
  40.8 1.5 collective-permute-start.12
  43.3 8.6 %collective-permute-done.12.refs_3_ = bf16[128,1024]{1,0:T(8,128)(2,1)S(1)} collective-permute-done((bf16[128,1024]{1,0:T(8,128)(2,1)S(1)}, bf16[128,1024]{1,0:T(8,128)(2,1)S(1)}, u32[]{:S(2)}, u32[]{:S(2)}) %collective-permute-start.12) | collective-permute-done | bytes 262176 | tf_op jit(solution)/shard_map/ppermute | solution.py:35
  52.0 1.0 down_project.2.refs_6_
  53.9 1.6 collective-permute-start.15
  55.5 6.9 %collective-permute-done.15.arrived = bf16[128,1024]{1,0:T(8,128)(2,1)S(1)} collective-permute-done((bf16[128,1024]{1,0:T(8,128)(2,1)S(1)}, bf16[128,1024]{1,0:T(8,128)(2,1)S(1)}, u32[]{:S(2)}, u32[]{:S(2)}) %collective-permute-start.15) | collective-permute-done | bytes 262176 | tf_op jit(solution)/shard_map/ppermute | solution.py:31
  62.3 7.8 %all-gather.5.cloned.1.call-done = bf16[2048,512]{1,0:T(8,128)(2,1)} async-done(((bf16[256,512]{1,0:T(8,128)(2,1)}), bf16[2048,512]{1,0:T(8,128)(2,1)}) %all-gather.5.cloned.1.call-update) | async-done | bytes 2097168 | tf_op jit(solution)/shard_map/all_gather | solution.py:358
  70.4 1.8 collective-permute-start.18
  72.2 6.8 %expert.5 = (bf16[128,1024]{1,0:T(8,128)(2,1)S(1)}, bf16[128,1024]{1,0:T(8,128)(2,1)S(1)}) custom-call(s32[1]{0:T(128)} %bitcast.4.where, bf16[144,1024]{1,0:T(8,128)(2,1)S(1)} %finish_latent.1.refs_0_, bf16[144,1024]{1,0:T(8,128)(2,1)S(1)} %collective-permute-done.16.refs_1_, bf16[1,1024,2048]{2,1,0:T(8,128)(2,1)} %refs_4_.9, ...), custom_call_target="tpu_custom_call" | custom-call | flops 3221225472 | bytes 1048576 | tf_op jit(solution)/shard_map/expert/pallas_call | solution.py:263
  79.7 5.3 %collective-permute-done.17.refs_0_ = bf16[144,1024]{1,0:T(8,128)(2,1)S(1)} collective-permute-done((bf16[144,1024]{1,0:T(8,128)(2,1)S(1)}, bf16[144,1024]{1,0:T(8,128)(2,1)S(1)}, u32[]{:S(2)}, u32[]{:S(2)}) %collective-permute-start.17) | collective-permute-done | bytes 294944 | tf_op jit(solution)/shard_map/ppermute | solution.py:35
  85.0 2.0 collective-permute-done.18.refs_1_
  87.4 1.1 collective-permute-start.23
  88.9 10.0 %expert.6 = (bf16[128,1024]{1,0:T(8,128)(2,1)S(1)}, bf16[128,1024]{1,0:T(8,128)(2,1)S(1)}, bf16[256,1024]{1,0:T(8,128)(2,1)S(1)}) custom-call(s32[1]{0:T(128)} %bitcast.4.where, bf16[144,1024]{1,0:T(8,128)(2,1)S(1)} %collective-permute-done.17.refs_0_, bf16[144,1024]{1,0:T(8,128)(2,1)S(1)} %collective-permute-done.18.refs_1_, ...), custom_call_target="tpu_custom_call" | custom-call | flops 6442450944 | bytes 2097152 | tf_op jit(solution)/shard_map/expert/pallas_call | solution.py:263
  99.5 1.2 collective-permute-start.26
  101.6 2.2 %copy-done.1 = bf16[1,1024,2048]{2,1,0:T(8,128)(2,1)S(1)} copy-done((bf16[1,1024,2048]{2,1,0:T(8,128)(2,1)S(1)}, bf16[1,1024,2048]{2,1,0:T(8,128)(2,1)}, u32[]{:S(2)}) %copy-start.1) | copy-done | bytes 4194328
  103.8 2.7 %copy-done.3 = bf16[1,1024,2048]{2,1,0:T(8,128)(2,1)S(1)} copy-done((bf16[1,1024,2048]{2,1,0:T(8,128)(2,1)S(1)}, bf16[1,1024,2048]{2,1,0:T(8,128)(2,1)}, u32[]{:S(2)}) %copy-start.3) | copy-done | bytes 4194328
  106.5 2.7 %copy-done.4 = bf16[1,2048,1024]{2,1,0:T(8,128)(2,1)S(1)} copy-done((bf16[1,2048,1024]{2,1,0:T(8,128)(2,1)S(1)}, bf16[1,2048,1024]{2,1,0:T(8,128)(2,1)}, u32[]{:S(2)}) %copy-start.4) | copy-done | bytes 4194328
  109.3 9.6 %expert.7 = (bf16[128,1024]{1,0:T(8,128)(2,1)S(1)}, bf16[128,1024]{1,0:T(8,128)(2,1)S(1)}, bf16[256,1024]{1,0:T(8,128)(2,1)S(1)}) custom-call(s32[1]{0:T(128)} %bitcast.4.where, bf16[144,1024]{1,0:T(8,128)(2,1)S(1)} %collective-permute-done.22.refs_0_, bf16[144,1024]{1,0:T(8,128)(2,1)S(1)} %collective-permute-done.23.refs_1_, ...), custom_call_target="tpu_custom_call" | custom-call | flops 6442450944 | bytes 2097152 | tf_op jit(solution)/shard_map/expert/pallas_call | solution.py:263
  119.5 1.0 collective-permute-start.32
  121.1 1.0 collective-permute-start.31
  122.2 5.2 %expert.8 = (bf16[128,1024]{1,0:T(8,128)(2,1)S(1)}, bf16[128,1024]{1,0:T(8,128)(2,1)S(1)}) custom-call(s32[1]{0:T(128)} %bitcast.4.where, bf16[144,1024]{1,0:T(8,128)(2,1)S(1)} %collective-permute-done.27.refs_0_, bf16[144,1024]{1,0:T(8,128)(2,1)S(1)} %collective-permute-done.28.refs_1_, bf16[1,1024,2048]{2,1,0:T(8,128)(2,1)S(1)} %copy-done.1, ...), custom_call_target="tpu_custom_call" | custom-call | flops 3221225472 | bytes 1048576 | tf_op jit(solution)/shard_map/expert/pallas_call | solution.py:263
  127.4 2.0 collective-permute-done.32.refs_1_
  129.4 4.7 %collective-permute-done.31 = bf16[128,1024]{1,0:T(8,128)(2,1)S(1)} collective-permute-done((bf16[128,1024]{1,0:T(8,128)(2,1)S(1)}, bf16[128,1024]{1,0:T(8,128)(2,1)S(1)}, u32[]{:S(2)}, u32[]{:S(2)}) %collective-permute-start.31) | collective-permute-done | bytes 262176 | tf_op jit(solution)/shard_map/ppermute | solution.py:35
  134.6 1.6 collective-permute-start.37
  138.0 8.7 %expert.9 = (bf16[128,1024]{1,0:T(8,128)(2,1)S(1)}, bf16[128,1024]{1,0:T(8,128)(2,1)S(1)}, bf16[256,1024]{1,0:T(8,128)(2,1)S(1)}) custom-call(s32[1]{0:T(128)} %bitcast.4.where, bf16[144,1024]{1,0:T(8,128)(2,1)S(1)} %collective-permute-done.26.refs_0_, bf16[144,1024]{1,0:T(8,128)(2,1)S(1)} %collective-permute-done.32.refs_1_, ...), custom_call_target="tpu_custom_call" | custom-call | flops 6442450944 | bytes 2097152 | tf_op jit(solution)/shard_map/expert/pallas_call | solution.py:263
  148.0 1.4 collective-permute-done.38
  149.4 1.0 add_convert_fusion.1
  150.4 1.2 collective-permute-start.39
  151.7 7.5 %collective-permute-done.39 = bf16[128,1024]{1,0:T(8,128)(2,1)} collective-permute-done((bf16[128,1024]{1,0:T(8,128)(2,1)}, bf16[128,1024]{1,0:T(8,128)(2,1)}, u32[]{:S(2)}, u32[]{:S(2)}) %collective-permute-start.39) | collective-permute-done | bytes 262176 | tf_op jit(solution)/shard_map/ppermute | solution.py:35
  159.2 1.2 add_convert_fusion.2.refs_0_
  160.5 3.2 %dynamic-slice_bitcast_fusion.refs_6_ = bf16[8,256,512]{2,1,0:T(8,128)(2,1)} fusion(bf16[2,8,256,512]{3,2,1,0:T(8,128)(2,1)} %bitcast.15, s32[]{:T(128)S(6)} %select_n.29), kind=kLoop, calls=%fused_computation | loop fusion | bytes 4194308 | tf_op jit(solution)/shard_map/jit(dynamic_index_in_dim)/squeeze | solution.py:480
  164.8 2.6 %collective-permute-start.42 = (bf16[128,1024]{1,0:T(8,128)(2,1)}, bf16[128,1024]{1,0:T(8,128)(2,1)}, u32[]{:S(2)}, u32[]{:S(2)}) collective-permute-start(bf16[128,1024]{1,0:T(8,128)(2,1)} %add_convert_fusion), channel_id=1, source_target_pairs={{0,6},{1,7},{2,4},{3,5},{4,2},{5,3},{6,0},{7,1},{8,14},{9,15},{10,... | collective-permute-start | bytes 786440 | tf_op jit(solution)/shard_map/ppermute | solution.py:35
  167.4 1.2 collective-permute-start.40
  168.7 16.3 %collective-permute-done.41.refs_3_ = bf16[128,1024]{1,0:T(8,128)(2,1)} collective-permute-done((bf16[128,1024]{1,0:T(8,128)(2,1)}, bf16[128,1024]{1,0:T(8,128)(2,1)}, u32[]{:S(2)}, u32[]{:S(2)}) %collective-permute-start.41) | collective-permute-done | bytes 262176 | tf_op jit(solution)/shard_map/ppermute | solution.py:35
  185.0 3.0 %collective-permute-done.40.refs_2_ = bf16[128,1024]{1,0:T(8,128)(2,1)} collective-permute-done((bf16[128,1024]{1,0:T(8,128)(2,1)}, bf16[128,1024]{1,0:T(8,128)(2,1)}, u32[]{:S(2)}, u32[]{:S(2)}) %collective-permute-start.40) | collective-permute-done | bytes 262176 | tf_op jit(solution)/shard_map/ppermute | solution.py:35
  187.9 0.9 copy-done.8
  188.9 6.4 %project.1 = bf16[128,4096]{1,0:T(8,128)(2,1)} custom-call(s32[4]{0:T(128)S(1)} %pad_add_fusion.where, bf16[128,1024]{1,0:T(8,128)(2,1)S(1)} %add_convert_fusion.2.refs_0_, bf16[128,1024]{1,0:T(8,128)(2,1)S(1)} %copy-done.8, bf16[128,1024]{1,0:T(8,128)(2,1)} %collective-permute-done.40.refs_2_, bf16[128,1024]{1,0:T(8,128)(2,1)} %collective-permute-done.41.refs_3_, ...), custom_call_target="tpu_custom_call" | custom-call | flops 1073741824 | bytes 8388608 | tf_op jit(solution)/shard_map/project/pallas_call | solution.py:319
  (105 shorter events, 15.4 us)
Async XLA Ops:
  6.5 63.6 %all-gather.5.cloned.1.call-start = ((), (), s32[]{:S(2)}) async-start(), calls=%async_computation | async-start | bytes 2359296 | tf_op jit(solution)/shard_map/all_gather | solution.py:358
  8.5 151.9 %all-gather.7.cloned.1.call-start = ((), (), s32[]{:S(2)}) async-start(), calls=%async_computation.1 | async-start | bytes 6291456 | tf_op jit(solution)/shard_map/all_gather | solution.py:394
  9.6 16.4 %collective-permute-start = (bf16[128,1024]{1,0:T(8,128)(2,1)S(1)}, bf16[128,1024]{1,0:T(8,128)(2,1)S(1)}, u32[]{:S(2)}, u32[]{:S(2)}) collective-permute-start(bf16[128,1024]{1,0:T(8,128)(2,1)S(1)} %get-tuple-element.144.refs_2_), channel_id=1, source_target_pairs={{0,2},{1,3},{2,0},{3,1},{4,6},{5,7},{6,4},{7,5},{8,10},{9,11},{10,... | collective-permute-start | bytes 786440 | tf_op jit(solution)/shard_map/ppermute | solution.py:35
  12.7 16.6 %collective-permute-start.2 = (bf16[128,1024]{1,0:T(8,128)(2,1)S(1)}, bf16[128,1024]{1,0:T(8,128)(2,1)S(1)}, u32[]{:S(2)}, u32[]{:S(2)}) collective-permute-start(bf16[128,1024]{1,0:T(8,128)(2,1)S(1)} %get-tuple-element.144.refs_2_), channel_id=1, source_target_pairs={{0,4},{1,5},{2,6},{3,7},{4,0},{5,1},{6,2},{7,3},{8,12},{9,13},{10,... | collective-permute-start | bytes 786440 | tf_op jit(solution)/shard_map/ppermute | solution.py:35
  15.3 19.0 %collective-permute-start.4 = (bf16[128,1024]{1,0:T(8,128)(2,1)S(1)}, bf16[128,1024]{1,0:T(8,128)(2,1)S(1)}, u32[]{:S(2)}, u32[]{:S(2)}) collective-permute-start(bf16[128,1024]{1,0:T(8,128)(2,1)S(1)} %get-tuple-element.144.refs_2_), channel_id=1, source_target_pairs={{0,1},{1,0},{2,3},{3,2},{4,5},{5,4},{6,7},{7,6},{8,9},{9,8},{10,11... | collective-permute-start | bytes 786440 | tf_op jit(solution)/shard_map/ppermute | solution.py:35
  19.0 15.6 %collective-permute-start.5 = (bf16[128,2048]{1,0:T(8,128)(2,1)S(1)}, bf16[128,2048]{1,0:T(8,128)(2,1)S(1)}, u32[]{:S(2)}, u32[]{:S(2)}) collective-permute-start(bf16[128,2048]{1,0:T(8,128)(2,1)S(1)} %get-tuple-element.79), channel_id=1, source_target_pairs={{0,16},{16,0},{1,17},{17,1},{2,18},{18,2},{3,19},{19,3},{4,20},{20... | collective-permute-start | bytes 1572872 | tf_op jit(solution)/shard_map/ppermute | solution.py:31
  26.1 6.6 %collective-permute-start.1 = (bf16[128,1024]{1,0:T(8,128)(2,1)S(1)}, bf16[128,1024]{1,0:T(8,128)(2,1)S(1)}, u32[]{:S(2)}, u32[]{:S(2)}) collective-permute-start(bf16[128,1024]{1,0:T(8,128)(2,1)S(1)} %collective-permute-done.refs_6_), channel_id=1, source_target_pairs={{0,1},{1,0},{2,3},{3,2},{4,5},{5,4},{6,7},{7,6},{8,9},{9,8},{10,11... | collective-permute-start | bytes 786440 | tf_op jit(solution)/shard_map/ppermute | solution.py:35
  32.7 8.1 %collective-permute-start.3 = (bf16[128,1024]{1,0:T(8,128)(2,1)S(1)}, bf16[128,1024]{1,0:T(8,128)(2,1)S(1)}, u32[]{:S(2)}, u32[]{:S(2)}) collective-permute-start(bf16[128,1024]{1,0:T(8,128)(2,1)S(1)} %collective-permute-done.2.refs_10_), channel_id=1, source_target_pairs={{0,2},{1,3},{2,0},{3,1},{4,6},{5,7},{6,4},{7,5},{8,10},{9,11},{10,... | collective-permute-start | bytes 786440 | tf_op jit(solution)/shard_map/ppermute | solution.py:35
  32.8 9.5 %collective-permute-start.7 = (bf16[128,1024]{1,0:T(8,128)(2,1)S(1)}, bf16[128,1024]{1,0:T(8,128)(2,1)S(1)}, u32[]{:S(2)}, u32[]{:S(2)}) collective-permute-start(bf16[128,1024]{1,0:T(8,128)(2,1)S(1)} %collective-permute-done.refs_6_), channel_id=1, source_target_pairs={{0,8},{8,0},{1,9},{9,1},{2,10},{10,2},{3,11},{11,3},{4,12},{12,4},... | collective-permute-start | bytes 786440 | tf_op jit(solution)/shard_map/ppermute | solution.py:27
  32.8 10.0 %collective-permute-start.9 = (bf16[128,1024]{1,0:T(8,128)(2,1)S(1)}, bf16[128,1024]{1,0:T(8,128)(2,1)S(1)}, u32[]{:S(2)}, u32[]{:S(2)}) collective-permute-start(bf16[128,1024]{1,0:T(8,128)(2,1)S(1)} %collective-permute-done.2.refs_10_), channel_id=1, source_target_pairs={{0,1},{1,0},{2,3},{3,2},{4,5},{5,4},{6,7},{7,6},{8,9},{9,8},{10,11... | collective-permute-start | bytes 786440 | tf_op jit(solution)/shard_map/ppermute | solution.py:35
  34.3 8.6 %collective-permute-start.10 = (bf16[128,1024]{1,0:T(8,128)(2,1)S(1)}, bf16[128,1024]{1,0:T(8,128)(2,1)S(1)}, u32[]{:S(2)}, u32[]{:S(2)}) collective-permute-start(bf16[128,1024]{1,0:T(8,128)(2,1)S(1)} %collective-permute-done.2.refs_10_), channel_id=1, source_target_pairs={{0,8},{8,0},{1,9},{9,1},{2,10},{10,2},{3,11},{11,3},{4,12},{12,4},... | collective-permute-start | bytes 786440 | tf_op jit(solution)/shard_map/ppermute | solution.py:27
  40.8 11.2 %collective-permute-start.12 = (bf16[128,1024]{1,0:T(8,128)(2,1)S(1)}, bf16[128,1024]{1,0:T(8,128)(2,1)S(1)}, u32[]{:S(2)}, u32[]{:S(2)}) collective-permute-start(bf16[128,1024]{1,0:T(8,128)(2,1)S(1)} %collective-permute-done.3.refs_2_), channel_id=1, source_target_pairs={{0,1},{1,0},{2,3},{3,2},{4,5},{5,4},{6,7},{7,6},{8,9},{9,8},{10,11... | collective-permute-start | bytes 786440 | tf_op jit(solution)/shard_map/ppermute | solution.py:35
  42.3 9.7 %collective-permute-start.8 = (bf16[128,1024]{1,0:T(8,128)(2,1)S(1)}, bf16[128,1024]{1,0:T(8,128)(2,1)S(1)}, u32[]{:S(2)}, u32[]{:S(2)}) collective-permute-start(bf16[128,1024]{1,0:T(8,128)(2,1)S(1)} %collective-permute-done.1.refs_7_), channel_id=1, source_target_pairs={{0,8},{8,0},{1,9},{9,1},{2,10},{10,2},{3,11},{11,3},{4,12},{12,4},... | collective-permute-start | bytes 786440 | tf_op jit(solution)/shard_map/ppermute | solution.py:27
  42.3 9.7 %collective-permute-start.6 = (bf16[128,1024]{1,0:T(8,128)(2,1)S(1)}, bf16[128,1024]{1,0:T(8,128)(2,1)S(1)}, u32[]{:S(2)}, u32[]{:S(2)}) collective-permute-start(bf16[128,1024]{1,0:T(8,128)(2,1)S(1)} %collective-permute-done.4.refs_3_), channel_id=1, source_target_pairs={{0,8},{8,0},{1,9},{9,1},{2,10},{10,2},{3,11},{11,3},{4,12},{12,4},... | collective-permute-start | bytes 786440 | tf_op jit(solution)/shard_map/ppermute | solution.py:27
  42.8 9.2 %collective-permute-start.11 = (bf16[128,1024]{1,0:T(8,128)(2,1)S(1)}, bf16[128,1024]{1,0:T(8,128)(2,1)S(1)}, u32[]{:S(2)}, u32[]{:S(2)}) collective-permute-start(bf16[128,1024]{1,0:T(8,128)(2,1)S(1)} %collective-permute-done.9.refs_11_), channel_id=1, source_target_pairs={{0,8},{8,0},{1,9},{9,1},{2,10},{10,2},{3,11},{11,3},{4,12},{12,4},... | collective-permute-start | bytes 786440 | tf_op jit(solution)/shard_map/ppermute | solution.py:27
  42.9 10.1 %collective-permute-start.13 = (bf16[128,1024]{1,0:T(8,128)(2,1)S(1)}, bf16[128,1024]{1,0:T(8,128)(2,1)S(1)}, u32[]{:S(2)}, u32[]{:S(2)}) collective-permute-start(bf16[128,1024]{1,0:T(8,128)(2,1)S(1)} %collective-permute-done.3.refs_2_), channel_id=1, source_target_pairs={{0,8},{8,0},{1,9},{9,1},{2,10},{10,2},{3,11},{11,3},{4,12},{12,4},... | collective-permute-start | bytes 786440 | tf_op jit(solution)/shard_map/ppermute | solution.py:27
  51.9 1.5 collective-permute-start.14
  53.9 8.4 %collective-permute-start.15 = (bf16[128,1024]{1,0:T(8,128)(2,1)S(1)}, bf16[128,1024]{1,0:T(8,128)(2,1)S(1)}, u32[]{:S(2)}, u32[]{:S(2)}) collective-permute-start(bf16[128,1024]{1,0:T(8,128)(2,1)S(1)} %get-tuple-element.86), channel_id=1, source_target_pairs={{0,16},{16,0},{1,17},{17,1},{2,18},{18,2},{3,19},{19,3},{4,20},{20... | collective-permute-start | bytes 786440 | tf_op jit(solution)/shard_map/ppermute | solution.py:31
  70.2 2.0 collective-permute-start.16
  70.3 14.7 %collective-permute-start.17 = (bf16[144,1024]{1,0:T(8,128)(2,1)S(1)}, bf16[144,1024]{1,0:T(8,128)(2,1)S(1)}, u32[]{:S(2)}, u32[]{:S(2)}) collective-permute-start(bf16[144,1024]{1,0:T(8,128)(2,1)S(1)} %finish_latent.1.refs_0_), channel_id=1, source_target_pairs={{0,2},{1,3},{2,0},{3,1},{4,6},{5,7},{6,4},{7,5},{8,10},{9,11},{10,... | collective-permute-start | bytes 884744 | tf_op jit(solution)/shard_map/ppermute | solution.py:35
  70.4 16.6 %collective-permute-start.18 = (bf16[144,1024]{1,0:T(8,128)(2,1)S(1)}, bf16[144,1024]{1,0:T(8,128)(2,1)S(1)}, u32[]{:S(2)}, u32[]{:S(2)}) collective-permute-start(bf16[144,1024]{1,0:T(8,128)(2,1)S(1)} %finish_latent.1.refs_0_), channel_id=1, source_target_pairs={{0,4},{1,5},{2,6},{3,7},{4,0},{5,1},{6,2},{7,3},{8,12},{9,13},{10,... | collective-permute-start | bytes 884744 | tf_op jit(solution)/shard_map/ppermute | solution.py:35
  86.9 1.6 collective-permute-start.20
  86.9 2.0 collective-permute-start.21
  87.4 11.5 %collective-permute-start.22 = (bf16[144,1024]{1,0:T(8,128)(2,1)S(1)}, bf16[144,1024]{1,0:T(8,128)(2,1)S(1)}, u32[]{:S(2)}, u32[]{:S(2)}) collective-permute-start(bf16[144,1024]{1,0:T(8,128)(2,1)S(1)} %collective-permute-done.18.refs_1_), channel_id=1, source_target_pairs={{0,2},{1,3},{2,0},{3,1},{4,6},{5,7},{6,4},{7,5},{8,10},{9,11},{10,... | collective-permute-start | bytes 884744 | tf_op jit(solution)/shard_map/ppermute | solution.py:35
  87.4 11.5 %collective-permute-start.23 = (bf16[144,1024]{1,0:T(8,128)(2,1)S(1)}, bf16[144,1024]{1,0:T(8,128)(2,1)S(1)}, u32[]{:S(2)}, u32[]{:S(2)}) collective-permute-start(bf16[144,1024]{1,0:T(8,128)(2,1)S(1)} %collective-permute-done.18.refs_1_), channel_id=1, source_target_pairs={{0,1},{1,0},{2,3},{3,2},{4,5},{5,4},{6,7},{7,6},{8,9},{9,8},{10,11... | collective-permute-start | bytes 884744 | tf_op jit(solution)/shard_map/ppermute | solution.py:35
  98.9 2.7 %collective-permute-start.24 = (bf16[144,1024]{1,0:T(8,128)(2,1)S(1)}, bf16[144,1024]{1,0:T(8,128)(2,1)}, u32[]{:S(2)}, u32[]{:S(2)}) collective-permute-start(bf16[144,1024]{1,0:T(8,128)(2,1)S(1)} %collective-permute-done.22.refs_0_), channel_id=1, source_target_pairs={{0,8},{8,0},{1,9},{9,1},{2,10},{10,2},{3,11},{11,3},{4,12},{12,4},... | collective-permute-start | bytes 884744 | tf_op jit(solution)/shard_map/ppermute | solution.py:27
  99.1 2.5 %collective-permute-start.25 = (bf16[144,1024]{1,0:T(8,128)(2,1)S(1)}, bf16[144,1024]{1,0:T(8,128)(2,1)}, u32[]{:S(2)}, u32[]{:S(2)}) collective-permute-start(bf16[144,1024]{1,0:T(8,128)(2,1)S(1)} %collective-permute-done.23.refs_1_), channel_id=1, source_target_pairs={{0,8},{8,0},{1,9},{9,1},{2,10},{10,2},{3,11},{11,3},{4,12},{12,4},... | collective-permute-start | bytes 884744 | tf_op jit(solution)/shard_map/ppermute | solution.py:27
  99.5 19.4 %collective-permute-start.26 = (bf16[144,1024]{1,0:T(8,128)(2,1)S(1)}, bf16[144,1024]{1,0:T(8,128)(2,1)S(1)}, u32[]{:S(2)}, u32[]{:S(2)}) collective-permute-start(bf16[144,1024]{1,0:T(8,128)(2,1)S(1)} %finish_latent.1.refs_0_), channel_id=1, source_target_pairs={{0,1},{1,0},{2,3},{3,2},{4,5},{5,4},{6,7},{7,6},{8,9},{9,8},{10,11... | collective-permute-start | bytes 884744 | tf_op jit(solution)/shard_map/ppermute | solution.py:35
  100.7 18.2 %collective-permute-start.27 = (bf16[144,1024]{1,0:T(8,128)(2,1)S(1)}, bf16[144,1024]{1,0:T(8,128)(2,1)S(1)}, u32[]{:S(2)}, u32[]{:S(2)}) collective-permute-start(bf16[144,1024]{1,0:T(8,128)(2,1)S(1)} %collective-permute-done.22.refs_0_), channel_id=1, source_target_pairs={{0,1},{1,0},{2,3},{3,2},{4,5},{5,4},{6,7},{7,6},{8,9},{9,8},{10,11... | collective-permute-start | bytes 884744 | tf_op jit(solution)/shard_map/ppermute | solution.py:35
  101.6 18.8 %collective-permute-start.29 = (bf16[256,1024]{1,0:T(8,128)(2,1)S(1)}, bf16[256,1024]{1,0:T(8,128)(2,1)S(1)}, u32[]{:S(2)}, u32[]{:S(2)}) collective-permute-start(bf16[256,1024]{1,0:T(8,128)(2,1)S(1)} %get-tuple-element.116), channel_id=1, source_target_pairs={{0,8},{8,0},{1,9},{9,1},{2,10},{10,2},{3,11},{11,3},{4,12},{12,4},... | collective-permute-start | bytes 1572872 | tf_op jit(solution)/shard_map/ppermute | solution.py:27
  118.9 2.1 %collective-permute-start.30 = (bf16[256,1024]{1,0:T(8,128)(2,1)S(1)}, bf16[256,1024]{1,0:T(8,128)(2,1)S(1)}, u32[]{:S(2)}, u32[]{:S(2)}) collective-permute-start(bf16[256,1024]{1,0:T(8,128)(2,1)S(1)} %get-tuple-element.118), channel_id=1, source_target_pairs={{0,8},{8,0},{1,9},{9,1},{2,10},{10,2},{3,11},{11,3},{4,12},{12,4},... | collective-permute-start | bytes 1572872 | tf_op jit(solution)/shard_map/ppermute | solution.py:27
  119.5 9.9 %collective-permute-start.32 = (bf16[144,1024]{1,0:T(8,128)(2,1)S(1)}, bf16[144,1024]{1,0:T(8,128)(2,1)S(1)}, u32[]{:S(2)}, u32[]{:S(2)}) collective-permute-start(bf16[144,1024]{1,0:T(8,128)(2,1)S(1)} %collective-permute-done.17.refs_0_), channel_id=1, source_target_pairs={{0,1},{1,0},{2,3},{3,2},{4,5},{5,4},{6,7},{7,6},{8,9},{9,8},{10,11... | collective-permute-start | bytes 884744 | tf_op jit(solution)/shard_map/ppermute | solution.py:35
  120.5 1.7 collective-permute-start.28
  121.1 16.9 %copy-start.2 = (bf16[1,1024,2048]{2,1,0:T(8,128)(2,1)S(1)}, bf16[1,1024,2048]{2,1,0:T(8,128)(2,1)}, u32[]{:S(2)}) copy-start(bf16[1,1024,2048]{2,1,0:T(8,128)(2,1)} %refs_4_.9) | copy-start | bytes 12582916
  121.1 13.0 %collective-permute-start.31 = (bf16[128,1024]{1,0:T(8,128)(2,1)S(1)}, bf16[128,1024]{1,0:T(8,128)(2,1)S(1)}, u32[]{:S(2)}, u32[]{:S(2)}) collective-permute-start(bf16[128,1024]{1,0:T(8,128)(2,1)S(1)} %add_convert_fusion.6), channel_id=1, source_target_pairs={{0,1},{1,0},{2,3},{3,2},{4,5},{5,4},{6,7},{7,6},{8,9},{9,8},{10,11... | collective-permute-start | bytes 786440 | tf_op jit(solution)/shard_map/ppermute | solution.py:35
  134.1 3.0 %collective-permute-start.35 = (bf16[128,1024]{1,0:T(8,128)(2,1)S(1)}, bf16[128,1024]{1,0:T(8,128)(2,1)S(1)}, u32[]{:S(2)}, u32[]{:S(2)}) collective-permute-start(bf16[128,1024]{1,0:T(8,128)(2,1)S(1)} %get-tuple-element.125), channel_id=1, source_target_pairs={{0,8},{8,0},{1,9},{9,1},{2,10},{10,2},{3,11},{11,3},{4,12},{12,4},... | collective-permute-start | bytes 786440 | tf_op jit(solution)/shard_map/ppermute | solution.py:27
  134.1 3.9 %collective-permute-start.33 = (bf16[144,1024]{1,0:T(8,128)(2,1)S(1)}, bf16[144,1024]{1,0:T(8,128)(2,1)S(1)}, u32[]{:S(2)}, u32[]{:S(2)}) collective-permute-start(bf16[144,1024]{1,0:T(8,128)(2,1)S(1)} %collective-permute-done.26.refs_0_), channel_id=1, source_target_pairs={{0,8},{8,0},{1,9},{9,1},{2,10},{10,2},{3,11},{11,3},{4,12},{12,4},... | collective-permute-start | bytes 884744 | tf_op jit(solution)/shard_map/ppermute | solution.py:27
  134.6 12.2 %collective-permute-start.37 = (bf16[128,1024]{1,0:T(8,128)(2,1)S(1)}, bf16[128,1024]{1,0:T(8,128)(2,1)S(1)}, u32[]{:S(2)}, u32[]{:S(2)}) collective-permute-start(bf16[128,1024]{1,0:T(8,128)(2,1)S(1)} %add_convert_fusion.7), channel_id=1, source_target_pairs={{0,2},{1,3},{2,0},{3,1},{4,6},{5,7},{6,4},{7,5},{8,10},{9,11},{10,... | collective-permute-start | bytes 786440 | tf_op jit(solution)/shard_map/ppermute | solution.py:35
  136.3 1.8 collective-permute-start.34
  137.2 10.3 %collective-permute-start.36 = (bf16[128,1024]{1,0:T(8,128)(2,1)S(1)}, bf16[128,1024]{1,0:T(8,128)(2,1)S(1)}, u32[]{:S(2)}, u32[]{:S(2)}) collective-permute-start(bf16[128,1024]{1,0:T(8,128)(2,1)S(1)} %add_convert_fusion.5), channel_id=1, source_target_pairs={{0,1},{1,0},{2,3},{3,2},{4,5},{5,4},{6,7},{7,6},{8,9},{9,8},{10,11... | collective-permute-start | bytes 786440 | tf_op jit(solution)/shard_map/ppermute | solution.py:35
  147.5 1.9 collective-permute-start.38
  147.7 3.9 %collective-permute-start.19 = (bf16[128,1024]{1,0:T(8,128)(2,1)S(1)}, bf16[128,1024]{1,0:T(8,128)(2,1)}, u32[]{:S(2)}, u32[]{:S(2)}) collective-permute-start(bf16[128,1024]{1,0:T(8,128)(2,1)S(1)} %get-tuple-element.94), channel_id=1, source_target_pairs={{0,8},{8,0},{1,9},{9,1},{2,10},{10,2},{3,11},{11,3},{4,12},{12,4},... | collective-permute-start | bytes 786440 | tf_op jit(solution)/shard_map/ppermute | solution.py:27
  150.4 8.8 %collective-permute-start.39 = (bf16[128,1024]{1,0:T(8,128)(2,1)}, bf16[128,1024]{1,0:T(8,128)(2,1)}, u32[]{:S(2)}, u32[]{:S(2)}) collective-permute-start(bf16[128,1024]{1,0:T(8,128)(2,1)} %get-tuple-element.146), channel_id=1, source_target_pairs={{0,1},{1,0},{2,3},{3,2},{4,5},{5,4},{6,7},{7,6},{8,9},{9,8},{10,11... | collective-permute-start | bytes 786440 | tf_op jit(solution)/shard_map/ppermute | solution.py:35
  151.6 33.3 %collective-permute-start.43 = (bf16[8,256,512]{2,1,0:T(8,128)(2,1)S(1)}, bf16[8,256,512]{2,1,0:T(8,128)(2,1)}, u32[]{:S(2)}, u32[]{:S(2)}) collective-permute-start(bf16[8,256,512]{2,1,0:T(8,128)(2,1)S(1)} %bitcast.13), channel_id=1, source_target_pairs={{0,8},{8,0},{1,9},{9,1},{2,10},{10,2},{3,11},{11,3},{4,12},{12,4},... | collective-permute-start | bytes 6291464 | tf_op jit(solution)/shard_map/ppermute | solution.py:27
  163.6 24.3 %collective-permute-start.44 = (bf16[8,256,512]{2,1,0:T(8,128)(2,1)}, bf16[8,256,512]{2,1,0:T(8,128)(2,1)}, u32[]{:S(2)}, u32[]{:S(2)}) collective-permute-start(bf16[8,256,512]{2,1,0:T(8,128)(2,1)} %dynamic-slice_bitcast_fusion.refs_6_), channel_id=1, source_target_pairs={{0,8},{8,0},{1,9},{9,1},{2,10},{10,2},{3,11},{11,3},{4,12},{12,4},... | collective-permute-start | bytes 6291464 | tf_op jit(solution)/shard_map/ppermute | solution.py:27
  163.6 21.3 %collective-permute-start.41 = (bf16[128,1024]{1,0:T(8,128)(2,1)}, bf16[128,1024]{1,0:T(8,128)(2,1)}, u32[]{:S(2)}, u32[]{:S(2)}) collective-permute-start(bf16[128,1024]{1,0:T(8,128)(2,1)} %add_convert_fusion.4), channel_id=1, source_target_pairs={{0,4},{1,5},{2,6},{3,7},{4,0},{5,1},{6,2},{7,3},{8,12},{9,13},{10,... | collective-permute-start | bytes 786440 | tf_op jit(solution)/shard_map/ppermute | solution.py:35
  164.8 20.2 %collective-permute-start.42 = (bf16[128,1024]{1,0:T(8,128)(2,1)}, bf16[128,1024]{1,0:T(8,128)(2,1)}, u32[]{:S(2)}, u32[]{:S(2)}) collective-permute-start(bf16[128,1024]{1,0:T(8,128)(2,1)} %add_convert_fusion), channel_id=1, source_target_pairs={{0,6},{1,7},{2,4},{3,5},{4,2},{5,3},{6,0},{7,1},{8,14},{9,15},{10,... | collective-permute-start | bytes 786440 | tf_op jit(solution)/shard_map/ppermute | solution.py:35
  167.4 20.5 %collective-permute-start.40 = (bf16[128,1024]{1,0:T(8,128)(2,1)}, bf16[128,1024]{1,0:T(8,128)(2,1)}, u32[]{:S(2)}, u32[]{:S(2)}) collective-permute-start(bf16[128,1024]{1,0:T(8,128)(2,1)} %get-tuple-element.145), channel_id=1, source_target_pairs={{0,3},{1,2},{2,1},{3,0},{4,7},{5,6},{6,5},{7,4},{8,11},{9,10},{10,... | collective-permute-start | bytes 786440 | tf_op jit(solution)/shard_map/ppermute | solution.py:35
  (15 other events, 43.6 us)
Sparse Core Ops, SparseCore 0:
  9.5 60.5 all-gather.4
  99.7 56.0 all-gather.6

commit v7 on v5

--- a/solution.py
+++ b/solution.py
@@ -155,10 +155,10 @@
 
 def expert_kernel(positions, count, where, *refs):
     pieces = refs[: 2 * positions]
-    gate, up, out = refs[2 * positions : 2 * positions + 3]
-    own_sums = refs[2 * positions + 3 : 3 * positions + 3]
-    other_sums, rows, hidden, held, gate_block, up_block, out_block, sems = refs[-8:]
-    width = 256
+    gate_first, up_first, gate, up, out = refs[2 * positions : 2 * positions + 5]
+    own_sums, refs = refs[2 * positions + 5 : 3 * positions + 5], refs[3 * positions + 5 :]
+    other_sums, rows, hidden, held, gate_block, up_block, out_block, sems = refs
+    width = gate_first.shape[1]
     blocks = gate.shape[2] // width
 
     def columns_at(start):
@@ -171,7 +171,7 @@
             source.at[0, :, columns], target.at[:, columns], sems.at[part * blocks + i]
         )
 
-    for i in range(blocks):
+    for i in range(1, blocks):
         read(i, 0).start()
         read(i, 1).start()
     for i in range(out.shape[2] // width):
@@ -193,19 +193,18 @@
         read(i, 0).wait()
         read(i, 1).wait()
 
+    def dots(*blocks):
+        return [jnp.dot(rows[...], b, preferred_element_type=jnp.float32) for b in blocks]
+
     def products(i):
         columns = columns_at(i * width)
-        return (
-            jnp.dot(rows[...], gate_block[:, columns], preferred_element_type=jnp.float32),
-            jnp.dot(rows[...], up_block[:, columns], preferred_element_type=jnp.float32),
-        )
+        return dots(gate_block[:, columns], up_block[:, columns])
 
     def activate(gate_value, up_value, i):
         value = gate_value / (1.0 + jnp.exp(-gate_value)) * up_value
         hidden[:, columns_at(i * width)] = value.astype(jnp.bfloat16)
 
-    arrive(0)
-    held[0], held[1] = products(0)
+    held[0], held[1] = dots(gate_first[...], up_first[...])
 
     def step(i, carry):
         arrive(2 * i + 1)
@@ -238,50 +237,48 @@
     lax.fori_loop(0, out.shape[2] // width, finish, 0)
 
 
-def expert_apply(expert, owns, others, gate_weight, up_weight, out_weight, count):
+def expert_apply(expert, owns, others, firsts, weights, count):
     positions = len(owns)
     latent_width = owns[0].shape[1]
-    hidden_width = gate_weight.shape[2]
-    rows = 2 * positions * count
+    hidden_width = weights[0].shape[2]
+    rows, width = 2 * positions * count, firsts[0].shape[1]
     own_sum = jax.ShapeDtypeStruct((count, latent_width), jnp.bfloat16)
     other_sums = jax.ShapeDtypeStruct((positions * count, latent_width), jnp.bfloat16)
     return pl.pallas_call(
         functools.partial(expert_kernel, positions, count),
         out_shape=(own_sum,) * positions + (other_sums,),
-        in_specs=[in_smem] + [in_vmem] * (2 * positions) + [in_hbm] * 3,
+        in_specs=[in_smem] + [in_vmem] * (2 * positions + 2) + [in_hbm] * 3,
         out_specs=(in_vmem,) * (positions + 1),
         scratch_shapes=[
             pltpu.VMEM((rows, latent_width), jnp.bfloat16),
             pltpu.VMEM((rows, hidden_width), jnp.bfloat16),
-            pltpu.VMEM((2, rows, 256), jnp.float32),
-            pltpu.VMEM((latent_width, hidden_width), jnp.bfloat16),
-            pltpu.VMEM((latent_width, hidden_width), jnp.bfloat16),
-            pltpu.VMEM((hidden_width, latent_width), jnp.bfloat16),
-            pltpu.SemaphoreType.DMA(((2 * hidden_width + latent_width) // 256,)),
-        ],
-        compiler_params=pltpu.CompilerParams(vmem_limit_bytes=32 * mebi),
+            pltpu.VMEM((2, rows, width), jnp.float32),
+        ]
+        + [pltpu.VMEM(w.shape[1:], w.dtype) for w in weights]
+        + [pltpu.SemaphoreType.DMA(((2 * hidden_width + latent_width) // width,))],
+        compiler_params=pltpu.CompilerParams(vmem_limit_bytes=28 * mebi),
         cost_estimate=pl.CostEstimate(
             flops=6 * rows * latent_width * hidden_width,
             bytes_accessed=4 * rows * latent_width,
             transcendentals=rows * hidden_width,
         ),
         name="expert",
-    )(expert, *owns, *others, gate_weight, up_weight, out_weight)
+    )(expert, *owns, *others, *firsts, *weights)
 
 
 def project_kernel(where, *refs):
-    terms, refs = refs[:-11], refs[-11:]
-    mine, across, near_core, far_core, layer_out, combined, held, held_across, blocks = refs[:9]
-    read_sems, sems = refs[9:]
-    ep_count, inner, width = mine.shape
-
-    def read(e, i):
-        source, target = ((mine, held), (across, held_across))[i]
-        return pltpu.make_async_copy(source.at[e], target.at[e], read_sems.at[2 * e + i])
+    terms, refs = refs[:-8], refs[-8:]
+    mine, swapped, layer_out, combined, held, blocks, read_sems, sems = refs
+    sides, ep_count, inner, width = mine.shape
+
+    def read(e, side):
+        return pltpu.make_async_copy(
+            mine.at[side, e], held.at[side, e], read_sems.at[sides * e + side]
+        )
 
     for e in range(ep_count):
-        for i in range(2):
-            read(e, i).start()
+        for side in range(sides):
+            read(e, side).start()
     total = terms[0][...].astype(jnp.float32)
     for term in terms[1:]:
         total += term[...].astype(jnp.float32)
@@ -293,31 +290,32 @@
 
     for e in range(ep_count):
         value = 0.0
-        for i, array in enumerate((near_core, far_core, held, held_across)):
-            if i >= 2:
-                read(e, i - 2).wait()
-            columns = pl.ds(pl.multiple_of(where[i] * inner, inner), inner)
-            value += jnp.dot(combined[:, columns], array[e], preferred_element_type=jnp.float32)
+        for side in range(sides):
+            read(e, side).wait()
+            for core, array in ((1 - where[0], swapped), (where[0], held)):
+                columns = pl.ds(pl.multiple_of((2 * side + core) * inner, inner), inner)
+                value += jnp.dot(
+                    combined[:, columns], array[side, e], preferred_element_type=jnp.float32
+                )
         blocks[:, e * width : (e + 1) * width] = value.astype(jnp.bfloat16)
         sent(e).start()
     for e in range(ep_count):
         sent(e).wait()
 
 
-def project(where, terms, mine, across, near_core, far_core):
+def project(group, terms, mine, swapped):
     count, latent_width = terms[0].shape
-    ep_count, inner, width = mine.shape
+    sides, ep_count, inner, width = mine.shape
     return pl.pallas_call(
         project_kernel,
-        in_specs=[in_smem] + [in_vmem] * len(terms) + [in_hbm] * 2 + [in_vmem] * 2,
+        in_specs=[in_smem] + [in_vmem] * len(terms) + [in_hbm, in_vmem],
         out_specs=anywhere,
         out_shape=jax.ShapeDtypeStruct((count, ep_count * width), jnp.bfloat16),
         scratch_shapes=[
             pltpu.VMEM((count, latent_width), jnp.bfloat16),
             pltpu.VMEM(mine.shape, mine.dtype),
-            pltpu.VMEM(mine.shape, mine.dtype),
             pltpu.VMEM((count, ep_count * width), jnp.bfloat16),
-            pltpu.SemaphoreType.DMA((2 * ep_count,)),
+            pltpu.SemaphoreType.DMA((sides * ep_count,)),
             pltpu.SemaphoreType.DMA((ep_count,)),
         ],
         compiler_params=pltpu.CompilerParams(vmem_limit_bytes=16 * mebi),
@@ -327,7 +325,7 @@
             transcendentals=0,
         ),
         name="project",
-    )(where, *terms, mine, across, near_core, far_core)
+    )(group.reshape(1).astype(jnp.int32), *terms, mine, swapped)
 
 
 def body(
@@ -361,14 +359,14 @@
     far[1] = swap_ep(near[1], 1)
     weights = dense_weights(after(expert_ids, near[1]), route_scores, expert_count)
     others = {k: near[k] for k in near if k > 1}
-    *arrived, weights = join(*others.values(), weights)
+    far[1], weights, *arrived = join(far[1], weights, *others.values())
     near.update(zip(others, arrived))
     for k in range(2, steps):
         if k & (k - 1):
             low = k & -k
             near[k] = swap_ep(near[k ^ low], 2 * low)
         if k == last:
-            near[k], far[1], taken = join(near[k], far[1], taken)
+            near[k], far[0], taken = join(near[k], far[0], taken)
         far[k] = swap_ep(near[k], 1)
     blocks = []
     for k in range(steps):
@@ -378,12 +376,18 @@
     (partial,) = down_project(early, kept, taken, [b for k in early for b in blocks[k]])
     late = [after(blocks[-1][0], partial), *blocks[-1][1:]]
     own_part, sent_part = down_project([last], kept, taken, late, partial)
-    latent = finish_latent(own_part, swap_reps(sent_part), weights.astype(jnp.bfloat16))
-
-    gate_weight, up_weight, out_weight = [
-        pltpu.with_memory_space_constraint(w, pltpu.HBM) for w in (gate_weight, up_weight, out_weight)
+    arrived, mine = join(swap_reps(sent_part), mine)
+    latent = finish_latent(own_part, arrived, weights.astype(jnp.bfloat16))
+
+    sides = [[i, i + 1] for i in range(0, lax.axis_size("rep"), 2)]
+    both_sides = lax.all_gather(mine, "rep", axis=0, axis_index_groups=sides)
+
+    expert = (group * ep_count + place).astype(jnp.int32).reshape(1)
+    firsts = [w[0, :, :256] for w in (gate_weight, up_weight)]
+    expert_weights = [
+        pltpu.with_memory_space_constraint(w, pltpu.HBM)
+        for w in (gate_weight, up_weight, out_weight)
     ]
-    expert = (group * ep_count + place).astype(jnp.int32).reshape(1)
     near = first_steps(latent, steps)
     far, away, sent, pairs, own_sums, swapped = {}, {}, {}, {}, {}, {}
 
@@ -396,9 +400,8 @@
             expert,
             operands[:count],
             operands[count:],
-            gate_weight,
-            up_weight,
-            out_weight,
+            firsts,
+            expert_weights,
             token_count,
         )
         names = [(table, key) for table, keys in coming for key in keys]
@@ -427,15 +430,12 @@
     def start_far(k):
         far[k] = swap_ep(near[k], 1)
 
-    gathered = {"mine": mine}
     powers = [k for k in near if k]
     run([(0, 0)], [(near, powers)])
     if last >= 3:
         start_near(3)
     start_far(2)
-    run([(1, 0), (2, 0)], [(near, [3]), (far, [2]), (gathered, ["mine"])])
-    mine = gathered["mine"]
-    gathered["across"] = swap_reps(mine)
+    run([(1, 0), (2, 0)], [(near, [3] if last >= 3 else []), (far, [2])])
     returning = []
     for k in range(3, steps):
         start_far(k)
@@ -456,24 +456,24 @@
     for j in returning:
         pair_sum(j)
     send_far(last)
-    homeward = {"near": swap_ep(near_home, 2)}
+    homeward = {("near", 1): swap_ep(near_home, 2)}
+    for k in range(2, last):
+        homeward["pair", k] = swap_ep(pairs[k], 2 * k)
     run(
         [(0, 1), (1, 1)],
-        [(away, [last]), (gathered, ["across"]), (homeward, ["near"])],
+        [(away, [last]), (homeward, list(homeward))],
         sent[last],
         *pairs.values(),
     )
-    across = gathered["across"]
     pair_sum(last)
     send_far(0)
-    far_home = chip_sum(1, 1).astype(jnp.bfloat16)
-    pair_sum(0)
-    terms = [pairs[0], homeward["near"], swap_ep(far_home, 3)]
-    terms += [swap_ep(pairs[k], 2 * k) for k in range(2, steps)]
-
-    where = [own_quarter ^ 1, own_quarter ^ 3, own_quarter, own_quarter ^ 2]
-    where = jnp.stack(where).astype(jnp.int32)
-    return project(where, terms, mine, across, swap_cores(mine), swap_cores(across))
+    homeward["far", 1] = swap_ep(chip_sum(1, 1).astype(jnp.bfloat16), 3)
+    homeward["pair", last] = swap_ep(pairs[last], 2 * last)
+    both_sides = after(both_sides, sent[0])
+    terms = [own_sums[0, 0], swapped[0, 0], away[0], *homeward.values()]
+    *terms, swapped_sides = join(*terms, swap_cores(both_sides))
+    both_sides = pltpu.with_memory_space_constraint(both_sides, pltpu.HBM)
+    return project(group, terms, both_sides, swapped_sides)
 
 
 def solution(mesh):

time: 219 us -> 183 us (0.84)
  waiting for transfers between devices: 98.7 us -> 71.1 us
  starting transfers between devices: 40.6 us -> 34.4 us
    ppermute x3 -> x2, waiting for transfers between devices: 23.6 us -> 6.83 us  [swap_reps(): lax.ppermute(array, 'rep', [(i, i ^ 1) for i in range(lax.axis_size('rep'...]
    ppermute x21, waiting for transfers between devices: 68.9 us -> 55 us  [swap_ep(): lax.ppermute(array, 'ep', [(i, i ^ mask) for i in range(lax.axis_size('ep...]
    ppermute x21, starting transfers between devices: 32.2 us -> 27.2 us  [swap_ep(): lax.ppermute(array, 'ep', [(i, i ^ mask) for i in range(lax.axis_size('ep...]
    all_gather x1, waiting for transfers between devices: 0.01 us -> 4.88 us  [body(): mine = lax.all_gather(up_piece, 'ep', axis=0)]
    ppermute x3 -> x2, starting transfers between devices: 5.08 us -> 3.15 us  [swap_reps(): lax.ppermute(array, 'rep', [(i, i ^ 1) for i in range(lax.axis_size('rep'...]
    ppermute x22 -> x21, waiting for transfers between devices: 6.24 us -> 4.32 us  [swap_cores(): return lax.ppermute(array, 'grp', [(0, 1), (1, 0)])]
    unnamed x36 -> x16, local copies, waits for them, and re-layouts: 5.08 us -> 4.14 us
  transfers between devices with their start and end apart: 47 -> 46, of which waited for: 21 -> 17; matrix products, arithmetic and copies ran while one was open for 3% -> 4% of each run, Pallas kernels for 22% -> 26%
where the time goes in v7:
time: 183 us
  waiting for transfers between devices  71.1 us (39%)
  Pallas kernels  52.1 us (28%)
  starting transfers between devices  34.4 us (19%)
  between operations  13.7 us (7%)
  local copies, waits for them, and re-layouts  7.2 us (4%)
  other arithmetic  4.59 us (3%)
    ppermute x21, waiting for transfers between devices, swap_ep(): lax.ppermute(array, 'ep', [(i, i ^ mask) for i in range(lax.axis_size('ep...  55 us
    pallas_call x5, Pallas kernels, expert_apply(): pl.pallas_call(functools.partial(expert_kernel, positions, count), out_sh...  45.1 us
    ppermute x21, starting transfers between devices, swap_ep(): lax.ppermute(array, 'ep', [(i, i ^ mask) for i in range(lax.axis_size('ep...  27.2 us
    ppermute x2, waiting for transfers between devices, swap_reps(): lax.ppermute(array, 'rep', [(i, i ^ 1) for i in range(lax.axis_size('rep'...  6.83 us
    all_gather x1, waiting for transfers between devices, body(): mine = lax.all_gather(up_piece, 'ep', axis=0)  4.88 us
    pallas_call x1, Pallas kernels, project(): pl.pallas_call(project_kernel, in_specs=[in_smem] + [in_vmem] * len(terms...  4.71 us
    ppermute x21, waiting for transfers between devices, swap_cores(): return lax.ppermute(array, 'grp', [(0, 1), (1, 0)])  4.32 us
    unnamed x16, local copies, waits for them, and re-layouts  4.14 us
  transfers between devices with their start and end apart: 46, of which 17 were waited for; matrix products, arithmetic and copies ran while one was open for 4% of the time, Pallas kernels for 26%

profile of v7, /device:TPU:0, one launch (start us, length us, event | category | flops | bytes accessed | tf_op | source)
XLA Modules:
  0.0 183.0 jit_solution(484874284844385029)
XLA Ops:
  6.5 1.2 copy-done
  8.6 1.1 constant_dynamic-slice_fusion.1
  9.6 3.1 %collective-permute-start = (bf16[128,1024]{1,0:T(8,128)(2,1)S(1)}, bf16[128,1024]{1,0:T(8,128)(2,1)S(1)}, u32[]{:S(2)}, u32[]{:S(2)}) collective-permute-start(bf16[128,1024]{1,0:T(8,128)(2,1)S(1)} %get-tuple-element.162.refs_2_), channel_id=1, source_target_pairs={{0,2},{1,3},{2,0},{3,1},{4,6},{5,7},{6,4},{7,5},{8,10},{9,11},{10,... | collective-permute-start | bytes 786440 | tf_op jit(solution)/shard_map/ppermute | solution.py:35
  12.7 1.5 collective-permute-start.4
  14.3 2.6 %collective-permute-start.2 = (bf16[128,1024]{1,0:T(8,128)(2,1)S(1)}, bf16[128,1024]{1,0:T(8,128)(2,1)S(1)}, u32[]{:S(2)}, u32[]{:S(2)}) collective-permute-start(bf16[128,1024]{1,0:T(8,128)(2,1)S(1)} %get-tuple-element.162.refs_2_), channel_id=1, source_target_pairs={{0,4},{1,5},{2,6},{3,7},{4,0},{5,1},{6,2},{7,3},{8,12},{9,13},{10,... | collective-permute-start | bytes 786440 | tf_op jit(solution)/shard_map/ppermute | solution.py:35
  16.9 1.2 copy-done.1
  18.1 0.8 split_columns.1
  19.0 1.6 collective-permute-start.5
  21.2 2.5 %collective-permute-done.refs_6_ = bf16[128,1024]{1,0:T(8,128)(2,1)S(1)} collective-permute-done((bf16[128,1024]{1,0:T(8,128)(2,1)S(1)}, bf16[128,1024]{1,0:T(8,128)(2,1)S(1)}, u32[]{:S(2)}, u32[]{:S(2)}) %collective-permute-start) | collective-permute-done | bytes 262176 | tf_op jit(solution)/shard_map/ppermute | solution.py:35
  23.7 3.8 %collective-permute-start.1 = (bf16[128,1024]{1,0:T(8,128)(2,1)S(1)}, bf16[128,1024]{1,0:T(8,128)(2,1)S(1)}, u32[]{:S(2)}, u32[]{:S(2)}) collective-permute-start(bf16[128,1024]{1,0:T(8,128)(2,1)S(1)} %collective-permute-done.refs_6_), channel_id=1, source_target_pairs={{0,1},{1,0},{2,3},{3,2},{4,5},{5,4},{6,7},{7,6},{8,9},{9,8},{10,11... | collective-permute-start | bytes 786440 | tf_op jit(solution)/shard_map/ppermute | solution.py:35
  28.2 0.7 select_reduce_fusion.weights
  28.9 4.1 %collective-permute-done.2.refs_10_ = bf16[128,1024]{1,0:T(8,128)(2,1)S(1)} collective-permute-done((bf16[128,1024]{1,0:T(8,128)(2,1)S(1)}, bf16[128,1024]{1,0:T(8,128)(2,1)S(1)}, u32[]{:S(2)}, u32[]{:S(2)}) %collective-permute-start.2) | collective-permute-done | bytes 262176 | tf_op jit(solution)/shard_map/ppermute | solution.py:35
  33.1 0.9 collective-permute-start.3
  34.5 7.3 %collective-permute-done.3.refs_2_ = bf16[128,1024]{1,0:T(8,128)(2,1)S(1)} collective-permute-done((bf16[128,1024]{1,0:T(8,128)(2,1)S(1)}, bf16[128,1024]{1,0:T(8,128)(2,1)S(1)}, u32[]{:S(2)}, u32[]{:S(2)}) %collective-permute-start.3) | collective-permute-done | bytes 262176 | tf_op jit(solution)/shard_map/ppermute | solution.py:35
  43.5 10.0 %collective-permute-done.12.refs_3_ = bf16[128,1024]{1,0:T(8,128)(2,1)S(1)} collective-permute-done((bf16[128,1024]{1,0:T(8,128)(2,1)S(1)}, bf16[128,1024]{1,0:T(8,128)(2,1)S(1)}, u32[]{:S(2)}, u32[]{:S(2)}) %collective-permute-start.12) | collective-permute-done | bytes 262176 | tf_op jit(solution)/shard_map/ppermute | solution.py:35
  53.5 1.0 down_project.2.refs_6_
  55.5 1.6 collective-permute-start.15
  57.1 6.8 %collective-permute-done.15.arrived = bf16[128,1024]{1,0:T(8,128)(2,1)S(1)} collective-permute-done((bf16[128,1024]{1,0:T(8,128)(2,1)S(1)}, bf16[128,1024]{1,0:T(8,128)(2,1)S(1)}, u32[]{:S(2)}, u32[]{:S(2)}) %collective-permute-start.15) | collective-permute-done | bytes 262176 | tf_op jit(solution)/shard_map/ppermute | solution.py:31
  63.9 4.9 %all-gather.5.cloned.1.call-done = bf16[2048,512]{1,0:T(8,128)(2,1)} async-done(((bf16[256,512]{1,0:T(8,128)(2,1)}), bf16[2048,512]{1,0:T(8,128)(2,1)}) %all-gather.5.cloned.1.call-update) | async-done | bytes 2097168 | tf_op jit(solution)/shard_map/all_gather | solution.py:347
  69.0 1.3 slice_bitcast_fusion
  70.3 1.3 collective-permute-start.18
  71.5 1.8 collective-permute-start.17
  73.3 6.7 %expert.5 = (bf16[128,1024]{1,0:T(8,128)(2,1)S(1)}, bf16[128,1024]{1,0:T(8,128)(2,1)S(1)}) custom-call(s32[1]{0:T(128)} %bitcast.1.where, bf16[144,1024]{1,0:T(8,128)(2,1)S(1)} %finish_latent.1.refs_0_, bf16[144,1024]{1,0:T(8,128)(2,1)S(1)} %collective-permute-done.16.refs_1_, bf16[1024,256]{1,0:T(8,128)(2,1)S(1)} %get-tuple-element.166.refs_2_.refs_4_, ...), custom_call_target="tpu_custom_call" | custom-call | flops 3221225472 | bytes 1048576 | tf_op jit(solution)/shard_map/expert/pallas_call | solution.py:247
  80.1 7.0 %collective-permute-done.18.refs_1_ = bf16[144,1024]{1,0:T(8,128)(2,1)} collective-permute-done((bf16[144,1024]{1,0:T(8,128)(2,1)S(1)}, bf16[144,1024]{1,0:T(8,128)(2,1)}, u32[]{:S(2)}, u32[]{:S(2)}) %collective-permute-start.18) | collective-permute-done | bytes 294944 | tf_op jit(solution)/shard_map/ppermute | solution.py:35
  87.5 1.5 collective-permute-start.23
  89.8 1.0 copy-done.3
  90.7 11.4 %expert.6 = (bf16[128,1024]{1,0:T(8,128)(2,1)S(1)}, bf16[128,1024]{1,0:T(8,128)(2,1)S(1)}, bf16[256,1024]{1,0:T(8,128)(2,1)S(1)}) custom-call(s32[1]{0:T(128)} %bitcast.1.where, bf16[144,1024]{1,0:T(8,128)(2,1)S(1)} %collective-permute-done.17.refs_0_, bf16[144,1024]{1,0:T(8,128)(2,1)} %collective-permute-done.18.refs_1_, bf16[144,1024]{1,0:T(8,128)(2,1)S(1)} %copy-done.3, ...), custom_call_target="tpu_custom_call" | custom-call | flops 6442450944 | bytes 2097152 | tf_op jit(solution)/shard_map/expert/pallas_call | solution.py:247
  102.7 0.9 collective-permute-start.26
  103.6 1.1 collective-permute-start.27
  104.8 10.0 %expert.7 = (bf16[128,1024]{1,0:T(8,128)(2,1)S(1)}, bf16[128,1024]{1,0:T(8,128)(2,1)S(1)}, bf16[256,1024]{1,0:T(8,128)(2,1)S(1)}) custom-call(s32[1]{0:T(128)} %bitcast.1.where, bf16[144,1024]{1,0:T(8,128)(2,1)S(1)} %collective-permute-done.22.refs_0_, bf16[144,1024]{1,0:T(8,128)(2,1)S(1)} %collective-permute-done.23.refs_1_, ...), custom_call_target="tpu_custom_call" | custom-call | flops 6442450944 | bytes 2097152 | tf_op jit(solution)/shard_map/expert/pallas_call | solution.py:247
  114.8 3.2 %collective-permute-done.27.refs_0_ = bf16[144,1024]{1,0:T(8,128)(2,1)S(1)} collective-permute-done((bf16[144,1024]{1,0:T(8,128)(2,1)S(1)}, bf16[144,1024]{1,0:T(8,128)(2,1)S(1)}, u32[]{:S(2)}, u32[]{:S(2)}) %collective-permute-start.27) | collective-permute-done | bytes 294944 | tf_op jit(solution)/shard_map/ppermute | solution.py:35
  118.0 0.9 collective-permute-start.32
  120.0 1.0 collective-permute-start.31
  121.0 6.7 %expert.8 = (bf16[128,1024]{1,0:T(8,128)(2,1)S(1)}, bf16[128,1024]{1,0:T(8,128)(2,1)S(1)}) custom-call(s32[1]{0:T(128)} %bitcast.1.where, bf16[144,1024]{1,0:T(8,128)(2,1)S(1)} %collective-permute-done.27.refs_0_, bf16[144,1024]{1,0:T(8,128)(2,1)S(1)} %collective-permute-done.28.refs_1_, bf16[1024,256]{1,0:T(8,128)(2,1)S(1)} %get-tuple-element.166.refs_2_.refs_4_, ...), custom_call_target="tpu_custom_call" | custom-call | flops 3221225472 | bytes 1048576 | tf_op jit(solution)/shard_map/expert/pallas_call | solution.py:247
  127.8 5.2 %collective-permute-done.31 = bf16[128,1024]{1,0:T(8,128)(2,1)S(1)} collective-permute-done((bf16[128,1024]{1,0:T(8,128)(2,1)S(1)}, bf16[128,1024]{1,0:T(8,128)(2,1)S(1)}, u32[]{:S(2)}, u32[]{:S(2)}) %collective-permute-start.31) | collective-permute-done | bytes 262176 | tf_op jit(solution)/shard_map/ppermute | solution.py:35
  133.6 2.0 %collective-permute-start.37 = (bf16[128,1024]{1,0:T(8,128)(2,1)S(1)}, bf16[128,1024]{1,0:T(8,128)(2,1)S(1)}, u32[]{:S(2)}, u32[]{:S(2)}) collective-permute-start(bf16[128,1024]{1,0:T(8,128)(2,1)S(1)} %add_convert_fusion.6), channel_id=1, source_target_pairs={{0,2},{1,3},{2,0},{3,1},{4,6},{5,7},{6,4},{7,5},{8,10},{9,11},{10,... | collective-permute-start | bytes 786440 | tf_op jit(solution)/shard_map/ppermute | solution.py:35
  136.1 1.2 collective-permute-start.36
  137.3 10.3 %expert.9 = (bf16[128,1024]{1,0:T(8,128)(2,1)S(1)}, bf16[128,1024]{1,0:T(8,128)(2,1)S(1)}, bf16[256,1024]{1,0:T(8,128)(2,1)S(1)}) custom-call(s32[1]{0:T(128)} %bitcast.1.where, bf16[144,1024]{1,0:T(8,128)(2,1)S(1)} %collective-permute-done.26.refs_0_, bf16[144,1024]{1,0:T(8,128)(2,1)S(1)} %collective-permute-done.32.refs_1_, ...), custom_call_target="tpu_custom_call" | custom-call | flops 6442450944 | bytes 2097152 | tf_op jit(solution)/shard_map/expert/pallas_call | solution.py:247
  147.6 3.5 %collective-permute-done.38.refs_4_ = bf16[128,1024]{1,0:T(8,128)(2,1)S(1)} collective-permute-done((bf16[128,1024]{1,0:T(8,128)(2,1)S(1)}, bf16[128,1024]{1,0:T(8,128)(2,1)S(1)}, u32[]{:S(2)}, u32[]{:S(2)}) %collective-permute-start.38) | collective-permute-done | bytes 262176 | tf_op jit(solution)/shard_map/ppermute | solution.py:35
  151.1 1.9 %collective-permute-done.39 = bf16[256,1024]{1,0:T(8,128)(2,1)S(1)} collective-permute-done((bf16[256,1024]{1,0:T(8,128)(2,1)S(1)}, bf16[256,1024]{1,0:T(8,128)(2,1)S(1)}, u32[]{:S(2)}, u32[]{:S(2)}) %collective-permute-start.39) | collective-permute-done | bytes 524320 | tf_op jit(solution)/shard_map/ppermute | solution.py:27
  153.0 0.9 add_convert_fusion.1
  154.4 1.2 add_convert_fusion
  155.6 1.7 collective-permute-start.42
  157.3 0.9 collective-permute-start.40
  158.2 1.2 collective-permute-done.19.refs_1_
  159.4 7.3 %collective-permute-done.42.refs_6_ = bf16[128,1024]{1,0:T(8,128)(2,1)S(1)} collective-permute-done((bf16[128,1024]{1,0:T(8,128)(2,1)S(1)}, bf16[128,1024]{1,0:T(8,128)(2,1)S(1)}, u32[]{:S(2)}, u32[]{:S(2)}) %collective-permute-start.42) | collective-permute-done | bytes 262176 | tf_op jit(solution)/shard_map/ppermute | solution.py:35
  166.7 4.7 %collective-permute-done.41.refs_5_ = bf16[128,1024]{1,0:T(8,128)(2,1)S(1)} collective-permute-done((bf16[128,1024]{1,0:T(8,128)(2,1)}, bf16[128,1024]{1,0:T(8,128)(2,1)S(1)}, u32[]{:S(2)}, u32[]{:S(2)}) %collective-permute-start.41) | collective-permute-done | bytes 262176 | tf_op jit(solution)/shard_map/ppermute | solution.py:35
  171.4 4.7 %project.1 = bf16[128,4096]{1,0:T(8,128)(2,1)} custom-call(s32[1]{0:T(128)} %bitcast.where, bf16[128,1024]{1,0:T(8,128)(2,1)S(1)} %get-tuple-element.153.refs_0_, bf16[128,1024]{1,0:T(8,128)(2,1)S(1)} %collective-permute-done.19.refs_1_, bf16[128,1024]{1,0:T(8,128)(2,1)S(1)} %collective-permute-done.40.refs_2_, ...), custom_call_target="tpu_custom_call" | custom-call | flops 1073741824 | bytes 8388608 | tf_op jit(solution)/shard_map/project/pallas_call | solution.py:309
  (85 shorter events, 10.2 us)
Async XLA Ops:
  6.5 62.3 %all-gather.5.cloned.1.call-start = ((), (), s32[]{:S(2)}) async-start(), calls=%async_computation | async-start | bytes 2359296 | tf_op jit(solution)/shard_map/all_gather | solution.py:347
  8.5 145.4 %all-gather.7.cloned.1.call-start = ((), (), s32[]{:S(2)}) async-start(), calls=%async_computation.1 | async-start | bytes 6291456 | tf_op jit(solution)/shard_map/all_gather | solution.py:383
  9.6 14.1 %collective-permute-start = (bf16[128,1024]{1,0:T(8,128)(2,1)S(1)}, bf16[128,1024]{1,0:T(8,128)(2,1)S(1)}, u32[]{:S(2)}, u32[]{:S(2)}) collective-permute-start(bf16[128,1024]{1,0:T(8,128)(2,1)S(1)} %get-tuple-element.162.refs_2_), channel_id=1, source_target_pairs={{0,2},{1,3},{2,0},{3,1},{4,6},{5,7},{6,4},{7,5},{8,10},{9,11},{10,... | collective-permute-start | bytes 786440 | tf_op jit(solution)/shard_map/ppermute | solution.py:35
  12.7 21.3 %collective-permute-start.4 = (bf16[128,1024]{1,0:T(8,128)(2,1)S(1)}, bf16[128,1024]{1,0:T(8,128)(2,1)S(1)}, u32[]{:S(2)}, u32[]{:S(2)}) collective-permute-start(bf16[128,1024]{1,0:T(8,128)(2,1)S(1)} %get-tuple-element.162.refs_2_), channel_id=1, source_target_pairs={{0,1},{1,0},{2,3},{3,2},{4,5},{5,4},{6,7},{7,6},{8,9},{9,8},{10,11... | collective-permute-start | bytes 786440 | tf_op jit(solution)/shard_map/ppermute | solution.py:35
  14.3 18.8 %collective-permute-start.2 = (bf16[128,1024]{1,0:T(8,128)(2,1)S(1)}, bf16[128,1024]{1,0:T(8,128)(2,1)S(1)}, u32[]{:S(2)}, u32[]{:S(2)}) collective-permute-start(bf16[128,1024]{1,0:T(8,128)(2,1)S(1)} %get-tuple-element.162.refs_2_), channel_id=1, source_target_pairs={{0,4},{1,5},{2,6},{3,7},{4,0},{5,1},{6,2},{7,3},{8,12},{9,13},{10,... | collective-permute-start | bytes 786440 | tf_op jit(solution)/shard_map/ppermute | solution.py:35
  19.0 15.5 %collective-permute-start.5 = (bf16[128,2048]{1,0:T(8,128)(2,1)S(1)}, bf16[128,2048]{1,0:T(8,128)(2,1)S(1)}, u32[]{:S(2)}, u32[]{:S(2)}) collective-permute-start(bf16[128,2048]{1,0:T(8,128)(2,1)S(1)} %get-tuple-element.88), channel_id=1, source_target_pairs={{0,16},{16,0},{1,17},{17,1},{2,18},{18,2},{3,19},{19,3},{4,20},{20... | collective-permute-start | bytes 1572872 | tf_op jit(solution)/shard_map/ppermute | solution.py:31
  23.7 9.3 %collective-permute-start.1 = (bf16[128,1024]{1,0:T(8,128)(2,1)S(1)}, bf16[128,1024]{1,0:T(8,128)(2,1)S(1)}, u32[]{:S(2)}, u32[]{:S(2)}) collective-permute-start(bf16[128,1024]{1,0:T(8,128)(2,1)S(1)} %collective-permute-done.refs_6_), channel_id=1, source_target_pairs={{0,1},{1,0},{2,3},{3,2},{4,5},{5,4},{6,7},{7,6},{8,9},{9,8},{10,11... | collective-permute-start | bytes 786440 | tf_op jit(solution)/shard_map/ppermute | solution.py:35
  33.1 8.8 %collective-permute-start.3 = (bf16[128,1024]{1,0:T(8,128)(2,1)S(1)}, bf16[128,1024]{1,0:T(8,128)(2,1)S(1)}, u32[]{:S(2)}, u32[]{:S(2)}) collective-permute-start(bf16[128,1024]{1,0:T(8,128)(2,1)S(1)} %collective-permute-done.2.refs_10_), channel_id=1, source_target_pairs={{0,2},{1,3},{2,0},{3,1},{4,6},{5,7},{6,4},{7,5},{8,10},{9,11},{10,... | collective-permute-start | bytes 786440 | tf_op jit(solution)/shard_map/ppermute | solution.py:35
  34.0 8.5 %collective-permute-start.9 = (bf16[128,1024]{1,0:T(8,128)(2,1)S(1)}, bf16[128,1024]{1,0:T(8,128)(2,1)S(1)}, u32[]{:S(2)}, u32[]{:S(2)}) collective-permute-start(bf16[128,1024]{1,0:T(8,128)(2,1)S(1)} %collective-permute-done.2.refs_10_), channel_id=1, source_target_pairs={{0,1},{1,0},{2,3},{3,2},{4,5},{5,4},{6,7},{7,6},{8,9},{9,8},{10,11... | collective-permute-start | bytes 786440 | tf_op jit(solution)/shard_map/ppermute | solution.py:35
  34.0 9.0 %collective-permute-start.7 = (bf16[128,1024]{1,0:T(8,128)(2,1)S(1)}, bf16[128,1024]{1,0:T(8,128)(2,1)S(1)}, u32[]{:S(2)}, u32[]{:S(2)}) collective-permute-start(bf16[128,1024]{1,0:T(8,128)(2,1)S(1)} %collective-permute-done.refs_6_), channel_id=1, source_target_pairs={{0,8},{8,0},{1,9},{9,1},{2,10},{10,2},{3,11},{11,3},{4,12},{12,4},... | collective-permute-start | bytes 786440 | tf_op jit(solution)/shard_map/ppermute | solution.py:27
  34.0 9.1 %collective-permute-start.8 = (bf16[128,1024]{1,0:T(8,128)(2,1)S(1)}, bf16[128,1024]{1,0:T(8,128)(2,1)S(1)}, u32[]{:S(2)}, u32[]{:S(2)}) collective-permute-start(bf16[128,1024]{1,0:T(8,128)(2,1)S(1)} %collective-permute-done.1.refs_7_), channel_id=1, source_target_pairs={{0,8},{8,0},{1,9},{9,1},{2,10},{10,2},{3,11},{11,3},{4,12},{12,4},... | collective-permute-start | bytes 786440 | tf_op jit(solution)/shard_map/ppermute | solution.py:27
  41.8 11.7 %collective-permute-start.12 = (bf16[128,1024]{1,0:T(8,128)(2,1)S(1)}, bf16[128,1024]{1,0:T(8,128)(2,1)S(1)}, u32[]{:S(2)}, u32[]{:S(2)}) collective-permute-start(bf16[128,1024]{1,0:T(8,128)(2,1)S(1)} %collective-permute-done.3.refs_2_), channel_id=1, source_target_pairs={{0,1},{1,0},{2,3},{3,2},{4,5},{5,4},{6,7},{7,6},{8,9},{9,8},{10,11... | collective-permute-start | bytes 786440 | tf_op jit(solution)/shard_map/ppermute | solution.py:35
  42.5 11.0 %collective-permute-start.10 = (bf16[128,1024]{1,0:T(8,128)(2,1)S(1)}, bf16[128,1024]{1,0:T(8,128)(2,1)S(1)}, u32[]{:S(2)}, u32[]{:S(2)}) collective-permute-start(bf16[128,1024]{1,0:T(8,128)(2,1)S(1)} %collective-permute-done.2.refs_10_), channel_id=1, source_target_pairs={{0,8},{8,0},{1,9},{9,1},{2,10},{10,2},{3,11},{11,3},{4,12},{12,4},... | collective-permute-start | bytes 786440 | tf_op jit(solution)/shard_map/ppermute | solution.py:27
  42.5 11.0 %collective-permute-start.11 = (bf16[128,1024]{1,0:T(8,128)(2,1)S(1)}, bf16[128,1024]{1,0:T(8,128)(2,1)S(1)}, u32[]{:S(2)}, u32[]{:S(2)}) collective-permute-start(bf16[128,1024]{1,0:T(8,128)(2,1)S(1)} %collective-permute-done.9.refs_11_), channel_id=1, source_target_pairs={{0,8},{8,0},{1,9},{9,1},{2,10},{10,2},{3,11},{11,3},{4,12},{12,4},... | collective-permute-start | bytes 786440 | tf_op jit(solution)/shard_map/ppermute | solution.py:27
  43.0 10.5 %collective-permute-start.6 = (bf16[128,1024]{1,0:T(8,128)(2,1)S(1)}, bf16[128,1024]{1,0:T(8,128)(2,1)S(1)}, u32[]{:S(2)}, u32[]{:S(2)}) collective-permute-start(bf16[128,1024]{1,0:T(8,128)(2,1)S(1)} %collective-permute-done.4.refs_3_), channel_id=1, source_target_pairs={{0,8},{8,0},{1,9},{9,1},{2,10},{10,2},{3,11},{11,3},{4,12},{12,4},... | collective-permute-start | bytes 786440 | tf_op jit(solution)/shard_map/ppermute | solution.py:27
  43.1 11.4 %collective-permute-start.13 = (bf16[128,1024]{1,0:T(8,128)(2,1)S(1)}, bf16[128,1024]{1,0:T(8,128)(2,1)S(1)}, u32[]{:S(2)}, u32[]{:S(2)}) collective-permute-start(bf16[128,1024]{1,0:T(8,128)(2,1)S(1)} %collective-permute-done.3.refs_2_), channel_id=1, source_target_pairs={{0,8},{8,0},{1,9},{9,1},{2,10},{10,2},{3,11},{11,3},{4,12},{12,4},... | collective-permute-start | bytes 786440 | tf_op jit(solution)/shard_map/ppermute | solution.py:27
  53.5 1.5 collective-permute-start.14
  55.5 8.4 %collective-permute-start.15 = (bf16[128,1024]{1,0:T(8,128)(2,1)S(1)}, bf16[128,1024]{1,0:T(8,128)(2,1)S(1)}, u32[]{:S(2)}, u32[]{:S(2)}) collective-permute-start(bf16[128,1024]{1,0:T(8,128)(2,1)S(1)} %get-tuple-element.95), channel_id=1, source_target_pairs={{0,16},{16,0},{1,17},{17,1},{2,18},{18,2},{3,19},{19,3},{4,20},{20... | collective-permute-start | bytes 786440 | tf_op jit(solution)/shard_map/ppermute | solution.py:31
  68.9 4.5 %collective-permute-start.16 = (bf16[144,1024]{1,0:T(8,128)(2,1)S(1)}, bf16[144,1024]{1,0:T(8,128)(2,1)S(1)}, u32[]{:S(2)}, u32[]{:S(2)}) collective-permute-start(bf16[144,1024]{1,0:T(8,128)(2,1)S(1)} %finish_latent.1.refs_0_), channel_id=1, source_target_pairs={{0,8},{8,0},{1,9},{9,1},{2,10},{10,2},{3,11},{11,3},{4,12},{12,4},... | collective-permute-start | bytes 884744 | tf_op jit(solution)/shard_map/ppermute | solution.py:27
  70.3 16.8 %collective-permute-start.18 = (bf16[144,1024]{1,0:T(8,128)(2,1)S(1)}, bf16[144,1024]{1,0:T(8,128)(2,1)}, u32[]{:S(2)}, u32[]{:S(2)}) collective-permute-start(bf16[144,1024]{1,0:T(8,128)(2,1)S(1)} %finish_latent.1.refs_0_), channel_id=1, source_target_pairs={{0,4},{1,5},{2,6},{3,7},{4,0},{5,1},{6,2},{7,3},{8,12},{9,13},{10,... | collective-permute-start | bytes 884744 | tf_op jit(solution)/shard_map/ppermute | solution.py:35
  71.5 15.5 %collective-permute-start.17 = (bf16[144,1024]{1,0:T(8,128)(2,1)S(1)}, bf16[144,1024]{1,0:T(8,128)(2,1)S(1)}, u32[]{:S(2)}, u32[]{:S(2)}) collective-permute-start(bf16[144,1024]{1,0:T(8,128)(2,1)S(1)} %finish_latent.1.refs_0_), channel_id=1, source_target_pairs={{0,2},{1,3},{2,0},{3,1},{4,6},{5,7},{6,4},{7,5},{8,10},{9,11},{10,... | collective-permute-start | bytes 884744 | tf_op jit(solution)/shard_map/ppermute | solution.py:35
  80.0 22.1 %copy-start.4 = (bf16[128,1024]{1,0:T(8,128)(2,1)}, bf16[128,1024]{1,0:T(8,128)(2,1)S(1)}, u32[]{:S(2)}) copy-start(bf16[128,1024]{1,0:T(8,128)(2,1)S(1)} %get-tuple-element.103) | copy-start | bytes 786436
  87.0 2.0 %collective-permute-start.20 = (bf16[144,1024]{1,0:T(8,128)(2,1)S(1)}, bf16[144,1024]{1,0:T(8,128)(2,1)S(1)}, u32[]{:S(2)}, u32[]{:S(2)}) collective-permute-start(bf16[144,1024]{1,0:T(8,128)(2,1)S(1)} %collective-permute-done.17.refs_0_), channel_id=1, source_target_pairs={{0,8},{8,0},{1,9},{9,1},{2,10},{10,2},{3,11},{11,3},{4,12},{12,4},... | collective-permute-start | bytes 884744 | tf_op jit(solution)/shard_map/ppermute | solution.py:27
  87.0 2.8 %collective-permute-start.21 = (bf16[144,1024]{1,0:T(8,128)(2,1)}, bf16[144,1024]{1,0:T(8,128)(2,1)}, u32[]{:S(2)}, u32[]{:S(2)}) collective-permute-start(bf16[144,1024]{1,0:T(8,128)(2,1)} %collective-permute-done.18.refs_1_), channel_id=1, source_target_pairs={{0,8},{8,0},{1,9},{9,1},{2,10},{10,2},{3,11},{11,3},{4,12},{12,4},... | collective-permute-start | bytes 884744 | tf_op jit(solution)/shard_map/ppermute | solution.py:27
  87.5 14.6 %collective-permute-start.23 = (bf16[144,1024]{1,0:T(8,128)(2,1)}, bf16[144,1024]{1,0:T(8,128)(2,1)S(1)}, u32[]{:S(2)}, u32[]{:S(2)}) collective-permute-start(bf16[144,1024]{1,0:T(8,128)(2,1)} %collective-permute-done.18.refs_1_), channel_id=1, source_target_pairs={{0,1},{1,0},{2,3},{3,2},{4,5},{5,4},{6,7},{7,6},{8,9},{9,8},{10,11... | collective-permute-start | bytes 884744 | tf_op jit(solution)/shard_map/ppermute | solution.py:35
  89.1 13.1 %collective-permute-start.22 = (bf16[144,1024]{1,0:T(8,128)(2,1)}, bf16[144,1024]{1,0:T(8,128)(2,1)S(1)}, u32[]{:S(2)}, u32[]{:S(2)}) collective-permute-start(bf16[144,1024]{1,0:T(8,128)(2,1)} %collective-permute-done.18.refs_1_), channel_id=1, source_target_pairs={{0,2},{1,3},{2,0},{3,1},{4,6},{5,7},{6,4},{7,5},{8,10},{9,11},{10,... | collective-permute-start | bytes 884744 | tf_op jit(solution)/shard_map/ppermute | solution.py:35
  102.1 2.6 %collective-permute-start.25 = (bf16[144,1024]{1,0:T(8,128)(2,1)S(1)}, bf16[144,1024]{1,0:T(8,128)(2,1)S(1)}, u32[]{:S(2)}, u32[]{:S(2)}) collective-permute-start(bf16[144,1024]{1,0:T(8,128)(2,1)S(1)} %collective-permute-done.23.refs_1_), channel_id=1, source_target_pairs={{0,8},{8,0},{1,9},{9,1},{2,10},{10,2},{3,11},{11,3},{4,12},{12,4},... | collective-permute-start | bytes 884744 | tf_op jit(solution)/shard_map/ppermute | solution.py:27
  102.3 2.5 %collective-permute-start.24 = (bf16[144,1024]{1,0:T(8,128)(2,1)S(1)}, bf16[144,1024]{1,0:T(8,128)(2,1)S(1)}, u32[]{:S(2)}, u32[]{:S(2)}) collective-permute-start(bf16[144,1024]{1,0:T(8,128)(2,1)S(1)} %collective-permute-done.22.refs_0_), channel_id=1, source_target_pairs={{0,8},{8,0},{1,9},{9,1},{2,10},{10,2},{3,11},{11,3},{4,12},{12,4},... | collective-permute-start | bytes 884744 | tf_op jit(solution)/shard_map/ppermute | solution.py:27
  102.7 12.1 %collective-permute-start.26 = (bf16[144,1024]{1,0:T(8,128)(2,1)S(1)}, bf16[144,1024]{1,0:T(8,128)(2,1)S(1)}, u32[]{:S(2)}, u32[]{:S(2)}) collective-permute-start(bf16[144,1024]{1,0:T(8,128)(2,1)S(1)} %finish_latent.1.refs_0_), channel_id=1, source_target_pairs={{0,1},{1,0},{2,3},{3,2},{4,5},{5,4},{6,7},{7,6},{8,9},{9,8},{10,11... | collective-permute-start | bytes 884744 | tf_op jit(solution)/shard_map/ppermute | solution.py:35
  103.6 14.4 %collective-permute-start.27 = (bf16[144,1024]{1,0:T(8,128)(2,1)S(1)}, bf16[144,1024]{1,0:T(8,128)(2,1)S(1)}, u32[]{:S(2)}, u32[]{:S(2)}) collective-permute-start(bf16[144,1024]{1,0:T(8,128)(2,1)S(1)} %collective-permute-done.22.refs_0_), channel_id=1, source_target_pairs={{0,1},{1,0},{2,3},{3,2},{4,5},{5,4},{6,7},{7,6},{8,9},{9,8},{10,11... | collective-permute-start | bytes 884744 | tf_op jit(solution)/shard_map/ppermute | solution.py:35
  104.7 14.4 %collective-permute-start.29 = (bf16[256,1024]{1,0:T(8,128)(2,1)S(1)}, bf16[256,1024]{1,0:T(8,128)(2,1)S(1)}, u32[]{:S(2)}, u32[]{:S(2)}) collective-permute-start(bf16[256,1024]{1,0:T(8,128)(2,1)S(1)} %get-tuple-element.125), channel_id=1, source_target_pairs={{0,8},{8,0},{1,9},{9,1},{2,10},{10,2},{3,11},{11,3},{4,12},{12,4},... | collective-permute-start | bytes 1572872 | tf_op jit(solution)/shard_map/ppermute | solution.py:27
  118.0 1.9 %collective-permute-start.30 = (bf16[256,1024]{1,0:T(8,128)(2,1)S(1)}, bf16[256,1024]{1,0:T(8,128)(2,1)S(1)}, u32[]{:S(2)}, u32[]{:S(2)}) collective-permute-start(bf16[256,1024]{1,0:T(8,128)(2,1)S(1)} %get-tuple-element.127), channel_id=1, source_target_pairs={{0,8},{8,0},{1,9},{9,1},{2,10},{10,2},{3,11},{11,3},{4,12},{12,4},... | collective-permute-start | bytes 1572872 | tf_op jit(solution)/shard_map/ppermute | solution.py:27
  118.0 9.8 %collective-permute-start.32 = (bf16[144,1024]{1,0:T(8,128)(2,1)S(1)}, bf16[144,1024]{1,0:T(8,128)(2,1)S(1)}, u32[]{:S(2)}, u32[]{:S(2)}) collective-permute-start(bf16[144,1024]{1,0:T(8,128)(2,1)S(1)} %collective-permute-done.17.refs_0_), channel_id=1, source_target_pairs={{0,1},{1,0},{2,3},{3,2},{4,5},{5,4},{6,7},{7,6},{8,9},{9,8},{10,11... | collective-permute-start | bytes 884744 | tf_op jit(solution)/shard_map/ppermute | solution.py:35
  118.9 2.1 %collective-permute-start.28 = (bf16[144,1024]{1,0:T(8,128)(2,1)S(1)}, bf16[144,1024]{1,0:T(8,128)(2,1)S(1)}, u32[]{:S(2)}, u32[]{:S(2)}) collective-permute-start(bf16[144,1024]{1,0:T(8,128)(2,1)S(1)} %collective-permute-done.27.refs_0_), channel_id=1, source_target_pairs={{0,8},{8,0},{1,9},{9,1},{2,10},{10,2},{3,11},{11,3},{4,12},{12,4},... | collective-permute-start | bytes 884744 | tf_op jit(solution)/shard_map/ppermute | solution.py:27
  120.0 13.1 %collective-permute-start.31 = (bf16[128,1024]{1,0:T(8,128)(2,1)S(1)}, bf16[128,1024]{1,0:T(8,128)(2,1)S(1)}, u32[]{:S(2)}, u32[]{:S(2)}) collective-permute-start(bf16[128,1024]{1,0:T(8,128)(2,1)S(1)} %add_convert_fusion.5), channel_id=1, source_target_pairs={{0,1},{1,0},{2,3},{3,2},{4,5},{5,4},{6,7},{7,6},{8,9},{9,8},{10,11... | collective-permute-start | bytes 786440 | tf_op jit(solution)/shard_map/ppermute | solution.py:35
  133.1 3.0 %collective-permute-start.35 = (bf16[128,1024]{1,0:T(8,128)(2,1)S(1)}, bf16[128,1024]{1,0:T(8,128)(2,1)S(1)}, u32[]{:S(2)}, u32[]{:S(2)}) collective-permute-start(bf16[128,1024]{1,0:T(8,128)(2,1)S(1)} %get-tuple-element.134), channel_id=1, source_target_pairs={{0,8},{8,0},{1,9},{9,1},{2,10},{10,2},{3,11},{11,3},{4,12},{12,4},... | collective-permute-start | bytes 786440 | tf_op jit(solution)/shard_map/ppermute | solution.py:27
  133.1 4.2 %collective-permute-start.33 = (bf16[144,1024]{1,0:T(8,128)(2,1)S(1)}, bf16[144,1024]{1,0:T(8,128)(2,1)S(1)}, u32[]{:S(2)}, u32[]{:S(2)}) collective-permute-start(bf16[144,1024]{1,0:T(8,128)(2,1)S(1)} %collective-permute-done.26.refs_0_), channel_id=1, source_target_pairs={{0,8},{8,0},{1,9},{9,1},{2,10},{10,2},{3,11},{11,3},{4,12},{12,4},... | collective-permute-start | bytes 884744 | tf_op jit(solution)/shard_map/ppermute | solution.py:27
  133.6 14.0 %collective-permute-start.37 = (bf16[128,1024]{1,0:T(8,128)(2,1)S(1)}, bf16[128,1024]{1,0:T(8,128)(2,1)S(1)}, u32[]{:S(2)}, u32[]{:S(2)}) collective-permute-start(bf16[128,1024]{1,0:T(8,128)(2,1)S(1)} %add_convert_fusion.6), channel_id=1, source_target_pairs={{0,2},{1,3},{2,0},{3,1},{4,6},{5,7},{6,4},{7,5},{8,10},{9,11},{10,... | collective-permute-start | bytes 786440 | tf_op jit(solution)/shard_map/ppermute | solution.py:35
  135.6 1.7 collective-permute-start.34
  135.7 15.3 %collective-permute-start.38 = (bf16[128,1024]{1,0:T(8,128)(2,1)S(1)}, bf16[128,1024]{1,0:T(8,128)(2,1)S(1)}, u32[]{:S(2)}, u32[]{:S(2)}) collective-permute-start(bf16[128,1024]{1,0:T(8,128)(2,1)S(1)} %add_convert_fusion.3), channel_id=1, source_target_pairs={{0,4},{1,5},{2,6},{3,7},{4,0},{5,1},{6,2},{7,3},{8,12},{9,13},{10,... | collective-permute-start | bytes 786440 | tf_op jit(solution)/shard_map/ppermute | solution.py:35
  136.1 18.0 %copy-start.5 = (bf16[128,1024]{1,0:T(8,128)(2,1)S(1)}, bf16[128,1024]{1,0:T(8,128)(2,1)}, u32[]{:S(2)}) copy-start(bf16[128,1024]{1,0:T(8,128)(2,1)} %copy-done.4) | copy-start | bytes 786436
  136.1 15.0 %collective-permute-start.36 = (bf16[128,1024]{1,0:T(8,128)(2,1)S(1)}, bf16[128,1024]{1,0:T(8,128)(2,1)S(1)}, u32[]{:S(2)}, u32[]{:S(2)}) collective-permute-start(bf16[128,1024]{1,0:T(8,128)(2,1)S(1)} %add_convert_fusion.4), channel_id=1, source_target_pairs={{0,1},{1,0},{2,3},{3,2},{4,5},{5,4},{6,7},{7,6},{8,9},{9,8},{10,11... | collective-permute-start | bytes 786440 | tf_op jit(solution)/shard_map/ppermute | solution.py:35
  151.1 1.9 %collective-permute-start.39 = (bf16[256,1024]{1,0:T(8,128)(2,1)S(1)}, bf16[256,1024]{1,0:T(8,128)(2,1)S(1)}, u32[]{:S(2)}, u32[]{:S(2)}) collective-permute-start(bf16[256,1024]{1,0:T(8,128)(2,1)S(1)} %get-tuple-element.145), channel_id=1, source_target_pairs={{0,8},{8,0},{1,9},{9,1},{2,10},{10,2},{3,11},{11,3},{4,12},{12,4},... | collective-permute-start | bytes 1572872 | tf_op jit(solution)/shard_map/ppermute | solution.py:27
  153.9 17.5 %collective-permute-start.43 = (bf16[2,8,256,512]{3,2,1,0:T(8,128)(2,1)}, bf16[2,8,256,512]{3,2,1,0:T(8,128)(2,1)S(1)}, u32[]{:S(2)}, u32[]{:S(2)}) collective-permute-start(bf16[2,8,256,512]{3,2,1,0:T(8,128)(2,1)} %bitcast.10), channel_id=1, source_target_pairs={{0,8},{8,0},{1,9},{9,1},{2,10},{10,2},{3,11},{11,3},{4,12},{12,4},... | collective-permute-start | bytes 12582920 | tf_op jit(solution)/shard_map/ppermute | solution.py:27
  154.0 5.3 %collective-permute-start.19 = (bf16[128,1024]{1,0:T(8,128)(2,1)S(1)}, bf16[128,1024]{1,0:T(8,128)(2,1)S(1)}, u32[]{:S(2)}, u32[]{:S(2)}) collective-permute-start(bf16[128,1024]{1,0:T(8,128)(2,1)S(1)} %copy-done.5), channel_id=1, source_target_pairs={{0,8},{8,0},{1,9},{9,1},{2,10},{10,2},{3,11},{11,3},{4,12},{12,4},... | collective-permute-start | bytes 786440 | tf_op jit(solution)/shard_map/ppermute | solution.py:27
  155.6 11.1 %collective-permute-start.42 = (bf16[128,1024]{1,0:T(8,128)(2,1)S(1)}, bf16[128,1024]{1,0:T(8,128)(2,1)S(1)}, u32[]{:S(2)}, u32[]{:S(2)}) collective-permute-start(bf16[128,1024]{1,0:T(8,128)(2,1)S(1)} %add_convert_fusion), channel_id=1, source_target_pairs={{0,6},{1,7},{2,4},{3,5},{4,2},{5,3},{6,0},{7,1},{8,14},{9,15},{10,... | collective-permute-start | bytes 786440 | tf_op jit(solution)/shard_map/ppermute | solution.py:35
  157.3 14.1 %collective-permute-start.41 = (bf16[128,1024]{1,0:T(8,128)(2,1)}, bf16[128,1024]{1,0:T(8,128)(2,1)S(1)}, u32[]{:S(2)}, u32[]{:S(2)}) collective-permute-start(bf16[128,1024]{1,0:T(8,128)(2,1)} %get-tuple-element.163), channel_id=1, source_target_pairs={{0,3},{1,2},{2,1},{3,0},{4,7},{5,6},{6,5},{7,4},{8,11},{9,10},{10,... | collective-permute-start | bytes 786440 | tf_op jit(solution)/shard_map/ppermute | solution.py:35
  157.3 14.1 %collective-permute-start.40 = (bf16[128,1024]{1,0:T(8,128)(2,1)S(1)}, bf16[128,1024]{1,0:T(8,128)(2,1)S(1)}, u32[]{:S(2)}, u32[]{:S(2)}) collective-permute-start(bf16[128,1024]{1,0:T(8,128)(2,1)S(1)} %get-tuple-element.164), channel_id=1, source_target_pairs={{0,1},{1,0},{2,3},{3,2},{4,5},{5,4},{6,7},{7,6},{8,9},{9,8},{10,11... | collective-permute-start | bytes 786440 | tf_op jit(solution)/shard_map/ppermute | solution.py:35
  (6 other events, 7.1 us)
Sparse Core Ops, SparseCore 0:
  9.5 59.2 all-gather.4
  87.7 56.0 all-gather.6

commit v8 on v7

--- a/solution.py
+++ b/solution.py
@@ -155,10 +155,10 @@
 
 def expert_kernel(positions, count, where, *refs):
     pieces = refs[: 2 * positions]
-    gate_first, up_first, gate, up, out = refs[2 * positions : 2 * positions + 5]
-    own_sums, refs = refs[2 * positions + 5 : 3 * positions + 5], refs[3 * positions + 5 :]
+    gate, up, out = refs[2 * positions : 2 * positions + 3]
+    own_sums, refs = refs[2 * positions + 3 : 3 * positions + 3], refs[3 * positions + 3 :]
     other_sums, rows, hidden, held, gate_block, up_block, out_block, sems = refs
-    width = gate_first.shape[1]
+    width = 256
     blocks = gate.shape[2] // width
 
     def columns_at(start):
@@ -171,7 +171,7 @@
             source.at[0, :, columns], target.at[:, columns], sems.at[part * blocks + i]
         )
 
-    for i in range(1, blocks):
+    for i in range(blocks):
         read(i, 0).start()
         read(i, 1).start()
     for i in range(out.shape[2] // width):
@@ -193,18 +193,19 @@
         read(i, 0).wait()
         read(i, 1).wait()
 
-    def dots(*blocks):
-        return [jnp.dot(rows[...], b, preferred_element_type=jnp.float32) for b in blocks]
-
     def products(i):
         columns = columns_at(i * width)
-        return dots(gate_block[:, columns], up_block[:, columns])
+        return [
+            jnp.dot(rows[...], block[:, columns], preferred_element_type=jnp.float32)
+            for block in (gate_block, up_block)
+        ]
 
     def activate(gate_value, up_value, i):
         value = gate_value / (1.0 + jnp.exp(-gate_value)) * up_value
         hidden[:, columns_at(i * width)] = value.astype(jnp.bfloat16)
 
-    held[0], held[1] = dots(gate_first[...], up_first[...])
+    arrive(0)
+    held[0], held[1] = products(0)
 
     def step(i, carry):
         arrive(2 * i + 1)
@@ -237,17 +238,17 @@
     lax.fori_loop(0, out.shape[2] // width, finish, 0)
 
 
-def expert_apply(expert, owns, others, firsts, weights, count):
+def expert_apply(expert, owns, others, weights, count):
     positions = len(owns)
     latent_width = owns[0].shape[1]
     hidden_width = weights[0].shape[2]
-    rows, width = 2 * positions * count, firsts[0].shape[1]
+    rows, width = 2 * positions * count, 256
     own_sum = jax.ShapeDtypeStruct((count, latent_width), jnp.bfloat16)
     other_sums = jax.ShapeDtypeStruct((positions * count, latent_width), jnp.bfloat16)
     return pl.pallas_call(
         functools.partial(expert_kernel, positions, count),
         out_shape=(own_sum,) * positions + (other_sums,),
-        in_specs=[in_smem] + [in_vmem] * (2 * positions + 2) + [in_hbm] * 3,
+        in_specs=[in_smem] + [in_vmem] * (2 * positions) + [in_hbm] * 3,
         out_specs=(in_vmem,) * (positions + 1),
         scratch_shapes=[
             pltpu.VMEM((rows, latent_width), jnp.bfloat16),
@@ -258,12 +259,12 @@
         + [pltpu.SemaphoreType.DMA(((2 * hidden_width + latent_width) // width,))],
         compiler_params=pltpu.CompilerParams(vmem_limit_bytes=28 * mebi),
         cost_estimate=pl.CostEstimate(
-            flops=6 * rows * latent_width * hidden_width,
+            flops=3 * rows * latent_width * hidden_width // 2,
             bytes_accessed=4 * rows * latent_width,
-            transcendentals=rows * hidden_width,
+            transcendentals=0,
         ),
         name="expert",
-    )(expert, *owns, *others, *firsts, *weights)
+    )(expert, *owns, *others, *weights)
 
 
 def project_kernel(where, *refs):
@@ -342,10 +343,6 @@
     steps = ep_count // 2
     last = steps - 1
 
-    inner = latent_width // 4
-    up_piece = lax.dynamic_slice_in_dim(up_latent, own_quarter * inner, inner, 0)
-    mine = lax.all_gather(up_piece, "ep", axis=0)
-
     quarter = down_latent.shape[0] // 4
 
     def own_piece(core):
@@ -357,6 +354,10 @@
     far = {0: swap_ep(near[0], 1)}
     near[1], kept = join(near[1], kept)
     far[1] = swap_ep(near[1], 1)
+
+    inner = latent_width // 4
+    up_piece = lax.dynamic_slice_in_dim(up_latent, own_quarter * inner, inner, 0)
+    mine = lax.all_gather(up_piece, "ep", axis=0)
     weights = dense_weights(after(expert_ids, near[1]), route_scores, expert_count)
     others = {k: near[k] for k in near if k > 1}
     far[1], weights, *arrived = join(far[1], weights, *others.values())
@@ -376,102 +377,67 @@
     (partial,) = down_project(early, kept, taken, [b for k in early for b in blocks[k]])
     late = [after(blocks[-1][0], partial), *blocks[-1][1:]]
     own_part, sent_part = down_project([last], kept, taken, late, partial)
-    arrived, mine = join(swap_reps(sent_part), mine)
-    latent = finish_latent(own_part, arrived, weights.astype(jnp.bfloat16))
-
-    sides = [[i, i + 1] for i in range(0, lax.axis_size("rep"), 2)]
-    both_sides = lax.all_gather(mine, "rep", axis=0, axis_index_groups=sides)
+    latent = finish_latent(own_part, swap_reps(sent_part), weights.astype(jnp.bfloat16))
 
     expert = (group * ep_count + place).astype(jnp.int32).reshape(1)
-    firsts = [w[0, :, :256] for w in (gate_weight, up_weight)]
     expert_weights = [
         pltpu.with_memory_space_constraint(w, pltpu.HBM)
         for w in (gate_weight, up_weight, out_weight)
     ]
     near = first_steps(latent, steps)
-    far, away, sent, pairs, own_sums, swapped = {}, {}, {}, {}, {}, {}
-
-    def run(which, coming, *waits):
-        owns = [(near, far)[y][k] for k, y in which]
-        operands = owns + [swap_cores(own) for own in owns]
-        operands = join(*operands, *waits)[: len(operands)]
-        count = len(which)
-        sums = expert_apply(
-            expert,
-            operands[:count],
-            operands[count:],
-            firsts,
-            expert_weights,
-            token_count,
-        )
-        names = [(table, key) for table, keys in coming for key in keys]
-        sums = join(*sums, *[table[key] for table, key in names])
-        for (table, key), value in zip(names, sums[count + 1 :]):
-            table[key] = value
-        others = swap_cores(sums[count])
-        for i, place_of in enumerate(which):
-            own_sums[place_of] = sums[i]
-            swapped[place_of] = others[i * token_count : (i + 1) * token_count]
-        return sums[0]
-
-    def chip_sum(k, y):
-        return own_sums[k, y].astype(jnp.float32) + swapped[k, y].astype(jnp.float32)
-
-    def send_far(k):
-        sent[k] = chip_sum(k, 1).astype(jnp.bfloat16)
-        away[k] = swap_ep(sent[k], 1)
-
-    def pair_sum(k):
-        pairs[k] = (chip_sum(k, 0) + away[k].astype(jnp.float32)).astype(jnp.bfloat16)
+    far = {0: swap_ep(latent, 1)}
+    sums, travel, taken_in = {}, {"up": mine}, set()
 
     def start_near(k):
         near[k] = swap_ep(near[k ^ (k & -k)], 2 * (k & -k))
+        return near, k
 
     def start_far(k):
         far[k] = swap_ep(near[k], 1)
-
-    powers = [k for k in near if k]
-    run([(0, 0)], [(near, powers)])
-    if last >= 3:
-        start_near(3)
-    start_far(2)
-    run([(1, 0), (2, 0)], [(near, [3] if last >= 3 else []), (far, [2])])
-    returning = []
-    for k in range(3, steps):
-        start_far(k)
-        if k == 3:
-            start_far(0)
-        coming = [(far, [0, k] if k == 3 else [k]), (away, returning)]
-        if k + 1 < steps and k + 1 not in near:
-            start_near(k + 1)
-            coming.append((near, [k + 1]))
-        run([(k, 0), (k - 1, 1)], coming, *pairs.values())
-        for j in returning:
-            pair_sum(j)
-        send_far(k - 1)
-        returning = [k - 1]
-    start_far(1)
-    near_home = chip_sum(1, 0).astype(jnp.bfloat16)
-    run([(last, 1)], [(away, returning), (far, [1])], near_home, *sent.values(), *pairs.values())
-    for j in returning:
-        pair_sum(j)
-    send_far(last)
-    homeward = {("near", 1): swap_ep(near_home, 2)}
-    for k in range(2, last):
-        homeward["pair", k] = swap_ep(pairs[k], 2 * k)
+        return far, k
+
+    def send(name, value, mask):
+        travel[name] = swap_ep(value.astype(jnp.bfloat16), mask)
+        return travel, name
+
+    def run(which, *coming):
+        owns = [(near, far)[y][k] for k, y in which]
+        operands = join(*owns, *[swap_cores(own) for own in owns])
+        count = len(which)
+        out = expert_apply(expert, operands[:count], operands[count:], expert_weights, token_count)
+        out = join(*out, *[table[key] for table, key in coming])
+        for (table, key), value in zip(coming, out[count + 1 :]):
+            table[key] = value
+        from_core = swap_cores(out[count])
+        for i, place_of in enumerate(which):
+            swapped = from_core[i * token_count : (i + 1) * token_count]
+            sums[place_of] = out[i].astype(jnp.float32) + swapped.astype(jnp.float32)
+
+    run([(0, 0)], (near, 1), (far, 0), (travel, "up"))
+    sides = [[i, i + 1] for i in range(0, lax.axis_size("rep"), 2)]
+    both_sides = lax.all_gather(travel.pop("up"), "rep", axis=0, axis_index_groups=sides)
+    run([(1, 0), (0, 1)], *[(near, k) for k in near if k > 1], start_far(1))
+    for k in range(2, steps):
+        coming = [start_far(k)]
+        for j in range(3, steps):
+            if j not in near and j ^ (j & -j) == k:
+                coming.append(start_near(j))
+        previous = [(k - 2, 1)] if k == last else [(k - 2, 1), (k - 1, 0)]
+        coming += [send(p, sums[p], 2 * p[0] + p[1]) for p in previous]
+        run([(k, 0), (k - 1, 1)], *coming)
     run(
-        [(0, 1), (1, 1)],
-        [(away, [last]), (homeward, list(homeward))],
-        sent[last],
-        *pairs.values(),
+        [(last, 1)],
+        send((last - 1, 1), sums[last - 1, 1], 1),
+        send((last, 0), sums[last, 0], 2),
     )
-    pair_sum(last)
-    send_far(0)
-    homeward["far", 1] = swap_ep(chip_sum(1, 1).astype(jnp.bfloat16), 3)
-    homeward["pair", last] = swap_ep(pairs[last], 2 * last)
-    both_sides = after(both_sides, sent[0])
-    terms = [own_sums[0, 0], swapped[0, 0], away[0], *homeward.values()]
-    *terms, swapped_sides = join(*terms, swap_cores(both_sides))
+    shared = sums[last - 1, 0]
+    for name in ((last - 1, 1), (last, 0)):
+        shared += travel.pop(name).astype(jnp.float32)
+    send("shared", shared, 2 * last - 2)
+    final = sums[last, 1].astype(jnp.bfloat16)
+    both_sides = after(both_sides, final)
+    send((last, 1), final, 2 * last + 1)
+    *terms, swapped_sides = join(sums[0, 0], *travel.values(), swap_cores(both_sides))
     both_sides = pltpu.with_memory_space_constraint(both_sides, pltpu.HBM)
     return project(group, terms, both_sides, swapped_sides)
 

time: 183 us -> 174 us (0.951)
  the two profiles are of different devices: /device:TPU:0 before, /device:TPU:9 now
where the time goes in v8:
time: 174 us; the launch traced here: 173 us
  waiting for transfers between devices  54.1 us (31%)
  Pallas kernels  50.6 us (29%)
  starting transfers between devices  46.1 us (26%)
  between operations  13.7 us (8%)
  other arithmetic  4.6 us (3%)
  local copies, waits for them, and re-layouts  4.24 us (2%)
    pallas_call x5, Pallas kernels, expert_apply(): pl.pallas_call(functools.partial(expert_kernel, positions, count), out_sh...  43.6 us
    ppermute x21, waiting for transfers between devices, swap_ep(): lax.ppermute(array, 'ep', [(i, i ^ mask) for i in range(lax.axis_size('ep...  42.9 us
    ppermute x21, starting transfers between devices, swap_cores(): return lax.ppermute(array, 'grp', [(0, 1), (1, 0)])  21.9 us
    ppermute x21, starting transfers between devices, swap_ep(): lax.ppermute(array, 'ep', [(i, i ^ mask) for i in range(lax.axis_size('ep...  21.6 us
    ppermute x2, waiting for transfers between devices, swap_reps(): lax.ppermute(array, 'rep', [(i, i ^ 1) for i in range(lax.axis_size('rep'...  6.37 us
    ppermute x21, waiting for transfers between devices, swap_cores(): return lax.ppermute(array, 'grp', [(0, 1), (1, 0)])  4.8 us
    pallas_call x1, Pallas kernels, project(): pl.pallas_call(project_kernel, in_specs=[in_smem] + [in_vmem] * len(terms...  4.7 us
  transfers between devices with their start and end apart: 46, of which 21 were waited for; matrix products, arithmetic and copies ran while one was open for 3% of the time, Pallas kernels for 26%

profile of v8, /device:TPU:9, one launch (start us, length us, event | category | flops | bytes accessed | tf_op | source)
XLA Modules:
  0.0 173.4 jit_solution(17941788658897948438)
XLA Ops:
  6.5 1.2 copy-done
  8.6 1.1 constant_dynamic-slice_fusion.1
  9.7 1.4 collective-permute-start.4
  11.1 2.3 %collective-permute-start.2 = (bf16[128,1024]{1,0:T(8,128)(2,1)S(1)}, bf16[128,1024]{1,0:T(8,128)(2,1)S(1)}, u32[]{:S(2)}, u32[]{:S(2)}) collective-permute-start(bf16[128,1024]{1,0:T(8,128)(2,1)S(1)} %get-tuple-element.160.refs_2_), channel_id=1, source_target_pairs={{0,4},{1,5},{2,6},{3,7},{4,0},{5,1},{6,2},{7,3},{8,12},{9,13},{10,... | collective-permute-start | bytes 786440 | tf_op jit(solution)/shard_map/ppermute | solution.py:35
  13.5 1.2 copy-done.1
  14.7 0.8 split_columns.1
  15.6 1.3 collective-permute-start.5
  17.5 1.1 collective-permute-done.refs_6_
  18.7 2.8 %collective-permute-start.1 = (bf16[128,1024]{1,0:T(8,128)(2,1)S(1)}, bf16[128,1024]{1,0:T(8,128)(2,1)S(1)}, u32[]{:S(2)}, u32[]{:S(2)}) collective-permute-start(bf16[128,1024]{1,0:T(8,128)(2,1)S(1)} %collective-permute-done.refs_6_), channel_id=1, source_target_pairs={{0,1},{1,0},{2,3},{3,2},{4,5},{5,4},{6,7},{7,6},{8,9},{9,8},{10,11... | collective-permute-start | bytes 786440 | tf_op jit(solution)/shard_map/ppermute | solution.py:35
  22.9 1.4 collective-permute-done.2.refs_10_
  24.3 4.2 %collective-permute-done.1.refs_7_ = bf16[128,1024]{1,0:T(8,128)(2,1)S(1)} collective-permute-done((bf16[128,1024]{1,0:T(8,128)(2,1)S(1)}, bf16[128,1024]{1,0:T(8,128)(2,1)S(1)}, u32[]{:S(2)}, u32[]{:S(2)}) %collective-permute-start.1) | collective-permute-done | bytes 262176 | tf_op jit(solution)/shard_map/ppermute | solution.py:35
  28.6 1.0 collective-permute-start.9
  29.5 4.1 %collective-permute-start.7 = (bf16[128,1024]{1,0:T(8,128)(2,1)S(1)}, bf16[128,1024]{1,0:T(8,128)(2,1)S(1)}, u32[]{:S(2)}, u32[]{:S(2)}) collective-permute-start(bf16[128,1024]{1,0:T(8,128)(2,1)S(1)} %collective-permute-done.refs_6_), channel_id=1, source_target_pairs={{0,8},{8,0},{1,9},{9,1},{2,10},{10,2},{3,11},{11,3},{4,12},{12,4},... | collective-permute-start | bytes 786440 | tf_op jit(solution)/shard_map/ppermute | solution.py:27
  33.6 5.6 %collective-permute-done.3.refs_2_ = bf16[128,1024]{1,0:T(8,128)(2,1)S(1)} collective-permute-done((bf16[128,1024]{1,0:T(8,128)(2,1)S(1)}, bf16[128,1024]{1,0:T(8,128)(2,1)S(1)}, u32[]{:S(2)}, u32[]{:S(2)}) %collective-permute-start.3) | collective-permute-done | bytes 262176 | tf_op jit(solution)/shard_map/ppermute | solution.py:35
  39.7 2.0 %collective-permute-start.10 = (bf16[128,1024]{1,0:T(8,128)(2,1)S(1)}, bf16[128,1024]{1,0:T(8,128)(2,1)S(1)}, u32[]{:S(2)}, u32[]{:S(2)}) collective-permute-start(bf16[128,1024]{1,0:T(8,128)(2,1)S(1)} %collective-permute-done.2.refs_10_), channel_id=1, source_target_pairs={{0,8},{8,0},{1,9},{9,1},{2,10},{10,2},{3,11},{11,3},{4,12},{12,4},... | collective-permute-start | bytes 786440 | tf_op jit(solution)/shard_map/ppermute | solution.py:27
  42.2 3.5 %collective-permute-done.12.refs_3_ = bf16[128,1024]{1,0:T(8,128)(2,1)S(1)} collective-permute-done((bf16[128,1024]{1,0:T(8,128)(2,1)S(1)}, bf16[128,1024]{1,0:T(8,128)(2,1)S(1)}, u32[]{:S(2)}, u32[]{:S(2)}) %collective-permute-start.12) | collective-permute-done | bytes 262176 | tf_op jit(solution)/shard_map/ppermute | solution.py:35
  45.7 6.8 %collective-permute-start.14 = (bf16[128,1024]{1,0:T(8,128)(2,1)S(1)}, bf16[128,1024]{1,0:T(8,128)(2,1)S(1)}, u32[]{:S(2)}, u32[]{:S(2)}) collective-permute-start(bf16[128,1024]{1,0:T(8,128)(2,1)S(1)} %collective-permute-done.12.refs_3_), channel_id=1, source_target_pairs={{0,8},{8,0},{1,9},{9,1},{2,10},{10,2},{3,11},{11,3},{4,12},{12,4},... | collective-permute-start | bytes 786440 | tf_op jit(solution)/shard_map/ppermute | solution.py:27
  52.6 1.0 down_project.2.refs_6_
  54.2 1.3 collective-permute-start.15
  55.5 6.4 %collective-permute-done.15.arrived = bf16[128,1024]{1,0:T(8,128)(2,1)S(1)} collective-permute-done((bf16[128,1024]{1,0:T(8,128)(2,1)S(1)}, bf16[128,1024]{1,0:T(8,128)(2,1)S(1)}, u32[]{:S(2)}, u32[]{:S(2)}) %collective-permute-start.15) | collective-permute-done | bytes 262176 | tf_op jit(solution)/shard_map/ppermute | solution.py:31
  61.9 1.2 collective-permute-start.16
  63.1 0.8 collective-permute-start.18
  64.3 6.8 %expert.5 = (bf16[128,1024]{1,0:T(8,128)(2,1)S(1)}, bf16[128,1024]{1,0:T(8,128)(2,1)S(1)}) custom-call(s32[1]{0:T(128)} %bitcast.1.where, bf16[144,1024]{1,0:T(8,128)(2,1)S(1)} %finish_latent.1.refs_0_, bf16[144,1024]{1,0:T(8,128)(2,1)S(1)} %collective-permute-done.16.refs_1_, bf16[1,1024,2048]{2,1,0:T(8,128)(2,1)} %refs_2_.3, ...), custom_call_target="tpu_custom_call" | custom-call | flops 805306368 | bytes 1048576 | tf_op jit(solution)/shard_map/expert/pallas_call | solution.py:248
  72.2 1.2 collective-permute-start.21
  73.5 1.0 collective-permute-start.22
  74.5 1.0 collective-permute-start.23
  75.5 10.0 %expert.6 = (bf16[128,1024]{1,0:T(8,128)(2,1)S(1)}, bf16[128,1024]{1,0:T(8,128)(2,1)S(1)}, bf16[256,1024]{1,0:T(8,128)(2,1)S(1)}) custom-call(s32[1]{0:T(128)} %bitcast.1.where, bf16[144,1024]{1,0:T(8,128)(2,1)S(1)} %collective-permute-done.17.refs_0_, bf16[144,1024]{1,0:T(8,128)(2,1)S(1)} %collective-permute-done.18.refs_1_, ...), custom_call_target="tpu_custom_call" | custom-call | flops 1610612736 | bytes 2097152 | tf_op jit(solution)/shard_map/expert/pallas_call | solution.py:248
  85.4 1.8 %collective-permute-done.22.refs_0_ = bf16[144,1024]{1,0:T(8,128)(2,1)S(1)} collective-permute-done((bf16[144,1024]{1,0:T(8,128)(2,1)S(1)}, bf16[144,1024]{1,0:T(8,128)(2,1)S(1)}, u32[]{:S(2)}, u32[]{:S(2)}) %collective-permute-start.22) | collective-permute-done | bytes 294944 | tf_op jit(solution)/shard_map/ppermute | solution.py:35
  88.0 2.8 %collective-permute-start.27 = (bf16[144,1024]{1,0:T(8,128)(2,1)S(1)}, bf16[144,1024]{1,0:T(8,128)(2,1)S(1)}, u32[]{:S(2)}, u32[]{:S(2)}) collective-permute-start(bf16[144,1024]{1,0:T(8,128)(2,1)S(1)} %collective-permute-done.22.refs_0_), channel_id=1, source_target_pairs={{0,2},{1,3},{2,0},{3,1},{4,6},{5,7},{6,4},{7,5},{8,10},{9,11},{10,... | collective-permute-start | bytes 884744 | tf_op jit(solution)/shard_map/ppermute | solution.py:35
  90.8 1.0 collective-permute-start.26
  91.8 1.1 collective-permute-start.24
  94.0 10.0 %expert.7 = (bf16[128,1024]{1,0:T(8,128)(2,1)S(1)}, bf16[128,1024]{1,0:T(8,128)(2,1)S(1)}, bf16[256,1024]{1,0:T(8,128)(2,1)S(1)}) custom-call(s32[1]{0:T(128)} %bitcast.1.where, bf16[144,1024]{1,0:T(8,128)(2,1)S(1)} %collective-permute-done.22.refs_0_, bf16[144,1024]{1,0:T(8,128)(2,1)S(1)} %collective-permute-done.23.refs_1_, ...), custom_call_target="tpu_custom_call" | custom-call | flops 1610612736 | bytes 2097152 | tf_op jit(solution)/shard_map/expert/pallas_call | solution.py:248
  104.3 1.6 collective-permute-start.34
  105.8 1.0 collective-permute-start.33
  108.8 10.0 %expert.8 = (bf16[128,1024]{1,0:T(8,128)(2,1)S(1)}, bf16[128,1024]{1,0:T(8,128)(2,1)S(1)}, bf16[256,1024]{1,0:T(8,128)(2,1)S(1)}) custom-call(s32[1]{0:T(128)} %bitcast.1.where, bf16[144,1024]{1,0:T(8,128)(2,1)S(1)} %collective-permute-done.27.refs_0_, bf16[144,1024]{1,0:T(8,128)(2,1)S(1)} %collective-permute-done.26.refs_1_, ...), custom_call_target="tpu_custom_call" | custom-call | flops 1610612736 | bytes 2097152 | tf_op jit(solution)/shard_map/expert/pallas_call | solution.py:248
  118.8 1.4 collective-permute-done.33.refs_0_
  120.9 1.5 collective-permute-done.37
  122.7 1.0 collective-permute-start.38
  123.7 6.9 %expert.9 = (bf16[128,1024]{1,0:T(8,128)(2,1)S(1)}, bf16[128,1024]{1,0:T(8,128)(2,1)S(1)}) custom-call(s32[1]{0:T(128)} %bitcast.1.where, bf16[144,1024]{1,0:T(8,128)(2,1)S(1)} %collective-permute-done.33.refs_0_, bf16[144,1024]{1,0:T(8,128)(2,1)S(1)} %collective-permute-done.36.refs_1_, bf16[1,1024,2048]{2,1,0:T(8,128)(2,1)} %refs_2_.3, ...), custom_call_target="tpu_custom_call" | custom-call | flops 805306368 | bytes 1048576 | tf_op jit(solution)/shard_map/expert/pallas_call | solution.py:248
  130.6 0.9 collective-permute-start.41
  131.6 1.2 collective-permute-done.41
  132.7 0.8 add_convert_fusion
  134.0 1.1 add_convert_fusion.1
  135.1 1.9 %collective-permute-start.40 = (bf16[128,1024]{1,0:T(8,128)(2,1)S(1)}, bf16[128,1024]{1,0:T(8,128)(2,1)S(1)}, u32[]{:S(2)}, u32[]{:S(2)}) collective-permute-start(bf16[128,1024]{1,0:T(8,128)(2,1)S(1)} %add_convert_fusion.1), channel_id=1, source_target_pairs={{0,4},{1,5},{2,6},{3,7},{4,0},{5,1},{6,2},{7,3},{8,12},{9,13},{10,... | collective-permute-start | bytes 786440 | tf_op jit(solution)/shard_map/ppermute | solution.py:35
  137.0 1.4 collective-permute-start.42
  139.2 14.8 %collective-permute-done.40.refs_4_ = bf16[128,1024]{1,0:T(8,128)(2,1)S(1)} collective-permute-done((bf16[128,1024]{1,0:T(8,128)(2,1)S(1)}, bf16[128,1024]{1,0:T(8,128)(2,1)S(1)}, u32[]{:S(2)}, u32[]{:S(2)}) %collective-permute-start.40) | collective-permute-done | bytes 262176 | tf_op jit(solution)/shard_map/ppermute | solution.py:35
  154.0 7.8 %collective-permute-done.42.refs_5_ = bf16[128,1024]{1,0:T(8,128)(2,1)S(1)} collective-permute-done((bf16[128,1024]{1,0:T(8,128)(2,1)}, bf16[128,1024]{1,0:T(8,128)(2,1)S(1)}, u32[]{:S(2)}, u32[]{:S(2)}) %collective-permute-start.42) | collective-permute-done | bytes 262176 | tf_op jit(solution)/shard_map/ppermute | solution.py:35
  161.8 4.7 %project.1 = bf16[128,4096]{1,0:T(8,128)(2,1)} custom-call(s32[1]{0:T(128)} %bitcast.where, f32[128,1024]{1,0:T(8,128)S(1)} %convert_add_fusion.refs_0_, bf16[128,1024]{1,0:T(8,128)(2,1)S(1)} %collective-permute-done.29.refs_1_, bf16[128,1024]{1,0:T(8,128)(2,1)S(1)} %collective-permute-done.30.refs_2_, ...), custom_call_target="tpu_custom_call" | custom-call | flops 1073741824 | bytes 8388608 | tf_op jit(solution)/shard_map/project/pallas_call | solution.py:310
  (74 shorter events, 12.8 us)
Async XLA Ops:
  6.5 65.6 %all-gather.5.cloned.1.call-start = ((), (), s32[]{:S(2)}) async-start(), calls=%async_computation | async-start | bytes 2359296 | tf_op jit(solution)/shard_map/all_gather | solution.py:360
  8.5 125.0 %all-gather.7.cloned.1.call-start = ((), (), s32[]{:S(2)}) async-start(), calls=%async_computation.1 | async-start | bytes 6291456 | tf_op jit(solution)/shard_map/all_gather | solution.py:418
  9.6 9.0 %collective-permute-start = (bf16[128,1024]{1,0:T(8,128)(2,1)S(1)}, bf16[128,1024]{1,0:T(8,128)(2,1)S(1)}, u32[]{:S(2)}, u32[]{:S(2)}) collective-permute-start(bf16[128,1024]{1,0:T(8,128)(2,1)S(1)} %get-tuple-element.160.refs_2_), channel_id=1, source_target_pairs={{0,2},{1,3},{2,0},{3,1},{4,6},{5,7},{6,4},{7,5},{8,10},{9,11},{10,... | collective-permute-start | bytes 786440 | tf_op jit(solution)/shard_map/ppermute | solution.py:35
  9.7 23.9 %collective-permute-start.4 = (bf16[128,1024]{1,0:T(8,128)(2,1)S(1)}, bf16[128,1024]{1,0:T(8,128)(2,1)S(1)}, u32[]{:S(2)}, u32[]{:S(2)}) collective-permute-start(bf16[128,1024]{1,0:T(8,128)(2,1)S(1)} %get-tuple-element.160.refs_2_), channel_id=1, source_target_pairs={{0,1},{1,0},{2,3},{3,2},{4,5},{5,4},{6,7},{7,6},{8,9},{9,8},{10,11... | collective-permute-start | bytes 786440 | tf_op jit(solution)/shard_map/ppermute | solution.py:35
  11.1 13.2 %collective-permute-start.2 = (bf16[128,1024]{1,0:T(8,128)(2,1)S(1)}, bf16[128,1024]{1,0:T(8,128)(2,1)S(1)}, u32[]{:S(2)}, u32[]{:S(2)}) collective-permute-start(bf16[128,1024]{1,0:T(8,128)(2,1)S(1)} %get-tuple-element.160.refs_2_), channel_id=1, source_target_pairs={{0,4},{1,5},{2,6},{3,7},{4,0},{5,1},{6,2},{7,3},{8,12},{9,13},{10,... | collective-permute-start | bytes 786440 | tf_op jit(solution)/shard_map/ppermute | solution.py:35
  13.5 1.2 copy-start.1
  15.6 18.0 %collective-permute-start.5 = (bf16[128,2048]{1,0:T(8,128)(2,1)S(1)}, bf16[128,2048]{1,0:T(8,128)(2,1)S(1)}, u32[]{:S(2)}, u32[]{:S(2)}) collective-permute-start(bf16[128,2048]{1,0:T(8,128)(2,1)S(1)} %get-tuple-element.87), channel_id=1, source_target_pairs={{0,16},{16,0},{1,17},{17,1},{2,18},{18,2},{3,19},{19,3},{4,20},{20... | collective-permute-start | bytes 1572872 | tf_op jit(solution)/shard_map/ppermute | solution.py:31
  18.7 9.9 %collective-permute-start.1 = (bf16[128,1024]{1,0:T(8,128)(2,1)S(1)}, bf16[128,1024]{1,0:T(8,128)(2,1)S(1)}, u32[]{:S(2)}, u32[]{:S(2)}) collective-permute-start(bf16[128,1024]{1,0:T(8,128)(2,1)S(1)} %collective-permute-done.refs_6_), channel_id=1, source_target_pairs={{0,1},{1,0},{2,3},{3,2},{4,5},{5,4},{6,7},{7,6},{8,9},{9,8},{10,11... | collective-permute-start | bytes 786440 | tf_op jit(solution)/shard_map/ppermute | solution.py:35
  28.6 10.6 %collective-permute-start.3 = (bf16[128,1024]{1,0:T(8,128)(2,1)S(1)}, bf16[128,1024]{1,0:T(8,128)(2,1)S(1)}, u32[]{:S(2)}, u32[]{:S(2)}) collective-permute-start(bf16[128,1024]{1,0:T(8,128)(2,1)S(1)} %collective-permute-done.2.refs_10_), channel_id=1, source_target_pairs={{0,2},{1,3},{2,0},{3,1},{4,6},{5,7},{6,4},{7,5},{8,10},{9,11},{10,... | collective-permute-start | bytes 786440 | tf_op jit(solution)/shard_map/ppermute | solution.py:35
  28.6 13.1 %collective-permute-start.9 = (bf16[128,1024]{1,0:T(8,128)(2,1)S(1)}, bf16[128,1024]{1,0:T(8,128)(2,1)S(1)}, u32[]{:S(2)}, u32[]{:S(2)}) collective-permute-start(bf16[128,1024]{1,0:T(8,128)(2,1)S(1)} %collective-permute-done.2.refs_10_), channel_id=1, source_target_pairs={{0,1},{1,0},{2,3},{3,2},{4,5},{5,4},{6,7},{7,6},{8,9},{9,8},{10,11... | collective-permute-start | bytes 786440 | tf_op jit(solution)/shard_map/ppermute | solution.py:35
  29.5 12.1 %collective-permute-start.7 = (bf16[128,1024]{1,0:T(8,128)(2,1)S(1)}, bf16[128,1024]{1,0:T(8,128)(2,1)S(1)}, u32[]{:S(2)}, u32[]{:S(2)}) collective-permute-start(bf16[128,1024]{1,0:T(8,128)(2,1)S(1)} %collective-permute-done.refs_6_), channel_id=1, source_target_pairs={{0,8},{8,0},{1,9},{9,1},{2,10},{10,2},{3,11},{11,3},{4,12},{12,4},... | collective-permute-start | bytes 786440 | tf_op jit(solution)/shard_map/ppermute | solution.py:27
  33.6 8.6 %collective-permute-start.8 = (bf16[128,1024]{1,0:T(8,128)(2,1)S(1)}, bf16[128,1024]{1,0:T(8,128)(2,1)S(1)}, u32[]{:S(2)}, u32[]{:S(2)}) collective-permute-start(bf16[128,1024]{1,0:T(8,128)(2,1)S(1)} %collective-permute-done.1.refs_7_), channel_id=1, source_target_pairs={{0,8},{8,0},{1,9},{9,1},{2,10},{10,2},{3,11},{11,3},{4,12},{12,4},... | collective-permute-start | bytes 786440 | tf_op jit(solution)/shard_map/ppermute | solution.py:27
  39.2 6.6 %collective-permute-start.12 = (bf16[128,1024]{1,0:T(8,128)(2,1)S(1)}, bf16[128,1024]{1,0:T(8,128)(2,1)S(1)}, u32[]{:S(2)}, u32[]{:S(2)}) collective-permute-start(bf16[128,1024]{1,0:T(8,128)(2,1)S(1)} %collective-permute-done.3.refs_2_), channel_id=1, source_target_pairs={{0,1},{1,0},{2,3},{3,2},{4,5},{5,4},{6,7},{7,6},{8,9},{9,8},{10,11... | collective-permute-start | bytes 786440 | tf_op jit(solution)/shard_map/ppermute | solution.py:35
  39.7 12.9 %collective-permute-start.10 = (bf16[128,1024]{1,0:T(8,128)(2,1)S(1)}, bf16[128,1024]{1,0:T(8,128)(2,1)S(1)}, u32[]{:S(2)}, u32[]{:S(2)}) collective-permute-start(bf16[128,1024]{1,0:T(8,128)(2,1)S(1)} %collective-permute-done.2.refs_10_), channel_id=1, source_target_pairs={{0,8},{8,0},{1,9},{9,1},{2,10},{10,2},{3,11},{11,3},{4,12},{12,4},... | collective-permute-start | bytes 786440 | tf_op jit(solution)/shard_map/ppermute | solution.py:27
  41.6 10.9 %collective-permute-start.11 = (bf16[128,1024]{1,0:T(8,128)(2,1)S(1)}, bf16[128,1024]{1,0:T(8,128)(2,1)S(1)}, u32[]{:S(2)}, u32[]{:S(2)}) collective-permute-start(bf16[128,1024]{1,0:T(8,128)(2,1)S(1)} %collective-permute-done.9.refs_11_), channel_id=1, source_target_pairs={{0,8},{8,0},{1,9},{9,1},{2,10},{10,2},{3,11},{11,3},{4,12},{12,4},... | collective-permute-start | bytes 786440 | tf_op jit(solution)/shard_map/ppermute | solution.py:27
  41.6 10.9 %collective-permute-start.6 = (bf16[128,1024]{1,0:T(8,128)(2,1)S(1)}, bf16[128,1024]{1,0:T(8,128)(2,1)S(1)}, u32[]{:S(2)}, u32[]{:S(2)}) collective-permute-start(bf16[128,1024]{1,0:T(8,128)(2,1)S(1)} %collective-permute-done.4.refs_3_), channel_id=1, source_target_pairs={{0,8},{8,0},{1,9},{9,1},{2,10},{10,2},{3,11},{11,3},{4,12},{12,4},... | collective-permute-start | bytes 786440 | tf_op jit(solution)/shard_map/ppermute | solution.py:27
  42.1 11.4 %collective-permute-start.13 = (bf16[128,1024]{1,0:T(8,128)(2,1)S(1)}, bf16[128,1024]{1,0:T(8,128)(2,1)S(1)}, u32[]{:S(2)}, u32[]{:S(2)}) collective-permute-start(bf16[128,1024]{1,0:T(8,128)(2,1)S(1)} %collective-permute-done.3.refs_2_), channel_id=1, source_target_pairs={{0,8},{8,0},{1,9},{9,1},{2,10},{10,2},{3,11},{11,3},{4,12},{12,4},... | collective-permute-start | bytes 786440 | tf_op jit(solution)/shard_map/ppermute | solution.py:27
  45.7 8.0 %collective-permute-start.14 = (bf16[128,1024]{1,0:T(8,128)(2,1)S(1)}, bf16[128,1024]{1,0:T(8,128)(2,1)S(1)}, u32[]{:S(2)}, u32[]{:S(2)}) collective-permute-start(bf16[128,1024]{1,0:T(8,128)(2,1)S(1)} %collective-permute-done.12.refs_3_), channel_id=1, source_target_pairs={{0,8},{8,0},{1,9},{9,1},{2,10},{10,2},{3,11},{11,3},{4,12},{12,4},... | collective-permute-start | bytes 786440 | tf_op jit(solution)/shard_map/ppermute | solution.py:27
  54.2 7.7 %collective-permute-start.15 = (bf16[128,1024]{1,0:T(8,128)(2,1)S(1)}, bf16[128,1024]{1,0:T(8,128)(2,1)S(1)}, u32[]{:S(2)}, u32[]{:S(2)}) collective-permute-start(bf16[128,1024]{1,0:T(8,128)(2,1)S(1)} %get-tuple-element.94), channel_id=1, source_target_pairs={{0,16},{16,0},{1,17},{17,1},{2,18},{18,2},{3,19},{19,3},{4,20},{20... | collective-permute-start | bytes 786440 | tf_op jit(solution)/shard_map/ppermute | solution.py:31
  61.9 2.4 %collective-permute-start.16 = (bf16[144,1024]{1,0:T(8,128)(2,1)S(1)}, bf16[144,1024]{1,0:T(8,128)(2,1)S(1)}, u32[]{:S(2)}, u32[]{:S(2)}) collective-permute-start(bf16[144,1024]{1,0:T(8,128)(2,1)S(1)} %finish_latent.1.refs_0_), channel_id=1, source_target_pairs={{0,8},{8,0},{1,9},{9,1},{2,10},{10,2},{3,11},{11,3},{4,12},{12,4},... | collective-permute-start | bytes 884744 | tf_op jit(solution)/shard_map/ppermute | solution.py:27
  63.1 8.6 %collective-permute-start.18 = (bf16[144,1024]{1,0:T(8,128)(2,1)S(1)}, bf16[144,1024]{1,0:T(8,128)(2,1)S(1)}, u32[]{:S(2)}, u32[]{:S(2)}) collective-permute-start(bf16[144,1024]{1,0:T(8,128)(2,1)S(1)} %finish_latent.1.refs_0_), channel_id=1, source_target_pairs={{0,1},{1,0},{2,3},{3,2},{4,5},{5,4},{6,7},{7,6},{8,9},{9,8},{10,11... | collective-permute-start | bytes 884744 | tf_op jit(solution)/shard_map/ppermute | solution.py:35
  63.9 8.2 %collective-permute-start.17 = (bf16[144,1024]{1,0:T(8,128)(2,1)S(1)}, bf16[144,1024]{1,0:T(8,128)(2,1)S(1)}, u32[]{:S(2)}, u32[]{:S(2)}) collective-permute-start(bf16[144,1024]{1,0:T(8,128)(2,1)S(1)} %finish_latent.1.refs_0_), channel_id=1, source_target_pairs={{0,2},{1,3},{2,0},{3,1},{4,6},{5,7},{6,4},{7,5},{8,10},{9,11},{10,... | collective-permute-start | bytes 884744 | tf_op jit(solution)/shard_map/ppermute | solution.py:35
  72.2 3.3 %collective-permute-start.21 = (bf16[144,1024]{1,0:T(8,128)(2,1)S(1)}, bf16[144,1024]{1,0:T(8,128)(2,1)S(1)}, u32[]{:S(2)}, u32[]{:S(2)}) collective-permute-start(bf16[144,1024]{1,0:T(8,128)(2,1)S(1)} %collective-permute-done.18.refs_1_), channel_id=1, source_target_pairs={{0,8},{8,0},{1,9},{9,1},{2,10},{10,2},{3,11},{11,3},{4,12},{12,4},... | collective-permute-start | bytes 884744 | tf_op jit(solution)/shard_map/ppermute | solution.py:27
  73.4 2.1 %collective-permute-start.20 = (bf16[144,1024]{1,0:T(8,128)(2,1)S(1)}, bf16[144,1024]{1,0:T(8,128)(2,1)S(1)}, u32[]{:S(2)}, u32[]{:S(2)}) collective-permute-start(bf16[144,1024]{1,0:T(8,128)(2,1)S(1)} %collective-permute-done.17.refs_0_), channel_id=1, source_target_pairs={{0,8},{8,0},{1,9},{9,1},{2,10},{10,2},{3,11},{11,3},{4,12},{12,4},... | collective-permute-start | bytes 884744 | tf_op jit(solution)/shard_map/ppermute | solution.py:27
  73.5 13.8 %collective-permute-start.22 = (bf16[144,1024]{1,0:T(8,128)(2,1)S(1)}, bf16[144,1024]{1,0:T(8,128)(2,1)S(1)}, u32[]{:S(2)}, u32[]{:S(2)}) collective-permute-start(bf16[144,1024]{1,0:T(8,128)(2,1)S(1)} %finish_latent.1.refs_0_), channel_id=1, source_target_pairs={{0,4},{1,5},{2,6},{3,7},{4,0},{5,1},{6,2},{7,3},{8,12},{9,13},{10,... | collective-permute-start | bytes 884744 | tf_op jit(solution)/shard_map/ppermute | solution.py:35
  74.5 12.8 %collective-permute-start.23 = (bf16[144,1024]{1,0:T(8,128)(2,1)S(1)}, bf16[144,1024]{1,0:T(8,128)(2,1)S(1)}, u32[]{:S(2)}, u32[]{:S(2)}) collective-permute-start(bf16[144,1024]{1,0:T(8,128)(2,1)S(1)} %collective-permute-done.17.refs_0_), channel_id=1, source_target_pairs={{0,1},{1,0},{2,3},{3,2},{4,5},{5,4},{6,7},{7,6},{8,9},{9,8},{10,11... | collective-permute-start | bytes 884744 | tf_op jit(solution)/shard_map/ppermute | solution.py:35
  87.3 5.6 %collective-permute-start.28 = (bf16[256,1024]{1,0:T(8,128)(2,1)S(1)}, bf16[256,1024]{1,0:T(8,128)(2,1)S(1)}, u32[]{:S(2)}, u32[]{:S(2)}) collective-permute-start(bf16[256,1024]{1,0:T(8,128)(2,1)S(1)} %get-tuple-element.121), channel_id=1, source_target_pairs={{0,8},{8,0},{1,9},{9,1},{2,10},{10,2},{3,11},{11,3},{4,12},{12,4},... | collective-permute-start | bytes 1572872 | tf_op jit(solution)/shard_map/ppermute | solution.py:27
  88.0 5.1 %collective-permute-start.25 = (bf16[144,1024]{1,0:T(8,128)(2,1)S(1)}, bf16[144,1024]{1,0:T(8,128)(2,1)S(1)}, u32[]{:S(2)}, u32[]{:S(2)}) collective-permute-start(bf16[144,1024]{1,0:T(8,128)(2,1)S(1)} %collective-permute-done.23.refs_1_), channel_id=1, source_target_pairs={{0,8},{8,0},{1,9},{9,1},{2,10},{10,2},{3,11},{11,3},{4,12},{12,4},... | collective-permute-start | bytes 884744 | tf_op jit(solution)/shard_map/ppermute | solution.py:27
  88.0 16.0 %collective-permute-start.27 = (bf16[144,1024]{1,0:T(8,128)(2,1)S(1)}, bf16[144,1024]{1,0:T(8,128)(2,1)S(1)}, u32[]{:S(2)}, u32[]{:S(2)}) collective-permute-start(bf16[144,1024]{1,0:T(8,128)(2,1)S(1)} %collective-permute-done.22.refs_0_), channel_id=1, source_target_pairs={{0,2},{1,3},{2,0},{3,1},{4,6},{5,7},{6,4},{7,5},{8,10},{9,11},{10,... | collective-permute-start | bytes 884744 | tf_op jit(solution)/shard_map/ppermute | solution.py:35
  90.8 13.2 %collective-permute-start.26 = (bf16[144,1024]{1,0:T(8,128)(2,1)S(1)}, bf16[144,1024]{1,0:T(8,128)(2,1)S(1)}, u32[]{:S(2)}, u32[]{:S(2)}) collective-permute-start(bf16[144,1024]{1,0:T(8,128)(2,1)S(1)} %collective-permute-done.22.refs_0_), channel_id=1, source_target_pairs={{0,1},{1,0},{2,3},{3,2},{4,5},{5,4},{6,7},{7,6},{8,9},{9,8},{10,11... | collective-permute-start | bytes 884744 | tf_op jit(solution)/shard_map/ppermute | solution.py:35
  91.8 2.3 %collective-permute-start.24 = (bf16[144,1024]{1,0:T(8,128)(2,1)S(1)}, bf16[144,1024]{1,0:T(8,128)(2,1)S(1)}, u32[]{:S(2)}, u32[]{:S(2)}) collective-permute-start(bf16[144,1024]{1,0:T(8,128)(2,1)S(1)} %collective-permute-done.22.refs_0_), channel_id=1, source_target_pairs={{0,8},{8,0},{1,9},{9,1},{2,10},{10,2},{3,11},{11,3},{4,12},{12,4},... | collective-permute-start | bytes 884744 | tf_op jit(solution)/shard_map/ppermute | solution.py:27
  93.0 11.0 %collective-permute-start.30 = (bf16[128,1024]{1,0:T(8,128)(2,1)S(1)}, bf16[128,1024]{1,0:T(8,128)(2,1)S(1)}, u32[]{:S(2)}, u32[]{:S(2)}) collective-permute-start(bf16[128,1024]{1,0:T(8,128)(2,1)S(1)} %get-tuple-element.163), channel_id=1, source_target_pairs={{0,2},{1,3},{2,0},{3,1},{4,6},{5,7},{6,4},{7,5},{8,10},{9,11},{10,... | collective-permute-start | bytes 786440 | tf_op jit(solution)/shard_map/ppermute | solution.py:35
  93.1 11.1 %collective-permute-start.29 = (bf16[128,1024]{1,0:T(8,128)(2,1)S(1)}, bf16[128,1024]{1,0:T(8,128)(2,1)S(1)}, u32[]{:S(2)}, u32[]{:S(2)}) collective-permute-start(bf16[128,1024]{1,0:T(8,128)(2,1)S(1)} %get-tuple-element.164), channel_id=1, source_target_pairs={{0,1},{1,0},{2,3},{3,2},{4,5},{5,4},{6,7},{7,6},{8,9},{9,8},{10,11... | collective-permute-start | bytes 786440 | tf_op jit(solution)/shard_map/ppermute | solution.py:35
  104.3 3.1 %collective-permute-start.34 = (bf16[256,1024]{1,0:T(8,128)(2,1)S(1)}, bf16[256,1024]{1,0:T(8,128)(2,1)S(1)}, u32[]{:S(2)}, u32[]{:S(2)}) collective-permute-start(bf16[256,1024]{1,0:T(8,128)(2,1)S(1)} %get-tuple-element.135), channel_id=1, source_target_pairs={{0,8},{8,0},{1,9},{9,1},{2,10},{10,2},{3,11},{11,3},{4,12},{12,4},... | collective-permute-start | bytes 1572872 | tf_op jit(solution)/shard_map/ppermute | solution.py:27
  105.8 14.4 %collective-permute-start.33 = (bf16[144,1024]{1,0:T(8,128)(2,1)S(1)}, bf16[144,1024]{1,0:T(8,128)(2,1)S(1)}, u32[]{:S(2)}, u32[]{:S(2)}) collective-permute-start(bf16[144,1024]{1,0:T(8,128)(2,1)S(1)} %collective-permute-done.27.refs_0_), channel_id=1, source_target_pairs={{0,1},{1,0},{2,3},{3,2},{4,5},{5,4},{6,7},{7,6},{8,9},{9,8},{10,11... | collective-permute-start | bytes 884744 | tf_op jit(solution)/shard_map/ppermute | solution.py:35
  106.8 2.0 %collective-permute-start.31 = (bf16[144,1024]{1,0:T(8,128)(2,1)S(1)}, bf16[144,1024]{1,0:T(8,128)(2,1)S(1)}, u32[]{:S(2)}, u32[]{:S(2)}) collective-permute-start(bf16[144,1024]{1,0:T(8,128)(2,1)S(1)} %collective-permute-done.27.refs_0_), channel_id=1, source_target_pairs={{0,8},{8,0},{1,9},{9,1},{2,10},{10,2},{3,11},{11,3},{4,12},{12,4},... | collective-permute-start | bytes 884744 | tf_op jit(solution)/shard_map/ppermute | solution.py:27
  107.1 1.7 collective-permute-start.32
  107.4 12.8 %collective-permute-start.35 = (bf16[128,1024]{1,0:T(8,128)(2,1)S(1)}, bf16[128,1024]{1,0:T(8,128)(2,1)S(1)}, u32[]{:S(2)}, u32[]{:S(2)}) collective-permute-start(bf16[128,1024]{1,0:T(8,128)(2,1)S(1)} %add_convert_fusion.4), channel_id=1, source_target_pairs={{0,3},{1,2},{2,1},{3,0},{4,7},{5,6},{6,5},{7,4},{8,11},{9,10},{10,... | collective-permute-start | bytes 786440 | tf_op jit(solution)/shard_map/ppermute | solution.py:35
  120.2 2.2 %collective-permute-start.37 = (bf16[256,1024]{1,0:T(8,128)(2,1)S(1)}, bf16[256,1024]{1,0:T(8,128)(2,1)S(1)}, u32[]{:S(2)}, u32[]{:S(2)}) collective-permute-start(bf16[256,1024]{1,0:T(8,128)(2,1)S(1)} %get-tuple-element.144), channel_id=1, source_target_pairs={{0,8},{8,0},{1,9},{9,1},{2,10},{10,2},{3,11},{11,3},{4,12},{12,4},... | collective-permute-start | bytes 1572872 | tf_op jit(solution)/shard_map/ppermute | solution.py:27
  120.9 2.9 %collective-permute-start.36 = (bf16[144,1024]{1,0:T(8,128)(2,1)S(1)}, bf16[144,1024]{1,0:T(8,128)(2,1)S(1)}, u32[]{:S(2)}, u32[]{:S(2)}) collective-permute-start(bf16[144,1024]{1,0:T(8,128)(2,1)S(1)} %collective-permute-done.33.refs_0_), channel_id=1, source_target_pairs={{0,8},{8,0},{1,9},{9,1},{2,10},{10,2},{3,11},{11,3},{4,12},{12,4},... | collective-permute-start | bytes 884744 | tf_op jit(solution)/shard_map/ppermute | solution.py:27
  122.6 8.0 %collective-permute-start.39 = (bf16[128,1024]{1,0:T(8,128)(2,1)S(1)}, bf16[128,1024]{1,0:T(8,128)(2,1)S(1)}, u32[]{:S(2)}, u32[]{:S(2)}) collective-permute-start(bf16[128,1024]{1,0:T(8,128)(2,1)S(1)} %get-tuple-element.161), channel_id=1, source_target_pairs={{0,2},{1,3},{2,0},{3,1},{4,6},{5,7},{6,4},{7,5},{8,10},{9,11},{10,... | collective-permute-start | bytes 786440 | tf_op jit(solution)/shard_map/ppermute | solution.py:35
  122.7 7.9 %collective-permute-start.38 = (bf16[128,1024]{1,0:T(8,128)(2,1)S(1)}, bf16[128,1024]{1,0:T(8,128)(2,1)S(1)}, u32[]{:S(2)}, u32[]{:S(2)}) collective-permute-start(bf16[128,1024]{1,0:T(8,128)(2,1)S(1)} %get-tuple-element.162), channel_id=1, source_target_pairs={{0,1},{1,0},{2,3},{3,2},{4,5},{5,4},{6,7},{7,6},{8,9},{9,8},{10,11... | collective-permute-start | bytes 786440 | tf_op jit(solution)/shard_map/ppermute | solution.py:35
  130.6 2.1 %copy-start.2 = (bf16[128,1024]{1,0:T(8,128)(2,1)}, bf16[128,1024]{1,0:T(8,128)(2,1)S(1)}, u32[]{:S(2)}) copy-start(bf16[128,1024]{1,0:T(8,128)(2,1)S(1)} %collective-permute-done.38) | copy-start | bytes 786436
  130.6 2.1 %collective-permute-start.41 = (bf16[128,1024]{1,0:T(8,128)(2,1)S(1)}, bf16[128,1024]{1,0:T(8,128)(2,1)S(1)}, u32[]{:S(2)}, u32[]{:S(2)}) collective-permute-start(bf16[128,1024]{1,0:T(8,128)(2,1)S(1)} %get-tuple-element.149), channel_id=1, source_target_pairs={{0,8},{8,0},{1,9},{9,1},{2,10},{10,2},{3,11},{11,3},{4,12},{12,4},... | collective-permute-start | bytes 786440 | tf_op jit(solution)/shard_map/ppermute | solution.py:27
  133.5 28.3 %collective-permute-start.43 = (bf16[2,8,256,512]{3,2,1,0:T(8,128)(2,1)}, bf16[2,8,256,512]{3,2,1,0:T(8,128)(2,1)S(1)}, u32[]{:S(2)}, u32[]{:S(2)}) collective-permute-start(bf16[2,8,256,512]{3,2,1,0:T(8,128)(2,1)} %bitcast.6), channel_id=1, source_target_pairs={{0,8},{8,0},{1,9},{9,1},{2,10},{10,2},{3,11},{11,3},{4,12},{12,4},... | collective-permute-start | bytes 12582920 | tf_op jit(solution)/shard_map/ppermute | solution.py:27
  133.9 5.3 %collective-permute-start.19 = (bf16[128,1024]{1,0:T(8,128)(2,1)S(1)}, bf16[128,1024]{1,0:T(8,128)(2,1)S(1)}, u32[]{:S(2)}, u32[]{:S(2)}) collective-permute-start(bf16[128,1024]{1,0:T(8,128)(2,1)S(1)} %get-tuple-element.101), channel_id=1, source_target_pairs={{0,8},{8,0},{1,9},{9,1},{2,10},{10,2},{3,11},{11,3},{4,12},{12,4},... | collective-permute-start | bytes 786440 | tf_op jit(solution)/shard_map/ppermute | solution.py:27
  135.1 18.9 %collective-permute-start.40 = (bf16[128,1024]{1,0:T(8,128)(2,1)S(1)}, bf16[128,1024]{1,0:T(8,128)(2,1)S(1)}, u32[]{:S(2)}, u32[]{:S(2)}) collective-permute-start(bf16[128,1024]{1,0:T(8,128)(2,1)S(1)} %add_convert_fusion.1), channel_id=1, source_target_pairs={{0,4},{1,5},{2,6},{3,7},{4,0},{5,1},{6,2},{7,3},{8,12},{9,13},{10,... | collective-permute-start | bytes 786440 | tf_op jit(solution)/shard_map/ppermute | solution.py:35
  137.0 24.8 %collective-permute-start.42 = (bf16[128,1024]{1,0:T(8,128)(2,1)}, bf16[128,1024]{1,0:T(8,128)(2,1)S(1)}, u32[]{:S(2)}, u32[]{:S(2)}) collective-permute-start(bf16[128,1024]{1,0:T(8,128)(2,1)} %add_convert_fusion), channel_id=1, source_target_pairs={{0,7},{1,6},{2,5},{3,4},{4,3},{5,2},{6,1},{7,0},{8,15},{9,14},{10,... | collective-permute-start | bytes 786440 | tf_op jit(solution)/shard_map/ppermute | solution.py:35
  (1 other events, 1.2 us)
Sparse Core Ops, SparseCore 0:
  9.5 56.7 all-gather.4
  72.3 56.7 all-gather.6

commit v9 on v8

--- a/solution.py
+++ b/solution.py
@@ -354,20 +354,21 @@
     far = {0: swap_ep(near[0], 1)}
     near[1], kept = join(near[1], kept)
     far[1] = swap_ep(near[1], 1)
+    weights = dense_weights(after(expert_ids, near[1]), route_scores, expert_count)
+    others = {k: near[k] for k in near if k > 1}
+    far[0], far[1], taken, weights, *arrived = join(
+        far[0], far[1], taken, weights, *others.values()
+    )
+    near.update(zip(others, arrived))
 
     inner = latent_width // 4
     up_piece = lax.dynamic_slice_in_dim(up_latent, own_quarter * inner, inner, 0)
-    mine = lax.all_gather(up_piece, "ep", axis=0)
-    weights = dense_weights(after(expert_ids, near[1]), route_scores, expert_count)
-    others = {k: near[k] for k in near if k > 1}
-    far[1], weights, *arrived = join(far[1], weights, *others.values())
-    near.update(zip(others, arrived))
+    mine = lax.all_gather(after(up_piece, weights), "ep", axis=0)
+
     for k in range(2, steps):
         if k & (k - 1):
             low = k & -k
             near[k] = swap_ep(near[k ^ low], 2 * low)
-        if k == last:
-            near[k], far[0], taken = join(near[k], far[0], taken)
         far[k] = swap_ep(near[k], 1)
     blocks = []
     for k in range(steps):
@@ -413,10 +414,10 @@
             swapped = from_core[i * token_count : (i + 1) * token_count]
             sums[place_of] = out[i].astype(jnp.float32) + swapped.astype(jnp.float32)
 
-    run([(0, 0)], (near, 1), (far, 0), (travel, "up"))
+    run([(0, 0)], (near, 1), (far, 0))
+    run([(1, 0), (0, 1)], *[(near, k) for k in near if k > 1], start_far(1), (travel, "up"))
     sides = [[i, i + 1] for i in range(0, lax.axis_size("rep"), 2)]
     both_sides = lax.all_gather(travel.pop("up"), "rep", axis=0, axis_index_groups=sides)
-    run([(1, 0), (0, 1)], *[(near, k) for k in near if k > 1], start_far(1))
     for k in range(2, steps):
         coming = [start_far(k)]
         for j in range(3, steps):
@@ -430,13 +431,13 @@
         send((last - 1, 1), sums[last - 1, 1], 1),
         send((last, 0), sums[last, 0], 2),
     )
+    send((last, 1), sums[last, 1], 3)
     shared = sums[last - 1, 0]
-    for name in ((last - 1, 1), (last, 0)):
+    for name in ((last - 1, 1), (last, 0), (last, 1)):
         shared += travel.pop(name).astype(jnp.float32)
+    shared = shared.astype(jnp.bfloat16)
+    both_sides = after(both_sides, shared)
     send("shared", shared, 2 * last - 2)
-    final = sums[last, 1].astype(jnp.bfloat16)
-    both_sides = after(both_sides, final)
-    send((last, 1), final, 2 * last + 1)
     *terms, swapped_sides = join(sums[0, 0], *travel.values(), swap_cores(both_sides))
     both_sides = pltpu.with_memory_space_constraint(both_sides, pltpu.HBM)
     return project(group, terms, both_sides, swapped_sides)

time: 174 us -> 183 us (1.052)
  the two profiles are of different devices: /device:TPU:9 before, /device:TPU:0 now
where the time goes in v9:
time: 183 us
  waiting for transfers between devices  72.3 us (40%)
  Pallas kernels  52.7 us (29%)
  starting transfers between devices  36.2 us (20%)
  between operations  13.7 us (7%)
  local copies, waits for them, and re-layouts  4.61 us (3%)
  other arithmetic  2.99 us (2%)
    ppermute x21, waiting for transfers between devices, swap_ep(): lax.ppermute(array, 'ep', [(i, i ^ mask) for i in range(lax.axis_size('ep...  55 us
    pallas_call x5, Pallas kernels, expert_apply(): pl.pallas_call(functools.partial(expert_kernel, positions, count), out_sh...  44 us
    ppermute x21, starting transfers between devices, swap_ep(): lax.ppermute(array, 'ep', [(i, i ^ mask) for i in range(lax.axis_size('ep...  29.1 us
    ppermute x2, waiting for transfers between devices, swap_reps(): lax.ppermute(array, 'rep', [(i, i ^ 1) for i in range(lax.axis_size('rep'...  7.88 us
    ppermute x21, waiting for transfers between devices, swap_cores(): return lax.ppermute(array, 'grp', [(0, 1), (1, 0)])  7 us
    pallas_call x1, Pallas kernels, project(): pl.pallas_call(project_kernel, in_specs=[in_smem] + [in_vmem] * len(terms...  4.7 us
    ppermute x21, starting transfers between devices, swap_cores(): return lax.ppermute(array, 'grp', [(0, 1), (1, 0)])  4.08 us
  transfers between devices with their start and end apart: 46, of which 18 were waited for; matrix products, arithmetic and copies ran while one was open for 2% of the time, Pallas kernels for 26%

profile of v9, /device:TPU:0, one launch (start us, length us, event | category | flops | bytes accessed | tf_op | source)
XLA Modules:
  0.0 182.5 jit_solution(7087003941880690888)
XLA Ops:
  6.5 1.2 constant_dynamic-slice_fusion.1
  7.7 3.1 %collective-permute-start = (bf16[128,1024]{1,0:T(8,128)(2,1)S(1)}, bf16[128,1024]{1,0:T(8,128)(2,1)S(1)}, u32[]{:S(2)}, u32[]{:S(2)}) collective-permute-start(bf16[128,1024]{1,0:T(8,128)(2,1)S(1)} %get-tuple-element.158.refs_2_), channel_id=1, source_target_pairs={{0,2},{1,3},{2,0},{3,1},{4,6},{5,7},{6,4},{7,5},{8,10},{9,11},{10,... | collective-permute-start | bytes 786440 | tf_op jit(solution)/shard_map/ppermute | solution.py:35
  10.8 2.6 %collective-permute-start.4 = (bf16[128,1024]{1,0:T(8,128)(2,1)S(1)}, bf16[128,1024]{1,0:T(8,128)(2,1)S(1)}, u32[]{:S(2)}, u32[]{:S(2)}) collective-permute-start(bf16[128,1024]{1,0:T(8,128)(2,1)S(1)} %get-tuple-element.158.refs_2_), channel_id=1, source_target_pairs={{0,4},{1,5},{2,6},{3,7},{4,0},{5,1},{6,2},{7,3},{8,12},{9,13},{10,... | collective-permute-start | bytes 786440 | tf_op jit(solution)/shard_map/ppermute | solution.py:35
  13.4 1.5 collective-permute-start.1
  15.0 1.2 copy-done.1
  16.2 1.6 split_columns.1
  17.8 1.5 collective-permute-start.3
  19.3 0.7 fusion.1
  20.0 2.6 %collective-permute-done.refs_6_ = bf16[128,1024]{1,0:T(8,128)(2,1)S(1)} collective-permute-done((bf16[128,1024]{1,0:T(8,128)(2,1)S(1)}, bf16[128,1024]{1,0:T(8,128)(2,1)S(1)}, u32[]{:S(2)}, u32[]{:S(2)}) %collective-permute-start) | collective-permute-done | bytes 262176 | tf_op jit(solution)/shard_map/ppermute | solution.py:35
  22.6 1.7 collective-permute-start.2
  25.0 0.7 constant_dynamic-slice_fusion
  25.7 0.7 select_reduce_fusion.weights
  26.4 3.8 %collective-permute-done.2.refs_7_ = bf16[128,1024]{1,0:T(8,128)(2,1)} collective-permute-done((bf16[128,1024]{1,0:T(8,128)(2,1)S(1)}, bf16[128,1024]{1,0:T(8,128)(2,1)}, u32[]{:S(2)}, u32[]{:S(2)}) %collective-permute-start.2) | collective-permute-done | bytes 262176 | tf_op jit(solution)/shard_map/ppermute | solution.py:35
  32.2 5.2 %collective-permute-done.5.refs_2_ = bf16[128,1024]{1,0:T(8,128)(2,1)S(1)} collective-permute-done((bf16[128,1024]{1,0:T(8,128)(2,1)S(1)}, bf16[128,1024]{1,0:T(8,128)(2,1)S(1)}, u32[]{:S(2)}, u32[]{:S(2)}) %collective-permute-start.5) | collective-permute-done | bytes 262176 | tf_op jit(solution)/shard_map/ppermute | solution.py:35
  37.4 0.7 collective-permute-start.12
  38.6 2.0 %collective-permute-done.9.refs_11_ = bf16[128,1024]{1,0:T(8,128)(2,1)S(1)} collective-permute-done((bf16[128,1024]{1,0:T(8,128)(2,1)S(1)}, bf16[128,1024]{1,0:T(8,128)(2,1)S(1)}, u32[]{:S(2)}, u32[]{:S(2)}) %collective-permute-start.9) | collective-permute-done | bytes 262176 | tf_op jit(solution)/shard_map/ppermute | solution.py:35
  41.1 7.5 %collective-permute-done.12.refs_3_ = bf16[128,1024]{1,0:T(8,128)(2,1)S(1)} collective-permute-done((bf16[128,1024]{1,0:T(8,128)(2,1)S(1)}, bf16[128,1024]{1,0:T(8,128)(2,1)S(1)}, u32[]{:S(2)}, u32[]{:S(2)}) %collective-permute-start.12) | collective-permute-done | bytes 262176 | tf_op jit(solution)/shard_map/ppermute | solution.py:35
  48.6 1.9 %down_project.2.refs_6_ = f32[256,1024]{1,0:T(8,128)S(1)} custom-call(bf16[128,2048]{1,0:T(8,128)(2,1)S(1)} %get-tuple-element.82.refs_0_, bf16[128,2048]{1,0:T(8,128)(2,1)S(1)} %collective-permute-done.3.refs_1_, bf16[128,1024]{1,0:T(8,128)(2,1)S(1)} %get-tuple-element.158.refs_2_, bf16[128,1024]{1,0:T(8,128)(2,1)S(1)} %collective-permute-done.1.refs_3_, ...), custom_call_target="tpu_custom_call" | custom-call | flops 805306368 | bytes 3145728 | tf_op jit(solution)/shard_map/down_project/pallas_call | solution.py:120
  51.0 1.6 collective-permute-start.15
  52.6 7.2 %collective-permute-done.15.arrived = bf16[128,1024]{1,0:T(8,128)(2,1)S(1)} collective-permute-done((bf16[128,1024]{1,0:T(8,128)(2,1)S(1)}, bf16[128,1024]{1,0:T(8,128)(2,1)S(1)}, u32[]{:S(2)}, u32[]{:S(2)}) %collective-permute-start.15) | collective-permute-done | bytes 262176 | tf_op jit(solution)/shard_map/ppermute | solution.py:31
  60.5 1.8 collective-permute-start.17
  62.3 6.9 %expert.5 = (bf16[128,1024]{1,0:T(8,128)(2,1)S(1)}, bf16[128,1024]{1,0:T(8,128)(2,1)S(1)}) custom-call(s32[1]{0:T(128)} %bitcast.1.where, bf16[144,1024]{1,0:T(8,128)(2,1)S(1)} %finish_latent.1.refs_0_, bf16[144,1024]{1,0:T(8,128)(2,1)S(1)} %collective-permute-done.16.refs_1_, bf16[1,1024,2048]{2,1,0:T(8,128)(2,1)} %refs_2_.3, ...), custom_call_target="tpu_custom_call" | custom-call | flops 805306368 | bytes 1048576 | tf_op jit(solution)/shard_map/expert/pallas_call | solution.py:248
  69.1 0.7 copy-done.3
  69.8 6.1 %collective-permute-done.18.refs_1_ = bf16[144,1024]{1,0:T(8,128)(2,1)S(1)} collective-permute-done((bf16[144,1024]{1,0:T(8,128)(2,1)S(1)}, bf16[144,1024]{1,0:T(8,128)(2,1)S(1)}, u32[]{:S(2)}, u32[]{:S(2)}) %collective-permute-start.18) | collective-permute-done | bytes 294944 | tf_op jit(solution)/shard_map/ppermute | solution.py:35
  75.9 1.6 collective-permute-done.17.refs_0_
  78.0 1.6 collective-permute-start.22
  80.1 10.0 %expert.6 = (bf16[128,1024]{1,0:T(8,128)(2,1)S(1)}, bf16[128,1024]{1,0:T(8,128)(2,1)S(1)}, bf16[256,1024]{1,0:T(8,128)(2,1)S(1)}) custom-call(s32[1]{0:T(128)} %bitcast.1.where, bf16[144,1024]{1,0:T(8,128)(2,1)S(1)} %collective-permute-done.17.refs_0_, bf16[144,1024]{1,0:T(8,128)(2,1)S(1)} %collective-permute-done.18.refs_1_, ...), custom_call_target="tpu_custom_call" | custom-call | flops 1610612736 | bytes 2097152 | tf_op jit(solution)/shard_map/expert/pallas_call | solution.py:248
  90.1 0.8 copy-done.2
  90.9 8.9 %collective-permute-done.22.refs_0_ = bf16[144,1024]{1,0:T(8,128)(2,1)S(1)} collective-permute-done((bf16[144,1024]{1,0:T(8,128)(2,1)S(1)}, bf16[144,1024]{1,0:T(8,128)(2,1)S(1)}, u32[]{:S(2)}, u32[]{:S(2)}) %collective-permute-start.22) | collective-permute-done | bytes 294944 | tf_op jit(solution)/shard_map/ppermute | solution.py:35
  100.4 1.3 collective-permute-start.26
  102.2 1.8 collective-permute-start.30
  104.0 0.7 collective-permute-start.29
  104.7 10.3 %expert.7 = (bf16[128,1024]{1,0:T(8,128)(2,1)S(1)}, bf16[128,1024]{1,0:T(8,128)(2,1)S(1)}, bf16[256,1024]{1,0:T(8,128)(2,1)S(1)}) custom-call(s32[1]{0:T(128)} %bitcast.1.where, bf16[144,1024]{1,0:T(8,128)(2,1)S(1)} %collective-permute-done.22.refs_0_, bf16[144,1024]{1,0:T(8,128)(2,1)S(1)} %collective-permute-done.23.refs_1_, ...), custom_call_target="tpu_custom_call" | custom-call | flops 1610612736 | bytes 2097152 | tf_op jit(solution)/shard_map/expert/pallas_call | solution.py:248
  115.2 1.4 collective-permute-start.33
  117.2 2.4 %collective-permute-start.35 = (bf16[128,1024]{1,0:T(8,128)(2,1)S(1)}, bf16[128,1024]{1,0:T(8,128)(2,1)S(1)}, u32[]{:S(2)}, u32[]{:S(2)}) collective-permute-start(bf16[128,1024]{1,0:T(8,128)(2,1)S(1)} %add_convert_fusion.4), channel_id=1, source_target_pairs={{0,3},{1,2},{2,1},{3,0},{4,7},{5,6},{6,5},{7,4},{8,11},{9,10},{10,... | collective-permute-start | bytes 786440 | tf_op jit(solution)/shard_map/ppermute | solution.py:35
  119.6 10.0 %expert.8 = (bf16[128,1024]{1,0:T(8,128)(2,1)S(1)}, bf16[128,1024]{1,0:T(8,128)(2,1)S(1)}, bf16[256,1024]{1,0:T(8,128)(2,1)S(1)}) custom-call(s32[1]{0:T(128)} %bitcast.1.where, bf16[144,1024]{1,0:T(8,128)(2,1)S(1)} %collective-permute-done.27.refs_0_, bf16[144,1024]{1,0:T(8,128)(2,1)S(1)} %collective-permute-done.26.refs_1_, ...), custom_call_target="tpu_custom_call" | custom-call | flops 1610612736 | bytes 2097152 | tf_op jit(solution)/shard_map/expert/pallas_call | solution.py:248
  130.7 1.4 collective-permute-done.37
  132.3 1.6 collective-permute-start.39
  134.0 1.3 collective-permute-start.38
  135.3 6.9 %expert.9 = (bf16[128,1024]{1,0:T(8,128)(2,1)S(1)}, bf16[128,1024]{1,0:T(8,128)(2,1)S(1)}) custom-call(s32[1]{0:T(128)} %bitcast.1.where, bf16[144,1024]{1,0:T(8,128)(2,1)S(1)} %collective-permute-done.33.refs_0_, bf16[144,1024]{1,0:T(8,128)(2,1)S(1)} %collective-permute-done.36.refs_1_, bf16[1,1024,2048]{2,1,0:T(8,128)(2,1)} %refs_2_.3, ...), custom_call_target="tpu_custom_call" | custom-call | flops 805306368 | bytes 1048576 | tf_op jit(solution)/shard_map/expert/pallas_call | solution.py:248
  142.3 1.5 collective-permute-done.40
  143.9 1.0 collective-permute-start.41
  144.9 8.3 %collective-permute-done.41 = bf16[128,1024]{1,0:T(8,128)(2,1)S(1)} collective-permute-done((bf16[128,1024]{1,0:T(8,128)(2,1)S(1)}, bf16[128,1024]{1,0:T(8,128)(2,1)S(1)}, u32[]{:S(2)}, u32[]{:S(2)}) %collective-permute-start.41) | collective-permute-done | bytes 262176 | tf_op jit(solution)/shard_map/ppermute | solution.py:35
  153.4 2.3 %all-gather.7.cloned.1.call-done = bf16[16,256,512]{2,1,0:T(8,128)(2,1)} async-done(((bf16[8,256,512]{2,1,0:T(8,128)(2,1)}), bf16[16,256,512]{2,1,0:T(8,128)(2,1)}) %all-gather.7.cloned.1.call-update) | async-done | bytes 4194320 | tf_op jit(solution)/shard_map/all_gather | solution.py:420
  156.2 2.4 %collective-permute-start.42 = (bf16[128,1024]{1,0:T(8,128)(2,1)S(1)}, bf16[128,1024]{1,0:T(8,128)(2,1)S(1)}, u32[]{:S(2)}, u32[]{:S(2)}) collective-permute-start(bf16[128,1024]{1,0:T(8,128)(2,1)S(1)} %add_convert_fusion), channel_id=1, source_target_pairs={{0,4},{1,5},{2,6},{3,7},{4,0},{5,1},{6,2},{7,3},{8,12},{9,13},{10,... | collective-permute-start | bytes 786440 | tf_op jit(solution)/shard_map/ppermute | solution.py:35
  158.7 3.7 %collective-permute-done.19 = bf16[128,1024]{1,0:T(8,128)(2,1)S(1)} collective-permute-done((bf16[128,1024]{1,0:T(8,128)(2,1)S(1)}, bf16[128,1024]{1,0:T(8,128)(2,1)S(1)}, u32[]{:S(2)}, u32[]{:S(2)}) %collective-permute-start.19) | collective-permute-done | bytes 262176 | tf_op jit(solution)/shard_map/ppermute | solution.py:27
  162.4 8.5 %collective-permute-done.42.refs_4_ = bf16[128,1024]{1,0:T(8,128)(2,1)S(1)} collective-permute-done((bf16[128,1024]{1,0:T(8,128)(2,1)S(1)}, bf16[128,1024]{1,0:T(8,128)(2,1)S(1)}, u32[]{:S(2)}, u32[]{:S(2)}) %collective-permute-start.42) | collective-permute-done | bytes 262176 | tf_op jit(solution)/shard_map/ppermute | solution.py:35
  171.0 4.7 %project.1 = bf16[128,4096]{1,0:T(8,128)(2,1)} custom-call(s32[1]{0:T(128)} %bitcast.where, f32[128,1024]{1,0:T(8,128)S(1)} %convert_add_fusion.refs_0_, bf16[128,1024]{1,0:T(8,128)(2,1)S(1)} %collective-permute-done.29.refs_1_, bf16[128,1024]{1,0:T(8,128)(2,1)S(1)} %collective-permute-done.30.refs_2_, ...), custom_call_target="tpu_custom_call" | custom-call | flops 1073741824 | bytes 8388608 | tf_op jit(solution)/shard_map/project/pallas_call | solution.py:310
  (78 shorter events, 10.0 us)
Async XLA Ops:
  6.5 18.4 %copy-start = (bf16[1024,512]{1,0:T(8,128)(2,1)S(1)}, bf16[1024,512]{1,0:T(8,128)(2,1)}, u32[]{:S(2)}) copy-start(bf16[1024,512]{1,0:T(8,128)(2,1)} %param.15) | copy-start | bytes 3145732
  6.5 93.2 %all-gather.5.cloned.1.call-start = ((), (), s32[]{:S(2)}) async-start(), calls=%async_computation | async-start | bytes 2359296 | tf_op jit(solution)/shard_map/all_gather | solution.py:366
  7.7 14.9 %collective-permute-start = (bf16[128,1024]{1,0:T(8,128)(2,1)S(1)}, bf16[128,1024]{1,0:T(8,128)(2,1)S(1)}, u32[]{:S(2)}, u32[]{:S(2)}) collective-permute-start(bf16[128,1024]{1,0:T(8,128)(2,1)S(1)} %get-tuple-element.158.refs_2_), channel_id=1, source_target_pairs={{0,2},{1,3},{2,0},{3,1},{4,6},{5,7},{6,4},{7,5},{8,10},{9,11},{10,... | collective-permute-start | bytes 786440 | tf_op jit(solution)/shard_map/ppermute | solution.py:35
  10.8 15.6 %collective-permute-start.4 = (bf16[128,1024]{1,0:T(8,128)(2,1)S(1)}, bf16[128,1024]{1,0:T(8,128)(2,1)S(1)}, u32[]{:S(2)}, u32[]{:S(2)}) collective-permute-start(bf16[128,1024]{1,0:T(8,128)(2,1)S(1)} %get-tuple-element.158.refs_2_), channel_id=1, source_target_pairs={{0,4},{1,5},{2,6},{3,7},{4,0},{5,1},{6,2},{7,3},{8,12},{9,13},{10,... | collective-permute-start | bytes 786440 | tf_op jit(solution)/shard_map/ppermute | solution.py:35
  13.4 13.1 %collective-permute-start.1 = (bf16[128,1024]{1,0:T(8,128)(2,1)S(1)}, bf16[128,1024]{1,0:T(8,128)(2,1)S(1)}, u32[]{:S(2)}, u32[]{:S(2)}) collective-permute-start(bf16[128,1024]{1,0:T(8,128)(2,1)S(1)} %get-tuple-element.158.refs_2_), channel_id=1, source_target_pairs={{0,1},{1,0},{2,3},{3,2},{4,5},{5,4},{6,7},{7,6},{8,9},{9,8},{10,11... | collective-permute-start | bytes 786440 | tf_op jit(solution)/shard_map/ppermute | solution.py:35
  17.8 13.0 %collective-permute-start.3 = (bf16[128,2048]{1,0:T(8,128)(2,1)}, bf16[128,2048]{1,0:T(8,128)(2,1)S(1)}, u32[]{:S(2)}, u32[]{:S(2)}) collective-permute-start(bf16[128,2048]{1,0:T(8,128)(2,1)} %get-tuple-element.84), channel_id=1, source_target_pairs={{0,16},{16,0},{1,17},{17,1},{2,18},{18,2},{3,19},{19,3},{4,20},{20... | collective-permute-start | bytes 1572872 | tf_op jit(solution)/shard_map/ppermute | solution.py:31
  22.6 7.6 %collective-permute-start.2 = (bf16[128,1024]{1,0:T(8,128)(2,1)S(1)}, bf16[128,1024]{1,0:T(8,128)(2,1)}, u32[]{:S(2)}, u32[]{:S(2)}) collective-permute-start(bf16[128,1024]{1,0:T(8,128)(2,1)S(1)} %collective-permute-done.refs_6_), channel_id=1, source_target_pairs={{0,1},{1,0},{2,3},{3,2},{4,5},{5,4},{6,7},{7,6},{8,9},{9,8},{10,11... | collective-permute-start | bytes 786440 | tf_op jit(solution)/shard_map/ppermute | solution.py:35
  30.9 124.9 %all-gather.7.cloned.1.call-start = ((), (), s32[]{:S(2)}) async-start(), calls=%async_computation.1 | async-start | bytes 6291456 | tf_op jit(solution)/shard_map/all_gather | solution.py:420
  30.9 6.5 %collective-permute-start.5 = (bf16[128,1024]{1,0:T(8,128)(2,1)S(1)}, bf16[128,1024]{1,0:T(8,128)(2,1)S(1)}, u32[]{:S(2)}, u32[]{:S(2)}) collective-permute-start(bf16[128,1024]{1,0:T(8,128)(2,1)S(1)} %collective-permute-done.4.refs_10_), channel_id=1, source_target_pairs={{0,2},{1,3},{2,0},{3,1},{4,6},{5,7},{6,4},{7,5},{8,10},{9,11},{10,... | collective-permute-start | bytes 786440 | tf_op jit(solution)/shard_map/ppermute | solution.py:35
  31.4 6.6 %collective-permute-start.7 = (bf16[128,1024]{1,0:T(8,128)(2,1)S(1)}, bf16[128,1024]{1,0:T(8,128)(2,1)S(1)}, u32[]{:S(2)}, u32[]{:S(2)}) collective-permute-start(bf16[128,1024]{1,0:T(8,128)(2,1)S(1)} %collective-permute-done.refs_6_), channel_id=1, source_target_pairs={{0,8},{8,0},{1,9},{9,1},{2,10},{10,2},{3,11},{11,3},{4,12},{12,4},... | collective-permute-start | bytes 786440 | tf_op jit(solution)/shard_map/ppermute | solution.py:27
  31.4 9.1 %collective-permute-start.9 = (bf16[128,1024]{1,0:T(8,128)(2,1)S(1)}, bf16[128,1024]{1,0:T(8,128)(2,1)S(1)}, u32[]{:S(2)}, u32[]{:S(2)}) collective-permute-start(bf16[128,1024]{1,0:T(8,128)(2,1)S(1)} %collective-permute-done.4.refs_10_), channel_id=1, source_target_pairs={{0,1},{1,0},{2,3},{3,2},{4,5},{5,4},{6,7},{7,6},{8,9},{9,8},{10,11... | collective-permute-start | bytes 786440 | tf_op jit(solution)/shard_map/ppermute | solution.py:35
  31.9 8.6 %collective-permute-start.6 = (bf16[128,1024]{1,0:T(8,128)(2,1)S(1)}, bf16[128,1024]{1,0:T(8,128)(2,1)S(1)}, u32[]{:S(2)}, u32[]{:S(2)}) collective-permute-start(bf16[128,1024]{1,0:T(8,128)(2,1)S(1)} %collective-permute-done.1.refs_3_), channel_id=1, source_target_pairs={{0,8},{8,0},{1,9},{9,1},{2,10},{10,2},{3,11},{11,3},{4,12},{12,4},... | collective-permute-start | bytes 786440 | tf_op jit(solution)/shard_map/ppermute | solution.py:27
  37.4 11.2 %collective-permute-start.12 = (bf16[128,1024]{1,0:T(8,128)(2,1)S(1)}, bf16[128,1024]{1,0:T(8,128)(2,1)S(1)}, u32[]{:S(2)}, u32[]{:S(2)}) collective-permute-start(bf16[128,1024]{1,0:T(8,128)(2,1)S(1)} %collective-permute-done.5.refs_2_), channel_id=1, source_target_pairs={{0,1},{1,0},{2,3},{3,2},{4,5},{5,4},{6,7},{7,6},{8,9},{9,8},{10,11... | collective-permute-start | bytes 786440 | tf_op jit(solution)/shard_map/ppermute | solution.py:35
  38.1 10.5 %collective-permute-start.10 = (bf16[128,1024]{1,0:T(8,128)(2,1)S(1)}, bf16[128,1024]{1,0:T(8,128)(2,1)S(1)}, u32[]{:S(2)}, u32[]{:S(2)}) collective-permute-start(bf16[128,1024]{1,0:T(8,128)(2,1)S(1)} %collective-permute-done.4.refs_10_), channel_id=1, source_target_pairs={{0,8},{8,0},{1,9},{9,1},{2,10},{10,2},{3,11},{11,3},{4,12},{12,4},... | collective-permute-start | bytes 786440 | tf_op jit(solution)/shard_map/ppermute | solution.py:27
  38.1 10.5 %collective-permute-start.8 = (bf16[128,1024]{1,0:T(8,128)(2,1)}, bf16[128,1024]{1,0:T(8,128)(2,1)S(1)}, u32[]{:S(2)}, u32[]{:S(2)}) collective-permute-start(bf16[128,1024]{1,0:T(8,128)(2,1)} %collective-permute-done.2.refs_7_), channel_id=1, source_target_pairs={{0,8},{8,0},{1,9},{9,1},{2,10},{10,2},{3,11},{11,3},{4,12},{12,4},... | collective-permute-start | bytes 786440 | tf_op jit(solution)/shard_map/ppermute | solution.py:27
  40.5 8.1 %collective-permute-start.11 = (bf16[128,1024]{1,0:T(8,128)(2,1)S(1)}, bf16[128,1024]{1,0:T(8,128)(2,1)S(1)}, u32[]{:S(2)}, u32[]{:S(2)}) collective-permute-start(bf16[128,1024]{1,0:T(8,128)(2,1)S(1)} %collective-permute-done.9.refs_11_), channel_id=1, source_target_pairs={{0,8},{8,0},{1,9},{9,1},{2,10},{10,2},{3,11},{11,3},{4,12},{12,4},... | collective-permute-start | bytes 786440 | tf_op jit(solution)/shard_map/ppermute | solution.py:27
  40.6 10.0 %collective-permute-start.13 = (bf16[128,1024]{1,0:T(8,128)(2,1)S(1)}, bf16[128,1024]{1,0:T(8,128)(2,1)S(1)}, u32[]{:S(2)}, u32[]{:S(2)}) collective-permute-start(bf16[128,1024]{1,0:T(8,128)(2,1)S(1)} %collective-permute-done.5.refs_2_), channel_id=1, source_target_pairs={{0,8},{8,0},{1,9},{9,1},{2,10},{10,2},{3,11},{11,3},{4,12},{12,4},... | collective-permute-start | bytes 786440 | tf_op jit(solution)/shard_map/ppermute | solution.py:27
  48.6 2.0 %collective-permute-start.14 = (bf16[128,1024]{1,0:T(8,128)(2,1)S(1)}, bf16[128,1024]{1,0:T(8,128)(2,1)S(1)}, u32[]{:S(2)}, u32[]{:S(2)}) collective-permute-start(bf16[128,1024]{1,0:T(8,128)(2,1)S(1)} %collective-permute-done.12.refs_3_), channel_id=1, source_target_pairs={{0,8},{8,0},{1,9},{9,1},{2,10},{10,2},{3,11},{11,3},{4,12},{12,4},... | collective-permute-start | bytes 786440 | tf_op jit(solution)/shard_map/ppermute | solution.py:27
  51.0 8.8 %collective-permute-start.15 = (bf16[128,1024]{1,0:T(8,128)(2,1)S(1)}, bf16[128,1024]{1,0:T(8,128)(2,1)S(1)}, u32[]{:S(2)}, u32[]{:S(2)}) collective-permute-start(bf16[128,1024]{1,0:T(8,128)(2,1)S(1)} %get-tuple-element.92), channel_id=1, source_target_pairs={{0,16},{16,0},{1,17},{17,1},{2,18},{18,2},{3,19},{19,3},{4,20},{20... | collective-permute-start | bytes 786440 | tf_op jit(solution)/shard_map/ppermute | solution.py:31
  59.8 2.4 %collective-permute-start.16 = (bf16[144,1024]{1,0:T(8,128)(2,1)S(1)}, bf16[144,1024]{1,0:T(8,128)(2,1)S(1)}, u32[]{:S(2)}, u32[]{:S(2)}) collective-permute-start(bf16[144,1024]{1,0:T(8,128)(2,1)S(1)} %finish_latent.1.refs_0_), channel_id=1, source_target_pairs={{0,8},{8,0},{1,9},{9,1},{2,10},{10,2},{3,11},{11,3},{4,12},{12,4},... | collective-permute-start | bytes 884744 | tf_op jit(solution)/shard_map/ppermute | solution.py:27
  59.9 16.0 %collective-permute-start.18 = (bf16[144,1024]{1,0:T(8,128)(2,1)S(1)}, bf16[144,1024]{1,0:T(8,128)(2,1)S(1)}, u32[]{:S(2)}, u32[]{:S(2)}) collective-permute-start(bf16[144,1024]{1,0:T(8,128)(2,1)S(1)} %finish_latent.1.refs_0_), channel_id=1, source_target_pairs={{0,1},{1,0},{2,3},{3,2},{4,5},{5,4},{6,7},{7,6},{8,9},{9,8},{10,11... | collective-permute-start | bytes 884744 | tf_op jit(solution)/shard_map/ppermute | solution.py:35
  60.5 17.0 %collective-permute-start.17 = (bf16[144,1024]{1,0:T(8,128)(2,1)S(1)}, bf16[144,1024]{1,0:T(8,128)(2,1)S(1)}, u32[]{:S(2)}, u32[]{:S(2)}) collective-permute-start(bf16[144,1024]{1,0:T(8,128)(2,1)S(1)} %finish_latent.1.refs_0_), channel_id=1, source_target_pairs={{0,2},{1,3},{2,0},{3,1},{4,6},{5,7},{6,4},{7,5},{8,10},{9,11},{10,... | collective-permute-start | bytes 884744 | tf_op jit(solution)/shard_map/ppermute | solution.py:35
  77.5 2.6 %collective-permute-start.21 = (bf16[144,1024]{1,0:T(8,128)(2,1)S(1)}, bf16[144,1024]{1,0:T(8,128)(2,1)S(1)}, u32[]{:S(2)}, u32[]{:S(2)}) collective-permute-start(bf16[144,1024]{1,0:T(8,128)(2,1)S(1)} %collective-permute-done.18.refs_1_), channel_id=1, source_target_pairs={{0,8},{8,0},{1,9},{9,1},{2,10},{10,2},{3,11},{11,3},{4,12},{12,4},... | collective-permute-start | bytes 884744 | tf_op jit(solution)/shard_map/ppermute | solution.py:27
  77.5 2.6 %collective-permute-start.20 = (bf16[144,1024]{1,0:T(8,128)(2,1)S(1)}, bf16[144,1024]{1,0:T(8,128)(2,1)S(1)}, u32[]{:S(2)}, u32[]{:S(2)}) collective-permute-start(bf16[144,1024]{1,0:T(8,128)(2,1)S(1)} %collective-permute-done.17.refs_0_), channel_id=1, source_target_pairs={{0,8},{8,0},{1,9},{9,1},{2,10},{10,2},{3,11},{11,3},{4,12},{12,4},... | collective-permute-start | bytes 884744 | tf_op jit(solution)/shard_map/ppermute | solution.py:27
  78.0 21.8 %collective-permute-start.22 = (bf16[144,1024]{1,0:T(8,128)(2,1)S(1)}, bf16[144,1024]{1,0:T(8,128)(2,1)S(1)}, u32[]{:S(2)}, u32[]{:S(2)}) collective-permute-start(bf16[144,1024]{1,0:T(8,128)(2,1)S(1)} %finish_latent.1.refs_0_), channel_id=1, source_target_pairs={{0,4},{1,5},{2,6},{3,7},{4,0},{5,1},{6,2},{7,3},{8,12},{9,13},{10,... | collective-permute-start | bytes 884744 | tf_op jit(solution)/shard_map/ppermute | solution.py:35
  79.7 20.1 %collective-permute-start.23 = (bf16[144,1024]{1,0:T(8,128)(2,1)S(1)}, bf16[144,1024]{1,0:T(8,128)(2,1)S(1)}, u32[]{:S(2)}, u32[]{:S(2)}) collective-permute-start(bf16[144,1024]{1,0:T(8,128)(2,1)S(1)} %collective-permute-done.17.refs_0_), channel_id=1, source_target_pairs={{0,1},{1,0},{2,3},{3,2},{4,5},{5,4},{6,7},{7,6},{8,9},{9,8},{10,11... | collective-permute-start | bytes 884744 | tf_op jit(solution)/shard_map/ppermute | solution.py:35
  99.8 2.2 %collective-permute-start.28 = (bf16[256,1024]{1,0:T(8,128)(2,1)}, bf16[256,1024]{1,0:T(8,128)(2,1)S(1)}, u32[]{:S(2)}, u32[]{:S(2)}) collective-permute-start(bf16[256,1024]{1,0:T(8,128)(2,1)} %copy-done.2), channel_id=1, source_target_pairs={{0,8},{8,0},{1,9},{9,1},{2,10},{10,2},{3,11},{11,3},{4,12},{12,4},... | collective-permute-start | bytes 1572872 | tf_op jit(solution)/shard_map/ppermute | solution.py:27
  99.9 4.1 %collective-permute-start.25 = (bf16[144,1024]{1,0:T(8,128)(2,1)S(1)}, bf16[144,1024]{1,0:T(8,128)(2,1)S(1)}, u32[]{:S(2)}, u32[]{:S(2)}) collective-permute-start(bf16[144,1024]{1,0:T(8,128)(2,1)S(1)} %collective-permute-done.23.refs_1_), channel_id=1, source_target_pairs={{0,8},{8,0},{1,9},{9,1},{2,10},{10,2},{3,11},{11,3},{4,12},{12,4},... | collective-permute-start | bytes 884744 | tf_op jit(solution)/shard_map/ppermute | solution.py:27
  100.4 14.7 %collective-permute-start.27 = (bf16[144,1024]{1,0:T(8,128)(2,1)S(1)}, bf16[144,1024]{1,0:T(8,128)(2,1)S(1)}, u32[]{:S(2)}, u32[]{:S(2)}) collective-permute-start(bf16[144,1024]{1,0:T(8,128)(2,1)S(1)} %collective-permute-done.22.refs_0_), channel_id=1, source_target_pairs={{0,2},{1,3},{2,0},{3,1},{4,6},{5,7},{6,4},{7,5},{8,10},{9,11},{10,... | collective-permute-start | bytes 884744 | tf_op jit(solution)/shard_map/ppermute | solution.py:35
  100.4 14.7 %collective-permute-start.26 = (bf16[144,1024]{1,0:T(8,128)(2,1)S(1)}, bf16[144,1024]{1,0:T(8,128)(2,1)S(1)}, u32[]{:S(2)}, u32[]{:S(2)}) collective-permute-start(bf16[144,1024]{1,0:T(8,128)(2,1)S(1)} %collective-permute-done.22.refs_0_), channel_id=1, source_target_pairs={{0,1},{1,0},{2,3},{3,2},{4,5},{5,4},{6,7},{7,6},{8,9},{9,8},{10,11... | collective-permute-start | bytes 884744 | tf_op jit(solution)/shard_map/ppermute | solution.py:35
  101.7 3.0 %collective-permute-start.24 = (bf16[144,1024]{1,0:T(8,128)(2,1)S(1)}, bf16[144,1024]{1,0:T(8,128)(2,1)S(1)}, u32[]{:S(2)}, u32[]{:S(2)}) collective-permute-start(bf16[144,1024]{1,0:T(8,128)(2,1)S(1)} %collective-permute-done.22.refs_0_), channel_id=1, source_target_pairs={{0,8},{8,0},{1,9},{9,1},{2,10},{10,2},{3,11},{11,3},{4,12},{12,4},... | collective-permute-start | bytes 884744 | tf_op jit(solution)/shard_map/ppermute | solution.py:27
  102.2 12.9 %collective-permute-start.30 = (bf16[128,1024]{1,0:T(8,128)(2,1)S(1)}, bf16[128,1024]{1,0:T(8,128)(2,1)S(1)}, u32[]{:S(2)}, u32[]{:S(2)}) collective-permute-start(bf16[128,1024]{1,0:T(8,128)(2,1)S(1)} %get-tuple-element.161), channel_id=1, source_target_pairs={{0,2},{1,3},{2,0},{3,1},{4,6},{5,7},{6,4},{7,5},{8,10},{9,11},{10,... | collective-permute-start | bytes 786440 | tf_op jit(solution)/shard_map/ppermute | solution.py:35
  104.0 11.1 %collective-permute-start.29 = (bf16[128,1024]{1,0:T(8,128)(2,1)S(1)}, bf16[128,1024]{1,0:T(8,128)(2,1)S(1)}, u32[]{:S(2)}, u32[]{:S(2)}) collective-permute-start(bf16[128,1024]{1,0:T(8,128)(2,1)S(1)} %get-tuple-element.162), channel_id=1, source_target_pairs={{0,1},{1,0},{2,3},{3,2},{4,5},{5,4},{6,7},{7,6},{8,9},{9,8},{10,11... | collective-permute-start | bytes 786440 | tf_op jit(solution)/shard_map/ppermute | solution.py:35
  115.1 2.0 %collective-permute-start.34 = (bf16[256,1024]{1,0:T(8,128)(2,1)S(1)}, bf16[256,1024]{1,0:T(8,128)(2,1)S(1)}, u32[]{:S(2)}, u32[]{:S(2)}) collective-permute-start(bf16[256,1024]{1,0:T(8,128)(2,1)S(1)} %get-tuple-element.134), channel_id=1, source_target_pairs={{0,8},{8,0},{1,9},{9,1},{2,10},{10,2},{3,11},{11,3},{4,12},{12,4},... | collective-permute-start | bytes 1572872 | tf_op jit(solution)/shard_map/ppermute | solution.py:27
  115.2 15.0 %collective-permute-start.33 = (bf16[144,1024]{1,0:T(8,128)(2,1)S(1)}, bf16[144,1024]{1,0:T(8,128)(2,1)S(1)}, u32[]{:S(2)}, u32[]{:S(2)}) collective-permute-start(bf16[144,1024]{1,0:T(8,128)(2,1)S(1)} %collective-permute-done.27.refs_0_), channel_id=1, source_target_pairs={{0,1},{1,0},{2,3},{3,2},{4,5},{5,4},{6,7},{7,6},{8,9},{9,8},{10,11... | collective-permute-start | bytes 884744 | tf_op jit(solution)/shard_map/ppermute | solution.py:35
  116.6 3.0 %collective-permute-start.31 = (bf16[144,1024]{1,0:T(8,128)(2,1)S(1)}, bf16[144,1024]{1,0:T(8,128)(2,1)S(1)}, u32[]{:S(2)}, u32[]{:S(2)}) collective-permute-start(bf16[144,1024]{1,0:T(8,128)(2,1)S(1)} %collective-permute-done.27.refs_0_), channel_id=1, source_target_pairs={{0,8},{8,0},{1,9},{9,1},{2,10},{10,2},{3,11},{11,3},{4,12},{12,4},... | collective-permute-start | bytes 884744 | tf_op jit(solution)/shard_map/ppermute | solution.py:27
  116.7 2.8 %collective-permute-start.32 = (bf16[144,1024]{1,0:T(8,128)(2,1)S(1)}, bf16[144,1024]{1,0:T(8,128)(2,1)S(1)}, u32[]{:S(2)}, u32[]{:S(2)}) collective-permute-start(bf16[144,1024]{1,0:T(8,128)(2,1)S(1)} %collective-permute-done.26.refs_1_), channel_id=1, source_target_pairs={{0,8},{8,0},{1,9},{9,1},{2,10},{10,2},{3,11},{11,3},{4,12},{12,4},... | collective-permute-start | bytes 884744 | tf_op jit(solution)/shard_map/ppermute | solution.py:27
  117.2 13.1 %collective-permute-start.35 = (bf16[128,1024]{1,0:T(8,128)(2,1)S(1)}, bf16[128,1024]{1,0:T(8,128)(2,1)S(1)}, u32[]{:S(2)}, u32[]{:S(2)}) collective-permute-start(bf16[128,1024]{1,0:T(8,128)(2,1)S(1)} %add_convert_fusion.4), channel_id=1, source_target_pairs={{0,3},{1,2},{2,1},{3,0},{4,7},{5,6},{6,5},{7,4},{8,11},{9,10},{10,... | collective-permute-start | bytes 786440 | tf_op jit(solution)/shard_map/ppermute | solution.py:35
  130.2 1.9 %collective-permute-start.37 = (bf16[256,1024]{1,0:T(8,128)(2,1)S(1)}, bf16[256,1024]{1,0:T(8,128)(2,1)S(1)}, u32[]{:S(2)}, u32[]{:S(2)}) collective-permute-start(bf16[256,1024]{1,0:T(8,128)(2,1)S(1)} %get-tuple-element.143), channel_id=1, source_target_pairs={{0,8},{8,0},{1,9},{9,1},{2,10},{10,2},{3,11},{11,3},{4,12},{12,4},... | collective-permute-start | bytes 1572872 | tf_op jit(solution)/shard_map/ppermute | solution.py:27
  130.2 5.1 %collective-permute-start.36 = (bf16[144,1024]{1,0:T(8,128)(2,1)S(1)}, bf16[144,1024]{1,0:T(8,128)(2,1)S(1)}, u32[]{:S(2)}, u32[]{:S(2)}) collective-permute-start(bf16[144,1024]{1,0:T(8,128)(2,1)S(1)} %collective-permute-done.33.refs_0_), channel_id=1, source_target_pairs={{0,8},{8,0},{1,9},{9,1},{2,10},{10,2},{3,11},{11,3},{4,12},{12,4},... | collective-permute-start | bytes 884744 | tf_op jit(solution)/shard_map/ppermute | solution.py:27
  132.3 9.8 %collective-permute-start.39 = (bf16[128,1024]{1,0:T(8,128)(2,1)S(1)}, bf16[128,1024]{1,0:T(8,128)(2,1)S(1)}, u32[]{:S(2)}, u32[]{:S(2)}) collective-permute-start(bf16[128,1024]{1,0:T(8,128)(2,1)S(1)} %get-tuple-element.159), channel_id=1, source_target_pairs={{0,2},{1,3},{2,0},{3,1},{4,6},{5,7},{6,4},{7,5},{8,10},{9,11},{10,... | collective-permute-start | bytes 786440 | tf_op jit(solution)/shard_map/ppermute | solution.py:35
  134.0 21.8 %copy-start.4 = (bf16[128,1024]{1,0:T(8,128)(2,1)S(1)}, bf16[128,1024]{1,0:T(8,128)(2,1)}, u32[]{:S(2)}) copy-start(bf16[128,1024]{1,0:T(8,128)(2,1)} %copy-done.3) | copy-start | bytes 786436
  134.0 8.2 %collective-permute-start.38 = (bf16[128,1024]{1,0:T(8,128)(2,1)S(1)}, bf16[128,1024]{1,0:T(8,128)(2,1)S(1)}, u32[]{:S(2)}, u32[]{:S(2)}) collective-permute-start(bf16[128,1024]{1,0:T(8,128)(2,1)S(1)} %get-tuple-element.160), channel_id=1, source_target_pairs={{0,1},{1,0},{2,3},{3,2},{4,5},{5,4},{6,7},{7,6},{8,9},{9,8},{10,11... | collective-permute-start | bytes 786440 | tf_op jit(solution)/shard_map/ppermute | solution.py:35
  142.2 1.6 collective-permute-start.40
  143.9 9.3 %collective-permute-start.41 = (bf16[128,1024]{1,0:T(8,128)(2,1)S(1)}, bf16[128,1024]{1,0:T(8,128)(2,1)S(1)}, u32[]{:S(2)}, u32[]{:S(2)}) collective-permute-start(bf16[128,1024]{1,0:T(8,128)(2,1)S(1)} %add_convert_fusion.1), channel_id=1, source_target_pairs={{0,3},{1,2},{2,1},{3,0},{4,7},{5,6},{6,5},{7,4},{8,11},{9,10},{10,... | collective-permute-start | bytes 786440 | tf_op jit(solution)/shard_map/ppermute | solution.py:35
  155.7 15.2 %collective-permute-start.43 = (bf16[2,8,256,512]{3,2,1,0:T(8,128)(2,1)}, bf16[2,8,256,512]{3,2,1,0:T(8,128)(2,1)S(1)}, u32[]{:S(2)}, u32[]{:S(2)}) collective-permute-start(bf16[2,8,256,512]{3,2,1,0:T(8,128)(2,1)} %bitcast.6), channel_id=1, source_target_pairs={{0,8},{8,0},{1,9},{9,1},{2,10},{10,2},{3,11},{11,3},{4,12},{12,4},... | collective-permute-start | bytes 12582920 | tf_op jit(solution)/shard_map/ppermute | solution.py:27
  155.7 6.6 %collective-permute-start.19 = (bf16[128,1024]{1,0:T(8,128)(2,1)S(1)}, bf16[128,1024]{1,0:T(8,128)(2,1)S(1)}, u32[]{:S(2)}, u32[]{:S(2)}) collective-permute-start(bf16[128,1024]{1,0:T(8,128)(2,1)S(1)} %copy-done.4), channel_id=1, source_target_pairs={{0,8},{8,0},{1,9},{9,1},{2,10},{10,2},{3,11},{11,3},{4,12},{12,4},... | collective-permute-start | bytes 786440 | tf_op jit(solution)/shard_map/ppermute | solution.py:27
  156.2 14.7 %collective-permute-start.42 = (bf16[128,1024]{1,0:T(8,128)(2,1)S(1)}, bf16[128,1024]{1,0:T(8,128)(2,1)S(1)}, u32[]{:S(2)}, u32[]{:S(2)}) collective-permute-start(bf16[128,1024]{1,0:T(8,128)(2,1)S(1)} %add_convert_fusion), channel_id=1, source_target_pairs={{0,4},{1,5},{2,6},{3,7},{4,0},{5,1},{6,2},{7,3},{8,12},{9,13},{10,... | collective-permute-start | bytes 786440 | tf_op jit(solution)/shard_map/ppermute | solution.py:35
  (3 other events, 2.7 us)
Sparse Core Ops, SparseCore 0:
  31.0 66.0 all-gather.4
  99.9 55.7 all-gather.6

commit v10 on v9

--- a/solution.py
+++ b/solution.py
@@ -33,6 +33,12 @@
 
 def swap_ep(array, mask):
     return lax.ppermute(array, "ep", [(i, i ^ mask) for i in range(lax.axis_size("ep"))])
+
+
+def swap_both(array):
+    names, sizes = ("rep", "ep"), (lax.axis_size("rep"), lax.axis_size("ep"))
+    pairs = [(i, i ^ (sizes[1] + 1)) for i in range(sizes[0] * sizes[1])]
+    return lax.ppermute(array, names, pairs)
 
 
 def first_steps(piece, steps):
@@ -48,75 +54,74 @@
     return jnp.sum(jnp.where(named, weights.astype(jnp.float32)[None, :, :], 0.0), axis=2)
 
 
-def columns_kernel(ep_count, quarter, where, tokens, kept, given):
+def columns_kernel(steps, quarter, where, tokens, *parts):
     place, side, group = where[0], where[1], where[2]
-    for offset in range(ep_count):
+    for k in range(steps):
         for core in range(2):
-            to = pl.ds(((offset // 2 * 2 + core) * 2 + offset % 2) * quarter, quarter)
-            shard = (place ^ offset) * 4 + (group ^ core)
-            for half, part in ((side, kept), (1 - side, given)):
-                start = pl.multiple_of((shard + 2 * half) * quarter, quarter)
+            to = pl.ds((2 * k + core) * quarter, quarter)
+            for i, part in enumerate(parts):
+                shard = (place ^ (2 * k + i % 2)) * 4 + 2 * (side ^ (i // 2)) + (group ^ core)
+                start = pl.multiple_of(shard * quarter, quarter)
                 part[:, to] = tokens[:, pl.ds(start, quarter)]
 
 
 def split_columns(tokens, ep_count, quarter, place, side, group):
     count = tokens.shape[0]
+    steps = ep_count // 2
     if quarter % 128 == 0:
-        half = jax.ShapeDtypeStruct((count, 2 * ep_count * quarter), tokens.dtype)
+        part = jax.ShapeDtypeStruct((count, 2 * steps * quarter), tokens.dtype)
         return pl.pallas_call(
-            functools.partial(columns_kernel, ep_count, quarter),
-            out_shape=(half, half),
+            functools.partial(columns_kernel, steps, quarter),
+            out_shape=(part,) * 4,
             in_specs=[in_smem, in_vmem],
-            out_specs=(in_vmem, in_vmem),
+            out_specs=(in_vmem,) * 4,
             compiler_params=pltpu.CompilerParams(vmem_limit_bytes=8 * mebi),
             name="split_columns",
         )(jnp.stack([place, side, group]).astype(jnp.int32), tokens)
     cut = tokens.reshape(count, ep_count, 2, 2, quarter)
-    parts = [], []
-    for step in range(ep_count // 2):
-        for core in (group, 1 - group):
-            for offset in (2 * step, 2 * step + 1):
-                for half, part in zip((side, 1 - side), parts):
-                    start = (0, place ^ offset, half, core, 0)
-                    part.append(lax.dynamic_slice(cut, start, (count, 1, 1, 1, quarter)))
-    kept, given = [jnp.stack(part, axis=1).reshape(count, -1) for part in parts]
-    return kept, given
+    parts = []
+    for i in range(4):
+        columns = []
+        for k in range(steps):
+            for core in (group, 1 - group):
+                start = (0, place ^ (2 * k + i % 2), side ^ (i // 2), core, 0)
+                columns.append(lax.dynamic_slice(cut, start, (count, 1, 1, 1, quarter)))
+        parts.append(jnp.stack(columns, axis=1).reshape(count, -1))
+    return parts
 
 
 def down_kernel(steps, last, *refs):
-    (kept, given), blocks = refs[:2], refs[2 : 2 + 4 * len(steps)]
-    so_far, results = (refs[-3], refs[-2:]) if last else (None, refs[-1:])
+    parts, blocks = refs[:4], refs[4 : 4 + 2 * len(steps)]
+    so_far, results = (refs[-5], refs[-4:]) if last else (None, refs[-1:])
     depth = 2 * blocks[0].shape[0]
     width = 256
     for start in range(0, blocks[0].shape[1], width):
         columns = slice(start, start + width)
         total = 0.0 if so_far is None else so_far[:, columns]
         for i, step in enumerate(steps):
-            for core in range(2):
-                inner = pl.ds((2 * step + core) * depth, depth)
-                rows = jnp.concatenate([kept[:, inner], given[:, inner]], axis=0)
-                near, far = blocks[4 * i + 2 * core], blocks[4 * i + 2 * core + 1]
-                block = jnp.concatenate([near[:, columns], far[:, columns]], axis=0)
-                total += jnp.dot(rows, block, preferred_element_type=jnp.float32)
+            inner = pl.ds(step * depth, depth)
+            rows = jnp.concatenate([part[:, inner] for part in parts], axis=0)
+            block = [core[:, columns] for core in blocks[2 * i : 2 * i + 2]]
+            block = jnp.concatenate(block, axis=0)
+            total += jnp.dot(rows, block, preferred_element_type=jnp.float32)
         if last:
-            count = kept.shape[0]
-            results[0][:, columns] = total[:count]
-            results[1][:, columns] = total[count:].astype(jnp.bfloat16)
+            count = parts[0].shape[0]
+            for i, result in enumerate(results):
+                rows = total[i * count : (i + 1) * count]
+                result[:, columns] = rows.astype(result.dtype)
         else:
             results[0][:, columns] = total
 
 
-def down_project(steps, kept, given, blocks, so_far=None):
-    count, inner = kept.shape
+def down_project(steps, parts, blocks, so_far=None):
+    count = parts[0].shape[0]
     latent_width = blocks[0].shape[1]
-    operands = (kept, given, *blocks) + (() if so_far is None else (so_far,))
+    operands = (*parts, *blocks) + (() if so_far is None else (so_far,))
     if so_far is None:
-        shapes = (jax.ShapeDtypeStruct((2 * count, latent_width), jnp.float32),)
+        shapes = (jax.ShapeDtypeStruct((4 * count, latent_width), jnp.float32),)
     else:
-        shapes = (
-            jax.ShapeDtypeStruct((count, latent_width), jnp.float32),
-            jax.ShapeDtypeStruct((count, latent_width), jnp.bfloat16),
-        )
+        types = (jnp.float32, jnp.bfloat16, jnp.bfloat16, jnp.bfloat16)
+        shapes = tuple(jax.ShapeDtypeStruct((count, latent_width), t) for t in types)
     return pl.pallas_call(
         functools.partial(down_kernel, steps, so_far is not None),
         out_shape=shapes,
@@ -132,25 +137,28 @@
     )(*operands)
 
 
-def latent_kernel(own_part, arrived, weights, piece):
+def latent_kernel(own_part, *refs):
+    arrived, (weights, piece) = refs[:-2], refs[-2:]
     count = own_part.shape[0]
-    total = own_part[...] + arrived[...].astype(jnp.float32)
+    total = own_part[...]
+    for part in arrived:
+        total += part[...].astype(jnp.float32)
     piece[:count] = total.astype(jnp.bfloat16)
     extra = piece.shape[0] - count
     piece[count:] = jnp.zeros((extra, piece.shape[1]), jnp.bfloat16)
     piece[count:, :count] = weights[...]
 
 
-def finish_latent(own_part, arrived, weights):
+def finish_latent(own_part, weights, *arrived):
     count, latent_width = own_part.shape
     return pl.pallas_call(
         latent_kernel,
         out_shape=jax.ShapeDtypeStruct((count + weights.shape[0], latent_width), jnp.bfloat16),
-        in_specs=[in_vmem] * 3,
+        in_specs=[in_vmem] * (2 + len(arrived)),
         out_specs=in_vmem,
         compiler_params=pltpu.CompilerParams(vmem_limit_bytes=4 * mebi),
         name="finish_latent",
-    )(own_part, arrived, weights)
+    )(own_part, *arrived, weights)
 
 
 def expert_kernel(positions, count, where, *refs):
@@ -348,37 +356,30 @@
     def own_piece(core):
         return lax.dynamic_slice_in_dim(down_latent, (2 * side + core) * quarter, quarter, 0)
 
-    kept, given = split_columns(tokens, ep_count, quarter, place, side, group)
-    taken = swap_reps(given)
     near = first_steps(own_piece(group), steps)
-    far = {0: swap_ep(near[0], 1)}
-    near[1], kept = join(near[1], kept)
-    far[1] = swap_ep(near[1], 1)
-    weights = dense_weights(after(expert_ids, near[1]), route_scores, expert_count)
-    others = {k: near[k] for k in near if k > 1}
-    far[0], far[1], taken, weights, *arrived = join(
-        far[0], far[1], taken, weights, *others.values()
-    )
-    near.update(zip(others, arrived))
 
     inner = latent_width // 4
     up_piece = lax.dynamic_slice_in_dim(up_latent, own_quarter * inner, inner, 0)
-    mine = lax.all_gather(after(up_piece, weights), "ep", axis=0)
-
-    for k in range(2, steps):
-        if k & (k - 1):
-            low = k & -k
-            near[k] = swap_ep(near[k ^ low], 2 * low)
-        far[k] = swap_ep(near[k], 1)
+    mine = lax.all_gather(after(up_piece, near[0]), "ep", axis=0)
+
+    parts = split_columns(tokens, ep_count, quarter, place, side, group)
+    parts = [parts[0], swap_ep(parts[1], 1), swap_reps(parts[2]), swap_both(parts[3])]
+    weights = dense_weights(after(expert_ids, parts[0]), route_scores, expert_count)
+    others = {k: near[k] for k in near if k}
+    weights, *arrived = join(weights, *parts[1:], *others.values())
+    parts[1:] = arrived[:3]
+    near.update(zip(others, arrived[3:]))
+    for k in range(3, steps):
+        if k not in near:
+            near[k] = swap_ep(near[k ^ (k & -k)], 2 * (k & -k))
     blocks = []
     for k in range(steps):
-        other = own_piece(1 - group) if k == 0 else swap_cores(near[k])
-        blocks.append((near[k], far[k], other, swap_cores(far[k])))
-    early = list(range(last))
-    (partial,) = down_project(early, kept, taken, [b for k in early for b in blocks[k]])
-    late = [after(blocks[-1][0], partial), *blocks[-1][1:]]
-    own_part, sent_part = down_project([last], kept, taken, late, partial)
-    latent = finish_latent(own_part, swap_reps(sent_part), weights.astype(jnp.bfloat16))
+        blocks += [near[k], swap_cores(near[k]) if k else own_piece(1 - group)]
+    (partial,) = down_project(list(range(last)), parts, blocks[:-2])
+    late = [after(blocks[-2], partial), blocks[-1]]
+    own_part, *sent_parts = down_project([last], parts, late, partial)
+    arrived = [swap(part) for swap, part in zip((lambda a: swap_ep(a, 1), swap_reps, swap_both), sent_parts)]
+    latent = finish_latent(own_part, weights.astype(jnp.bfloat16), *arrived)
 
     expert = (group * ep_count + place).astype(jnp.int32).reshape(1)
     expert_weights = [

time: 183 us -> 180 us (0.984)
  starting transfers between devices: 36.2 us -> 30.1 us
  waiting for transfers between devices: 72.3 us -> 76.1 us
    ppermute x21 -> x19, waiting for transfers between devices: 55 us -> 64.6 us  [swap_ep(): lax.ppermute(array, 'ep', [(i, i ^ mask) for i in range(lax.axis_size('ep...]
    ppermute x2, waiting for transfers between devices: 7.88 us -> 0.01 us  [swap_reps(): lax.ppermute(array, 'rep', [(i, i ^ 1) for i in range(lax.axis_size('rep'...]
    ppermute x21 -> x19, starting transfers between devices: 29.1 us -> 22.3 us  [swap_ep(): lax.ppermute(array, 'ep', [(i, i ^ mask) for i in range(lax.axis_size('ep...]
    ppermute x21 -> x17, waiting for transfers between devices: 7 us -> 8.97 us  [swap_cores(): return lax.ppermute(array, 'grp', [(0, 1), (1, 0)])]
    ppermute x21 -> x17, starting transfers between devices: 4.08 us -> 3.33 us  [swap_cores(): return lax.ppermute(array, 'grp', [(0, 1), (1, 0)])]
  transfers between devices with their start and end apart: 46 -> 42, of which waited for: 18 -> 19; matrix products, arithmetic and copies ran while one was open for 2% -> 2% of each run, Pallas kernels for 26% -> 26%
where the time goes in v10:
time: 180 us
  waiting for transfers between devices  76.1 us (42%)
  Pallas kernels  51.1 us (28%)
  starting transfers between devices  30.1 us (17%)
  between operations  13.7 us (8%)
  local copies, waits for them, and re-layouts  5.72 us (3%)
  other arithmetic  3.01 us (2%)
    ppermute x19, waiting for transfers between devices, swap_ep(): lax.ppermute(array, 'ep', [(i, i ^ mask) for i in range(lax.axis_size('ep...  64.6 us
    pallas_call x5, Pallas kernels, expert_apply(): pl.pallas_call(functools.partial(expert_kernel, positions, count), out_sh...  44 us
    ppermute x19, starting transfers between devices, swap_ep(): lax.ppermute(array, 'ep', [(i, i ^ mask) for i in range(lax.axis_size('ep...  22.3 us
    ppermute x17, waiting for transfers between devices, swap_cores(): return lax.ppermute(array, 'grp', [(0, 1), (1, 0)])  8.97 us
    pallas_call x1, Pallas kernels, project(): pl.pallas_call(project_kernel, in_specs=[in_smem] + [in_vmem] * len(terms...  4.7 us
    unnamed x10, local copies, waits for them, and re-layouts  3.94 us
  transfers between devices with their start and end apart: 42, of which 19 were waited for; matrix products, arithmetic and copies ran while one was open for 2% of the time, Pallas kernels for 26%

profile of v10, /device:TPU:0, one launch (start us, length us, event | category | flops | bytes accessed | tf_op | source)
XLA Modules:
  0.0 179.7 jit_solution(2094447716159935584)
XLA Ops:
  6.5 1.2 copy-done
  7.8 0.7 constant_dynamic-slice_fusion
  8.5 1.1 constant_dynamic-slice_fusion.1
  9.6 4.1 %collective-permute-start.4 = (bf16[128,1024]{1,0:T(8,128)(2,1)S(1)}, bf16[128,1024]{1,0:T(8,128)(2,1)S(1)}, u32[]{:S(2)}, u32[]{:S(2)}) collective-permute-start(bf16[128,1024]{1,0:T(8,128)(2,1)S(1)} %get-tuple-element.164.refs_4_), channel_id=1, source_target_pairs={{0,4},{1,5},{2,6},{3,7},{4,0},{5,1},{6,2},{7,3},{8,12},{9,13},{10,... | collective-permute-start | bytes 786440 | tf_op jit(solution)/shard_map/ppermute | solution.py:35
  13.7 1.6 collective-permute-start.3
  15.4 1.2 copy-done.1
  16.6 0.8 split_columns.1
  17.4 1.6 collective-permute-start
  19.0 1.5 collective-permute-start.1
  21.0 0.7 fusion.1
  21.7 0.7 fusion
  22.4 0.7 select_reduce_fusion.refs_3_
  23.1 5.0 %collective-permute-done.4.refs_8_ = bf16[128,1024]{1,0:T(8,128)(2,1)S(1)} collective-permute-done((bf16[128,1024]{1,0:T(8,128)(2,1)S(1)}, bf16[128,1024]{1,0:T(8,128)(2,1)S(1)}, u32[]{:S(2)}, u32[]{:S(2)}) %collective-permute-start.4) | collective-permute-done | bytes 262176 | tf_op jit(solution)/shard_map/ppermute | solution.py:35
  28.1 5.3 %collective-permute-done.refs_1_ = bf16[128,1024]{1,0:T(8,128)(2,1)S(1)} collective-permute-done((bf16[128,1024]{1,0:T(8,128)(2,1)S(1)}, bf16[128,1024]{1,0:T(8,128)(2,1)S(1)}, u32[]{:S(2)}, u32[]{:S(2)}) %collective-permute-start) | collective-permute-done | bytes 262176 | tf_op jit(solution)/shard_map/ppermute | solution.py:35
  34.0 9.1 %collective-permute-done.5.refs_4_ = bf16[128,1024]{1,0:T(8,128)(2,1)S(1)} collective-permute-done((bf16[128,1024]{1,0:T(8,128)(2,1)S(1)}, bf16[128,1024]{1,0:T(8,128)(2,1)S(1)}, u32[]{:S(2)}, u32[]{:S(2)}) %collective-permute-start.5) | collective-permute-done | bytes 262176 | tf_op jit(solution)/shard_map/ppermute | solution.py:35
  43.1 1.0 down_project.2.refs_6_
  45.1 1.1 collective-permute-start.9
  46.2 1.5 collective-permute-start.10
  47.7 1.0 collective-permute-start.11
  48.7 15.6 %collective-permute-done.9.refs_0_ = bf16[128,1024]{1,0:T(8,128)(2,1)S(1)} collective-permute-done((bf16[128,1024]{1,0:T(8,128)(2,1)S(1)}, bf16[128,1024]{1,0:T(8,128)(2,1)S(1)}, u32[]{:S(2)}, u32[]{:S(2)}) %collective-permute-start.9) | collective-permute-done | bytes 262176 | tf_op jit(solution)/shard_map/ppermute | solution.py:35
  64.4 1.6 collective-permute-start.14
  66.1 6.8 %expert.5 = (bf16[128,1024]{1,0:T(8,128)(2,1)S(1)}, bf16[128,1024]{1,0:T(8,128)(2,1)S(1)}) custom-call(s32[1]{0:T(128)} %bitcast.1.where, bf16[144,1024]{1,0:T(8,128)(2,1)S(1)} %finish_latent.1.refs_0_, bf16[144,1024]{1,0:T(8,128)(2,1)S(1)} %collective-permute-done.12.refs_1_, bf16[1,1024,2048]{2,1,0:T(8,128)(2,1)} %refs_2_.3, ...), custom_call_target="tpu_custom_call" | custom-call | flops 805306368 | bytes 1048576 | tf_op jit(solution)/shard_map/expert/pallas_call | solution.py:256
  73.6 3.1 %collective-permute-done.14.refs_1_ = bf16[144,1024]{1,0:T(8,128)(2,1)S(1)} collective-permute-done((bf16[144,1024]{1,0:T(8,128)(2,1)S(1)}, bf16[144,1024]{1,0:T(8,128)(2,1)S(1)}, u32[]{:S(2)}, u32[]{:S(2)}) %collective-permute-start.14) | collective-permute-done | bytes 294944 | tf_op jit(solution)/shard_map/ppermute | solution.py:35
  76.7 3.7 %collective-permute-done.13.refs_0_ = bf16[144,1024]{1,0:T(8,128)(2,1)S(1)} collective-permute-done((bf16[144,1024]{1,0:T(8,128)(2,1)S(1)}, bf16[144,1024]{1,0:T(8,128)(2,1)S(1)}, u32[]{:S(2)}, u32[]{:S(2)}) %collective-permute-start.13) | collective-permute-done | bytes 294944 | tf_op jit(solution)/shard_map/ppermute | solution.py:35
  80.9 1.4 collective-permute-start.18
  82.4 10.0 %expert.6 = (bf16[128,1024]{1,0:T(8,128)(2,1)S(1)}, bf16[128,1024]{1,0:T(8,128)(2,1)S(1)}, bf16[256,1024]{1,0:T(8,128)(2,1)S(1)}) custom-call(s32[1]{0:T(128)} %bitcast.1.where, bf16[144,1024]{1,0:T(8,128)(2,1)S(1)} %collective-permute-done.13.refs_0_, bf16[144,1024]{1,0:T(8,128)(2,1)S(1)} %collective-permute-done.14.refs_1_, ...), custom_call_target="tpu_custom_call" | custom-call | flops 1610612736 | bytes 2097152 | tf_op jit(solution)/shard_map/expert/pallas_call | solution.py:256
  92.3 0.8 copy-done.2
  93.1 3.9 %collective-permute-done.18.refs_0_ = bf16[144,1024]{1,0:T(8,128)(2,1)S(1)} collective-permute-done((bf16[144,1024]{1,0:T(8,128)(2,1)S(1)}, bf16[144,1024]{1,0:T(8,128)(2,1)S(1)}, u32[]{:S(2)}, u32[]{:S(2)}) %collective-permute-start.18) | collective-permute-done | bytes 294944 | tf_op jit(solution)/shard_map/ppermute | solution.py:35
  97.6 0.9 collective-permute-start.22
  98.5 0.7 collective-permute-done.24
  99.4 1.0 collective-permute-start.26
  100.4 1.5 collective-permute-start.25
  102.0 10.4 %expert.7 = (bf16[128,1024]{1,0:T(8,128)(2,1)S(1)}, bf16[128,1024]{1,0:T(8,128)(2,1)S(1)}, bf16[256,1024]{1,0:T(8,128)(2,1)S(1)}) custom-call(s32[1]{0:T(128)} %bitcast.1.where, bf16[144,1024]{1,0:T(8,128)(2,1)S(1)} %collective-permute-done.18.refs_0_, bf16[144,1024]{1,0:T(8,128)(2,1)S(1)} %collective-permute-done.19.refs_1_, ...), custom_call_target="tpu_custom_call" | custom-call | flops 1610612736 | bytes 2097152 | tf_op jit(solution)/shard_map/expert/pallas_call | solution.py:256
  113.4 1.0 collective-permute-done.30
  114.4 1.7 collective-permute-start.31
  116.1 10.0 %expert.8 = (bf16[128,1024]{1,0:T(8,128)(2,1)S(1)}, bf16[128,1024]{1,0:T(8,128)(2,1)S(1)}, bf16[256,1024]{1,0:T(8,128)(2,1)S(1)}) custom-call(s32[1]{0:T(128)} %bitcast.1.where, bf16[144,1024]{1,0:T(8,128)(2,1)S(1)} %collective-permute-done.23.refs_0_, bf16[144,1024]{1,0:T(8,128)(2,1)S(1)} %collective-permute-done.22.refs_1_, ...), custom_call_target="tpu_custom_call" | custom-call | flops 1610612736 | bytes 2097152 | tf_op jit(solution)/shard_map/expert/pallas_call | solution.py:256
  126.1 1.4 collective-permute-done.29.refs_0_
  128.0 1.4 collective-permute-done.33
  129.6 1.6 collective-permute-start.35
  131.7 6.9 %expert.9 = (bf16[128,1024]{1,0:T(8,128)(2,1)S(1)}, bf16[128,1024]{1,0:T(8,128)(2,1)S(1)}) custom-call(s32[1]{0:T(128)} %bitcast.1.where, bf16[144,1024]{1,0:T(8,128)(2,1)S(1)} %collective-permute-done.29.refs_0_, bf16[144,1024]{1,0:T(8,128)(2,1)S(1)} %collective-permute-done.32.refs_1_, bf16[1,1024,2048]{2,1,0:T(8,128)(2,1)} %refs_2_.3, ...), custom_call_target="tpu_custom_call" | custom-call | flops 805306368 | bytes 1048576 | tf_op jit(solution)/shard_map/expert/pallas_call | solution.py:256
  139.3 1.5 collective-permute-done.36
  140.9 0.9 collective-permute-start.37
  141.8 8.4 %collective-permute-done.37 = bf16[128,1024]{1,0:T(8,128)(2,1)S(1)} collective-permute-done((bf16[128,1024]{1,0:T(8,128)(2,1)S(1)}, bf16[128,1024]{1,0:T(8,128)(2,1)S(1)}, u32[]{:S(2)}, u32[]{:S(2)}) %collective-permute-start.37) | collective-permute-done | bytes 262176 | tf_op jit(solution)/shard_map/ppermute | solution.py:35
  150.4 2.5 %all-gather.7.cloned.1.call-done = bf16[16,256,512]{2,1,0:T(8,128)(2,1)} async-done(((bf16[8,256,512]{2,1,0:T(8,128)(2,1)}), bf16[16,256,512]{2,1,0:T(8,128)(2,1)}) %all-gather.7.cloned.1.call-update) | async-done | bytes 4194320 | tf_op jit(solution)/shard_map/all_gather | solution.py:421
  153.4 2.4 %collective-permute-start.38 = (bf16[128,1024]{1,0:T(8,128)(2,1)S(1)}, bf16[128,1024]{1,0:T(8,128)(2,1)S(1)}, u32[]{:S(2)}, u32[]{:S(2)}) collective-permute-start(bf16[128,1024]{1,0:T(8,128)(2,1)S(1)} %add_convert_fusion), channel_id=1, source_target_pairs={{0,4},{1,5},{2,6},{3,7},{4,0},{5,1},{6,2},{7,3},{8,12},{9,13},{10,... | collective-permute-start | bytes 786440 | tf_op jit(solution)/shard_map/ppermute | solution.py:35
  155.8 3.7 %collective-permute-done.15 = bf16[128,1024]{1,0:T(8,128)(2,1)S(1)} collective-permute-done((bf16[128,1024]{1,0:T(8,128)(2,1)S(1)}, bf16[128,1024]{1,0:T(8,128)(2,1)S(1)}, u32[]{:S(2)}, u32[]{:S(2)}) %collective-permute-start.15) | collective-permute-done | bytes 262176 | tf_op jit(solution)/shard_map/ppermute | solution.py:27
  159.6 8.5 %collective-permute-done.38.refs_4_ = bf16[128,1024]{1,0:T(8,128)(2,1)S(1)} collective-permute-done((bf16[128,1024]{1,0:T(8,128)(2,1)S(1)}, bf16[128,1024]{1,0:T(8,128)(2,1)S(1)}, u32[]{:S(2)}, u32[]{:S(2)}) %collective-permute-start.38) | collective-permute-done | bytes 262176 | tf_op jit(solution)/shard_map/ppermute | solution.py:35
  168.1 4.7 %project.1 = bf16[128,4096]{1,0:T(8,128)(2,1)} custom-call(s32[1]{0:T(128)} %bitcast.where, f32[128,1024]{1,0:T(8,128)S(1)} %convert_add_fusion.refs_0_, bf16[128,1024]{1,0:T(8,128)(2,1)S(1)} %collective-permute-done.25.refs_1_, bf16[128,1024]{1,0:T(8,128)(2,1)S(1)} %collective-permute-done.26.refs_2_, ...), custom_call_target="tpu_custom_call" | custom-call | flops 1073741824 | bytes 8388608 | tf_op jit(solution)/shard_map/project/pallas_call | solution.py:318
  (70 shorter events, 8.3 us)
Async XLA Ops:
  6.5 1.2 copy-start
  6.5 90.5 %all-gather.5.cloned.1.call-start = ((), (), s32[]{:S(2)}) async-start(), calls=%async_computation | async-start | bytes 2359296 | tf_op jit(solution)/shard_map/all_gather | solution.py:363
  9.6 143.3 %all-gather.7.cloned.1.call-start = ((), (), s32[]{:S(2)}) async-start(), calls=%async_computation.1 | async-start | bytes 6291456 | tf_op jit(solution)/shard_map/all_gather | solution.py:421
  9.6 18.5 %collective-permute-start.4 = (bf16[128,1024]{1,0:T(8,128)(2,1)S(1)}, bf16[128,1024]{1,0:T(8,128)(2,1)S(1)}, u32[]{:S(2)}, u32[]{:S(2)}) collective-permute-start(bf16[128,1024]{1,0:T(8,128)(2,1)S(1)} %get-tuple-element.164.refs_4_), channel_id=1, source_target_pairs={{0,4},{1,5},{2,6},{3,7},{4,0},{5,1},{6,2},{7,3},{8,12},{9,13},{10,... | collective-permute-start | bytes 786440 | tf_op jit(solution)/shard_map/ppermute | solution.py:35
  13.7 14.4 %collective-permute-start.3 = (bf16[128,1024]{1,0:T(8,128)(2,1)S(1)}, bf16[128,1024]{1,0:T(8,128)(2,1)S(1)}, u32[]{:S(2)}, u32[]{:S(2)}) collective-permute-start(bf16[128,1024]{1,0:T(8,128)(2,1)S(1)} %get-tuple-element.164.refs_4_), channel_id=1, source_target_pairs={{0,2},{1,3},{2,0},{3,1},{4,6},{5,7},{6,4},{7,5},{8,10},{9,11},{10,... | collective-permute-start | bytes 786440 | tf_op jit(solution)/shard_map/ppermute | solution.py:35
  15.4 1.2 copy-start.1
  17.4 16.0 %collective-permute-start = (bf16[128,1024]{1,0:T(8,128)(2,1)S(1)}, bf16[128,1024]{1,0:T(8,128)(2,1)S(1)}, u32[]{:S(2)}, u32[]{:S(2)}) collective-permute-start(bf16[128,1024]{1,0:T(8,128)(2,1)S(1)} %get-tuple-element.86), channel_id=1, source_target_pairs={{0,1},{1,0},{2,3},{3,2},{4,5},{5,4},{6,7},{7,6},{8,9},{9,8},{10,11... | collective-permute-start | bytes 786440 | tf_op jit(solution)/shard_map/ppermute | solution.py:35
  19.0 14.4 %collective-permute-start.1 = (bf16[128,1024]{1,0:T(8,128)(2,1)S(1)}, bf16[128,1024]{1,0:T(8,128)(2,1)S(1)}, u32[]{:S(2)}, u32[]{:S(2)}) collective-permute-start(bf16[128,1024]{1,0:T(8,128)(2,1)S(1)} %get-tuple-element.87), channel_id=1, source_target_pairs={{0,16},{16,0},{1,17},{17,1},{2,18},{18,2},{3,19},{19,3},{4,20},{20... | collective-permute-start | bytes 786440 | tf_op jit(solution)/shard_map/ppermute | solution.py:31
  20.5 12.9 %collective-permute-start.2 = (bf16[128,1024]{1,0:T(8,128)(2,1)S(1)}, bf16[128,1024]{1,0:T(8,128)(2,1)S(1)}, u32[]{:S(2)}, u32[]{:S(2)}) collective-permute-start(bf16[128,1024]{1,0:T(8,128)(2,1)S(1)} %get-tuple-element.88), channel_id=1, source_target_pairs={{0,17},{1,16},{2,19},{3,18},{4,21},{5,20},{6,23},{7,22},{16,1},{17... | collective-permute-start | bytes 786440 | tf_op jit(solution)/shard_map/ppermute | solution.py:41
  33.4 9.7 %collective-permute-start.5 = (bf16[128,1024]{1,0:T(8,128)(2,1)S(1)}, bf16[128,1024]{1,0:T(8,128)(2,1)S(1)}, u32[]{:S(2)}, u32[]{:S(2)}) collective-permute-start(bf16[128,1024]{1,0:T(8,128)(2,1)S(1)} %collective-permute-done.4.refs_8_), channel_id=1, source_target_pairs={{0,2},{1,3},{2,0},{3,1},{4,6},{5,7},{6,4},{7,5},{8,10},{9,11},{10,... | collective-permute-start | bytes 786440 | tf_op jit(solution)/shard_map/ppermute | solution.py:35
  33.4 9.7 %collective-permute-start.6 = (bf16[128,1024]{1,0:T(8,128)(2,1)S(1)}, bf16[128,1024]{1,0:T(8,128)(2,1)S(1)}, u32[]{:S(2)}, u32[]{:S(2)}) collective-permute-start(bf16[128,1024]{1,0:T(8,128)(2,1)S(1)} %collective-permute-done.3.refs_6_), channel_id=1, source_target_pairs={{0,8},{8,0},{1,9},{9,1},{2,10},{10,2},{3,11},{11,3},{4,12},{12,4},... | collective-permute-start | bytes 786440 | tf_op jit(solution)/shard_map/ppermute | solution.py:27
  33.5 9.6 %collective-permute-start.7 = (bf16[128,1024]{1,0:T(8,128)(2,1)S(1)}, bf16[128,1024]{1,0:T(8,128)(2,1)S(1)}, u32[]{:S(2)}, u32[]{:S(2)}) collective-permute-start(bf16[128,1024]{1,0:T(8,128)(2,1)S(1)} %collective-permute-done.4.refs_8_), channel_id=1, source_target_pairs={{0,8},{8,0},{1,9},{9,1},{2,10},{10,2},{3,11},{11,3},{4,12},{12,4},... | collective-permute-start | bytes 786440 | tf_op jit(solution)/shard_map/ppermute | solution.py:27
  43.1 1.5 collective-permute-start.8
  45.1 19.1 %collective-permute-start.9 = (bf16[128,1024]{1,0:T(8,128)(2,1)S(1)}, bf16[128,1024]{1,0:T(8,128)(2,1)S(1)}, u32[]{:S(2)}, u32[]{:S(2)}) collective-permute-start(bf16[128,1024]{1,0:T(8,128)(2,1)S(1)} %get-tuple-element.96), channel_id=1, source_target_pairs={{0,1},{1,0},{2,3},{3,2},{4,5},{5,4},{6,7},{7,6},{8,9},{9,8},{10,11... | collective-permute-start | bytes 786440 | tf_op jit(solution)/shard_map/ppermute | solution.py:35
  46.2 18.0 %collective-permute-start.10 = (bf16[128,1024]{1,0:T(8,128)(2,1)S(1)}, bf16[128,1024]{1,0:T(8,128)(2,1)S(1)}, u32[]{:S(2)}, u32[]{:S(2)}) collective-permute-start(bf16[128,1024]{1,0:T(8,128)(2,1)S(1)} %get-tuple-element.97), channel_id=1, source_target_pairs={{0,16},{16,0},{1,17},{17,1},{2,18},{18,2},{3,19},{19,3},{4,20},{20... | collective-permute-start | bytes 786440 | tf_op jit(solution)/shard_map/ppermute | solution.py:31
  47.7 16.5 %collective-permute-start.11 = (bf16[128,1024]{1,0:T(8,128)(2,1)S(1)}, bf16[128,1024]{1,0:T(8,128)(2,1)S(1)}, u32[]{:S(2)}, u32[]{:S(2)}) collective-permute-start(bf16[128,1024]{1,0:T(8,128)(2,1)S(1)} %get-tuple-element.98), channel_id=1, source_target_pairs={{0,17},{1,16},{2,19},{3,18},{4,21},{5,20},{6,23},{7,22},{16,1},{17... | collective-permute-start | bytes 786440 | tf_op jit(solution)/shard_map/ppermute | solution.py:41
  64.3 1.7 collective-permute-start.12
  64.4 12.3 %collective-permute-start.14 = (bf16[144,1024]{1,0:T(8,128)(2,1)S(1)}, bf16[144,1024]{1,0:T(8,128)(2,1)S(1)}, u32[]{:S(2)}, u32[]{:S(2)}) collective-permute-start(bf16[144,1024]{1,0:T(8,128)(2,1)S(1)} %finish_latent.1.refs_0_), channel_id=1, source_target_pairs={{0,1},{1,0},{2,3},{3,2},{4,5},{5,4},{6,7},{7,6},{8,9},{9,8},{10,11... | collective-permute-start | bytes 884744 | tf_op jit(solution)/shard_map/ppermute | solution.py:35
  66.1 14.3 %collective-permute-start.13 = (bf16[144,1024]{1,0:T(8,128)(2,1)S(1)}, bf16[144,1024]{1,0:T(8,128)(2,1)S(1)}, u32[]{:S(2)}, u32[]{:S(2)}) collective-permute-start(bf16[144,1024]{1,0:T(8,128)(2,1)S(1)} %finish_latent.1.refs_0_), channel_id=1, source_target_pairs={{0,2},{1,3},{2,0},{3,1},{4,6},{5,7},{6,4},{7,5},{8,10},{9,11},{10,... | collective-permute-start | bytes 884744 | tf_op jit(solution)/shard_map/ppermute | solution.py:35
  72.9 0.7 copy-start.3
  80.4 1.9 %collective-permute-start.17 = (bf16[144,1024]{1,0:T(8,128)(2,1)S(1)}, bf16[144,1024]{1,0:T(8,128)(2,1)S(1)}, u32[]{:S(2)}, u32[]{:S(2)}) collective-permute-start(bf16[144,1024]{1,0:T(8,128)(2,1)S(1)} %collective-permute-done.14.refs_1_), channel_id=1, source_target_pairs={{0,8},{8,0},{1,9},{9,1},{2,10},{10,2},{3,11},{11,3},{4,12},{12,4},... | collective-permute-start | bytes 884744 | tf_op jit(solution)/shard_map/ppermute | solution.py:27
  80.4 2.0 %collective-permute-start.16 = (bf16[144,1024]{1,0:T(8,128)(2,1)S(1)}, bf16[144,1024]{1,0:T(8,128)(2,1)S(1)}, u32[]{:S(2)}, u32[]{:S(2)}) collective-permute-start(bf16[144,1024]{1,0:T(8,128)(2,1)S(1)} %collective-permute-done.13.refs_0_), channel_id=1, source_target_pairs={{0,8},{8,0},{1,9},{9,1},{2,10},{10,2},{3,11},{11,3},{4,12},{12,4},... | collective-permute-start | bytes 884744 | tf_op jit(solution)/shard_map/ppermute | solution.py:27
  80.9 16.1 %collective-permute-start.18 = (bf16[144,1024]{1,0:T(8,128)(2,1)S(1)}, bf16[144,1024]{1,0:T(8,128)(2,1)S(1)}, u32[]{:S(2)}, u32[]{:S(2)}) collective-permute-start(bf16[144,1024]{1,0:T(8,128)(2,1)S(1)} %finish_latent.1.refs_0_), channel_id=1, source_target_pairs={{0,4},{1,5},{2,6},{3,7},{4,0},{5,1},{6,2},{7,3},{8,12},{9,13},{10,... | collective-permute-start | bytes 884744 | tf_op jit(solution)/shard_map/ppermute | solution.py:35
  82.3 14.7 %collective-permute-start.19 = (bf16[144,1024]{1,0:T(8,128)(2,1)S(1)}, bf16[144,1024]{1,0:T(8,128)(2,1)S(1)}, u32[]{:S(2)}, u32[]{:S(2)}) collective-permute-start(bf16[144,1024]{1,0:T(8,128)(2,1)S(1)} %collective-permute-done.13.refs_0_), channel_id=1, source_target_pairs={{0,1},{1,0},{2,3},{3,2},{4,5},{5,4},{6,7},{7,6},{8,9},{9,8},{10,11... | collective-permute-start | bytes 884744 | tf_op jit(solution)/shard_map/ppermute | solution.py:35
  92.3 0.8 copy-start.2
  97.0 2.2 %collective-permute-start.24 = (bf16[256,1024]{1,0:T(8,128)(2,1)}, bf16[256,1024]{1,0:T(8,128)(2,1)S(1)}, u32[]{:S(2)}, u32[]{:S(2)}) collective-permute-start(bf16[256,1024]{1,0:T(8,128)(2,1)} %copy-done.2), channel_id=1, source_target_pairs={{0,8},{8,0},{1,9},{9,1},{2,10},{10,2},{3,11},{11,3},{4,12},{12,4},... | collective-permute-start | bytes 1572872 | tf_op jit(solution)/shard_map/ppermute | solution.py:27
  97.1 3.3 %collective-permute-start.21 = (bf16[144,1024]{1,0:T(8,128)(2,1)S(1)}, bf16[144,1024]{1,0:T(8,128)(2,1)S(1)}, u32[]{:S(2)}, u32[]{:S(2)}) collective-permute-start(bf16[144,1024]{1,0:T(8,128)(2,1)S(1)} %collective-permute-done.19.refs_1_), channel_id=1, source_target_pairs={{0,8},{8,0},{1,9},{9,1},{2,10},{10,2},{3,11},{11,3},{4,12},{12,4},... | collective-permute-start | bytes 884744 | tf_op jit(solution)/shard_map/ppermute | solution.py:27
  97.6 14.7 %collective-permute-start.23 = (bf16[144,1024]{1,0:T(8,128)(2,1)S(1)}, bf16[144,1024]{1,0:T(8,128)(2,1)S(1)}, u32[]{:S(2)}, u32[]{:S(2)}) collective-permute-start(bf16[144,1024]{1,0:T(8,128)(2,1)S(1)} %collective-permute-done.18.refs_0_), channel_id=1, source_target_pairs={{0,2},{1,3},{2,0},{3,1},{4,6},{5,7},{6,4},{7,5},{8,10},{9,11},{10,... | collective-permute-start | bytes 884744 | tf_op jit(solution)/shard_map/ppermute | solution.py:35
  97.6 14.7 %collective-permute-start.22 = (bf16[144,1024]{1,0:T(8,128)(2,1)S(1)}, bf16[144,1024]{1,0:T(8,128)(2,1)S(1)}, u32[]{:S(2)}, u32[]{:S(2)}) collective-permute-start(bf16[144,1024]{1,0:T(8,128)(2,1)S(1)} %collective-permute-done.18.refs_0_), channel_id=1, source_target_pairs={{0,1},{1,0},{2,3},{3,2},{4,5},{5,4},{6,7},{7,6},{8,9},{9,8},{10,11... | collective-permute-start | bytes 884744 | tf_op jit(solution)/shard_map/ppermute | solution.py:35
  98.5 3.4 %collective-permute-start.20 = (bf16[144,1024]{1,0:T(8,128)(2,1)S(1)}, bf16[144,1024]{1,0:T(8,128)(2,1)S(1)}, u32[]{:S(2)}, u32[]{:S(2)}) collective-permute-start(bf16[144,1024]{1,0:T(8,128)(2,1)S(1)} %collective-permute-done.18.refs_0_), channel_id=1, source_target_pairs={{0,8},{8,0},{1,9},{9,1},{2,10},{10,2},{3,11},{11,3},{4,12},{12,4},... | collective-permute-start | bytes 884744 | tf_op jit(solution)/shard_map/ppermute | solution.py:27
  99.4 12.9 %collective-permute-start.26 = (bf16[128,1024]{1,0:T(8,128)(2,1)S(1)}, bf16[128,1024]{1,0:T(8,128)(2,1)S(1)}, u32[]{:S(2)}, u32[]{:S(2)}) collective-permute-start(bf16[128,1024]{1,0:T(8,128)(2,1)S(1)} %get-tuple-element.167), channel_id=1, source_target_pairs={{0,2},{1,3},{2,0},{3,1},{4,6},{5,7},{6,4},{7,5},{8,10},{9,11},{10,... | collective-permute-start | bytes 786440 | tf_op jit(solution)/shard_map/ppermute | solution.py:35
  100.4 11.9 %collective-permute-start.25 = (bf16[128,1024]{1,0:T(8,128)(2,1)S(1)}, bf16[128,1024]{1,0:T(8,128)(2,1)S(1)}, u32[]{:S(2)}, u32[]{:S(2)}) collective-permute-start(bf16[128,1024]{1,0:T(8,128)(2,1)S(1)} %get-tuple-element.168), channel_id=1, source_target_pairs={{0,1},{1,0},{2,3},{3,2},{4,5},{5,4},{6,7},{7,6},{8,9},{9,8},{10,11... | collective-permute-start | bytes 786440 | tf_op jit(solution)/shard_map/ppermute | solution.py:35
  112.4 2.0 %collective-permute-start.30 = (bf16[256,1024]{1,0:T(8,128)(2,1)S(1)}, bf16[256,1024]{1,0:T(8,128)(2,1)S(1)}, u32[]{:S(2)}, u32[]{:S(2)}) collective-permute-start(bf16[256,1024]{1,0:T(8,128)(2,1)S(1)} %get-tuple-element.140), channel_id=1, source_target_pairs={{0,8},{8,0},{1,9},{9,1},{2,10},{10,2},{3,11},{11,3},{4,12},{12,4},... | collective-permute-start | bytes 1572872 | tf_op jit(solution)/shard_map/ppermute | solution.py:27
  112.4 15.0 %collective-permute-start.29 = (bf16[144,1024]{1,0:T(8,128)(2,1)S(1)}, bf16[144,1024]{1,0:T(8,128)(2,1)S(1)}, u32[]{:S(2)}, u32[]{:S(2)}) collective-permute-start(bf16[144,1024]{1,0:T(8,128)(2,1)S(1)} %collective-permute-done.23.refs_0_), channel_id=1, source_target_pairs={{0,1},{1,0},{2,3},{3,2},{4,5},{5,4},{6,7},{7,6},{8,9},{9,8},{10,11... | collective-permute-start | bytes 884744 | tf_op jit(solution)/shard_map/ppermute | solution.py:35
  112.9 3.2 %collective-permute-start.27 = (bf16[144,1024]{1,0:T(8,128)(2,1)S(1)}, bf16[144,1024]{1,0:T(8,128)(2,1)S(1)}, u32[]{:S(2)}, u32[]{:S(2)}) collective-permute-start(bf16[144,1024]{1,0:T(8,128)(2,1)S(1)} %collective-permute-done.23.refs_0_), channel_id=1, source_target_pairs={{0,8},{8,0},{1,9},{9,1},{2,10},{10,2},{3,11},{11,3},{4,12},{12,4},... | collective-permute-start | bytes 884744 | tf_op jit(solution)/shard_map/ppermute | solution.py:27
  113.1 3.0 %collective-permute-start.28 = (bf16[144,1024]{1,0:T(8,128)(2,1)S(1)}, bf16[144,1024]{1,0:T(8,128)(2,1)S(1)}, u32[]{:S(2)}, u32[]{:S(2)}) collective-permute-start(bf16[144,1024]{1,0:T(8,128)(2,1)S(1)} %collective-permute-done.22.refs_1_), channel_id=1, source_target_pairs={{0,8},{8,0},{1,9},{9,1},{2,10},{10,2},{3,11},{11,3},{4,12},{12,4},... | collective-permute-start | bytes 884744 | tf_op jit(solution)/shard_map/ppermute | solution.py:27
  114.4 13.1 %collective-permute-start.31 = (bf16[128,1024]{1,0:T(8,128)(2,1)S(1)}, bf16[128,1024]{1,0:T(8,128)(2,1)S(1)}, u32[]{:S(2)}, u32[]{:S(2)}) collective-permute-start(bf16[128,1024]{1,0:T(8,128)(2,1)S(1)} %add_convert_fusion.4), channel_id=1, source_target_pairs={{0,3},{1,2},{2,1},{3,0},{4,7},{5,6},{6,5},{7,4},{8,11},{9,10},{10,... | collective-permute-start | bytes 786440 | tf_op jit(solution)/shard_map/ppermute | solution.py:35
  127.5 1.9 %collective-permute-start.33 = (bf16[256,1024]{1,0:T(8,128)(2,1)S(1)}, bf16[256,1024]{1,0:T(8,128)(2,1)S(1)}, u32[]{:S(2)}, u32[]{:S(2)}) collective-permute-start(bf16[256,1024]{1,0:T(8,128)(2,1)S(1)} %get-tuple-element.149), channel_id=1, source_target_pairs={{0,8},{8,0},{1,9},{9,1},{2,10},{10,2},{3,11},{11,3},{4,12},{12,4},... | collective-permute-start | bytes 1572872 | tf_op jit(solution)/shard_map/ppermute | solution.py:27
  127.5 4.2 %collective-permute-start.32 = (bf16[144,1024]{1,0:T(8,128)(2,1)S(1)}, bf16[144,1024]{1,0:T(8,128)(2,1)S(1)}, u32[]{:S(2)}, u32[]{:S(2)}) collective-permute-start(bf16[144,1024]{1,0:T(8,128)(2,1)S(1)} %collective-permute-done.29.refs_0_), channel_id=1, source_target_pairs={{0,8},{8,0},{1,9},{9,1},{2,10},{10,2},{3,11},{11,3},{4,12},{12,4},... | collective-permute-start | bytes 884744 | tf_op jit(solution)/shard_map/ppermute | solution.py:27
  129.6 9.0 %collective-permute-start.35 = (bf16[128,1024]{1,0:T(8,128)(2,1)S(1)}, bf16[128,1024]{1,0:T(8,128)(2,1)S(1)}, u32[]{:S(2)}, u32[]{:S(2)}) collective-permute-start(bf16[128,1024]{1,0:T(8,128)(2,1)S(1)} %get-tuple-element.165), channel_id=1, source_target_pairs={{0,2},{1,3},{2,0},{3,1},{4,6},{5,7},{6,4},{7,5},{8,10},{9,11},{10,... | collective-permute-start | bytes 786440 | tf_op jit(solution)/shard_map/ppermute | solution.py:35
  131.2 21.7 %copy-start.4 = (bf16[128,1024]{1,0:T(8,128)(2,1)S(1)}, bf16[128,1024]{1,0:T(8,128)(2,1)}, u32[]{:S(2)}) copy-start(bf16[128,1024]{1,0:T(8,128)(2,1)} %copy-done.3) | copy-start | bytes 786436
  131.2 8.1 %collective-permute-start.34 = (bf16[128,1024]{1,0:T(8,128)(2,1)S(1)}, bf16[128,1024]{1,0:T(8,128)(2,1)S(1)}, u32[]{:S(2)}, u32[]{:S(2)}) collective-permute-start(bf16[128,1024]{1,0:T(8,128)(2,1)S(1)} %get-tuple-element.166), channel_id=1, source_target_pairs={{0,1},{1,0},{2,3},{3,2},{4,5},{5,4},{6,7},{7,6},{8,9},{9,8},{10,11... | collective-permute-start | bytes 786440 | tf_op jit(solution)/shard_map/ppermute | solution.py:35
  139.3 1.5 collective-permute-start.36
  140.9 9.3 %collective-permute-start.37 = (bf16[128,1024]{1,0:T(8,128)(2,1)S(1)}, bf16[128,1024]{1,0:T(8,128)(2,1)S(1)}, u32[]{:S(2)}, u32[]{:S(2)}) collective-permute-start(bf16[128,1024]{1,0:T(8,128)(2,1)S(1)} %add_convert_fusion.1), channel_id=1, source_target_pairs={{0,3},{1,2},{2,1},{3,0},{4,7},{5,6},{6,5},{7,4},{8,11},{9,10},{10,... | collective-permute-start | bytes 786440 | tf_op jit(solution)/shard_map/ppermute | solution.py:35
  152.9 15.2 %collective-permute-start.39 = (bf16[2,8,256,512]{3,2,1,0:T(8,128)(2,1)}, bf16[2,8,256,512]{3,2,1,0:T(8,128)(2,1)S(1)}, u32[]{:S(2)}, u32[]{:S(2)}) collective-permute-start(bf16[2,8,256,512]{3,2,1,0:T(8,128)(2,1)} %bitcast.6), channel_id=1, source_target_pairs={{0,8},{8,0},{1,9},{9,1},{2,10},{10,2},{3,11},{11,3},{4,12},{12,4},... | collective-permute-start | bytes 12582920 | tf_op jit(solution)/shard_map/ppermute | solution.py:27
  152.9 6.6 %collective-permute-start.15 = (bf16[128,1024]{1,0:T(8,128)(2,1)S(1)}, bf16[128,1024]{1,0:T(8,128)(2,1)S(1)}, u32[]{:S(2)}, u32[]{:S(2)}) collective-permute-start(bf16[128,1024]{1,0:T(8,128)(2,1)S(1)} %copy-done.4), channel_id=1, source_target_pairs={{0,8},{8,0},{1,9},{9,1},{2,10},{10,2},{3,11},{11,3},{4,12},{12,4},... | collective-permute-start | bytes 786440 | tf_op jit(solution)/shard_map/ppermute | solution.py:27
  153.4 14.7 %collective-permute-start.38 = (bf16[128,1024]{1,0:T(8,128)(2,1)S(1)}, bf16[128,1024]{1,0:T(8,128)(2,1)S(1)}, u32[]{:S(2)}, u32[]{:S(2)}) collective-permute-start(bf16[128,1024]{1,0:T(8,128)(2,1)S(1)} %add_convert_fusion), channel_id=1, source_target_pairs={{0,4},{1,5},{2,6},{3,7},{4,0},{5,1},{6,2},{7,3},{8,12},{9,13},{10,... | collective-permute-start | bytes 786440 | tf_op jit(solution)/shard_map/ppermute | solution.py:35
Sparse Core Ops, SparseCore 0:
  9.7 72.9 all-gather.4
  97.2 55.6 all-gather.6

commit v11 on v8

--- a/solution.py
+++ b/solution.py
@@ -430,13 +430,13 @@
         send((last - 1, 1), sums[last - 1, 1], 1),
         send((last, 0), sums[last, 0], 2),
     )
+    send((last, 1), sums[last, 1], 3)
     shared = sums[last - 1, 0]
-    for name in ((last - 1, 1), (last, 0)):
+    for name in ((last - 1, 1), (last, 0), (last, 1)):
         shared += travel.pop(name).astype(jnp.float32)
+    shared = shared.astype(jnp.bfloat16)
+    both_sides = after(both_sides, sums[last, 1])
     send("shared", shared, 2 * last - 2)
-    final = sums[last, 1].astype(jnp.bfloat16)
-    both_sides = after(both_sides, final)
-    send((last, 1), final, 2 * last + 1)
     *terms, swapped_sides = join(sums[0, 0], *travel.values(), swap_cores(both_sides))
     both_sides = pltpu.with_memory_space_constraint(both_sides, pltpu.HBM)
     return project(group, terms, both_sides, swapped_sides)

time: 174 us -> 214 us (1.23)
  the two profiles are of different devices: /device:TPU:9 before, /device:TPU:0 now
where the time goes in v11:
time: 214 us; the launch traced here: 213 us
  waiting for transfers between devices  102 us (48%)
  Pallas kernels  51.3 us (24%)
  starting transfers between devices  37.6 us (18%)
  between operations  13.7 us (6%)
  local copies, waits for them, and re-layouts  4.94 us (2%)
  other arithmetic  4 us (2%)
    ppermute x21, waiting for transfers between devices, swap_ep(): lax.ppermute(array, 'ep', [(i, i ^ mask) for i in range(lax.axis_size('ep...  49.5 us
    pallas_call x5, Pallas kernels, expert_apply(): pl.pallas_call(functools.partial(expert_kernel, positions, count), out_sh...  44.3 us
    all_gather x1, waiting for transfers between devices, body(): lax.all_gather(travel.pop('up'), 'rep', axis=0, axis_index_groups=sides)  39.3 us
    ppermute x21, starting transfers between devices, swap_ep(): lax.ppermute(array, 'ep', [(i, i ^ mask) for i in range(lax.axis_size('ep...  30.6 us
    ppermute x2, waiting for transfers between devices, swap_reps(): lax.ppermute(array, 'rep', [(i, i ^ 1) for i in range(lax.axis_size('rep'...  6.83 us
    ppermute x21, waiting for transfers between devices, swap_cores(): return lax.ppermute(array, 'grp', [(0, 1), (1, 0)])  6.27 us
    pallas_call x1, Pallas kernels, project(): pl.pallas_call(project_kernel, in_specs=[in_smem] + [in_vmem] * len(terms...  4.7 us
  transfers between devices with their start and end apart: 46, of which 18 were waited for; matrix products, arithmetic and copies ran while one was open for 2% of the time, Pallas kernels for 22%

profile of v11, /device:TPU:0, one launch (start us, length us, event | category | flops | bytes accessed | tf_op | source)
XLA Modules:
  0.0 213.4 jit_solution(7297448791986521875)
XLA Ops:
  6.5 1.2 copy-done
  7.8 0.7 constant_dynamic-slice_fusion
  8.6 1.1 constant_dynamic-slice_fusion.1
  9.6 3.1 %collective-permute-start = (bf16[128,1024]{1,0:T(8,128)(2,1)S(1)}, bf16[128,1024]{1,0:T(8,128)(2,1)S(1)}, u32[]{:S(2)}, u32[]{:S(2)}) collective-permute-start(bf16[128,1024]{1,0:T(8,128)(2,1)S(1)} %get-tuple-element.158.refs_2_), channel_id=1, source_target_pairs={{0,2},{1,3},{2,0},{3,1},{4,6},{5,7},{6,4},{7,5},{8,10},{9,11},{10,... | collective-permute-start | bytes 786440 | tf_op jit(solution)/shard_map/ppermute | solution.py:35
  12.7 1.5 collective-permute-start.4
  14.3 2.6 %collective-permute-start.2 = (bf16[128,1024]{1,0:T(8,128)(2,1)S(1)}, bf16[128,1024]{1,0:T(8,128)(2,1)S(1)}, u32[]{:S(2)}, u32[]{:S(2)}) collective-permute-start(bf16[128,1024]{1,0:T(8,128)(2,1)S(1)} %get-tuple-element.158.refs_2_), channel_id=1, source_target_pairs={{0,4},{1,5},{2,6},{3,7},{4,0},{5,1},{6,2},{7,3},{8,12},{9,13},{10,... | collective-permute-start | bytes 786440 | tf_op jit(solution)/shard_map/ppermute | solution.py:35
  16.9 1.2 copy-done.1
  18.1 0.8 split_columns.1
  19.0 1.6 collective-permute-start.5
  20.5 0.7 fusion.1
  21.2 2.5 %collective-permute-done.refs_6_ = bf16[128,1024]{1,0:T(8,128)(2,1)S(1)} collective-permute-done((bf16[128,1024]{1,0:T(8,128)(2,1)S(1)}, bf16[128,1024]{1,0:T(8,128)(2,1)S(1)}, u32[]{:S(2)}, u32[]{:S(2)}) %collective-permute-start) | collective-permute-done | bytes 262176 | tf_op jit(solution)/shard_map/ppermute | solution.py:35
  23.7 3.8 %collective-permute-start.1 = (bf16[128,1024]{1,0:T(8,128)(2,1)S(1)}, bf16[128,1024]{1,0:T(8,128)(2,1)S(1)}, u32[]{:S(2)}, u32[]{:S(2)}) collective-permute-start(bf16[128,1024]{1,0:T(8,128)(2,1)S(1)} %collective-permute-done.refs_6_), channel_id=1, source_target_pairs={{0,1},{1,0},{2,3},{3,2},{4,5},{5,4},{6,7},{7,6},{8,9},{9,8},{10,11... | collective-permute-start | bytes 786440 | tf_op jit(solution)/shard_map/ppermute | solution.py:35
  28.2 0.7 select_reduce_fusion.weights
  28.9 4.1 %collective-permute-done.2.refs_10_ = bf16[128,1024]{1,0:T(8,128)(2,1)S(1)} collective-permute-done((bf16[128,1024]{1,0:T(8,128)(2,1)S(1)}, bf16[128,1024]{1,0:T(8,128)(2,1)S(1)}, u32[]{:S(2)}, u32[]{:S(2)}) %collective-permute-start.2) | collective-permute-done | bytes 262176 | tf_op jit(solution)/shard_map/ppermute | solution.py:35
  33.1 0.9 collective-permute-start.3
  34.5 7.3 %collective-permute-done.3.refs_2_ = bf16[128,1024]{1,0:T(8,128)(2,1)S(1)} collective-permute-done((bf16[128,1024]{1,0:T(8,128)(2,1)S(1)}, bf16[128,1024]{1,0:T(8,128)(2,1)S(1)}, u32[]{:S(2)}, u32[]{:S(2)}) %collective-permute-start.3) | collective-permute-done | bytes 262176 | tf_op jit(solution)/shard_map/ppermute | solution.py:35
  43.5 10.0 %collective-permute-done.12.refs_3_ = bf16[128,1024]{1,0:T(8,128)(2,1)S(1)} collective-permute-done((bf16[128,1024]{1,0:T(8,128)(2,1)S(1)}, bf16[128,1024]{1,0:T(8,128)(2,1)S(1)}, u32[]{:S(2)}, u32[]{:S(2)}) %collective-permute-start.12) | collective-permute-done | bytes 262176 | tf_op jit(solution)/shard_map/ppermute | solution.py:35
  53.5 1.0 down_project.2.refs_6_
  55.5 1.6 collective-permute-start.15
  57.1 6.8 %collective-permute-done.15.arrived = bf16[128,1024]{1,0:T(8,128)(2,1)S(1)} collective-permute-done((bf16[128,1024]{1,0:T(8,128)(2,1)S(1)}, bf16[128,1024]{1,0:T(8,128)(2,1)S(1)}, u32[]{:S(2)}, u32[]{:S(2)}) %collective-permute-start.15) | collective-permute-done | bytes 262176 | tf_op jit(solution)/shard_map/ppermute | solution.py:31
  64.0 1.0 collective-permute-start.18
  65.1 1.5 collective-permute-start.17
  66.6 6.8 %expert.5 = (bf16[128,1024]{1,0:T(8,128)(2,1)S(1)}, bf16[128,1024]{1,0:T(8,128)(2,1)S(1)}) custom-call(s32[1]{0:T(128)} %bitcast.1.where, bf16[144,1024]{1,0:T(8,128)(2,1)S(1)} %finish_latent.1.refs_0_, bf16[144,1024]{1,0:T(8,128)(2,1)S(1)} %collective-permute-done.16.refs_1_, bf16[1,1024,2048]{2,1,0:T(8,128)(2,1)} %refs_2_.3, ...), custom_call_target="tpu_custom_call" | custom-call | flops 805306368 | bytes 1048576 | tf_op jit(solution)/shard_map/expert/pallas_call | solution.py:248
  75.2 1.2 collective-permute-start.22
  76.4 1.1 collective-permute-start.23
  77.5 10.7 %expert.6 = (bf16[128,1024]{1,0:T(8,128)(2,1)S(1)}, bf16[128,1024]{1,0:T(8,128)(2,1)S(1)}, bf16[256,1024]{1,0:T(8,128)(2,1)}) custom-call(s32[1]{0:T(128)} %bitcast.1.where, bf16[144,1024]{1,0:T(8,128)(2,1)S(1)} %collective-permute-done.17.refs_0_, bf16[144,1024]{1,0:T(8,128)(2,1)S(1)} %collective-permute-done.18.refs_1_, ...), custom_call_target="tpu_custom_call" | custom-call | flops 1610612736 | bytes 2097152 | tf_op jit(solution)/shard_map/expert/pallas_call | solution.py:248
  88.2 3.2 %collective-permute-done.22.refs_0_ = bf16[144,1024]{1,0:T(8,128)(2,1)S(1)} collective-permute-done((bf16[144,1024]{1,0:T(8,128)(2,1)S(1)}, bf16[144,1024]{1,0:T(8,128)(2,1)S(1)}, u32[]{:S(2)}, u32[]{:S(2)}) %collective-permute-start.22) | collective-permute-done | bytes 294944 | tf_op jit(solution)/shard_map/ppermute | solution.py:35
  91.4 39.3 %all-gather.7.cloned.1.call-done = bf16[16,256,512]{2,1,0:T(8,128)(2,1)} async-done(((bf16[8,256,512]{2,1,0:T(8,128)(2,1)}), bf16[16,256,512]{2,1,0:T(8,128)(2,1)}) %all-gather.7.cloned.1.call-update) | async-done | bytes 4194320 | tf_op jit(solution)/shard_map/all_gather | solution.py:418
  131.2 1.5 collective-permute-start.27
  132.7 1.5 collective-permute-start.26
  134.2 1.2 add_convert_fusion.4
  135.4 2.0 collective-permute-done.25.refs_3_
  137.4 1.5 collective-permute-start.30
  138.9 1.5 collective-permute-start.29
  140.4 10.0 %expert.7 = (bf16[128,1024]{1,0:T(8,128)(2,1)S(1)}, bf16[128,1024]{1,0:T(8,128)(2,1)S(1)}, bf16[256,1024]{1,0:T(8,128)(2,1)S(1)}) custom-call(s32[1]{0:T(128)} %bitcast.1.where, bf16[144,1024]{1,0:T(8,128)(2,1)S(1)} %collective-permute-done.22.refs_0_, bf16[144,1024]{1,0:T(8,128)(2,1)S(1)} %collective-permute-done.23.refs_1_, ...), custom_call_target="tpu_custom_call" | custom-call | flops 1610612736 | bytes 2097152 | tf_op jit(solution)/shard_map/expert/pallas_call | solution.py:248
  151.6 0.8 collective-permute-done.34
  152.5 1.1 collective-permute-start.35
  153.5 10.0 %expert.8 = (bf16[128,1024]{1,0:T(8,128)(2,1)S(1)}, bf16[128,1024]{1,0:T(8,128)(2,1)S(1)}, bf16[256,1024]{1,0:T(8,128)(2,1)S(1)}) custom-call(s32[1]{0:T(128)} %bitcast.1.where, bf16[144,1024]{1,0:T(8,128)(2,1)S(1)} %collective-permute-done.27.refs_0_, bf16[144,1024]{1,0:T(8,128)(2,1)S(1)} %collective-permute-done.26.refs_1_, ...), custom_call_target="tpu_custom_call" | custom-call | flops 1610612736 | bytes 2097152 | tf_op jit(solution)/shard_map/expert/pallas_call | solution.py:248
  163.5 2.0 collective-permute-done.33.refs_0_
  166.0 1.4 collective-permute-done.37
  167.6 0.9 collective-permute-start.39
  169.1 6.9 %expert.9 = (bf16[128,1024]{1,0:T(8,128)(2,1)S(1)}, bf16[128,1024]{1,0:T(8,128)(2,1)S(1)}) custom-call(s32[1]{0:T(128)} %bitcast.1.where, bf16[144,1024]{1,0:T(8,128)(2,1)S(1)} %collective-permute-done.33.refs_0_, bf16[144,1024]{1,0:T(8,128)(2,1)S(1)} %collective-permute-done.36.refs_1_, bf16[1,1024,2048]{2,1,0:T(8,128)(2,1)} %refs_2_.3, ...), custom_call_target="tpu_custom_call" | custom-call | flops 805306368 | bytes 1048576 | tf_op jit(solution)/shard_map/expert/pallas_call | solution.py:248
  176.6 1.5 collective-permute-done.40
  178.2 1.6 collective-permute-start.41
  179.8 7.7 %collective-permute-done.41 = bf16[128,1024]{1,0:T(8,128)(2,1)S(1)} collective-permute-done((bf16[128,1024]{1,0:T(8,128)(2,1)S(1)}, bf16[128,1024]{1,0:T(8,128)(2,1)S(1)}, u32[]{:S(2)}, u32[]{:S(2)}) %collective-permute-start.41) | collective-permute-done | bytes 262176 | tf_op jit(solution)/shard_map/ppermute | solution.py:35
  187.7 2.4 %collective-permute-start.42 = (bf16[128,1024]{1,0:T(8,128)(2,1)S(1)}, bf16[128,1024]{1,0:T(8,128)(2,1)S(1)}, u32[]{:S(2)}, u32[]{:S(2)}) collective-permute-start(bf16[128,1024]{1,0:T(8,128)(2,1)S(1)} %add_convert_fusion), channel_id=1, source_target_pairs={{0,4},{1,5},{2,6},{3,7},{4,0},{5,1},{6,2},{7,3},{8,12},{9,13},{10,... | collective-permute-start | bytes 786440 | tf_op jit(solution)/shard_map/ppermute | solution.py:35
  190.3 11.6 %collective-permute-done.42.refs_4_ = bf16[128,1024]{1,0:T(8,128)(2,1)S(1)} collective-permute-done((bf16[128,1024]{1,0:T(8,128)(2,1)S(1)}, bf16[128,1024]{1,0:T(8,128)(2,1)S(1)}, u32[]{:S(2)}, u32[]{:S(2)}) %collective-permute-start.42) | collective-permute-done | bytes 262176 | tf_op jit(solution)/shard_map/ppermute | solution.py:35
  201.9 4.7 %project.1 = bf16[128,4096]{1,0:T(8,128)(2,1)} custom-call(s32[1]{0:T(128)} %bitcast.where, f32[128,1024]{1,0:T(8,128)S(1)} %convert_add_fusion.1.refs_0_, bf16[128,1024]{1,0:T(8,128)(2,1)S(1)} %collective-permute-done.29.refs_1_, bf16[128,1024]{1,0:T(8,128)(2,1)S(1)} %collective-permute-done.30.refs_2_, ...), custom_call_target="tpu_custom_call" | custom-call | flops 1073741824 | bytes 8388608 | tf_op jit(solution)/shard_map/project/pallas_call | solution.py:310
  (76 shorter events, 9.9 us)
Async XLA Ops:
  6.5 68.0 %all-gather.5.cloned.1.call-start = ((), (), s32[]{:S(2)}) async-start(), calls=%async_computation | async-start | bytes 2359296 | tf_op jit(solution)/shard_map/all_gather | solution.py:360
  8.5 122.2 %all-gather.7.cloned.1.call-start = ((), (), s32[]{:S(2)}) async-start(), calls=%async_computation.1 | async-start | bytes 6291456 | tf_op jit(solution)/shard_map/all_gather | solution.py:418
  9.6 14.1 %collective-permute-start = (bf16[128,1024]{1,0:T(8,128)(2,1)S(1)}, bf16[128,1024]{1,0:T(8,128)(2,1)S(1)}, u32[]{:S(2)}, u32[]{:S(2)}) collective-permute-start(bf16[128,1024]{1,0:T(8,128)(2,1)S(1)} %get-tuple-element.158.refs_2_), channel_id=1, source_target_pairs={{0,2},{1,3},{2,0},{3,1},{4,6},{5,7},{6,4},{7,5},{8,10},{9,11},{10,... | collective-permute-start | bytes 786440 | tf_op jit(solution)/shard_map/ppermute | solution.py:35
  12.7 21.3 %collective-permute-start.4 = (bf16[128,1024]{1,0:T(8,128)(2,1)S(1)}, bf16[128,1024]{1,0:T(8,128)(2,1)S(1)}, u32[]{:S(2)}, u32[]{:S(2)}) collective-permute-start(bf16[128,1024]{1,0:T(8,128)(2,1)S(1)} %get-tuple-element.158.refs_2_), channel_id=1, source_target_pairs={{0,1},{1,0},{2,3},{3,2},{4,5},{5,4},{6,7},{7,6},{8,9},{9,8},{10,11... | collective-permute-start | bytes 786440 | tf_op jit(solution)/shard_map/ppermute | solution.py:35
  14.3 18.8 %collective-permute-start.2 = (bf16[128,1024]{1,0:T(8,128)(2,1)S(1)}, bf16[128,1024]{1,0:T(8,128)(2,1)S(1)}, u32[]{:S(2)}, u32[]{:S(2)}) collective-permute-start(bf16[128,1024]{1,0:T(8,128)(2,1)S(1)} %get-tuple-element.158.refs_2_), channel_id=1, source_target_pairs={{0,4},{1,5},{2,6},{3,7},{4,0},{5,1},{6,2},{7,3},{8,12},{9,13},{10,... | collective-permute-start | bytes 786440 | tf_op jit(solution)/shard_map/ppermute | solution.py:35
  16.9 1.2 copy-start.1
  19.0 15.5 %collective-permute-start.5 = (bf16[128,2048]{1,0:T(8,128)(2,1)S(1)}, bf16[128,2048]{1,0:T(8,128)(2,1)S(1)}, u32[]{:S(2)}, u32[]{:S(2)}) collective-permute-start(bf16[128,2048]{1,0:T(8,128)(2,1)S(1)} %get-tuple-element.86), channel_id=1, source_target_pairs={{0,16},{16,0},{1,17},{17,1},{2,18},{18,2},{3,19},{19,3},{4,20},{20... | collective-permute-start | bytes 1572872 | tf_op jit(solution)/shard_map/ppermute | solution.py:31
  23.7 9.3 %collective-permute-start.1 = (bf16[128,1024]{1,0:T(8,128)(2,1)S(1)}, bf16[128,1024]{1,0:T(8,128)(2,1)S(1)}, u32[]{:S(2)}, u32[]{:S(2)}) collective-permute-start(bf16[128,1024]{1,0:T(8,128)(2,1)S(1)} %collective-permute-done.refs_6_), channel_id=1, source_target_pairs={{0,1},{1,0},{2,3},{3,2},{4,5},{5,4},{6,7},{7,6},{8,9},{9,8},{10,11... | collective-permute-start | bytes 786440 | tf_op jit(solution)/shard_map/ppermute | solution.py:35
  33.1 8.8 %collective-permute-start.3 = (bf16[128,1024]{1,0:T(8,128)(2,1)S(1)}, bf16[128,1024]{1,0:T(8,128)(2,1)S(1)}, u32[]{:S(2)}, u32[]{:S(2)}) collective-permute-start(bf16[128,1024]{1,0:T(8,128)(2,1)S(1)} %collective-permute-done.2.refs_10_), channel_id=1, source_target_pairs={{0,2},{1,3},{2,0},{3,1},{4,6},{5,7},{6,4},{7,5},{8,10},{9,11},{10,... | collective-permute-start | bytes 786440 | tf_op jit(solution)/shard_map/ppermute | solution.py:35
  34.0 8.5 %collective-permute-start.9 = (bf16[128,1024]{1,0:T(8,128)(2,1)S(1)}, bf16[128,1024]{1,0:T(8,128)(2,1)S(1)}, u32[]{:S(2)}, u32[]{:S(2)}) collective-permute-start(bf16[128,1024]{1,0:T(8,128)(2,1)S(1)} %collective-permute-done.2.refs_10_), channel_id=1, source_target_pairs={{0,1},{1,0},{2,3},{3,2},{4,5},{5,4},{6,7},{7,6},{8,9},{9,8},{10,11... | collective-permute-start | bytes 786440 | tf_op jit(solution)/shard_map/ppermute | solution.py:35
  34.0 9.0 %collective-permute-start.7 = (bf16[128,1024]{1,0:T(8,128)(2,1)S(1)}, bf16[128,1024]{1,0:T(8,128)(2,1)S(1)}, u32[]{:S(2)}, u32[]{:S(2)}) collective-permute-start(bf16[128,1024]{1,0:T(8,128)(2,1)S(1)} %collective-permute-done.refs_6_), channel_id=1, source_target_pairs={{0,8},{8,0},{1,9},{9,1},{2,10},{10,2},{3,11},{11,3},{4,12},{12,4},... | collective-permute-start | bytes 786440 | tf_op jit(solution)/shard_map/ppermute | solution.py:27
  34.0 9.1 %collective-permute-start.8 = (bf16[128,1024]{1,0:T(8,128)(2,1)S(1)}, bf16[128,1024]{1,0:T(8,128)(2,1)S(1)}, u32[]{:S(2)}, u32[]{:S(2)}) collective-permute-start(bf16[128,1024]{1,0:T(8,128)(2,1)S(1)} %collective-permute-done.1.refs_7_), channel_id=1, source_target_pairs={{0,8},{8,0},{1,9},{9,1},{2,10},{10,2},{3,11},{11,3},{4,12},{12,4},... | collective-permute-start | bytes 786440 | tf_op jit(solution)/shard_map/ppermute | solution.py:27
  41.8 11.7 %collective-permute-start.12 = (bf16[128,1024]{1,0:T(8,128)(2,1)S(1)}, bf16[128,1024]{1,0:T(8,128)(2,1)S(1)}, u32[]{:S(2)}, u32[]{:S(2)}) collective-permute-start(bf16[128,1024]{1,0:T(8,128)(2,1)S(1)} %collective-permute-done.3.refs_2_), channel_id=1, source_target_pairs={{0,1},{1,0},{2,3},{3,2},{4,5},{5,4},{6,7},{7,6},{8,9},{9,8},{10,11... | collective-permute-start | bytes 786440 | tf_op jit(solution)/shard_map/ppermute | solution.py:35
  42.5 11.0 %collective-permute-start.10 = (bf16[128,1024]{1,0:T(8,128)(2,1)S(1)}, bf16[128,1024]{1,0:T(8,128)(2,1)S(1)}, u32[]{:S(2)}, u32[]{:S(2)}) collective-permute-start(bf16[128,1024]{1,0:T(8,128)(2,1)S(1)} %collective-permute-done.2.refs_10_), channel_id=1, source_target_pairs={{0,8},{8,0},{1,9},{9,1},{2,10},{10,2},{3,11},{11,3},{4,12},{12,4},... | collective-permute-start | bytes 786440 | tf_op jit(solution)/shard_map/ppermute | solution.py:27
  42.5 11.0 %collective-permute-start.11 = (bf16[128,1024]{1,0:T(8,128)(2,1)S(1)}, bf16[128,1024]{1,0:T(8,128)(2,1)S(1)}, u32[]{:S(2)}, u32[]{:S(2)}) collective-permute-start(bf16[128,1024]{1,0:T(8,128)(2,1)S(1)} %collective-permute-done.9.refs_11_), channel_id=1, source_target_pairs={{0,8},{8,0},{1,9},{9,1},{2,10},{10,2},{3,11},{11,3},{4,12},{12,4},... | collective-permute-start | bytes 786440 | tf_op jit(solution)/shard_map/ppermute | solution.py:27
  43.0 10.5 %collective-permute-start.6 = (bf16[128,1024]{1,0:T(8,128)(2,1)S(1)}, bf16[128,1024]{1,0:T(8,128)(2,1)S(1)}, u32[]{:S(2)}, u32[]{:S(2)}) collective-permute-start(bf16[128,1024]{1,0:T(8,128)(2,1)S(1)} %collective-permute-done.4.refs_3_), channel_id=1, source_target_pairs={{0,8},{8,0},{1,9},{9,1},{2,10},{10,2},{3,11},{11,3},{4,12},{12,4},... | collective-permute-start | bytes 786440 | tf_op jit(solution)/shard_map/ppermute | solution.py:27
  43.1 11.4 %collective-permute-start.13 = (bf16[128,1024]{1,0:T(8,128)(2,1)S(1)}, bf16[128,1024]{1,0:T(8,128)(2,1)S(1)}, u32[]{:S(2)}, u32[]{:S(2)}) collective-permute-start(bf16[128,1024]{1,0:T(8,128)(2,1)S(1)} %collective-permute-done.3.refs_2_), channel_id=1, source_target_pairs={{0,8},{8,0},{1,9},{9,1},{2,10},{10,2},{3,11},{11,3},{4,12},{12,4},... | collective-permute-start | bytes 786440 | tf_op jit(solution)/shard_map/ppermute | solution.py:27
  53.5 1.5 collective-permute-start.14
  55.5 8.4 %collective-permute-start.15 = (bf16[128,1024]{1,0:T(8,128)(2,1)S(1)}, bf16[128,1024]{1,0:T(8,128)(2,1)S(1)}, u32[]{:S(2)}, u32[]{:S(2)}) collective-permute-start(bf16[128,1024]{1,0:T(8,128)(2,1)S(1)} %get-tuple-element.93), channel_id=1, source_target_pairs={{0,16},{16,0},{1,17},{17,1},{2,18},{18,2},{3,19},{19,3},{4,20},{20... | collective-permute-start | bytes 786440 | tf_op jit(solution)/shard_map/ppermute | solution.py:31
  64.0 2.6 %collective-permute-start.16 = (bf16[144,1024]{1,0:T(8,128)(2,1)S(1)}, bf16[144,1024]{1,0:T(8,128)(2,1)S(1)}, u32[]{:S(2)}, u32[]{:S(2)}) collective-permute-start(bf16[144,1024]{1,0:T(8,128)(2,1)S(1)} %finish_latent.1.refs_0_), channel_id=1, source_target_pairs={{0,8},{8,0},{1,9},{9,1},{2,10},{10,2},{3,11},{11,3},{4,12},{12,4},... | collective-permute-start | bytes 884744 | tf_op jit(solution)/shard_map/ppermute | solution.py:27
  64.0 10.1 %collective-permute-start.18 = (bf16[144,1024]{1,0:T(8,128)(2,1)S(1)}, bf16[144,1024]{1,0:T(8,128)(2,1)S(1)}, u32[]{:S(2)}, u32[]{:S(2)}) collective-permute-start(bf16[144,1024]{1,0:T(8,128)(2,1)S(1)} %finish_latent.1.refs_0_), channel_id=1, source_target_pairs={{0,1},{1,0},{2,3},{3,2},{4,5},{5,4},{6,7},{7,6},{8,9},{9,8},{10,11... | collective-permute-start | bytes 884744 | tf_op jit(solution)/shard_map/ppermute | solution.py:35
  65.1 9.5 %collective-permute-start.17 = (bf16[144,1024]{1,0:T(8,128)(2,1)S(1)}, bf16[144,1024]{1,0:T(8,128)(2,1)S(1)}, u32[]{:S(2)}, u32[]{:S(2)}) collective-permute-start(bf16[144,1024]{1,0:T(8,128)(2,1)S(1)} %finish_latent.1.refs_0_), channel_id=1, source_target_pairs={{0,2},{1,3},{2,0},{3,1},{4,6},{5,7},{6,4},{7,5},{8,10},{9,11},{10,... | collective-permute-start | bytes 884744 | tf_op jit(solution)/shard_map/ppermute | solution.py:35
  74.6 2.9 %collective-permute-start.21 = (bf16[144,1024]{1,0:T(8,128)(2,1)S(1)}, bf16[144,1024]{1,0:T(8,128)(2,1)S(1)}, u32[]{:S(2)}, u32[]{:S(2)}) collective-permute-start(bf16[144,1024]{1,0:T(8,128)(2,1)S(1)} %collective-permute-done.18.refs_1_), channel_id=1, source_target_pairs={{0,8},{8,0},{1,9},{9,1},{2,10},{10,2},{3,11},{11,3},{4,12},{12,4},... | collective-permute-start | bytes 884744 | tf_op jit(solution)/shard_map/ppermute | solution.py:27
  74.7 2.9 %collective-permute-start.20 = (bf16[144,1024]{1,0:T(8,128)(2,1)S(1)}, bf16[144,1024]{1,0:T(8,128)(2,1)S(1)}, u32[]{:S(2)}, u32[]{:S(2)}) collective-permute-start(bf16[144,1024]{1,0:T(8,128)(2,1)S(1)} %collective-permute-done.17.refs_0_), channel_id=1, source_target_pairs={{0,8},{8,0},{1,9},{9,1},{2,10},{10,2},{3,11},{11,3},{4,12},{12,4},... | collective-permute-start | bytes 884744 | tf_op jit(solution)/shard_map/ppermute | solution.py:27
  75.2 16.2 %collective-permute-start.22 = (bf16[144,1024]{1,0:T(8,128)(2,1)S(1)}, bf16[144,1024]{1,0:T(8,128)(2,1)S(1)}, u32[]{:S(2)}, u32[]{:S(2)}) collective-permute-start(bf16[144,1024]{1,0:T(8,128)(2,1)S(1)} %finish_latent.1.refs_0_), channel_id=1, source_target_pairs={{0,4},{1,5},{2,6},{3,7},{4,0},{5,1},{6,2},{7,3},{8,12},{9,13},{10,... | collective-permute-start | bytes 884744 | tf_op jit(solution)/shard_map/ppermute | solution.py:35
  76.4 15.0 %collective-permute-start.23 = (bf16[144,1024]{1,0:T(8,128)(2,1)S(1)}, bf16[144,1024]{1,0:T(8,128)(2,1)S(1)}, u32[]{:S(2)}, u32[]{:S(2)}) collective-permute-start(bf16[144,1024]{1,0:T(8,128)(2,1)S(1)} %collective-permute-done.17.refs_0_), channel_id=1, source_target_pairs={{0,1},{1,0},{2,3},{3,2},{4,5},{5,4},{6,7},{7,6},{8,9},{9,8},{10,11... | collective-permute-start | bytes 884744 | tf_op jit(solution)/shard_map/ppermute | solution.py:35
  91.4 41.3 %collective-permute-start.28 = (bf16[256,1024]{1,0:T(8,128)(2,1)}, bf16[256,1024]{1,0:T(8,128)(2,1)}, u32[]{:S(2)}, u32[]{:S(2)}) collective-permute-start(bf16[256,1024]{1,0:T(8,128)(2,1)} %get-tuple-element.120), channel_id=1, source_target_pairs={{0,8},{8,0},{1,9},{9,1},{2,10},{10,2},{3,11},{11,3},{4,12},{12,4},... | collective-permute-start | bytes 1572872 | tf_op jit(solution)/shard_map/ppermute | solution.py:27
  130.7 71.2 %collective-permute-start.43 = (bf16[2,8,256,512]{3,2,1,0:T(8,128)(2,1)}, bf16[2,8,256,512]{3,2,1,0:T(8,128)(2,1)S(1)}, u32[]{:S(2)}, u32[]{:S(2)}) collective-permute-start(bf16[2,8,256,512]{3,2,1,0:T(8,128)(2,1)} %bitcast.6), channel_id=1, source_target_pairs={{0,8},{8,0},{1,9},{9,1},{2,10},{10,2},{3,11},{11,3},{4,12},{12,4},... | collective-permute-start | bytes 12582920 | tf_op jit(solution)/shard_map/ppermute | solution.py:27
  130.7 6.7 %collective-permute-start.25 = (bf16[144,1024]{1,0:T(8,128)(2,1)S(1)}, bf16[144,1024]{1,0:T(8,128)(2,1)S(1)}, u32[]{:S(2)}, u32[]{:S(2)}) collective-permute-start(bf16[144,1024]{1,0:T(8,128)(2,1)S(1)} %collective-permute-done.23.refs_1_), channel_id=1, source_target_pairs={{0,8},{8,0},{1,9},{9,1},{2,10},{10,2},{3,11},{11,3},{4,12},{12,4},... | collective-permute-start | bytes 884744 | tf_op jit(solution)/shard_map/ppermute | solution.py:27
  131.2 7.7 %collective-permute-start.24 = (bf16[144,1024]{1,0:T(8,128)(2,1)S(1)}, bf16[144,1024]{1,0:T(8,128)(2,1)S(1)}, u32[]{:S(2)}, u32[]{:S(2)}) collective-permute-start(bf16[144,1024]{1,0:T(8,128)(2,1)S(1)} %collective-permute-done.22.refs_0_), channel_id=1, source_target_pairs={{0,8},{8,0},{1,9},{9,1},{2,10},{10,2},{3,11},{11,3},{4,12},{12,4},... | collective-permute-start | bytes 884744 | tf_op jit(solution)/shard_map/ppermute | solution.py:27
  131.2 19.2 %collective-permute-start.27 = (bf16[144,1024]{1,0:T(8,128)(2,1)S(1)}, bf16[144,1024]{1,0:T(8,128)(2,1)S(1)}, u32[]{:S(2)}, u32[]{:S(2)}) collective-permute-start(bf16[144,1024]{1,0:T(8,128)(2,1)S(1)} %collective-permute-done.22.refs_0_), channel_id=1, source_target_pairs={{0,2},{1,3},{2,0},{3,1},{4,6},{5,7},{6,4},{7,5},{8,10},{9,11},{10,... | collective-permute-start | bytes 884744 | tf_op jit(solution)/shard_map/ppermute | solution.py:35
  132.7 17.7 %collective-permute-start.26 = (bf16[144,1024]{1,0:T(8,128)(2,1)S(1)}, bf16[144,1024]{1,0:T(8,128)(2,1)S(1)}, u32[]{:S(2)}, u32[]{:S(2)}) collective-permute-start(bf16[144,1024]{1,0:T(8,128)(2,1)S(1)} %collective-permute-done.22.refs_0_), channel_id=1, source_target_pairs={{0,1},{1,0},{2,3},{3,2},{4,5},{5,4},{6,7},{7,6},{8,9},{9,8},{10,11... | collective-permute-start | bytes 884744 | tf_op jit(solution)/shard_map/ppermute | solution.py:35
  137.4 13.0 %collective-permute-start.30 = (bf16[128,1024]{1,0:T(8,128)(2,1)S(1)}, bf16[128,1024]{1,0:T(8,128)(2,1)S(1)}, u32[]{:S(2)}, u32[]{:S(2)}) collective-permute-start(bf16[128,1024]{1,0:T(8,128)(2,1)S(1)} %get-tuple-element.161), channel_id=1, source_target_pairs={{0,2},{1,3},{2,0},{3,1},{4,6},{5,7},{6,4},{7,5},{8,10},{9,11},{10,... | collective-permute-start | bytes 786440 | tf_op jit(solution)/shard_map/ppermute | solution.py:35
  138.9 11.5 %collective-permute-start.29 = (bf16[128,1024]{1,0:T(8,128)(2,1)S(1)}, bf16[128,1024]{1,0:T(8,128)(2,1)S(1)}, u32[]{:S(2)}, u32[]{:S(2)}) collective-permute-start(bf16[128,1024]{1,0:T(8,128)(2,1)S(1)} %get-tuple-element.162), channel_id=1, source_target_pairs={{0,1},{1,0},{2,3},{3,2},{4,5},{5,4},{6,7},{7,6},{8,9},{9,8},{10,11... | collective-permute-start | bytes 786440 | tf_op jit(solution)/shard_map/ppermute | solution.py:35
  150.4 2.0 collective-permute-start.34
  150.5 15.0 %collective-permute-start.33 = (bf16[144,1024]{1,0:T(8,128)(2,1)S(1)}, bf16[144,1024]{1,0:T(8,128)(2,1)S(1)}, u32[]{:S(2)}, u32[]{:S(2)}) collective-permute-start(bf16[144,1024]{1,0:T(8,128)(2,1)S(1)} %collective-permute-done.27.refs_0_), channel_id=1, source_target_pairs={{0,1},{1,0},{2,3},{3,2},{4,5},{5,4},{6,7},{7,6},{8,9},{9,8},{10,11... | collective-permute-start | bytes 884744 | tf_op jit(solution)/shard_map/ppermute | solution.py:35
  151.1 2.4 %collective-permute-start.31 = (bf16[144,1024]{1,0:T(8,128)(2,1)S(1)}, bf16[144,1024]{1,0:T(8,128)(2,1)S(1)}, u32[]{:S(2)}, u32[]{:S(2)}) collective-permute-start(bf16[144,1024]{1,0:T(8,128)(2,1)S(1)} %collective-permute-done.27.refs_0_), channel_id=1, source_target_pairs={{0,8},{8,0},{1,9},{9,1},{2,10},{10,2},{3,11},{11,3},{4,12},{12,4},... | collective-permute-start | bytes 884744 | tf_op jit(solution)/shard_map/ppermute | solution.py:27
  151.2 2.3 %collective-permute-start.32 = (bf16[144,1024]{1,0:T(8,128)(2,1)S(1)}, bf16[144,1024]{1,0:T(8,128)(2,1)S(1)}, u32[]{:S(2)}, u32[]{:S(2)}) collective-permute-start(bf16[144,1024]{1,0:T(8,128)(2,1)S(1)} %collective-permute-done.26.refs_1_), channel_id=1, source_target_pairs={{0,8},{8,0},{1,9},{9,1},{2,10},{10,2},{3,11},{11,3},{4,12},{12,4},... | collective-permute-start | bytes 884744 | tf_op jit(solution)/shard_map/ppermute | solution.py:27
  152.5 13.1 %collective-permute-start.35 = (bf16[128,1024]{1,0:T(8,128)(2,1)S(1)}, bf16[128,1024]{1,0:T(8,128)(2,1)S(1)}, u32[]{:S(2)}, u32[]{:S(2)}) collective-permute-start(bf16[128,1024]{1,0:T(8,128)(2,1)S(1)} %add_convert_fusion.3), channel_id=1, source_target_pairs={{0,3},{1,2},{2,1},{3,0},{4,7},{5,6},{6,5},{7,4},{8,11},{9,10},{10,... | collective-permute-start | bytes 786440 | tf_op jit(solution)/shard_map/ppermute | solution.py:35
  165.5 1.9 collective-permute-start.37
  165.5 3.5 %collective-permute-start.36 = (bf16[144,1024]{1,0:T(8,128)(2,1)S(1)}, bf16[144,1024]{1,0:T(8,128)(2,1)S(1)}, u32[]{:S(2)}, u32[]{:S(2)}) collective-permute-start(bf16[144,1024]{1,0:T(8,128)(2,1)S(1)} %collective-permute-done.33.refs_0_), channel_id=1, source_target_pairs={{0,8},{8,0},{1,9},{9,1},{2,10},{10,2},{3,11},{11,3},{4,12},{12,4},... | collective-permute-start | bytes 884744 | tf_op jit(solution)/shard_map/ppermute | solution.py:27
  167.6 8.4 %collective-permute-start.39 = (bf16[128,1024]{1,0:T(8,128)(2,1)S(1)}, bf16[128,1024]{1,0:T(8,128)(2,1)S(1)}, u32[]{:S(2)}, u32[]{:S(2)}) collective-permute-start(bf16[128,1024]{1,0:T(8,128)(2,1)S(1)} %get-tuple-element.159), channel_id=1, source_target_pairs={{0,2},{1,3},{2,0},{3,1},{4,6},{5,7},{6,4},{7,5},{8,10},{9,11},{10,... | collective-permute-start | bytes 786440 | tf_op jit(solution)/shard_map/ppermute | solution.py:35
  168.5 11.3 %copy-start.3 = (bf16[128,1024]{1,0:T(8,128)(2,1)S(1)}, bf16[128,1024]{1,0:T(8,128)(2,1)}, u32[]{:S(2)}) copy-start(bf16[128,1024]{1,0:T(8,128)(2,1)} %copy-done.2) | copy-start | bytes 786436
  168.5 8.1 %collective-permute-start.38 = (bf16[128,1024]{1,0:T(8,128)(2,1)S(1)}, bf16[128,1024]{1,0:T(8,128)(2,1)S(1)}, u32[]{:S(2)}, u32[]{:S(2)}) collective-permute-start(bf16[128,1024]{1,0:T(8,128)(2,1)S(1)} %get-tuple-element.160), channel_id=1, source_target_pairs={{0,1},{1,0},{2,3},{3,2},{4,5},{5,4},{6,7},{7,6},{8,9},{9,8},{10,11... | collective-permute-start | bytes 786440 | tf_op jit(solution)/shard_map/ppermute | solution.py:35
  176.6 1.5 collective-permute-start.40
  178.2 9.3 %collective-permute-start.41 = (bf16[128,1024]{1,0:T(8,128)(2,1)S(1)}, bf16[128,1024]{1,0:T(8,128)(2,1)S(1)}, u32[]{:S(2)}, u32[]{:S(2)}) collective-permute-start(bf16[128,1024]{1,0:T(8,128)(2,1)S(1)} %fusion.2), channel_id=1, source_target_pairs={{0,3},{1,2},{2,1},{3,0},{4,7},{5,6},{6,5},{7,4},{8,11},{9,10},{10,... | collective-permute-start | bytes 786440 | tf_op jit(solution)/shard_map/ppermute | solution.py:35
  179.8 10.4 %collective-permute-start.19 = (bf16[128,1024]{1,0:T(8,128)(2,1)S(1)}, bf16[128,1024]{1,0:T(8,128)(2,1)S(1)}, u32[]{:S(2)}, u32[]{:S(2)}) collective-permute-start(bf16[128,1024]{1,0:T(8,128)(2,1)S(1)} %copy-done.3), channel_id=1, source_target_pairs={{0,8},{8,0},{1,9},{9,1},{2,10},{10,2},{3,11},{11,3},{4,12},{12,4},... | collective-permute-start | bytes 786440 | tf_op jit(solution)/shard_map/ppermute | solution.py:27
  187.7 14.1 %collective-permute-start.42 = (bf16[128,1024]{1,0:T(8,128)(2,1)S(1)}, bf16[128,1024]{1,0:T(8,128)(2,1)S(1)}, u32[]{:S(2)}, u32[]{:S(2)}) collective-permute-start(bf16[128,1024]{1,0:T(8,128)(2,1)S(1)} %add_convert_fusion), channel_id=1, source_target_pairs={{0,4},{1,5},{2,6},{3,7},{4,0},{5,1},{6,2},{7,3},{8,12},{9,13},{10,... | collective-permute-start | bytes 786440 | tf_op jit(solution)/shard_map/ppermute | solution.py:35
  (2 other events, 1.9 us)
Sparse Core Ops, SparseCore 0:
  9.5 59.4 all-gather.4
  74.7 55.9 all-gather.6

commit v12 on v11

--- a/solution.py
+++ b/solution.py
@@ -435,7 +435,7 @@
     for name in ((last - 1, 1), (last, 0), (last, 1)):
         shared += travel.pop(name).astype(jnp.float32)
     shared = shared.astype(jnp.bfloat16)
-    both_sides = after(both_sides, sums[last, 1])
+    both_sides = after(both_sides, shared)
     send("shared", shared, 2 * last - 2)
     *terms, swapped_sides = join(sums[0, 0], *travel.values(), swap_cores(both_sides))
     both_sides = pltpu.with_memory_space_constraint(both_sides, pltpu.HBM)

time: 214 us -> 172 us (0.80)
  waiting for transfers between devices: 102 us -> 61.7 us
    all_gather x1, waiting for transfers between devices: 39.3 us -> 0.02 us  [body(): lax.all_gather(travel.pop('up'), 'rep', axis=0, axis_index_groups=sides)]
    ppermute x21, waiting for transfers between devices: 49.5 us -> 45.6 us  [swap_ep(): lax.ppermute(array, 'ep', [(i, i ^ mask) for i in range(lax.axis_size('ep...]
    ppermute x21, waiting for transfers between devices: 6.27 us -> 9.18 us  [swap_cores(): return lax.ppermute(array, 'grp', [(0, 1), (1, 0)])]
  transfers between devices with their start and end apart: 46 -> 46, of which waited for: 18 -> 17; matrix products, arithmetic and copies ran while one was open for 2% -> 2% of each run, Pallas kernels for 22% -> 27%
where the time goes in v12:
time: 172 us; the launch traced here: 171 us
  waiting for transfers between devices  61.7 us (36%)
  Pallas kernels  50.6 us (29%)
  starting transfers between devices  37.4 us (22%)
  between operations  13.7 us (8%)
  local copies, waits for them, and re-layouts  4.93 us (3%)
  other arithmetic  2.99 us (2%)
    ppermute x21, waiting for transfers between devices, swap_ep(): lax.ppermute(array, 'ep', [(i, i ^ mask) for i in range(lax.axis_size('ep...  45.6 us
    pallas_call x5, Pallas kernels, expert_apply(): pl.pallas_call(functools.partial(expert_kernel, positions, count), out_sh...  43.6 us
    ppermute x21, starting transfers between devices, swap_ep(): lax.ppermute(array, 'ep', [(i, i ^ mask) for i in range(lax.axis_size('ep...  29.9 us
    ppermute x21, waiting for transfers between devices, swap_cores(): return lax.ppermute(array, 'grp', [(0, 1), (1, 0)])  9.18 us
    ppermute x2, waiting for transfers between devices, swap_reps(): lax.ppermute(array, 'rep', [(i, i ^ 1) for i in range(lax.axis_size('rep'...  6.83 us
    pallas_call x1, Pallas kernels, project(): pl.pallas_call(project_kernel, in_specs=[in_smem] + [in_vmem] * len(terms...  4.72 us
    ppermute x21, starting transfers between devices, swap_cores(): return lax.ppermute(array, 'grp', [(0, 1), (1, 0)])  4.28 us
  transfers between devices with their start and end apart: 46, of which 17 were waited for; matrix products, arithmetic and copies ran while one was open for 2% of the time, Pallas kernels for 27%

profile of v12, /device:TPU:0, one launch (start us, length us, event | category | flops | bytes accessed | tf_op | source)
XLA Modules:
  0.0 171.3 jit_solution(13057239774924932113)
XLA Ops:
  6.5 1.2 copy-done
  7.8 0.7 constant_dynamic-slice_fusion
  8.6 1.1 constant_dynamic-slice_fusion.1
  9.6 3.1 %collective-permute-start = (bf16[128,1024]{1,0:T(8,128)(2,1)S(1)}, bf16[128,1024]{1,0:T(8,128)(2,1)S(1)}, u32[]{:S(2)}, u32[]{:S(2)}) collective-permute-start(bf16[128,1024]{1,0:T(8,128)(2,1)S(1)} %get-tuple-element.158.refs_2_), channel_id=1, source_target_pairs={{0,2},{1,3},{2,0},{3,1},{4,6},{5,7},{6,4},{7,5},{8,10},{9,11},{10,... | collective-permute-start | bytes 786440 | tf_op jit(solution)/shard_map/ppermute | solution.py:35
  12.7 1.5 collective-permute-start.4
  14.2 2.6 %collective-permute-start.2 = (bf16[128,1024]{1,0:T(8,128)(2,1)S(1)}, bf16[128,1024]{1,0:T(8,128)(2,1)S(1)}, u32[]{:S(2)}, u32[]{:S(2)}) collective-permute-start(bf16[128,1024]{1,0:T(8,128)(2,1)S(1)} %get-tuple-element.158.refs_2_), channel_id=1, source_target_pairs={{0,4},{1,5},{2,6},{3,7},{4,0},{5,1},{6,2},{7,3},{8,12},{9,13},{10,... | collective-permute-start | bytes 786440 | tf_op jit(solution)/shard_map/ppermute | solution.py:35
  16.9 1.2 copy-done.1
  18.1 0.8 split_columns.1
  19.0 1.6 collective-permute-start.5
  20.5 0.7 fusion.1
  21.2 2.5 %collective-permute-done.refs_6_ = bf16[128,1024]{1,0:T(8,128)(2,1)S(1)} collective-permute-done((bf16[128,1024]{1,0:T(8,128)(2,1)S(1)}, bf16[128,1024]{1,0:T(8,128)(2,1)S(1)}, u32[]{:S(2)}, u32[]{:S(2)}) %collective-permute-start) | collective-permute-done | bytes 262176 | tf_op jit(solution)/shard_map/ppermute | solution.py:35
  23.7 3.8 %collective-permute-start.1 = (bf16[128,1024]{1,0:T(8,128)(2,1)S(1)}, bf16[128,1024]{1,0:T(8,128)(2,1)S(1)}, u32[]{:S(2)}, u32[]{:S(2)}) collective-permute-start(bf16[128,1024]{1,0:T(8,128)(2,1)S(1)} %collective-permute-done.refs_6_), channel_id=1, source_target_pairs={{0,1},{1,0},{2,3},{3,2},{4,5},{5,4},{6,7},{7,6},{8,9},{9,8},{10,11... | collective-permute-start | bytes 786440 | tf_op jit(solution)/shard_map/ppermute | solution.py:35
  27.5 0.7 fusion
  28.2 0.7 select_reduce_fusion.weights
  28.9 4.1 %collective-permute-done.2.refs_10_ = bf16[128,1024]{1,0:T(8,128)(2,1)S(1)} collective-permute-done((bf16[128,1024]{1,0:T(8,128)(2,1)S(1)}, bf16[128,1024]{1,0:T(8,128)(2,1)S(1)}, u32[]{:S(2)}, u32[]{:S(2)}) %collective-permute-start.2) | collective-permute-done | bytes 262176 | tf_op jit(solution)/shard_map/ppermute | solution.py:35
  33.0 0.9 collective-permute-start.3
  34.5 7.3 %collective-permute-done.3.refs_2_ = bf16[128,1024]{1,0:T(8,128)(2,1)S(1)} collective-permute-done((bf16[128,1024]{1,0:T(8,128)(2,1)S(1)}, bf16[128,1024]{1,0:T(8,128)(2,1)S(1)}, u32[]{:S(2)}, u32[]{:S(2)}) %collective-permute-start.3) | collective-permute-done | bytes 262176 | tf_op jit(solution)/shard_map/ppermute | solution.py:35
  41.8 0.7 collective-permute-start.12
  43.5 10.0 %collective-permute-done.12.refs_3_ = bf16[128,1024]{1,0:T(8,128)(2,1)S(1)} collective-permute-done((bf16[128,1024]{1,0:T(8,128)(2,1)S(1)}, bf16[128,1024]{1,0:T(8,128)(2,1)S(1)}, u32[]{:S(2)}, u32[]{:S(2)}) %collective-permute-start.12) | collective-permute-done | bytes 262176 | tf_op jit(solution)/shard_map/ppermute | solution.py:35
  53.5 1.0 down_project.2.refs_6_
  55.5 1.6 collective-permute-start.15
  57.1 6.8 %collective-permute-done.15.arrived = bf16[128,1024]{1,0:T(8,128)(2,1)S(1)} collective-permute-done((bf16[128,1024]{1,0:T(8,128)(2,1)S(1)}, bf16[128,1024]{1,0:T(8,128)(2,1)S(1)}, u32[]{:S(2)}, u32[]{:S(2)}) %collective-permute-start.15) | collective-permute-done | bytes 262176 | tf_op jit(solution)/shard_map/ppermute | solution.py:31
  64.0 1.0 collective-permute-start.18
  65.1 1.5 collective-permute-start.17
  66.6 6.8 %expert.5 = (bf16[128,1024]{1,0:T(8,128)(2,1)S(1)}, bf16[128,1024]{1,0:T(8,128)(2,1)S(1)}) custom-call(s32[1]{0:T(128)} %bitcast.1.where, bf16[144,1024]{1,0:T(8,128)(2,1)S(1)} %finish_latent.1.refs_0_, bf16[144,1024]{1,0:T(8,128)(2,1)S(1)} %collective-permute-done.16.refs_1_, bf16[1,1024,2048]{2,1,0:T(8,128)(2,1)} %refs_2_.3, ...), custom_call_target="tpu_custom_call" | custom-call | flops 805306368 | bytes 1048576 | tf_op jit(solution)/shard_map/expert/pallas_call | solution.py:248
  73.4 0.7 copy-done.2
  75.1 1.2 collective-permute-start.22
  76.3 1.2 collective-permute-start.23
  77.5 10.0 %expert.6 = (bf16[128,1024]{1,0:T(8,128)(2,1)S(1)}, bf16[128,1024]{1,0:T(8,128)(2,1)S(1)}, bf16[256,1024]{1,0:T(8,128)(2,1)S(1)}) custom-call(s32[1]{0:T(128)} %bitcast.1.where, bf16[144,1024]{1,0:T(8,128)(2,1)S(1)} %collective-permute-done.17.refs_0_, bf16[144,1024]{1,0:T(8,128)(2,1)S(1)} %collective-permute-done.18.refs_1_, ...), custom_call_target="tpu_custom_call" | custom-call | flops 1610612736 | bytes 2097152 | tf_op jit(solution)/shard_map/expert/pallas_call | solution.py:248
  87.5 3.8 %collective-permute-done.22.refs_0_ = bf16[144,1024]{1,0:T(8,128)(2,1)S(1)} collective-permute-done((bf16[144,1024]{1,0:T(8,128)(2,1)S(1)}, bf16[144,1024]{1,0:T(8,128)(2,1)S(1)}, u32[]{:S(2)}, u32[]{:S(2)}) %collective-permute-start.22) | collective-permute-done | bytes 294944 | tf_op jit(solution)/shard_map/ppermute | solution.py:35
  91.7 1.2 collective-permute-start.26
  93.3 1.9 %collective-permute-start.30 = (bf16[128,1024]{1,0:T(8,128)(2,1)S(1)}, bf16[128,1024]{1,0:T(8,128)(2,1)S(1)}, u32[]{:S(2)}, u32[]{:S(2)}) collective-permute-start(bf16[128,1024]{1,0:T(8,128)(2,1)S(1)} %get-tuple-element.161), channel_id=1, source_target_pairs={{0,2},{1,3},{2,0},{3,1},{4,6},{5,7},{6,4},{7,5},{8,10},{9,11},{10,... | collective-permute-start | bytes 786440 | tf_op jit(solution)/shard_map/ppermute | solution.py:35
  95.3 0.8 collective-permute-start.29
  96.1 10.0 %expert.7 = (bf16[128,1024]{1,0:T(8,128)(2,1)S(1)}, bf16[128,1024]{1,0:T(8,128)(2,1)S(1)}, bf16[256,1024]{1,0:T(8,128)(2,1)S(1)}) custom-call(s32[1]{0:T(128)} %bitcast.1.where, bf16[144,1024]{1,0:T(8,128)(2,1)S(1)} %collective-permute-done.22.refs_0_, bf16[144,1024]{1,0:T(8,128)(2,1)S(1)} %collective-permute-done.23.refs_1_, ...), custom_call_target="tpu_custom_call" | custom-call | flops 1610612736 | bytes 2097152 | tf_op jit(solution)/shard_map/expert/pallas_call | solution.py:248
  106.3 1.2 collective-permute-start.33
  108.2 2.5 %collective-permute-start.35 = (bf16[128,1024]{1,0:T(8,128)(2,1)S(1)}, bf16[128,1024]{1,0:T(8,128)(2,1)S(1)}, u32[]{:S(2)}, u32[]{:S(2)}) collective-permute-start(bf16[128,1024]{1,0:T(8,128)(2,1)S(1)} %add_convert_fusion.4), channel_id=1, source_target_pairs={{0,3},{1,2},{2,1},{3,0},{4,7},{5,6},{6,5},{7,4},{8,11},{9,10},{10,... | collective-permute-start | bytes 786440 | tf_op jit(solution)/shard_map/ppermute | solution.py:35
  110.7 10.0 %expert.8 = (bf16[128,1024]{1,0:T(8,128)(2,1)S(1)}, bf16[128,1024]{1,0:T(8,128)(2,1)S(1)}, bf16[256,1024]{1,0:T(8,128)(2,1)S(1)}) custom-call(s32[1]{0:T(128)} %bitcast.1.where, bf16[144,1024]{1,0:T(8,128)(2,1)S(1)} %collective-permute-done.27.refs_0_, bf16[144,1024]{1,0:T(8,128)(2,1)S(1)} %collective-permute-done.26.refs_1_, ...), custom_call_target="tpu_custom_call" | custom-call | flops 1610612736 | bytes 2097152 | tf_op jit(solution)/shard_map/expert/pallas_call | solution.py:248
  121.8 1.4 collective-permute-done.37
  123.4 1.8 %collective-permute-start.39 = (bf16[128,1024]{1,0:T(8,128)(2,1)S(1)}, bf16[128,1024]{1,0:T(8,128)(2,1)S(1)}, u32[]{:S(2)}, u32[]{:S(2)}) collective-permute-start(bf16[128,1024]{1,0:T(8,128)(2,1)S(1)} %get-tuple-element.159), channel_id=1, source_target_pairs={{0,2},{1,3},{2,0},{3,1},{4,6},{5,7},{6,4},{7,5},{8,10},{9,11},{10,... | collective-permute-start | bytes 786440 | tf_op jit(solution)/shard_map/ppermute | solution.py:35
  125.2 1.2 collective-permute-start.38
  126.5 6.9 %expert.9 = (bf16[128,1024]{1,0:T(8,128)(2,1)S(1)}, bf16[128,1024]{1,0:T(8,128)(2,1)S(1)}) custom-call(s32[1]{0:T(128)} %bitcast.1.where, bf16[144,1024]{1,0:T(8,128)(2,1)S(1)} %collective-permute-done.33.refs_0_, bf16[144,1024]{1,0:T(8,128)(2,1)S(1)} %collective-permute-done.36.refs_1_, bf16[1,1024,2048]{2,1,0:T(8,128)(2,1)} %refs_2_.3, ...), custom_call_target="tpu_custom_call" | custom-call | flops 805306368 | bytes 1048576 | tf_op jit(solution)/shard_map/expert/pallas_call | solution.py:248
  133.4 1.5 collective-permute-done.40
  135.0 1.0 collective-permute-start.41
  136.0 8.3 %collective-permute-done.41 = bf16[128,1024]{1,0:T(8,128)(2,1)S(1)} collective-permute-done((bf16[128,1024]{1,0:T(8,128)(2,1)S(1)}, bf16[128,1024]{1,0:T(8,128)(2,1)S(1)}, u32[]{:S(2)}, u32[]{:S(2)}) %collective-permute-start.41) | collective-permute-done | bytes 262176 | tf_op jit(solution)/shard_map/ppermute | solution.py:35
  145.2 0.7 collective-permute-start.42
  145.9 5.4 %collective-permute-done.19 = bf16[128,1024]{1,0:T(8,128)(2,1)S(1)} collective-permute-done((bf16[128,1024]{1,0:T(8,128)(2,1)S(1)}, bf16[128,1024]{1,0:T(8,128)(2,1)S(1)}, u32[]{:S(2)}, u32[]{:S(2)}) %collective-permute-start.19) | collective-permute-done | bytes 262176 | tf_op jit(solution)/shard_map/ppermute | solution.py:27
  151.4 8.4 %collective-permute-done.42.refs_4_ = bf16[128,1024]{1,0:T(8,128)(2,1)S(1)} collective-permute-done((bf16[128,1024]{1,0:T(8,128)(2,1)S(1)}, bf16[128,1024]{1,0:T(8,128)(2,1)S(1)}, u32[]{:S(2)}, u32[]{:S(2)}) %collective-permute-start.42) | collective-permute-done | bytes 262176 | tf_op jit(solution)/shard_map/ppermute | solution.py:35
  159.7 4.7 %project.1 = bf16[128,4096]{1,0:T(8,128)(2,1)} custom-call(s32[1]{0:T(128)} %bitcast.where, f32[128,1024]{1,0:T(8,128)S(1)} %convert_add_fusion.refs_0_, bf16[128,1024]{1,0:T(8,128)(2,1)S(1)} %collective-permute-done.29.refs_1_, bf16[128,1024]{1,0:T(8,128)(2,1)S(1)} %collective-permute-done.30.refs_2_, ...), custom_call_target="tpu_custom_call" | custom-call | flops 1073741824 | bytes 8388608 | tf_op jit(solution)/shard_map/project/pallas_call | solution.py:310
  (76 shorter events, 7.9 us)
Async XLA Ops:
  6.5 68.0 %all-gather.5.cloned.1.call-start = ((), (), s32[]{:S(2)}) async-start(), calls=%async_computation | async-start | bytes 2359296 | tf_op jit(solution)/shard_map/all_gather | solution.py:360
  8.5 136.1 %all-gather.7.cloned.1.call-start = ((), (), s32[]{:S(2)}) async-start(), calls=%async_computation.1 | async-start | bytes 6291456 | tf_op jit(solution)/shard_map/all_gather | solution.py:418
  9.6 14.1 %collective-permute-start = (bf16[128,1024]{1,0:T(8,128)(2,1)S(1)}, bf16[128,1024]{1,0:T(8,128)(2,1)S(1)}, u32[]{:S(2)}, u32[]{:S(2)}) collective-permute-start(bf16[128,1024]{1,0:T(8,128)(2,1)S(1)} %get-tuple-element.158.refs_2_), channel_id=1, source_target_pairs={{0,2},{1,3},{2,0},{3,1},{4,6},{5,7},{6,4},{7,5},{8,10},{9,11},{10,... | collective-permute-start | bytes 786440 | tf_op jit(solution)/shard_map/ppermute | solution.py:35
  12.7 21.3 %collective-permute-start.4 = (bf16[128,1024]{1,0:T(8,128)(2,1)S(1)}, bf16[128,1024]{1,0:T(8,128)(2,1)S(1)}, u32[]{:S(2)}, u32[]{:S(2)}) collective-permute-start(bf16[128,1024]{1,0:T(8,128)(2,1)S(1)} %get-tuple-element.158.refs_2_), channel_id=1, source_target_pairs={{0,1},{1,0},{2,3},{3,2},{4,5},{5,4},{6,7},{7,6},{8,9},{9,8},{10,11... | collective-permute-start | bytes 786440 | tf_op jit(solution)/shard_map/ppermute | solution.py:35
  14.2 18.8 %collective-permute-start.2 = (bf16[128,1024]{1,0:T(8,128)(2,1)S(1)}, bf16[128,1024]{1,0:T(8,128)(2,1)S(1)}, u32[]{:S(2)}, u32[]{:S(2)}) collective-permute-start(bf16[128,1024]{1,0:T(8,128)(2,1)S(1)} %get-tuple-element.158.refs_2_), channel_id=1, source_target_pairs={{0,4},{1,5},{2,6},{3,7},{4,0},{5,1},{6,2},{7,3},{8,12},{9,13},{10,... | collective-permute-start | bytes 786440 | tf_op jit(solution)/shard_map/ppermute | solution.py:35
  16.9 1.2 copy-start.1
  19.0 15.5 %collective-permute-start.5 = (bf16[128,2048]{1,0:T(8,128)(2,1)S(1)}, bf16[128,2048]{1,0:T(8,128)(2,1)S(1)}, u32[]{:S(2)}, u32[]{:S(2)}) collective-permute-start(bf16[128,2048]{1,0:T(8,128)(2,1)S(1)} %get-tuple-element.86), channel_id=1, source_target_pairs={{0,16},{16,0},{1,17},{17,1},{2,18},{18,2},{3,19},{19,3},{4,20},{20... | collective-permute-start | bytes 1572872 | tf_op jit(solution)/shard_map/ppermute | solution.py:31
  23.7 9.3 %collective-permute-start.1 = (bf16[128,1024]{1,0:T(8,128)(2,1)S(1)}, bf16[128,1024]{1,0:T(8,128)(2,1)S(1)}, u32[]{:S(2)}, u32[]{:S(2)}) collective-permute-start(bf16[128,1024]{1,0:T(8,128)(2,1)S(1)} %collective-permute-done.refs_6_), channel_id=1, source_target_pairs={{0,1},{1,0},{2,3},{3,2},{4,5},{5,4},{6,7},{7,6},{8,9},{9,8},{10,11... | collective-permute-start | bytes 786440 | tf_op jit(solution)/shard_map/ppermute | solution.py:35
  33.0 8.8 %collective-permute-start.3 = (bf16[128,1024]{1,0:T(8,128)(2,1)S(1)}, bf16[128,1024]{1,0:T(8,128)(2,1)S(1)}, u32[]{:S(2)}, u32[]{:S(2)}) collective-permute-start(bf16[128,1024]{1,0:T(8,128)(2,1)S(1)} %collective-permute-done.2.refs_10_), channel_id=1, source_target_pairs={{0,2},{1,3},{2,0},{3,1},{4,6},{5,7},{6,4},{7,5},{8,10},{9,11},{10,... | collective-permute-start | bytes 786440 | tf_op jit(solution)/shard_map/ppermute | solution.py:35
  34.0 8.5 %collective-permute-start.9 = (bf16[128,1024]{1,0:T(8,128)(2,1)S(1)}, bf16[128,1024]{1,0:T(8,128)(2,1)S(1)}, u32[]{:S(2)}, u32[]{:S(2)}) collective-permute-start(bf16[128,1024]{1,0:T(8,128)(2,1)S(1)} %collective-permute-done.2.refs_10_), channel_id=1, source_target_pairs={{0,1},{1,0},{2,3},{3,2},{4,5},{5,4},{6,7},{7,6},{8,9},{9,8},{10,11... | collective-permute-start | bytes 786440 | tf_op jit(solution)/shard_map/ppermute | solution.py:35
  34.0 9.0 %collective-permute-start.7 = (bf16[128,1024]{1,0:T(8,128)(2,1)S(1)}, bf16[128,1024]{1,0:T(8,128)(2,1)S(1)}, u32[]{:S(2)}, u32[]{:S(2)}) collective-permute-start(bf16[128,1024]{1,0:T(8,128)(2,1)S(1)} %collective-permute-done.refs_6_), channel_id=1, source_target_pairs={{0,8},{8,0},{1,9},{9,1},{2,10},{10,2},{3,11},{11,3},{4,12},{12,4},... | collective-permute-start | bytes 786440 | tf_op jit(solution)/shard_map/ppermute | solution.py:27
  34.0 9.1 %collective-permute-start.8 = (bf16[128,1024]{1,0:T(8,128)(2,1)S(1)}, bf16[128,1024]{1,0:T(8,128)(2,1)S(1)}, u32[]{:S(2)}, u32[]{:S(2)}) collective-permute-start(bf16[128,1024]{1,0:T(8,128)(2,1)S(1)} %collective-permute-done.1.refs_7_), channel_id=1, source_target_pairs={{0,8},{8,0},{1,9},{9,1},{2,10},{10,2},{3,11},{11,3},{4,12},{12,4},... | collective-permute-start | bytes 786440 | tf_op jit(solution)/shard_map/ppermute | solution.py:27
  41.8 11.7 %collective-permute-start.12 = (bf16[128,1024]{1,0:T(8,128)(2,1)S(1)}, bf16[128,1024]{1,0:T(8,128)(2,1)S(1)}, u32[]{:S(2)}, u32[]{:S(2)}) collective-permute-start(bf16[128,1024]{1,0:T(8,128)(2,1)S(1)} %collective-permute-done.3.refs_2_), channel_id=1, source_target_pairs={{0,1},{1,0},{2,3},{3,2},{4,5},{5,4},{6,7},{7,6},{8,9},{9,8},{10,11... | collective-permute-start | bytes 786440 | tf_op jit(solution)/shard_map/ppermute | solution.py:35
  42.5 11.0 %collective-permute-start.10 = (bf16[128,1024]{1,0:T(8,128)(2,1)S(1)}, bf16[128,1024]{1,0:T(8,128)(2,1)S(1)}, u32[]{:S(2)}, u32[]{:S(2)}) collective-permute-start(bf16[128,1024]{1,0:T(8,128)(2,1)S(1)} %collective-permute-done.2.refs_10_), channel_id=1, source_target_pairs={{0,8},{8,0},{1,9},{9,1},{2,10},{10,2},{3,11},{11,3},{4,12},{12,4},... | collective-permute-start | bytes 786440 | tf_op jit(solution)/shard_map/ppermute | solution.py:27
  42.5 11.0 %collective-permute-start.11 = (bf16[128,1024]{1,0:T(8,128)(2,1)S(1)}, bf16[128,1024]{1,0:T(8,128)(2,1)S(1)}, u32[]{:S(2)}, u32[]{:S(2)}) collective-permute-start(bf16[128,1024]{1,0:T(8,128)(2,1)S(1)} %collective-permute-done.9.refs_11_), channel_id=1, source_target_pairs={{0,8},{8,0},{1,9},{9,1},{2,10},{10,2},{3,11},{11,3},{4,12},{12,4},... | collective-permute-start | bytes 786440 | tf_op jit(solution)/shard_map/ppermute | solution.py:27
  43.0 10.5 %collective-permute-start.6 = (bf16[128,1024]{1,0:T(8,128)(2,1)S(1)}, bf16[128,1024]{1,0:T(8,128)(2,1)S(1)}, u32[]{:S(2)}, u32[]{:S(2)}) collective-permute-start(bf16[128,1024]{1,0:T(8,128)(2,1)S(1)} %collective-permute-done.4.refs_3_), channel_id=1, source_target_pairs={{0,8},{8,0},{1,9},{9,1},{2,10},{10,2},{3,11},{11,3},{4,12},{12,4},... | collective-permute-start | bytes 786440 | tf_op jit(solution)/shard_map/ppermute | solution.py:27
  43.1 11.4 %collective-permute-start.13 = (bf16[128,1024]{1,0:T(8,128)(2,1)S(1)}, bf16[128,1024]{1,0:T(8,128)(2,1)S(1)}, u32[]{:S(2)}, u32[]{:S(2)}) collective-permute-start(bf16[128,1024]{1,0:T(8,128)(2,1)S(1)} %collective-permute-done.3.refs_2_), channel_id=1, source_target_pairs={{0,8},{8,0},{1,9},{9,1},{2,10},{10,2},{3,11},{11,3},{4,12},{12,4},... | collective-permute-start | bytes 786440 | tf_op jit(solution)/shard_map/ppermute | solution.py:27
  53.5 1.5 collective-permute-start.14
  55.5 8.4 %collective-permute-start.15 = (bf16[128,1024]{1,0:T(8,128)(2,1)S(1)}, bf16[128,1024]{1,0:T(8,128)(2,1)S(1)}, u32[]{:S(2)}, u32[]{:S(2)}) collective-permute-start(bf16[128,1024]{1,0:T(8,128)(2,1)S(1)} %get-tuple-element.93), channel_id=1, source_target_pairs={{0,16},{16,0},{1,17},{17,1},{2,18},{18,2},{3,19},{19,3},{4,20},{20... | collective-permute-start | bytes 786440 | tf_op jit(solution)/shard_map/ppermute | solution.py:31
  63.9 2.6 %collective-permute-start.16 = (bf16[144,1024]{1,0:T(8,128)(2,1)S(1)}, bf16[144,1024]{1,0:T(8,128)(2,1)S(1)}, u32[]{:S(2)}, u32[]{:S(2)}) collective-permute-start(bf16[144,1024]{1,0:T(8,128)(2,1)S(1)} %finish_latent.1.refs_0_), channel_id=1, source_target_pairs={{0,8},{8,0},{1,9},{9,1},{2,10},{10,2},{3,11},{11,3},{4,12},{12,4},... | collective-permute-start | bytes 884744 | tf_op jit(solution)/shard_map/ppermute | solution.py:27
  64.0 10.1 %collective-permute-start.18 = (bf16[144,1024]{1,0:T(8,128)(2,1)S(1)}, bf16[144,1024]{1,0:T(8,128)(2,1)S(1)}, u32[]{:S(2)}, u32[]{:S(2)}) collective-permute-start(bf16[144,1024]{1,0:T(8,128)(2,1)S(1)} %finish_latent.1.refs_0_), channel_id=1, source_target_pairs={{0,1},{1,0},{2,3},{3,2},{4,5},{5,4},{6,7},{7,6},{8,9},{9,8},{10,11... | collective-permute-start | bytes 884744 | tf_op jit(solution)/shard_map/ppermute | solution.py:35
  65.1 9.5 %collective-permute-start.17 = (bf16[144,1024]{1,0:T(8,128)(2,1)S(1)}, bf16[144,1024]{1,0:T(8,128)(2,1)S(1)}, u32[]{:S(2)}, u32[]{:S(2)}) collective-permute-start(bf16[144,1024]{1,0:T(8,128)(2,1)S(1)} %finish_latent.1.refs_0_), channel_id=1, source_target_pairs={{0,2},{1,3},{2,0},{3,1},{4,6},{5,7},{6,4},{7,5},{8,10},{9,11},{10,... | collective-permute-start | bytes 884744 | tf_op jit(solution)/shard_map/ppermute | solution.py:35
  74.6 2.9 %collective-permute-start.21 = (bf16[144,1024]{1,0:T(8,128)(2,1)S(1)}, bf16[144,1024]{1,0:T(8,128)(2,1)S(1)}, u32[]{:S(2)}, u32[]{:S(2)}) collective-permute-start(bf16[144,1024]{1,0:T(8,128)(2,1)S(1)} %collective-permute-done.18.refs_1_), channel_id=1, source_target_pairs={{0,8},{8,0},{1,9},{9,1},{2,10},{10,2},{3,11},{11,3},{4,12},{12,4},... | collective-permute-start | bytes 884744 | tf_op jit(solution)/shard_map/ppermute | solution.py:27
  74.6 2.9 %collective-permute-start.20 = (bf16[144,1024]{1,0:T(8,128)(2,1)S(1)}, bf16[144,1024]{1,0:T(8,128)(2,1)S(1)}, u32[]{:S(2)}, u32[]{:S(2)}) collective-permute-start(bf16[144,1024]{1,0:T(8,128)(2,1)S(1)} %collective-permute-done.17.refs_0_), channel_id=1, source_target_pairs={{0,8},{8,0},{1,9},{9,1},{2,10},{10,2},{3,11},{11,3},{4,12},{12,4},... | collective-permute-start | bytes 884744 | tf_op jit(solution)/shard_map/ppermute | solution.py:27
  75.1 16.1 %collective-permute-start.22 = (bf16[144,1024]{1,0:T(8,128)(2,1)S(1)}, bf16[144,1024]{1,0:T(8,128)(2,1)S(1)}, u32[]{:S(2)}, u32[]{:S(2)}) collective-permute-start(bf16[144,1024]{1,0:T(8,128)(2,1)S(1)} %finish_latent.1.refs_0_), channel_id=1, source_target_pairs={{0,4},{1,5},{2,6},{3,7},{4,0},{5,1},{6,2},{7,3},{8,12},{9,13},{10,... | collective-permute-start | bytes 884744 | tf_op jit(solution)/shard_map/ppermute | solution.py:35
  76.3 14.9 %collective-permute-start.23 = (bf16[144,1024]{1,0:T(8,128)(2,1)S(1)}, bf16[144,1024]{1,0:T(8,128)(2,1)S(1)}, u32[]{:S(2)}, u32[]{:S(2)}) collective-permute-start(bf16[144,1024]{1,0:T(8,128)(2,1)S(1)} %collective-permute-done.17.refs_0_), channel_id=1, source_target_pairs={{0,1},{1,0},{2,3},{3,2},{4,5},{5,4},{6,7},{7,6},{8,9},{9,8},{10,11... | collective-permute-start | bytes 884744 | tf_op jit(solution)/shard_map/ppermute | solution.py:35
  91.2 1.9 %collective-permute-start.28 = (bf16[256,1024]{1,0:T(8,128)(2,1)S(1)}, bf16[256,1024]{1,0:T(8,128)(2,1)S(1)}, u32[]{:S(2)}, u32[]{:S(2)}) collective-permute-start(bf16[256,1024]{1,0:T(8,128)(2,1)S(1)} %get-tuple-element.120), channel_id=1, source_target_pairs={{0,8},{8,0},{1,9},{9,1},{2,10},{10,2},{3,11},{11,3},{4,12},{12,4},... | collective-permute-start | bytes 1572872 | tf_op jit(solution)/shard_map/ppermute | solution.py:27
  91.2 4.1 %collective-permute-start.25 = (bf16[144,1024]{1,0:T(8,128)(2,1)S(1)}, bf16[144,1024]{1,0:T(8,128)(2,1)S(1)}, u32[]{:S(2)}, u32[]{:S(2)}) collective-permute-start(bf16[144,1024]{1,0:T(8,128)(2,1)S(1)} %collective-permute-done.23.refs_1_), channel_id=1, source_target_pairs={{0,8},{8,0},{1,9},{9,1},{2,10},{10,2},{3,11},{11,3},{4,12},{12,4},... | collective-permute-start | bytes 884744 | tf_op jit(solution)/shard_map/ppermute | solution.py:27
  91.7 14.3 %collective-permute-start.27 = (bf16[144,1024]{1,0:T(8,128)(2,1)S(1)}, bf16[144,1024]{1,0:T(8,128)(2,1)S(1)}, u32[]{:S(2)}, u32[]{:S(2)}) collective-permute-start(bf16[144,1024]{1,0:T(8,128)(2,1)S(1)} %collective-permute-done.22.refs_0_), channel_id=1, source_target_pairs={{0,2},{1,3},{2,0},{3,1},{4,6},{5,7},{6,4},{7,5},{8,10},{9,11},{10,... | collective-permute-start | bytes 884744 | tf_op jit(solution)/shard_map/ppermute | solution.py:35
  91.7 14.3 %collective-permute-start.26 = (bf16[144,1024]{1,0:T(8,128)(2,1)S(1)}, bf16[144,1024]{1,0:T(8,128)(2,1)S(1)}, u32[]{:S(2)}, u32[]{:S(2)}) collective-permute-start(bf16[144,1024]{1,0:T(8,128)(2,1)S(1)} %collective-permute-done.22.refs_0_), channel_id=1, source_target_pairs={{0,1},{1,0},{2,3},{3,2},{4,5},{5,4},{6,7},{7,6},{8,9},{9,8},{10,11... | collective-permute-start | bytes 884744 | tf_op jit(solution)/shard_map/ppermute | solution.py:35
  93.0 3.1 %collective-permute-start.24 = (bf16[144,1024]{1,0:T(8,128)(2,1)S(1)}, bf16[144,1024]{1,0:T(8,128)(2,1)S(1)}, u32[]{:S(2)}, u32[]{:S(2)}) collective-permute-start(bf16[144,1024]{1,0:T(8,128)(2,1)S(1)} %collective-permute-done.22.refs_0_), channel_id=1, source_target_pairs={{0,8},{8,0},{1,9},{9,1},{2,10},{10,2},{3,11},{11,3},{4,12},{12,4},... | collective-permute-start | bytes 884744 | tf_op jit(solution)/shard_map/ppermute | solution.py:27
  93.3 12.9 %collective-permute-start.30 = (bf16[128,1024]{1,0:T(8,128)(2,1)S(1)}, bf16[128,1024]{1,0:T(8,128)(2,1)S(1)}, u32[]{:S(2)}, u32[]{:S(2)}) collective-permute-start(bf16[128,1024]{1,0:T(8,128)(2,1)S(1)} %get-tuple-element.161), channel_id=1, source_target_pairs={{0,2},{1,3},{2,0},{3,1},{4,6},{5,7},{6,4},{7,5},{8,10},{9,11},{10,... | collective-permute-start | bytes 786440 | tf_op jit(solution)/shard_map/ppermute | solution.py:35
  95.3 11.0 %collective-permute-start.29 = (bf16[128,1024]{1,0:T(8,128)(2,1)S(1)}, bf16[128,1024]{1,0:T(8,128)(2,1)S(1)}, u32[]{:S(2)}, u32[]{:S(2)}) collective-permute-start(bf16[128,1024]{1,0:T(8,128)(2,1)S(1)} %get-tuple-element.162), channel_id=1, source_target_pairs={{0,1},{1,0},{2,3},{3,2},{4,5},{5,4},{6,7},{7,6},{8,9},{9,8},{10,11... | collective-permute-start | bytes 786440 | tf_op jit(solution)/shard_map/ppermute | solution.py:35
  106.3 1.9 %collective-permute-start.34 = (bf16[256,1024]{1,0:T(8,128)(2,1)S(1)}, bf16[256,1024]{1,0:T(8,128)(2,1)S(1)}, u32[]{:S(2)}, u32[]{:S(2)}) collective-permute-start(bf16[256,1024]{1,0:T(8,128)(2,1)S(1)} %get-tuple-element.134), channel_id=1, source_target_pairs={{0,8},{8,0},{1,9},{9,1},{2,10},{10,2},{3,11},{11,3},{4,12},{12,4},... | collective-permute-start | bytes 1572872 | tf_op jit(solution)/shard_map/ppermute | solution.py:27
  106.3 15.0 %collective-permute-start.33 = (bf16[144,1024]{1,0:T(8,128)(2,1)S(1)}, bf16[144,1024]{1,0:T(8,128)(2,1)S(1)}, u32[]{:S(2)}, u32[]{:S(2)}) collective-permute-start(bf16[144,1024]{1,0:T(8,128)(2,1)S(1)} %collective-permute-done.27.refs_0_), channel_id=1, source_target_pairs={{0,1},{1,0},{2,3},{3,2},{4,5},{5,4},{6,7},{7,6},{8,9},{9,8},{10,11... | collective-permute-start | bytes 884744 | tf_op jit(solution)/shard_map/ppermute | solution.py:35
  107.5 3.2 %collective-permute-start.31 = (bf16[144,1024]{1,0:T(8,128)(2,1)S(1)}, bf16[144,1024]{1,0:T(8,128)(2,1)S(1)}, u32[]{:S(2)}, u32[]{:S(2)}) collective-permute-start(bf16[144,1024]{1,0:T(8,128)(2,1)S(1)} %collective-permute-done.27.refs_0_), channel_id=1, source_target_pairs={{0,8},{8,0},{1,9},{9,1},{2,10},{10,2},{3,11},{11,3},{4,12},{12,4},... | collective-permute-start | bytes 884744 | tf_op jit(solution)/shard_map/ppermute | solution.py:27
  107.7 3.0 %collective-permute-start.32 = (bf16[144,1024]{1,0:T(8,128)(2,1)S(1)}, bf16[144,1024]{1,0:T(8,128)(2,1)S(1)}, u32[]{:S(2)}, u32[]{:S(2)}) collective-permute-start(bf16[144,1024]{1,0:T(8,128)(2,1)S(1)} %collective-permute-done.26.refs_1_), channel_id=1, source_target_pairs={{0,8},{8,0},{1,9},{9,1},{2,10},{10,2},{3,11},{11,3},{4,12},{12,4},... | collective-permute-start | bytes 884744 | tf_op jit(solution)/shard_map/ppermute | solution.py:27
  108.2 13.1 %collective-permute-start.35 = (bf16[128,1024]{1,0:T(8,128)(2,1)S(1)}, bf16[128,1024]{1,0:T(8,128)(2,1)S(1)}, u32[]{:S(2)}, u32[]{:S(2)}) collective-permute-start(bf16[128,1024]{1,0:T(8,128)(2,1)S(1)} %add_convert_fusion.4), channel_id=1, source_target_pairs={{0,3},{1,2},{2,1},{3,0},{4,7},{5,6},{6,5},{7,4},{8,11},{9,10},{10,... | collective-permute-start | bytes 786440 | tf_op jit(solution)/shard_map/ppermute | solution.py:35
  121.3 1.9 %collective-permute-start.37 = (bf16[256,1024]{1,0:T(8,128)(2,1)S(1)}, bf16[256,1024]{1,0:T(8,128)(2,1)S(1)}, u32[]{:S(2)}, u32[]{:S(2)}) collective-permute-start(bf16[256,1024]{1,0:T(8,128)(2,1)S(1)} %get-tuple-element.143), channel_id=1, source_target_pairs={{0,8},{8,0},{1,9},{9,1},{2,10},{10,2},{3,11},{11,3},{4,12},{12,4},... | collective-permute-start | bytes 1572872 | tf_op jit(solution)/shard_map/ppermute | solution.py:27
  121.3 5.2 %collective-permute-start.36 = (bf16[144,1024]{1,0:T(8,128)(2,1)S(1)}, bf16[144,1024]{1,0:T(8,128)(2,1)S(1)}, u32[]{:S(2)}, u32[]{:S(2)}) collective-permute-start(bf16[144,1024]{1,0:T(8,128)(2,1)S(1)} %collective-permute-done.33.refs_0_), channel_id=1, source_target_pairs={{0,8},{8,0},{1,9},{9,1},{2,10},{10,2},{3,11},{11,3},{4,12},{12,4},... | collective-permute-start | bytes 884744 | tf_op jit(solution)/shard_map/ppermute | solution.py:27
  123.4 9.9 %collective-permute-start.39 = (bf16[128,1024]{1,0:T(8,128)(2,1)S(1)}, bf16[128,1024]{1,0:T(8,128)(2,1)S(1)}, u32[]{:S(2)}, u32[]{:S(2)}) collective-permute-start(bf16[128,1024]{1,0:T(8,128)(2,1)S(1)} %get-tuple-element.159), channel_id=1, source_target_pairs={{0,2},{1,3},{2,0},{3,1},{4,6},{5,7},{6,4},{7,5},{8,10},{9,11},{10,... | collective-permute-start | bytes 786440 | tf_op jit(solution)/shard_map/ppermute | solution.py:35
  125.2 19.5 %copy-start.3 = (bf16[128,1024]{1,0:T(8,128)(2,1)S(1)}, bf16[128,1024]{1,0:T(8,128)(2,1)}, u32[]{:S(2)}) copy-start(bf16[128,1024]{1,0:T(8,128)(2,1)} %copy-done.2) | copy-start | bytes 786436
  125.2 8.1 %collective-permute-start.38 = (bf16[128,1024]{1,0:T(8,128)(2,1)S(1)}, bf16[128,1024]{1,0:T(8,128)(2,1)S(1)}, u32[]{:S(2)}, u32[]{:S(2)}) collective-permute-start(bf16[128,1024]{1,0:T(8,128)(2,1)S(1)} %get-tuple-element.160), channel_id=1, source_target_pairs={{0,1},{1,0},{2,3},{3,2},{4,5},{5,4},{6,7},{7,6},{8,9},{9,8},{10,11... | collective-permute-start | bytes 786440 | tf_op jit(solution)/shard_map/ppermute | solution.py:35
  133.4 1.6 collective-permute-start.40
  135.0 9.3 %collective-permute-start.41 = (bf16[128,1024]{1,0:T(8,128)(2,1)S(1)}, bf16[128,1024]{1,0:T(8,128)(2,1)S(1)}, u32[]{:S(2)}, u32[]{:S(2)}) collective-permute-start(bf16[128,1024]{1,0:T(8,128)(2,1)S(1)} %add_convert_fusion.1), channel_id=1, source_target_pairs={{0,3},{1,2},{2,1},{3,0},{4,7},{5,6},{6,5},{7,4},{8,11},{9,10},{10,... | collective-permute-start | bytes 786440 | tf_op jit(solution)/shard_map/ppermute | solution.py:35
  144.6 15.1 %collective-permute-start.43 = (bf16[2,8,256,512]{3,2,1,0:T(8,128)(2,1)}, bf16[2,8,256,512]{3,2,1,0:T(8,128)(2,1)S(1)}, u32[]{:S(2)}, u32[]{:S(2)}) collective-permute-start(bf16[2,8,256,512]{3,2,1,0:T(8,128)(2,1)} %bitcast.6), channel_id=1, source_target_pairs={{0,8},{8,0},{1,9},{9,1},{2,10},{10,2},{3,11},{11,3},{4,12},{12,4},... | collective-permute-start | bytes 12582920 | tf_op jit(solution)/shard_map/ppermute | solution.py:27
  144.7 6.6 %collective-permute-start.19 = (bf16[128,1024]{1,0:T(8,128)(2,1)S(1)}, bf16[128,1024]{1,0:T(8,128)(2,1)S(1)}, u32[]{:S(2)}, u32[]{:S(2)}) collective-permute-start(bf16[128,1024]{1,0:T(8,128)(2,1)S(1)} %copy-done.3), channel_id=1, source_target_pairs={{0,8},{8,0},{1,9},{9,1},{2,10},{10,2},{3,11},{11,3},{4,12},{12,4},... | collective-permute-start | bytes 786440 | tf_op jit(solution)/shard_map/ppermute | solution.py:27
  145.2 14.5 %collective-permute-start.42 = (bf16[128,1024]{1,0:T(8,128)(2,1)S(1)}, bf16[128,1024]{1,0:T(8,128)(2,1)S(1)}, u32[]{:S(2)}, u32[]{:S(2)}) collective-permute-start(bf16[128,1024]{1,0:T(8,128)(2,1)S(1)} %add_convert_fusion), channel_id=1, source_target_pairs={{0,4},{1,5},{2,6},{3,7},{4,0},{5,1},{6,2},{7,3},{8,12},{9,13},{10,... | collective-permute-start | bytes 786440 | tf_op jit(solution)/shard_map/ppermute | solution.py:35
  (2 other events, 1.9 us)
Sparse Core Ops, SparseCore 0:
  9.5 59.4 all-gather.4
  77.6 55.9 all-gather.6

commit v13 on v12

--- a/solution.py
+++ b/solution.py
@@ -164,18 +164,26 @@
     def columns_at(start):
         return pl.ds(pl.multiple_of(start, width), width)
 
-    def read(i, part):
+    chunks = blocks // 2 + 1
+
+    def read(j, part, size):
         source, target = ((gate, gate_block), (up, up_block), (out, out_block))[part]
-        columns = columns_at(i * width)
-        return pltpu.make_async_copy(
-            source.at[0, :, columns], target.at[:, columns], sems.at[part * blocks + i]
-        )
-
-    for i in range(blocks):
-        read(i, 0).start()
-        read(i, 1).start()
-    for i in range(out.shape[2] // width):
-        read(i, 2).start()
+        start = 2 * j * width if part == 2 else max(2 * j - 1, 0) * width
+        return copy_columns(source, target, start, size, sems.at[part * chunks + j])
+
+    def copy_columns(source, target, start, size, sem):
+        columns = pl.ds(pl.multiple_of(start, width), size)
+        return pltpu.make_async_copy(source.at[0, :, columns], target.at[:, columns], sem)
+
+    def size_of(j):
+        return width if j in (0, chunks - 1) else 2 * width
+
+    out_chunks = out.shape[2] // (2 * width)
+    for j in range(chunks):
+        read(j, 0, size_of(j)).start()
+        read(j, 1, size_of(j)).start()
+    for j in range(out_chunks):
+        read(j, 2, 2 * width).start()
     for i, piece in enumerate(pieces):
         rows[i * count : (i + 1) * count] = piece[:count]
 
@@ -189,9 +197,9 @@
 
     scales = [scale_of(piece) for piece in pieces]
 
-    def arrive(i):
-        read(i, 0).wait()
-        read(i, 1).wait()
+    def arrive(j, start, size):
+        copy_columns(gate, gate_block, start, size, sems.at[j]).wait()
+        copy_columns(up, up_block, start, size, sems.at[chunks + j]).wait()
 
     def products(i):
         columns = columns_at(i * width)
@@ -204,12 +212,11 @@
         value = gate_value / (1.0 + jnp.exp(-gate_value)) * up_value
         hidden[:, columns_at(i * width)] = value.astype(jnp.bfloat16)
 
-    arrive(0)
+    arrive(0, 0, width)
     held[0], held[1] = products(0)
 
     def step(i, carry):
-        arrive(2 * i + 1)
-        arrive(2 * i + 2)
+        arrive(i + 1, (2 * i + 1) * width, 2 * width)
         first = products(2 * i + 1)
         activate(held[0], held[1], 2 * i)
         second = products(2 * i + 2)
@@ -218,24 +225,26 @@
         return carry
 
     lax.fori_loop(0, blocks // 2 - 1, step, 0)
-    arrive(blocks - 1)
+    arrive(chunks - 1, (blocks - 1) * width, width)
     last = products(blocks - 1)
     activate(held[0], held[1], blocks - 2)
     activate(*last, blocks - 1)
 
     def finish(i, carry):
-        columns = columns_at(i * width)
-        read(i, 2).wait()
-        value = jnp.dot(hidden[...], out_block[:, columns], preferred_element_type=jnp.float32)
-        for j, scale in enumerate(scales):
-            scaled = (value[j * count : (j + 1) * count] * scale).astype(jnp.bfloat16)
-            if j < positions:
-                own_sums[j][:, columns] = scaled
-            else:
-                other_sums[(j - positions) * count : (j - positions + 1) * count, columns] = scaled
+        copy_columns(out, out_block, 2 * i * width, 2 * width, sems.at[2 * chunks + i]).wait()
+        for half in range(2):
+            columns = columns_at((2 * i + half) * width)
+            value = jnp.dot(hidden[...], out_block[:, columns], preferred_element_type=jnp.float32)
+            for j, scale in enumerate(scales):
+                scaled = (value[j * count : (j + 1) * count] * scale).astype(jnp.bfloat16)
+                if j < positions:
+                    own_sums[j][:, columns] = scaled
+                else:
+                    start = (j - positions) * count
+                    other_sums[start : start + count, columns] = scaled
         return carry
 
-    lax.fori_loop(0, out.shape[2] // width, finish, 0)
+    lax.fori_loop(0, out_chunks, finish, 0)
 
 
 def expert_apply(expert, owns, others, weights, count):
@@ -256,7 +265,7 @@
             pltpu.VMEM((2, rows, width), jnp.float32),
         ]
         + [pltpu.VMEM(w.shape[1:], w.dtype) for w in weights]
-        + [pltpu.SemaphoreType.DMA(((2 * hidden_width + latent_width) // width,))],
+        + [pltpu.SemaphoreType.DMA((hidden_width // width + 2 + latent_width // (2 * width),))],
         compiler_params=pltpu.CompilerParams(vmem_limit_bytes=28 * mebi),
         cost_estimate=pl.CostEstimate(
             flops=3 * rows * latent_width * hidden_width // 2,
@@ -413,30 +422,37 @@
             swapped = from_core[i * token_count : (i + 1) * token_count]
             sums[place_of] = out[i].astype(jnp.float32) + swapped.astype(jnp.float32)
 
-    run([(0, 0)], (near, 1), (far, 0), (travel, "up"))
+    special = [(0, 0), (last - 1, 0), (last - 1, 1), (last, 0)]
+
+    def homeward(*previous):
+        return [send(p, sums[p], 2 * p[0] + p[1]) for p in previous if p not in special]
+
+    run([(0, 0)], *[(near, k) for k in near if k], (travel, "up"))
     sides = [[i, i + 1] for i in range(0, lax.axis_size("rep"), 2)]
     both_sides = lax.all_gather(travel.pop("up"), "rep", axis=0, axis_index_groups=sides)
-    run([(1, 0), (0, 1)], *[(near, k) for k in near if k > 1], start_far(1))
-    for k in range(2, steps):
-        coming = [start_far(k)]
-        for j in range(3, steps):
-            if j not in near and j ^ (j & -j) == k:
-                coming.append(start_near(j))
-        previous = [(k - 2, 1)] if k == last else [(k - 2, 1), (k - 1, 0)]
-        coming += [send(p, sums[p], 2 * p[0] + p[1]) for p in previous]
-        run([(k, 0), (k - 1, 1)], *coming)
+    previous = [(2, 0), (1, 0)]
+    run(previous, *[start_near(3)] * (last >= 3), start_far(2))
+    for k in range(3, steps):
+        coming = homeward(*previous) + [start_far(k)] + [(far, 0)] * (k == last)
+        if k + 1 < steps and k + 1 not in near:
+            coming.append(start_near(k + 1))
+        previous = [(k, 0), (k - 1, 1)]
+        run(previous, *coming)
     run(
-        [(last, 1)],
+        [(last, 1), (0, 1)],
         send((last - 1, 1), sums[last - 1, 1], 1),
         send((last, 0), sums[last, 0], 2),
+        start_far(1),
     )
-    send((last, 1), sums[last, 1], 3)
+    run([(1, 1)], send((last, 1), sums[last, 1], 3), *homeward((0, 1)))
     shared = sums[last - 1, 0]
     for name in ((last - 1, 1), (last, 0), (last, 1)):
         shared += travel.pop(name).astype(jnp.float32)
     shared = shared.astype(jnp.bfloat16)
-    both_sides = after(both_sides, shared)
     send("shared", shared, 2 * last - 2)
+    sums[1, 1] = sums[1, 1].astype(jnp.bfloat16)
+    both_sides = after(both_sides, sums[1, 1], shared)
+    homeward((1, 1))
     *terms, swapped_sides = join(sums[0, 0], *travel.values(), swap_cores(both_sides))
     both_sides = pltpu.with_memory_space_constraint(both_sides, pltpu.HBM)
     return project(group, terms, both_sides, swapped_sides)

time: 172 us -> 170 us (0.988)
  Pallas kernels: 50.6 us -> 48.6 us
    ppermute x21, waiting for transfers between devices: 45.6 us -> 50.2 us  [swap_ep(): lax.ppermute(array, 'ep', [(i, i ^ mask) for i in range(lax.axis_size('ep...]
    ppermute x21, waiting for transfers between devices: 9.18 us -> 4.92 us  [swap_cores(): return lax.ppermute(array, 'grp', [(0, 1), (1, 0)])]
    pallas_call x5, Pallas kernels: 43.6 us -> 41.6 us  [expert_apply(): pl.pallas_call(functools.partial(expert_kernel, positions, count), out_sh...]
  transfers between devices with their start and end apart: 46 -> 46, of which waited for: 17 -> 16; matrix products, arithmetic and copies ran while one was open for 2% -> 2% of each run, Pallas kernels for 27% -> 26%
where the time goes in v13:
time: 170 us
  waiting for transfers between devices  62.1 us (37%)
  Pallas kernels  48.6 us (29%)
  starting transfers between devices  38.4 us (23%)
  between operations  13.7 us (8%)
  local copies, waits for them, and re-layouts  4.24 us (2%)
  other arithmetic  3 us (2%)
    ppermute x21, waiting for transfers between devices, swap_ep(): lax.ppermute(array, 'ep', [(i, i ^ mask) for i in range(lax.axis_size('ep...  50.2 us
    pallas_call x5, Pallas kernels, expert_apply(): pl.pallas_call(functools.partial(expert_kernel, positions, count), out_sh...  41.6 us
    ppermute x21, starting transfers between devices, swap_ep(): lax.ppermute(array, 'ep', [(i, i ^ mask) for i in range(lax.axis_size('ep...  30.8 us
    ppermute x2, waiting for transfers between devices, swap_reps(): lax.ppermute(array, 'rep', [(i, i ^ 1) for i in range(lax.axis_size('rep'...  6.83 us
    ppermute x21, waiting for transfers between devices, swap_cores(): return lax.ppermute(array, 'grp', [(0, 1), (1, 0)])  4.92 us
    pallas_call x1, Pallas kernels, project(): pl.pallas_call(project_kernel, in_specs=[in_smem] + [in_vmem] * len(terms...  4.7 us
    ppermute x21, starting transfers between devices, swap_cores(): return lax.ppermute(array, 'grp', [(0, 1), (1, 0)])  4.38 us
  transfers between devices with their start and end apart: 46, of which 16 were waited for; matrix products, arithmetic and copies ran while one was open for 2% of the time, Pallas kernels for 26%

profile of v13, /device:TPU:0, one launch (start us, length us, event | category | flops | bytes accessed | tf_op | source)
XLA Modules:
  0.0 169.9 jit_solution(996831727218118000)
XLA Ops:
  6.5 1.2 copy-done
  7.8 0.7 constant_dynamic-slice_fusion
  8.6 1.1 constant_dynamic-slice_fusion.1
  9.6 3.1 %collective-permute-start = (bf16[128,1024]{1,0:T(8,128)(2,1)S(1)}, bf16[128,1024]{1,0:T(8,128)(2,1)S(1)}, u32[]{:S(2)}, u32[]{:S(2)}) collective-permute-start(bf16[128,1024]{1,0:T(8,128)(2,1)S(1)} %get-tuple-element.158.refs_2_), channel_id=1, source_target_pairs={{0,2},{1,3},{2,0},{3,1},{4,6},{5,7},{6,4},{7,5},{8,10},{9,11},{10,... | collective-permute-start | bytes 786440 | tf_op jit(solution)/shard_map/ppermute | solution.py:35
  12.7 1.5 collective-permute-start.4
  14.3 2.6 %collective-permute-start.2 = (bf16[128,1024]{1,0:T(8,128)(2,1)S(1)}, bf16[128,1024]{1,0:T(8,128)(2,1)S(1)}, u32[]{:S(2)}, u32[]{:S(2)}) collective-permute-start(bf16[128,1024]{1,0:T(8,128)(2,1)S(1)} %get-tuple-element.158.refs_2_), channel_id=1, source_target_pairs={{0,4},{1,5},{2,6},{3,7},{4,0},{5,1},{6,2},{7,3},{8,12},{9,13},{10,... | collective-permute-start | bytes 786440 | tf_op jit(solution)/shard_map/ppermute | solution.py:35
  16.9 1.2 copy-done.1
  18.1 0.8 split_columns.1
  19.0 1.6 collective-permute-start.5
  20.5 0.7 fusion.1
  21.2 2.5 %collective-permute-done.refs_6_ = bf16[128,1024]{1,0:T(8,128)(2,1)S(1)} collective-permute-done((bf16[128,1024]{1,0:T(8,128)(2,1)S(1)}, bf16[128,1024]{1,0:T(8,128)(2,1)S(1)}, u32[]{:S(2)}, u32[]{:S(2)}) %collective-permute-start) | collective-permute-done | bytes 262176 | tf_op jit(solution)/shard_map/ppermute | solution.py:35
  23.7 3.8 %collective-permute-start.1 = (bf16[128,1024]{1,0:T(8,128)(2,1)S(1)}, bf16[128,1024]{1,0:T(8,128)(2,1)S(1)}, u32[]{:S(2)}, u32[]{:S(2)}) collective-permute-start(bf16[128,1024]{1,0:T(8,128)(2,1)S(1)} %collective-permute-done.refs_6_), channel_id=1, source_target_pairs={{0,1},{1,0},{2,3},{3,2},{4,5},{5,4},{6,7},{7,6},{8,9},{9,8},{10,11... | collective-permute-start | bytes 786440 | tf_op jit(solution)/shard_map/ppermute | solution.py:35
  27.5 0.7 fusion
  28.2 0.7 select_reduce_fusion.weights
  28.9 4.1 %collective-permute-done.2.refs_10_ = bf16[128,1024]{1,0:T(8,128)(2,1)S(1)} collective-permute-done((bf16[128,1024]{1,0:T(8,128)(2,1)S(1)}, bf16[128,1024]{1,0:T(8,128)(2,1)S(1)}, u32[]{:S(2)}, u32[]{:S(2)}) %collective-permute-start.2) | collective-permute-done | bytes 262176 | tf_op jit(solution)/shard_map/ppermute | solution.py:35
  33.1 0.9 collective-permute-start.3
  34.5 7.3 %collective-permute-done.3.refs_2_ = bf16[128,1024]{1,0:T(8,128)(2,1)S(1)} collective-permute-done((bf16[128,1024]{1,0:T(8,128)(2,1)S(1)}, bf16[128,1024]{1,0:T(8,128)(2,1)S(1)}, u32[]{:S(2)}, u32[]{:S(2)}) %collective-permute-start.3) | collective-permute-done | bytes 262176 | tf_op jit(solution)/shard_map/ppermute | solution.py:35
  41.8 0.7 collective-permute-start.12
  42.5 0.5 collective-permute-start.11
  43.5 10.0 %collective-permute-done.12.refs_3_ = bf16[128,1024]{1,0:T(8,128)(2,1)S(1)} collective-permute-done((bf16[128,1024]{1,0:T(8,128)(2,1)S(1)}, bf16[128,1024]{1,0:T(8,128)(2,1)S(1)}, u32[]{:S(2)}, u32[]{:S(2)}) %collective-permute-start.12) | collective-permute-done | bytes 262176 | tf_op jit(solution)/shard_map/ppermute | solution.py:35
  53.5 1.0 down_project.2.refs_6_
  55.5 1.6 collective-permute-start.15
  57.1 6.8 %collective-permute-done.15.arrived = bf16[128,1024]{1,0:T(8,128)(2,1)S(1)} collective-permute-done((bf16[128,1024]{1,0:T(8,128)(2,1)S(1)}, bf16[128,1024]{1,0:T(8,128)(2,1)S(1)}, u32[]{:S(2)}, u32[]{:S(2)}) %collective-permute-start.15) | collective-permute-done | bytes 262176 | tf_op jit(solution)/shard_map/ppermute | solution.py:31
  64.1 1.4 collective-permute-start.17
  65.6 6.4 %expert.5 = (bf16[128,1024]{1,0:T(8,128)(2,1)S(1)}, bf16[128,1024]{1,0:T(8,128)(2,1)S(1)}) custom-call(s32[1]{0:T(128)} %bitcast.1.where, bf16[144,1024]{1,0:T(8,128)(2,1)S(1)} %finish_latent.1.refs_0_, bf16[144,1024]{1,0:T(8,128)(2,1)S(1)} %collective-permute-done.16.refs_1_, bf16[1,1024,2048]{2,1,0:T(8,128)(2,1)} %refs_2_.3, ...), custom_call_target="tpu_custom_call" | custom-call | flops 805306368 | bytes 1048576 | tf_op jit(solution)/shard_map/expert/pallas_call | solution.py:257
  72.0 8.9 %collective-permute-done.18.refs_0_ = bf16[144,1024]{1,0:T(8,128)(2,1)S(1)} collective-permute-done((bf16[144,1024]{1,0:T(8,128)(2,1)S(1)}, bf16[144,1024]{1,0:T(8,128)(2,1)S(1)}, u32[]{:S(2)}, u32[]{:S(2)}) %collective-permute-start.18) | collective-permute-done | bytes 294944 | tf_op jit(solution)/shard_map/ppermute | solution.py:35
  81.6 1.6 collective-permute-start.23
  83.1 9.5 %expert.6 = (bf16[128,1024]{1,0:T(8,128)(2,1)S(1)}, bf16[128,1024]{1,0:T(8,128)(2,1)S(1)}, bf16[256,1024]{1,0:T(8,128)(2,1)S(1)}) custom-call(s32[1]{0:T(128)} %bitcast.1.where, bf16[144,1024]{1,0:T(8,128)(2,1)S(1)} %collective-permute-done.18.refs_0_, bf16[144,1024]{1,0:T(8,128)(2,1)S(1)} %collective-permute-done.17.refs_1_, ...), custom_call_target="tpu_custom_call" | custom-call | flops 1610612736 | bytes 2097152 | tf_op jit(solution)/shard_map/expert/pallas_call | solution.py:257
  92.8 1.6 collective-permute-start.29
  95.4 2.1 %collective-permute-start.27 = (bf16[128,1024]{1,0:T(8,128)(2,1)S(1)}, bf16[128,1024]{1,0:T(8,128)(2,1)S(1)}, u32[]{:S(2)}, u32[]{:S(2)}) collective-permute-start(bf16[128,1024]{1,0:T(8,128)(2,1)S(1)} %add_convert_fusion.6), channel_id=1, source_target_pairs={{0,2},{1,3},{2,0},{3,1},{4,6},{5,7},{6,4},{7,5},{8,10},{9,11},{10,... | collective-permute-start | bytes 786440 | tf_op jit(solution)/shard_map/ppermute | solution.py:35
  97.5 9.5 %expert.7 = (bf16[128,1024]{1,0:T(8,128)(2,1)S(1)}, bf16[128,1024]{1,0:T(8,128)(2,1)S(1)}, bf16[256,1024]{1,0:T(8,128)(2,1)S(1)}) custom-call(s32[1]{0:T(128)} %bitcast.1.where, bf16[144,1024]{1,0:T(8,128)(2,1)S(1)} %collective-permute-done.22.refs_0_, bf16[144,1024]{1,0:T(8,128)(2,1)S(1)} %collective-permute-done.23.refs_1_, ...), custom_call_target="tpu_custom_call" | custom-call | flops 1610612736 | bytes 2097152 | tf_op jit(solution)/shard_map/expert/pallas_call | solution.py:257
  107.0 1.4 collective-permute-done.28.refs_0_
  108.5 1.5 collective-permute-start.35
  110.7 2.0 %collective-permute-start.34 = (bf16[128,1024]{1,0:T(8,128)(2,1)S(1)}, bf16[128,1024]{1,0:T(8,128)(2,1)S(1)}, u32[]{:S(2)}, u32[]{:S(2)}) collective-permute-start(bf16[128,1024]{1,0:T(8,128)(2,1)S(1)} %get-tuple-element.161), channel_id=1, source_target_pairs={{0,2},{1,3},{2,0},{3,1},{4,6},{5,7},{6,4},{7,5},{8,10},{9,11},{10,... | collective-permute-start | bytes 786440 | tf_op jit(solution)/shard_map/ppermute | solution.py:35
  112.7 0.6 collective-permute-start.33
  113.3 9.7 %expert.8 = (bf16[128,1024]{1,0:T(8,128)(2,1)S(1)}, bf16[128,1024]{1,0:T(8,128)(2,1)S(1)}, bf16[256,1024]{1,0:T(8,128)(2,1)S(1)}) custom-call(s32[1]{0:T(128)} %bitcast.1.where, bf16[144,1024]{1,0:T(8,128)(2,1)S(1)} %collective-permute-done.28.refs_0_, bf16[144,1024]{1,0:T(8,128)(2,1)S(1)} %collective-permute-done.29.refs_1_, ...), custom_call_target="tpu_custom_call" | custom-call | flops 1610612736 | bytes 2097152 | tf_op jit(solution)/shard_map/expert/pallas_call | solution.py:257
  124.0 1.4 collective-permute-done.37
  125.6 1.5 collective-permute-start.39
  127.2 2.0 %collective-permute-start.38 = (bf16[128,1024]{1,0:T(8,128)(2,1)S(1)}, bf16[128,1024]{1,0:T(8,128)(2,1)S(1)}, u32[]{:S(2)}, u32[]{:S(2)}) collective-permute-start(bf16[128,1024]{1,0:T(8,128)(2,1)S(1)} %get-tuple-element.160), channel_id=1, source_target_pairs={{0,3},{1,2},{2,1},{3,0},{4,7},{5,6},{6,5},{7,4},{8,11},{9,10},{10,... | collective-permute-start | bytes 786440 | tf_op jit(solution)/shard_map/ppermute | solution.py:35
  129.2 6.4 %expert.9 = (bf16[128,1024]{1,0:T(8,128)(2,1)S(1)}, bf16[128,1024]{1,0:T(8,128)(2,1)S(1)}) custom-call(s32[1]{0:T(128)} %bitcast.1.where, bf16[144,1024]{1,0:T(8,128)(2,1)S(1)} %collective-permute-done.35.refs_0_, bf16[144,1024]{1,0:T(8,128)(2,1)S(1)} %collective-permute-done.36.refs_1_, bf16[1,1024,2048]{2,1,0:T(8,128)(2,1)} %refs_2_.3, ...), custom_call_target="tpu_custom_call" | custom-call | flops 805306368 | bytes 1048576 | tf_op jit(solution)/shard_map/expert/pallas_call | solution.py:257
  135.6 4.1 %collective-permute-done.39.refs_2_ = bf16[128,1024]{1,0:T(8,128)(2,1)S(1)} collective-permute-done((bf16[128,1024]{1,0:T(8,128)(2,1)S(1)}, bf16[128,1024]{1,0:T(8,128)(2,1)S(1)}, u32[]{:S(2)}, u32[]{:S(2)}) %collective-permute-start.39) | collective-permute-done | bytes 262176 | tf_op jit(solution)/shard_map/ppermute | solution.py:35
  139.9 1.3 collective-permute-done.41
  141.9 2.4 %collective-permute-start.40 = (bf16[128,1024]{1,0:T(8,128)(2,1)S(1)}, bf16[128,1024]{1,0:T(8,128)(2,1)S(1)}, u32[]{:S(2)}, u32[]{:S(2)}) collective-permute-start(bf16[128,1024]{1,0:T(8,128)(2,1)S(1)} %add_convert_fusion.1), channel_id=1, source_target_pairs={{0,4},{1,5},{2,6},{3,7},{4,0},{5,1},{6,2},{7,3},{8,12},{9,13},{10,... | collective-permute-start | bytes 786440 | tf_op jit(solution)/shard_map/ppermute | solution.py:35
  144.3 0.9 collective-permute-start.42
  145.2 1.6 collective-permute-done.19
  146.9 10.0 %collective-permute-done.40.refs_3_ = bf16[128,1024]{1,0:T(8,128)(2,1)S(1)} collective-permute-done((bf16[128,1024]{1,0:T(8,128)(2,1)S(1)}, bf16[128,1024]{1,0:T(8,128)(2,1)S(1)}, u32[]{:S(2)}, u32[]{:S(2)}) %collective-permute-start.40) | collective-permute-done | bytes 262176 | tf_op jit(solution)/shard_map/ppermute | solution.py:35
  156.9 1.5 collective-permute-done.42.refs_4_
  158.3 4.7 %project.1 = bf16[128,4096]{1,0:T(8,128)(2,1)} custom-call(s32[1]{0:T(128)} %bitcast.where, f32[128,1024]{1,0:T(8,128)S(1)} %convert_add_fusion.refs_0_, bf16[128,1024]{1,0:T(8,128)(2,1)S(1)} %collective-permute-done.27.refs_1_, bf16[128,1024]{1,0:T(8,128)(2,1)S(1)} %collective-permute-done.39.refs_2_, ...), custom_call_target="tpu_custom_call" | custom-call | flops 1073741824 | bytes 8388608 | tf_op jit(solution)/shard_map/project/pallas_call | solution.py:319
  (72 shorter events, 7.0 us)
Async XLA Ops:
  6.5 1.2 copy-start
  6.5 74.4 %all-gather.5.cloned.1.call-start = ((), (), s32[]{:S(2)}) async-start(), calls=%async_computation | async-start | bytes 2359296 | tf_op jit(solution)/shard_map/all_gather | solution.py:369
  8.5 132.8 %all-gather.7.cloned.1.call-start = ((), (), s32[]{:S(2)}) async-start(), calls=%async_computation.1 | async-start | bytes 6291456 | tf_op jit(solution)/shard_map/all_gather | solution.py:432
  9.6 14.1 %collective-permute-start = (bf16[128,1024]{1,0:T(8,128)(2,1)S(1)}, bf16[128,1024]{1,0:T(8,128)(2,1)S(1)}, u32[]{:S(2)}, u32[]{:S(2)}) collective-permute-start(bf16[128,1024]{1,0:T(8,128)(2,1)S(1)} %get-tuple-element.158.refs_2_), channel_id=1, source_target_pairs={{0,2},{1,3},{2,0},{3,1},{4,6},{5,7},{6,4},{7,5},{8,10},{9,11},{10,... | collective-permute-start | bytes 786440 | tf_op jit(solution)/shard_map/ppermute | solution.py:35
  12.7 21.3 %collective-permute-start.4 = (bf16[128,1024]{1,0:T(8,128)(2,1)S(1)}, bf16[128,1024]{1,0:T(8,128)(2,1)S(1)}, u32[]{:S(2)}, u32[]{:S(2)}) collective-permute-start(bf16[128,1024]{1,0:T(8,128)(2,1)S(1)} %get-tuple-element.158.refs_2_), channel_id=1, source_target_pairs={{0,1},{1,0},{2,3},{3,2},{4,5},{5,4},{6,7},{7,6},{8,9},{9,8},{10,11... | collective-permute-start | bytes 786440 | tf_op jit(solution)/shard_map/ppermute | solution.py:35
  14.3 18.8 %collective-permute-start.2 = (bf16[128,1024]{1,0:T(8,128)(2,1)S(1)}, bf16[128,1024]{1,0:T(8,128)(2,1)S(1)}, u32[]{:S(2)}, u32[]{:S(2)}) collective-permute-start(bf16[128,1024]{1,0:T(8,128)(2,1)S(1)} %get-tuple-element.158.refs_2_), channel_id=1, source_target_pairs={{0,4},{1,5},{2,6},{3,7},{4,0},{5,1},{6,2},{7,3},{8,12},{9,13},{10,... | collective-permute-start | bytes 786440 | tf_op jit(solution)/shard_map/ppermute | solution.py:35
  16.9 1.2 copy-start.1
  19.0 15.5 %collective-permute-start.5 = (bf16[128,2048]{1,0:T(8,128)(2,1)S(1)}, bf16[128,2048]{1,0:T(8,128)(2,1)S(1)}, u32[]{:S(2)}, u32[]{:S(2)}) collective-permute-start(bf16[128,2048]{1,0:T(8,128)(2,1)S(1)} %get-tuple-element.86), channel_id=1, source_target_pairs={{0,16},{16,0},{1,17},{17,1},{2,18},{18,2},{3,19},{19,3},{4,20},{20... | collective-permute-start | bytes 1572872 | tf_op jit(solution)/shard_map/ppermute | solution.py:31
  23.7 9.3 %collective-permute-start.1 = (bf16[128,1024]{1,0:T(8,128)(2,1)S(1)}, bf16[128,1024]{1,0:T(8,128)(2,1)S(1)}, u32[]{:S(2)}, u32[]{:S(2)}) collective-permute-start(bf16[128,1024]{1,0:T(8,128)(2,1)S(1)} %collective-permute-done.refs_6_), channel_id=1, source_target_pairs={{0,1},{1,0},{2,3},{3,2},{4,5},{5,4},{6,7},{7,6},{8,9},{9,8},{10,11... | collective-permute-start | bytes 786440 | tf_op jit(solution)/shard_map/ppermute | solution.py:35
  33.1 8.8 %collective-permute-start.3 = (bf16[128,1024]{1,0:T(8,128)(2,1)S(1)}, bf16[128,1024]{1,0:T(8,128)(2,1)S(1)}, u32[]{:S(2)}, u32[]{:S(2)}) collective-permute-start(bf16[128,1024]{1,0:T(8,128)(2,1)S(1)} %collective-permute-done.2.refs_10_), channel_id=1, source_target_pairs={{0,2},{1,3},{2,0},{3,1},{4,6},{5,7},{6,4},{7,5},{8,10},{9,11},{10,... | collective-permute-start | bytes 786440 | tf_op jit(solution)/shard_map/ppermute | solution.py:35
  34.0 8.5 %collective-permute-start.9 = (bf16[128,1024]{1,0:T(8,128)(2,1)S(1)}, bf16[128,1024]{1,0:T(8,128)(2,1)S(1)}, u32[]{:S(2)}, u32[]{:S(2)}) collective-permute-start(bf16[128,1024]{1,0:T(8,128)(2,1)S(1)} %collective-permute-done.2.refs_10_), channel_id=1, source_target_pairs={{0,1},{1,0},{2,3},{3,2},{4,5},{5,4},{6,7},{7,6},{8,9},{9,8},{10,11... | collective-permute-start | bytes 786440 | tf_op jit(solution)/shard_map/ppermute | solution.py:35
  34.0 9.0 %collective-permute-start.7 = (bf16[128,1024]{1,0:T(8,128)(2,1)S(1)}, bf16[128,1024]{1,0:T(8,128)(2,1)S(1)}, u32[]{:S(2)}, u32[]{:S(2)}) collective-permute-start(bf16[128,1024]{1,0:T(8,128)(2,1)S(1)} %collective-permute-done.refs_6_), channel_id=1, source_target_pairs={{0,8},{8,0},{1,9},{9,1},{2,10},{10,2},{3,11},{11,3},{4,12},{12,4},... | collective-permute-start | bytes 786440 | tf_op jit(solution)/shard_map/ppermute | solution.py:27
  34.0 9.1 %collective-permute-start.8 = (bf16[128,1024]{1,0:T(8,128)(2,1)S(1)}, bf16[128,1024]{1,0:T(8,128)(2,1)S(1)}, u32[]{:S(2)}, u32[]{:S(2)}) collective-permute-start(bf16[128,1024]{1,0:T(8,128)(2,1)S(1)} %collective-permute-done.1.refs_7_), channel_id=1, source_target_pairs={{0,8},{8,0},{1,9},{9,1},{2,10},{10,2},{3,11},{11,3},{4,12},{12,4},... | collective-permute-start | bytes 786440 | tf_op jit(solution)/shard_map/ppermute | solution.py:27
  41.8 11.7 %collective-permute-start.12 = (bf16[128,1024]{1,0:T(8,128)(2,1)S(1)}, bf16[128,1024]{1,0:T(8,128)(2,1)S(1)}, u32[]{:S(2)}, u32[]{:S(2)}) collective-permute-start(bf16[128,1024]{1,0:T(8,128)(2,1)S(1)} %collective-permute-done.3.refs_2_), channel_id=1, source_target_pairs={{0,1},{1,0},{2,3},{3,2},{4,5},{5,4},{6,7},{7,6},{8,9},{9,8},{10,11... | collective-permute-start | bytes 786440 | tf_op jit(solution)/shard_map/ppermute | solution.py:35
  42.5 11.0 %collective-permute-start.10 = (bf16[128,1024]{1,0:T(8,128)(2,1)S(1)}, bf16[128,1024]{1,0:T(8,128)(2,1)S(1)}, u32[]{:S(2)}, u32[]{:S(2)}) collective-permute-start(bf16[128,1024]{1,0:T(8,128)(2,1)S(1)} %collective-permute-done.2.refs_10_), channel_id=1, source_target_pairs={{0,8},{8,0},{1,9},{9,1},{2,10},{10,2},{3,11},{11,3},{4,12},{12,4},... | collective-permute-start | bytes 786440 | tf_op jit(solution)/shard_map/ppermute | solution.py:27
  42.5 11.0 %collective-permute-start.11 = (bf16[128,1024]{1,0:T(8,128)(2,1)S(1)}, bf16[128,1024]{1,0:T(8,128)(2,1)S(1)}, u32[]{:S(2)}, u32[]{:S(2)}) collective-permute-start(bf16[128,1024]{1,0:T(8,128)(2,1)S(1)} %collective-permute-done.9.refs_11_), channel_id=1, source_target_pairs={{0,8},{8,0},{1,9},{9,1},{2,10},{10,2},{3,11},{11,3},{4,12},{12,4},... | collective-permute-start | bytes 786440 | tf_op jit(solution)/shard_map/ppermute | solution.py:27
  43.0 10.5 %collective-permute-start.6 = (bf16[128,1024]{1,0:T(8,128)(2,1)S(1)}, bf16[128,1024]{1,0:T(8,128)(2,1)S(1)}, u32[]{:S(2)}, u32[]{:S(2)}) collective-permute-start(bf16[128,1024]{1,0:T(8,128)(2,1)S(1)} %collective-permute-done.4.refs_3_), channel_id=1, source_target_pairs={{0,8},{8,0},{1,9},{9,1},{2,10},{10,2},{3,11},{11,3},{4,12},{12,4},... | collective-permute-start | bytes 786440 | tf_op jit(solution)/shard_map/ppermute | solution.py:27
  43.1 11.4 %collective-permute-start.13 = (bf16[128,1024]{1,0:T(8,128)(2,1)S(1)}, bf16[128,1024]{1,0:T(8,128)(2,1)S(1)}, u32[]{:S(2)}, u32[]{:S(2)}) collective-permute-start(bf16[128,1024]{1,0:T(8,128)(2,1)S(1)} %collective-permute-done.3.refs_2_), channel_id=1, source_target_pairs={{0,8},{8,0},{1,9},{9,1},{2,10},{10,2},{3,11},{11,3},{4,12},{12,4},... | collective-permute-start | bytes 786440 | tf_op jit(solution)/shard_map/ppermute | solution.py:27
  53.5 1.5 collective-permute-start.14
  55.5 8.4 %collective-permute-start.15 = (bf16[128,1024]{1,0:T(8,128)(2,1)S(1)}, bf16[128,1024]{1,0:T(8,128)(2,1)S(1)}, u32[]{:S(2)}, u32[]{:S(2)}) collective-permute-start(bf16[128,1024]{1,0:T(8,128)(2,1)S(1)} %get-tuple-element.93), channel_id=1, source_target_pairs={{0,16},{16,0},{1,17},{17,1},{2,18},{18,2},{3,19},{19,3},{4,20},{20... | collective-permute-start | bytes 786440 | tf_op jit(solution)/shard_map/ppermute | solution.py:31
  64.0 1.6 collective-permute-start.16
  64.0 16.9 %collective-permute-start.18 = (bf16[144,1024]{1,0:T(8,128)(2,1)S(1)}, bf16[144,1024]{1,0:T(8,128)(2,1)S(1)}, u32[]{:S(2)}, u32[]{:S(2)}) collective-permute-start(bf16[144,1024]{1,0:T(8,128)(2,1)S(1)} %finish_latent.1.refs_0_), channel_id=1, source_target_pairs={{0,4},{1,5},{2,6},{3,7},{4,0},{5,1},{6,2},{7,3},{8,12},{9,13},{10,... | collective-permute-start | bytes 884744 | tf_op jit(solution)/shard_map/ppermute | solution.py:35
  64.1 16.8 %collective-permute-start.17 = (bf16[144,1024]{1,0:T(8,128)(2,1)S(1)}, bf16[144,1024]{1,0:T(8,128)(2,1)S(1)}, u32[]{:S(2)}, u32[]{:S(2)}) collective-permute-start(bf16[144,1024]{1,0:T(8,128)(2,1)S(1)} %finish_latent.1.refs_0_), channel_id=1, source_target_pairs={{0,2},{1,3},{2,0},{3,1},{4,6},{5,7},{6,4},{7,5},{8,10},{9,11},{10,... | collective-permute-start | bytes 884744 | tf_op jit(solution)/shard_map/ppermute | solution.py:35
  81.0 2.2 %collective-permute-start.21 = (bf16[144,1024]{1,0:T(8,128)(2,1)S(1)}, bf16[144,1024]{1,0:T(8,128)(2,1)S(1)}, u32[]{:S(2)}, u32[]{:S(2)}) collective-permute-start(bf16[144,1024]{1,0:T(8,128)(2,1)S(1)} %collective-permute-done.17.refs_1_), channel_id=1, source_target_pairs={{0,8},{8,0},{1,9},{9,1},{2,10},{10,2},{3,11},{11,3},{4,12},{12,4},... | collective-permute-start | bytes 884744 | tf_op jit(solution)/shard_map/ppermute | solution.py:27
  81.1 2.1 %collective-permute-start.20 = (bf16[144,1024]{1,0:T(8,128)(2,1)S(1)}, bf16[144,1024]{1,0:T(8,128)(2,1)S(1)}, u32[]{:S(2)}, u32[]{:S(2)}) collective-permute-start(bf16[144,1024]{1,0:T(8,128)(2,1)S(1)} %collective-permute-done.18.refs_0_), channel_id=1, source_target_pairs={{0,8},{8,0},{1,9},{9,1},{2,10},{10,2},{3,11},{11,3},{4,12},{12,4},... | collective-permute-start | bytes 884744 | tf_op jit(solution)/shard_map/ppermute | solution.py:27
  81.6 11.1 %collective-permute-start.23 = (bf16[144,1024]{1,0:T(8,128)(2,1)S(1)}, bf16[144,1024]{1,0:T(8,128)(2,1)S(1)}, u32[]{:S(2)}, u32[]{:S(2)}) collective-permute-start(bf16[144,1024]{1,0:T(8,128)(2,1)S(1)} %collective-permute-done.18.refs_0_), channel_id=1, source_target_pairs={{0,1},{1,0},{2,3},{3,2},{4,5},{5,4},{6,7},{7,6},{8,9},{9,8},{10,11... | collective-permute-start | bytes 884744 | tf_op jit(solution)/shard_map/ppermute | solution.py:35
  83.1 9.5 %collective-permute-start.22 = (bf16[144,1024]{1,0:T(8,128)(2,1)S(1)}, bf16[144,1024]{1,0:T(8,128)(2,1)S(1)}, u32[]{:S(2)}, u32[]{:S(2)}) collective-permute-start(bf16[144,1024]{1,0:T(8,128)(2,1)S(1)} %collective-permute-done.18.refs_0_), channel_id=1, source_target_pairs={{0,2},{1,3},{2,0},{3,1},{4,6},{5,7},{6,4},{7,5},{8,10},{9,11},{10,... | collective-permute-start | bytes 884744 | tf_op jit(solution)/shard_map/ppermute | solution.py:35
  92.7 2.7 %collective-permute-start.26 = (bf16[256,1024]{1,0:T(8,128)(2,1)S(1)}, bf16[256,1024]{1,0:T(8,128)(2,1)S(1)}, u32[]{:S(2)}, u32[]{:S(2)}) collective-permute-start(bf16[256,1024]{1,0:T(8,128)(2,1)S(1)} %get-tuple-element.120), channel_id=1, source_target_pairs={{0,8},{8,0},{1,9},{9,1},{2,10},{10,2},{3,11},{11,3},{4,12},{12,4},... | collective-permute-start | bytes 1572872 | tf_op jit(solution)/shard_map/ppermute | solution.py:27
  92.8 14.3 %collective-permute-start.29 = (bf16[144,1024]{1,0:T(8,128)(2,1)S(1)}, bf16[144,1024]{1,0:T(8,128)(2,1)S(1)}, u32[]{:S(2)}, u32[]{:S(2)}) collective-permute-start(bf16[144,1024]{1,0:T(8,128)(2,1)S(1)} %finish_latent.1.refs_0_), channel_id=1, source_target_pairs={{0,1},{1,0},{2,3},{3,2},{4,5},{5,4},{6,7},{7,6},{8,9},{9,8},{10,11... | collective-permute-start | bytes 884744 | tf_op jit(solution)/shard_map/ppermute | solution.py:35
  94.4 14.1 %collective-permute-start.28 = (bf16[144,1024]{1,0:T(8,128)(2,1)S(1)}, bf16[144,1024]{1,0:T(8,128)(2,1)S(1)}, u32[]{:S(2)}, u32[]{:S(2)}) collective-permute-start(bf16[144,1024]{1,0:T(8,128)(2,1)S(1)} %collective-permute-done.22.refs_0_), channel_id=1, source_target_pairs={{0,1},{1,0},{2,3},{3,2},{4,5},{5,4},{6,7},{7,6},{8,9},{9,8},{10,11... | collective-permute-start | bytes 884744 | tf_op jit(solution)/shard_map/ppermute | solution.py:35
  94.8 2.7 %collective-permute-start.24 = (bf16[144,1024]{1,0:T(8,128)(2,1)S(1)}, bf16[144,1024]{1,0:T(8,128)(2,1)S(1)}, u32[]{:S(2)}, u32[]{:S(2)}) collective-permute-start(bf16[144,1024]{1,0:T(8,128)(2,1)S(1)} %collective-permute-done.22.refs_0_), channel_id=1, source_target_pairs={{0,8},{8,0},{1,9},{9,1},{2,10},{10,2},{3,11},{11,3},{4,12},{12,4},... | collective-permute-start | bytes 884744 | tf_op jit(solution)/shard_map/ppermute | solution.py:27
  94.8 2.7 %collective-permute-start.25 = (bf16[144,1024]{1,0:T(8,128)(2,1)S(1)}, bf16[144,1024]{1,0:T(8,128)(2,1)S(1)}, u32[]{:S(2)}, u32[]{:S(2)}) collective-permute-start(bf16[144,1024]{1,0:T(8,128)(2,1)S(1)} %collective-permute-done.23.refs_1_), channel_id=1, source_target_pairs={{0,8},{8,0},{1,9},{9,1},{2,10},{10,2},{3,11},{11,3},{4,12},{12,4},... | collective-permute-start | bytes 884744 | tf_op jit(solution)/shard_map/ppermute | solution.py:27
  95.4 13.1 %collective-permute-start.27 = (bf16[128,1024]{1,0:T(8,128)(2,1)S(1)}, bf16[128,1024]{1,0:T(8,128)(2,1)S(1)}, u32[]{:S(2)}, u32[]{:S(2)}) collective-permute-start(bf16[128,1024]{1,0:T(8,128)(2,1)S(1)} %add_convert_fusion.6), channel_id=1, source_target_pairs={{0,2},{1,3},{2,0},{3,1},{4,6},{5,7},{6,4},{7,5},{8,10},{9,11},{10,... | collective-permute-start | bytes 786440 | tf_op jit(solution)/shard_map/ppermute | solution.py:35
  108.5 2.0 %collective-permute-start.32 = (bf16[256,1024]{1,0:T(8,128)(2,1)S(1)}, bf16[256,1024]{1,0:T(8,128)(2,1)S(1)}, u32[]{:S(2)}, u32[]{:S(2)}) collective-permute-start(bf16[256,1024]{1,0:T(8,128)(2,1)S(1)} %get-tuple-element.132), channel_id=1, source_target_pairs={{0,8},{8,0},{1,9},{9,1},{2,10},{10,2},{3,11},{11,3},{4,12},{12,4},... | collective-permute-start | bytes 1572872 | tf_op jit(solution)/shard_map/ppermute | solution.py:27
  108.5 14.6 %collective-permute-start.35 = (bf16[144,1024]{1,0:T(8,128)(2,1)S(1)}, bf16[144,1024]{1,0:T(8,128)(2,1)S(1)}, u32[]{:S(2)}, u32[]{:S(2)}) collective-permute-start(bf16[144,1024]{1,0:T(8,128)(2,1)S(1)} %collective-permute-done.17.refs_1_), channel_id=1, source_target_pairs={{0,1},{1,0},{2,3},{3,2},{4,5},{5,4},{6,7},{7,6},{8,9},{9,8},{10,11... | collective-permute-start | bytes 884744 | tf_op jit(solution)/shard_map/ppermute | solution.py:35
  110.0 3.4 %collective-permute-start.30 = (bf16[144,1024]{1,0:T(8,128)(2,1)S(1)}, bf16[144,1024]{1,0:T(8,128)(2,1)S(1)}, u32[]{:S(2)}, u32[]{:S(2)}) collective-permute-start(bf16[144,1024]{1,0:T(8,128)(2,1)S(1)} %collective-permute-done.28.refs_0_), channel_id=1, source_target_pairs={{0,8},{8,0},{1,9},{9,1},{2,10},{10,2},{3,11},{11,3},{4,12},{12,4},... | collective-permute-start | bytes 884744 | tf_op jit(solution)/shard_map/ppermute | solution.py:27
  110.2 3.1 %collective-permute-start.31 = (bf16[144,1024]{1,0:T(8,128)(2,1)S(1)}, bf16[144,1024]{1,0:T(8,128)(2,1)S(1)}, u32[]{:S(2)}, u32[]{:S(2)}) collective-permute-start(bf16[144,1024]{1,0:T(8,128)(2,1)S(1)} %collective-permute-done.29.refs_1_), channel_id=1, source_target_pairs={{0,8},{8,0},{1,9},{9,1},{2,10},{10,2},{3,11},{11,3},{4,12},{12,4},... | collective-permute-start | bytes 884744 | tf_op jit(solution)/shard_map/ppermute | solution.py:27
  110.7 12.4 %collective-permute-start.34 = (bf16[128,1024]{1,0:T(8,128)(2,1)S(1)}, bf16[128,1024]{1,0:T(8,128)(2,1)S(1)}, u32[]{:S(2)}, u32[]{:S(2)}) collective-permute-start(bf16[128,1024]{1,0:T(8,128)(2,1)S(1)} %get-tuple-element.161), channel_id=1, source_target_pairs={{0,2},{1,3},{2,0},{3,1},{4,6},{5,7},{6,4},{7,5},{8,10},{9,11},{10,... | collective-permute-start | bytes 786440 | tf_op jit(solution)/shard_map/ppermute | solution.py:35
  112.7 10.8 %collective-permute-start.33 = (bf16[128,1024]{1,0:T(8,128)(2,1)S(1)}, bf16[128,1024]{1,0:T(8,128)(2,1)S(1)}, u32[]{:S(2)}, u32[]{:S(2)}) collective-permute-start(bf16[128,1024]{1,0:T(8,128)(2,1)S(1)} %get-tuple-element.162), channel_id=1, source_target_pairs={{0,1},{1,0},{2,3},{3,2},{4,5},{5,4},{6,7},{7,6},{8,9},{9,8},{10,11... | collective-permute-start | bytes 786440 | tf_op jit(solution)/shard_map/ppermute | solution.py:35
  123.5 1.9 %collective-permute-start.37 = (bf16[256,1024]{1,0:T(8,128)(2,1)S(1)}, bf16[256,1024]{1,0:T(8,128)(2,1)S(1)}, u32[]{:S(2)}, u32[]{:S(2)}) collective-permute-start(bf16[256,1024]{1,0:T(8,128)(2,1)S(1)} %get-tuple-element.140), channel_id=1, source_target_pairs={{0,8},{8,0},{1,9},{9,1},{2,10},{10,2},{3,11},{11,3},{4,12},{12,4},... | collective-permute-start | bytes 1572872 | tf_op jit(solution)/shard_map/ppermute | solution.py:27
  123.5 5.7 %collective-permute-start.36 = (bf16[144,1024]{1,0:T(8,128)(2,1)S(1)}, bf16[144,1024]{1,0:T(8,128)(2,1)S(1)}, u32[]{:S(2)}, u32[]{:S(2)}) collective-permute-start(bf16[144,1024]{1,0:T(8,128)(2,1)S(1)} %collective-permute-done.35.refs_0_), channel_id=1, source_target_pairs={{0,8},{8,0},{1,9},{9,1},{2,10},{10,2},{3,11},{11,3},{4,12},{12,4},... | collective-permute-start | bytes 884744 | tf_op jit(solution)/shard_map/ppermute | solution.py:27
  125.6 14.0 %collective-permute-start.39 = (bf16[128,1024]{1,0:T(8,128)(2,1)S(1)}, bf16[128,1024]{1,0:T(8,128)(2,1)S(1)}, u32[]{:S(2)}, u32[]{:S(2)}) collective-permute-start(bf16[128,1024]{1,0:T(8,128)(2,1)S(1)} %get-tuple-element.159), channel_id=1, source_target_pairs={{0,1},{1,0},{2,3},{3,2},{4,5},{5,4},{6,7},{7,6},{8,9},{9,8},{10,11... | collective-permute-start | bytes 786440 | tf_op jit(solution)/shard_map/ppermute | solution.py:35
  127.2 12.5 %collective-permute-start.38 = (bf16[128,1024]{1,0:T(8,128)(2,1)S(1)}, bf16[128,1024]{1,0:T(8,128)(2,1)S(1)}, u32[]{:S(2)}, u32[]{:S(2)}) collective-permute-start(bf16[128,1024]{1,0:T(8,128)(2,1)S(1)} %get-tuple-element.160), channel_id=1, source_target_pairs={{0,3},{1,2},{2,1},{3,0},{4,7},{5,6},{6,5},{7,4},{8,11},{9,10},{10,... | collective-permute-start | bytes 786440 | tf_op jit(solution)/shard_map/ppermute | solution.py:35
  139.7 1.5 collective-permute-start.41
  141.3 17.0 %collective-permute-start.43 = (bf16[2,8,256,512]{3,2,1,0:T(8,128)(2,1)}, bf16[2,8,256,512]{3,2,1,0:T(8,128)(2,1)S(1)}, u32[]{:S(2)}, u32[]{:S(2)}) collective-permute-start(bf16[2,8,256,512]{3,2,1,0:T(8,128)(2,1)} %bitcast.6), channel_id=1, source_target_pairs={{0,8},{8,0},{1,9},{9,1},{2,10},{10,2},{3,11},{11,3},{4,12},{12,4},... | collective-permute-start | bytes 12582920 | tf_op jit(solution)/shard_map/ppermute | solution.py:27
  141.5 5.3 %collective-permute-start.19 = (bf16[128,1024]{1,0:T(8,128)(2,1)S(1)}, bf16[128,1024]{1,0:T(8,128)(2,1)S(1)}, u32[]{:S(2)}, u32[]{:S(2)}) collective-permute-start(bf16[128,1024]{1,0:T(8,128)(2,1)S(1)} %get-tuple-element.100), channel_id=1, source_target_pairs={{0,8},{8,0},{1,9},{9,1},{2,10},{10,2},{3,11},{11,3},{4,12},{12,4},... | collective-permute-start | bytes 786440 | tf_op jit(solution)/shard_map/ppermute | solution.py:27
  141.9 15.0 %collective-permute-start.40 = (bf16[128,1024]{1,0:T(8,128)(2,1)S(1)}, bf16[128,1024]{1,0:T(8,128)(2,1)S(1)}, u32[]{:S(2)}, u32[]{:S(2)}) collective-permute-start(bf16[128,1024]{1,0:T(8,128)(2,1)S(1)} %add_convert_fusion.1), channel_id=1, source_target_pairs={{0,4},{1,5},{2,6},{3,7},{4,0},{5,1},{6,2},{7,3},{8,12},{9,13},{10,... | collective-permute-start | bytes 786440 | tf_op jit(solution)/shard_map/ppermute | solution.py:35
  144.3 14.0 %collective-permute-start.42 = (bf16[128,1024]{1,0:T(8,128)(2,1)S(1)}, bf16[128,1024]{1,0:T(8,128)(2,1)S(1)}, u32[]{:S(2)}, u32[]{:S(2)}) collective-permute-start(bf16[128,1024]{1,0:T(8,128)(2,1)S(1)} %add_convert_fusion), channel_id=1, source_target_pairs={{0,3},{1,2},{2,1},{3,0},{4,7},{5,6},{6,5},{7,4},{8,11},{9,10},{10,... | collective-permute-start | bytes 786440 | tf_op jit(solution)/shard_map/ppermute | solution.py:35
Sparse Core Ops, SparseCore 0:
  9.5 60.4 all-gather.4
  81.1 56.2 all-gather.6

commit v14 on v13

--- a/solution.py
+++ b/solution.py
@@ -46,6 +46,38 @@
     )
     named = expert_ids[None, :, :] == jnp.arange(expert_count, dtype=jnp.int32)[:, None, None]
     return jnp.sum(jnp.where(named, weights.astype(jnp.float32)[None, :, :], 0.0), axis=2)
+
+
+def cut_kernel(where, down, up, own, other, up_piece, sems):
+    pairs = []
+    for core, piece, shard in ((0, own, down), (1, other, down), (0, up_piece, up)):
+        rows = piece.shape[0]
+        start = pl.multiple_of((where[0] ^ core) * rows, rows)
+        pairs.append((shard.at[pl.ds(start, rows)], piece))
+    copies = [pltpu.make_async_copy(*pair, sems.at[i]) for i, pair in enumerate(pairs)]
+    for copy in copies:
+        copy.start()
+    for copy in copies:
+        copy.wait()
+
+
+def cut_quarters(quarter, down, up):
+    shapes = [
+        jax.ShapeDtypeStruct((array.shape[0] // 4, array.shape[1]), array.dtype)
+        for array in (down, down, up)
+    ]
+    return pl.pallas_call(
+        cut_kernel,
+        out_shape=shapes,
+        in_specs=[in_smem] + [in_hbm] * 2,
+        out_specs=[anywhere] * 3,
+        scratch_shapes=[pltpu.SemaphoreType.DMA((3,))],
+        compiler_params=pltpu.CompilerParams(vmem_limit_bytes=mebi),
+        name="cut_quarters",
+    )(
+        quarter.reshape(1).astype(jnp.int32),
+        *[pltpu.with_memory_space_constraint(array, pltpu.HBM) for array in (down, up)],
+    )
 
 
 def columns_kernel(ep_count, quarter, where, tokens, kept, given):
@@ -354,18 +386,14 @@
 
     quarter = down_latent.shape[0] // 4
 
-    def own_piece(core):
-        return lax.dynamic_slice_in_dim(down_latent, (2 * side + core) * quarter, quarter, 0)
-
+    own_piece, other_piece, up_piece = cut_quarters(own_quarter, down_latent, up_latent)
     kept, given = split_columns(tokens, ep_count, quarter, place, side, group)
     taken = swap_reps(given)
-    near = first_steps(own_piece(group), steps)
+    near = first_steps(own_piece, steps)
     far = {0: swap_ep(near[0], 1)}
     near[1], kept = join(near[1], kept)
     far[1] = swap_ep(near[1], 1)
 
-    inner = latent_width // 4
-    up_piece = lax.dynamic_slice_in_dim(up_latent, own_quarter * inner, inner, 0)
     mine = lax.all_gather(up_piece, "ep", axis=0)
     weights = dense_weights(after(expert_ids, near[1]), route_scores, expert_count)
     others = {k: near[k] for k in near if k > 1}
@@ -380,7 +408,7 @@
         far[k] = swap_ep(near[k], 1)
     blocks = []
     for k in range(steps):
-        other = own_piece(1 - group) if k == 0 else swap_cores(near[k])
+        other = other_piece if k == 0 else swap_cores(near[k])
         blocks.append((near[k], far[k], other, swap_cores(far[k])))
     early = list(range(last))
     (partial,) = down_project(early, kept, taken, [b for k in early for b in blocks[k]])
@@ -444,7 +472,7 @@
         send((last, 0), sums[last, 0], 2),
         start_far(1),
     )
-    run([(1, 1)], send((last, 1), sums[last, 1], 3), *homeward((0, 1)))
+    run([(1, 1)], send((last, 1), sums[last, 1], 3))
     shared = sums[last - 1, 0]
     for name in ((last - 1, 1), (last, 0), (last, 1)):
         shared += travel.pop(name).astype(jnp.float32)
@@ -452,7 +480,7 @@
     send("shared", shared, 2 * last - 2)
     sums[1, 1] = sums[1, 1].astype(jnp.bfloat16)
     both_sides = after(both_sides, sums[1, 1], shared)
-    homeward((1, 1))
+    homeward((0, 1), (1, 1))
     *terms, swapped_sides = join(sums[0, 0], *travel.values(), swap_cores(both_sides))
     both_sides = pltpu.with_memory_space_constraint(both_sides, pltpu.HBM)
     return project(group, terms, both_sides, swapped_sides)

time: 170 us -> 173 us (1.018)
  Pallas kernels: 48.6 us -> 57.6 us
  waiting for transfers between devices: 62.1 us -> 58.4 us
  local copies, waits for them, and re-layouts: 4.24 us -> 1.23 us
    pallas_call x0 -> x1, Pallas kernels: none -> 9.07 us  [cut_quarters(): pl.pallas_call(cut_kernel, out_shape=shapes, in_specs=[in_smem] + [in_hbm...]
    ppermute x21, waiting for transfers between devices: 50.2 us -> 46.7 us  [swap_ep(): lax.ppermute(array, 'ep', [(i, i ^ mask) for i in range(lax.axis_size('ep...]
    dynamic_slice x2 -> x0, local copies, waits for them, and re-layouts: 1.79 us -> none  [the longest x1 1.07 us: own_piece(): lax.dynamic_slice_in_dim(down_latent, (2 * side + core) * quarter, quarte...]
  transfers between devices with their start and end apart: 46 -> 46, of which waited for: 16 -> 17; matrix products, arithmetic and copies ran while one was open for 2% -> 2% of each run, Pallas kernels for 26% -> 25%
where the time goes in v14:
time: 173 us
  waiting for transfers between devices  58.4 us (34%)
  Pallas kernels  57.6 us (33%)
  starting transfers between devices  39.1 us (23%)
  between operations  13.7 us (8%)
  other arithmetic  3 us (2%)
    ppermute x21, waiting for transfers between devices, swap_ep(): lax.ppermute(array, 'ep', [(i, i ^ mask) for i in range(lax.axis_size('ep...  46.7 us
    pallas_call x5, Pallas kernels, expert_apply(): pl.pallas_call(functools.partial(expert_kernel, positions, count), out_sh...  41.5 us
    ppermute x21, starting transfers between devices, swap_ep(): lax.ppermute(array, 'ep', [(i, i ^ mask) for i in range(lax.axis_size('ep...  31.6 us
    pallas_call x1, Pallas kernels, cut_quarters(): pl.pallas_call(cut_kernel, out_shape=shapes, in_specs=[in_smem] + [in_hbm...  9.07 us
    ppermute x2, waiting for transfers between devices, swap_reps(): lax.ppermute(array, 'rep', [(i, i ^ 1) for i in range(lax.axis_size('rep'...  6.87 us
    pallas_call x1, Pallas kernels, project(): pl.pallas_call(project_kernel, in_specs=[in_smem] + [in_vmem] * len(terms...  4.71 us
    ppermute x21, starting transfers between devices, swap_cores(): return lax.ppermute(array, 'grp', [(0, 1), (1, 0)])  4.29 us
    ppermute x21, waiting for transfers between devices, swap_cores(): return lax.ppermute(array, 'grp', [(0, 1), (1, 0)])  4.01 us
  transfers between devices with their start and end apart: 46, of which 17 were waited for; matrix products, arithmetic and copies ran while one was open for 2% of the time, Pallas kernels for 25%

profile of v14, /device:TPU:0, one launch (start us, length us, event | category | flops | bytes accessed | tf_op | source)
XLA Modules:
  0.0 173.0 jit_solution(9043225503819445102)
XLA Ops:
  6.5 9.1 %cut_quarters.1 = (bf16[128,1024]{1,0:T(8,128)(2,1)S(1)}, bf16[128,1024]{1,0:T(8,128)(2,1)S(1)}, bf16[256,512]{1,0:T(8,128)(2,1)}) custom-call(s32[1]{0:T(128)} %bitcast.2.where, bf16[512,1024]{1,0:T(8,128)(2,1)} %down.1, bf16[1024,512]{1,0:T(8,128)(2,1)} %up.1), custom_call_target="tpu_custom_call" | custom-call | tf_op jit(solution)/shard_map/cut_quarters/pallas_call | solution.py:69
  15.7 3.1 %collective-permute-start = (bf16[128,1024]{1,0:T(8,128)(2,1)S(1)}, bf16[128,1024]{1,0:T(8,128)(2,1)S(1)}, u32[]{:S(2)}, u32[]{:S(2)}) collective-permute-start(bf16[128,1024]{1,0:T(8,128)(2,1)S(1)} %get-tuple-element.83.refs_2_), channel_id=1, source_target_pairs={{0,2},{1,3},{2,0},{3,1},{4,6},{5,7},{6,4},{7,5},{8,10},{9,11},{10,... | collective-permute-start | bytes 786440 | tf_op jit(solution)/shard_map/ppermute | solution.py:35
  18.8 1.5 collective-permute-start.4
  20.3 2.6 %collective-permute-start.2 = (bf16[128,1024]{1,0:T(8,128)(2,1)S(1)}, bf16[128,1024]{1,0:T(8,128)(2,1)S(1)}, u32[]{:S(2)}, u32[]{:S(2)}) collective-permute-start(bf16[128,1024]{1,0:T(8,128)(2,1)S(1)} %get-tuple-element.83.refs_2_), channel_id=1, source_target_pairs={{0,4},{1,5},{2,6},{3,7},{4,0},{5,1},{6,2},{7,3},{8,12},{9,13},{10,... | collective-permute-start | bytes 786440 | tf_op jit(solution)/shard_map/ppermute | solution.py:35
  23.0 1.2 copy-done
  24.2 0.8 split_columns.1
  25.0 1.6 collective-permute-start.5
  26.6 0.7 fusion.1
  27.3 2.1 %collective-permute-done.refs_6_ = bf16[128,1024]{1,0:T(8,128)(2,1)S(1)} collective-permute-done((bf16[128,1024]{1,0:T(8,128)(2,1)S(1)}, bf16[128,1024]{1,0:T(8,128)(2,1)S(1)}, u32[]{:S(2)}, u32[]{:S(2)}) %collective-permute-start) | collective-permute-done | bytes 262176 | tf_op jit(solution)/shard_map/ppermute | solution.py:35
  29.3 4.1 %collective-permute-start.1 = (bf16[128,1024]{1,0:T(8,128)(2,1)S(1)}, bf16[128,1024]{1,0:T(8,128)(2,1)S(1)}, u32[]{:S(2)}, u32[]{:S(2)}) collective-permute-start(bf16[128,1024]{1,0:T(8,128)(2,1)S(1)} %collective-permute-done.refs_6_), channel_id=1, source_target_pairs={{0,1},{1,0},{2,3},{3,2},{4,5},{5,4},{6,7},{7,6},{8,9},{9,8},{10,11... | collective-permute-start | bytes 786440 | tf_op jit(solution)/shard_map/ppermute | solution.py:35
  33.4 0.7 fusion
  34.1 0.7 select_reduce_fusion.weights
  34.9 4.2 %collective-permute-done.2.refs_10_ = bf16[128,1024]{1,0:T(8,128)(2,1)S(1)} collective-permute-done((bf16[128,1024]{1,0:T(8,128)(2,1)S(1)}, bf16[128,1024]{1,0:T(8,128)(2,1)S(1)}, u32[]{:S(2)}, u32[]{:S(2)}) %collective-permute-start.2) | collective-permute-done | bytes 262176 | tf_op jit(solution)/shard_map/ppermute | solution.py:35
  39.1 0.8 collective-permute-start.3
  40.4 7.6 %collective-permute-done.3.refs_2_ = bf16[128,1024]{1,0:T(8,128)(2,1)S(1)} collective-permute-done((bf16[128,1024]{1,0:T(8,128)(2,1)S(1)}, bf16[128,1024]{1,0:T(8,128)(2,1)S(1)}, u32[]{:S(2)}, u32[]{:S(2)}) %collective-permute-start.3) | collective-permute-done | bytes 262176 | tf_op jit(solution)/shard_map/ppermute | solution.py:35
  48.0 0.6 collective-permute-start.12
  48.6 0.5 collective-permute-start.11
  49.6 9.9 %collective-permute-done.12.refs_3_ = bf16[128,1024]{1,0:T(8,128)(2,1)S(1)} collective-permute-done((bf16[128,1024]{1,0:T(8,128)(2,1)S(1)}, bf16[128,1024]{1,0:T(8,128)(2,1)S(1)}, u32[]{:S(2)}, u32[]{:S(2)}) %collective-permute-start.12) | collective-permute-done | bytes 262176 | tf_op jit(solution)/shard_map/ppermute | solution.py:35
  59.5 1.0 down_project.2.refs_6_
  61.5 1.5 collective-permute-start.15
  63.0 6.9 %collective-permute-done.15.arrived = bf16[128,1024]{1,0:T(8,128)(2,1)S(1)} collective-permute-done((bf16[128,1024]{1,0:T(8,128)(2,1)S(1)}, bf16[128,1024]{1,0:T(8,128)(2,1)S(1)}, u32[]{:S(2)}, u32[]{:S(2)}) %collective-permute-start.15) | collective-permute-done | bytes 262176 | tf_op jit(solution)/shard_map/ppermute | solution.py:31
  70.2 1.7 collective-permute-start.17
  71.8 6.4 %expert.5 = (bf16[128,1024]{1,0:T(8,128)(2,1)S(1)}, bf16[128,1024]{1,0:T(8,128)(2,1)S(1)}) custom-call(s32[1]{0:T(128)} %bitcast.1.where, bf16[144,1024]{1,0:T(8,128)(2,1)S(1)} %finish_latent.1.refs_0_, bf16[144,1024]{1,0:T(8,128)(2,1)S(1)} %collective-permute-done.16.refs_1_, bf16[1,1024,2048]{2,1,0:T(8,128)(2,1)} %refs_2_.3, ...), custom_call_target="tpu_custom_call" | custom-call | flops 805306368 | bytes 1048576 | tf_op jit(solution)/shard_map/expert/pallas_call | solution.py:289
  78.2 9.1 %collective-permute-done.18.refs_0_ = bf16[144,1024]{1,0:T(8,128)(2,1)S(1)} collective-permute-done((bf16[144,1024]{1,0:T(8,128)(2,1)S(1)}, bf16[144,1024]{1,0:T(8,128)(2,1)S(1)}, u32[]{:S(2)}, u32[]{:S(2)}) %collective-permute-start.18) | collective-permute-done | bytes 294944 | tf_op jit(solution)/shard_map/ppermute | solution.py:35
  87.9 1.7 collective-permute-start.23
  89.6 9.5 %expert.6 = (bf16[128,1024]{1,0:T(8,128)(2,1)S(1)}, bf16[128,1024]{1,0:T(8,128)(2,1)S(1)}, bf16[256,1024]{1,0:T(8,128)(2,1)S(1)}) custom-call(s32[1]{0:T(128)} %bitcast.1.where, bf16[144,1024]{1,0:T(8,128)(2,1)S(1)} %collective-permute-done.18.refs_0_, bf16[144,1024]{1,0:T(8,128)(2,1)S(1)} %collective-permute-done.17.refs_1_, ...), custom_call_target="tpu_custom_call" | custom-call | flops 1610612736 | bytes 2097152 | tf_op jit(solution)/shard_map/expert/pallas_call | solution.py:289
  99.2 1.6 collective-permute-start.29
  101.9 2.1 %collective-permute-start.27 = (bf16[128,1024]{1,0:T(8,128)(2,1)S(1)}, bf16[128,1024]{1,0:T(8,128)(2,1)S(1)}, u32[]{:S(2)}, u32[]{:S(2)}) collective-permute-start(bf16[128,1024]{1,0:T(8,128)(2,1)S(1)} %add_convert_fusion.6), channel_id=1, source_target_pairs={{0,2},{1,3},{2,0},{3,1},{4,6},{5,7},{6,4},{7,5},{8,10},{9,11},{10,... | collective-permute-start | bytes 786440 | tf_op jit(solution)/shard_map/ppermute | solution.py:35
  104.0 9.5 %expert.7 = (bf16[128,1024]{1,0:T(8,128)(2,1)S(1)}, bf16[128,1024]{1,0:T(8,128)(2,1)S(1)}, bf16[256,1024]{1,0:T(8,128)(2,1)S(1)}) custom-call(s32[1]{0:T(128)} %bitcast.1.where, bf16[144,1024]{1,0:T(8,128)(2,1)S(1)} %collective-permute-done.22.refs_0_, bf16[144,1024]{1,0:T(8,128)(2,1)S(1)} %collective-permute-done.23.refs_1_, ...), custom_call_target="tpu_custom_call" | custom-call | flops 1610612736 | bytes 2097152 | tf_op jit(solution)/shard_map/expert/pallas_call | solution.py:289
  113.5 1.4 collective-permute-done.28.refs_0_
  115.0 1.5 collective-permute-start.35
  117.1 2.0 %collective-permute-start.34 = (bf16[128,1024]{1,0:T(8,128)(2,1)S(1)}, bf16[128,1024]{1,0:T(8,128)(2,1)S(1)}, u32[]{:S(2)}, u32[]{:S(2)}) collective-permute-start(bf16[128,1024]{1,0:T(8,128)(2,1)S(1)} %get-tuple-element.163), channel_id=1, source_target_pairs={{0,2},{1,3},{2,0},{3,1},{4,6},{5,7},{6,4},{7,5},{8,10},{9,11},{10,... | collective-permute-start | bytes 786440 | tf_op jit(solution)/shard_map/ppermute | solution.py:35
  119.2 0.6 collective-permute-start.33
  119.8 9.7 %expert.8 = (bf16[128,1024]{1,0:T(8,128)(2,1)S(1)}, bf16[128,1024]{1,0:T(8,128)(2,1)S(1)}, bf16[256,1024]{1,0:T(8,128)(2,1)S(1)}) custom-call(s32[1]{0:T(128)} %bitcast.1.where, bf16[144,1024]{1,0:T(8,128)(2,1)S(1)} %collective-permute-done.28.refs_0_, bf16[144,1024]{1,0:T(8,128)(2,1)S(1)} %collective-permute-done.29.refs_1_, ...), custom_call_target="tpu_custom_call" | custom-call | flops 1610612736 | bytes 2097152 | tf_op jit(solution)/shard_map/expert/pallas_call | solution.py:289
  130.5 1.4 collective-permute-done.37
  132.1 1.9 %collective-permute-start.38 = (bf16[128,1024]{1,0:T(8,128)(2,1)S(1)}, bf16[128,1024]{1,0:T(8,128)(2,1)S(1)}, u32[]{:S(2)}, u32[]{:S(2)}) collective-permute-start(bf16[128,1024]{1,0:T(8,128)(2,1)S(1)} %get-tuple-element.162), channel_id=1, source_target_pairs={{0,3},{1,2},{2,1},{3,0},{4,7},{5,6},{6,5},{7,4},{8,11},{9,10},{10,... | collective-permute-start | bytes 786440 | tf_op jit(solution)/shard_map/ppermute | solution.py:35
  134.0 6.4 %expert.9 = (bf16[128,1024]{1,0:T(8,128)(2,1)S(1)}, bf16[128,1024]{1,0:T(8,128)(2,1)S(1)}) custom-call(s32[1]{0:T(128)} %bitcast.1.where, bf16[144,1024]{1,0:T(8,128)(2,1)S(1)} %collective-permute-done.35.refs_0_, bf16[144,1024]{1,0:T(8,128)(2,1)S(1)} %collective-permute-done.36.refs_1_, bf16[1,1024,2048]{2,1,0:T(8,128)(2,1)} %refs_2_.3, ...), custom_call_target="tpu_custom_call" | custom-call | flops 805306368 | bytes 1048576 | tf_op jit(solution)/shard_map/expert/pallas_call | solution.py:289
  140.4 1.0 collective-permute-done.38
  141.6 1.3 collective-permute-done.41
  143.0 0.8 all-gather.7.cloned.1.call-done
  144.3 1.5 collective-permute-start.40
  145.8 2.4 %collective-permute-start.39 = (bf16[128,1024]{1,0:T(8,128)(2,1)S(1)}, bf16[128,1024]{1,0:T(8,128)(2,1)S(1)}, u32[]{:S(2)}, u32[]{:S(2)}) collective-permute-start(bf16[128,1024]{1,0:T(8,128)(2,1)S(1)} %add_convert_fusion.2), channel_id=1, source_target_pairs={{0,4},{1,5},{2,6},{3,7},{4,0},{5,1},{6,2},{7,3},{8,12},{9,13},{10,... | collective-permute-start | bytes 786440 | tf_op jit(solution)/shard_map/ppermute | solution.py:35
  148.2 1.5 collective-permute-start.42
  149.7 0.8 collective-permute-done.19
  150.5 6.6 %collective-permute-done.40.refs_3_ = bf16[128,1024]{1,0:T(8,128)(2,1)S(1)} collective-permute-done((bf16[128,1024]{1,0:T(8,128)(2,1)S(1)}, bf16[128,1024]{1,0:T(8,128)(2,1)S(1)}, u32[]{:S(2)}, u32[]{:S(2)}) %collective-permute-start.40) | collective-permute-done | bytes 262176 | tf_op jit(solution)/shard_map/ppermute | solution.py:35
  157.1 3.3 %collective-permute-done.39.refs_2_ = bf16[128,1024]{1,0:T(8,128)(2,1)S(1)} collective-permute-done((bf16[128,1024]{1,0:T(8,128)(2,1)S(1)}, bf16[128,1024]{1,0:T(8,128)(2,1)S(1)}, u32[]{:S(2)}, u32[]{:S(2)}) %collective-permute-start.39) | collective-permute-done | bytes 262176 | tf_op jit(solution)/shard_map/ppermute | solution.py:35
  160.3 1.1 collective-permute-done.42.refs_4_
  161.4 4.7 %project.1 = bf16[128,4096]{1,0:T(8,128)(2,1)} custom-call(s32[1]{0:T(128)} %bitcast.where, f32[128,1024]{1,0:T(8,128)S(1)} %convert_add_fusion.refs_0_, bf16[128,1024]{1,0:T(8,128)(2,1)S(1)} %collective-permute-done.27.refs_1_, bf16[128,1024]{1,0:T(8,128)(2,1)S(1)} %collective-permute-done.39.refs_2_, ...), custom_call_target="tpu_custom_call" | custom-call | flops 1073741824 | bytes 8388608 | tf_op jit(solution)/shard_map/project/pallas_call | solution.py:351
  (69 shorter events, 6.9 us)
Async XLA Ops:
  6.5 80.8 %all-gather.5.cloned.1.call-start = ((), (), s32[]{:S(2)}) async-start(), calls=%async_computation | async-start | bytes 2359296 | tf_op jit(solution)/shard_map/all_gather | solution.py:397
  15.6 128.2 %all-gather.7.cloned.1.call-start = ((), (), s32[]{:S(2)}) async-start(), calls=%async_computation.1 | async-start | bytes 6291456 | tf_op jit(solution)/shard_map/all_gather | solution.py:460
  15.7 13.7 %collective-permute-start = (bf16[128,1024]{1,0:T(8,128)(2,1)S(1)}, bf16[128,1024]{1,0:T(8,128)(2,1)S(1)}, u32[]{:S(2)}, u32[]{:S(2)}) collective-permute-start(bf16[128,1024]{1,0:T(8,128)(2,1)S(1)} %get-tuple-element.83.refs_2_), channel_id=1, source_target_pairs={{0,2},{1,3},{2,0},{3,1},{4,6},{5,7},{6,4},{7,5},{8,10},{9,11},{10,... | collective-permute-start | bytes 786440 | tf_op jit(solution)/shard_map/ppermute | solution.py:35
  18.8 21.1 %collective-permute-start.4 = (bf16[128,1024]{1,0:T(8,128)(2,1)S(1)}, bf16[128,1024]{1,0:T(8,128)(2,1)S(1)}, u32[]{:S(2)}, u32[]{:S(2)}) collective-permute-start(bf16[128,1024]{1,0:T(8,128)(2,1)S(1)} %get-tuple-element.83.refs_2_), channel_id=1, source_target_pairs={{0,1},{1,0},{2,3},{3,2},{4,5},{5,4},{6,7},{7,6},{8,9},{9,8},{10,11... | collective-permute-start | bytes 786440 | tf_op jit(solution)/shard_map/ppermute | solution.py:35
  20.3 18.8 %collective-permute-start.2 = (bf16[128,1024]{1,0:T(8,128)(2,1)S(1)}, bf16[128,1024]{1,0:T(8,128)(2,1)S(1)}, u32[]{:S(2)}, u32[]{:S(2)}) collective-permute-start(bf16[128,1024]{1,0:T(8,128)(2,1)S(1)} %get-tuple-element.83.refs_2_), channel_id=1, source_target_pairs={{0,4},{1,5},{2,6},{3,7},{4,0},{5,1},{6,2},{7,3},{8,12},{9,13},{10,... | collective-permute-start | bytes 786440 | tf_op jit(solution)/shard_map/ppermute | solution.py:35
  23.0 1.2 copy-start
  25.0 15.3 %collective-permute-start.5 = (bf16[128,2048]{1,0:T(8,128)(2,1)S(1)}, bf16[128,2048]{1,0:T(8,128)(2,1)S(1)}, u32[]{:S(2)}, u32[]{:S(2)}) collective-permute-start(bf16[128,2048]{1,0:T(8,128)(2,1)S(1)} %get-tuple-element.89), channel_id=1, source_target_pairs={{0,16},{16,0},{1,17},{17,1},{2,18},{18,2},{3,19},{19,3},{4,20},{20... | collective-permute-start | bytes 1572872 | tf_op jit(solution)/shard_map/ppermute | solution.py:31
  29.3 9.7 %collective-permute-start.1 = (bf16[128,1024]{1,0:T(8,128)(2,1)S(1)}, bf16[128,1024]{1,0:T(8,128)(2,1)S(1)}, u32[]{:S(2)}, u32[]{:S(2)}) collective-permute-start(bf16[128,1024]{1,0:T(8,128)(2,1)S(1)} %collective-permute-done.refs_6_), channel_id=1, source_target_pairs={{0,1},{1,0},{2,3},{3,2},{4,5},{5,4},{6,7},{7,6},{8,9},{9,8},{10,11... | collective-permute-start | bytes 786440 | tf_op jit(solution)/shard_map/ppermute | solution.py:35
  39.1 8.9 %collective-permute-start.3 = (bf16[128,1024]{1,0:T(8,128)(2,1)S(1)}, bf16[128,1024]{1,0:T(8,128)(2,1)S(1)}, u32[]{:S(2)}, u32[]{:S(2)}) collective-permute-start(bf16[128,1024]{1,0:T(8,128)(2,1)S(1)} %collective-permute-done.2.refs_10_), channel_id=1, source_target_pairs={{0,2},{1,3},{2,0},{3,1},{4,6},{5,7},{6,4},{7,5},{8,10},{9,11},{10,... | collective-permute-start | bytes 786440 | tf_op jit(solution)/shard_map/ppermute | solution.py:35
  39.8 8.7 %collective-permute-start.9 = (bf16[128,1024]{1,0:T(8,128)(2,1)S(1)}, bf16[128,1024]{1,0:T(8,128)(2,1)S(1)}, u32[]{:S(2)}, u32[]{:S(2)}) collective-permute-start(bf16[128,1024]{1,0:T(8,128)(2,1)S(1)} %collective-permute-done.2.refs_10_), channel_id=1, source_target_pairs={{0,1},{1,0},{2,3},{3,2},{4,5},{5,4},{6,7},{7,6},{8,9},{9,8},{10,11... | collective-permute-start | bytes 786440 | tf_op jit(solution)/shard_map/ppermute | solution.py:35
  39.8 9.2 %collective-permute-start.7 = (bf16[128,1024]{1,0:T(8,128)(2,1)S(1)}, bf16[128,1024]{1,0:T(8,128)(2,1)S(1)}, u32[]{:S(2)}, u32[]{:S(2)}) collective-permute-start(bf16[128,1024]{1,0:T(8,128)(2,1)S(1)} %collective-permute-done.refs_6_), channel_id=1, source_target_pairs={{0,8},{8,0},{1,9},{9,1},{2,10},{10,2},{3,11},{11,3},{4,12},{12,4},... | collective-permute-start | bytes 786440 | tf_op jit(solution)/shard_map/ppermute | solution.py:27
  39.9 9.3 %collective-permute-start.8 = (bf16[128,1024]{1,0:T(8,128)(2,1)S(1)}, bf16[128,1024]{1,0:T(8,128)(2,1)S(1)}, u32[]{:S(2)}, u32[]{:S(2)}) collective-permute-start(bf16[128,1024]{1,0:T(8,128)(2,1)S(1)} %collective-permute-done.1.refs_7_), channel_id=1, source_target_pairs={{0,8},{8,0},{1,9},{9,1},{2,10},{10,2},{3,11},{11,3},{4,12},{12,4},... | collective-permute-start | bytes 786440 | tf_op jit(solution)/shard_map/ppermute | solution.py:27
  48.0 11.5 %collective-permute-start.12 = (bf16[128,1024]{1,0:T(8,128)(2,1)S(1)}, bf16[128,1024]{1,0:T(8,128)(2,1)S(1)}, u32[]{:S(2)}, u32[]{:S(2)}) collective-permute-start(bf16[128,1024]{1,0:T(8,128)(2,1)S(1)} %collective-permute-done.3.refs_2_), channel_id=1, source_target_pairs={{0,1},{1,0},{2,3},{3,2},{4,5},{5,4},{6,7},{7,6},{8,9},{9,8},{10,11... | collective-permute-start | bytes 786440 | tf_op jit(solution)/shard_map/ppermute | solution.py:35
  48.5 10.9 %collective-permute-start.10 = (bf16[128,1024]{1,0:T(8,128)(2,1)S(1)}, bf16[128,1024]{1,0:T(8,128)(2,1)S(1)}, u32[]{:S(2)}, u32[]{:S(2)}) collective-permute-start(bf16[128,1024]{1,0:T(8,128)(2,1)S(1)} %collective-permute-done.2.refs_10_), channel_id=1, source_target_pairs={{0,8},{8,0},{1,9},{9,1},{2,10},{10,2},{3,11},{11,3},{4,12},{12,4},... | collective-permute-start | bytes 786440 | tf_op jit(solution)/shard_map/ppermute | solution.py:27
  48.6 10.9 %collective-permute-start.11 = (bf16[128,1024]{1,0:T(8,128)(2,1)S(1)}, bf16[128,1024]{1,0:T(8,128)(2,1)S(1)}, u32[]{:S(2)}, u32[]{:S(2)}) collective-permute-start(bf16[128,1024]{1,0:T(8,128)(2,1)S(1)} %collective-permute-done.9.refs_11_), channel_id=1, source_target_pairs={{0,8},{8,0},{1,9},{9,1},{2,10},{10,2},{3,11},{11,3},{4,12},{12,4},... | collective-permute-start | bytes 786440 | tf_op jit(solution)/shard_map/ppermute | solution.py:27
  49.1 10.4 %collective-permute-start.6 = (bf16[128,1024]{1,0:T(8,128)(2,1)S(1)}, bf16[128,1024]{1,0:T(8,128)(2,1)S(1)}, u32[]{:S(2)}, u32[]{:S(2)}) collective-permute-start(bf16[128,1024]{1,0:T(8,128)(2,1)S(1)} %collective-permute-done.4.refs_3_), channel_id=1, source_target_pairs={{0,8},{8,0},{1,9},{9,1},{2,10},{10,2},{3,11},{11,3},{4,12},{12,4},... | collective-permute-start | bytes 786440 | tf_op jit(solution)/shard_map/ppermute | solution.py:27
  49.1 11.4 %collective-permute-start.13 = (bf16[128,1024]{1,0:T(8,128)(2,1)S(1)}, bf16[128,1024]{1,0:T(8,128)(2,1)S(1)}, u32[]{:S(2)}, u32[]{:S(2)}) collective-permute-start(bf16[128,1024]{1,0:T(8,128)(2,1)S(1)} %collective-permute-done.3.refs_2_), channel_id=1, source_target_pairs={{0,8},{8,0},{1,9},{9,1},{2,10},{10,2},{3,11},{11,3},{4,12},{12,4},... | collective-permute-start | bytes 786440 | tf_op jit(solution)/shard_map/ppermute | solution.py:27
  59.5 1.5 collective-permute-start.14
  61.5 8.4 %collective-permute-start.15 = (bf16[128,1024]{1,0:T(8,128)(2,1)S(1)}, bf16[128,1024]{1,0:T(8,128)(2,1)S(1)}, u32[]{:S(2)}, u32[]{:S(2)}) collective-permute-start(bf16[128,1024]{1,0:T(8,128)(2,1)S(1)} %get-tuple-element.97), channel_id=1, source_target_pairs={{0,16},{16,0},{1,17},{17,1},{2,18},{18,2},{3,19},{19,3},{4,20},{20... | collective-permute-start | bytes 786440 | tf_op jit(solution)/shard_map/ppermute | solution.py:31
  69.9 1.9 %collective-permute-start.16 = (bf16[144,1024]{1,0:T(8,128)(2,1)S(1)}, bf16[144,1024]{1,0:T(8,128)(2,1)S(1)}, u32[]{:S(2)}, u32[]{:S(2)}) collective-permute-start(bf16[144,1024]{1,0:T(8,128)(2,1)S(1)} %finish_latent.1.refs_0_), channel_id=1, source_target_pairs={{0,8},{8,0},{1,9},{9,1},{2,10},{10,2},{3,11},{11,3},{4,12},{12,4},... | collective-permute-start | bytes 884744 | tf_op jit(solution)/shard_map/ppermute | solution.py:27
  70.0 17.3 %collective-permute-start.18 = (bf16[144,1024]{1,0:T(8,128)(2,1)S(1)}, bf16[144,1024]{1,0:T(8,128)(2,1)S(1)}, u32[]{:S(2)}, u32[]{:S(2)}) collective-permute-start(bf16[144,1024]{1,0:T(8,128)(2,1)S(1)} %finish_latent.1.refs_0_), channel_id=1, source_target_pairs={{0,4},{1,5},{2,6},{3,7},{4,0},{5,1},{6,2},{7,3},{8,12},{9,13},{10,... | collective-permute-start | bytes 884744 | tf_op jit(solution)/shard_map/ppermute | solution.py:35
  70.2 17.2 %collective-permute-start.17 = (bf16[144,1024]{1,0:T(8,128)(2,1)S(1)}, bf16[144,1024]{1,0:T(8,128)(2,1)S(1)}, u32[]{:S(2)}, u32[]{:S(2)}) collective-permute-start(bf16[144,1024]{1,0:T(8,128)(2,1)S(1)} %finish_latent.1.refs_0_), channel_id=1, source_target_pairs={{0,2},{1,3},{2,0},{3,1},{4,6},{5,7},{6,4},{7,5},{8,10},{9,11},{10,... | collective-permute-start | bytes 884744 | tf_op jit(solution)/shard_map/ppermute | solution.py:35
  87.3 2.3 %collective-permute-start.21 = (bf16[144,1024]{1,0:T(8,128)(2,1)S(1)}, bf16[144,1024]{1,0:T(8,128)(2,1)S(1)}, u32[]{:S(2)}, u32[]{:S(2)}) collective-permute-start(bf16[144,1024]{1,0:T(8,128)(2,1)S(1)} %collective-permute-done.17.refs_1_), channel_id=1, source_target_pairs={{0,8},{8,0},{1,9},{9,1},{2,10},{10,2},{3,11},{11,3},{4,12},{12,4},... | collective-permute-start | bytes 884744 | tf_op jit(solution)/shard_map/ppermute | solution.py:27
  87.4 2.2 %collective-permute-start.20 = (bf16[144,1024]{1,0:T(8,128)(2,1)S(1)}, bf16[144,1024]{1,0:T(8,128)(2,1)S(1)}, u32[]{:S(2)}, u32[]{:S(2)}) collective-permute-start(bf16[144,1024]{1,0:T(8,128)(2,1)S(1)} %collective-permute-done.18.refs_0_), channel_id=1, source_target_pairs={{0,8},{8,0},{1,9},{9,1},{2,10},{10,2},{3,11},{11,3},{4,12},{12,4},... | collective-permute-start | bytes 884744 | tf_op jit(solution)/shard_map/ppermute | solution.py:27
  87.9 11.2 %collective-permute-start.23 = (bf16[144,1024]{1,0:T(8,128)(2,1)S(1)}, bf16[144,1024]{1,0:T(8,128)(2,1)S(1)}, u32[]{:S(2)}, u32[]{:S(2)}) collective-permute-start(bf16[144,1024]{1,0:T(8,128)(2,1)S(1)} %collective-permute-done.18.refs_0_), channel_id=1, source_target_pairs={{0,1},{1,0},{2,3},{3,2},{4,5},{5,4},{6,7},{7,6},{8,9},{9,8},{10,11... | collective-permute-start | bytes 884744 | tf_op jit(solution)/shard_map/ppermute | solution.py:35
  89.6 9.5 %collective-permute-start.22 = (bf16[144,1024]{1,0:T(8,128)(2,1)S(1)}, bf16[144,1024]{1,0:T(8,128)(2,1)S(1)}, u32[]{:S(2)}, u32[]{:S(2)}) collective-permute-start(bf16[144,1024]{1,0:T(8,128)(2,1)S(1)} %collective-permute-done.18.refs_0_), channel_id=1, source_target_pairs={{0,2},{1,3},{2,0},{3,1},{4,6},{5,7},{6,4},{7,5},{8,10},{9,11},{10,... | collective-permute-start | bytes 884744 | tf_op jit(solution)/shard_map/ppermute | solution.py:35
  99.1 2.7 %collective-permute-start.26 = (bf16[256,1024]{1,0:T(8,128)(2,1)S(1)}, bf16[256,1024]{1,0:T(8,128)(2,1)S(1)}, u32[]{:S(2)}, u32[]{:S(2)}) collective-permute-start(bf16[256,1024]{1,0:T(8,128)(2,1)S(1)} %get-tuple-element.125), channel_id=1, source_target_pairs={{0,8},{8,0},{1,9},{9,1},{2,10},{10,2},{3,11},{11,3},{4,12},{12,4},... | collective-permute-start | bytes 1572872 | tf_op jit(solution)/shard_map/ppermute | solution.py:27
  99.2 14.3 %collective-permute-start.29 = (bf16[144,1024]{1,0:T(8,128)(2,1)S(1)}, bf16[144,1024]{1,0:T(8,128)(2,1)S(1)}, u32[]{:S(2)}, u32[]{:S(2)}) collective-permute-start(bf16[144,1024]{1,0:T(8,128)(2,1)S(1)} %finish_latent.1.refs_0_), channel_id=1, source_target_pairs={{0,1},{1,0},{2,3},{3,2},{4,5},{5,4},{6,7},{7,6},{8,9},{9,8},{10,11... | collective-permute-start | bytes 884744 | tf_op jit(solution)/shard_map/ppermute | solution.py:35
  100.8 14.1 %collective-permute-start.28 = (bf16[144,1024]{1,0:T(8,128)(2,1)S(1)}, bf16[144,1024]{1,0:T(8,128)(2,1)S(1)}, u32[]{:S(2)}, u32[]{:S(2)}) collective-permute-start(bf16[144,1024]{1,0:T(8,128)(2,1)S(1)} %collective-permute-done.22.refs_0_), channel_id=1, source_target_pairs={{0,1},{1,0},{2,3},{3,2},{4,5},{5,4},{6,7},{7,6},{8,9},{9,8},{10,11... | collective-permute-start | bytes 884744 | tf_op jit(solution)/shard_map/ppermute | solution.py:35
  101.3 2.7 %collective-permute-start.24 = (bf16[144,1024]{1,0:T(8,128)(2,1)S(1)}, bf16[144,1024]{1,0:T(8,128)(2,1)S(1)}, u32[]{:S(2)}, u32[]{:S(2)}) collective-permute-start(bf16[144,1024]{1,0:T(8,128)(2,1)S(1)} %collective-permute-done.22.refs_0_), channel_id=1, source_target_pairs={{0,8},{8,0},{1,9},{9,1},{2,10},{10,2},{3,11},{11,3},{4,12},{12,4},... | collective-permute-start | bytes 884744 | tf_op jit(solution)/shard_map/ppermute | solution.py:27
  101.3 2.7 %collective-permute-start.25 = (bf16[144,1024]{1,0:T(8,128)(2,1)S(1)}, bf16[144,1024]{1,0:T(8,128)(2,1)S(1)}, u32[]{:S(2)}, u32[]{:S(2)}) collective-permute-start(bf16[144,1024]{1,0:T(8,128)(2,1)S(1)} %collective-permute-done.23.refs_1_), channel_id=1, source_target_pairs={{0,8},{8,0},{1,9},{9,1},{2,10},{10,2},{3,11},{11,3},{4,12},{12,4},... | collective-permute-start | bytes 884744 | tf_op jit(solution)/shard_map/ppermute | solution.py:27
  101.9 13.1 %collective-permute-start.27 = (bf16[128,1024]{1,0:T(8,128)(2,1)S(1)}, bf16[128,1024]{1,0:T(8,128)(2,1)S(1)}, u32[]{:S(2)}, u32[]{:S(2)}) collective-permute-start(bf16[128,1024]{1,0:T(8,128)(2,1)S(1)} %add_convert_fusion.6), channel_id=1, source_target_pairs={{0,2},{1,3},{2,0},{3,1},{4,6},{5,7},{6,4},{7,5},{8,10},{9,11},{10,... | collective-permute-start | bytes 786440 | tf_op jit(solution)/shard_map/ppermute | solution.py:35
  115.0 2.0 %collective-permute-start.32 = (bf16[256,1024]{1,0:T(8,128)(2,1)S(1)}, bf16[256,1024]{1,0:T(8,128)(2,1)S(1)}, u32[]{:S(2)}, u32[]{:S(2)}) collective-permute-start(bf16[256,1024]{1,0:T(8,128)(2,1)S(1)} %get-tuple-element.138), channel_id=1, source_target_pairs={{0,8},{8,0},{1,9},{9,1},{2,10},{10,2},{3,11},{11,3},{4,12},{12,4},... | collective-permute-start | bytes 1572872 | tf_op jit(solution)/shard_map/ppermute | solution.py:27
  115.0 14.6 %collective-permute-start.35 = (bf16[144,1024]{1,0:T(8,128)(2,1)S(1)}, bf16[144,1024]{1,0:T(8,128)(2,1)S(1)}, u32[]{:S(2)}, u32[]{:S(2)}) collective-permute-start(bf16[144,1024]{1,0:T(8,128)(2,1)S(1)} %collective-permute-done.17.refs_1_), channel_id=1, source_target_pairs={{0,1},{1,0},{2,3},{3,2},{4,5},{5,4},{6,7},{7,6},{8,9},{9,8},{10,11... | collective-permute-start | bytes 884744 | tf_op jit(solution)/shard_map/ppermute | solution.py:35
  116.4 3.4 %collective-permute-start.30 = (bf16[144,1024]{1,0:T(8,128)(2,1)S(1)}, bf16[144,1024]{1,0:T(8,128)(2,1)S(1)}, u32[]{:S(2)}, u32[]{:S(2)}) collective-permute-start(bf16[144,1024]{1,0:T(8,128)(2,1)S(1)} %collective-permute-done.28.refs_0_), channel_id=1, source_target_pairs={{0,8},{8,0},{1,9},{9,1},{2,10},{10,2},{3,11},{11,3},{4,12},{12,4},... | collective-permute-start | bytes 884744 | tf_op jit(solution)/shard_map/ppermute | solution.py:27
  116.7 3.1 %collective-permute-start.31 = (bf16[144,1024]{1,0:T(8,128)(2,1)S(1)}, bf16[144,1024]{1,0:T(8,128)(2,1)S(1)}, u32[]{:S(2)}, u32[]{:S(2)}) collective-permute-start(bf16[144,1024]{1,0:T(8,128)(2,1)S(1)} %collective-permute-done.29.refs_1_), channel_id=1, source_target_pairs={{0,8},{8,0},{1,9},{9,1},{2,10},{10,2},{3,11},{11,3},{4,12},{12,4},... | collective-permute-start | bytes 884744 | tf_op jit(solution)/shard_map/ppermute | solution.py:27
  117.1 12.4 %collective-permute-start.34 = (bf16[128,1024]{1,0:T(8,128)(2,1)S(1)}, bf16[128,1024]{1,0:T(8,128)(2,1)S(1)}, u32[]{:S(2)}, u32[]{:S(2)}) collective-permute-start(bf16[128,1024]{1,0:T(8,128)(2,1)S(1)} %get-tuple-element.163), channel_id=1, source_target_pairs={{0,2},{1,3},{2,0},{3,1},{4,6},{5,7},{6,4},{7,5},{8,10},{9,11},{10,... | collective-permute-start | bytes 786440 | tf_op jit(solution)/shard_map/ppermute | solution.py:35
  119.2 10.8 %collective-permute-start.33 = (bf16[128,1024]{1,0:T(8,128)(2,1)S(1)}, bf16[128,1024]{1,0:T(8,128)(2,1)S(1)}, u32[]{:S(2)}, u32[]{:S(2)}) collective-permute-start(bf16[128,1024]{1,0:T(8,128)(2,1)S(1)} %get-tuple-element.164), channel_id=1, source_target_pairs={{0,1},{1,0},{2,3},{3,2},{4,5},{5,4},{6,7},{7,6},{8,9},{9,8},{10,11... | collective-permute-start | bytes 786440 | tf_op jit(solution)/shard_map/ppermute | solution.py:35
  130.0 1.9 %collective-permute-start.37 = (bf16[256,1024]{1,0:T(8,128)(2,1)S(1)}, bf16[256,1024]{1,0:T(8,128)(2,1)S(1)}, u32[]{:S(2)}, u32[]{:S(2)}) collective-permute-start(bf16[256,1024]{1,0:T(8,128)(2,1)S(1)} %get-tuple-element.148), channel_id=1, source_target_pairs={{0,8},{8,0},{1,9},{9,1},{2,10},{10,2},{3,11},{11,3},{4,12},{12,4},... | collective-permute-start | bytes 1572872 | tf_op jit(solution)/shard_map/ppermute | solution.py:27
  130.0 4.0 %collective-permute-start.36 = (bf16[144,1024]{1,0:T(8,128)(2,1)S(1)}, bf16[144,1024]{1,0:T(8,128)(2,1)S(1)}, u32[]{:S(2)}, u32[]{:S(2)}) collective-permute-start(bf16[144,1024]{1,0:T(8,128)(2,1)S(1)} %collective-permute-done.35.refs_0_), channel_id=1, source_target_pairs={{0,8},{8,0},{1,9},{9,1},{2,10},{10,2},{3,11},{11,3},{4,12},{12,4},... | collective-permute-start | bytes 884744 | tf_op jit(solution)/shard_map/ppermute | solution.py:27
  132.1 9.3 %collective-permute-start.38 = (bf16[128,1024]{1,0:T(8,128)(2,1)S(1)}, bf16[128,1024]{1,0:T(8,128)(2,1)S(1)}, u32[]{:S(2)}, u32[]{:S(2)}) collective-permute-start(bf16[128,1024]{1,0:T(8,128)(2,1)S(1)} %get-tuple-element.162), channel_id=1, source_target_pairs={{0,3},{1,2},{2,1},{3,0},{4,7},{5,6},{6,5},{7,4},{8,11},{9,10},{10,... | collective-permute-start | bytes 786440 | tf_op jit(solution)/shard_map/ppermute | solution.py:35
  141.4 1.5 collective-permute-start.41
  143.8 17.6 %collective-permute-start.43 = (bf16[2,8,256,512]{3,2,1,0:T(8,128)(2,1)}, bf16[2,8,256,512]{3,2,1,0:T(8,128)(2,1)S(1)}, u32[]{:S(2)}, u32[]{:S(2)}) collective-permute-start(bf16[2,8,256,512]{3,2,1,0:T(8,128)(2,1)} %bitcast.7), channel_id=1, source_target_pairs={{0,8},{8,0},{1,9},{9,1},{2,10},{10,2},{3,11},{11,3},{4,12},{12,4},... | collective-permute-start | bytes 12582920 | tf_op jit(solution)/shard_map/ppermute | solution.py:27
  143.8 6.6 %collective-permute-start.19 = (bf16[128,1024]{1,0:T(8,128)(2,1)S(1)}, bf16[128,1024]{1,0:T(8,128)(2,1)S(1)}, u32[]{:S(2)}, u32[]{:S(2)}) collective-permute-start(bf16[128,1024]{1,0:T(8,128)(2,1)S(1)} %get-tuple-element.105), channel_id=1, source_target_pairs={{0,8},{8,0},{1,9},{9,1},{2,10},{10,2},{3,11},{11,3},{4,12},{12,4},... | collective-permute-start | bytes 786440 | tf_op jit(solution)/shard_map/ppermute | solution.py:27
  144.3 12.8 %collective-permute-start.40 = (bf16[128,1024]{1,0:T(8,128)(2,1)S(1)}, bf16[128,1024]{1,0:T(8,128)(2,1)S(1)}, u32[]{:S(2)}, u32[]{:S(2)}) collective-permute-start(bf16[128,1024]{1,0:T(8,128)(2,1)S(1)} %get-tuple-element.161), channel_id=1, source_target_pairs={{0,1},{1,0},{2,3},{3,2},{4,5},{5,4},{6,7},{7,6},{8,9},{9,8},{10,11... | collective-permute-start | bytes 786440 | tf_op jit(solution)/shard_map/ppermute | solution.py:35
  145.8 14.6 %collective-permute-start.39 = (bf16[128,1024]{1,0:T(8,128)(2,1)S(1)}, bf16[128,1024]{1,0:T(8,128)(2,1)S(1)}, u32[]{:S(2)}, u32[]{:S(2)}) collective-permute-start(bf16[128,1024]{1,0:T(8,128)(2,1)S(1)} %add_convert_fusion.2), channel_id=1, source_target_pairs={{0,4},{1,5},{2,6},{3,7},{4,0},{5,1},{6,2},{7,3},{8,12},{9,13},{10,... | collective-permute-start | bytes 786440 | tf_op jit(solution)/shard_map/ppermute | solution.py:35
  148.2 13.2 %collective-permute-start.42 = (bf16[128,1024]{1,0:T(8,128)(2,1)S(1)}, bf16[128,1024]{1,0:T(8,128)(2,1)S(1)}, u32[]{:S(2)}, u32[]{:S(2)}) collective-permute-start(bf16[128,1024]{1,0:T(8,128)(2,1)S(1)} %add_convert_fusion), channel_id=1, source_target_pairs={{0,3},{1,2},{2,1},{3,0},{4,7},{5,6},{6,5},{7,4},{8,11},{9,10},{10,... | collective-permute-start | bytes 786440 | tf_op jit(solution)/shard_map/ppermute | solution.py:35
Sparse Core Ops, SparseCore 0:
  15.8 60.8 all-gather.4
  87.5 56.2 all-gather.6

commit v15 on v13

--- a/solution.py
+++ b/solution.py
@@ -444,7 +444,7 @@
         send((last, 0), sums[last, 0], 2),
         start_far(1),
     )
-    run([(1, 1)], send((last, 1), sums[last, 1], 3), *homeward((0, 1)))
+    run([(1, 1)], send((last, 1), sums[last, 1], 3))
     shared = sums[last - 1, 0]
     for name in ((last - 1, 1), (last, 0), (last, 1)):
         shared += travel.pop(name).astype(jnp.float32)
@@ -452,7 +452,7 @@
     send("shared", shared, 2 * last - 2)
     sums[1, 1] = sums[1, 1].astype(jnp.bfloat16)
     both_sides = after(both_sides, sums[1, 1], shared)
-    homeward((1, 1))
+    homeward((0, 1), (1, 1))
     *terms, swapped_sides = join(sums[0, 0], *travel.values(), swap_cores(both_sides))
     both_sides = pltpu.with_memory_space_constraint(both_sides, pltpu.HBM)
     return project(group, terms, both_sides, swapped_sides)

time: 170 us -> 167 us (0.982)
  waiting for transfers between devices: 62.1 us -> 58.3 us
    ppermute x21, waiting for transfers between devices: 50.2 us -> 46.5 us  [swap_ep(): lax.ppermute(array, 'ep', [(i, i ^ mask) for i in range(lax.axis_size('ep...]
  transfers between devices with their start and end apart: 46 -> 46, of which waited for: 16 -> 18; matrix products, arithmetic and copies ran while one was open for 2% -> 2% of each run, Pallas kernels for 26% -> 26%
where the time goes in v15:
time: 167 us
  waiting for transfers between devices  58.3 us (35%)
  Pallas kernels  48.5 us (29%)
  starting transfers between devices  38.8 us (23%)
  between operations  13.7 us (8%)
  local copies, waits for them, and re-layouts  4.24 us (3%)
  other arithmetic  3 us (2%)
    ppermute x21, waiting for transfers between devices, swap_ep(): lax.ppermute(array, 'ep', [(i, i ^ mask) for i in range(lax.axis_size('ep...  46.5 us
    pallas_call x5, Pallas kernels, expert_apply(): pl.pallas_call(functools.partial(expert_kernel, positions, count), out_sh...  41.5 us
    ppermute x21, starting transfers between devices, swap_ep(): lax.ppermute(array, 'ep', [(i, i ^ mask) for i in range(lax.axis_size('ep...  31.3 us
    ppermute x2, waiting for transfers between devices, swap_reps(): lax.ppermute(array, 'rep', [(i, i ^ 1) for i in range(lax.axis_size('rep'...  6.83 us
    pallas_call x1, Pallas kernels, project(): pl.pallas_call(project_kernel, in_specs=[in_smem] + [in_vmem] * len(terms...  4.7 us
    ppermute x21, starting transfers between devices, swap_cores(): return lax.ppermute(array, 'grp', [(0, 1), (1, 0)])  4.32 us
    ppermute x21, waiting for transfers between devices, swap_cores(): return lax.ppermute(array, 'grp', [(0, 1), (1, 0)])  4.06 us
  transfers between devices with their start and end apart: 46, of which 18 were waited for; matrix products, arithmetic and copies ran while one was open for 2% of the time, Pallas kernels for 26%

profile of v15, /device:TPU:0, one launch (start us, length us, event | category | flops | bytes accessed | tf_op | source)
XLA Modules:
  0.0 166.6 jit_solution(16249517113041165167)
XLA Ops:
  6.5 1.2 copy-done
  7.8 0.7 constant_dynamic-slice_fusion
  8.6 1.1 constant_dynamic-slice_fusion.1
  9.6 3.1 %collective-permute-start = (bf16[128,1024]{1,0:T(8,128)(2,1)S(1)}, bf16[128,1024]{1,0:T(8,128)(2,1)S(1)}, u32[]{:S(2)}, u32[]{:S(2)}) collective-permute-start(bf16[128,1024]{1,0:T(8,128)(2,1)S(1)} %get-tuple-element.156.refs_2_), channel_id=1, source_target_pairs={{0,2},{1,3},{2,0},{3,1},{4,6},{5,7},{6,4},{7,5},{8,10},{9,11},{10,... | collective-permute-start | bytes 786440 | tf_op jit(solution)/shard_map/ppermute | solution.py:35
  12.7 1.5 collective-permute-start.4
  14.3 2.6 %collective-permute-start.2 = (bf16[128,1024]{1,0:T(8,128)(2,1)S(1)}, bf16[128,1024]{1,0:T(8,128)(2,1)S(1)}, u32[]{:S(2)}, u32[]{:S(2)}) collective-permute-start(bf16[128,1024]{1,0:T(8,128)(2,1)S(1)} %get-tuple-element.156.refs_2_), channel_id=1, source_target_pairs={{0,4},{1,5},{2,6},{3,7},{4,0},{5,1},{6,2},{7,3},{8,12},{9,13},{10,... | collective-permute-start | bytes 786440 | tf_op jit(solution)/shard_map/ppermute | solution.py:35
  16.9 1.2 copy-done.1
  18.1 0.8 split_columns.1
  19.0 1.6 collective-permute-start.5
  20.5 0.7 fusion.1
  21.2 2.5 %collective-permute-done.refs_6_ = bf16[128,1024]{1,0:T(8,128)(2,1)S(1)} collective-permute-done((bf16[128,1024]{1,0:T(8,128)(2,1)S(1)}, bf16[128,1024]{1,0:T(8,128)(2,1)S(1)}, u32[]{:S(2)}, u32[]{:S(2)}) %collective-permute-start) | collective-permute-done | bytes 262176 | tf_op jit(solution)/shard_map/ppermute | solution.py:35
  23.7 3.8 %collective-permute-start.1 = (bf16[128,1024]{1,0:T(8,128)(2,1)S(1)}, bf16[128,1024]{1,0:T(8,128)(2,1)S(1)}, u32[]{:S(2)}, u32[]{:S(2)}) collective-permute-start(bf16[128,1024]{1,0:T(8,128)(2,1)S(1)} %collective-permute-done.refs_6_), channel_id=1, source_target_pairs={{0,1},{1,0},{2,3},{3,2},{4,5},{5,4},{6,7},{7,6},{8,9},{9,8},{10,11... | collective-permute-start | bytes 786440 | tf_op jit(solution)/shard_map/ppermute | solution.py:35
  27.5 0.7 fusion
  28.2 0.7 select_reduce_fusion.weights
  28.9 4.1 %collective-permute-done.2.refs_10_ = bf16[128,1024]{1,0:T(8,128)(2,1)S(1)} collective-permute-done((bf16[128,1024]{1,0:T(8,128)(2,1)S(1)}, bf16[128,1024]{1,0:T(8,128)(2,1)S(1)}, u32[]{:S(2)}, u32[]{:S(2)}) %collective-permute-start.2) | collective-permute-done | bytes 262176 | tf_op jit(solution)/shard_map/ppermute | solution.py:35
  33.1 0.9 collective-permute-start.3
  34.5 7.3 %collective-permute-done.3.refs_2_ = bf16[128,1024]{1,0:T(8,128)(2,1)S(1)} collective-permute-done((bf16[128,1024]{1,0:T(8,128)(2,1)S(1)}, bf16[128,1024]{1,0:T(8,128)(2,1)S(1)}, u32[]{:S(2)}, u32[]{:S(2)}) %collective-permute-start.3) | collective-permute-done | bytes 262176 | tf_op jit(solution)/shard_map/ppermute | solution.py:35
  41.8 0.7 collective-permute-start.12
  43.5 10.0 %collective-permute-done.12.refs_3_ = bf16[128,1024]{1,0:T(8,128)(2,1)S(1)} collective-permute-done((bf16[128,1024]{1,0:T(8,128)(2,1)S(1)}, bf16[128,1024]{1,0:T(8,128)(2,1)S(1)}, u32[]{:S(2)}, u32[]{:S(2)}) %collective-permute-start.12) | collective-permute-done | bytes 262176 | tf_op jit(solution)/shard_map/ppermute | solution.py:35
  53.5 1.0 down_project.2.refs_6_
  55.5 1.6 collective-permute-start.15
  57.1 6.8 %collective-permute-done.15.arrived = bf16[128,1024]{1,0:T(8,128)(2,1)S(1)} collective-permute-done((bf16[128,1024]{1,0:T(8,128)(2,1)S(1)}, bf16[128,1024]{1,0:T(8,128)(2,1)S(1)}, u32[]{:S(2)}, u32[]{:S(2)}) %collective-permute-start.15) | collective-permute-done | bytes 262176 | tf_op jit(solution)/shard_map/ppermute | solution.py:31
  64.1 1.4 collective-permute-start.17
  65.6 6.4 %expert.5 = (bf16[128,1024]{1,0:T(8,128)(2,1)S(1)}, bf16[128,1024]{1,0:T(8,128)(2,1)S(1)}) custom-call(s32[1]{0:T(128)} %bitcast.1.where, bf16[144,1024]{1,0:T(8,128)(2,1)S(1)} %finish_latent.1.refs_0_, bf16[144,1024]{1,0:T(8,128)(2,1)S(1)} %collective-permute-done.16.refs_1_, bf16[1,1024,2048]{2,1,0:T(8,128)(2,1)} %refs_2_.3, ...), custom_call_target="tpu_custom_call" | custom-call | flops 805306368 | bytes 1048576 | tf_op jit(solution)/shard_map/expert/pallas_call | solution.py:257
  72.0 8.9 %collective-permute-done.18.refs_0_ = bf16[144,1024]{1,0:T(8,128)(2,1)S(1)} collective-permute-done((bf16[144,1024]{1,0:T(8,128)(2,1)S(1)}, bf16[144,1024]{1,0:T(8,128)(2,1)S(1)}, u32[]{:S(2)}, u32[]{:S(2)}) %collective-permute-start.18) | collective-permute-done | bytes 294944 | tf_op jit(solution)/shard_map/ppermute | solution.py:35
  81.6 1.6 collective-permute-start.23
  83.1 9.5 %expert.6 = (bf16[128,1024]{1,0:T(8,128)(2,1)S(1)}, bf16[128,1024]{1,0:T(8,128)(2,1)S(1)}, bf16[256,1024]{1,0:T(8,128)(2,1)S(1)}) custom-call(s32[1]{0:T(128)} %bitcast.1.where, bf16[144,1024]{1,0:T(8,128)(2,1)S(1)} %collective-permute-done.18.refs_0_, bf16[144,1024]{1,0:T(8,128)(2,1)S(1)} %collective-permute-done.17.refs_1_, ...), custom_call_target="tpu_custom_call" | custom-call | flops 1610612736 | bytes 2097152 | tf_op jit(solution)/shard_map/expert/pallas_call | solution.py:257
  92.8 1.6 collective-permute-start.29
  95.4 2.1 %collective-permute-start.27 = (bf16[128,1024]{1,0:T(8,128)(2,1)S(1)}, bf16[128,1024]{1,0:T(8,128)(2,1)S(1)}, u32[]{:S(2)}, u32[]{:S(2)}) collective-permute-start(bf16[128,1024]{1,0:T(8,128)(2,1)S(1)} %add_convert_fusion.6), channel_id=1, source_target_pairs={{0,2},{1,3},{2,0},{3,1},{4,6},{5,7},{6,4},{7,5},{8,10},{9,11},{10,... | collective-permute-start | bytes 786440 | tf_op jit(solution)/shard_map/ppermute | solution.py:35
  97.5 9.5 %expert.7 = (bf16[128,1024]{1,0:T(8,128)(2,1)S(1)}, bf16[128,1024]{1,0:T(8,128)(2,1)S(1)}, bf16[256,1024]{1,0:T(8,128)(2,1)S(1)}) custom-call(s32[1]{0:T(128)} %bitcast.1.where, bf16[144,1024]{1,0:T(8,128)(2,1)S(1)} %collective-permute-done.22.refs_0_, bf16[144,1024]{1,0:T(8,128)(2,1)S(1)} %collective-permute-done.23.refs_1_, ...), custom_call_target="tpu_custom_call" | custom-call | flops 1610612736 | bytes 2097152 | tf_op jit(solution)/shard_map/expert/pallas_call | solution.py:257
  107.0 1.4 collective-permute-done.28.refs_0_
  108.5 1.5 collective-permute-start.35
  110.7 2.0 %collective-permute-start.34 = (bf16[128,1024]{1,0:T(8,128)(2,1)S(1)}, bf16[128,1024]{1,0:T(8,128)(2,1)S(1)}, u32[]{:S(2)}, u32[]{:S(2)}) collective-permute-start(bf16[128,1024]{1,0:T(8,128)(2,1)S(1)} %get-tuple-element.159), channel_id=1, source_target_pairs={{0,2},{1,3},{2,0},{3,1},{4,6},{5,7},{6,4},{7,5},{8,10},{9,11},{10,... | collective-permute-start | bytes 786440 | tf_op jit(solution)/shard_map/ppermute | solution.py:35
  113.3 9.7 %expert.8 = (bf16[128,1024]{1,0:T(8,128)(2,1)S(1)}, bf16[128,1024]{1,0:T(8,128)(2,1)S(1)}, bf16[256,1024]{1,0:T(8,128)(2,1)S(1)}) custom-call(s32[1]{0:T(128)} %bitcast.1.where, bf16[144,1024]{1,0:T(8,128)(2,1)S(1)} %collective-permute-done.28.refs_0_, bf16[144,1024]{1,0:T(8,128)(2,1)S(1)} %collective-permute-done.29.refs_1_, ...), custom_call_target="tpu_custom_call" | custom-call | flops 1610612736 | bytes 2097152 | tf_op jit(solution)/shard_map/expert/pallas_call | solution.py:257
  124.0 1.4 collective-permute-done.37
  125.6 2.0 %collective-permute-start.38 = (bf16[128,1024]{1,0:T(8,128)(2,1)S(1)}, bf16[128,1024]{1,0:T(8,128)(2,1)S(1)}, u32[]{:S(2)}, u32[]{:S(2)}) collective-permute-start(bf16[128,1024]{1,0:T(8,128)(2,1)S(1)} %get-tuple-element.158), channel_id=1, source_target_pairs={{0,3},{1,2},{2,1},{3,0},{4,7},{5,6},{6,5},{7,4},{8,11},{9,10},{10,... | collective-permute-start | bytes 786440 | tf_op jit(solution)/shard_map/ppermute | solution.py:35
  127.6 6.4 %expert.9 = (bf16[128,1024]{1,0:T(8,128)(2,1)S(1)}, bf16[128,1024]{1,0:T(8,128)(2,1)S(1)}) custom-call(s32[1]{0:T(128)} %bitcast.1.where, bf16[144,1024]{1,0:T(8,128)(2,1)S(1)} %collective-permute-done.35.refs_0_, bf16[144,1024]{1,0:T(8,128)(2,1)S(1)} %collective-permute-done.36.refs_1_, bf16[1,1024,2048]{2,1,0:T(8,128)(2,1)} %refs_2_.3, ...), custom_call_target="tpu_custom_call" | custom-call | flops 805306368 | bytes 1048576 | tf_op jit(solution)/shard_map/expert/pallas_call | solution.py:257
  134.0 0.9 collective-permute-done.38
  135.2 1.3 collective-permute-done.41
  136.6 0.9 all-gather.7.cloned.1.call-done
  137.9 1.5 collective-permute-start.40
  139.4 2.4 %collective-permute-start.39 = (bf16[128,1024]{1,0:T(8,128)(2,1)S(1)}, bf16[128,1024]{1,0:T(8,128)(2,1)S(1)}, u32[]{:S(2)}, u32[]{:S(2)}) collective-permute-start(bf16[128,1024]{1,0:T(8,128)(2,1)S(1)} %add_convert_fusion.2), channel_id=1, source_target_pairs={{0,4},{1,5},{2,6},{3,7},{4,0},{5,1},{6,2},{7,3},{8,12},{9,13},{10,... | collective-permute-start | bytes 786440 | tf_op jit(solution)/shard_map/ppermute | solution.py:35
  141.8 1.5 collective-permute-start.42
  143.3 0.8 collective-permute-done.19
  144.1 6.6 %collective-permute-done.40.refs_3_ = bf16[128,1024]{1,0:T(8,128)(2,1)S(1)} collective-permute-done((bf16[128,1024]{1,0:T(8,128)(2,1)S(1)}, bf16[128,1024]{1,0:T(8,128)(2,1)S(1)}, u32[]{:S(2)}, u32[]{:S(2)}) %collective-permute-start.40) | collective-permute-done | bytes 262176 | tf_op jit(solution)/shard_map/ppermute | solution.py:35
  150.7 3.3 %collective-permute-done.39.refs_2_ = bf16[128,1024]{1,0:T(8,128)(2,1)S(1)} collective-permute-done((bf16[128,1024]{1,0:T(8,128)(2,1)S(1)}, bf16[128,1024]{1,0:T(8,128)(2,1)S(1)}, u32[]{:S(2)}, u32[]{:S(2)}) %collective-permute-start.39) | collective-permute-done | bytes 262176 | tf_op jit(solution)/shard_map/ppermute | solution.py:35
  154.0 1.1 collective-permute-done.42.refs_4_
  155.0 4.7 %project.1 = bf16[128,4096]{1,0:T(8,128)(2,1)} custom-call(s32[1]{0:T(128)} %bitcast.where, f32[128,1024]{1,0:T(8,128)S(1)} %convert_add_fusion.refs_0_, bf16[128,1024]{1,0:T(8,128)(2,1)S(1)} %collective-permute-done.27.refs_1_, bf16[128,1024]{1,0:T(8,128)(2,1)S(1)} %collective-permute-done.39.refs_2_, ...), custom_call_target="tpu_custom_call" | custom-call | flops 1073741824 | bytes 8388608 | tf_op jit(solution)/shard_map/project/pallas_call | solution.py:319
  (72 shorter events, 8.0 us)
Async XLA Ops:
  6.5 1.2 copy-start
  6.5 74.4 %all-gather.5.cloned.1.call-start = ((), (), s32[]{:S(2)}) async-start(), calls=%async_computation | async-start | bytes 2359296 | tf_op jit(solution)/shard_map/all_gather | solution.py:369
  8.5 128.9 %all-gather.7.cloned.1.call-start = ((), (), s32[]{:S(2)}) async-start(), calls=%async_computation.1 | async-start | bytes 6291456 | tf_op jit(solution)/shard_map/all_gather | solution.py:432
  9.6 14.1 %collective-permute-start = (bf16[128,1024]{1,0:T(8,128)(2,1)S(1)}, bf16[128,1024]{1,0:T(8,128)(2,1)S(1)}, u32[]{:S(2)}, u32[]{:S(2)}) collective-permute-start(bf16[128,1024]{1,0:T(8,128)(2,1)S(1)} %get-tuple-element.156.refs_2_), channel_id=1, source_target_pairs={{0,2},{1,3},{2,0},{3,1},{4,6},{5,7},{6,4},{7,5},{8,10},{9,11},{10,... | collective-permute-start | bytes 786440 | tf_op jit(solution)/shard_map/ppermute | solution.py:35
  12.7 21.3 %collective-permute-start.4 = (bf16[128,1024]{1,0:T(8,128)(2,1)S(1)}, bf16[128,1024]{1,0:T(8,128)(2,1)S(1)}, u32[]{:S(2)}, u32[]{:S(2)}) collective-permute-start(bf16[128,1024]{1,0:T(8,128)(2,1)S(1)} %get-tuple-element.156.refs_2_), channel_id=1, source_target_pairs={{0,1},{1,0},{2,3},{3,2},{4,5},{5,4},{6,7},{7,6},{8,9},{9,8},{10,11... | collective-permute-start | bytes 786440 | tf_op jit(solution)/shard_map/ppermute | solution.py:35
  14.3 18.8 %collective-permute-start.2 = (bf16[128,1024]{1,0:T(8,128)(2,1)S(1)}, bf16[128,1024]{1,0:T(8,128)(2,1)S(1)}, u32[]{:S(2)}, u32[]{:S(2)}) collective-permute-start(bf16[128,1024]{1,0:T(8,128)(2,1)S(1)} %get-tuple-element.156.refs_2_), channel_id=1, source_target_pairs={{0,4},{1,5},{2,6},{3,7},{4,0},{5,1},{6,2},{7,3},{8,12},{9,13},{10,... | collective-permute-start | bytes 786440 | tf_op jit(solution)/shard_map/ppermute | solution.py:35
  16.9 1.2 copy-start.1
  19.0 15.5 %collective-permute-start.5 = (bf16[128,2048]{1,0:T(8,128)(2,1)S(1)}, bf16[128,2048]{1,0:T(8,128)(2,1)S(1)}, u32[]{:S(2)}, u32[]{:S(2)}) collective-permute-start(bf16[128,2048]{1,0:T(8,128)(2,1)S(1)} %get-tuple-element.85), channel_id=1, source_target_pairs={{0,16},{16,0},{1,17},{17,1},{2,18},{18,2},{3,19},{19,3},{4,20},{20... | collective-permute-start | bytes 1572872 | tf_op jit(solution)/shard_map/ppermute | solution.py:31
  23.7 9.3 %collective-permute-start.1 = (bf16[128,1024]{1,0:T(8,128)(2,1)S(1)}, bf16[128,1024]{1,0:T(8,128)(2,1)S(1)}, u32[]{:S(2)}, u32[]{:S(2)}) collective-permute-start(bf16[128,1024]{1,0:T(8,128)(2,1)S(1)} %collective-permute-done.refs_6_), channel_id=1, source_target_pairs={{0,1},{1,0},{2,3},{3,2},{4,5},{5,4},{6,7},{7,6},{8,9},{9,8},{10,11... | collective-permute-start | bytes 786440 | tf_op jit(solution)/shard_map/ppermute | solution.py:35
  33.1 8.8 %collective-permute-start.3 = (bf16[128,1024]{1,0:T(8,128)(2,1)S(1)}, bf16[128,1024]{1,0:T(8,128)(2,1)S(1)}, u32[]{:S(2)}, u32[]{:S(2)}) collective-permute-start(bf16[128,1024]{1,0:T(8,128)(2,1)S(1)} %collective-permute-done.2.refs_10_), channel_id=1, source_target_pairs={{0,2},{1,3},{2,0},{3,1},{4,6},{5,7},{6,4},{7,5},{8,10},{9,11},{10,... | collective-permute-start | bytes 786440 | tf_op jit(solution)/shard_map/ppermute | solution.py:35
  34.0 8.5 %collective-permute-start.9 = (bf16[128,1024]{1,0:T(8,128)(2,1)S(1)}, bf16[128,1024]{1,0:T(8,128)(2,1)S(1)}, u32[]{:S(2)}, u32[]{:S(2)}) collective-permute-start(bf16[128,1024]{1,0:T(8,128)(2,1)S(1)} %collective-permute-done.2.refs_10_), channel_id=1, source_target_pairs={{0,1},{1,0},{2,3},{3,2},{4,5},{5,4},{6,7},{7,6},{8,9},{9,8},{10,11... | collective-permute-start | bytes 786440 | tf_op jit(solution)/shard_map/ppermute | solution.py:35
  34.0 9.0 %collective-permute-start.7 = (bf16[128,1024]{1,0:T(8,128)(2,1)S(1)}, bf16[128,1024]{1,0:T(8,128)(2,1)S(1)}, u32[]{:S(2)}, u32[]{:S(2)}) collective-permute-start(bf16[128,1024]{1,0:T(8,128)(2,1)S(1)} %collective-permute-done.refs_6_), channel_id=1, source_target_pairs={{0,8},{8,0},{1,9},{9,1},{2,10},{10,2},{3,11},{11,3},{4,12},{12,4},... | collective-permute-start | bytes 786440 | tf_op jit(solution)/shard_map/ppermute | solution.py:27
  34.0 9.1 %collective-permute-start.8 = (bf16[128,1024]{1,0:T(8,128)(2,1)S(1)}, bf16[128,1024]{1,0:T(8,128)(2,1)S(1)}, u32[]{:S(2)}, u32[]{:S(2)}) collective-permute-start(bf16[128,1024]{1,0:T(8,128)(2,1)S(1)} %collective-permute-done.1.refs_7_), channel_id=1, source_target_pairs={{0,8},{8,0},{1,9},{9,1},{2,10},{10,2},{3,11},{11,3},{4,12},{12,4},... | collective-permute-start | bytes 786440 | tf_op jit(solution)/shard_map/ppermute | solution.py:27
  41.8 11.7 %collective-permute-start.12 = (bf16[128,1024]{1,0:T(8,128)(2,1)S(1)}, bf16[128,1024]{1,0:T(8,128)(2,1)S(1)}, u32[]{:S(2)}, u32[]{:S(2)}) collective-permute-start(bf16[128,1024]{1,0:T(8,128)(2,1)S(1)} %collective-permute-done.3.refs_2_), channel_id=1, source_target_pairs={{0,1},{1,0},{2,3},{3,2},{4,5},{5,4},{6,7},{7,6},{8,9},{9,8},{10,11... | collective-permute-start | bytes 786440 | tf_op jit(solution)/shard_map/ppermute | solution.py:35
  42.5 11.0 %collective-permute-start.10 = (bf16[128,1024]{1,0:T(8,128)(2,1)S(1)}, bf16[128,1024]{1,0:T(8,128)(2,1)S(1)}, u32[]{:S(2)}, u32[]{:S(2)}) collective-permute-start(bf16[128,1024]{1,0:T(8,128)(2,1)S(1)} %collective-permute-done.2.refs_10_), channel_id=1, source_target_pairs={{0,8},{8,0},{1,9},{9,1},{2,10},{10,2},{3,11},{11,3},{4,12},{12,4},... | collective-permute-start | bytes 786440 | tf_op jit(solution)/shard_map/ppermute | solution.py:27
  42.5 11.0 %collective-permute-start.11 = (bf16[128,1024]{1,0:T(8,128)(2,1)S(1)}, bf16[128,1024]{1,0:T(8,128)(2,1)S(1)}, u32[]{:S(2)}, u32[]{:S(2)}) collective-permute-start(bf16[128,1024]{1,0:T(8,128)(2,1)S(1)} %collective-permute-done.9.refs_11_), channel_id=1, source_target_pairs={{0,8},{8,0},{1,9},{9,1},{2,10},{10,2},{3,11},{11,3},{4,12},{12,4},... | collective-permute-start | bytes 786440 | tf_op jit(solution)/shard_map/ppermute | solution.py:27
  43.0 10.5 %collective-permute-start.6 = (bf16[128,1024]{1,0:T(8,128)(2,1)S(1)}, bf16[128,1024]{1,0:T(8,128)(2,1)S(1)}, u32[]{:S(2)}, u32[]{:S(2)}) collective-permute-start(bf16[128,1024]{1,0:T(8,128)(2,1)S(1)} %collective-permute-done.4.refs_3_), channel_id=1, source_target_pairs={{0,8},{8,0},{1,9},{9,1},{2,10},{10,2},{3,11},{11,3},{4,12},{12,4},... | collective-permute-start | bytes 786440 | tf_op jit(solution)/shard_map/ppermute | solution.py:27
  43.1 11.4 %collective-permute-start.13 = (bf16[128,1024]{1,0:T(8,128)(2,1)S(1)}, bf16[128,1024]{1,0:T(8,128)(2,1)S(1)}, u32[]{:S(2)}, u32[]{:S(2)}) collective-permute-start(bf16[128,1024]{1,0:T(8,128)(2,1)S(1)} %collective-permute-done.3.refs_2_), channel_id=1, source_target_pairs={{0,8},{8,0},{1,9},{9,1},{2,10},{10,2},{3,11},{11,3},{4,12},{12,4},... | collective-permute-start | bytes 786440 | tf_op jit(solution)/shard_map/ppermute | solution.py:27
  53.5 1.5 collective-permute-start.14
  55.5 8.4 %collective-permute-start.15 = (bf16[128,1024]{1,0:T(8,128)(2,1)S(1)}, bf16[128,1024]{1,0:T(8,128)(2,1)S(1)}, u32[]{:S(2)}, u32[]{:S(2)}) collective-permute-start(bf16[128,1024]{1,0:T(8,128)(2,1)S(1)} %get-tuple-element.92), channel_id=1, source_target_pairs={{0,16},{16,0},{1,17},{17,1},{2,18},{18,2},{3,19},{19,3},{4,20},{20... | collective-permute-start | bytes 786440 | tf_op jit(solution)/shard_map/ppermute | solution.py:31
  64.0 1.6 collective-permute-start.16
  64.0 16.9 %collective-permute-start.18 = (bf16[144,1024]{1,0:T(8,128)(2,1)S(1)}, bf16[144,1024]{1,0:T(8,128)(2,1)S(1)}, u32[]{:S(2)}, u32[]{:S(2)}) collective-permute-start(bf16[144,1024]{1,0:T(8,128)(2,1)S(1)} %finish_latent.1.refs_0_), channel_id=1, source_target_pairs={{0,4},{1,5},{2,6},{3,7},{4,0},{5,1},{6,2},{7,3},{8,12},{9,13},{10,... | collective-permute-start | bytes 884744 | tf_op jit(solution)/shard_map/ppermute | solution.py:35
  64.1 16.8 %collective-permute-start.17 = (bf16[144,1024]{1,0:T(8,128)(2,1)S(1)}, bf16[144,1024]{1,0:T(8,128)(2,1)S(1)}, u32[]{:S(2)}, u32[]{:S(2)}) collective-permute-start(bf16[144,1024]{1,0:T(8,128)(2,1)S(1)} %finish_latent.1.refs_0_), channel_id=1, source_target_pairs={{0,2},{1,3},{2,0},{3,1},{4,6},{5,7},{6,4},{7,5},{8,10},{9,11},{10,... | collective-permute-start | bytes 884744 | tf_op jit(solution)/shard_map/ppermute | solution.py:35
  81.0 2.2 %collective-permute-start.21 = (bf16[144,1024]{1,0:T(8,128)(2,1)S(1)}, bf16[144,1024]{1,0:T(8,128)(2,1)S(1)}, u32[]{:S(2)}, u32[]{:S(2)}) collective-permute-start(bf16[144,1024]{1,0:T(8,128)(2,1)S(1)} %collective-permute-done.17.refs_1_), channel_id=1, source_target_pairs={{0,8},{8,0},{1,9},{9,1},{2,10},{10,2},{3,11},{11,3},{4,12},{12,4},... | collective-permute-start | bytes 884744 | tf_op jit(solution)/shard_map/ppermute | solution.py:27
  81.1 2.1 %collective-permute-start.20 = (bf16[144,1024]{1,0:T(8,128)(2,1)S(1)}, bf16[144,1024]{1,0:T(8,128)(2,1)S(1)}, u32[]{:S(2)}, u32[]{:S(2)}) collective-permute-start(bf16[144,1024]{1,0:T(8,128)(2,1)S(1)} %collective-permute-done.18.refs_0_), channel_id=1, source_target_pairs={{0,8},{8,0},{1,9},{9,1},{2,10},{10,2},{3,11},{11,3},{4,12},{12,4},... | collective-permute-start | bytes 884744 | tf_op jit(solution)/shard_map/ppermute | solution.py:27
  81.6 11.1 %collective-permute-start.23 = (bf16[144,1024]{1,0:T(8,128)(2,1)S(1)}, bf16[144,1024]{1,0:T(8,128)(2,1)S(1)}, u32[]{:S(2)}, u32[]{:S(2)}) collective-permute-start(bf16[144,1024]{1,0:T(8,128)(2,1)S(1)} %collective-permute-done.18.refs_0_), channel_id=1, source_target_pairs={{0,1},{1,0},{2,3},{3,2},{4,5},{5,4},{6,7},{7,6},{8,9},{9,8},{10,11... | collective-permute-start | bytes 884744 | tf_op jit(solution)/shard_map/ppermute | solution.py:35
  83.1 9.5 %collective-permute-start.22 = (bf16[144,1024]{1,0:T(8,128)(2,1)S(1)}, bf16[144,1024]{1,0:T(8,128)(2,1)S(1)}, u32[]{:S(2)}, u32[]{:S(2)}) collective-permute-start(bf16[144,1024]{1,0:T(8,128)(2,1)S(1)} %collective-permute-done.18.refs_0_), channel_id=1, source_target_pairs={{0,2},{1,3},{2,0},{3,1},{4,6},{5,7},{6,4},{7,5},{8,10},{9,11},{10,... | collective-permute-start | bytes 884744 | tf_op jit(solution)/shard_map/ppermute | solution.py:35
  92.7 2.7 %collective-permute-start.26 = (bf16[256,1024]{1,0:T(8,128)(2,1)S(1)}, bf16[256,1024]{1,0:T(8,128)(2,1)S(1)}, u32[]{:S(2)}, u32[]{:S(2)}) collective-permute-start(bf16[256,1024]{1,0:T(8,128)(2,1)S(1)} %get-tuple-element.119), channel_id=1, source_target_pairs={{0,8},{8,0},{1,9},{9,1},{2,10},{10,2},{3,11},{11,3},{4,12},{12,4},... | collective-permute-start | bytes 1572872 | tf_op jit(solution)/shard_map/ppermute | solution.py:27
  92.8 14.3 %collective-permute-start.29 = (bf16[144,1024]{1,0:T(8,128)(2,1)S(1)}, bf16[144,1024]{1,0:T(8,128)(2,1)S(1)}, u32[]{:S(2)}, u32[]{:S(2)}) collective-permute-start(bf16[144,1024]{1,0:T(8,128)(2,1)S(1)} %finish_latent.1.refs_0_), channel_id=1, source_target_pairs={{0,1},{1,0},{2,3},{3,2},{4,5},{5,4},{6,7},{7,6},{8,9},{9,8},{10,11... | collective-permute-start | bytes 884744 | tf_op jit(solution)/shard_map/ppermute | solution.py:35
  94.4 14.1 %collective-permute-start.28 = (bf16[144,1024]{1,0:T(8,128)(2,1)S(1)}, bf16[144,1024]{1,0:T(8,128)(2,1)S(1)}, u32[]{:S(2)}, u32[]{:S(2)}) collective-permute-start(bf16[144,1024]{1,0:T(8,128)(2,1)S(1)} %collective-permute-done.22.refs_0_), channel_id=1, source_target_pairs={{0,1},{1,0},{2,3},{3,2},{4,5},{5,4},{6,7},{7,6},{8,9},{9,8},{10,11... | collective-permute-start | bytes 884744 | tf_op jit(solution)/shard_map/ppermute | solution.py:35
  94.8 2.7 %collective-permute-start.24 = (bf16[144,1024]{1,0:T(8,128)(2,1)S(1)}, bf16[144,1024]{1,0:T(8,128)(2,1)S(1)}, u32[]{:S(2)}, u32[]{:S(2)}) collective-permute-start(bf16[144,1024]{1,0:T(8,128)(2,1)S(1)} %collective-permute-done.22.refs_0_), channel_id=1, source_target_pairs={{0,8},{8,0},{1,9},{9,1},{2,10},{10,2},{3,11},{11,3},{4,12},{12,4},... | collective-permute-start | bytes 884744 | tf_op jit(solution)/shard_map/ppermute | solution.py:27
  94.8 2.7 %collective-permute-start.25 = (bf16[144,1024]{1,0:T(8,128)(2,1)S(1)}, bf16[144,1024]{1,0:T(8,128)(2,1)S(1)}, u32[]{:S(2)}, u32[]{:S(2)}) collective-permute-start(bf16[144,1024]{1,0:T(8,128)(2,1)S(1)} %collective-permute-done.23.refs_1_), channel_id=1, source_target_pairs={{0,8},{8,0},{1,9},{9,1},{2,10},{10,2},{3,11},{11,3},{4,12},{12,4},... | collective-permute-start | bytes 884744 | tf_op jit(solution)/shard_map/ppermute | solution.py:27
  95.4 13.1 %collective-permute-start.27 = (bf16[128,1024]{1,0:T(8,128)(2,1)S(1)}, bf16[128,1024]{1,0:T(8,128)(2,1)S(1)}, u32[]{:S(2)}, u32[]{:S(2)}) collective-permute-start(bf16[128,1024]{1,0:T(8,128)(2,1)S(1)} %add_convert_fusion.6), channel_id=1, source_target_pairs={{0,2},{1,3},{2,0},{3,1},{4,6},{5,7},{6,4},{7,5},{8,10},{9,11},{10,... | collective-permute-start | bytes 786440 | tf_op jit(solution)/shard_map/ppermute | solution.py:35
  108.5 2.0 %collective-permute-start.32 = (bf16[256,1024]{1,0:T(8,128)(2,1)S(1)}, bf16[256,1024]{1,0:T(8,128)(2,1)S(1)}, u32[]{:S(2)}, u32[]{:S(2)}) collective-permute-start(bf16[256,1024]{1,0:T(8,128)(2,1)S(1)} %get-tuple-element.132), channel_id=1, source_target_pairs={{0,8},{8,0},{1,9},{9,1},{2,10},{10,2},{3,11},{11,3},{4,12},{12,4},... | collective-permute-start | bytes 1572872 | tf_op jit(solution)/shard_map/ppermute | solution.py:27
  108.5 14.6 %collective-permute-start.35 = (bf16[144,1024]{1,0:T(8,128)(2,1)S(1)}, bf16[144,1024]{1,0:T(8,128)(2,1)S(1)}, u32[]{:S(2)}, u32[]{:S(2)}) collective-permute-start(bf16[144,1024]{1,0:T(8,128)(2,1)S(1)} %collective-permute-done.17.refs_1_), channel_id=1, source_target_pairs={{0,1},{1,0},{2,3},{3,2},{4,5},{5,4},{6,7},{7,6},{8,9},{9,8},{10,11... | collective-permute-start | bytes 884744 | tf_op jit(solution)/shard_map/ppermute | solution.py:35
  110.0 3.4 %collective-permute-start.30 = (bf16[144,1024]{1,0:T(8,128)(2,1)S(1)}, bf16[144,1024]{1,0:T(8,128)(2,1)S(1)}, u32[]{:S(2)}, u32[]{:S(2)}) collective-permute-start(bf16[144,1024]{1,0:T(8,128)(2,1)S(1)} %collective-permute-done.28.refs_0_), channel_id=1, source_target_pairs={{0,8},{8,0},{1,9},{9,1},{2,10},{10,2},{3,11},{11,3},{4,12},{12,4},... | collective-permute-start | bytes 884744 | tf_op jit(solution)/shard_map/ppermute | solution.py:27
  110.2 3.1 %collective-permute-start.31 = (bf16[144,1024]{1,0:T(8,128)(2,1)S(1)}, bf16[144,1024]{1,0:T(8,128)(2,1)S(1)}, u32[]{:S(2)}, u32[]{:S(2)}) collective-permute-start(bf16[144,1024]{1,0:T(8,128)(2,1)S(1)} %collective-permute-done.29.refs_1_), channel_id=1, source_target_pairs={{0,8},{8,0},{1,9},{9,1},{2,10},{10,2},{3,11},{11,3},{4,12},{12,4},... | collective-permute-start | bytes 884744 | tf_op jit(solution)/shard_map/ppermute | solution.py:27
  110.7 12.4 %collective-permute-start.34 = (bf16[128,1024]{1,0:T(8,128)(2,1)S(1)}, bf16[128,1024]{1,0:T(8,128)(2,1)S(1)}, u32[]{:S(2)}, u32[]{:S(2)}) collective-permute-start(bf16[128,1024]{1,0:T(8,128)(2,1)S(1)} %get-tuple-element.159), channel_id=1, source_target_pairs={{0,2},{1,3},{2,0},{3,1},{4,6},{5,7},{6,4},{7,5},{8,10},{9,11},{10,... | collective-permute-start | bytes 786440 | tf_op jit(solution)/shard_map/ppermute | solution.py:35
  112.7 10.8 %collective-permute-start.33 = (bf16[128,1024]{1,0:T(8,128)(2,1)S(1)}, bf16[128,1024]{1,0:T(8,128)(2,1)S(1)}, u32[]{:S(2)}, u32[]{:S(2)}) collective-permute-start(bf16[128,1024]{1,0:T(8,128)(2,1)S(1)} %get-tuple-element.160), channel_id=1, source_target_pairs={{0,1},{1,0},{2,3},{3,2},{4,5},{5,4},{6,7},{7,6},{8,9},{9,8},{10,11... | collective-permute-start | bytes 786440 | tf_op jit(solution)/shard_map/ppermute | solution.py:35
  123.5 1.9 %collective-permute-start.37 = (bf16[256,1024]{1,0:T(8,128)(2,1)S(1)}, bf16[256,1024]{1,0:T(8,128)(2,1)S(1)}, u32[]{:S(2)}, u32[]{:S(2)}) collective-permute-start(bf16[256,1024]{1,0:T(8,128)(2,1)S(1)} %get-tuple-element.142), channel_id=1, source_target_pairs={{0,8},{8,0},{1,9},{9,1},{2,10},{10,2},{3,11},{11,3},{4,12},{12,4},... | collective-permute-start | bytes 1572872 | tf_op jit(solution)/shard_map/ppermute | solution.py:27
  123.5 4.1 %collective-permute-start.36 = (bf16[144,1024]{1,0:T(8,128)(2,1)S(1)}, bf16[144,1024]{1,0:T(8,128)(2,1)S(1)}, u32[]{:S(2)}, u32[]{:S(2)}) collective-permute-start(bf16[144,1024]{1,0:T(8,128)(2,1)S(1)} %collective-permute-done.35.refs_0_), channel_id=1, source_target_pairs={{0,8},{8,0},{1,9},{9,1},{2,10},{10,2},{3,11},{11,3},{4,12},{12,4},... | collective-permute-start | bytes 884744 | tf_op jit(solution)/shard_map/ppermute | solution.py:27
  125.6 9.3 %collective-permute-start.38 = (bf16[128,1024]{1,0:T(8,128)(2,1)S(1)}, bf16[128,1024]{1,0:T(8,128)(2,1)S(1)}, u32[]{:S(2)}, u32[]{:S(2)}) collective-permute-start(bf16[128,1024]{1,0:T(8,128)(2,1)S(1)} %get-tuple-element.158), channel_id=1, source_target_pairs={{0,3},{1,2},{2,1},{3,0},{4,7},{5,6},{6,5},{7,4},{8,11},{9,10},{10,... | collective-permute-start | bytes 786440 | tf_op jit(solution)/shard_map/ppermute | solution.py:35
  135.0 1.5 collective-permute-start.41
  137.4 17.6 %collective-permute-start.43 = (bf16[2,8,256,512]{3,2,1,0:T(8,128)(2,1)}, bf16[2,8,256,512]{3,2,1,0:T(8,128)(2,1)S(1)}, u32[]{:S(2)}, u32[]{:S(2)}) collective-permute-start(bf16[2,8,256,512]{3,2,1,0:T(8,128)(2,1)} %bitcast.6), channel_id=1, source_target_pairs={{0,8},{8,0},{1,9},{9,1},{2,10},{10,2},{3,11},{11,3},{4,12},{12,4},... | collective-permute-start | bytes 12582920 | tf_op jit(solution)/shard_map/ppermute | solution.py:27
  137.4 6.6 %collective-permute-start.19 = (bf16[128,1024]{1,0:T(8,128)(2,1)S(1)}, bf16[128,1024]{1,0:T(8,128)(2,1)S(1)}, u32[]{:S(2)}, u32[]{:S(2)}) collective-permute-start(bf16[128,1024]{1,0:T(8,128)(2,1)S(1)} %get-tuple-element.99), channel_id=1, source_target_pairs={{0,8},{8,0},{1,9},{9,1},{2,10},{10,2},{3,11},{11,3},{4,12},{12,4},... | collective-permute-start | bytes 786440 | tf_op jit(solution)/shard_map/ppermute | solution.py:27
  137.9 12.8 %collective-permute-start.40 = (bf16[128,1024]{1,0:T(8,128)(2,1)S(1)}, bf16[128,1024]{1,0:T(8,128)(2,1)S(1)}, u32[]{:S(2)}, u32[]{:S(2)}) collective-permute-start(bf16[128,1024]{1,0:T(8,128)(2,1)S(1)} %get-tuple-element.157), channel_id=1, source_target_pairs={{0,1},{1,0},{2,3},{3,2},{4,5},{5,4},{6,7},{7,6},{8,9},{9,8},{10,11... | collective-permute-start | bytes 786440 | tf_op jit(solution)/shard_map/ppermute | solution.py:35
  139.4 14.6 %collective-permute-start.39 = (bf16[128,1024]{1,0:T(8,128)(2,1)S(1)}, bf16[128,1024]{1,0:T(8,128)(2,1)S(1)}, u32[]{:S(2)}, u32[]{:S(2)}) collective-permute-start(bf16[128,1024]{1,0:T(8,128)(2,1)S(1)} %add_convert_fusion.2), channel_id=1, source_target_pairs={{0,4},{1,5},{2,6},{3,7},{4,0},{5,1},{6,2},{7,3},{8,12},{9,13},{10,... | collective-permute-start | bytes 786440 | tf_op jit(solution)/shard_map/ppermute | solution.py:35
  141.8 13.2 %collective-permute-start.42 = (bf16[128,1024]{1,0:T(8,128)(2,1)S(1)}, bf16[128,1024]{1,0:T(8,128)(2,1)S(1)}, u32[]{:S(2)}, u32[]{:S(2)}) collective-permute-start(bf16[128,1024]{1,0:T(8,128)(2,1)S(1)} %add_convert_fusion), channel_id=1, source_target_pairs={{0,3},{1,2},{2,1},{3,0},{4,7},{5,6},{6,5},{7,4},{8,11},{9,10},{10,... | collective-permute-start | bytes 786440 | tf_op jit(solution)/shard_map/ppermute | solution.py:35
Sparse Core Ops, SparseCore 0:
  9.5 60.4 all-gather.4
  81.1 56.2 all-gather.6

commit v16 on v15

--- a/solution.py
+++ b/solution.py
@@ -277,8 +277,8 @@
 
 
 def project_kernel(where, *refs):
-    terms, refs = refs[:-8], refs[-8:]
-    mine, swapped, layer_out, combined, held, blocks, read_sems, sems = refs
+    terms, refs = refs[:-9], refs[-9:]
+    mine, swapped, layer_out, in_order, combined, held, blocks, read_sems, sems = refs
     sides, ep_count, inner, width = mine.shape
 
     def read(e, side):
@@ -292,21 +292,25 @@
     total = terms[0][...].astype(jnp.float32)
     for term in terms[1:]:
         total += term[...].astype(jnp.float32)
-    combined[...] = total.astype(jnp.bfloat16)
+    in_order[...] = total.astype(jnp.bfloat16)
+    for side in range(sides):
+        for i, core in enumerate((1 - where[0], where[0])):
+            start = pl.multiple_of((2 * side + core) * inner, inner)
+            to = pl.ds((2 * side + i) * inner, inner)
+            combined[:, to] = in_order[:, pl.ds(start, inner)]
 
     def sent(e):
         columns = pl.ds(e * width, width)
         return pltpu.make_async_copy(blocks.at[:, columns], layer_out.at[:, columns], sems.at[e])
 
     for e in range(ep_count):
-        value = 0.0
+        rows = []
         for side in range(sides):
             read(e, side).wait()
-            for core, array in ((1 - where[0], swapped), (where[0], held)):
-                columns = pl.ds(pl.multiple_of((2 * side + core) * inner, inner), inner)
-                value += jnp.dot(
-                    combined[:, columns], array[side, e], preferred_element_type=jnp.float32
-                )
+            rows += [swapped[side, e], held[side, e]]
+        value = jnp.dot(
+            combined[...], jnp.concatenate(rows, axis=0), preferred_element_type=jnp.float32
+        )
         blocks[:, e * width : (e + 1) * width] = value.astype(jnp.bfloat16)
         sent(e).start()
     for e in range(ep_count):
@@ -322,6 +326,7 @@
         out_specs=anywhere,
         out_shape=jax.ShapeDtypeStruct((count, ep_count * width), jnp.bfloat16),
         scratch_shapes=[
+            pltpu.VMEM((count, latent_width), jnp.bfloat16),
             pltpu.VMEM((count, latent_width), jnp.bfloat16),
             pltpu.VMEM(mine.shape, mine.dtype),
             pltpu.VMEM((count, ep_count * width), jnp.bfloat16),
@@ -427,10 +432,14 @@
     def homeward(*previous):
         return [send(p, sums[p], 2 * p[0] + p[1]) for p in previous if p not in special]
 
-    run([(0, 0)], *[(near, k) for k in near if k], (travel, "up"))
+    run([(0, 0)], (near, 1), (travel, "up"))
+    start_far(1)
+    arrived = [k for k in near if k > 1]
+    far[1], *values = join(far[1], *[near[k] for k in arrived])
+    near.update(zip(arrived, values))
     sides = [[i, i + 1] for i in range(0, lax.axis_size("rep"), 2)]
     both_sides = lax.all_gather(travel.pop("up"), "rep", axis=0, axis_index_groups=sides)
-    previous = [(2, 0), (1, 0)]
+    previous = [(2, 0), (1, 1)]
     run(previous, *[start_near(3)] * (last >= 3), start_far(2))
     for k in range(3, steps):
         coming = homeward(*previous) + [start_far(k)] + [(far, 0)] * (k == last)
@@ -442,17 +451,16 @@
         [(last, 1), (0, 1)],
         send((last - 1, 1), sums[last - 1, 1], 1),
         send((last, 0), sums[last, 0], 2),
-        start_far(1),
     )
-    run([(1, 1)], send((last, 1), sums[last, 1], 3))
+    run([(1, 0)], send((last, 1), sums[last, 1], 3))
     shared = sums[last - 1, 0]
     for name in ((last - 1, 1), (last, 0), (last, 1)):
         shared += travel.pop(name).astype(jnp.float32)
     shared = shared.astype(jnp.bfloat16)
     send("shared", shared, 2 * last - 2)
-    sums[1, 1] = sums[1, 1].astype(jnp.bfloat16)
-    both_sides = after(both_sides, sums[1, 1], shared)
-    homeward((0, 1), (1, 1))
+    sums[1, 0] = sums[1, 0].astype(jnp.bfloat16)
+    both_sides = after(both_sides, sums[1, 0], shared)
+    homeward((0, 1), (1, 0))
     *terms, swapped_sides = join(sums[0, 0], *travel.values(), swap_cores(both_sides))
     both_sides = pltpu.with_memory_space_constraint(both_sides, pltpu.HBM)
     return project(group, terms, both_sides, swapped_sides)

time: 167 us -> 178 us (1.066)
  waiting for transfers between devices: 58.3 us -> 72.4 us
  starting transfers between devices: 38.8 us -> 36 us
    ppermute x21, waiting for transfers between devices: 46.5 us -> 59.6 us  [swap_ep(): lax.ppermute(array, 'ep', [(i, i ^ mask) for i in range(lax.axis_size('ep...]
    ppermute x21, starting transfers between devices: 31.3 us -> 28.3 us  [swap_ep(): lax.ppermute(array, 'ep', [(i, i ^ mask) for i in range(lax.axis_size('ep...]
    ppermute x21, waiting for transfers between devices: 4.06 us -> 5.88 us  [swap_cores(): return lax.ppermute(array, 'grp', [(0, 1), (1, 0)])]
  transfers between devices with their start and end apart: 46 -> 46, of which waited for: 18 -> 21; matrix products, arithmetic and copies ran while one was open for 2% -> 2% of each run, Pallas kernels for 26% -> 25%
where the time goes in v16:
time: 178 us
  waiting for transfers between devices  72.4 us (41%)
  Pallas kernels  48.7 us (27%)
  starting transfers between devices  36 us (20%)
  between operations  13.7 us (8%)
  local copies, waits for them, and re-layouts  4.24 us (2%)
  other arithmetic  3 us (2%)
    ppermute x21, waiting for transfers between devices, swap_ep(): lax.ppermute(array, 'ep', [(i, i ^ mask) for i in range(lax.axis_size('ep...  59.6 us
    pallas_call x5, Pallas kernels, expert_apply(): pl.pallas_call(functools.partial(expert_kernel, positions, count), out_sh...  41.8 us
    ppermute x21, starting transfers between devices, swap_ep(): lax.ppermute(array, 'ep', [(i, i ^ mask) for i in range(lax.axis_size('ep...  28.3 us
    ppermute x2, waiting for transfers between devices, swap_reps(): lax.ppermute(array, 'rep', [(i, i ^ 1) for i in range(lax.axis_size('rep'...  6.83 us
    ppermute x21, waiting for transfers between devices, swap_cores(): return lax.ppermute(array, 'grp', [(0, 1), (1, 0)])  5.88 us
    pallas_call x1, Pallas kernels, project(): pl.pallas_call(project_kernel, in_specs=[in_smem] + [in_vmem] * len(terms...  4.6 us
    ppermute x21, starting transfers between devices, swap_cores(): return lax.ppermute(array, 'grp', [(0, 1), (1, 0)])  4.51 us
  transfers between devices with their start and end apart: 46, of which 21 were waited for; matrix products, arithmetic and copies ran while one was open for 2% of the time, Pallas kernels for 25%

profile of v16, /device:TPU:0, one launch (start us, length us, event | category | flops | bytes accessed | tf_op | source)
XLA Modules:
  0.0 178.0 jit_solution(1589738300139327828)
XLA Ops:
  6.5 1.2 copy-done
  7.8 0.7 constant_dynamic-slice_fusion
  8.6 1.1 constant_dynamic-slice_fusion.1
  9.6 3.1 %collective-permute-start = (bf16[128,1024]{1,0:T(8,128)(2,1)S(1)}, bf16[128,1024]{1,0:T(8,128)(2,1)S(1)}, u32[]{:S(2)}, u32[]{:S(2)}) collective-permute-start(bf16[128,1024]{1,0:T(8,128)(2,1)S(1)} %get-tuple-element.156.refs_2_), channel_id=1, source_target_pairs={{0,2},{1,3},{2,0},{3,1},{4,6},{5,7},{6,4},{7,5},{8,10},{9,11},{10,... | collective-permute-start | bytes 786440 | tf_op jit(solution)/shard_map/ppermute | solution.py:35
  12.7 1.5 collective-permute-start.4
  14.3 2.6 %collective-permute-start.2 = (bf16[128,1024]{1,0:T(8,128)(2,1)S(1)}, bf16[128,1024]{1,0:T(8,128)(2,1)S(1)}, u32[]{:S(2)}, u32[]{:S(2)}) collective-permute-start(bf16[128,1024]{1,0:T(8,128)(2,1)S(1)} %get-tuple-element.156.refs_2_), channel_id=1, source_target_pairs={{0,4},{1,5},{2,6},{3,7},{4,0},{5,1},{6,2},{7,3},{8,12},{9,13},{10,... | collective-permute-start | bytes 786440 | tf_op jit(solution)/shard_map/ppermute | solution.py:35
  16.9 1.2 copy-done.1
  18.1 0.8 split_columns.1
  19.0 1.6 collective-permute-start.5
  21.2 2.5 %collective-permute-done.refs_6_ = bf16[128,1024]{1,0:T(8,128)(2,1)S(1)} collective-permute-done((bf16[128,1024]{1,0:T(8,128)(2,1)S(1)}, bf16[128,1024]{1,0:T(8,128)(2,1)S(1)}, u32[]{:S(2)}, u32[]{:S(2)}) %collective-permute-start) | collective-permute-done | bytes 262176 | tf_op jit(solution)/shard_map/ppermute | solution.py:35
  23.7 3.8 %collective-permute-start.1 = (bf16[128,1024]{1,0:T(8,128)(2,1)S(1)}, bf16[128,1024]{1,0:T(8,128)(2,1)S(1)}, u32[]{:S(2)}, u32[]{:S(2)}) collective-permute-start(bf16[128,1024]{1,0:T(8,128)(2,1)S(1)} %collective-permute-done.refs_6_), channel_id=1, source_target_pairs={{0,1},{1,0},{2,3},{3,2},{4,5},{5,4},{6,7},{7,6},{8,9},{9,8},{10,11... | collective-permute-start | bytes 786440 | tf_op jit(solution)/shard_map/ppermute | solution.py:35
  28.2 0.7 select_reduce_fusion.weights
  28.9 4.1 %collective-permute-done.2.refs_10_ = bf16[128,1024]{1,0:T(8,128)(2,1)S(1)} collective-permute-done((bf16[128,1024]{1,0:T(8,128)(2,1)S(1)}, bf16[128,1024]{1,0:T(8,128)(2,1)S(1)}, u32[]{:S(2)}, u32[]{:S(2)}) %collective-permute-start.2) | collective-permute-done | bytes 262176 | tf_op jit(solution)/shard_map/ppermute | solution.py:35
  33.1 0.9 collective-permute-start.3
  34.5 7.3 %collective-permute-done.3.refs_2_ = bf16[128,1024]{1,0:T(8,128)(2,1)S(1)} collective-permute-done((bf16[128,1024]{1,0:T(8,128)(2,1)S(1)}, bf16[128,1024]{1,0:T(8,128)(2,1)S(1)}, u32[]{:S(2)}, u32[]{:S(2)}) %collective-permute-start.3) | collective-permute-done | bytes 262176 | tf_op jit(solution)/shard_map/ppermute | solution.py:35
  43.5 10.0 %collective-permute-done.12.refs_3_ = bf16[128,1024]{1,0:T(8,128)(2,1)S(1)} collective-permute-done((bf16[128,1024]{1,0:T(8,128)(2,1)S(1)}, bf16[128,1024]{1,0:T(8,128)(2,1)S(1)}, u32[]{:S(2)}, u32[]{:S(2)}) %collective-permute-start.12) | collective-permute-done | bytes 262176 | tf_op jit(solution)/shard_map/ppermute | solution.py:35
  53.5 1.0 down_project.2.refs_6_
  55.5 1.6 collective-permute-start.15
  57.1 6.8 %collective-permute-done.15.arrived = bf16[128,1024]{1,0:T(8,128)(2,1)S(1)} collective-permute-done((bf16[128,1024]{1,0:T(8,128)(2,1)S(1)}, bf16[128,1024]{1,0:T(8,128)(2,1)S(1)}, u32[]{:S(2)}, u32[]{:S(2)}) %collective-permute-start.15) | collective-permute-done | bytes 262176 | tf_op jit(solution)/shard_map/ppermute | solution.py:31
  64.0 1.4 collective-permute-start.17
  65.6 6.4 %expert.5 = (bf16[128,1024]{1,0:T(8,128)(2,1)S(1)}, bf16[128,1024]{1,0:T(8,128)(2,1)S(1)}) custom-call(s32[1]{0:T(128)} %bitcast.1.where, bf16[144,1024]{1,0:T(8,128)(2,1)S(1)} %finish_latent.1.refs_0_, bf16[144,1024]{1,0:T(8,128)(2,1)S(1)} %collective-permute-done.16.refs_1_, bf16[1,1024,2048]{2,1,0:T(8,128)(2,1)} %refs_2_.3, ...), custom_call_target="tpu_custom_call" | custom-call | flops 805306368 | bytes 1048576 | tf_op jit(solution)/shard_map/expert/pallas_call | solution.py:257
  72.0 8.4 %collective-permute-done.17.refs_0_ = bf16[144,1024]{1,0:T(8,128)(2,1)S(1)} collective-permute-done((bf16[144,1024]{1,0:T(8,128)(2,1)S(1)}, bf16[144,1024]{1,0:T(8,128)(2,1)S(1)}, u32[]{:S(2)}, u32[]{:S(2)}) %collective-permute-start.17) | collective-permute-done | bytes 294944 | tf_op jit(solution)/shard_map/ppermute | solution.py:35
  80.4 1.3 collective-permute-start.19
  82.1 7.2 %collective-permute-done.19.refs_1_ = bf16[144,1024]{1,0:T(8,128)(2,1)S(1)} collective-permute-done((bf16[144,1024]{1,0:T(8,128)(2,1)S(1)}, bf16[144,1024]{1,0:T(8,128)(2,1)S(1)}, u32[]{:S(2)}, u32[]{:S(2)}) %collective-permute-start.19) | collective-permute-done | bytes 294944 | tf_op jit(solution)/shard_map/ppermute | solution.py:35
  89.9 1.2 collective-permute-start.24
  91.4 9.8 %expert.6 = (bf16[128,1024]{1,0:T(8,128)(2,1)S(1)}, bf16[128,1024]{1,0:T(8,128)(2,1)S(1)}, bf16[256,1024]{1,0:T(8,128)(2,1)S(1)}) custom-call(s32[1]{0:T(128)} %bitcast.1.where, bf16[144,1024]{1,0:T(8,128)(2,1)S(1)} %collective-permute-done.20.refs_0_, bf16[144,1024]{1,0:T(8,128)(2,1)S(1)} %collective-permute-done.19.refs_1_, ...), custom_call_target="tpu_custom_call" | custom-call | flops 1610612736 | bytes 2097152 | tf_op jit(solution)/shard_map/expert/pallas_call | solution.py:257
  101.4 1.2 collective-permute-start.30
  102.6 0.8 collective-permute-start.29
  104.0 2.0 %collective-permute-start.28 = (bf16[128,1024]{1,0:T(8,128)(2,1)S(1)}, bf16[128,1024]{1,0:T(8,128)(2,1)S(1)}, u32[]{:S(2)}, u32[]{:S(2)}) collective-permute-start(bf16[128,1024]{1,0:T(8,128)(2,1)S(1)} %add_convert_fusion.6), channel_id=1, source_target_pairs={{0,3},{1,2},{2,1},{3,0},{4,7},{5,6},{6,5},{7,4},{8,11},{9,10},{10,... | collective-permute-start | bytes 786440 | tf_op jit(solution)/shard_map/ppermute | solution.py:35
  106.0 9.5 %expert.7 = (bf16[128,1024]{1,0:T(8,128)(2,1)S(1)}, bf16[128,1024]{1,0:T(8,128)(2,1)S(1)}, bf16[256,1024]{1,0:T(8,128)(2,1)S(1)}) custom-call(s32[1]{0:T(128)} %bitcast.1.where, bf16[144,1024]{1,0:T(8,128)(2,1)S(1)} %collective-permute-done.23.refs_0_, bf16[144,1024]{1,0:T(8,128)(2,1)S(1)} %collective-permute-done.24.refs_1_, ...), custom_call_target="tpu_custom_call" | custom-call | flops 1610612736 | bytes 2097152 | tf_op jit(solution)/shard_map/expert/pallas_call | solution.py:257
  115.5 1.3 collective-permute-done.30.refs_1_
  116.8 5.8 %collective-permute-done.29.refs_0_ = bf16[144,1024]{1,0:T(8,128)(2,1)S(1)} collective-permute-done((bf16[144,1024]{1,0:T(8,128)(2,1)S(1)}, bf16[144,1024]{1,0:T(8,128)(2,1)S(1)}, u32[]{:S(2)}, u32[]{:S(2)}) %collective-permute-start.29) | collective-permute-done | bytes 294944 | tf_op jit(solution)/shard_map/ppermute | solution.py:35
  123.1 1.4 collective-permute-done.33
  124.7 1.9 %collective-permute-start.35 = (bf16[128,1024]{1,0:T(8,128)(2,1)S(1)}, bf16[128,1024]{1,0:T(8,128)(2,1)S(1)}, u32[]{:S(2)}, u32[]{:S(2)}) collective-permute-start(bf16[128,1024]{1,0:T(8,128)(2,1)S(1)} %get-tuple-element.159), channel_id=1, source_target_pairs={{0,2},{1,3},{2,0},{3,1},{4,6},{5,7},{6,4},{7,5},{8,10},{9,11},{10,... | collective-permute-start | bytes 786440 | tf_op jit(solution)/shard_map/ppermute | solution.py:35
  126.5 0.8 collective-permute-start.34
  127.4 9.7 %expert.8 = (bf16[128,1024]{1,0:T(8,128)(2,1)S(1)}, bf16[128,1024]{1,0:T(8,128)(2,1)S(1)}, bf16[256,1024]{1,0:T(8,128)(2,1)S(1)}) custom-call(s32[1]{0:T(128)} %bitcast.1.where, bf16[144,1024]{1,0:T(8,128)(2,1)S(1)} %collective-permute-done.29.refs_0_, bf16[144,1024]{1,0:T(8,128)(2,1)S(1)} %collective-permute-done.30.refs_1_, ...), custom_call_target="tpu_custom_call" | custom-call | flops 1610612736 | bytes 2097152 | tf_op jit(solution)/shard_map/expert/pallas_call | solution.py:257
  137.7 1.4 collective-permute-done.37
  139.3 1.0 collective-permute-start.38
  140.2 6.4 %expert.9 = (bf16[128,1024]{1,0:T(8,128)(2,1)S(1)}, bf16[128,1024]{1,0:T(8,128)(2,1)S(1)}) custom-call(s32[1]{0:T(128)} %bitcast.1.where, bf16[144,1024]{1,0:T(8,128)(2,1)S(1)} %collective-permute-done.17.refs_0_, bf16[144,1024]{1,0:T(8,128)(2,1)S(1)} %collective-permute-done.36.refs_1_, bf16[1,1024,2048]{2,1,0:T(8,128)(2,1)} %refs_2_.3, ...), custom_call_target="tpu_custom_call" | custom-call | flops 805306368 | bytes 1048576 | tf_op jit(solution)/shard_map/expert/pallas_call | solution.py:257
  146.6 1.9 %collective-permute-done.38 = bf16[128,1024]{1,0:T(8,128)(2,1)S(1)} collective-permute-done((bf16[128,1024]{1,0:T(8,128)(2,1)S(1)}, bf16[128,1024]{1,0:T(8,128)(2,1)S(1)}, u32[]{:S(2)}, u32[]{:S(2)}) %collective-permute-start.38) | collective-permute-done | bytes 262176 | tf_op jit(solution)/shard_map/ppermute | solution.py:35
  148.8 1.3 collective-permute-done.41
  150.8 1.2 collective-permute-start.40
  152.0 0.9 collective-permute-start.39
  152.9 2.0 %collective-permute-start.42 = (bf16[128,1024]{1,0:T(8,128)(2,1)S(1)}, bf16[128,1024]{1,0:T(8,128)(2,1)S(1)}, u32[]{:S(2)}, u32[]{:S(2)}) collective-permute-start(bf16[128,1024]{1,0:T(8,128)(2,1)S(1)} %add_convert_fusion), channel_id=1, source_target_pairs={{0,2},{1,3},{2,0},{3,1},{4,6},{5,7},{6,4},{7,5},{8,10},{9,11},{10,... | collective-permute-start | bytes 786440 | tf_op jit(solution)/shard_map/ppermute | solution.py:35
  154.9 0.8 collective-permute-done.18
  155.8 3.4 %collective-permute-done.40.refs_3_ = bf16[128,1024]{1,0:T(8,128)(2,1)S(1)} collective-permute-done((bf16[128,1024]{1,0:T(8,128)(2,1)S(1)}, bf16[128,1024]{1,0:T(8,128)(2,1)S(1)}, u32[]{:S(2)}, u32[]{:S(2)}) %collective-permute-start.40) | collective-permute-done | bytes 262176 | tf_op jit(solution)/shard_map/ppermute | solution.py:35
  159.1 7.2 %collective-permute-done.39.refs_2_ = bf16[128,1024]{1,0:T(8,128)(2,1)S(1)} collective-permute-done((bf16[128,1024]{1,0:T(8,128)(2,1)S(1)}, bf16[128,1024]{1,0:T(8,128)(2,1)S(1)}, u32[]{:S(2)}, u32[]{:S(2)}) %collective-permute-start.39) | collective-permute-done | bytes 262176 | tf_op jit(solution)/shard_map/ppermute | solution.py:35
  166.5 4.6 %project.1 = bf16[128,4096]{1,0:T(8,128)(2,1)} custom-call(s32[1]{0:T(128)} %bitcast.where, f32[128,1024]{1,0:T(8,128)S(1)} %convert_add_fusion.refs_0_, bf16[128,1024]{1,0:T(8,128)(2,1)S(1)} %collective-permute-done.28.refs_1_, bf16[128,1024]{1,0:T(8,128)(2,1)S(1)} %collective-permute-done.39.refs_2_, ...), custom_call_target="tpu_custom_call" | custom-call | flops 1073741824 | bytes 8388608 | tf_op jit(solution)/shard_map/project/pallas_call | solution.py:323
  (72 shorter events, 9.5 us)
Async XLA Ops:
  6.5 1.2 copy-start
  6.5 73.9 %all-gather.5.cloned.1.call-start = ((), (), s32[]{:S(2)}) async-start(), calls=%async_computation | async-start | bytes 2359296 | tf_op jit(solution)/shard_map/all_gather | solution.py:374
  8.5 141.7 %all-gather.7.cloned.1.call-start = ((), (), s32[]{:S(2)}) async-start(), calls=%async_computation.1 | async-start | bytes 6291456 | tf_op jit(solution)/shard_map/all_gather | solution.py:441
  9.6 14.1 %collective-permute-start = (bf16[128,1024]{1,0:T(8,128)(2,1)S(1)}, bf16[128,1024]{1,0:T(8,128)(2,1)S(1)}, u32[]{:S(2)}, u32[]{:S(2)}) collective-permute-start(bf16[128,1024]{1,0:T(8,128)(2,1)S(1)} %get-tuple-element.156.refs_2_), channel_id=1, source_target_pairs={{0,2},{1,3},{2,0},{3,1},{4,6},{5,7},{6,4},{7,5},{8,10},{9,11},{10,... | collective-permute-start | bytes 786440 | tf_op jit(solution)/shard_map/ppermute | solution.py:35
  12.7 21.3 %collective-permute-start.4 = (bf16[128,1024]{1,0:T(8,128)(2,1)S(1)}, bf16[128,1024]{1,0:T(8,128)(2,1)S(1)}, u32[]{:S(2)}, u32[]{:S(2)}) collective-permute-start(bf16[128,1024]{1,0:T(8,128)(2,1)S(1)} %get-tuple-element.156.refs_2_), channel_id=1, source_target_pairs={{0,1},{1,0},{2,3},{3,2},{4,5},{5,4},{6,7},{7,6},{8,9},{9,8},{10,11... | collective-permute-start | bytes 786440 | tf_op jit(solution)/shard_map/ppermute | solution.py:35
  14.3 18.8 %collective-permute-start.2 = (bf16[128,1024]{1,0:T(8,128)(2,1)S(1)}, bf16[128,1024]{1,0:T(8,128)(2,1)S(1)}, u32[]{:S(2)}, u32[]{:S(2)}) collective-permute-start(bf16[128,1024]{1,0:T(8,128)(2,1)S(1)} %get-tuple-element.156.refs_2_), channel_id=1, source_target_pairs={{0,4},{1,5},{2,6},{3,7},{4,0},{5,1},{6,2},{7,3},{8,12},{9,13},{10,... | collective-permute-start | bytes 786440 | tf_op jit(solution)/shard_map/ppermute | solution.py:35
  16.9 1.2 copy-start.1
  19.0 15.5 %collective-permute-start.5 = (bf16[128,2048]{1,0:T(8,128)(2,1)S(1)}, bf16[128,2048]{1,0:T(8,128)(2,1)S(1)}, u32[]{:S(2)}, u32[]{:S(2)}) collective-permute-start(bf16[128,2048]{1,0:T(8,128)(2,1)S(1)} %get-tuple-element.85), channel_id=1, source_target_pairs={{0,16},{16,0},{1,17},{17,1},{2,18},{18,2},{3,19},{19,3},{4,20},{20... | collective-permute-start | bytes 1572872 | tf_op jit(solution)/shard_map/ppermute | solution.py:31
  23.7 9.3 %collective-permute-start.1 = (bf16[128,1024]{1,0:T(8,128)(2,1)S(1)}, bf16[128,1024]{1,0:T(8,128)(2,1)S(1)}, u32[]{:S(2)}, u32[]{:S(2)}) collective-permute-start(bf16[128,1024]{1,0:T(8,128)(2,1)S(1)} %collective-permute-done.refs_6_), channel_id=1, source_target_pairs={{0,1},{1,0},{2,3},{3,2},{4,5},{5,4},{6,7},{7,6},{8,9},{9,8},{10,11... | collective-permute-start | bytes 786440 | tf_op jit(solution)/shard_map/ppermute | solution.py:35
  33.1 8.8 %collective-permute-start.3 = (bf16[128,1024]{1,0:T(8,128)(2,1)S(1)}, bf16[128,1024]{1,0:T(8,128)(2,1)S(1)}, u32[]{:S(2)}, u32[]{:S(2)}) collective-permute-start(bf16[128,1024]{1,0:T(8,128)(2,1)S(1)} %collective-permute-done.2.refs_10_), channel_id=1, source_target_pairs={{0,2},{1,3},{2,0},{3,1},{4,6},{5,7},{6,4},{7,5},{8,10},{9,11},{10,... | collective-permute-start | bytes 786440 | tf_op jit(solution)/shard_map/ppermute | solution.py:35
  34.0 8.5 %collective-permute-start.9 = (bf16[128,1024]{1,0:T(8,128)(2,1)S(1)}, bf16[128,1024]{1,0:T(8,128)(2,1)S(1)}, u32[]{:S(2)}, u32[]{:S(2)}) collective-permute-start(bf16[128,1024]{1,0:T(8,128)(2,1)S(1)} %collective-permute-done.2.refs_10_), channel_id=1, source_target_pairs={{0,1},{1,0},{2,3},{3,2},{4,5},{5,4},{6,7},{7,6},{8,9},{9,8},{10,11... | collective-permute-start | bytes 786440 | tf_op jit(solution)/shard_map/ppermute | solution.py:35
  34.0 9.0 %collective-permute-start.7 = (bf16[128,1024]{1,0:T(8,128)(2,1)S(1)}, bf16[128,1024]{1,0:T(8,128)(2,1)S(1)}, u32[]{:S(2)}, u32[]{:S(2)}) collective-permute-start(bf16[128,1024]{1,0:T(8,128)(2,1)S(1)} %collective-permute-done.refs_6_), channel_id=1, source_target_pairs={{0,8},{8,0},{1,9},{9,1},{2,10},{10,2},{3,11},{11,3},{4,12},{12,4},... | collective-permute-start | bytes 786440 | tf_op jit(solution)/shard_map/ppermute | solution.py:27
  34.0 9.1 %collective-permute-start.8 = (bf16[128,1024]{1,0:T(8,128)(2,1)S(1)}, bf16[128,1024]{1,0:T(8,128)(2,1)S(1)}, u32[]{:S(2)}, u32[]{:S(2)}) collective-permute-start(bf16[128,1024]{1,0:T(8,128)(2,1)S(1)} %collective-permute-done.1.refs_7_), channel_id=1, source_target_pairs={{0,8},{8,0},{1,9},{9,1},{2,10},{10,2},{3,11},{11,3},{4,12},{12,4},... | collective-permute-start | bytes 786440 | tf_op jit(solution)/shard_map/ppermute | solution.py:27
  41.8 11.7 %collective-permute-start.12 = (bf16[128,1024]{1,0:T(8,128)(2,1)S(1)}, bf16[128,1024]{1,0:T(8,128)(2,1)S(1)}, u32[]{:S(2)}, u32[]{:S(2)}) collective-permute-start(bf16[128,1024]{1,0:T(8,128)(2,1)S(1)} %collective-permute-done.3.refs_2_), channel_id=1, source_target_pairs={{0,1},{1,0},{2,3},{3,2},{4,5},{5,4},{6,7},{7,6},{8,9},{9,8},{10,11... | collective-permute-start | bytes 786440 | tf_op jit(solution)/shard_map/ppermute | solution.py:35
  42.5 11.0 %collective-permute-start.10 = (bf16[128,1024]{1,0:T(8,128)(2,1)S(1)}, bf16[128,1024]{1,0:T(8,128)(2,1)S(1)}, u32[]{:S(2)}, u32[]{:S(2)}) collective-permute-start(bf16[128,1024]{1,0:T(8,128)(2,1)S(1)} %collective-permute-done.2.refs_10_), channel_id=1, source_target_pairs={{0,8},{8,0},{1,9},{9,1},{2,10},{10,2},{3,11},{11,3},{4,12},{12,4},... | collective-permute-start | bytes 786440 | tf_op jit(solution)/shard_map/ppermute | solution.py:27
  42.5 11.0 %collective-permute-start.11 = (bf16[128,1024]{1,0:T(8,128)(2,1)S(1)}, bf16[128,1024]{1,0:T(8,128)(2,1)S(1)}, u32[]{:S(2)}, u32[]{:S(2)}) collective-permute-start(bf16[128,1024]{1,0:T(8,128)(2,1)S(1)} %collective-permute-done.9.refs_11_), channel_id=1, source_target_pairs={{0,8},{8,0},{1,9},{9,1},{2,10},{10,2},{3,11},{11,3},{4,12},{12,4},... | collective-permute-start | bytes 786440 | tf_op jit(solution)/shard_map/ppermute | solution.py:27
  43.0 10.5 %collective-permute-start.6 = (bf16[128,1024]{1,0:T(8,128)(2,1)S(1)}, bf16[128,1024]{1,0:T(8,128)(2,1)S(1)}, u32[]{:S(2)}, u32[]{:S(2)}) collective-permute-start(bf16[128,1024]{1,0:T(8,128)(2,1)S(1)} %collective-permute-done.4.refs_3_), channel_id=1, source_target_pairs={{0,8},{8,0},{1,9},{9,1},{2,10},{10,2},{3,11},{11,3},{4,12},{12,4},... | collective-permute-start | bytes 786440 | tf_op jit(solution)/shard_map/ppermute | solution.py:27
  43.1 11.4 %collective-permute-start.13 = (bf16[128,1024]{1,0:T(8,128)(2,1)S(1)}, bf16[128,1024]{1,0:T(8,128)(2,1)S(1)}, u32[]{:S(2)}, u32[]{:S(2)}) collective-permute-start(bf16[128,1024]{1,0:T(8,128)(2,1)S(1)} %collective-permute-done.3.refs_2_), channel_id=1, source_target_pairs={{0,8},{8,0},{1,9},{9,1},{2,10},{10,2},{3,11},{11,3},{4,12},{12,4},... | collective-permute-start | bytes 786440 | tf_op jit(solution)/shard_map/ppermute | solution.py:27
  53.5 1.5 collective-permute-start.14
  55.5 8.4 %collective-permute-start.15 = (bf16[128,1024]{1,0:T(8,128)(2,1)S(1)}, bf16[128,1024]{1,0:T(8,128)(2,1)S(1)}, u32[]{:S(2)}, u32[]{:S(2)}) collective-permute-start(bf16[128,1024]{1,0:T(8,128)(2,1)S(1)} %get-tuple-element.92), channel_id=1, source_target_pairs={{0,16},{16,0},{1,17},{17,1},{2,18},{18,2},{3,19},{19,3},{4,20},{20... | collective-permute-start | bytes 786440 | tf_op jit(solution)/shard_map/ppermute | solution.py:31
  64.0 1.6 collective-permute-start.16
  64.0 16.4 %collective-permute-start.17 = (bf16[144,1024]{1,0:T(8,128)(2,1)S(1)}, bf16[144,1024]{1,0:T(8,128)(2,1)S(1)}, u32[]{:S(2)}, u32[]{:S(2)}) collective-permute-start(bf16[144,1024]{1,0:T(8,128)(2,1)S(1)} %finish_latent.1.refs_0_), channel_id=1, source_target_pairs={{0,2},{1,3},{2,0},{3,1},{4,6},{5,7},{6,4},{7,5},{8,10},{9,11},{10,... | collective-permute-start | bytes 884744 | tf_op jit(solution)/shard_map/ppermute | solution.py:35
  65.5 16.6 %collective-permute-start.20 = (bf16[144,1024]{1,0:T(8,128)(2,1)S(1)}, bf16[144,1024]{1,0:T(8,128)(2,1)S(1)}, u32[]{:S(2)}, u32[]{:S(2)}) collective-permute-start(bf16[144,1024]{1,0:T(8,128)(2,1)S(1)} %finish_latent.1.refs_0_), channel_id=1, source_target_pairs={{0,4},{1,5},{2,6},{3,7},{4,0},{5,1},{6,2},{7,3},{8,12},{9,13},{10,... | collective-permute-start | bytes 884744 | tf_op jit(solution)/shard_map/ppermute | solution.py:35
  80.4 8.9 %collective-permute-start.19 = (bf16[144,1024]{1,0:T(8,128)(2,1)S(1)}, bf16[144,1024]{1,0:T(8,128)(2,1)S(1)}, u32[]{:S(2)}, u32[]{:S(2)}) collective-permute-start(bf16[144,1024]{1,0:T(8,128)(2,1)S(1)} %collective-permute-done.17.refs_0_), channel_id=1, source_target_pairs={{0,1},{1,0},{2,3},{3,2},{4,5},{5,4},{6,7},{7,6},{8,9},{9,8},{10,11... | collective-permute-start | bytes 884744 | tf_op jit(solution)/shard_map/ppermute | solution.py:35
  89.4 1.7 collective-permute-start.22
  89.4 2.0 %collective-permute-start.21 = (bf16[144,1024]{1,0:T(8,128)(2,1)S(1)}, bf16[144,1024]{1,0:T(8,128)(2,1)S(1)}, u32[]{:S(2)}, u32[]{:S(2)}) collective-permute-start(bf16[144,1024]{1,0:T(8,128)(2,1)S(1)} %collective-permute-done.20.refs_0_), channel_id=1, source_target_pairs={{0,8},{8,0},{1,9},{9,1},{2,10},{10,2},{3,11},{11,3},{4,12},{12,4},... | collective-permute-start | bytes 884744 | tf_op jit(solution)/shard_map/ppermute | solution.py:27
  89.9 11.3 %collective-permute-start.24 = (bf16[144,1024]{1,0:T(8,128)(2,1)S(1)}, bf16[144,1024]{1,0:T(8,128)(2,1)S(1)}, u32[]{:S(2)}, u32[]{:S(2)}) collective-permute-start(bf16[144,1024]{1,0:T(8,128)(2,1)S(1)} %collective-permute-done.20.refs_0_), channel_id=1, source_target_pairs={{0,1},{1,0},{2,3},{3,2},{4,5},{5,4},{6,7},{7,6},{8,9},{9,8},{10,11... | collective-permute-start | bytes 884744 | tf_op jit(solution)/shard_map/ppermute | solution.py:35
  91.1 10.0 %collective-permute-start.23 = (bf16[144,1024]{1,0:T(8,128)(2,1)S(1)}, bf16[144,1024]{1,0:T(8,128)(2,1)S(1)}, u32[]{:S(2)}, u32[]{:S(2)}) collective-permute-start(bf16[144,1024]{1,0:T(8,128)(2,1)S(1)} %collective-permute-done.20.refs_0_), channel_id=1, source_target_pairs={{0,2},{1,3},{2,0},{3,1},{4,6},{5,7},{6,4},{7,5},{8,10},{9,11},{10,... | collective-permute-start | bytes 884744 | tf_op jit(solution)/shard_map/ppermute | solution.py:35
  101.1 2.8 %collective-permute-start.27 = (bf16[256,1024]{1,0:T(8,128)(2,1)S(1)}, bf16[256,1024]{1,0:T(8,128)(2,1)S(1)}, u32[]{:S(2)}, u32[]{:S(2)}) collective-permute-start(bf16[256,1024]{1,0:T(8,128)(2,1)S(1)} %get-tuple-element.120), channel_id=1, source_target_pairs={{0,8},{8,0},{1,9},{9,1},{2,10},{10,2},{3,11},{11,3},{4,12},{12,4},... | collective-permute-start | bytes 1572872 | tf_op jit(solution)/shard_map/ppermute | solution.py:27
  101.4 15.4 %collective-permute-start.30 = (bf16[144,1024]{1,0:T(8,128)(2,1)S(1)}, bf16[144,1024]{1,0:T(8,128)(2,1)S(1)}, u32[]{:S(2)}, u32[]{:S(2)}) collective-permute-start(bf16[144,1024]{1,0:T(8,128)(2,1)S(1)} %finish_latent.1.refs_0_), channel_id=1, source_target_pairs={{0,1},{1,0},{2,3},{3,2},{4,5},{5,4},{6,7},{7,6},{8,9},{9,8},{10,11... | collective-permute-start | bytes 884744 | tf_op jit(solution)/shard_map/ppermute | solution.py:35
  102.6 20.0 %collective-permute-start.29 = (bf16[144,1024]{1,0:T(8,128)(2,1)S(1)}, bf16[144,1024]{1,0:T(8,128)(2,1)S(1)}, u32[]{:S(2)}, u32[]{:S(2)}) collective-permute-start(bf16[144,1024]{1,0:T(8,128)(2,1)S(1)} %collective-permute-done.23.refs_0_), channel_id=1, source_target_pairs={{0,1},{1,0},{2,3},{3,2},{4,5},{5,4},{6,7},{7,6},{8,9},{9,8},{10,11... | collective-permute-start | bytes 884744 | tf_op jit(solution)/shard_map/ppermute | solution.py:35
  103.4 2.6 %collective-permute-start.25 = (bf16[144,1024]{1,0:T(8,128)(2,1)S(1)}, bf16[144,1024]{1,0:T(8,128)(2,1)S(1)}, u32[]{:S(2)}, u32[]{:S(2)}) collective-permute-start(bf16[144,1024]{1,0:T(8,128)(2,1)S(1)} %collective-permute-done.23.refs_0_), channel_id=1, source_target_pairs={{0,8},{8,0},{1,9},{9,1},{2,10},{10,2},{3,11},{11,3},{4,12},{12,4},... | collective-permute-start | bytes 884744 | tf_op jit(solution)/shard_map/ppermute | solution.py:27
  103.4 2.6 %collective-permute-start.26 = (bf16[144,1024]{1,0:T(8,128)(2,1)S(1)}, bf16[144,1024]{1,0:T(8,128)(2,1)S(1)}, u32[]{:S(2)}, u32[]{:S(2)}) collective-permute-start(bf16[144,1024]{1,0:T(8,128)(2,1)S(1)} %collective-permute-done.24.refs_1_), channel_id=1, source_target_pairs={{0,8},{8,0},{1,9},{9,1},{2,10},{10,2},{3,11},{11,3},{4,12},{12,4},... | collective-permute-start | bytes 884744 | tf_op jit(solution)/shard_map/ppermute | solution.py:27
  104.0 18.6 %collective-permute-start.28 = (bf16[128,1024]{1,0:T(8,128)(2,1)S(1)}, bf16[128,1024]{1,0:T(8,128)(2,1)S(1)}, u32[]{:S(2)}, u32[]{:S(2)}) collective-permute-start(bf16[128,1024]{1,0:T(8,128)(2,1)S(1)} %add_convert_fusion.6), channel_id=1, source_target_pairs={{0,3},{1,2},{2,1},{3,0},{4,7},{5,6},{6,5},{7,4},{8,11},{9,10},{10,... | collective-permute-start | bytes 786440 | tf_op jit(solution)/shard_map/ppermute | solution.py:35
  122.6 1.9 %collective-permute-start.33 = (bf16[256,1024]{1,0:T(8,128)(2,1)S(1)}, bf16[256,1024]{1,0:T(8,128)(2,1)S(1)}, u32[]{:S(2)}, u32[]{:S(2)}) collective-permute-start(bf16[256,1024]{1,0:T(8,128)(2,1)S(1)} %get-tuple-element.133), channel_id=1, source_target_pairs={{0,8},{8,0},{1,9},{9,1},{2,10},{10,2},{3,11},{11,3},{4,12},{12,4},... | collective-permute-start | bytes 1572872 | tf_op jit(solution)/shard_map/ppermute | solution.py:27
  122.6 4.8 %collective-permute-start.31 = (bf16[144,1024]{1,0:T(8,128)(2,1)S(1)}, bf16[144,1024]{1,0:T(8,128)(2,1)S(1)}, u32[]{:S(2)}, u32[]{:S(2)}) collective-permute-start(bf16[144,1024]{1,0:T(8,128)(2,1)S(1)} %collective-permute-done.29.refs_0_), channel_id=1, source_target_pairs={{0,8},{8,0},{1,9},{9,1},{2,10},{10,2},{3,11},{11,3},{4,12},{12,4},... | collective-permute-start | bytes 884744 | tf_op jit(solution)/shard_map/ppermute | solution.py:27
  123.1 4.3 %collective-permute-start.32 = (bf16[144,1024]{1,0:T(8,128)(2,1)S(1)}, bf16[144,1024]{1,0:T(8,128)(2,1)S(1)}, u32[]{:S(2)}, u32[]{:S(2)}) collective-permute-start(bf16[144,1024]{1,0:T(8,128)(2,1)S(1)} %collective-permute-done.30.refs_1_), channel_id=1, source_target_pairs={{0,8},{8,0},{1,9},{9,1},{2,10},{10,2},{3,11},{11,3},{4,12},{12,4},... | collective-permute-start | bytes 884744 | tf_op jit(solution)/shard_map/ppermute | solution.py:27
  124.7 12.4 %collective-permute-start.35 = (bf16[128,1024]{1,0:T(8,128)(2,1)S(1)}, bf16[128,1024]{1,0:T(8,128)(2,1)S(1)}, u32[]{:S(2)}, u32[]{:S(2)}) collective-permute-start(bf16[128,1024]{1,0:T(8,128)(2,1)S(1)} %get-tuple-element.159), channel_id=1, source_target_pairs={{0,2},{1,3},{2,0},{3,1},{4,6},{5,7},{6,4},{7,5},{8,10},{9,11},{10,... | collective-permute-start | bytes 786440 | tf_op jit(solution)/shard_map/ppermute | solution.py:35
  126.5 10.5 %collective-permute-start.34 = (bf16[128,1024]{1,0:T(8,128)(2,1)S(1)}, bf16[128,1024]{1,0:T(8,128)(2,1)S(1)}, u32[]{:S(2)}, u32[]{:S(2)}) collective-permute-start(bf16[128,1024]{1,0:T(8,128)(2,1)S(1)} %get-tuple-element.160), channel_id=1, source_target_pairs={{0,1},{1,0},{2,3},{3,2},{4,5},{5,4},{6,7},{7,6},{8,9},{9,8},{10,11... | collective-permute-start | bytes 786440 | tf_op jit(solution)/shard_map/ppermute | solution.py:35
  137.1 2.0 %collective-permute-start.37 = (bf16[256,1024]{1,0:T(8,128)(2,1)S(1)}, bf16[256,1024]{1,0:T(8,128)(2,1)S(1)}, u32[]{:S(2)}, u32[]{:S(2)}) collective-permute-start(bf16[256,1024]{1,0:T(8,128)(2,1)S(1)} %get-tuple-element.142), channel_id=1, source_target_pairs={{0,8},{8,0},{1,9},{9,1},{2,10},{10,2},{3,11},{11,3},{4,12},{12,4},... | collective-permute-start | bytes 1572872 | tf_op jit(solution)/shard_map/ppermute | solution.py:27
  137.2 3.1 %collective-permute-start.36 = (bf16[144,1024]{1,0:T(8,128)(2,1)S(1)}, bf16[144,1024]{1,0:T(8,128)(2,1)S(1)}, u32[]{:S(2)}, u32[]{:S(2)}) collective-permute-start(bf16[144,1024]{1,0:T(8,128)(2,1)S(1)} %collective-permute-done.17.refs_0_), channel_id=1, source_target_pairs={{0,8},{8,0},{1,9},{9,1},{2,10},{10,2},{3,11},{11,3},{4,12},{12,4},... | collective-permute-start | bytes 884744 | tf_op jit(solution)/shard_map/ppermute | solution.py:27
  139.3 9.3 %collective-permute-start.38 = (bf16[128,1024]{1,0:T(8,128)(2,1)S(1)}, bf16[128,1024]{1,0:T(8,128)(2,1)S(1)}, u32[]{:S(2)}, u32[]{:S(2)}) collective-permute-start(bf16[128,1024]{1,0:T(8,128)(2,1)S(1)} %get-tuple-element.158), channel_id=1, source_target_pairs={{0,3},{1,2},{2,1},{3,0},{4,7},{5,6},{6,5},{7,4},{8,11},{9,10},{10,... | collective-permute-start | bytes 786440 | tf_op jit(solution)/shard_map/ppermute | solution.py:35
  148.6 1.5 collective-permute-start.41
  150.2 16.3 %collective-permute-start.43 = (bf16[2,8,256,512]{3,2,1,0:T(8,128)(2,1)}, bf16[2,8,256,512]{3,2,1,0:T(8,128)(2,1)S(1)}, u32[]{:S(2)}, u32[]{:S(2)}) collective-permute-start(bf16[2,8,256,512]{3,2,1,0:T(8,128)(2,1)} %bitcast.6), channel_id=1, source_target_pairs={{0,8},{8,0},{1,9},{9,1},{2,10},{10,2},{3,11},{11,3},{4,12},{12,4},... | collective-permute-start | bytes 12582920 | tf_op jit(solution)/shard_map/ppermute | solution.py:27
  150.4 5.3 %collective-permute-start.18 = (bf16[128,1024]{1,0:T(8,128)(2,1)S(1)}, bf16[128,1024]{1,0:T(8,128)(2,1)S(1)}, u32[]{:S(2)}, u32[]{:S(2)}) collective-permute-start(bf16[128,1024]{1,0:T(8,128)(2,1)S(1)} %get-tuple-element.99), channel_id=1, source_target_pairs={{0,8},{8,0},{1,9},{9,1},{2,10},{10,2},{3,11},{11,3},{4,12},{12,4},... | collective-permute-start | bytes 786440 | tf_op jit(solution)/shard_map/ppermute | solution.py:27
  150.8 8.3 %collective-permute-start.40 = (bf16[128,1024]{1,0:T(8,128)(2,1)S(1)}, bf16[128,1024]{1,0:T(8,128)(2,1)S(1)}, u32[]{:S(2)}, u32[]{:S(2)}) collective-permute-start(bf16[128,1024]{1,0:T(8,128)(2,1)S(1)} %get-tuple-element.157), channel_id=1, source_target_pairs={{0,1},{1,0},{2,3},{3,2},{4,5},{5,4},{6,7},{7,6},{8,9},{9,8},{10,11... | collective-permute-start | bytes 786440 | tf_op jit(solution)/shard_map/ppermute | solution.py:35
  152.0 14.3 %collective-permute-start.39 = (bf16[128,1024]{1,0:T(8,128)(2,1)S(1)}, bf16[128,1024]{1,0:T(8,128)(2,1)S(1)}, u32[]{:S(2)}, u32[]{:S(2)}) collective-permute-start(bf16[128,1024]{1,0:T(8,128)(2,1)S(1)} %add_convert_fusion.2), channel_id=1, source_target_pairs={{0,4},{1,5},{2,6},{3,7},{4,0},{5,1},{6,2},{7,3},{8,12},{9,13},{10,... | collective-permute-start | bytes 786440 | tf_op jit(solution)/shard_map/ppermute | solution.py:35
  152.9 13.6 %collective-permute-start.42 = (bf16[128,1024]{1,0:T(8,128)(2,1)S(1)}, bf16[128,1024]{1,0:T(8,128)(2,1)S(1)}, u32[]{:S(2)}, u32[]{:S(2)}) collective-permute-start(bf16[128,1024]{1,0:T(8,128)(2,1)S(1)} %add_convert_fusion), channel_id=1, source_target_pairs={{0,2},{1,3},{2,0},{3,1},{4,6},{5,7},{6,4},{7,5},{8,10},{9,11},{10,... | collective-permute-start | bytes 786440 | tf_op jit(solution)/shard_map/ppermute | solution.py:35
Sparse Core Ops, SparseCore 0:
  9.5 60.0 all-gather.4
  81.9 55.5 all-gather.6

commit v17 on v15

--- a/solution.py
+++ b/solution.py
@@ -369,14 +369,14 @@
     mine = lax.all_gather(up_piece, "ep", axis=0)
     weights = dense_weights(after(expert_ids, near[1]), route_scores, expert_count)
     others = {k: near[k] for k in near if k > 1}
-    far[1], weights, *arrived = join(far[1], weights, *others.values())
+    weights, *arrived = join(weights, *others.values())
     near.update(zip(others, arrived))
     for k in range(2, steps):
         if k & (k - 1):
             low = k & -k
             near[k] = swap_ep(near[k ^ low], 2 * low)
         if k == last:
-            near[k], far[0], taken = join(near[k], far[0], taken)
+            near[k], far[0], far[1], taken = join(near[k], far[0], far[1], taken)
         far[k] = swap_ep(near[k], 1)
     blocks = []
     for k in range(steps):

time: 167 us -> 178 us (1.066)
  waiting for transfers between devices: 58.3 us -> 71.3 us
  starting transfers between devices: 38.8 us -> 36.5 us
    ppermute x21, waiting for transfers between devices: 46.5 us -> 57.7 us  [swap_ep(): lax.ppermute(array, 'ep', [(i, i ^ mask) for i in range(lax.axis_size('ep...]
    ppermute x21, waiting for transfers between devices: 4.06 us -> 6.96 us  [swap_cores(): return lax.ppermute(array, 'grp', [(0, 1), (1, 0)])]
    ppermute x21, starting transfers between devices: 31.3 us -> 29.3 us  [swap_ep(): lax.ppermute(array, 'ep', [(i, i ^ mask) for i in range(lax.axis_size('ep...]
  transfers between devices with their start and end apart: 46 -> 46, of which waited for: 18 -> 22; matrix products, arithmetic and copies ran while one was open for 2% -> 2% of each run, Pallas kernels for 26% -> 25%
where the time goes in v17:
time: 178 us; the launch traced here: 177 us
  waiting for transfers between devices  71.3 us (40%)
  Pallas kernels  48.8 us (27%)
  starting transfers between devices  36.5 us (21%)
  between operations  13.7 us (8%)
  local copies, waits for them, and re-layouts  4.24 us (2%)
  other arithmetic  3 us (2%)
    ppermute x21, waiting for transfers between devices, swap_ep(): lax.ppermute(array, 'ep', [(i, i ^ mask) for i in range(lax.axis_size('ep...  57.7 us
    pallas_call x5, Pallas kernels, expert_apply(): pl.pallas_call(functools.partial(expert_kernel, positions, count), out_sh...  41.8 us
    ppermute x21, starting transfers between devices, swap_ep(): lax.ppermute(array, 'ep', [(i, i ^ mask) for i in range(lax.axis_size('ep...  29.3 us
    ppermute x21, waiting for transfers between devices, swap_cores(): return lax.ppermute(array, 'grp', [(0, 1), (1, 0)])  6.96 us
    ppermute x2, waiting for transfers between devices, swap_reps(): lax.ppermute(array, 'rep', [(i, i ^ 1) for i in range(lax.axis_size('rep'...  6.61 us
    pallas_call x1, Pallas kernels, project(): pl.pallas_call(project_kernel, in_specs=[in_smem] + [in_vmem] * len(terms...  4.71 us
    ppermute x2, starting transfers between devices, swap_reps(): lax.ppermute(array, 'rep', [(i, i ^ 1) for i in range(lax.axis_size('rep'...  3.62 us
  transfers between devices with their start and end apart: 46, of which 22 were waited for; matrix products, arithmetic and copies ran while one was open for 2% of the time, Pallas kernels for 25%

profile of v17, /device:TPU:0, one launch (start us, length us, event | category | flops | bytes accessed | tf_op | source)
XLA Modules:
  0.0 177.5 jit_solution(15897048699594675828)
XLA Ops:
  6.5 1.2 copy-done
  7.8 0.7 constant_dynamic-slice_fusion
  8.6 1.1 constant_dynamic-slice_fusion.1
  9.6 3.0 %collective-permute-start.3 = (bf16[128,1024]{1,0:T(8,128)(2,1)S(1)}, bf16[128,1024]{1,0:T(8,128)(2,1)S(1)}, u32[]{:S(2)}, u32[]{:S(2)}) collective-permute-start(bf16[128,1024]{1,0:T(8,128)(2,1)S(1)} %get-tuple-element.156.refs_2_), channel_id=1, source_target_pairs={{0,1},{1,0},{2,3},{3,2},{4,5},{5,4},{6,7},{7,6},{8,9},{9,8},{10,11... | collective-permute-start | bytes 786440 | tf_op jit(solution)/shard_map/ppermute | solution.py:35
  12.7 2.6 %collective-permute-start.1 = (bf16[128,1024]{1,0:T(8,128)(2,1)S(1)}, bf16[128,1024]{1,0:T(8,128)(2,1)S(1)}, u32[]{:S(2)}, u32[]{:S(2)}) collective-permute-start(bf16[128,1024]{1,0:T(8,128)(2,1)S(1)} %get-tuple-element.156.refs_2_), channel_id=1, source_target_pairs={{0,4},{1,5},{2,6},{3,7},{4,0},{5,1},{6,2},{7,3},{8,12},{9,13},{10,... | collective-permute-start | bytes 786440 | tf_op jit(solution)/shard_map/ppermute | solution.py:35
  15.3 1.6 collective-permute-start
  16.9 1.2 copy-done.1
  18.1 0.8 split_columns.1
  19.0 1.6 collective-permute-start.5
  22.0 9.0 %collective-permute-done.refs_6_ = bf16[128,1024]{1,0:T(8,128)(2,1)S(1)} collective-permute-done((bf16[128,1024]{1,0:T(8,128)(2,1)S(1)}, bf16[128,1024]{1,0:T(8,128)(2,1)S(1)}, u32[]{:S(2)}, u32[]{:S(2)}) %collective-permute-start) | collective-permute-done | bytes 262176 | tf_op jit(solution)/shard_map/ppermute | solution.py:35
  31.0 0.7 select_reduce_fusion.weights
  31.7 2.5 %collective-permute-start.2 = (bf16[128,1024]{1,0:T(8,128)(2,1)S(1)}, bf16[128,1024]{1,0:T(8,128)(2,1)S(1)}, u32[]{:S(2)}, u32[]{:S(2)}) collective-permute-start(bf16[128,1024]{1,0:T(8,128)(2,1)S(1)} %collective-permute-done.1.refs_10_), channel_id=1, source_target_pairs={{0,2},{1,3},{2,0},{3,1},{4,6},{5,7},{6,4},{7,5},{8,10},{9,11},{10,... | collective-permute-start | bytes 786440 | tf_op jit(solution)/shard_map/ppermute | solution.py:35
  34.2 2.0 %collective-permute-start.9 = (bf16[128,1024]{1,0:T(8,128)(2,1)S(1)}, bf16[128,1024]{1,0:T(8,128)(2,1)S(1)}, u32[]{:S(2)}, u32[]{:S(2)}) collective-permute-start(bf16[128,1024]{1,0:T(8,128)(2,1)S(1)} %collective-permute-done.1.refs_10_), channel_id=1, source_target_pairs={{0,1},{1,0},{2,3},{3,2},{4,5},{5,4},{6,7},{7,6},{8,9},{9,8},{10,11... | collective-permute-start | bytes 786440 | tf_op jit(solution)/shard_map/ppermute | solution.py:35
  36.3 5.1 %collective-permute-done.2.refs_2_ = bf16[128,1024]{1,0:T(8,128)(2,1)S(1)} collective-permute-done((bf16[128,1024]{1,0:T(8,128)(2,1)S(1)}, bf16[128,1024]{1,0:T(8,128)(2,1)S(1)}, u32[]{:S(2)}, u32[]{:S(2)}) %collective-permute-start.2) | collective-permute-done | bytes 262176 | tf_op jit(solution)/shard_map/ppermute | solution.py:35
  41.4 2.1 %collective-permute-done.4.refs_7_ = bf16[128,1024]{1,0:T(8,128)(2,1)S(1)} collective-permute-done((bf16[128,1024]{1,0:T(8,128)(2,1)S(1)}, bf16[128,1024]{1,0:T(8,128)(2,1)S(1)}, u32[]{:S(2)}, u32[]{:S(2)}) %collective-permute-start.4) | collective-permute-done | bytes 262176 | tf_op jit(solution)/shard_map/ppermute | solution.py:35
  43.5 8.3 %collective-permute-done.9.refs_11_ = bf16[128,1024]{1,0:T(8,128)(2,1)S(1)} collective-permute-done((bf16[128,1024]{1,0:T(8,128)(2,1)S(1)}, bf16[128,1024]{1,0:T(8,128)(2,1)S(1)}, u32[]{:S(2)}, u32[]{:S(2)}) %collective-permute-start.9) | collective-permute-done | bytes 262176 | tf_op jit(solution)/shard_map/ppermute | solution.py:35
  52.4 8.7 %collective-permute-done.12.refs_3_ = bf16[128,1024]{1,0:T(8,128)(2,1)S(1)} collective-permute-done((bf16[128,1024]{1,0:T(8,128)(2,1)S(1)}, bf16[128,1024]{1,0:T(8,128)(2,1)S(1)}, u32[]{:S(2)}, u32[]{:S(2)}) %collective-permute-start.12) | collective-permute-done | bytes 262176 | tf_op jit(solution)/shard_map/ppermute | solution.py:35
  61.1 1.0 down_project.2.refs_6_
  63.0 2.1 %collective-permute-start.15 = (bf16[128,1024]{1,0:T(8,128)(2,1)S(1)}, bf16[128,1024]{1,0:T(8,128)(2,1)S(1)}, u32[]{:S(2)}, u32[]{:S(2)}) collective-permute-start(bf16[128,1024]{1,0:T(8,128)(2,1)S(1)} %get-tuple-element.92), channel_id=1, source_target_pairs={{0,16},{16,0},{1,17},{17,1},{2,18},{18,2},{3,19},{19,3},{4,20},{20... | collective-permute-start | bytes 786440 | tf_op jit(solution)/shard_map/ppermute | solution.py:31
  65.1 6.6 %collective-permute-done.15.arrived = bf16[128,1024]{1,0:T(8,128)(2,1)S(1)} collective-permute-done((bf16[128,1024]{1,0:T(8,128)(2,1)S(1)}, bf16[128,1024]{1,0:T(8,128)(2,1)S(1)}, u32[]{:S(2)}, u32[]{:S(2)}) %collective-permute-start.15) | collective-permute-done | bytes 262176 | tf_op jit(solution)/shard_map/ppermute | solution.py:31
  71.8 5.9 %collective-permute-start.18 = (bf16[144,1024]{1,0:T(8,128)(2,1)S(1)}, bf16[144,1024]{1,0:T(8,128)(2,1)S(1)}, u32[]{:S(2)}, u32[]{:S(2)}) collective-permute-start(bf16[144,1024]{1,0:T(8,128)(2,1)S(1)} %finish_latent.1.refs_0_), channel_id=1, source_target_pairs={{0,4},{1,5},{2,6},{3,7},{4,0},{5,1},{6,2},{7,3},{8,12},{9,13},{10,... | collective-permute-start | bytes 884744 | tf_op jit(solution)/shard_map/ppermute | solution.py:35
  77.7 6.4 %expert.5 = (bf16[128,1024]{1,0:T(8,128)(2,1)S(1)}, bf16[128,1024]{1,0:T(8,128)(2,1)S(1)}) custom-call(s32[1]{0:T(128)} %bitcast.1.where, bf16[144,1024]{1,0:T(8,128)(2,1)S(1)} %finish_latent.1.refs_0_, bf16[144,1024]{1,0:T(8,128)(2,1)S(1)} %collective-permute-done.16.refs_1_, bf16[1,1024,2048]{2,1,0:T(8,128)(2,1)} %refs_2_.3, ...), custom_call_target="tpu_custom_call" | custom-call | flops 805306368 | bytes 1048576 | tf_op jit(solution)/shard_map/expert/pallas_call | solution.py:257
  84.1 5.8 %collective-permute-done.18.refs_0_ = bf16[144,1024]{1,0:T(8,128)(2,1)S(1)} collective-permute-done((bf16[144,1024]{1,0:T(8,128)(2,1)S(1)}, bf16[144,1024]{1,0:T(8,128)(2,1)S(1)}, u32[]{:S(2)}, u32[]{:S(2)}) %collective-permute-start.18) | collective-permute-done | bytes 294944 | tf_op jit(solution)/shard_map/ppermute | solution.py:35
  89.9 3.1 %collective-permute-done.17.refs_1_ = bf16[144,1024]{1,0:T(8,128)(2,1)S(1)} collective-permute-done((bf16[144,1024]{1,0:T(8,128)(2,1)S(1)}, bf16[144,1024]{1,0:T(8,128)(2,1)S(1)}, u32[]{:S(2)}, u32[]{:S(2)}) %collective-permute-start.17) | collective-permute-done | bytes 294944 | tf_op jit(solution)/shard_map/ppermute | solution.py:35
  95.1 9.8 %expert.6 = (bf16[128,1024]{1,0:T(8,128)(2,1)S(1)}, bf16[128,1024]{1,0:T(8,128)(2,1)S(1)}, bf16[256,1024]{1,0:T(8,128)(2,1)S(1)}) custom-call(s32[1]{0:T(128)} %bitcast.1.where, bf16[144,1024]{1,0:T(8,128)(2,1)S(1)} %collective-permute-done.18.refs_0_, bf16[144,1024]{1,0:T(8,128)(2,1)S(1)} %collective-permute-done.17.refs_1_, ...), custom_call_target="tpu_custom_call" | custom-call | flops 1610612736 | bytes 2097152 | tf_op jit(solution)/shard_map/expert/pallas_call | solution.py:257
  105.0 0.7 collective-permute-start.29
  105.7 1.3 collective-permute-start.28
  108.1 1.0 collective-permute-done.25.refs_3_
  109.0 9.5 %expert.7 = (bf16[128,1024]{1,0:T(8,128)(2,1)S(1)}, bf16[128,1024]{1,0:T(8,128)(2,1)S(1)}, bf16[256,1024]{1,0:T(8,128)(2,1)S(1)}) custom-call(s32[1]{0:T(128)} %bitcast.1.where, bf16[144,1024]{1,0:T(8,128)(2,1)S(1)} %collective-permute-done.22.refs_0_, bf16[144,1024]{1,0:T(8,128)(2,1)S(1)} %collective-permute-done.23.refs_1_, ...), custom_call_target="tpu_custom_call" | custom-call | flops 1610612736 | bytes 2097152 | tf_op jit(solution)/shard_map/expert/pallas_call | solution.py:257
  118.6 2.1 %collective-permute-done.28.refs_0_ = bf16[144,1024]{1,0:T(8,128)(2,1)S(1)} collective-permute-done((bf16[144,1024]{1,0:T(8,128)(2,1)S(1)}, bf16[144,1024]{1,0:T(8,128)(2,1)S(1)}, u32[]{:S(2)}, u32[]{:S(2)}) %collective-permute-start.28) | collective-permute-done | bytes 294944 | tf_op jit(solution)/shard_map/ppermute | solution.py:35
  120.7 0.7 collective-permute-start.35
  122.8 1.0 collective-permute-start.34
  123.8 1.4 collective-permute-start.33
  125.2 9.7 %expert.8 = (bf16[128,1024]{1,0:T(8,128)(2,1)S(1)}, bf16[128,1024]{1,0:T(8,128)(2,1)S(1)}, bf16[256,1024]{1,0:T(8,128)(2,1)S(1)}) custom-call(s32[1]{0:T(128)} %bitcast.1.where, bf16[144,1024]{1,0:T(8,128)(2,1)S(1)} %collective-permute-done.28.refs_0_, bf16[144,1024]{1,0:T(8,128)(2,1)S(1)} %collective-permute-done.29.refs_1_, ...), custom_call_target="tpu_custom_call" | custom-call | flops 1610612736 | bytes 2097152 | tf_op jit(solution)/shard_map/expert/pallas_call | solution.py:257
  134.9 0.8 collective-permute-done.33
  136.2 1.4 collective-permute-done.37
  137.8 1.8 %collective-permute-start.38 = (bf16[128,1024]{1,0:T(8,128)(2,1)S(1)}, bf16[128,1024]{1,0:T(8,128)(2,1)S(1)}, u32[]{:S(2)}, u32[]{:S(2)}) collective-permute-start(bf16[128,1024]{1,0:T(8,128)(2,1)S(1)} %get-tuple-element.158), channel_id=1, source_target_pairs={{0,3},{1,2},{2,1},{3,0},{4,7},{5,6},{6,5},{7,4},{8,11},{9,10},{10,... | collective-permute-start | bytes 786440 | tf_op jit(solution)/shard_map/ppermute | solution.py:35
  139.6 6.4 %expert.9 = (bf16[128,1024]{1,0:T(8,128)(2,1)S(1)}, bf16[128,1024]{1,0:T(8,128)(2,1)S(1)}) custom-call(s32[1]{0:T(128)} %bitcast.1.where, bf16[144,1024]{1,0:T(8,128)(2,1)S(1)} %collective-permute-done.35.refs_0_, bf16[144,1024]{1,0:T(8,128)(2,1)S(1)} %collective-permute-done.36.refs_1_, bf16[1,1024,2048]{2,1,0:T(8,128)(2,1)} %refs_2_.3, ...), custom_call_target="tpu_custom_call" | custom-call | flops 805306368 | bytes 1048576 | tf_op jit(solution)/shard_map/expert/pallas_call | solution.py:257
  146.1 1.1 collective-permute-done.38
  147.4 1.3 collective-permute-done.41
  149.4 0.7 collective-permute-start.40
  150.1 1.7 collective-permute-start.39
  151.8 1.5 collective-permute-start.42
  153.3 1.0 collective-permute-done.19
  154.3 8.6 %collective-permute-done.40.refs_3_ = bf16[128,1024]{1,0:T(8,128)(2,1)S(1)} collective-permute-done((bf16[128,1024]{1,0:T(8,128)(2,1)S(1)}, bf16[128,1024]{1,0:T(8,128)(2,1)S(1)}, u32[]{:S(2)}, u32[]{:S(2)}) %collective-permute-start.40) | collective-permute-done | bytes 262176 | tf_op jit(solution)/shard_map/ppermute | solution.py:35
  162.9 1.8 %collective-permute-done.39.refs_2_ = bf16[128,1024]{1,0:T(8,128)(2,1)S(1)} collective-permute-done((bf16[128,1024]{1,0:T(8,128)(2,1)S(1)}, bf16[128,1024]{1,0:T(8,128)(2,1)S(1)}, u32[]{:S(2)}, u32[]{:S(2)}) %collective-permute-start.39) | collective-permute-done | bytes 262176 | tf_op jit(solution)/shard_map/ppermute | solution.py:35
  164.7 1.2 collective-permute-done.42.refs_4_
  165.9 4.7 %project.1 = bf16[128,4096]{1,0:T(8,128)(2,1)} custom-call(s32[1]{0:T(128)} %bitcast.where, f32[128,1024]{1,0:T(8,128)S(1)} %convert_add_fusion.refs_0_, bf16[128,1024]{1,0:T(8,128)(2,1)S(1)} %collective-permute-done.27.refs_1_, bf16[128,1024]{1,0:T(8,128)(2,1)S(1)} %collective-permute-done.39.refs_2_, ...), custom_call_target="tpu_custom_call" | custom-call | flops 1073741824 | bytes 8388608 | tf_op jit(solution)/shard_map/project/pallas_call | solution.py:319
  (72 shorter events, 9.5 us)
Async XLA Ops:
  6.5 1.2 copy-start
  6.5 86.4 %all-gather.5.cloned.1.call-start = ((), (), s32[]{:S(2)}) async-start(), calls=%async_computation | async-start | bytes 2359296 | tf_op jit(solution)/shard_map/all_gather | solution.py:369
  8.5 140.3 %all-gather.7.cloned.1.call-start = ((), (), s32[]{:S(2)}) async-start(), calls=%async_computation.1 | async-start | bytes 6291456 | tf_op jit(solution)/shard_map/all_gather | solution.py:432
  9.6 26.6 %collective-permute-start.3 = (bf16[128,1024]{1,0:T(8,128)(2,1)S(1)}, bf16[128,1024]{1,0:T(8,128)(2,1)S(1)}, u32[]{:S(2)}, u32[]{:S(2)}) collective-permute-start(bf16[128,1024]{1,0:T(8,128)(2,1)S(1)} %get-tuple-element.156.refs_2_), channel_id=1, source_target_pairs={{0,1},{1,0},{2,3},{3,2},{4,5},{5,4},{6,7},{7,6},{8,9},{9,8},{10,11... | collective-permute-start | bytes 786440 | tf_op jit(solution)/shard_map/ppermute | solution.py:35
  12.7 19.0 %collective-permute-start.1 = (bf16[128,1024]{1,0:T(8,128)(2,1)S(1)}, bf16[128,1024]{1,0:T(8,128)(2,1)S(1)}, u32[]{:S(2)}, u32[]{:S(2)}) collective-permute-start(bf16[128,1024]{1,0:T(8,128)(2,1)S(1)} %get-tuple-element.156.refs_2_), channel_id=1, source_target_pairs={{0,4},{1,5},{2,6},{3,7},{4,0},{5,1},{6,2},{7,3},{8,12},{9,13},{10,... | collective-permute-start | bytes 786440 | tf_op jit(solution)/shard_map/ppermute | solution.py:35
  15.3 15.7 %collective-permute-start = (bf16[128,1024]{1,0:T(8,128)(2,1)S(1)}, bf16[128,1024]{1,0:T(8,128)(2,1)S(1)}, u32[]{:S(2)}, u32[]{:S(2)}) collective-permute-start(bf16[128,1024]{1,0:T(8,128)(2,1)S(1)} %get-tuple-element.156.refs_2_), channel_id=1, source_target_pairs={{0,2},{1,3},{2,0},{3,1},{4,6},{5,7},{6,4},{7,5},{8,10},{9,11},{10,... | collective-permute-start | bytes 786440 | tf_op jit(solution)/shard_map/ppermute | solution.py:35
  16.9 1.2 copy-start.1
  19.0 24.5 %collective-permute-start.5 = (bf16[128,2048]{1,0:T(8,128)(2,1)S(1)}, bf16[128,2048]{1,0:T(8,128)(2,1)S(1)}, u32[]{:S(2)}, u32[]{:S(2)}) collective-permute-start(bf16[128,2048]{1,0:T(8,128)(2,1)S(1)} %get-tuple-element.85), channel_id=1, source_target_pairs={{0,16},{16,0},{1,17},{17,1},{2,18},{18,2},{3,19},{19,3},{4,20},{20... | collective-permute-start | bytes 1572872 | tf_op jit(solution)/shard_map/ppermute | solution.py:31
  31.7 9.7 %collective-permute-start.2 = (bf16[128,1024]{1,0:T(8,128)(2,1)S(1)}, bf16[128,1024]{1,0:T(8,128)(2,1)S(1)}, u32[]{:S(2)}, u32[]{:S(2)}) collective-permute-start(bf16[128,1024]{1,0:T(8,128)(2,1)S(1)} %collective-permute-done.1.refs_10_), channel_id=1, source_target_pairs={{0,2},{1,3},{2,0},{3,1},{4,6},{5,7},{6,4},{7,5},{8,10},{9,11},{10,... | collective-permute-start | bytes 786440 | tf_op jit(solution)/shard_map/ppermute | solution.py:35
  34.2 9.2 %collective-permute-start.4 = (bf16[128,1024]{1,0:T(8,128)(2,1)S(1)}, bf16[128,1024]{1,0:T(8,128)(2,1)S(1)}, u32[]{:S(2)}, u32[]{:S(2)}) collective-permute-start(bf16[128,1024]{1,0:T(8,128)(2,1)S(1)} %collective-permute-done.refs_6_), channel_id=1, source_target_pairs={{0,1},{1,0},{2,3},{3,2},{4,5},{5,4},{6,7},{7,6},{8,9},{9,8},{10,11... | collective-permute-start | bytes 786440 | tf_op jit(solution)/shard_map/ppermute | solution.py:35
  34.2 17.5 %collective-permute-start.9 = (bf16[128,1024]{1,0:T(8,128)(2,1)S(1)}, bf16[128,1024]{1,0:T(8,128)(2,1)S(1)}, u32[]{:S(2)}, u32[]{:S(2)}) collective-permute-start(bf16[128,1024]{1,0:T(8,128)(2,1)S(1)} %collective-permute-done.1.refs_10_), channel_id=1, source_target_pairs={{0,1},{1,0},{2,3},{3,2},{4,5},{5,4},{6,7},{7,6},{8,9},{9,8},{10,11... | collective-permute-start | bytes 786440 | tf_op jit(solution)/shard_map/ppermute | solution.py:35
  36.3 15.5 %collective-permute-start.10 = (bf16[128,1024]{1,0:T(8,128)(2,1)S(1)}, bf16[128,1024]{1,0:T(8,128)(2,1)S(1)}, u32[]{:S(2)}, u32[]{:S(2)}) collective-permute-start(bf16[128,1024]{1,0:T(8,128)(2,1)S(1)} %collective-permute-done.1.refs_10_), channel_id=1, source_target_pairs={{0,8},{8,0},{1,9},{9,1},{2,10},{10,2},{3,11},{11,3},{4,12},{12,4},... | collective-permute-start | bytes 786440 | tf_op jit(solution)/shard_map/ppermute | solution.py:27
  41.4 10.9 %collective-permute-start.7 = (bf16[128,1024]{1,0:T(8,128)(2,1)S(1)}, bf16[128,1024]{1,0:T(8,128)(2,1)S(1)}, u32[]{:S(2)}, u32[]{:S(2)}) collective-permute-start(bf16[128,1024]{1,0:T(8,128)(2,1)S(1)} %collective-permute-done.refs_6_), channel_id=1, source_target_pairs={{0,8},{8,0},{1,9},{9,1},{2,10},{10,2},{3,11},{11,3},{4,12},{12,4},... | collective-permute-start | bytes 786440 | tf_op jit(solution)/shard_map/ppermute | solution.py:27
  43.5 17.5 %collective-permute-start.12 = (bf16[128,1024]{1,0:T(8,128)(2,1)S(1)}, bf16[128,1024]{1,0:T(8,128)(2,1)S(1)}, u32[]{:S(2)}, u32[]{:S(2)}) collective-permute-start(bf16[128,1024]{1,0:T(8,128)(2,1)S(1)} %collective-permute-done.2.refs_2_), channel_id=1, source_target_pairs={{0,1},{1,0},{2,3},{3,2},{4,5},{5,4},{6,7},{7,6},{8,9},{9,8},{10,11... | collective-permute-start | bytes 786440 | tf_op jit(solution)/shard_map/ppermute | solution.py:35
  43.5 17.6 %collective-permute-start.6 = (bf16[128,1024]{1,0:T(8,128)(2,1)S(1)}, bf16[128,1024]{1,0:T(8,128)(2,1)S(1)}, u32[]{:S(2)}, u32[]{:S(2)}) collective-permute-start(bf16[128,1024]{1,0:T(8,128)(2,1)S(1)} %collective-permute-done.3.refs_3_), channel_id=1, source_target_pairs={{0,8},{8,0},{1,9},{9,1},{2,10},{10,2},{3,11},{11,3},{4,12},{12,4},... | collective-permute-start | bytes 786440 | tf_op jit(solution)/shard_map/ppermute | solution.py:27
  51.8 9.3 %collective-permute-start.11 = (bf16[128,1024]{1,0:T(8,128)(2,1)S(1)}, bf16[128,1024]{1,0:T(8,128)(2,1)S(1)}, u32[]{:S(2)}, u32[]{:S(2)}) collective-permute-start(bf16[128,1024]{1,0:T(8,128)(2,1)S(1)} %collective-permute-done.9.refs_11_), channel_id=1, source_target_pairs={{0,8},{8,0},{1,9},{9,1},{2,10},{10,2},{3,11},{11,3},{4,12},{12,4},... | collective-permute-start | bytes 786440 | tf_op jit(solution)/shard_map/ppermute | solution.py:27
  51.8 9.3 %collective-permute-start.8 = (bf16[128,1024]{1,0:T(8,128)(2,1)S(1)}, bf16[128,1024]{1,0:T(8,128)(2,1)S(1)}, u32[]{:S(2)}, u32[]{:S(2)}) collective-permute-start(bf16[128,1024]{1,0:T(8,128)(2,1)S(1)} %collective-permute-done.4.refs_7_), channel_id=1, source_target_pairs={{0,8},{8,0},{1,9},{9,1},{2,10},{10,2},{3,11},{11,3},{4,12},{12,4},... | collective-permute-start | bytes 786440 | tf_op jit(solution)/shard_map/ppermute | solution.py:27
  52.3 9.8 %collective-permute-start.13 = (bf16[128,1024]{1,0:T(8,128)(2,1)S(1)}, bf16[128,1024]{1,0:T(8,128)(2,1)S(1)}, u32[]{:S(2)}, u32[]{:S(2)}) collective-permute-start(bf16[128,1024]{1,0:T(8,128)(2,1)S(1)} %collective-permute-done.2.refs_2_), channel_id=1, source_target_pairs={{0,8},{8,0},{1,9},{9,1},{2,10},{10,2},{3,11},{11,3},{4,12},{12,4},... | collective-permute-start | bytes 786440 | tf_op jit(solution)/shard_map/ppermute | solution.py:27
  61.0 1.5 collective-permute-start.14
  63.0 8.7 %collective-permute-start.15 = (bf16[128,1024]{1,0:T(8,128)(2,1)S(1)}, bf16[128,1024]{1,0:T(8,128)(2,1)S(1)}, u32[]{:S(2)}, u32[]{:S(2)}) collective-permute-start(bf16[128,1024]{1,0:T(8,128)(2,1)S(1)} %get-tuple-element.92), channel_id=1, source_target_pairs={{0,16},{16,0},{1,17},{17,1},{2,18},{18,2},{3,19},{19,3},{4,20},{20... | collective-permute-start | bytes 786440 | tf_op jit(solution)/shard_map/ppermute | solution.py:31
  71.7 5.9 %collective-permute-start.16 = (bf16[144,1024]{1,0:T(8,128)(2,1)S(1)}, bf16[144,1024]{1,0:T(8,128)(2,1)S(1)}, u32[]{:S(2)}, u32[]{:S(2)}) collective-permute-start(bf16[144,1024]{1,0:T(8,128)(2,1)S(1)} %finish_latent.1.refs_0_), channel_id=1, source_target_pairs={{0,8},{8,0},{1,9},{9,1},{2,10},{10,2},{3,11},{11,3},{4,12},{12,4},... | collective-permute-start | bytes 884744 | tf_op jit(solution)/shard_map/ppermute | solution.py:27
  71.8 18.1 %collective-permute-start.18 = (bf16[144,1024]{1,0:T(8,128)(2,1)S(1)}, bf16[144,1024]{1,0:T(8,128)(2,1)S(1)}, u32[]{:S(2)}, u32[]{:S(2)}) collective-permute-start(bf16[144,1024]{1,0:T(8,128)(2,1)S(1)} %finish_latent.1.refs_0_), channel_id=1, source_target_pairs={{0,4},{1,5},{2,6},{3,7},{4,0},{5,1},{6,2},{7,3},{8,12},{9,13},{10,... | collective-permute-start | bytes 884744 | tf_op jit(solution)/shard_map/ppermute | solution.py:35
  77.7 15.3 %collective-permute-start.17 = (bf16[144,1024]{1,0:T(8,128)(2,1)S(1)}, bf16[144,1024]{1,0:T(8,128)(2,1)S(1)}, u32[]{:S(2)}, u32[]{:S(2)}) collective-permute-start(bf16[144,1024]{1,0:T(8,128)(2,1)S(1)} %finish_latent.1.refs_0_), channel_id=1, source_target_pairs={{0,2},{1,3},{2,0},{3,1},{4,6},{5,7},{6,4},{7,5},{8,10},{9,11},{10,... | collective-permute-start | bytes 884744 | tf_op jit(solution)/shard_map/ppermute | solution.py:35
  93.0 1.6 collective-permute-start.21
  93.1 2.0 %collective-permute-start.20 = (bf16[144,1024]{1,0:T(8,128)(2,1)S(1)}, bf16[144,1024]{1,0:T(8,128)(2,1)S(1)}, u32[]{:S(2)}, u32[]{:S(2)}) collective-permute-start(bf16[144,1024]{1,0:T(8,128)(2,1)S(1)} %collective-permute-done.18.refs_0_), channel_id=1, source_target_pairs={{0,8},{8,0},{1,9},{9,1},{2,10},{10,2},{3,11},{11,3},{4,12},{12,4},... | collective-permute-start | bytes 884744 | tf_op jit(solution)/shard_map/ppermute | solution.py:27
  93.6 11.3 %collective-permute-start.23 = (bf16[144,1024]{1,0:T(8,128)(2,1)S(1)}, bf16[144,1024]{1,0:T(8,128)(2,1)S(1)}, u32[]{:S(2)}, u32[]{:S(2)}) collective-permute-start(bf16[144,1024]{1,0:T(8,128)(2,1)S(1)} %collective-permute-done.18.refs_0_), channel_id=1, source_target_pairs={{0,1},{1,0},{2,3},{3,2},{4,5},{5,4},{6,7},{7,6},{8,9},{9,8},{10,11... | collective-permute-start | bytes 884744 | tf_op jit(solution)/shard_map/ppermute | solution.py:35
  93.6 11.3 %collective-permute-start.22 = (bf16[144,1024]{1,0:T(8,128)(2,1)S(1)}, bf16[144,1024]{1,0:T(8,128)(2,1)S(1)}, u32[]{:S(2)}, u32[]{:S(2)}) collective-permute-start(bf16[144,1024]{1,0:T(8,128)(2,1)S(1)} %collective-permute-done.18.refs_0_), channel_id=1, source_target_pairs={{0,2},{1,3},{2,0},{3,1},{4,6},{5,7},{6,4},{7,5},{8,10},{9,11},{10,... | collective-permute-start | bytes 884744 | tf_op jit(solution)/shard_map/ppermute | solution.py:35
  104.9 2.7 %collective-permute-start.26 = (bf16[256,1024]{1,0:T(8,128)(2,1)S(1)}, bf16[256,1024]{1,0:T(8,128)(2,1)S(1)}, u32[]{:S(2)}, u32[]{:S(2)}) collective-permute-start(bf16[256,1024]{1,0:T(8,128)(2,1)S(1)} %get-tuple-element.119), channel_id=1, source_target_pairs={{0,8},{8,0},{1,9},{9,1},{2,10},{10,2},{3,11},{11,3},{4,12},{12,4},... | collective-permute-start | bytes 1572872 | tf_op jit(solution)/shard_map/ppermute | solution.py:27
  105.0 13.6 %collective-permute-start.29 = (bf16[144,1024]{1,0:T(8,128)(2,1)S(1)}, bf16[144,1024]{1,0:T(8,128)(2,1)S(1)}, u32[]{:S(2)}, u32[]{:S(2)}) collective-permute-start(bf16[144,1024]{1,0:T(8,128)(2,1)S(1)} %finish_latent.1.refs_0_), channel_id=1, source_target_pairs={{0,1},{1,0},{2,3},{3,2},{4,5},{5,4},{6,7},{7,6},{8,9},{9,8},{10,11... | collective-permute-start | bytes 884744 | tf_op jit(solution)/shard_map/ppermute | solution.py:35
  105.7 15.0 %collective-permute-start.28 = (bf16[144,1024]{1,0:T(8,128)(2,1)S(1)}, bf16[144,1024]{1,0:T(8,128)(2,1)S(1)}, u32[]{:S(2)}, u32[]{:S(2)}) collective-permute-start(bf16[144,1024]{1,0:T(8,128)(2,1)S(1)} %collective-permute-done.22.refs_0_), channel_id=1, source_target_pairs={{0,1},{1,0},{2,3},{3,2},{4,5},{5,4},{6,7},{7,6},{8,9},{9,8},{10,11... | collective-permute-start | bytes 884744 | tf_op jit(solution)/shard_map/ppermute | solution.py:35
  107.0 2.0 %collective-permute-start.24 = (bf16[144,1024]{1,0:T(8,128)(2,1)S(1)}, bf16[144,1024]{1,0:T(8,128)(2,1)S(1)}, u32[]{:S(2)}, u32[]{:S(2)}) collective-permute-start(bf16[144,1024]{1,0:T(8,128)(2,1)S(1)} %collective-permute-done.22.refs_0_), channel_id=1, source_target_pairs={{0,8},{8,0},{1,9},{9,1},{2,10},{10,2},{3,11},{11,3},{4,12},{12,4},... | collective-permute-start | bytes 884744 | tf_op jit(solution)/shard_map/ppermute | solution.py:27
  107.0 2.0 %collective-permute-start.25 = (bf16[144,1024]{1,0:T(8,128)(2,1)S(1)}, bf16[144,1024]{1,0:T(8,128)(2,1)S(1)}, u32[]{:S(2)}, u32[]{:S(2)}) collective-permute-start(bf16[144,1024]{1,0:T(8,128)(2,1)S(1)} %collective-permute-done.23.refs_1_), channel_id=1, source_target_pairs={{0,8},{8,0},{1,9},{9,1},{2,10},{10,2},{3,11},{11,3},{4,12},{12,4},... | collective-permute-start | bytes 884744 | tf_op jit(solution)/shard_map/ppermute | solution.py:27
  107.6 13.1 %collective-permute-start.27 = (bf16[128,1024]{1,0:T(8,128)(2,1)S(1)}, bf16[128,1024]{1,0:T(8,128)(2,1)S(1)}, u32[]{:S(2)}, u32[]{:S(2)}) collective-permute-start(bf16[128,1024]{1,0:T(8,128)(2,1)S(1)} %add_convert_fusion.6), channel_id=1, source_target_pairs={{0,2},{1,3},{2,0},{3,1},{4,6},{5,7},{6,4},{7,5},{8,10},{9,11},{10,... | collective-permute-start | bytes 786440 | tf_op jit(solution)/shard_map/ppermute | solution.py:35
  120.7 1.9 %collective-permute-start.32 = (bf16[256,1024]{1,0:T(8,128)(2,1)S(1)}, bf16[256,1024]{1,0:T(8,128)(2,1)S(1)}, u32[]{:S(2)}, u32[]{:S(2)}) collective-permute-start(bf16[256,1024]{1,0:T(8,128)(2,1)S(1)} %get-tuple-element.132), channel_id=1, source_target_pairs={{0,8},{8,0},{1,9},{9,1},{2,10},{10,2},{3,11},{11,3},{4,12},{12,4},... | collective-permute-start | bytes 1572872 | tf_op jit(solution)/shard_map/ppermute | solution.py:27
  120.7 14.2 %collective-permute-start.35 = (bf16[144,1024]{1,0:T(8,128)(2,1)S(1)}, bf16[144,1024]{1,0:T(8,128)(2,1)S(1)}, u32[]{:S(2)}, u32[]{:S(2)}) collective-permute-start(bf16[144,1024]{1,0:T(8,128)(2,1)S(1)} %collective-permute-done.17.refs_1_), channel_id=1, source_target_pairs={{0,1},{1,0},{2,3},{3,2},{4,5},{5,4},{6,7},{7,6},{8,9},{9,8},{10,11... | collective-permute-start | bytes 884744 | tf_op jit(solution)/shard_map/ppermute | solution.py:35
  121.4 3.8 %collective-permute-start.30 = (bf16[144,1024]{1,0:T(8,128)(2,1)S(1)}, bf16[144,1024]{1,0:T(8,128)(2,1)S(1)}, u32[]{:S(2)}, u32[]{:S(2)}) collective-permute-start(bf16[144,1024]{1,0:T(8,128)(2,1)S(1)} %collective-permute-done.28.refs_0_), channel_id=1, source_target_pairs={{0,8},{8,0},{1,9},{9,1},{2,10},{10,2},{3,11},{11,3},{4,12},{12,4},... | collective-permute-start | bytes 884744 | tf_op jit(solution)/shard_map/ppermute | solution.py:27
  121.6 3.5 %collective-permute-start.31 = (bf16[144,1024]{1,0:T(8,128)(2,1)S(1)}, bf16[144,1024]{1,0:T(8,128)(2,1)S(1)}, u32[]{:S(2)}, u32[]{:S(2)}) collective-permute-start(bf16[144,1024]{1,0:T(8,128)(2,1)S(1)} %collective-permute-done.29.refs_1_), channel_id=1, source_target_pairs={{0,8},{8,0},{1,9},{9,1},{2,10},{10,2},{3,11},{11,3},{4,12},{12,4},... | collective-permute-start | bytes 884744 | tf_op jit(solution)/shard_map/ppermute | solution.py:27
  122.8 12.1 %collective-permute-start.34 = (bf16[128,1024]{1,0:T(8,128)(2,1)S(1)}, bf16[128,1024]{1,0:T(8,128)(2,1)S(1)}, u32[]{:S(2)}, u32[]{:S(2)}) collective-permute-start(bf16[128,1024]{1,0:T(8,128)(2,1)S(1)} %get-tuple-element.159), channel_id=1, source_target_pairs={{0,2},{1,3},{2,0},{3,1},{4,6},{5,7},{6,4},{7,5},{8,10},{9,11},{10,... | collective-permute-start | bytes 786440 | tf_op jit(solution)/shard_map/ppermute | solution.py:35
  123.8 11.9 %collective-permute-start.33 = (bf16[128,1024]{1,0:T(8,128)(2,1)S(1)}, bf16[128,1024]{1,0:T(8,128)(2,1)S(1)}, u32[]{:S(2)}, u32[]{:S(2)}) collective-permute-start(bf16[128,1024]{1,0:T(8,128)(2,1)S(1)} %get-tuple-element.160), channel_id=1, source_target_pairs={{0,1},{1,0},{2,3},{3,2},{4,5},{5,4},{6,7},{7,6},{8,9},{9,8},{10,11... | collective-permute-start | bytes 786440 | tf_op jit(solution)/shard_map/ppermute | solution.py:35
  135.7 1.9 %collective-permute-start.37 = (bf16[256,1024]{1,0:T(8,128)(2,1)S(1)}, bf16[256,1024]{1,0:T(8,128)(2,1)S(1)}, u32[]{:S(2)}, u32[]{:S(2)}) collective-permute-start(bf16[256,1024]{1,0:T(8,128)(2,1)S(1)} %get-tuple-element.142), channel_id=1, source_target_pairs={{0,8},{8,0},{1,9},{9,1},{2,10},{10,2},{3,11},{11,3},{4,12},{12,4},... | collective-permute-start | bytes 1572872 | tf_op jit(solution)/shard_map/ppermute | solution.py:27
  135.7 3.9 %collective-permute-start.36 = (bf16[144,1024]{1,0:T(8,128)(2,1)S(1)}, bf16[144,1024]{1,0:T(8,128)(2,1)S(1)}, u32[]{:S(2)}, u32[]{:S(2)}) collective-permute-start(bf16[144,1024]{1,0:T(8,128)(2,1)S(1)} %collective-permute-done.35.refs_0_), channel_id=1, source_target_pairs={{0,8},{8,0},{1,9},{9,1},{2,10},{10,2},{3,11},{11,3},{4,12},{12,4},... | collective-permute-start | bytes 884744 | tf_op jit(solution)/shard_map/ppermute | solution.py:27
  137.8 9.3 %collective-permute-start.38 = (bf16[128,1024]{1,0:T(8,128)(2,1)S(1)}, bf16[128,1024]{1,0:T(8,128)(2,1)S(1)}, u32[]{:S(2)}, u32[]{:S(2)}) collective-permute-start(bf16[128,1024]{1,0:T(8,128)(2,1)S(1)} %get-tuple-element.158), channel_id=1, source_target_pairs={{0,3},{1,2},{2,1},{3,0},{4,7},{5,6},{6,5},{7,4},{8,11},{9,10},{10,... | collective-permute-start | bytes 786440 | tf_op jit(solution)/shard_map/ppermute | solution.py:35
  147.1 1.5 collective-permute-start.41
  148.8 17.1 %collective-permute-start.43 = (bf16[2,8,256,512]{3,2,1,0:T(8,128)(2,1)}, bf16[2,8,256,512]{3,2,1,0:T(8,128)(2,1)S(1)}, u32[]{:S(2)}, u32[]{:S(2)}) collective-permute-start(bf16[2,8,256,512]{3,2,1,0:T(8,128)(2,1)} %bitcast.6), channel_id=1, source_target_pairs={{0,8},{8,0},{1,9},{9,1},{2,10},{10,2},{3,11},{11,3},{4,12},{12,4},... | collective-permute-start | bytes 12582920 | tf_op jit(solution)/shard_map/ppermute | solution.py:27
  149.0 5.3 %collective-permute-start.19 = (bf16[128,1024]{1,0:T(8,128)(2,1)S(1)}, bf16[128,1024]{1,0:T(8,128)(2,1)S(1)}, u32[]{:S(2)}, u32[]{:S(2)}) collective-permute-start(bf16[128,1024]{1,0:T(8,128)(2,1)S(1)} %get-tuple-element.99), channel_id=1, source_target_pairs={{0,8},{8,0},{1,9},{9,1},{2,10},{10,2},{3,11},{11,3},{4,12},{12,4},... | collective-permute-start | bytes 786440 | tf_op jit(solution)/shard_map/ppermute | solution.py:27
  149.4 13.6 %collective-permute-start.40 = (bf16[128,1024]{1,0:T(8,128)(2,1)S(1)}, bf16[128,1024]{1,0:T(8,128)(2,1)S(1)}, u32[]{:S(2)}, u32[]{:S(2)}) collective-permute-start(bf16[128,1024]{1,0:T(8,128)(2,1)S(1)} %get-tuple-element.157), channel_id=1, source_target_pairs={{0,1},{1,0},{2,3},{3,2},{4,5},{5,4},{6,7},{7,6},{8,9},{9,8},{10,11... | collective-permute-start | bytes 786440 | tf_op jit(solution)/shard_map/ppermute | solution.py:35
  150.1 14.6 %collective-permute-start.39 = (bf16[128,1024]{1,0:T(8,128)(2,1)S(1)}, bf16[128,1024]{1,0:T(8,128)(2,1)S(1)}, u32[]{:S(2)}, u32[]{:S(2)}) collective-permute-start(bf16[128,1024]{1,0:T(8,128)(2,1)S(1)} %add_convert_fusion.2), channel_id=1, source_target_pairs={{0,4},{1,5},{2,6},{3,7},{4,0},{5,1},{6,2},{7,3},{8,12},{9,13},{10,... | collective-permute-start | bytes 786440 | tf_op jit(solution)/shard_map/ppermute | solution.py:35
  151.8 14.1 %collective-permute-start.42 = (bf16[128,1024]{1,0:T(8,128)(2,1)S(1)}, bf16[128,1024]{1,0:T(8,128)(2,1)S(1)}, u32[]{:S(2)}, u32[]{:S(2)}) collective-permute-start(bf16[128,1024]{1,0:T(8,128)(2,1)S(1)} %add_convert_fusion), channel_id=1, source_target_pairs={{0,3},{1,2},{2,1},{3,0},{4,7},{5,6},{6,5},{7,4},{8,11},{9,10},{10,... | collective-permute-start | bytes 786440 | tf_op jit(solution)/shard_map/ppermute | solution.py:35
Sparse Core Ops, SparseCore 0:
  9.5 65.3 all-gather.4
  93.1 54.2 all-gather.6

commit v18 on v15

--- a/solution.py
+++ b/solution.py
@@ -266,7 +266,7 @@
         ]
         + [pltpu.VMEM(w.shape[1:], w.dtype) for w in weights]
         + [pltpu.SemaphoreType.DMA((hidden_width // width + 2 + latent_width // (2 * width),))],
-        compiler_params=pltpu.CompilerParams(vmem_limit_bytes=28 * mebi),
+        compiler_params=pltpu.CompilerParams(vmem_limit_bytes=32 * mebi),
         cost_estimate=pl.CostEstimate(
             flops=3 * rows * latent_width * hidden_width // 2,
             bytes_accessed=4 * rows * latent_width,
@@ -427,19 +427,19 @@
     def homeward(*previous):
         return [send(p, sums[p], 2 * p[0] + p[1]) for p in previous if p not in special]
 
-    run([(0, 0)], *[(near, k) for k in near if k], (travel, "up"))
+    run([(0, 0)], *[(near, k) for k in near if k], (far, 0), (travel, "up"))
     sides = [[i, i + 1] for i in range(0, lax.axis_size("rep"), 2)]
     both_sides = lax.all_gather(travel.pop("up"), "rep", axis=0, axis_index_groups=sides)
-    previous = [(2, 0), (1, 0)]
+    previous = [(2, 0), (1, 0), (0, 1)]
     run(previous, *[start_near(3)] * (last >= 3), start_far(2))
     for k in range(3, steps):
-        coming = homeward(*previous) + [start_far(k)] + [(far, 0)] * (k == last)
+        coming = homeward(*previous) + [start_far(k)]
         if k + 1 < steps and k + 1 not in near:
             coming.append(start_near(k + 1))
         previous = [(k, 0), (k - 1, 1)]
         run(previous, *coming)
     run(
-        [(last, 1), (0, 1)],
+        [(last, 1)],
         send((last - 1, 1), sums[last - 1, 1], 1),
         send((last, 0), sums[last, 0], 2),
         start_far(1),
@@ -452,7 +452,7 @@
     send("shared", shared, 2 * last - 2)
     sums[1, 1] = sums[1, 1].astype(jnp.bfloat16)
     both_sides = after(both_sides, sums[1, 1], shared)
-    homeward((0, 1), (1, 1))
+    homeward((1, 1))
     *terms, swapped_sides = join(sums[0, 0], *travel.values(), swap_cores(both_sides))
     both_sides = pltpu.with_memory_space_constraint(both_sides, pltpu.HBM)
     return project(group, terms, both_sides, swapped_sides)

time: 167 us -> 168 us (level)
  waiting for transfers between devices: 58.3 us -> 62.2 us
  starting transfers between devices: 38.8 us -> 36 us
    ppermute x21, waiting for transfers between devices: 46.5 us -> 49.4 us  [swap_ep(): lax.ppermute(array, 'ep', [(i, i ^ mask) for i in range(lax.axis_size('ep...]
    ppermute x21, starting transfers between devices: 31.3 us -> 28.5 us  [swap_ep(): lax.ppermute(array, 'ep', [(i, i ^ mask) for i in range(lax.axis_size('ep...]
    ppermute x21, waiting for transfers between devices: 4.06 us -> 5.94 us  [swap_cores(): return lax.ppermute(array, 'grp', [(0, 1), (1, 0)])]
  transfers between devices with their start and end apart: 46 -> 46, of which waited for: 18 -> 20; matrix products, arithmetic and copies ran while one was open for 2% -> 2% of each run, Pallas kernels for 26% -> 26%
where the time goes in v18:
time: 168 us
  waiting for transfers between devices  62.2 us (37%)
  Pallas kernels  48.9 us (29%)
  starting transfers between devices  36 us (21%)
  between operations  13.7 us (8%)
  local copies, waits for them, and re-layouts  4.24 us (3%)
  other arithmetic  3 us (2%)
    ppermute x21, waiting for transfers between devices, swap_ep(): lax.ppermute(array, 'ep', [(i, i ^ mask) for i in range(lax.axis_size('ep...  49.4 us
    pallas_call x5, Pallas kernels, expert_apply(): pl.pallas_call(functools.partial(expert_kernel, positions, count), out_sh...  41.9 us
    ppermute x21, starting transfers between devices, swap_ep(): lax.ppermute(array, 'ep', [(i, i ^ mask) for i in range(lax.axis_size('ep...  28.5 us
    ppermute x2, waiting for transfers between devices, swap_reps(): lax.ppermute(array, 'rep', [(i, i ^ 1) for i in range(lax.axis_size('rep'...  6.83 us
    ppermute x21, waiting for transfers between devices, swap_cores(): return lax.ppermute(array, 'grp', [(0, 1), (1, 0)])  5.94 us
    pallas_call x1, Pallas kernels, project(): pl.pallas_call(project_kernel, in_specs=[in_smem] + [in_vmem] * len(terms...  4.7 us
    ppermute x21, starting transfers between devices, swap_cores(): return lax.ppermute(array, 'grp', [(0, 1), (1, 0)])  4.28 us
  transfers between devices with their start and end apart: 46, of which 20 were waited for; matrix products, arithmetic and copies ran while one was open for 2% of the time, Pallas kernels for 26%

profile of v18, /device:TPU:0, one launch (start us, length us, event | category | flops | bytes accessed | tf_op | source)
XLA Modules:
  0.0 168.0 jit_solution(17175851102802463956)
XLA Ops:
  6.5 1.2 copy-done
  7.8 0.7 constant_dynamic-slice_fusion
  8.6 1.1 constant_dynamic-slice_fusion.1
  9.6 3.1 %collective-permute-start = (bf16[128,1024]{1,0:T(8,128)(2,1)S(1)}, bf16[128,1024]{1,0:T(8,128)(2,1)S(1)}, u32[]{:S(2)}, u32[]{:S(2)}) collective-permute-start(bf16[128,1024]{1,0:T(8,128)(2,1)S(1)} %get-tuple-element.158.refs_2_), channel_id=1, source_target_pairs={{0,2},{1,3},{2,0},{3,1},{4,6},{5,7},{6,4},{7,5},{8,10},{9,11},{10,... | collective-permute-start | bytes 786440 | tf_op jit(solution)/shard_map/ppermute | solution.py:35
  12.7 1.5 collective-permute-start.4
  14.3 2.6 %collective-permute-start.2 = (bf16[128,1024]{1,0:T(8,128)(2,1)S(1)}, bf16[128,1024]{1,0:T(8,128)(2,1)S(1)}, u32[]{:S(2)}, u32[]{:S(2)}) collective-permute-start(bf16[128,1024]{1,0:T(8,128)(2,1)S(1)} %get-tuple-element.158.refs_2_), channel_id=1, source_target_pairs={{0,4},{1,5},{2,6},{3,7},{4,0},{5,1},{6,2},{7,3},{8,12},{9,13},{10,... | collective-permute-start | bytes 786440 | tf_op jit(solution)/shard_map/ppermute | solution.py:35
  16.9 1.2 copy-done.1
  18.1 0.8 split_columns.1
  19.0 1.6 collective-permute-start.5
  20.5 0.7 fusion.1
  21.2 2.5 %collective-permute-done.refs_6_ = bf16[128,1024]{1,0:T(8,128)(2,1)S(1)} collective-permute-done((bf16[128,1024]{1,0:T(8,128)(2,1)S(1)}, bf16[128,1024]{1,0:T(8,128)(2,1)S(1)}, u32[]{:S(2)}, u32[]{:S(2)}) %collective-permute-start) | collective-permute-done | bytes 262176 | tf_op jit(solution)/shard_map/ppermute | solution.py:35
  23.7 3.8 %collective-permute-start.1 = (bf16[128,1024]{1,0:T(8,128)(2,1)S(1)}, bf16[128,1024]{1,0:T(8,128)(2,1)S(1)}, u32[]{:S(2)}, u32[]{:S(2)}) collective-permute-start(bf16[128,1024]{1,0:T(8,128)(2,1)S(1)} %collective-permute-done.refs_6_), channel_id=1, source_target_pairs={{0,1},{1,0},{2,3},{3,2},{4,5},{5,4},{6,7},{7,6},{8,9},{9,8},{10,11... | collective-permute-start | bytes 786440 | tf_op jit(solution)/shard_map/ppermute | solution.py:35
  27.5 0.7 fusion
  28.2 0.7 select_reduce_fusion.weights
  28.9 4.1 %collective-permute-done.2.refs_10_ = bf16[128,1024]{1,0:T(8,128)(2,1)S(1)} collective-permute-done((bf16[128,1024]{1,0:T(8,128)(2,1)S(1)}, bf16[128,1024]{1,0:T(8,128)(2,1)S(1)}, u32[]{:S(2)}, u32[]{:S(2)}) %collective-permute-start.2) | collective-permute-done | bytes 262176 | tf_op jit(solution)/shard_map/ppermute | solution.py:35
  33.1 0.9 collective-permute-start.3
  34.5 7.3 %collective-permute-done.3.refs_2_ = bf16[128,1024]{1,0:T(8,128)(2,1)S(1)} collective-permute-done((bf16[128,1024]{1,0:T(8,128)(2,1)S(1)}, bf16[128,1024]{1,0:T(8,128)(2,1)S(1)}, u32[]{:S(2)}, u32[]{:S(2)}) %collective-permute-start.3) | collective-permute-done | bytes 262176 | tf_op jit(solution)/shard_map/ppermute | solution.py:35
  43.5 10.0 %collective-permute-done.12.refs_3_ = bf16[128,1024]{1,0:T(8,128)(2,1)S(1)} collective-permute-done((bf16[128,1024]{1,0:T(8,128)(2,1)S(1)}, bf16[128,1024]{1,0:T(8,128)(2,1)S(1)}, u32[]{:S(2)}, u32[]{:S(2)}) %collective-permute-start.12) | collective-permute-done | bytes 262176 | tf_op jit(solution)/shard_map/ppermute | solution.py:35
  53.5 1.0 down_project.2.refs_6_
  55.5 1.6 collective-permute-start.15
  57.1 6.8 %collective-permute-done.15.arrived = bf16[128,1024]{1,0:T(8,128)(2,1)S(1)} collective-permute-done((bf16[128,1024]{1,0:T(8,128)(2,1)S(1)}, bf16[128,1024]{1,0:T(8,128)(2,1)S(1)}, u32[]{:S(2)}, u32[]{:S(2)}) %collective-permute-start.15) | collective-permute-done | bytes 262176 | tf_op jit(solution)/shard_map/ppermute | solution.py:31
  64.0 1.0 collective-permute-start.19
  65.1 1.4 collective-permute-start.18
  66.6 6.4 %expert.5 = (bf16[128,1024]{1,0:T(8,128)(2,1)S(1)}, bf16[128,1024]{1,0:T(8,128)(2,1)S(1)}) custom-call(s32[1]{0:T(128)} %bitcast.1.where, bf16[144,1024]{1,0:T(8,128)(2,1)S(1)} %finish_latent.1.refs_0_, bf16[144,1024]{1,0:T(8,128)(2,1)S(1)} %collective-permute-done.16.refs_1_, bf16[1,1024,2048]{2,1,0:T(8,128)(2,1)} %refs_2_.5, ...), custom_call_target="tpu_custom_call" | custom-call | flops 805306368 | bytes 1048576 | tf_op jit(solution)/shard_map/expert/pallas_call | solution.py:257
  73.5 7.9 %collective-permute-done.18.refs_0_ = bf16[144,1024]{1,0:T(8,128)(2,1)S(1)} collective-permute-done((bf16[144,1024]{1,0:T(8,128)(2,1)S(1)}, bf16[144,1024]{1,0:T(8,128)(2,1)S(1)}, u32[]{:S(2)}, u32[]{:S(2)}) %collective-permute-start.18) | collective-permute-done | bytes 294944 | tf_op jit(solution)/shard_map/ppermute | solution.py:35
  82.1 1.1 collective-permute-start.25
  83.9 12.9 %expert.6 = (bf16[128,1024]{1,0:T(8,128)(2,1)S(1)}, bf16[128,1024]{1,0:T(8,128)(2,1)S(1)}, bf16[128,1024]{1,0:T(8,128)(2,1)S(1)}, bf16[384,1024]{1,0:T(8,128)(2,1)S(1)}) custom-call(s32[1]{0:T(128)} %bitcast.1.where, bf16[144,1024]{1,0:T(8,128)(2,1)S(1)} %collective-permute-done.18.refs_0_, bf16[144,1024]{1,0:T(8,128)(2,1)S(1)} %collective-permute-done.17.refs_1_, ...), custom_call_target="tpu_custom_call" | custom-call | flops 2415919104 | bytes 3145728 | tf_op jit(solution)/shard_map/expert/pallas_call | solution.py:257
  97.1 1.1 collective-permute-start.31
  99.4 1.2 collective-permute-start.30
  100.6 1.1 collective-permute-start.29
  101.7 9.5 %expert.7 = (bf16[128,1024]{1,0:T(8,128)(2,1)S(1)}, bf16[128,1024]{1,0:T(8,128)(2,1)S(1)}, bf16[256,1024]{1,0:T(8,128)(2,1)S(1)}) custom-call(s32[1]{0:T(128)} %bitcast.1.where, bf16[144,1024]{1,0:T(8,128)(2,1)S(1)} %collective-permute-done.24.refs_0_, bf16[144,1024]{1,0:T(8,128)(2,1)S(1)} %collective-permute-done.25.refs_1_, ...), custom_call_target="tpu_custom_call" | custom-call | flops 1610612736 | bytes 2097152 | tf_op jit(solution)/shard_map/expert/pallas_call | solution.py:257
  111.3 0.7 collective-permute-done.30.refs_2_
  112.0 1.1 collective-permute-start.36
  114.1 1.4 collective-permute-start.35
  115.5 0.9 collective-permute-start.34
  116.4 6.6 %expert.8 = (bf16[128,1024]{1,0:T(8,128)(2,1)S(1)}, bf16[128,1024]{1,0:T(8,128)(2,1)S(1)}) custom-call(s32[1]{0:T(128)} %bitcast.1.where, bf16[144,1024]{1,0:T(8,128)(2,1)S(1)} %collective-permute-done.31.refs_0_, bf16[144,1024]{1,0:T(8,128)(2,1)S(1)} %collective-permute-done.32.refs_1_, bf16[1,1024,2048]{2,1,0:T(8,128)(2,1)} %refs_2_.5, ...), custom_call_target="tpu_custom_call" | custom-call | flops 805306368 | bytes 1048576 | tf_op jit(solution)/shard_map/expert/pallas_call | solution.py:257
  123.1 4.0 %collective-permute-done.34 = bf16[128,1024]{1,0:T(8,128)(2,1)S(1)} collective-permute-done((bf16[128,1024]{1,0:T(8,128)(2,1)S(1)}, bf16[128,1024]{1,0:T(8,128)(2,1)S(1)}, u32[]{:S(2)}, u32[]{:S(2)}) %collective-permute-start.34) | collective-permute-done | bytes 262176 | tf_op jit(solution)/shard_map/ppermute | solution.py:35
  127.5 1.0 collective-permute-done.38
  128.6 1.8 %collective-permute-start.39 = (bf16[128,1024]{1,0:T(8,128)(2,1)S(1)}, bf16[128,1024]{1,0:T(8,128)(2,1)S(1)}, u32[]{:S(2)}, u32[]{:S(2)}) collective-permute-start(bf16[128,1024]{1,0:T(8,128)(2,1)S(1)} %add_convert_fusion.2), channel_id=1, source_target_pairs={{0,3},{1,2},{2,1},{3,0},{4,7},{5,6},{6,5},{7,4},{8,11},{9,10},{10,... | collective-permute-start | bytes 786440 | tf_op jit(solution)/shard_map/ppermute | solution.py:35
  130.4 6.4 %expert.9 = (bf16[128,1024]{1,0:T(8,128)(2,1)S(1)}, bf16[128,1024]{1,0:T(8,128)(2,1)S(1)}) custom-call(s32[1]{0:T(128)} %bitcast.1.where, bf16[144,1024]{1,0:T(8,128)(2,1)S(1)} %collective-permute-done.36.refs_0_, bf16[144,1024]{1,0:T(8,128)(2,1)S(1)} %collective-permute-done.37.refs_1_, bf16[1,1024,2048]{2,1,0:T(8,128)(2,1)} %refs_2_.5, ...), custom_call_target="tpu_custom_call" | custom-call | flops 805306368 | bytes 1048576 | tf_op jit(solution)/shard_map/expert/pallas_call | solution.py:257
  136.8 1.1 collective-permute-done.39
  138.2 1.3 collective-permute-done.41
  140.2 2.4 %collective-permute-start.40 = (bf16[128,1024]{1,0:T(8,128)(2,1)S(1)}, bf16[128,1024]{1,0:T(8,128)(2,1)S(1)}, u32[]{:S(2)}, u32[]{:S(2)}) collective-permute-start(bf16[128,1024]{1,0:T(8,128)(2,1)S(1)} %add_convert_fusion.1), channel_id=1, source_target_pairs={{0,4},{1,5},{2,6},{3,7},{4,0},{5,1},{6,2},{7,3},{8,12},{9,13},{10,... | collective-permute-start | bytes 786440 | tf_op jit(solution)/shard_map/ppermute | solution.py:35
  142.5 1.2 collective-permute-start.42
  143.7 1.3 collective-permute-done.20
  145.1 10.0 %collective-permute-done.40.refs_3_ = bf16[128,1024]{1,0:T(8,128)(2,1)S(1)} collective-permute-done((bf16[128,1024]{1,0:T(8,128)(2,1)S(1)}, bf16[128,1024]{1,0:T(8,128)(2,1)S(1)}, u32[]{:S(2)}, u32[]{:S(2)}) %collective-permute-start.40) | collective-permute-done | bytes 262176 | tf_op jit(solution)/shard_map/ppermute | solution.py:35
  155.1 1.3 collective-permute-done.42.refs_4_
  156.4 4.7 %project.1 = bf16[128,4096]{1,0:T(8,128)(2,1)} custom-call(s32[1]{0:T(128)} %bitcast.where, f32[128,1024]{1,0:T(8,128)S(1)} %convert_add_fusion.refs_0_, bf16[128,1024]{1,0:T(8,128)(2,1)S(1)} %collective-permute-done.29.refs_1_, bf16[128,1024]{1,0:T(8,128)(2,1)S(1)} %collective-permute-done.30.refs_2_, ...), custom_call_target="tpu_custom_call" | custom-call | flops 1073741824 | bytes 8388608 | tf_op jit(solution)/shard_map/project/pallas_call | solution.py:319
  (72 shorter events, 9.3 us)
Async XLA Ops:
  6.5 1.2 copy-start
  6.5 74.9 %all-gather.5.cloned.1.call-start = ((), (), s32[]{:S(2)}) async-start(), calls=%async_computation | async-start | bytes 2359296 | tf_op jit(solution)/shard_map/all_gather | solution.py:369
  8.5 131.1 %all-gather.7.cloned.1.call-start = ((), (), s32[]{:S(2)}) async-start(), calls=%async_computation.1 | async-start | bytes 6291456 | tf_op jit(solution)/shard_map/all_gather | solution.py:432
  9.6 14.1 %collective-permute-start = (bf16[128,1024]{1,0:T(8,128)(2,1)S(1)}, bf16[128,1024]{1,0:T(8,128)(2,1)S(1)}, u32[]{:S(2)}, u32[]{:S(2)}) collective-permute-start(bf16[128,1024]{1,0:T(8,128)(2,1)S(1)} %get-tuple-element.158.refs_2_), channel_id=1, source_target_pairs={{0,2},{1,3},{2,0},{3,1},{4,6},{5,7},{6,4},{7,5},{8,10},{9,11},{10,... | collective-permute-start | bytes 786440 | tf_op jit(solution)/shard_map/ppermute | solution.py:35
  12.7 21.3 %collective-permute-start.4 = (bf16[128,1024]{1,0:T(8,128)(2,1)S(1)}, bf16[128,1024]{1,0:T(8,128)(2,1)S(1)}, u32[]{:S(2)}, u32[]{:S(2)}) collective-permute-start(bf16[128,1024]{1,0:T(8,128)(2,1)S(1)} %get-tuple-element.158.refs_2_), channel_id=1, source_target_pairs={{0,1},{1,0},{2,3},{3,2},{4,5},{5,4},{6,7},{7,6},{8,9},{9,8},{10,11... | collective-permute-start | bytes 786440 | tf_op jit(solution)/shard_map/ppermute | solution.py:35
  14.3 18.8 %collective-permute-start.2 = (bf16[128,1024]{1,0:T(8,128)(2,1)S(1)}, bf16[128,1024]{1,0:T(8,128)(2,1)S(1)}, u32[]{:S(2)}, u32[]{:S(2)}) collective-permute-start(bf16[128,1024]{1,0:T(8,128)(2,1)S(1)} %get-tuple-element.158.refs_2_), channel_id=1, source_target_pairs={{0,4},{1,5},{2,6},{3,7},{4,0},{5,1},{6,2},{7,3},{8,12},{9,13},{10,... | collective-permute-start | bytes 786440 | tf_op jit(solution)/shard_map/ppermute | solution.py:35
  16.9 1.2 copy-start.1
  19.0 15.5 %collective-permute-start.5 = (bf16[128,2048]{1,0:T(8,128)(2,1)S(1)}, bf16[128,2048]{1,0:T(8,128)(2,1)S(1)}, u32[]{:S(2)}, u32[]{:S(2)}) collective-permute-start(bf16[128,2048]{1,0:T(8,128)(2,1)S(1)} %get-tuple-element.86), channel_id=1, source_target_pairs={{0,16},{16,0},{1,17},{17,1},{2,18},{18,2},{3,19},{19,3},{4,20},{20... | collective-permute-start | bytes 1572872 | tf_op jit(solution)/shard_map/ppermute | solution.py:31
  23.7 9.3 %collective-permute-start.1 = (bf16[128,1024]{1,0:T(8,128)(2,1)S(1)}, bf16[128,1024]{1,0:T(8,128)(2,1)S(1)}, u32[]{:S(2)}, u32[]{:S(2)}) collective-permute-start(bf16[128,1024]{1,0:T(8,128)(2,1)S(1)} %collective-permute-done.refs_6_), channel_id=1, source_target_pairs={{0,1},{1,0},{2,3},{3,2},{4,5},{5,4},{6,7},{7,6},{8,9},{9,8},{10,11... | collective-permute-start | bytes 786440 | tf_op jit(solution)/shard_map/ppermute | solution.py:35
  33.1 8.8 %collective-permute-start.3 = (bf16[128,1024]{1,0:T(8,128)(2,1)S(1)}, bf16[128,1024]{1,0:T(8,128)(2,1)S(1)}, u32[]{:S(2)}, u32[]{:S(2)}) collective-permute-start(bf16[128,1024]{1,0:T(8,128)(2,1)S(1)} %collective-permute-done.2.refs_10_), channel_id=1, source_target_pairs={{0,2},{1,3},{2,0},{3,1},{4,6},{5,7},{6,4},{7,5},{8,10},{9,11},{10,... | collective-permute-start | bytes 786440 | tf_op jit(solution)/shard_map/ppermute | solution.py:35
  34.0 8.5 %collective-permute-start.9 = (bf16[128,1024]{1,0:T(8,128)(2,1)S(1)}, bf16[128,1024]{1,0:T(8,128)(2,1)S(1)}, u32[]{:S(2)}, u32[]{:S(2)}) collective-permute-start(bf16[128,1024]{1,0:T(8,128)(2,1)S(1)} %collective-permute-done.2.refs_10_), channel_id=1, source_target_pairs={{0,1},{1,0},{2,3},{3,2},{4,5},{5,4},{6,7},{7,6},{8,9},{9,8},{10,11... | collective-permute-start | bytes 786440 | tf_op jit(solution)/shard_map/ppermute | solution.py:35
  34.0 9.0 %collective-permute-start.7 = (bf16[128,1024]{1,0:T(8,128)(2,1)S(1)}, bf16[128,1024]{1,0:T(8,128)(2,1)S(1)}, u32[]{:S(2)}, u32[]{:S(2)}) collective-permute-start(bf16[128,1024]{1,0:T(8,128)(2,1)S(1)} %collective-permute-done.refs_6_), channel_id=1, source_target_pairs={{0,8},{8,0},{1,9},{9,1},{2,10},{10,2},{3,11},{11,3},{4,12},{12,4},... | collective-permute-start | bytes 786440 | tf_op jit(solution)/shard_map/ppermute | solution.py:27
  34.0 9.1 %collective-permute-start.8 = (bf16[128,1024]{1,0:T(8,128)(2,1)S(1)}, bf16[128,1024]{1,0:T(8,128)(2,1)S(1)}, u32[]{:S(2)}, u32[]{:S(2)}) collective-permute-start(bf16[128,1024]{1,0:T(8,128)(2,1)S(1)} %collective-permute-done.1.refs_7_), channel_id=1, source_target_pairs={{0,8},{8,0},{1,9},{9,1},{2,10},{10,2},{3,11},{11,3},{4,12},{12,4},... | collective-permute-start | bytes 786440 | tf_op jit(solution)/shard_map/ppermute | solution.py:27
  41.8 11.7 %collective-permute-start.12 = (bf16[128,1024]{1,0:T(8,128)(2,1)S(1)}, bf16[128,1024]{1,0:T(8,128)(2,1)S(1)}, u32[]{:S(2)}, u32[]{:S(2)}) collective-permute-start(bf16[128,1024]{1,0:T(8,128)(2,1)S(1)} %collective-permute-done.3.refs_2_), channel_id=1, source_target_pairs={{0,1},{1,0},{2,3},{3,2},{4,5},{5,4},{6,7},{7,6},{8,9},{9,8},{10,11... | collective-permute-start | bytes 786440 | tf_op jit(solution)/shard_map/ppermute | solution.py:35
  42.5 11.0 %collective-permute-start.10 = (bf16[128,1024]{1,0:T(8,128)(2,1)S(1)}, bf16[128,1024]{1,0:T(8,128)(2,1)S(1)}, u32[]{:S(2)}, u32[]{:S(2)}) collective-permute-start(bf16[128,1024]{1,0:T(8,128)(2,1)S(1)} %collective-permute-done.2.refs_10_), channel_id=1, source_target_pairs={{0,8},{8,0},{1,9},{9,1},{2,10},{10,2},{3,11},{11,3},{4,12},{12,4},... | collective-permute-start | bytes 786440 | tf_op jit(solution)/shard_map/ppermute | solution.py:27
  42.5 11.0 %collective-permute-start.11 = (bf16[128,1024]{1,0:T(8,128)(2,1)S(1)}, bf16[128,1024]{1,0:T(8,128)(2,1)S(1)}, u32[]{:S(2)}, u32[]{:S(2)}) collective-permute-start(bf16[128,1024]{1,0:T(8,128)(2,1)S(1)} %collective-permute-done.9.refs_11_), channel_id=1, source_target_pairs={{0,8},{8,0},{1,9},{9,1},{2,10},{10,2},{3,11},{11,3},{4,12},{12,4},... | collective-permute-start | bytes 786440 | tf_op jit(solution)/shard_map/ppermute | solution.py:27
  43.0 10.5 %collective-permute-start.6 = (bf16[128,1024]{1,0:T(8,128)(2,1)S(1)}, bf16[128,1024]{1,0:T(8,128)(2,1)S(1)}, u32[]{:S(2)}, u32[]{:S(2)}) collective-permute-start(bf16[128,1024]{1,0:T(8,128)(2,1)S(1)} %collective-permute-done.4.refs_3_), channel_id=1, source_target_pairs={{0,8},{8,0},{1,9},{9,1},{2,10},{10,2},{3,11},{11,3},{4,12},{12,4},... | collective-permute-start | bytes 786440 | tf_op jit(solution)/shard_map/ppermute | solution.py:27
  43.1 11.4 %collective-permute-start.13 = (bf16[128,1024]{1,0:T(8,128)(2,1)S(1)}, bf16[128,1024]{1,0:T(8,128)(2,1)S(1)}, u32[]{:S(2)}, u32[]{:S(2)}) collective-permute-start(bf16[128,1024]{1,0:T(8,128)(2,1)S(1)} %collective-permute-done.3.refs_2_), channel_id=1, source_target_pairs={{0,8},{8,0},{1,9},{9,1},{2,10},{10,2},{3,11},{11,3},{4,12},{12,4},... | collective-permute-start | bytes 786440 | tf_op jit(solution)/shard_map/ppermute | solution.py:27
  53.5 1.5 collective-permute-start.14
  55.5 8.4 %collective-permute-start.15 = (bf16[128,1024]{1,0:T(8,128)(2,1)S(1)}, bf16[128,1024]{1,0:T(8,128)(2,1)S(1)}, u32[]{:S(2)}, u32[]{:S(2)}) collective-permute-start(bf16[128,1024]{1,0:T(8,128)(2,1)S(1)} %get-tuple-element.93), channel_id=1, source_target_pairs={{0,16},{16,0},{1,17},{17,1},{2,18},{18,2},{3,19},{19,3},{4,20},{20... | collective-permute-start | bytes 786440 | tf_op jit(solution)/shard_map/ppermute | solution.py:31
  64.0 2.6 %collective-permute-start.16 = (bf16[144,1024]{1,0:T(8,128)(2,1)S(1)}, bf16[144,1024]{1,0:T(8,128)(2,1)S(1)}, u32[]{:S(2)}, u32[]{:S(2)}) collective-permute-start(bf16[144,1024]{1,0:T(8,128)(2,1)S(1)} %finish_latent.1.refs_0_), channel_id=1, source_target_pairs={{0,8},{8,0},{1,9},{9,1},{2,10},{10,2},{3,11},{11,3},{4,12},{12,4},... | collective-permute-start | bytes 884744 | tf_op jit(solution)/shard_map/ppermute | solution.py:27
  64.0 9.4 %collective-permute-start.19 = (bf16[144,1024]{1,0:T(8,128)(2,1)S(1)}, bf16[144,1024]{1,0:T(8,128)(2,1)S(1)}, u32[]{:S(2)}, u32[]{:S(2)}) collective-permute-start(bf16[144,1024]{1,0:T(8,128)(2,1)S(1)} %finish_latent.1.refs_0_), channel_id=1, source_target_pairs={{0,1},{1,0},{2,3},{3,2},{4,5},{5,4},{6,7},{7,6},{8,9},{9,8},{10,11... | collective-permute-start | bytes 884744 | tf_op jit(solution)/shard_map/ppermute | solution.py:35
  65.1 16.3 %collective-permute-start.18 = (bf16[144,1024]{1,0:T(8,128)(2,1)S(1)}, bf16[144,1024]{1,0:T(8,128)(2,1)S(1)}, u32[]{:S(2)}, u32[]{:S(2)}) collective-permute-start(bf16[144,1024]{1,0:T(8,128)(2,1)S(1)} %finish_latent.1.refs_0_), channel_id=1, source_target_pairs={{0,4},{1,5},{2,6},{3,7},{4,0},{5,1},{6,2},{7,3},{8,12},{9,13},{10,... | collective-permute-start | bytes 884744 | tf_op jit(solution)/shard_map/ppermute | solution.py:35
  66.5 14.9 %collective-permute-start.17 = (bf16[144,1024]{1,0:T(8,128)(2,1)S(1)}, bf16[144,1024]{1,0:T(8,128)(2,1)S(1)}, u32[]{:S(2)}, u32[]{:S(2)}) collective-permute-start(bf16[144,1024]{1,0:T(8,128)(2,1)S(1)} %finish_latent.1.refs_0_), channel_id=1, source_target_pairs={{0,2},{1,3},{2,0},{3,1},{4,6},{5,7},{6,4},{7,5},{8,10},{9,11},{10,... | collective-permute-start | bytes 884744 | tf_op jit(solution)/shard_map/ppermute | solution.py:35
  81.4 1.8 %collective-permute-start.23 = (bf16[144,1024]{1,0:T(8,128)(2,1)S(1)}, bf16[144,1024]{1,0:T(8,128)(2,1)S(1)}, u32[]{:S(2)}, u32[]{:S(2)}) collective-permute-start(bf16[144,1024]{1,0:T(8,128)(2,1)S(1)} %collective-permute-done.19.refs_2_), channel_id=1, source_target_pairs={{0,8},{8,0},{1,9},{9,1},{2,10},{10,2},{3,11},{11,3},{4,12},{12,4},... | collective-permute-start | bytes 884744 | tf_op jit(solution)/shard_map/ppermute | solution.py:27
  81.5 2.0 %collective-permute-start.22 = (bf16[144,1024]{1,0:T(8,128)(2,1)S(1)}, bf16[144,1024]{1,0:T(8,128)(2,1)S(1)}, u32[]{:S(2)}, u32[]{:S(2)}) collective-permute-start(bf16[144,1024]{1,0:T(8,128)(2,1)S(1)} %collective-permute-done.17.refs_1_), channel_id=1, source_target_pairs={{0,8},{8,0},{1,9},{9,1},{2,10},{10,2},{3,11},{11,3},{4,12},{12,4},... | collective-permute-start | bytes 884744 | tf_op jit(solution)/shard_map/ppermute | solution.py:27
  82.0 1.9 %collective-permute-start.21 = (bf16[144,1024]{1,0:T(8,128)(2,1)S(1)}, bf16[144,1024]{1,0:T(8,128)(2,1)S(1)}, u32[]{:S(2)}, u32[]{:S(2)}) collective-permute-start(bf16[144,1024]{1,0:T(8,128)(2,1)S(1)} %collective-permute-done.18.refs_0_), channel_id=1, source_target_pairs={{0,8},{8,0},{1,9},{9,1},{2,10},{10,2},{3,11},{11,3},{4,12},{12,4},... | collective-permute-start | bytes 884744 | tf_op jit(solution)/shard_map/ppermute | solution.py:27
  82.1 14.8 %collective-permute-start.25 = (bf16[144,1024]{1,0:T(8,128)(2,1)S(1)}, bf16[144,1024]{1,0:T(8,128)(2,1)S(1)}, u32[]{:S(2)}, u32[]{:S(2)}) collective-permute-start(bf16[144,1024]{1,0:T(8,128)(2,1)S(1)} %collective-permute-done.18.refs_0_), channel_id=1, source_target_pairs={{0,1},{1,0},{2,3},{3,2},{4,5},{5,4},{6,7},{7,6},{8,9},{9,8},{10,11... | collective-permute-start | bytes 884744 | tf_op jit(solution)/shard_map/ppermute | solution.py:35
  83.2 13.7 %collective-permute-start.24 = (bf16[144,1024]{1,0:T(8,128)(2,1)S(1)}, bf16[144,1024]{1,0:T(8,128)(2,1)S(1)}, u32[]{:S(2)}, u32[]{:S(2)}) collective-permute-start(bf16[144,1024]{1,0:T(8,128)(2,1)S(1)} %collective-permute-done.18.refs_0_), channel_id=1, source_target_pairs={{0,2},{1,3},{2,0},{3,1},{4,6},{5,7},{6,4},{7,5},{8,10},{9,11},{10,... | collective-permute-start | bytes 884744 | tf_op jit(solution)/shard_map/ppermute | solution.py:35
  96.9 2.4 %collective-permute-start.28 = (bf16[384,1024]{1,0:T(8,128)(2,1)S(1)}, bf16[384,1024]{1,0:T(8,128)(2,1)S(1)}, u32[]{:S(2)}, u32[]{:S(2)}) collective-permute-start(bf16[384,1024]{1,0:T(8,128)(2,1)S(1)} %get-tuple-element.124), channel_id=1, source_target_pairs={{0,8},{8,0},{1,9},{9,1},{2,10},{10,2},{3,11},{11,3},{4,12},{12,4},... | collective-permute-start | bytes 2359304 | tf_op jit(solution)/shard_map/ppermute | solution.py:27
  97.1 14.2 %collective-permute-start.31 = (bf16[144,1024]{1,0:T(8,128)(2,1)S(1)}, bf16[144,1024]{1,0:T(8,128)(2,1)S(1)}, u32[]{:S(2)}, u32[]{:S(2)}) collective-permute-start(bf16[144,1024]{1,0:T(8,128)(2,1)S(1)} %collective-permute-done.24.refs_0_), channel_id=1, source_target_pairs={{0,1},{1,0},{2,3},{3,2},{4,5},{5,4},{6,7},{7,6},{8,9},{9,8},{10,11... | collective-permute-start | bytes 884744 | tf_op jit(solution)/shard_map/ppermute | solution.py:35
  98.2 3.5 %collective-permute-start.26 = (bf16[144,1024]{1,0:T(8,128)(2,1)S(1)}, bf16[144,1024]{1,0:T(8,128)(2,1)S(1)}, u32[]{:S(2)}, u32[]{:S(2)}) collective-permute-start(bf16[144,1024]{1,0:T(8,128)(2,1)S(1)} %collective-permute-done.24.refs_0_), channel_id=1, source_target_pairs={{0,8},{8,0},{1,9},{9,1},{2,10},{10,2},{3,11},{11,3},{4,12},{12,4},... | collective-permute-start | bytes 884744 | tf_op jit(solution)/shard_map/ppermute | solution.py:27
  98.3 3.4 %collective-permute-start.27 = (bf16[144,1024]{1,0:T(8,128)(2,1)S(1)}, bf16[144,1024]{1,0:T(8,128)(2,1)S(1)}, u32[]{:S(2)}, u32[]{:S(2)}) collective-permute-start(bf16[144,1024]{1,0:T(8,128)(2,1)S(1)} %collective-permute-done.25.refs_1_), channel_id=1, source_target_pairs={{0,8},{8,0},{1,9},{9,1},{2,10},{10,2},{3,11},{11,3},{4,12},{12,4},... | collective-permute-start | bytes 884744 | tf_op jit(solution)/shard_map/ppermute | solution.py:27
  99.4 12.6 %collective-permute-start.30 = (bf16[128,1024]{1,0:T(8,128)(2,1)S(1)}, bf16[128,1024]{1,0:T(8,128)(2,1)S(1)}, u32[]{:S(2)}, u32[]{:S(2)}) collective-permute-start(bf16[128,1024]{1,0:T(8,128)(2,1)S(1)} %get-tuple-element.159), channel_id=1, source_target_pairs={{0,1},{1,0},{2,3},{3,2},{4,5},{5,4},{6,7},{7,6},{8,9},{9,8},{10,11... | collective-permute-start | bytes 786440 | tf_op jit(solution)/shard_map/ppermute | solution.py:35
  100.6 11.4 %collective-permute-start.29 = (bf16[128,1024]{1,0:T(8,128)(2,1)S(1)}, bf16[128,1024]{1,0:T(8,128)(2,1)S(1)}, u32[]{:S(2)}, u32[]{:S(2)}) collective-permute-start(bf16[128,1024]{1,0:T(8,128)(2,1)S(1)} %get-tuple-element.160), channel_id=1, source_target_pairs={{0,2},{1,3},{2,0},{3,1},{4,6},{5,7},{6,4},{7,5},{8,10},{9,11},{10,... | collective-permute-start | bytes 786440 | tf_op jit(solution)/shard_map/ppermute | solution.py:35
  112.0 1.9 %collective-permute-start.33 = (bf16[256,1024]{1,0:T(8,128)(2,1)S(1)}, bf16[256,1024]{1,0:T(8,128)(2,1)S(1)}, u32[]{:S(2)}, u32[]{:S(2)}) collective-permute-start(bf16[256,1024]{1,0:T(8,128)(2,1)S(1)} %get-tuple-element.135), channel_id=1, source_target_pairs={{0,8},{8,0},{1,9},{9,1},{2,10},{10,2},{3,11},{11,3},{4,12},{12,4},... | collective-permute-start | bytes 1572872 | tf_op jit(solution)/shard_map/ppermute | solution.py:27
  112.0 11.1 %collective-permute-start.36 = (bf16[144,1024]{1,0:T(8,128)(2,1)S(1)}, bf16[144,1024]{1,0:T(8,128)(2,1)S(1)}, u32[]{:S(2)}, u32[]{:S(2)}) collective-permute-start(bf16[144,1024]{1,0:T(8,128)(2,1)S(1)} %collective-permute-done.17.refs_1_), channel_id=1, source_target_pairs={{0,1},{1,0},{2,3},{3,2},{4,5},{5,4},{6,7},{7,6},{8,9},{9,8},{10,11... | collective-permute-start | bytes 884744 | tf_op jit(solution)/shard_map/ppermute | solution.py:35
  113.1 3.3 %collective-permute-start.32 = (bf16[144,1024]{1,0:T(8,128)(2,1)S(1)}, bf16[144,1024]{1,0:T(8,128)(2,1)S(1)}, u32[]{:S(2)}, u32[]{:S(2)}) collective-permute-start(bf16[144,1024]{1,0:T(8,128)(2,1)S(1)} %collective-permute-done.31.refs_0_), channel_id=1, source_target_pairs={{0,8},{8,0},{1,9},{9,1},{2,10},{10,2},{3,11},{11,3},{4,12},{12,4},... | collective-permute-start | bytes 884744 | tf_op jit(solution)/shard_map/ppermute | solution.py:27
  114.1 9.0 %collective-permute-start.35 = (bf16[128,1024]{1,0:T(8,128)(2,1)S(1)}, bf16[128,1024]{1,0:T(8,128)(2,1)S(1)}, u32[]{:S(2)}, u32[]{:S(2)}) collective-permute-start(bf16[128,1024]{1,0:T(8,128)(2,1)S(1)} %get-tuple-element.161), channel_id=1, source_target_pairs={{0,2},{1,3},{2,0},{3,1},{4,6},{5,7},{6,4},{7,5},{8,10},{9,11},{10,... | collective-permute-start | bytes 786440 | tf_op jit(solution)/shard_map/ppermute | solution.py:35
  115.5 11.5 %collective-permute-start.34 = (bf16[128,1024]{1,0:T(8,128)(2,1)S(1)}, bf16[128,1024]{1,0:T(8,128)(2,1)S(1)}, u32[]{:S(2)}, u32[]{:S(2)}) collective-permute-start(bf16[128,1024]{1,0:T(8,128)(2,1)S(1)} %get-tuple-element.162), channel_id=1, source_target_pairs={{0,1},{1,0},{2,3},{3,2},{4,5},{5,4},{6,7},{7,6},{8,9},{9,8},{10,11... | collective-permute-start | bytes 786440 | tf_op jit(solution)/shard_map/ppermute | solution.py:35
  127.0 1.5 collective-permute-start.38
  127.0 3.4 %collective-permute-start.37 = (bf16[144,1024]{1,0:T(8,128)(2,1)S(1)}, bf16[144,1024]{1,0:T(8,128)(2,1)S(1)}, u32[]{:S(2)}, u32[]{:S(2)}) collective-permute-start(bf16[144,1024]{1,0:T(8,128)(2,1)S(1)} %collective-permute-done.36.refs_0_), channel_id=1, source_target_pairs={{0,8},{8,0},{1,9},{9,1},{2,10},{10,2},{3,11},{11,3},{4,12},{12,4},... | collective-permute-start | bytes 884744 | tf_op jit(solution)/shard_map/ppermute | solution.py:27
  128.6 9.3 %collective-permute-start.39 = (bf16[128,1024]{1,0:T(8,128)(2,1)S(1)}, bf16[128,1024]{1,0:T(8,128)(2,1)S(1)}, u32[]{:S(2)}, u32[]{:S(2)}) collective-permute-start(bf16[128,1024]{1,0:T(8,128)(2,1)S(1)} %add_convert_fusion.2), channel_id=1, source_target_pairs={{0,3},{1,2},{2,1},{3,0},{4,7},{5,6},{6,5},{7,4},{8,11},{9,10},{10,... | collective-permute-start | bytes 786440 | tf_op jit(solution)/shard_map/ppermute | solution.py:35
  137.9 1.5 collective-permute-start.41
  139.6 16.9 %collective-permute-start.43 = (bf16[2,8,256,512]{3,2,1,0:T(8,128)(2,1)}, bf16[2,8,256,512]{3,2,1,0:T(8,128)(2,1)S(1)}, u32[]{:S(2)}, u32[]{:S(2)}) collective-permute-start(bf16[2,8,256,512]{3,2,1,0:T(8,128)(2,1)} %bitcast.6), channel_id=1, source_target_pairs={{0,8},{8,0},{1,9},{9,1},{2,10},{10,2},{3,11},{11,3},{4,12},{12,4},... | collective-permute-start | bytes 12582920 | tf_op jit(solution)/shard_map/ppermute | solution.py:27
  139.8 5.3 %collective-permute-start.20 = (bf16[128,1024]{1,0:T(8,128)(2,1)S(1)}, bf16[128,1024]{1,0:T(8,128)(2,1)S(1)}, u32[]{:S(2)}, u32[]{:S(2)}) collective-permute-start(bf16[128,1024]{1,0:T(8,128)(2,1)S(1)} %get-tuple-element.100), channel_id=1, source_target_pairs={{0,8},{8,0},{1,9},{9,1},{2,10},{10,2},{3,11},{11,3},{4,12},{12,4},... | collective-permute-start | bytes 786440 | tf_op jit(solution)/shard_map/ppermute | solution.py:27
  140.2 15.0 %collective-permute-start.40 = (bf16[128,1024]{1,0:T(8,128)(2,1)S(1)}, bf16[128,1024]{1,0:T(8,128)(2,1)S(1)}, u32[]{:S(2)}, u32[]{:S(2)}) collective-permute-start(bf16[128,1024]{1,0:T(8,128)(2,1)S(1)} %add_convert_fusion.1), channel_id=1, source_target_pairs={{0,4},{1,5},{2,6},{3,7},{4,0},{5,1},{6,2},{7,3},{8,12},{9,13},{10,... | collective-permute-start | bytes 786440 | tf_op jit(solution)/shard_map/ppermute | solution.py:35
  142.5 13.9 %collective-permute-start.42 = (bf16[128,1024]{1,0:T(8,128)(2,1)S(1)}, bf16[128,1024]{1,0:T(8,128)(2,1)S(1)}, u32[]{:S(2)}, u32[]{:S(2)}) collective-permute-start(bf16[128,1024]{1,0:T(8,128)(2,1)S(1)} %add_convert_fusion), channel_id=1, source_target_pairs={{0,3},{1,2},{2,1},{3,0},{4,7},{5,6},{6,5},{7,4},{8,11},{9,10},{10,... | collective-permute-start | bytes 786440 | tf_op jit(solution)/shard_map/ppermute | solution.py:35
Sparse Core Ops, SparseCore 0:
  9.5 59.2 all-gather.4
  81.5 56.4 all-gather.6

commit v19 on v18

--- a/solution.py
+++ b/solution.py
@@ -431,7 +431,7 @@
     sides = [[i, i + 1] for i in range(0, lax.axis_size("rep"), 2)]
     both_sides = lax.all_gather(travel.pop("up"), "rep", axis=0, axis_index_groups=sides)
     previous = [(2, 0), (1, 0), (0, 1)]
-    run(previous, *[start_near(3)] * (last >= 3), start_far(2))
+    run(previous, *[start_near(3)] * (last >= 3), start_far(2), start_far(1))
     for k in range(3, steps):
         coming = homeward(*previous) + [start_far(k)]
         if k + 1 < steps and k + 1 not in near:
@@ -439,12 +439,11 @@
         previous = [(k, 0), (k - 1, 1)]
         run(previous, *coming)
     run(
-        [(last, 1)],
+        [(last, 1), (1, 1)],
         send((last - 1, 1), sums[last - 1, 1], 1),
         send((last, 0), sums[last, 0], 2),
-        start_far(1),
     )
-    run([(1, 1)], send((last, 1), sums[last, 1], 3))
+    send((last, 1), sums[last, 1], 3)
     shared = sums[last - 1, 0]
     for name in ((last - 1, 1), (last, 0), (last, 1)):
         shared += travel.pop(name).astype(jnp.float32)

time: 168 us -> 167 us (level)
  Pallas kernels: 48.9 us -> 45.6 us
  waiting for transfers between devices: 62.2 us -> 64.5 us
    pallas_call x5 -> x4, Pallas kernels: 41.9 us -> 38.6 us  [expert_apply(): pl.pallas_call(functools.partial(expert_kernel, positions, count), out_sh...]
    ppermute x21 -> x20, waiting for transfers between devices: 5.94 us -> 6.61 us  [swap_cores(): return lax.ppermute(array, 'grp', [(0, 1), (1, 0)])]
    ppermute x21 -> x20, starting transfers between devices: 4.28 us -> 3.92 us  [swap_cores(): return lax.ppermute(array, 'grp', [(0, 1), (1, 0)])]
  transfers between devices with their start and end apart: 46 -> 45, of which waited for: 20 -> 17; matrix products, arithmetic and copies ran while one was open for 2% -> 2% of each run, Pallas kernels for 26% -> 24%
where the time goes in v19:
time: 167 us
  waiting for transfers between devices  64.5 us (39%)
  Pallas kernels  45.6 us (27%)
  starting transfers between devices  36.1 us (22%)
  between operations  13.7 us (8%)
  local copies, waits for them, and re-layouts  4.24 us (3%)
  other arithmetic  3.05 us (2%)
    ppermute x21, waiting for transfers between devices, swap_ep(): lax.ppermute(array, 'ep', [(i, i ^ mask) for i in range(lax.axis_size('ep...  51 us
    pallas_call x4, Pallas kernels, expert_apply(): pl.pallas_call(functools.partial(expert_kernel, positions, count), out_sh...  38.6 us
    ppermute x21, starting transfers between devices, swap_ep(): lax.ppermute(array, 'ep', [(i, i ^ mask) for i in range(lax.axis_size('ep...  29 us
    ppermute x2, waiting for transfers between devices, swap_reps(): lax.ppermute(array, 'rep', [(i, i ^ 1) for i in range(lax.axis_size('rep'...  6.83 us
    ppermute x20, waiting for transfers between devices, swap_cores(): return lax.ppermute(array, 'grp', [(0, 1), (1, 0)])  6.61 us
    pallas_call x1, Pallas kernels, project(): pl.pallas_call(project_kernel, in_specs=[in_smem] + [in_vmem] * len(terms...  4.7 us
    ppermute x20, starting transfers between devices, swap_cores(): return lax.ppermute(array, 'grp', [(0, 1), (1, 0)])  3.92 us
  transfers between devices with their start and end apart: 45, of which 17 were waited for; matrix products, arithmetic and copies ran while one was open for 2% of the time, Pallas kernels for 24%

profile of v19, /device:TPU:0, one launch (start us, length us, event | category | flops | bytes accessed | tf_op | source)
XLA Modules:
  0.0 167.2 jit_solution(9494525732063069536)
XLA Ops:
  6.5 1.2 copy-done
  7.8 0.7 constant_dynamic-slice_fusion
  8.6 1.1 constant_dynamic-slice_fusion.1
  9.6 3.1 %collective-permute-start = (bf16[128,1024]{1,0:T(8,128)(2,1)S(1)}, bf16[128,1024]{1,0:T(8,128)(2,1)S(1)}, u32[]{:S(2)}, u32[]{:S(2)}) collective-permute-start(bf16[128,1024]{1,0:T(8,128)(2,1)S(1)} %get-tuple-element.152.refs_2_), channel_id=1, source_target_pairs={{0,2},{1,3},{2,0},{3,1},{4,6},{5,7},{6,4},{7,5},{8,10},{9,11},{10,... | collective-permute-start | bytes 786440 | tf_op jit(solution)/shard_map/ppermute | solution.py:35
  12.7 1.5 collective-permute-start.4
  14.3 2.6 %collective-permute-start.2 = (bf16[128,1024]{1,0:T(8,128)(2,1)S(1)}, bf16[128,1024]{1,0:T(8,128)(2,1)S(1)}, u32[]{:S(2)}, u32[]{:S(2)}) collective-permute-start(bf16[128,1024]{1,0:T(8,128)(2,1)S(1)} %get-tuple-element.152.refs_2_), channel_id=1, source_target_pairs={{0,4},{1,5},{2,6},{3,7},{4,0},{5,1},{6,2},{7,3},{8,12},{9,13},{10,... | collective-permute-start | bytes 786440 | tf_op jit(solution)/shard_map/ppermute | solution.py:35
  16.9 1.2 copy-done.1
  18.1 0.8 split_columns.1
  19.0 1.6 collective-permute-start.5
  20.5 0.7 fusion.1
  21.2 2.5 %collective-permute-done.refs_6_ = bf16[128,1024]{1,0:T(8,128)(2,1)S(1)} collective-permute-done((bf16[128,1024]{1,0:T(8,128)(2,1)S(1)}, bf16[128,1024]{1,0:T(8,128)(2,1)S(1)}, u32[]{:S(2)}, u32[]{:S(2)}) %collective-permute-start) | collective-permute-done | bytes 262176 | tf_op jit(solution)/shard_map/ppermute | solution.py:35
  23.7 3.8 %collective-permute-start.1 = (bf16[128,1024]{1,0:T(8,128)(2,1)S(1)}, bf16[128,1024]{1,0:T(8,128)(2,1)S(1)}, u32[]{:S(2)}, u32[]{:S(2)}) collective-permute-start(bf16[128,1024]{1,0:T(8,128)(2,1)S(1)} %collective-permute-done.refs_6_), channel_id=1, source_target_pairs={{0,1},{1,0},{2,3},{3,2},{4,5},{5,4},{6,7},{7,6},{8,9},{9,8},{10,11... | collective-permute-start | bytes 786440 | tf_op jit(solution)/shard_map/ppermute | solution.py:35
  27.5 0.7 fusion
  28.2 0.7 select_reduce_fusion.weights
  28.9 4.1 %collective-permute-done.2.refs_10_ = bf16[128,1024]{1,0:T(8,128)(2,1)S(1)} collective-permute-done((bf16[128,1024]{1,0:T(8,128)(2,1)S(1)}, bf16[128,1024]{1,0:T(8,128)(2,1)S(1)}, u32[]{:S(2)}, u32[]{:S(2)}) %collective-permute-start.2) | collective-permute-done | bytes 262176 | tf_op jit(solution)/shard_map/ppermute | solution.py:35
  33.1 0.9 collective-permute-start.3
  34.5 7.3 %collective-permute-done.3.refs_2_ = bf16[128,1024]{1,0:T(8,128)(2,1)S(1)} collective-permute-done((bf16[128,1024]{1,0:T(8,128)(2,1)S(1)}, bf16[128,1024]{1,0:T(8,128)(2,1)S(1)}, u32[]{:S(2)}, u32[]{:S(2)}) %collective-permute-start.3) | collective-permute-done | bytes 262176 | tf_op jit(solution)/shard_map/ppermute | solution.py:35
  41.8 0.7 collective-permute-start.12
  43.5 10.0 %collective-permute-done.12.refs_3_ = bf16[128,1024]{1,0:T(8,128)(2,1)S(1)} collective-permute-done((bf16[128,1024]{1,0:T(8,128)(2,1)S(1)}, bf16[128,1024]{1,0:T(8,128)(2,1)S(1)}, u32[]{:S(2)}, u32[]{:S(2)}) %collective-permute-start.12) | collective-permute-done | bytes 262176 | tf_op jit(solution)/shard_map/ppermute | solution.py:35
  53.5 1.0 down_project.2.refs_6_
  55.5 1.6 collective-permute-start.15
  57.1 6.8 %collective-permute-done.15.arrived = bf16[128,1024]{1,0:T(8,128)(2,1)S(1)} collective-permute-done((bf16[128,1024]{1,0:T(8,128)(2,1)S(1)}, bf16[128,1024]{1,0:T(8,128)(2,1)S(1)}, u32[]{:S(2)}, u32[]{:S(2)}) %collective-permute-start.15) | collective-permute-done | bytes 262176 | tf_op jit(solution)/shard_map/ppermute | solution.py:31
  64.0 1.0 collective-permute-start.19
  65.1 1.4 collective-permute-start.18
  66.6 6.4 %expert.4 = (bf16[128,1024]{1,0:T(8,128)(2,1)S(1)}, bf16[128,1024]{1,0:T(8,128)(2,1)S(1)}) custom-call(s32[1]{0:T(128)} %bitcast.1.where, bf16[144,1024]{1,0:T(8,128)(2,1)S(1)} %finish_latent.1.refs_0_, bf16[144,1024]{1,0:T(8,128)(2,1)S(1)} %collective-permute-done.16.refs_1_, bf16[1,1024,2048]{2,1,0:T(8,128)(2,1)} %refs_4_.5, ...), custom_call_target="tpu_custom_call" | custom-call | flops 805306368 | bytes 1048576 | tf_op jit(solution)/shard_map/expert/pallas_call | solution.py:257
  73.5 7.9 %collective-permute-done.18.refs_0_ = bf16[144,1024]{1,0:T(8,128)(2,1)S(1)} collective-permute-done((bf16[144,1024]{1,0:T(8,128)(2,1)S(1)}, bf16[144,1024]{1,0:T(8,128)(2,1)S(1)}, u32[]{:S(2)}, u32[]{:S(2)}) %collective-permute-start.18) | collective-permute-done | bytes 294944 | tf_op jit(solution)/shard_map/ppermute | solution.py:35
  81.4 0.6 collective-permute-start.22
  82.1 1.1 collective-permute-start.26
  83.2 0.9 collective-permute-start.25
  84.7 12.9 %expert.5 = (bf16[128,1024]{1,0:T(8,128)(2,1)S(1)}, bf16[128,1024]{1,0:T(8,128)(2,1)S(1)}, bf16[128,1024]{1,0:T(8,128)(2,1)S(1)}, bf16[384,1024]{1,0:T(8,128)(2,1)S(1)}) custom-call(s32[1]{0:T(128)} %bitcast.1.where, bf16[144,1024]{1,0:T(8,128)(2,1)S(1)} %collective-permute-done.18.refs_0_, bf16[144,1024]{1,0:T(8,128)(2,1)S(1)} %collective-permute-done.17.refs_1_, ...), custom_call_target="tpu_custom_call" | custom-call | flops 2415919104 | bytes 3145728 | tf_op jit(solution)/shard_map/expert/pallas_call | solution.py:257
  97.8 1.1 collective-permute-start.32
  99.4 0.7 collective-permute-done.29
  100.2 1.2 collective-permute-start.31
  101.4 1.4 collective-permute-start.30
  102.9 9.5 %expert.6 = (bf16[128,1024]{1,0:T(8,128)(2,1)S(1)}, bf16[128,1024]{1,0:T(8,128)(2,1)S(1)}, bf16[256,1024]{1,0:T(8,128)(2,1)S(1)}) custom-call(s32[1]{0:T(128)} %bitcast.1.where, bf16[144,1024]{1,0:T(8,128)(2,1)S(1)} %collective-permute-done.24.refs_0_, bf16[144,1024]{1,0:T(8,128)(2,1)S(1)} %collective-permute-done.25.refs_1_, ...), custom_call_target="tpu_custom_call" | custom-call | flops 1610612736 | bytes 2097152 | tf_op jit(solution)/shard_map/expert/pallas_call | solution.py:257
  113.3 1.4 collective-permute-done.35
  114.9 1.5 collective-permute-start.37
  116.4 1.1 collective-permute-start.36
  117.5 9.7 %expert.7 = (bf16[128,1024]{1,0:T(8,128)(2,1)S(1)}, bf16[128,1024]{1,0:T(8,128)(2,1)S(1)}, bf16[256,1024]{1,0:T(8,128)(2,1)S(1)}) custom-call(s32[1]{0:T(128)} %bitcast.1.where, bf16[144,1024]{1,0:T(8,128)(2,1)S(1)} %collective-permute-done.32.refs_0_, bf16[144,1024]{1,0:T(8,128)(2,1)S(1)} %collective-permute-done.26.refs_1_, ...), custom_call_target="tpu_custom_call" | custom-call | flops 1610612736 | bytes 2097152 | tf_op jit(solution)/shard_map/expert/pallas_call | solution.py:257
  127.4 1.9 %collective-permute-done.38 = bf16[256,1024]{1,0:T(8,128)(2,1)S(1)} collective-permute-done((bf16[256,1024]{1,0:T(8,128)(2,1)S(1)}, bf16[256,1024]{1,0:T(8,128)(2,1)S(1)}, u32[]{:S(2)}, u32[]{:S(2)}) %collective-permute-start.38) | collective-permute-done | bytes 524320 | tf_op jit(solution)/shard_map/ppermute | solution.py:27
  129.5 1.0 collective-permute-start.39
  130.5 8.3 %collective-permute-done.39 = bf16[128,1024]{1,0:T(8,128)(2,1)S(1)} collective-permute-done((bf16[128,1024]{1,0:T(8,128)(2,1)S(1)}, bf16[128,1024]{1,0:T(8,128)(2,1)S(1)}, u32[]{:S(2)}, u32[]{:S(2)}) %collective-permute-start.39) | collective-permute-done | bytes 262176 | tf_op jit(solution)/shard_map/ppermute | solution.py:35
  139.6 1.5 collective-permute-start.41
  141.1 2.4 %collective-permute-start.40 = (bf16[128,1024]{1,0:T(8,128)(2,1)S(1)}, bf16[128,1024]{1,0:T(8,128)(2,1)S(1)}, u32[]{:S(2)}, u32[]{:S(2)}) collective-permute-start(bf16[128,1024]{1,0:T(8,128)(2,1)S(1)} %add_convert_fusion.1), channel_id=1, source_target_pairs={{0,4},{1,5},{2,6},{3,7},{4,0},{5,1},{6,2},{7,3},{8,12},{9,13},{10,... | collective-permute-start | bytes 786440 | tf_op jit(solution)/shard_map/ppermute | solution.py:35
  143.6 2.1 %collective-permute-done.20 = bf16[128,1024]{1,0:T(8,128)(2,1)S(1)} collective-permute-done((bf16[128,1024]{1,0:T(8,128)(2,1)S(1)}, bf16[128,1024]{1,0:T(8,128)(2,1)S(1)}, u32[]{:S(2)}, u32[]{:S(2)}) %collective-permute-start.20) | collective-permute-done | bytes 262176 | tf_op jit(solution)/shard_map/ppermute | solution.py:27
  145.8 8.5 %collective-permute-done.41.refs_4_ = bf16[128,1024]{1,0:T(8,128)(2,1)S(1)} collective-permute-done((bf16[128,1024]{1,0:T(8,128)(2,1)S(1)}, bf16[128,1024]{1,0:T(8,128)(2,1)S(1)}, u32[]{:S(2)}, u32[]{:S(2)}) %collective-permute-start.41) | collective-permute-done | bytes 262176 | tf_op jit(solution)/shard_map/ppermute | solution.py:35
  154.3 1.3 collective-permute-done.40.refs_3_
  155.6 4.7 %project.1 = bf16[128,4096]{1,0:T(8,128)(2,1)} custom-call(s32[1]{0:T(128)} %bitcast.where, f32[128,1024]{1,0:T(8,128)S(1)} %convert_add_fusion.refs_0_, bf16[128,1024]{1,0:T(8,128)(2,1)S(1)} %collective-permute-done.30.refs_1_, bf16[128,1024]{1,0:T(8,128)(2,1)S(1)} %collective-permute-done.31.refs_2_, ...), custom_call_target="tpu_custom_call" | custom-call | flops 1073741824 | bytes 8388608 | tf_op jit(solution)/shard_map/project/pallas_call | solution.py:319
  (68 shorter events, 7.1 us)
Async XLA Ops:
  6.5 1.2 copy-start
  6.5 74.9 %all-gather.5.cloned.1.call-start = ((), (), s32[]{:S(2)}) async-start(), calls=%async_computation | async-start | bytes 2359296 | tf_op jit(solution)/shard_map/all_gather | solution.py:369
  8.5 130.5 %all-gather.7.cloned.1.call-start = ((), (), s32[]{:S(2)}) async-start(), calls=%async_computation.1 | async-start | bytes 6291456 | tf_op jit(solution)/shard_map/all_gather | solution.py:432
  9.6 14.1 %collective-permute-start = (bf16[128,1024]{1,0:T(8,128)(2,1)S(1)}, bf16[128,1024]{1,0:T(8,128)(2,1)S(1)}, u32[]{:S(2)}, u32[]{:S(2)}) collective-permute-start(bf16[128,1024]{1,0:T(8,128)(2,1)S(1)} %get-tuple-element.152.refs_2_), channel_id=1, source_target_pairs={{0,2},{1,3},{2,0},{3,1},{4,6},{5,7},{6,4},{7,5},{8,10},{9,11},{10,... | collective-permute-start | bytes 786440 | tf_op jit(solution)/shard_map/ppermute | solution.py:35
  12.7 21.3 %collective-permute-start.4 = (bf16[128,1024]{1,0:T(8,128)(2,1)S(1)}, bf16[128,1024]{1,0:T(8,128)(2,1)S(1)}, u32[]{:S(2)}, u32[]{:S(2)}) collective-permute-start(bf16[128,1024]{1,0:T(8,128)(2,1)S(1)} %get-tuple-element.152.refs_2_), channel_id=1, source_target_pairs={{0,1},{1,0},{2,3},{3,2},{4,5},{5,4},{6,7},{7,6},{8,9},{9,8},{10,11... | collective-permute-start | bytes 786440 | tf_op jit(solution)/shard_map/ppermute | solution.py:35
  14.3 18.8 %collective-permute-start.2 = (bf16[128,1024]{1,0:T(8,128)(2,1)S(1)}, bf16[128,1024]{1,0:T(8,128)(2,1)S(1)}, u32[]{:S(2)}, u32[]{:S(2)}) collective-permute-start(bf16[128,1024]{1,0:T(8,128)(2,1)S(1)} %get-tuple-element.152.refs_2_), channel_id=1, source_target_pairs={{0,4},{1,5},{2,6},{3,7},{4,0},{5,1},{6,2},{7,3},{8,12},{9,13},{10,... | collective-permute-start | bytes 786440 | tf_op jit(solution)/shard_map/ppermute | solution.py:35
  16.9 1.2 copy-start.1
  19.0 15.5 %collective-permute-start.5 = (bf16[128,2048]{1,0:T(8,128)(2,1)S(1)}, bf16[128,2048]{1,0:T(8,128)(2,1)S(1)}, u32[]{:S(2)}, u32[]{:S(2)}) collective-permute-start(bf16[128,2048]{1,0:T(8,128)(2,1)S(1)} %get-tuple-element.83), channel_id=1, source_target_pairs={{0,16},{16,0},{1,17},{17,1},{2,18},{18,2},{3,19},{19,3},{4,20},{20... | collective-permute-start | bytes 1572872 | tf_op jit(solution)/shard_map/ppermute | solution.py:31
  23.7 9.3 %collective-permute-start.1 = (bf16[128,1024]{1,0:T(8,128)(2,1)S(1)}, bf16[128,1024]{1,0:T(8,128)(2,1)S(1)}, u32[]{:S(2)}, u32[]{:S(2)}) collective-permute-start(bf16[128,1024]{1,0:T(8,128)(2,1)S(1)} %collective-permute-done.refs_6_), channel_id=1, source_target_pairs={{0,1},{1,0},{2,3},{3,2},{4,5},{5,4},{6,7},{7,6},{8,9},{9,8},{10,11... | collective-permute-start | bytes 786440 | tf_op jit(solution)/shard_map/ppermute | solution.py:35
  33.1 8.8 %collective-permute-start.3 = (bf16[128,1024]{1,0:T(8,128)(2,1)S(1)}, bf16[128,1024]{1,0:T(8,128)(2,1)S(1)}, u32[]{:S(2)}, u32[]{:S(2)}) collective-permute-start(bf16[128,1024]{1,0:T(8,128)(2,1)S(1)} %collective-permute-done.2.refs_10_), channel_id=1, source_target_pairs={{0,2},{1,3},{2,0},{3,1},{4,6},{5,7},{6,4},{7,5},{8,10},{9,11},{10,... | collective-permute-start | bytes 786440 | tf_op jit(solution)/shard_map/ppermute | solution.py:35
  34.0 8.5 %collective-permute-start.9 = (bf16[128,1024]{1,0:T(8,128)(2,1)S(1)}, bf16[128,1024]{1,0:T(8,128)(2,1)S(1)}, u32[]{:S(2)}, u32[]{:S(2)}) collective-permute-start(bf16[128,1024]{1,0:T(8,128)(2,1)S(1)} %collective-permute-done.2.refs_10_), channel_id=1, source_target_pairs={{0,1},{1,0},{2,3},{3,2},{4,5},{5,4},{6,7},{7,6},{8,9},{9,8},{10,11... | collective-permute-start | bytes 786440 | tf_op jit(solution)/shard_map/ppermute | solution.py:35
  34.0 9.0 %collective-permute-start.7 = (bf16[128,1024]{1,0:T(8,128)(2,1)S(1)}, bf16[128,1024]{1,0:T(8,128)(2,1)S(1)}, u32[]{:S(2)}, u32[]{:S(2)}) collective-permute-start(bf16[128,1024]{1,0:T(8,128)(2,1)S(1)} %collective-permute-done.refs_6_), channel_id=1, source_target_pairs={{0,8},{8,0},{1,9},{9,1},{2,10},{10,2},{3,11},{11,3},{4,12},{12,4},... | collective-permute-start | bytes 786440 | tf_op jit(solution)/shard_map/ppermute | solution.py:27
  34.0 9.1 %collective-permute-start.8 = (bf16[128,1024]{1,0:T(8,128)(2,1)S(1)}, bf16[128,1024]{1,0:T(8,128)(2,1)S(1)}, u32[]{:S(2)}, u32[]{:S(2)}) collective-permute-start(bf16[128,1024]{1,0:T(8,128)(2,1)S(1)} %collective-permute-done.1.refs_7_), channel_id=1, source_target_pairs={{0,8},{8,0},{1,9},{9,1},{2,10},{10,2},{3,11},{11,3},{4,12},{12,4},... | collective-permute-start | bytes 786440 | tf_op jit(solution)/shard_map/ppermute | solution.py:27
  41.8 11.7 %collective-permute-start.12 = (bf16[128,1024]{1,0:T(8,128)(2,1)S(1)}, bf16[128,1024]{1,0:T(8,128)(2,1)S(1)}, u32[]{:S(2)}, u32[]{:S(2)}) collective-permute-start(bf16[128,1024]{1,0:T(8,128)(2,1)S(1)} %collective-permute-done.3.refs_2_), channel_id=1, source_target_pairs={{0,1},{1,0},{2,3},{3,2},{4,5},{5,4},{6,7},{7,6},{8,9},{9,8},{10,11... | collective-permute-start | bytes 786440 | tf_op jit(solution)/shard_map/ppermute | solution.py:35
  42.5 11.0 %collective-permute-start.10 = (bf16[128,1024]{1,0:T(8,128)(2,1)S(1)}, bf16[128,1024]{1,0:T(8,128)(2,1)S(1)}, u32[]{:S(2)}, u32[]{:S(2)}) collective-permute-start(bf16[128,1024]{1,0:T(8,128)(2,1)S(1)} %collective-permute-done.2.refs_10_), channel_id=1, source_target_pairs={{0,8},{8,0},{1,9},{9,1},{2,10},{10,2},{3,11},{11,3},{4,12},{12,4},... | collective-permute-start | bytes 786440 | tf_op jit(solution)/shard_map/ppermute | solution.py:27
  42.5 11.0 %collective-permute-start.11 = (bf16[128,1024]{1,0:T(8,128)(2,1)S(1)}, bf16[128,1024]{1,0:T(8,128)(2,1)S(1)}, u32[]{:S(2)}, u32[]{:S(2)}) collective-permute-start(bf16[128,1024]{1,0:T(8,128)(2,1)S(1)} %collective-permute-done.9.refs_11_), channel_id=1, source_target_pairs={{0,8},{8,0},{1,9},{9,1},{2,10},{10,2},{3,11},{11,3},{4,12},{12,4},... | collective-permute-start | bytes 786440 | tf_op jit(solution)/shard_map/ppermute | solution.py:27
  43.0 10.5 %collective-permute-start.6 = (bf16[128,1024]{1,0:T(8,128)(2,1)S(1)}, bf16[128,1024]{1,0:T(8,128)(2,1)S(1)}, u32[]{:S(2)}, u32[]{:S(2)}) collective-permute-start(bf16[128,1024]{1,0:T(8,128)(2,1)S(1)} %collective-permute-done.4.refs_3_), channel_id=1, source_target_pairs={{0,8},{8,0},{1,9},{9,1},{2,10},{10,2},{3,11},{11,3},{4,12},{12,4},... | collective-permute-start | bytes 786440 | tf_op jit(solution)/shard_map/ppermute | solution.py:27
  43.1 11.4 %collective-permute-start.13 = (bf16[128,1024]{1,0:T(8,128)(2,1)S(1)}, bf16[128,1024]{1,0:T(8,128)(2,1)S(1)}, u32[]{:S(2)}, u32[]{:S(2)}) collective-permute-start(bf16[128,1024]{1,0:T(8,128)(2,1)S(1)} %collective-permute-done.3.refs_2_), channel_id=1, source_target_pairs={{0,8},{8,0},{1,9},{9,1},{2,10},{10,2},{3,11},{11,3},{4,12},{12,4},... | collective-permute-start | bytes 786440 | tf_op jit(solution)/shard_map/ppermute | solution.py:27
  53.5 1.5 collective-permute-start.14
  55.5 8.4 %collective-permute-start.15 = (bf16[128,1024]{1,0:T(8,128)(2,1)S(1)}, bf16[128,1024]{1,0:T(8,128)(2,1)S(1)}, u32[]{:S(2)}, u32[]{:S(2)}) collective-permute-start(bf16[128,1024]{1,0:T(8,128)(2,1)S(1)} %get-tuple-element.90), channel_id=1, source_target_pairs={{0,16},{16,0},{1,17},{17,1},{2,18},{18,2},{3,19},{19,3},{4,20},{20... | collective-permute-start | bytes 786440 | tf_op jit(solution)/shard_map/ppermute | solution.py:31
  64.0 2.6 %collective-permute-start.16 = (bf16[144,1024]{1,0:T(8,128)(2,1)S(1)}, bf16[144,1024]{1,0:T(8,128)(2,1)S(1)}, u32[]{:S(2)}, u32[]{:S(2)}) collective-permute-start(bf16[144,1024]{1,0:T(8,128)(2,1)S(1)} %finish_latent.1.refs_0_), channel_id=1, source_target_pairs={{0,8},{8,0},{1,9},{9,1},{2,10},{10,2},{3,11},{11,3},{4,12},{12,4},... | collective-permute-start | bytes 884744 | tf_op jit(solution)/shard_map/ppermute | solution.py:27
  64.0 9.4 %collective-permute-start.19 = (bf16[144,1024]{1,0:T(8,128)(2,1)S(1)}, bf16[144,1024]{1,0:T(8,128)(2,1)S(1)}, u32[]{:S(2)}, u32[]{:S(2)}) collective-permute-start(bf16[144,1024]{1,0:T(8,128)(2,1)S(1)} %finish_latent.1.refs_0_), channel_id=1, source_target_pairs={{0,1},{1,0},{2,3},{3,2},{4,5},{5,4},{6,7},{7,6},{8,9},{9,8},{10,11... | collective-permute-start | bytes 884744 | tf_op jit(solution)/shard_map/ppermute | solution.py:35
  65.1 16.3 %collective-permute-start.18 = (bf16[144,1024]{1,0:T(8,128)(2,1)S(1)}, bf16[144,1024]{1,0:T(8,128)(2,1)S(1)}, u32[]{:S(2)}, u32[]{:S(2)}) collective-permute-start(bf16[144,1024]{1,0:T(8,128)(2,1)S(1)} %finish_latent.1.refs_0_), channel_id=1, source_target_pairs={{0,4},{1,5},{2,6},{3,7},{4,0},{5,1},{6,2},{7,3},{8,12},{9,13},{10,... | collective-permute-start | bytes 884744 | tf_op jit(solution)/shard_map/ppermute | solution.py:35
  66.5 14.9 %collective-permute-start.17 = (bf16[144,1024]{1,0:T(8,128)(2,1)S(1)}, bf16[144,1024]{1,0:T(8,128)(2,1)S(1)}, u32[]{:S(2)}, u32[]{:S(2)}) collective-permute-start(bf16[144,1024]{1,0:T(8,128)(2,1)S(1)} %finish_latent.1.refs_0_), channel_id=1, source_target_pairs={{0,2},{1,3},{2,0},{3,1},{4,6},{5,7},{6,4},{7,5},{8,10},{9,11},{10,... | collective-permute-start | bytes 884744 | tf_op jit(solution)/shard_map/ppermute | solution.py:35
  81.4 2.7 %collective-permute-start.23 = (bf16[144,1024]{1,0:T(8,128)(2,1)S(1)}, bf16[144,1024]{1,0:T(8,128)(2,1)S(1)}, u32[]{:S(2)}, u32[]{:S(2)}) collective-permute-start(bf16[144,1024]{1,0:T(8,128)(2,1)S(1)} %collective-permute-done.19.refs_2_), channel_id=1, source_target_pairs={{0,8},{8,0},{1,9},{9,1},{2,10},{10,2},{3,11},{11,3},{4,12},{12,4},... | collective-permute-start | bytes 884744 | tf_op jit(solution)/shard_map/ppermute | solution.py:27
  81.4 3.3 %collective-permute-start.22 = (bf16[144,1024]{1,0:T(8,128)(2,1)S(1)}, bf16[144,1024]{1,0:T(8,128)(2,1)S(1)}, u32[]{:S(2)}, u32[]{:S(2)}) collective-permute-start(bf16[144,1024]{1,0:T(8,128)(2,1)S(1)} %collective-permute-done.17.refs_1_), channel_id=1, source_target_pairs={{0,8},{8,0},{1,9},{9,1},{2,10},{10,2},{3,11},{11,3},{4,12},{12,4},... | collective-permute-start | bytes 884744 | tf_op jit(solution)/shard_map/ppermute | solution.py:27
  82.0 2.7 %collective-permute-start.21 = (bf16[144,1024]{1,0:T(8,128)(2,1)S(1)}, bf16[144,1024]{1,0:T(8,128)(2,1)S(1)}, u32[]{:S(2)}, u32[]{:S(2)}) collective-permute-start(bf16[144,1024]{1,0:T(8,128)(2,1)S(1)} %collective-permute-done.18.refs_0_), channel_id=1, source_target_pairs={{0,8},{8,0},{1,9},{9,1},{2,10},{10,2},{3,11},{11,3},{4,12},{12,4},... | collective-permute-start | bytes 884744 | tf_op jit(solution)/shard_map/ppermute | solution.py:27
  82.1 15.5 %collective-permute-start.26 = (bf16[144,1024]{1,0:T(8,128)(2,1)S(1)}, bf16[144,1024]{1,0:T(8,128)(2,1)S(1)}, u32[]{:S(2)}, u32[]{:S(2)}) collective-permute-start(bf16[144,1024]{1,0:T(8,128)(2,1)S(1)} %collective-permute-done.17.refs_1_), channel_id=1, source_target_pairs={{0,1},{1,0},{2,3},{3,2},{4,5},{5,4},{6,7},{7,6},{8,9},{9,8},{10,11... | collective-permute-start | bytes 884744 | tf_op jit(solution)/shard_map/ppermute | solution.py:35
  83.2 14.6 %collective-permute-start.25 = (bf16[144,1024]{1,0:T(8,128)(2,1)S(1)}, bf16[144,1024]{1,0:T(8,128)(2,1)S(1)}, u32[]{:S(2)}, u32[]{:S(2)}) collective-permute-start(bf16[144,1024]{1,0:T(8,128)(2,1)S(1)} %collective-permute-done.18.refs_0_), channel_id=1, source_target_pairs={{0,1},{1,0},{2,3},{3,2},{4,5},{5,4},{6,7},{7,6},{8,9},{9,8},{10,11... | collective-permute-start | bytes 884744 | tf_op jit(solution)/shard_map/ppermute | solution.py:35
  84.1 13.7 %collective-permute-start.24 = (bf16[144,1024]{1,0:T(8,128)(2,1)S(1)}, bf16[144,1024]{1,0:T(8,128)(2,1)S(1)}, u32[]{:S(2)}, u32[]{:S(2)}) collective-permute-start(bf16[144,1024]{1,0:T(8,128)(2,1)S(1)} %collective-permute-done.18.refs_0_), channel_id=1, source_target_pairs={{0,2},{1,3},{2,0},{3,1},{4,6},{5,7},{6,4},{7,5},{8,10},{9,11},{10,... | collective-permute-start | bytes 884744 | tf_op jit(solution)/shard_map/ppermute | solution.py:35
  97.8 2.3 %collective-permute-start.29 = (bf16[384,1024]{1,0:T(8,128)(2,1)S(1)}, bf16[384,1024]{1,0:T(8,128)(2,1)S(1)}, u32[]{:S(2)}, u32[]{:S(2)}) collective-permute-start(bf16[384,1024]{1,0:T(8,128)(2,1)S(1)} %get-tuple-element.121), channel_id=1, source_target_pairs={{0,8},{8,0},{1,9},{9,1},{2,10},{10,2},{3,11},{11,3},{4,12},{12,4},... | collective-permute-start | bytes 2359304 | tf_op jit(solution)/shard_map/ppermute | solution.py:27
  97.8 14.6 %collective-permute-start.32 = (bf16[144,1024]{1,0:T(8,128)(2,1)S(1)}, bf16[144,1024]{1,0:T(8,128)(2,1)S(1)}, u32[]{:S(2)}, u32[]{:S(2)}) collective-permute-start(bf16[144,1024]{1,0:T(8,128)(2,1)S(1)} %collective-permute-done.24.refs_0_), channel_id=1, source_target_pairs={{0,1},{1,0},{2,3},{3,2},{4,5},{5,4},{6,7},{7,6},{8,9},{9,8},{10,11... | collective-permute-start | bytes 884744 | tf_op jit(solution)/shard_map/ppermute | solution.py:35
  98.9 4.0 %collective-permute-start.27 = (bf16[144,1024]{1,0:T(8,128)(2,1)S(1)}, bf16[144,1024]{1,0:T(8,128)(2,1)S(1)}, u32[]{:S(2)}, u32[]{:S(2)}) collective-permute-start(bf16[144,1024]{1,0:T(8,128)(2,1)S(1)} %collective-permute-done.24.refs_0_), channel_id=1, source_target_pairs={{0,8},{8,0},{1,9},{9,1},{2,10},{10,2},{3,11},{11,3},{4,12},{12,4},... | collective-permute-start | bytes 884744 | tf_op jit(solution)/shard_map/ppermute | solution.py:27
  99.1 3.7 %collective-permute-start.28 = (bf16[144,1024]{1,0:T(8,128)(2,1)S(1)}, bf16[144,1024]{1,0:T(8,128)(2,1)S(1)}, u32[]{:S(2)}, u32[]{:S(2)}) collective-permute-start(bf16[144,1024]{1,0:T(8,128)(2,1)S(1)} %collective-permute-done.25.refs_1_), channel_id=1, source_target_pairs={{0,8},{8,0},{1,9},{9,1},{2,10},{10,2},{3,11},{11,3},{4,12},{12,4},... | collective-permute-start | bytes 884744 | tf_op jit(solution)/shard_map/ppermute | solution.py:27
  100.2 12.6 %collective-permute-start.31 = (bf16[128,1024]{1,0:T(8,128)(2,1)S(1)}, bf16[128,1024]{1,0:T(8,128)(2,1)S(1)}, u32[]{:S(2)}, u32[]{:S(2)}) collective-permute-start(bf16[128,1024]{1,0:T(8,128)(2,1)S(1)} %get-tuple-element.153), channel_id=1, source_target_pairs={{0,1},{1,0},{2,3},{3,2},{4,5},{5,4},{6,7},{7,6},{8,9},{9,8},{10,11... | collective-permute-start | bytes 786440 | tf_op jit(solution)/shard_map/ppermute | solution.py:35
  101.4 11.4 %collective-permute-start.30 = (bf16[128,1024]{1,0:T(8,128)(2,1)S(1)}, bf16[128,1024]{1,0:T(8,128)(2,1)S(1)}, u32[]{:S(2)}, u32[]{:S(2)}) collective-permute-start(bf16[128,1024]{1,0:T(8,128)(2,1)S(1)} %get-tuple-element.154), channel_id=1, source_target_pairs={{0,2},{1,3},{2,0},{3,1},{4,6},{5,7},{6,4},{7,5},{8,10},{9,11},{10,... | collective-permute-start | bytes 786440 | tf_op jit(solution)/shard_map/ppermute | solution.py:35
  112.8 1.9 %collective-permute-start.35 = (bf16[256,1024]{1,0:T(8,128)(2,1)S(1)}, bf16[256,1024]{1,0:T(8,128)(2,1)S(1)}, u32[]{:S(2)}, u32[]{:S(2)}) collective-permute-start(bf16[256,1024]{1,0:T(8,128)(2,1)S(1)} %get-tuple-element.136), channel_id=1, source_target_pairs={{0,8},{8,0},{1,9},{9,1},{2,10},{10,2},{3,11},{11,3},{4,12},{12,4},... | collective-permute-start | bytes 1572872 | tf_op jit(solution)/shard_map/ppermute | solution.py:27
  112.8 4.7 %collective-permute-start.34 = (bf16[144,1024]{1,0:T(8,128)(2,1)S(1)}, bf16[144,1024]{1,0:T(8,128)(2,1)S(1)}, u32[]{:S(2)}, u32[]{:S(2)}) collective-permute-start(bf16[144,1024]{1,0:T(8,128)(2,1)S(1)} %collective-permute-done.26.refs_1_), channel_id=1, source_target_pairs={{0,8},{8,0},{1,9},{9,1},{2,10},{10,2},{3,11},{11,3},{4,12},{12,4},... | collective-permute-start | bytes 884744 | tf_op jit(solution)/shard_map/ppermute | solution.py:27
  113.3 4.2 %collective-permute-start.33 = (bf16[144,1024]{1,0:T(8,128)(2,1)S(1)}, bf16[144,1024]{1,0:T(8,128)(2,1)S(1)}, u32[]{:S(2)}, u32[]{:S(2)}) collective-permute-start(bf16[144,1024]{1,0:T(8,128)(2,1)S(1)} %collective-permute-done.32.refs_0_), channel_id=1, source_target_pairs={{0,8},{8,0},{1,9},{9,1},{2,10},{10,2},{3,11},{11,3},{4,12},{12,4},... | collective-permute-start | bytes 884744 | tf_op jit(solution)/shard_map/ppermute | solution.py:27
  114.9 12.4 %collective-permute-start.37 = (bf16[128,1024]{1,0:T(8,128)(2,1)S(1)}, bf16[128,1024]{1,0:T(8,128)(2,1)S(1)}, u32[]{:S(2)}, u32[]{:S(2)}) collective-permute-start(bf16[128,1024]{1,0:T(8,128)(2,1)S(1)} %get-tuple-element.157), channel_id=1, source_target_pairs={{0,2},{1,3},{2,0},{3,1},{4,6},{5,7},{6,4},{7,5},{8,10},{9,11},{10,... | collective-permute-start | bytes 786440 | tf_op jit(solution)/shard_map/ppermute | solution.py:35
  116.4 10.9 %collective-permute-start.36 = (bf16[128,1024]{1,0:T(8,128)(2,1)S(1)}, bf16[128,1024]{1,0:T(8,128)(2,1)S(1)}, u32[]{:S(2)}, u32[]{:S(2)}) collective-permute-start(bf16[128,1024]{1,0:T(8,128)(2,1)S(1)} %get-tuple-element.158), channel_id=1, source_target_pairs={{0,1},{1,0},{2,3},{3,2},{4,5},{5,4},{6,7},{7,6},{8,9},{9,8},{10,11... | collective-permute-start | bytes 786440 | tf_op jit(solution)/shard_map/ppermute | solution.py:35
  127.3 2.0 %collective-permute-start.38 = (bf16[256,1024]{1,0:T(8,128)(2,1)S(1)}, bf16[256,1024]{1,0:T(8,128)(2,1)S(1)}, u32[]{:S(2)}, u32[]{:S(2)}) collective-permute-start(bf16[256,1024]{1,0:T(8,128)(2,1)S(1)} %get-tuple-element.141), channel_id=1, source_target_pairs={{0,8},{8,0},{1,9},{9,1},{2,10},{10,2},{3,11},{11,3},{4,12},{12,4},... | collective-permute-start | bytes 1572872 | tf_op jit(solution)/shard_map/ppermute | solution.py:27
  129.5 9.3 %collective-permute-start.39 = (bf16[128,1024]{1,0:T(8,128)(2,1)S(1)}, bf16[128,1024]{1,0:T(8,128)(2,1)S(1)}, u32[]{:S(2)}, u32[]{:S(2)}) collective-permute-start(bf16[128,1024]{1,0:T(8,128)(2,1)S(1)} %get-tuple-element.156), channel_id=1, source_target_pairs={{0,3},{1,2},{2,1},{3,0},{4,7},{5,6},{6,5},{7,4},{8,11},{9,10},{10,... | collective-permute-start | bytes 786440 | tf_op jit(solution)/shard_map/ppermute | solution.py:35
  139.0 16.6 %collective-permute-start.42 = (bf16[2,8,256,512]{3,2,1,0:T(8,128)(2,1)}, bf16[2,8,256,512]{3,2,1,0:T(8,128)(2,1)S(1)}, u32[]{:S(2)}, u32[]{:S(2)}) collective-permute-start(bf16[2,8,256,512]{3,2,1,0:T(8,128)(2,1)} %bitcast.6), channel_id=1, source_target_pairs={{0,8},{8,0},{1,9},{9,1},{2,10},{10,2},{3,11},{11,3},{4,12},{12,4},... | collective-permute-start | bytes 12582920 | tf_op jit(solution)/shard_map/ppermute | solution.py:27
  139.1 6.6 %collective-permute-start.20 = (bf16[128,1024]{1,0:T(8,128)(2,1)S(1)}, bf16[128,1024]{1,0:T(8,128)(2,1)S(1)}, u32[]{:S(2)}, u32[]{:S(2)}) collective-permute-start(bf16[128,1024]{1,0:T(8,128)(2,1)S(1)} %get-tuple-element.97), channel_id=1, source_target_pairs={{0,8},{8,0},{1,9},{9,1},{2,10},{10,2},{3,11},{11,3},{4,12},{12,4},... | collective-permute-start | bytes 786440 | tf_op jit(solution)/shard_map/ppermute | solution.py:27
  139.6 14.7 %collective-permute-start.41 = (bf16[128,1024]{1,0:T(8,128)(2,1)S(1)}, bf16[128,1024]{1,0:T(8,128)(2,1)S(1)}, u32[]{:S(2)}, u32[]{:S(2)}) collective-permute-start(bf16[128,1024]{1,0:T(8,128)(2,1)S(1)} %get-tuple-element.155), channel_id=1, source_target_pairs={{0,3},{1,2},{2,1},{3,0},{4,7},{5,6},{6,5},{7,4},{8,11},{9,10},{10,... | collective-permute-start | bytes 786440 | tf_op jit(solution)/shard_map/ppermute | solution.py:35
  141.1 14.5 %collective-permute-start.40 = (bf16[128,1024]{1,0:T(8,128)(2,1)S(1)}, bf16[128,1024]{1,0:T(8,128)(2,1)S(1)}, u32[]{:S(2)}, u32[]{:S(2)}) collective-permute-start(bf16[128,1024]{1,0:T(8,128)(2,1)S(1)} %add_convert_fusion.1), channel_id=1, source_target_pairs={{0,4},{1,5},{2,6},{3,7},{4,0},{5,1},{6,2},{7,3},{8,12},{9,13},{10,... | collective-permute-start | bytes 786440 | tf_op jit(solution)/shard_map/ppermute | solution.py:35
Sparse Core Ops, SparseCore 0:
  9.5 59.2 all-gather.4
  81.6 56.6 all-gather.6
